TPU v7x, 32 devices: a whole 2x2x4 slice. The times are simulated.
32 devices in a mesh: groups: 2 (over y), tile: 4 (over x, core), head: 4 (over z).
Axes of the slice: x: 2, y: 2, z: 4, core: 2. Of those that a mesh axis runs over, the one named last changes fastest.
Arguments:
- features: bfloat16 [24, 192, 7680], P('groups', 'tile'), parts along dimension 0, may hold values from -6 to 6
- proj_weight: bfloat16 [7680, 8192], P('tile', 'head'), may hold values from -0.0625 to 0.0625
- proj_bias: bfloat16 [8192], P('head'), may hold values from -3 to 3
- kv_weight: bfloat16 [8192, 2048], P('tile', 'head'), may hold values from -0.0625 to 0.0625
- key_gain: float32 [1, 128], replicated, may hold values from 0.1 to 1.9
- tile_map: int32 [8, 4], P('groups'), parts along dimension 0, may hold values from 0 to 11, as said below
- tile_count: int32 [8], P('groups'), parts along dimension 0, may hold values from 1 to 4, as said below
- decode_owner: int32 [8], P('groups'), parts along dimension 0, may hold values from 0 to 15, as said below
Outputs:
- cache: bfloat16 [8, 4, 768, 4, 128], P(('groups', 'tile'), 'head'), parts along dimension 0
There are 2 independent parts, one for each index of `groups`. A program takes and returns all parts, laid end to end along the dimension named above; an argument that names none is the same for every part. Nothing has to cross between parts.
Inputs may be any that keep to these rules, and one draw needn't show every extreme that they name: For each request r the entries tile_map[r, j] with j < tile_count[r] are its packed tiles in order, and every packed tile appears exactly once among all such entries; entries with j >= tile_count[r] repeat entry 0. `tile_count`: the counts sum to 12. The tile indices decode_owner[r] // 4 are distinct over the requests.
All inputs are finite; a program needn't handle non-finite values.
Results may differ from a plain program's by a relative error of at most 0.0049.
Values may be sent and summed in bfloat16 or wider, within the bound.
No kernel may reach another device: no remote copies, remote signals or barrier semaphores. Data moves between devices by JAX's collectives and lax.ppermute only.
A program may use at most 128 MiB of HBM per device.

v0:
```python
import jax
import jax.numpy as jnp
from jax import lax
from jax.sharding import PartitionSpec as P

eps_norm = 1e-05


def shifted_2(shard, axis, by):
    count = lax.axis_size(axis)
    return lax.ppermute(shard, axis, [(i, (i + by) % count) for i in range(count)])


def add_columns(operand, portion):
    return jnp.dot(operand, portion, preferred_element_type=jnp.float32)


def on_device(
    features, proj_weight, proj_bias, kv_weight, key_gain, tile_map, tile_count, decode_owner
):
    tile_slots, shard_len, feature_width = features.shape
    token_rows = tile_slots * shard_len
    feature_rows = features.reshape(token_rows, feature_width)
    weight_cols = lax.all_gather(proj_weight, "tile", axis=0, tiled=True)
    projected = jnp.dot(feature_rows, weight_cols, preferred_element_type=jnp.float32)
    projected_local = (projected + proj_bias.astype(jnp.float32)).astype(jnp.bfloat16)
    kv_width = kv_weight.shape[1]
    projected_all = lax.all_gather(projected_local, "head", axis=1, tiled=True)
    key_value = add_columns(projected_all, lax.all_gather(kv_weight, "tile", axis=0, tiled=True))
    layers, head_dim = key_gain.shape
    blocks = key_value.reshape(token_rows, -1, layers, 2, head_dim)
    keys_raw = blocks[:, :, :, 0]
    inv_rms = lax.rsqrt(jnp.mean(keys_raw * keys_raw, axis=-1, keepdims=True) + eps_norm)
    keys_normed = keys_raw * inv_rms * key_gain[None, None]
    stacked = jnp.stack([keys_normed, blocks[:, :, :, 1]], axis=3).astype(jnp.bfloat16)
    per_tile = stacked.reshape(tile_slots, shard_len * kv_width)
    tile_ranks = lax.axis_size("tile")
    head_groups = lax.axis_size("head")
    most_tiles = tile_map.shape[1]
    owner_tile = decode_owner // head_groups
    owner_turn = decode_owner % head_groups
    owned_by = (owner_tile[:, None] == jnp.arange(tile_ranks)[None, :]).astype(jnp.float32)
    usable = jnp.arange(most_tiles)[None, :] < tile_count[:, None]
    matched = (
        (tile_map[:, :, None] == jnp.arange(tile_slots)[None, None, :]) & usable[:, :, None]
    ).astype(jnp.float32)
    selector = jnp.einsum("rd,rjs->jds", owned_by, matched).astype(jnp.bfloat16)
    selector = selector.reshape(most_tiles * tile_ranks, tile_slots)
    outgoing = jnp.dot(selector, per_tile, preferred_element_type=jnp.float32).astype(jnp.bfloat16)
    outgoing = outgoing.reshape(most_tiles, tile_ranks, shard_len, kv_width)
    arrived = lax.all_to_all(outgoing, "tile", split_axis=1, concat_axis=1, tiled=True)
    gathered_rows = arrived.reshape(
        most_tiles * tile_ranks * shard_len, kv_width // head_dim, head_dim
    )
    my_turn = jnp.sum(jnp.where(owner_tile == lax.axis_index("tile"), owner_turn, 0))
    stride = 1
    while stride < head_groups:
        shifted = shifted_2(gathered_rows, "head", stride)
        gathered_rows = jnp.where(my_turn // stride % 2 == 1, shifted, gathered_rows)
        stride = stride * 2
    return gathered_rows[None, None]


def solution(mesh):
    placed = (
        P("groups", "tile", None),
        P("tile", "head"),
        P("head"),
        P("tile", "head"),
        P(),
        P("groups", None),
        P("groups"),
        P("groups"),
    )
    return jax.shard_map(
        on_device,
        mesh=mesh,
        in_specs=placed,
        out_specs=P(("groups", "tile"), "head", None, None, None),
        check_vma=False,
    )
```

profile of v0, /device:TPU:0, one launch (start us, length us, event | category | flops | bytes accessed | tf_op | source)
XLA Modules:
  0.0 524.1 jit_solution(13301731459679222602)
XLA Ops:
  6.5 0.0 copy-start
  6.5 0.0 all-gather.4.cloned.1.call-start
  6.5 0.7 all-gather.4.cloned.1.call-update
  7.3 0.0 all-gather.8.cloned.1.call-start
  7.3 0.7 all-gather.8.cloned.1.call-update
  8.0 0.0 all-gather.6.cloned.1.call-start
  8.1 0.0 copy-done
  8.1 193.2 %all-gather.4.cloned.1.call-done = bf16[7680,2048]{1,0:T(8,128)(2,1)} async-done(((bf16[1920,2048]{1,0:T(8,128)(2,1)}), bf16[7680,2048]{1,0:T(8,128)(2,1)}) %all-gather.4.cloned.1.call-update) | async-done | bytes 31457296 | tf_op jit(solution)/shard_map/all_gather | solution.py:24
  201.3 0.0 copy-start.1
  201.3 0.0 copy-start.4
  201.3 0.0 copy-start.3
  201.3 25.7 %add_convert_fusion = bf16[576,2048]{1,0:T(8,128)(2,1)} fusion(bf16[576,7680]{1,0:T(8,128)(2,1)} %bitcast.34, bf16[7680,2048]{1,0:T(8,128)(2,1)} %all-gather.4.cloned.1.call-done, f32[2048]{0:T(1024)S(1)} %convert_element_type.38), kind=kOutput, calls=%fused_computation.1 | convolution fusion | flops 18121752576 | bytes 42672128 | tf_op jit(solution)/shard_map/dot_general | solution.py:25
  227.0 0.0 all-gather.6.cloned.1.call-update
  227.1 0.0 copy-done.1
  227.1 0.1 copy.19
  227.2 0.0 copy-done.4
  227.2 0.0 copy-done.3
  227.2 0.6 fusion.7
  227.8 0.2 convolution_convert_fusion.1
  228.0 0.0 copy-start.2
  228.0 33.1 %all-gather.8.cloned.1.call-done = bf16[8192,512]{1,0:T(8,128)(2,1)} async-done(((bf16[2048,512]{1,0:T(8,128)(2,1)}), bf16[8192,512]{1,0:T(8,128)(2,1)}) %all-gather.8.cloned.1.call-update) | async-done | bytes 8388624 | tf_op jit(solution)/shard_map/all_gather | solution.py:29
  261.2 168.4 %all-gather.6.cloned.1.call-done = bf16[576,8192]{1,0:T(8,128)(2,1)} async-done(((bf16[576,2048]{1,0:T(8,128)(2,1)}), bf16[576,8192]{1,0:T(8,128)(2,1)}) %all-gather.6.cloned.1.call-update) | async-done | bytes 9437200 | tf_op jit(solution)/shard_map/all_gather | solution.py:28
  429.6 10.0 %fusion.8 = f32[576,512]{1,0:T(8,128)S(1)} fusion(bf16[576,8192]{1,0:T(8,128)(2,1)} %all-gather.6.cloned.1.call-done, bf16[8192,512]{1,0:T(8,128)(2,1)} %all-gather.8.cloned.1.call-done), kind=kOutput, calls=%fused_computation.25 | convolution fusion | flops 4831838208 | bytes 19005440 | tf_op jit(solution)/shard_map/dot_general | solution.py:15
  439.6 0.8 reshape.111
  440.4 2.0 multiply_reduce_fusion
  442.4 0.6 slice.14
  443.1 0.0 copy-done.2
  443.1 1.5 multiply_convert_fusion
  444.6 1.3 pad_maximum_fusion
  445.9 0.4 convert_element_type.40
  446.3 0.3 convolution_convert_fusion
  446.6 0.2 copy.24
  446.9 0.1 copy.22
  446.9 14.2 %all_to_all.5 = bf16[4,4,48,512]{3,2,0,1:T(8,128)(2,1)S(1)} all-to-all(bf16[4,4,48,512]{3,2,0,1:T(8,128)(2,1)S(1)} %copy.22), channel_id=1, replica_groups=mesh['groups'=2,'tile'=4,'head'=4] {'tile'}, dimensions={1} | all-to-all | bytes 1572864 | tf_op jit(solution)/shard_map/all_to_all | solution.py:51
  461.1 0.1 copy.23
  461.2 0.2 reshape.113
  461.4 0.1 collective-permute-start
  463.4 18.7 %collective-permute-done = bf16[768,4,128]{2,1,0:T(4,128)(2,1)S(1)} collective-permute-done((bf16[768,4,128]{2,1,0:T(4,128)(2,1)S(1)}, bf16[768,4,128]{2,1,0:T(4,128)(2,1)S(1)}, u32[]{:S(2)}, u32[]{:S(2)}) %collective-permute-start) | collective-permute-done | bytes 786464 | tf_op jit(solution)/shard_map/ppermute | solution.py:11
  482.2 0.1 broadcast_select_fusion
  482.2 0.1 collective-permute-start.1
  483.0 33.3 %collective-permute-done.1 = bf16[768,4,128]{2,1,0:T(4,128)(2,1)S(1)} collective-permute-done((bf16[768,4,128]{2,1,0:T(4,128)(2,1)S(1)}, bf16[768,4,128]{2,1,0:T(4,128)(2,1)S(1)}, u32[]{:S(2)}, u32[]{:S(2)}) %collective-permute-start.1) | collective-permute-done | bytes 786464 | tf_op jit(solution)/shard_map/ppermute | solution.py:11
  516.3 1.3 select_bitcast_fusion
  (3 shorter events, 0.1 us)
Async XLA Ops:
  6.5 1.5 copy-start
  6.5 194.7 %all-gather.4.cloned.1.call-start = ((), (), s32[]{:S(2)}) async-start(), calls=%async_computation.1 | async-start | bytes 39321600 | tf_op jit(solution)/shard_map/all_gather | solution.py:24
  7.3 253.9 %all-gather.8.cloned.1.call-start = ((), (), s32[]{:S(2)}) async-start(), calls=%async_computation.3 | async-start | bytes 10485760 | tf_op jit(solution)/shard_map/all_gather | solution.py:29
  8.0 421.5 %all-gather.6.cloned.1.call-start = ((), (), s32[]{:S(2)}) async-start(), calls=%async_computation.2 | async-start | bytes 11796480 | tf_op jit(solution)/shard_map/all_gather | solution.py:28
  201.3 25.8 %copy-start.1 = (s32[4,4]{1,0:T(4,128)S(1)}, s32[4,4]{1,0:T(4,128)}, u32[]{:S(2)}) copy-start(s32[4,4]{1,0:T(4,128)} %param.13) | copy-start | bytes 196
  201.3 25.9 %copy-start.4 = (s32[4]{0:T(128)S(1)}, s32[4]{0:T(128)}, u32[]{:S(2)}) copy-start(s32[4]{0:T(128)} %param.14) | copy-start | bytes 52
  201.3 25.9 %copy-start.3 = (s32[4]{0:T(128)S(1)}, s32[4]{0:T(128)}, u32[]{:S(2)}) copy-start(s32[4]{0:T(128)} %param.15) | copy-start | bytes 52
  228.0 215.0 %copy-start.2 = (f32[1,128]{1,0:T(1,128)S(1)}, f32[1,128]{1,0:T(1,128)}, u32[]{:S(2)}) copy-start(f32[1,128]{1,0:T(1,128)} %param.12) | copy-start | bytes 1540
  461.4 20.8 %collective-permute-start = (bf16[768,4,128]{2,1,0:T(4,128)(2,1)S(1)}, bf16[768,4,128]{2,1,0:T(4,128)(2,1)S(1)}, u32[]{:S(2)}, u32[]{:S(2)}) collective-permute-start(bf16[768,4,128]{2,1,0:T(4,128)(2,1)S(1)} %reshape.113), channel_id=1, source_target_pairs={{0,1},{1,2},{2,3},{3,0},{4,5},{5,6},{6,7},{7,4},{8,9},{9,10},{10,1... | collective-permute-start | bytes 2359304 | tf_op jit(solution)/shard_map/ppermute | solution.py:11
  482.2 34.1 %collective-permute-start.1 = (bf16[768,4,128]{2,1,0:T(4,128)(2,1)S(1)}, bf16[768,4,128]{2,1,0:T(4,128)(2,1)S(1)}, u32[]{:S(2)}, u32[]{:S(2)}) collective-permute-start(bf16[768,4,128]{2,1,0:T(4,128)(2,1)S(1)} %bitcast.26), channel_id=1, source_target_pairs={{0,2},{1,3},{2,0},{3,1},{4,6},{5,7},{6,4},{7,5},{8,10},{9,11},{10,... | collective-permute-start | bytes 2359304 | tf_op jit(solution)/shard_map/ppermute | solution.py:11
Sparse Core Ops, SparseCore 0:
  8.9 192.2 all-gather.3
  202.8 58.2 all-gather.7
  262.7 166.7 all-gather.5
where the time goes:
time: 524 us
  waiting for transfers between devices  448 us (85%)
  matrix products  36.3 us (7%)
  between operations  15.9 us (3%)
  blocking collectives  14.2 us (3%)
  other arithmetic  6.92 us (1%)
    all_gather x1, waiting for transfers between devices, on_device(): weight_cols = lax.all_gather(proj_weight, 'tile', axis=0, tiled=True)  193 us
    all_gather x1, waiting for transfers between devices, on_device(): projected_all = lax.all_gather(projected_local, 'head', axis=1, tiled=True)  168 us
    ppermute x2, waiting for transfers between devices, shifted_2(): lax.ppermute(shard, axis, [(i, (i + by) % count) for i in range(count)])  52 us
    all_gather x1, waiting for transfers between devices, on_device(): lax.all_gather(kv_weight, 'tile', axis=0, tiled=True)  33.1 us
    dot_general x1, matrix products, on_device(): jnp.dot(feature_rows, weight_cols, preferred_element_type=jnp.float32)  25.7 us
    all_to_all x1, blocking collectives, on_device(): lax.all_to_all(outgoing, 'tile', split_axis=1, concat_axis=1, tiled=True)  14.2 us
  transfers between devices with their start and end apart: 5, of which 5 were waited for; matrix products, arithmetic and copies ran while one was open for 5% of the time, Pallas kernels for 0%

commit v1 on v0

--- a/solution.py
+++ b/solution.py
@@ -11,11 +11,24 @@
     return lax.ppermute(shard, axis, [(i, (i + by) % count) for i in range(count)])
 
 
+def swapped(shard, axis, bit):
+    return lax.ppermute(shard, axis, [(i, i ^ bit) for i in range(lax.axis_size(axis))])
+
+
 def add_columns(operand, portion):
     return jnp.dot(operand, portion, preferred_element_type=jnp.float32)
 
 
-def on_device(
+def routing(tile_map, tile_count, decode_owner, tile_slots, head_groups):
+    most_tiles = tile_map.shape[1]
+    owner_tile = decode_owner // head_groups
+    owner_turn = decode_owner % head_groups
+    usable = jnp.arange(most_tiles)[None, :] < tile_count[:, None]
+    matched = (tile_map[:, :, None] == jnp.arange(tile_slots)[None, None, :]) & usable[:, :, None]
+    return owner_tile, owner_turn, matched
+
+
+def gather_plan(
     features, proj_weight, proj_bias, kv_weight, key_gain, tile_map, tile_count, decode_owner
 ):
     tile_slots, shard_len, feature_width = features.shape
@@ -37,16 +50,13 @@
     tile_ranks = lax.axis_size("tile")
     head_groups = lax.axis_size("head")
     most_tiles = tile_map.shape[1]
-    owner_tile = decode_owner // head_groups
-    owner_turn = decode_owner % head_groups
+    owner_tile, owner_turn, matched = routing(
+        tile_map, tile_count, decode_owner, tile_slots, head_groups
+    )
     owned_by = (owner_tile[:, None] == jnp.arange(tile_ranks)[None, :]).astype(jnp.float32)
-    usable = jnp.arange(most_tiles)[None, :] < tile_count[:, None]
-    matched = (
-        (tile_map[:, :, None] == jnp.arange(tile_slots)[None, None, :]) & usable[:, :, None]
-    ).astype(jnp.float32)
-    selector = jnp.einsum("rd,rjs->jds", owned_by, matched).astype(jnp.bfloat16)
-    selector = selector.reshape(most_tiles * tile_ranks, tile_slots)
-    outgoing = jnp.dot(selector, per_tile, preferred_element_type=jnp.float32).astype(jnp.bfloat16)
+    selector = jnp.einsum("rd,rjs->jds", owned_by, matched.astype(jnp.float32))
+    selector = selector.astype(jnp.bfloat16).reshape(most_tiles * tile_ranks, tile_slots)
+    outgoing = add_columns(selector, per_tile).astype(jnp.bfloat16)
     outgoing = outgoing.reshape(most_tiles, tile_ranks, shard_len, kv_width)
     arrived = lax.all_to_all(outgoing, "tile", split_axis=1, concat_axis=1, tiled=True)
     gathered_rows = arrived.reshape(
@@ -61,6 +71,100 @@
     return gathered_rows[None, None]
 
 
+block_order = ((3, 2, 1, 0), (3, 2, 0, 1), (0, 1, 3, 2), (0, 1, 2, 3))
+inward = [(0, 1), (3, 2)]
+across = [(1, 2), (2, 1)]
+outward = [(2, 3), (1, 0)]
+
+
+def sum_over_planes(block):
+    def send(value, pairs):
+        return lax.ppermute(value.astype(jnp.bfloat16), "head", pairs).astype(jnp.float32)
+
+    first_in = send(block(0), inward)
+    second_in = send(block(1), inward)
+    third_in = send(block(2), inward)
+    first_across = send(block(0) + first_in, across)
+    second_across = send(block(1) + second_in, across)
+    first_out = send(block(2) + first_across, outward)
+    return (block(3) + third_in + second_across + first_out).astype(jnp.bfloat16)
+
+
+def product_plan(
+    features, proj_weight, proj_bias, kv_weight, key_gain, tile_map, tile_count, decode_owner
+):
+    tile_slots, shard_len, feature_width = features.shape
+    token_rows = tile_slots * shard_len
+    depth = proj_weight.shape[0]
+    layers, head_dim = key_gain.shape
+    most_tiles = tile_map.shape[1]
+    group, tile, head = (lax.axis_index(name) for name in ("groups", "tile", "head"))
+    feature_rows = features.reshape(token_rows, feature_width)
+    feature_parts = [
+        lax.dynamic_slice_in_dim(feature_rows, (tile ^ r) * depth, depth, axis=1) for r in range(4)
+    ]
+    flip = [(t * 4 + h, h * 4 + t) for t in range(4) for h in range(4)]
+
+    def turned(shard):
+        return lax.ppermute(shard, ("tile", "head"), flip)
+
+    bias_rows = turned(proj_bias)
+    bias_part = add_columns(bias_rows[None], kv_weight)
+    bias_part = bias_part + swapped(bias_part, "tile", 1)
+    bias_part = bias_part + swapped(bias_part, "tile", 2)
+    bias_part = bias_part.reshape(2, layers, 2, head_dim)
+
+    owner_tile, owner_turn, matched = routing(tile_map, tile_count, decode_owner, tile_slots, 4)
+    turn_of = jnp.sum(jnp.where(matched, owner_turn[:, None, None], 0), axis=(0, 1))
+    owned_by = (owner_tile[:, None] == (tile ^ jnp.arange(4))[None, :]).astype(jnp.float32)
+    selector = jnp.einsum("rd,rjs->djs", owned_by, matched.astype(jnp.float32))
+    selector = selector.astype(jnp.bfloat16).reshape(4 * most_tiles, tile_slots)
+
+    order = jnp.array(block_order, jnp.int32)[head]
+    per_head = kv_weight.reshape(-1, 2, layers, 2, head_dim)
+    mine = lax.dynamic_index_in_dim(per_head, group, axis=1, keepdims=False)
+    width = layers * head_dim
+    routed = []
+    for part in range(2):
+        block_0 = turned(mine[:, :, part].reshape(-1, width))
+        block_2 = swapped(block_0, "tile", 2)
+        near = jnp.concatenate([block_0, swapped(block_0, "tile", 1)], axis=1)
+        far = jnp.concatenate([block_2, swapped(block_2, "tile", 1)], axis=1)
+        near_product = add_columns(proj_weight, near)
+        far_product = add_columns(proj_weight, far)
+
+        def block(k):
+            which = order[k] ^ tile
+            from_near = lax.dynamic_slice_in_dim(near_product, which % 2 * width, width, axis=1)
+            from_far = lax.dynamic_slice_in_dim(far_product, which % 2 * width, width, axis=1)
+            return jnp.where(which >= 2, from_far, from_near)
+
+        own = sum_over_planes(block)
+        across_x, across_y = swapped(own, "tile", 2), swapped(own, "groups", 1)
+        diagonal = swapped(across_y, "tile", 2) if part == 0 else swapped(across_x, "groups", 1)
+        rows_0 = jnp.concatenate([own, across_y], axis=1)
+        rows_2 = jnp.concatenate([across_x, diagonal], axis=1)
+        rows = [rows_0, swapped(rows_0, "tile", 1), rows_2, swapped(rows_2, "tile", 1)]
+        total = sum(add_columns(feature_parts[r], rows[r]) for r in range(4))
+        total = total.reshape(token_rows, 2, layers, head_dim)
+        total = jnp.where(group == 0, total, total[:, ::-1]) + bias_part[None, :, :, part]
+        if part == 0:
+            inv_rms = lax.rsqrt(jnp.mean(total * total, axis=-1, keepdims=True) + eps_norm)
+            total = total * inv_rms * key_gain[None, None]
+        rolled = total.astype(jnp.bfloat16).reshape(tile_slots, shard_len, 2 * width)
+        for stride in (1, 2):
+            odd = (turn_of // stride % 2 == 1)[:, None, None]
+            rolled = jnp.where(odd, shifted_2(rolled, "head", stride), rolled)
+        outgoing = add_columns(selector, rolled.reshape(tile_slots, -1)).astype(jnp.bfloat16)
+        outgoing = outgoing.reshape(4, most_tiles, shard_len, 2, layers, head_dim)
+        arrived = [outgoing[0]] + [swapped(outgoing[r], "tile", r) for r in (1, 2, 3)]
+        even = [jnp.where(tile % 2 == 0, arrived[r], arrived[r ^ 1]) for r in range(4)]
+        ranked = [jnp.where(tile < 2, even[r], even[r ^ 2]) for r in range(4)]
+        routed.append(jnp.stack(ranked, axis=1))
+    cache = jnp.stack(routed, axis=-2)
+    return cache.reshape(1, 1, most_tiles * 4 * shard_len, 4 * layers, head_dim)
+
+
 def solution(mesh):
     placed = (
         P("groups", "tile", None),
@@ -72,8 +176,9 @@
         P("groups"),
         P("groups"),
     )
+    sizes = tuple(mesh.shape[name] for name in ("groups", "tile", "head"))
     return jax.shard_map(
-        on_device,
+        product_plan if sizes == (2, 4, 4) else gather_plan,
         mesh=mesh,
         in_specs=placed,
         out_specs=P(("groups", "tile"), "head", None, None, None),

time: 524 us -> 290 us (0.55)
  waiting for transfers between devices: 448 us -> 105 us
  starting transfers between devices: 0.21 us -> 120 us
  blocking collectives: 14.2 us -> 0 us
  local copies, waits for them, and re-layouts: 2.39 us -> 15.2 us
  between operations: 15.9 us -> 3.44 us
  other arithmetic: 6.92 us -> 14.5 us
  matrix products: 36.3 us -> 30.6 us
    all_gather x3 -> x0, waiting for transfers between devices: 395 us -> none  [the longest x1 193 us: on_device(): weight_cols = lax.all_gather(proj_weight, 'tile', axis=0, tiled=True)]
    ppermute x0 -> x39, starting transfers between devices: none -> 113 us  [the longest x24 71.6 us: swapped(): lax.ppermute(shard, axis, [(i, i ^ bit) for i in range(lax.axis_size(axis...]
    ppermute x0 -> x39, waiting for transfers between devices: none -> 71.2 us  [the longest x12 45.5 us: send(): lax.ppermute(value.astype(jnp.bfloat16), 'head', pairs).astype(jnp.float32)]
    dot_general x3 -> x1, matrix products: 26.3 us -> 0.19 us  [product_plan(): selector = jnp.einsum('rd,rjs->djs', owned_by, matched.astype(jnp.float32))]
    dot_general x1 -> x15, matrix products: 10 us -> 30.4 us  [add_columns(): return jnp.dot(operand, portion, preferred_element_type=jnp.float32)]
    ppermute x2 -> x4, waiting for transfers between devices: 52 us -> 33.5 us  [shifted_2(): lax.ppermute(shard, axis, [(i, (i + by) % count) for i in range(count)])]
    all_to_all x1 -> x0, blocking collectives: 14.2 us -> none  [on_device(): lax.all_to_all(outgoing, 'tile', split_axis=1, concat_axis=1, tiled=True)]
    convert_element_type x1 -> x10, other arithmetic: 0.01 us -> 8.75 us  [the longest x6 5.55 us: send(): value.astype(jnp.bfloat16)]
  transfers between devices with their start and end apart: 5 -> 43, of which waited for: 5 -> 18; matrix products, arithmetic and copies ran while one was open for 5% -> 17% of each run, Pallas kernels for 0% -> 0%
where the time goes in v1:
time: 290 us; the launch traced here: 289 us
  starting transfers between devices  120 us (41%)
  waiting for transfers between devices  105 us (36%)
  matrix products  30.6 us (11%)
  local copies, waits for them, and re-layouts  15.2 us (5%)
  other arithmetic  14.5 us (5%)
  between operations  3.44 us (1%)
    ppermute x24, starting transfers between devices, swapped(): lax.ppermute(shard, axis, [(i, i ^ bit) for i in range(lax.axis_size(axis...  71.6 us
    ppermute x12, waiting for transfers between devices, send(): lax.ppermute(value.astype(jnp.bfloat16), 'head', pairs).astype(jnp.float32)  45.5 us
    ppermute x12, starting transfers between devices, send(): lax.ppermute(value.astype(jnp.bfloat16), 'head', pairs).astype(jnp.float32)  39.4 us
    ppermute x4, waiting for transfers between devices, shifted_2(): lax.ppermute(shard, axis, [(i, (i + by) % count) for i in range(count)])  33.5 us
    dot_general x15, matrix products, add_columns(): return jnp.dot(operand, portion, preferred_element_type=jnp.float32)  30.4 us
    ppermute x24, waiting for transfers between devices, swapped(): lax.ppermute(shard, axis, [(i, i ^ bit) for i in range(lax.axis_size(axis...  25.7 us
    ppermute x4, starting transfers between devices, shifted_2(): lax.ppermute(shard, axis, [(i, (i + by) % count) for i in range(count)])  7.19 us
  transfers between devices with their start and end apart: 43, of which 18 were waited for; matrix products, arithmetic and copies ran while one was open for 17% of the time, Pallas kernels for 0%

profile of v1, /device:TPU:0, one launch (start us, length us, event | category | flops | bytes accessed | tf_op | source)
XLA Modules:
  0.0 288.8 jit_solution(14586099595082197433)
XLA Ops:
  0.0 2.5 reshape.157
  5.1 42.4 %collective-permute-start.24 = (bf16[2048,128]{1,0:T(8,128)(2,1)S(1)}, bf16[2048,128]{1,0:T(8,128)(2,1)}, u32[]{:S(2)}, u32[]{:S(2)}) collective-permute-start(bf16[2048,128]{1,0:T(8,128)(2,1)S(1)} %collective-permute-done.23), channel_id=1, source_target_pairs={{0,8},{4,12},{8,0},{12,4},{1,9},{5,13},{9,1},{13,5},{2,10},{6,14},... | collective-permute-start | bytes 1572872 | tf_op jit(solution)/shard_map/ppermute | solution.py:15
  47.5 10.9 %collective-permute-start.1 = (bf16[2048,128]{1,0:T(8,128)(2,1)S(1)}, bf16[2048,128]{1,0:T(8,128)(2,1)}, u32[]{:S(2)}, u32[]{:S(2)}) collective-permute-start(bf16[2048,128]{1,0:T(8,128)(2,1)S(1)} %collective-permute-done), channel_id=1, source_target_pairs={{0,8},{4,12},{8,0},{12,4},{1,9},{5,13},{9,1},{13,5},{2,10},{6,14},... | collective-permute-start | bytes 1572872 | tf_op jit(solution)/shard_map/ppermute | solution.py:15
  62.8 1.9 collective-permute-start.16
  65.7 5.8 %fusion.46 = f32[256,1920]{1,0:T(8,128)S(1)} fusion(bf16[1920,2048]{1,0:T(8,128)(2,1)} %param.10, bf16[2048,128]{1,0:T(8,128)(2,1)} %collective-permute-done.26, bf16[2048,128]{1,0:T(8,128)(2,1)S(1)} %collective-permute-done.23), kind=kOutput, calls=%fused_computation.37 | convolution fusion | flops 2015363072 | bytes 10878976 | tf_op jit(solution)/shard_map/dot_general | solution.py:19
  71.6 2.4 fusion.38
  74.0 3.5 %fusion.42 = f32[256,1920]{1,0:T(8,128)S(1)} fusion(bf16[1920,2048]{1,0:T(8,128)(2,1)S(1)} %bitcast.143, bf16[2048,128]{1,0:T(8,128)(2,1)S(1)} %collective-permute-done.25, bf16[2048,128]{1,0:T(8,128)(2,1)} %collective-permute-done.24), kind=kOutput, calls=%fused_computation.33 | convolution fusion | flops 2015363072 | bytes 10878976 | tf_op jit(solution)/shard_map/dot_general | solution.py:19
  77.8 10.1 %collective-permute-start.28 = (bf16[1920,128]{0,1:T(8,128)(2,1)S(1)}, bf16[1920,128]{0,1:T(8,128)(2,1)S(1)}, u32[]{:S(2)}, u32[]{:S(2)}) collective-permute-start(bf16[1920,128]{0,1:T(8,128)(2,1)S(1)} %get-tuple-element.12), channel_id=1, source_target_pairs={{0,1},{3,2},{4,5},{7,6},{8,9},{11,10},{12,13},{15,14},{16,17},{19,... | collective-permute-start | bytes 1474568 | tf_op jit(solution)/shard_map/ppermute | solution.py:82
  87.9 1.3 collective-permute-start.30
  89.2 1.5 collective-permute-start.27
  90.7 3.5 %fusion.34 = f32[256,1920]{1,0:T(8,128)S(1)} fusion(bf16[1920,2048]{1,0:T(8,128)(2,1)S(1)} %bitcast.143, bf16[2048,128]{1,0:T(8,128)(2,1)S(1)} %collective-permute-done.2, bf16[2048,128]{1,0:T(8,128)(2,1)} %collective-permute-done.1), kind=kOutput, calls=%fused_computation.25 | convolution fusion | flops 2015363072 | bytes 10878976 | tf_op jit(solution)/shard_map/dot_general | solution.py:19
  96.0 3.4 %collective-permute-done.28 = bf16[1920,128]{0,1:T(8,128)(2,1)S(1)} collective-permute-done((bf16[1920,128]{0,1:T(8,128)(2,1)S(1)}, bf16[1920,128]{0,1:T(8,128)(2,1)S(1)}, u32[]{:S(2)}, u32[]{:S(2)}) %collective-permute-start.28) | collective-permute-done | bytes 491552 | tf_op jit(solution)/shard_map/ppermute | solution.py:82
  99.4 4.4 %collective-permute-start.7 = (bf16[1920,128]{0,1:T(8,128)(2,1)S(1)}, bf16[1920,128]{0,1:T(8,128)(2,1)S(1)}, u32[]{:S(2)}, u32[]{:S(2)}) collective-permute-start(bf16[1920,128]{0,1:T(8,128)(2,1)S(1)} %get-tuple-element.6), channel_id=1, source_target_pairs={{0,1},{3,2},{4,5},{7,6},{8,9},{11,10},{12,13},{15,14},{16,17},{19,... | collective-permute-start | bytes 1474568 | tf_op jit(solution)/shard_map/ppermute | solution.py:82
  103.8 6.1 %collective-permute-done.30 = bf16[1920,128]{0,1:T(8,128)(2,1)S(1)} collective-permute-done((bf16[1920,128]{0,1:T(8,128)(2,1)S(1)}, bf16[1920,128]{0,1:T(8,128)(2,1)S(1)}, u32[]{:S(2)}, u32[]{:S(2)}) %collective-permute-start.30) | collective-permute-done | bytes 491552 | tf_op jit(solution)/shard_map/ppermute | solution.py:82
  111.7 19.3 %collective-permute-done.5 = bf16[1920,128]{0,1:T(8,128)(2,1)S(1)} collective-permute-done((bf16[1920,128]{0,1:T(8,128)(2,1)S(1)}, bf16[1920,128]{0,1:T(8,128)(2,1)S(1)}, u32[]{:S(2)}, u32[]{:S(2)}) %collective-permute-start.5) | collective-permute-done | bytes 491552 | tf_op jit(solution)/shard_map/ppermute | solution.py:82
  131.0 1.4 collective-permute-start.29
  132.4 8.7 %collective-permute-done.7 = bf16[1920,128]{0,1:T(8,128)(2,1)S(1)} collective-permute-done((bf16[1920,128]{0,1:T(8,128)(2,1)S(1)}, bf16[1920,128]{0,1:T(8,128)(2,1)S(1)}, u32[]{:S(2)}, u32[]{:S(2)}) %collective-permute-start.7) | collective-permute-done | bytes 491552 | tf_op jit(solution)/shard_map/ppermute | solution.py:82
  141.1 1.4 fusion.57
  142.5 1.6 collective-permute-start.8
  147.0 2.7 collective-permute-start.17
  149.7 13.7 %collective-permute-start.4 = (bf16[1920,128]{0,1:T(8,128)(2,1)S(1)}, bf16[1920,128]{0,1:T(8,128)(2,1)S(1)}, u32[]{:S(2)}, u32[]{:S(2)}) collective-permute-start(bf16[1920,128]{0,1:T(8,128)(2,1)S(1)} %get-tuple-element.5), channel_id=1, source_target_pairs={{0,1},{3,2},{4,5},{7,6},{8,9},{11,10},{12,13},{15,14},{16,17},{19,... | collective-permute-start | bytes 1474568 | tf_op jit(solution)/shard_map/ppermute | solution.py:82
  163.3 1.5 fusion.58
  167.0 1.8 fusion.55
  168.8 1.6 collective-permute-start.33
  170.4 2.7 collective-permute-done.4
  174.3 5.3 %collective-permute-done.9 = bf16[1920,128]{0,1:T(8,128)(2,1)S(1)} collective-permute-done((bf16[1920,128]{0,1:T(8,128)(2,1)S(1)}, bf16[1920,128]{0,1:T(8,128)(2,1)S(1)}, u32[]{:S(2)}, u32[]{:S(2)}) %collective-permute-start.9) | collective-permute-done | bytes 491552 | tf_op jit(solution)/shard_map/ppermute | solution.py:82
  179.9 1.6 collective-permute-start.10
  184.2 2.6 collective-permute-done.35
  186.8 1.9 collective-permute-start.36
  188.8 5.3 %collective-permute-done.10 = bf16[1920,128]{0,1:T(8,128)(2,1)S(1)} collective-permute-done((bf16[1920,128]{0,1:T(8,128)(2,1)S(1)}, bf16[1920,128]{0,1:T(8,128)(2,1)S(1)}, u32[]{:S(2)}, u32[]{:S(2)}) %collective-permute-start.10) | collective-permute-done | bytes 491552 | tf_op jit(solution)/shard_map/ppermute | solution.py:15
  196.5 5.5 %collective-permute-done.36 = bf16[1920,128]{0,1:T(8,128)(2,1)S(1)} collective-permute-done((bf16[1920,128]{0,1:T(8,128)(2,1)S(1)}, bf16[1920,128]{0,1:T(8,128)(2,1)S(1)}, u32[]{:S(2)}, u32[]{:S(2)}) %collective-permute-start.36) | collective-permute-done | bytes 491552 | tf_op jit(solution)/shard_map/ppermute | solution.py:15
  202.1 5.8 %collective-permute-done.13 = bf16[1920,128]{0,1:T(8,128)(2,1)S(1)} collective-permute-done((bf16[1920,128]{0,1:T(8,128)(2,1)S(1)}, bf16[1920,128]{0,1:T(8,128)(2,1)S(1)}, u32[]{:S(2)}, u32[]{:S(2)}) %collective-permute-start.13) | collective-permute-done | bytes 491552 | tf_op jit(solution)/shard_map/ppermute | solution.py:15
  208.7 2.4 fusion.8
  211.2 2.6 fusion.19
  214.6 1.6 fusion.16
  218.2 1.9 rev.7
  220.7 2.4 collective-permute-start.38
  223.1 2.7 fusion.2
  225.8 2.7 fusion.31
  228.8 1.9 rev.6
  232.5 1.8 collective-permute-start.18
  234.4 9.1 %collective-permute-done.18 = bf16[12,48,256]{2,1,0:T(8,128)(2,1)S(1)} collective-permute-done((bf16[12,48,256]{2,1,0:T(8,128)(2,1)S(1)}, bf16[12,48,256]{2,1,0:T(8,128)(2,1)S(1)}, u32[]{:S(2)}, u32[]{:S(2)}) %collective-permute-start.18) | collective-permute-done | bytes 294944 | tf_op jit(solution)/shard_map/ppermute | solution.py:11
  243.7 2.9 %collective-permute-start.39 = (bf16[12,48,256]{2,1,0:T(8,128)(2,1)S(1)}, bf16[12,48,256]{2,1,0:T(8,128)(2,1)S(1)}, u32[]{:S(2)}, u32[]{:S(2)}) collective-permute-start(bf16[12,48,256]{2,1,0:T(8,128)(2,1)S(1)} %get-tuple-element.38), channel_id=1, source_target_pairs={{0,2},{1,3},{2,0},{3,1},{4,6},{5,7},{6,4},{7,5},{8,10},{9,11},{10,... | collective-permute-start | bytes 884744 | tf_op jit(solution)/shard_map/ppermute | solution.py:11
  246.8 18.2 %collective-permute-done.19 = bf16[12,48,256]{2,1,0:T(8,128)(2,1)S(1)} collective-permute-done((bf16[12,48,256]{2,1,0:T(8,128)(2,1)S(1)}, bf16[12,48,256]{2,1,0:T(8,128)(2,1)S(1)}, u32[]{:S(2)}, u32[]{:S(2)}) %collective-permute-start.19) | collective-permute-done | bytes 294944 | tf_op jit(solution)/shard_map/ppermute | solution.py:11
  265.0 6.2 %collective-permute-done.39 = bf16[12,48,256]{2,1,0:T(8,128)(2,1)S(1)} collective-permute-done((bf16[12,48,256]{2,1,0:T(8,128)(2,1)S(1)}, bf16[12,48,256]{2,1,0:T(8,128)(2,1)S(1)}, u32[]{:S(2)}, u32[]{:S(2)}) %collective-permute-start.39) | collective-permute-done | bytes 294944 | tf_op jit(solution)/shard_map/ppermute | solution.py:11
  272.7 1.6 collective-permute-start.42
  279.2 2.9 %collective-permute-done.21 = bf16[4,48,2,1,128]{4,2,1,0,3:T(2,128)(2,1)S(1)} collective-permute-done((bf16[4,48,2,1,128]{4,2,1,0,3:T(2,128)(2,1)S(1)}, bf16[4,48,2,1,128]{4,2,1,0,3:T(2,128)(2,1)S(1)}, u32[]{:S(2)}, u32[]{:S(2)}) %collective-permute-start.21) | collective-permute-done | bytes 98336 | tf_op jit(solution)/shard_map/ppermute | solution.py:15
  286.7 2.1 copy.38
  (154 shorter events, 38.4 us)
Async XLA Ops:
  3.3 55.1 %copy-start.9 = (bf16[2048]{0:T(1024)(128)(2,1)S(1)}, bf16[2048]{0:T(1024)(128)(2,1)}, u32[]{:S(2)}) copy-start(bf16[2048]{0:T(1024)(128)(2,1)} %param.11) | copy-start | bytes 12292
  3.4 59.0 %copy-start.5 = (bf16[2048,512]{1,0:T(8,128)(2,1)S(1)}, bf16[2048,512]{1,0:T(8,128)(2,1)}, u32[]{:S(2)}) copy-start(bf16[2048,512]{1,0:T(8,128)(2,1)} %param.12) | copy-start | bytes 6291460
  3.6 1.5 collective-permute-start.23
  4.4 43.1 %collective-permute-start = (bf16[2048,128]{1,0:T(8,128)(2,1)S(1)}, bf16[2048,128]{1,0:T(8,128)(2,1)S(1)}, u32[]{:S(2)}, u32[]{:S(2)}) collective-permute-start(bf16[2048,128]{1,0:T(8,128)(2,1)S(1)} %get-tuple-element.15), channel_id=1, source_target_pairs={{0,0},{1,4},{2,8},{3,12},{4,1},{5,5},{6,9},{7,13},{8,2},{9,6},{10,... | collective-permute-start | bytes 1572872 | tf_op jit(solution)/shard_map/ppermute | solution.py:109
  5.1 59.6 %collective-permute-start.24 = (bf16[2048,128]{1,0:T(8,128)(2,1)S(1)}, bf16[2048,128]{1,0:T(8,128)(2,1)}, u32[]{:S(2)}, u32[]{:S(2)}) collective-permute-start(bf16[2048,128]{1,0:T(8,128)(2,1)S(1)} %collective-permute-done.23), channel_id=1, source_target_pairs={{0,8},{4,12},{8,0},{12,4},{1,9},{5,13},{9,1},{13,5},{2,10},{6,14},... | collective-permute-start | bytes 1572872 | tf_op jit(solution)/shard_map/ppermute | solution.py:15
  47.5 18.2 %collective-permute-start.1 = (bf16[2048,128]{1,0:T(8,128)(2,1)S(1)}, bf16[2048,128]{1,0:T(8,128)(2,1)}, u32[]{:S(2)}, u32[]{:S(2)}) collective-permute-start(bf16[2048,128]{1,0:T(8,128)(2,1)S(1)} %collective-permute-done), channel_id=1, source_target_pairs={{0,8},{4,12},{8,0},{12,4},{1,9},{5,13},{9,1},{13,5},{2,10},{6,14},... | collective-permute-start | bytes 1572872 | tf_op jit(solution)/shard_map/ppermute | solution.py:15
  58.4 7.3 %collective-permute-start.26 = (bf16[2048,128]{1,0:T(8,128)(2,1)S(1)}, bf16[2048,128]{1,0:T(8,128)(2,1)}, u32[]{:S(2)}, u32[]{:S(2)}) collective-permute-start(bf16[2048,128]{1,0:T(8,128)(2,1)S(1)} %collective-permute-done.23), channel_id=1, source_target_pairs={{0,4},{4,0},{8,12},{12,8},{1,5},{5,1},{9,13},{13,9},{2,6},{6,2},{1... | collective-permute-start | bytes 1572872 | tf_op jit(solution)/shard_map/ppermute | solution.py:15
  58.4 3.9 %collective-permute-start.15 = (bf16[2048]{0:T(1024)(128)(2,1)S(1)}, bf16[2048]{0:T(1024)(128)(2,1)S(1)}, u32[]{:S(2)}, u32[]{:S(2)}) collective-permute-start(bf16[2048]{0:T(1024)(128)(2,1)S(1)} %copy-done.9), channel_id=1, source_target_pairs={{0,0},{1,4},{2,8},{3,12},{4,1},{5,5},{6,9},{7,13},{8,2},{9,6},{10,... | collective-permute-start | bytes 12296 | tf_op jit(solution)/shard_map/ppermute | solution.py:109
  62.8 84.2 %collective-permute-start.16 = (f32[1,512]{1,0:T(1,128)S(1)}, f32[1,512]{1,0:T(1,128)S(1)}, u32[]{:S(2)}, u32[]{:S(2)}) collective-permute-start(f32[1,512]{1,0:T(1,128)S(1)} %fusion.97), channel_id=1, source_target_pairs={{0,4},{4,0},{8,12},{12,8},{1,5},{5,1},{9,13},{13,9},{2,6},{6,2},{1... | collective-permute-start | bytes 6152 | tf_op jit(solution)/shard_map/ppermute | solution.py:15
  64.7 6.9 %collective-permute-start.3 = (bf16[2048,128]{1,0:T(8,128)(2,1)S(1)}, bf16[2048,128]{1,0:T(8,128)(2,1)S(1)}, u32[]{:S(2)}, u32[]{:S(2)}) collective-permute-start(bf16[2048,128]{1,0:T(8,128)(2,1)S(1)} %collective-permute-done), channel_id=1, source_target_pairs={{0,4},{4,0},{8,12},{12,8},{1,5},{5,1},{9,13},{13,9},{2,6},{6,2},{1... | collective-permute-start | bytes 1572872 | tf_op jit(solution)/shard_map/ppermute | solution.py:15
  64.7 9.3 %collective-permute-start.25 = (bf16[2048,128]{1,0:T(8,128)(2,1)}, bf16[2048,128]{1,0:T(8,128)(2,1)S(1)}, u32[]{:S(2)}, u32[]{:S(2)}) collective-permute-start(bf16[2048,128]{1,0:T(8,128)(2,1)} %collective-permute-done.24), channel_id=1, source_target_pairs={{0,4},{4,0},{8,12},{12,8},{1,5},{5,1},{9,13},{13,9},{2,6},{6,2},{1... | collective-permute-start | bytes 1572872 | tf_op jit(solution)/shard_map/ppermute | solution.py:15
  65.7 25.0 %collective-permute-start.2 = (bf16[2048,128]{1,0:T(8,128)(2,1)}, bf16[2048,128]{1,0:T(8,128)(2,1)S(1)}, u32[]{:S(2)}, u32[]{:S(2)}) collective-permute-start(bf16[2048,128]{1,0:T(8,128)(2,1)} %collective-permute-done.1), channel_id=1, source_target_pairs={{0,4},{4,0},{8,12},{12,8},{1,5},{5,1},{9,13},{13,9},{2,6},{6,2},{1... | collective-permute-start | bytes 1572872 | tf_op jit(solution)/shard_map/ppermute | solution.py:15
  71.6 72.5 %copy-start = (f32[256,1920]{1,0:T(8,128)}, f32[256,1920]{1,0:T(8,128)S(1)}, u32[]{:S(2)}) copy-start(f32[256,1920]{1,0:T(8,128)S(1)} %fusion.46) | copy-start | bytes 5898244
  77.5 66.6 %copy-start.4 = (f32[256,1920]{1,0:T(8,128)}, f32[256,1920]{1,0:T(8,128)S(1)}, u32[]{:S(2)}) copy-start(f32[256,1920]{1,0:T(8,128)S(1)} %fusion.42) | copy-start | bytes 5898244
  77.8 21.6 %collective-permute-start.28 = (bf16[1920,128]{0,1:T(8,128)(2,1)S(1)}, bf16[1920,128]{0,1:T(8,128)(2,1)S(1)}, u32[]{:S(2)}, u32[]{:S(2)}) collective-permute-start(bf16[1920,128]{0,1:T(8,128)(2,1)S(1)} %get-tuple-element.12), channel_id=1, source_target_pairs={{0,1},{3,2},{4,5},{7,6},{8,9},{11,10},{12,13},{15,14},{16,17},{19,... | collective-permute-start | bytes 1474568 | tf_op jit(solution)/shard_map/ppermute | solution.py:82
  87.9 22.0 %collective-permute-start.30 = (bf16[1920,128]{0,1:T(8,128)(2,1)S(1)}, bf16[1920,128]{0,1:T(8,128)(2,1)S(1)}, u32[]{:S(2)}, u32[]{:S(2)}) collective-permute-start(bf16[1920,128]{0,1:T(8,128)(2,1)S(1)} %get-tuple-element.11), channel_id=1, source_target_pairs={{0,1},{3,2},{4,5},{7,6},{8,9},{11,10},{12,13},{15,14},{16,17},{19,... | collective-permute-start | bytes 1474568 | tf_op jit(solution)/shard_map/ppermute | solution.py:82
  89.2 75.6 %collective-permute-start.27 = (bf16[1920,128]{0,1:T(8,128)(2,1)S(1)}, bf16[1920,128]{0,1:T(8,128)(2,1)S(1)}, u32[]{:S(2)}, u32[]{:S(2)}) collective-permute-start(bf16[1920,128]{0,1:T(8,128)(2,1)S(1)} %get-tuple-element.10), channel_id=1, source_target_pairs={{0,1},{3,2},{4,5},{7,6},{8,9},{11,10},{12,13},{15,14},{16,17},{19,... | collective-permute-start | bytes 1474568 | tf_op jit(solution)/shard_map/ppermute | solution.py:82
  94.2 46.9 %copy-start.2 = (f32[256,1920]{1,0:T(8,128)}, f32[256,1920]{1,0:T(8,128)S(1)}, u32[]{:S(2)}) copy-start(f32[256,1920]{1,0:T(8,128)S(1)} %fusion.34) | copy-start | bytes 5898244
  94.6 36.3 %collective-permute-start.5 = (bf16[1920,128]{0,1:T(8,128)(2,1)S(1)}, bf16[1920,128]{0,1:T(8,128)(2,1)S(1)}, u32[]{:S(2)}, u32[]{:S(2)}) collective-permute-start(bf16[1920,128]{0,1:T(8,128)(2,1)S(1)} %get-tuple-element.7), channel_id=1, source_target_pairs={{0,1},{3,2},{4,5},{7,6},{8,9},{11,10},{12,13},{15,14},{16,17},{19,... | collective-permute-start | bytes 1474568 | tf_op jit(solution)/shard_map/ppermute | solution.py:82
  99.4 41.7 %collective-permute-start.7 = (bf16[1920,128]{0,1:T(8,128)(2,1)S(1)}, bf16[1920,128]{0,1:T(8,128)(2,1)S(1)}, u32[]{:S(2)}, u32[]{:S(2)}) collective-permute-start(bf16[1920,128]{0,1:T(8,128)(2,1)S(1)} %get-tuple-element.6), channel_id=1, source_target_pairs={{0,1},{3,2},{4,5},{7,6},{8,9},{11,10},{12,13},{15,14},{16,17},{19,... | collective-permute-start | bytes 1474568 | tf_op jit(solution)/shard_map/ppermute | solution.py:82
  111.0 33.1 %collective-permute-start.31 = (bf16[1920,128]{0,1:T(8,128)(2,1)S(1)}, bf16[1920,128]{0,1:T(8,128)(2,1)S(1)}, u32[]{:S(2)}, u32[]{:S(2)}) collective-permute-start(bf16[1920,128]{0,1:T(8,128)(2,1)S(1)} %get-tuple-element.14), channel_id=1, source_target_pairs={{1,2},{2,1},{5,6},{6,5},{9,10},{10,9},{13,14},{14,13},{17,18},{18,... | collective-permute-start | bytes 1474568 | tf_op jit(solution)/shard_map/ppermute | solution.py:82
  131.0 34.7 %collective-permute-start.29 = (bf16[1920,128]{0,1:T(8,128)(2,1)}, bf16[1920,128]{0,1:T(8,128)(2,1)}, u32[]{:S(2)}, u32[]{:S(2)}) collective-permute-start(bf16[1920,128]{0,1:T(8,128)(2,1)} %get-tuple-element.13), channel_id=1, source_target_pairs={{1,2},{2,1},{5,6},{6,5},{9,10},{10,9},{13,14},{14,13},{17,18},{18,... | collective-permute-start | bytes 1474568 | tf_op jit(solution)/shard_map/ppermute | solution.py:82
  142.5 7.2 %collective-permute-start.8 = (bf16[1920,128]{0,1:T(8,128)(2,1)}, bf16[1920,128]{0,1:T(8,128)(2,1)}, u32[]{:S(2)}, u32[]{:S(2)}) collective-permute-start(bf16[1920,128]{0,1:T(8,128)(2,1)} %get-tuple-element.9), channel_id=1, source_target_pairs={{1,2},{2,1},{5,6},{6,5},{9,10},{10,9},{13,14},{14,13},{17,18},{18,... | collective-permute-start | bytes 1474568 | tf_op jit(solution)/shard_map/ppermute | solution.py:82
  145.0 22.0 %collective-permute-start.32 = (bf16[1920,128]{0,1:T(8,128)(2,1)}, bf16[1920,128]{0,1:T(8,128)(2,1)}, u32[]{:S(2)}, u32[]{:S(2)}) collective-permute-start(bf16[1920,128]{0,1:T(8,128)(2,1)} %fusion.52), channel_id=1, source_target_pairs={{2,3},{1,0},{6,7},{5,4},{10,11},{9,8},{14,15},{13,12},{18,19},{17,... | collective-permute-start | bytes 1474568 | tf_op jit(solution)/shard_map/ppermute | solution.py:82
  147.0 34.6 %collective-permute-start.17 = (f32[1,512]{1,0:T(1,128)S(1)}, f32[1,512]{1,0:T(1,128)S(1)}, u32[]{:S(2)}, u32[]{:S(2)}) collective-permute-start(f32[1,512]{1,0:T(1,128)S(1)} %add.256), channel_id=1, source_target_pairs={{0,8},{4,12},{8,0},{12,4},{1,9},{5,13},{9,1},{13,5},{2,10},{6,14},... | collective-permute-start | bytes 6152 | tf_op jit(solution)/shard_map/ppermute | solution.py:15
  149.7 23.4 %collective-permute-start.4 = (bf16[1920,128]{0,1:T(8,128)(2,1)S(1)}, bf16[1920,128]{0,1:T(8,128)(2,1)S(1)}, u32[]{:S(2)}, u32[]{:S(2)}) collective-permute-start(bf16[1920,128]{0,1:T(8,128)(2,1)S(1)} %get-tuple-element.5), channel_id=1, source_target_pairs={{0,1},{3,2},{4,5},{7,6},{8,9},{11,10},{12,13},{15,14},{16,17},{19,... | collective-permute-start | bytes 1474568 | tf_op jit(solution)/shard_map/ppermute | solution.py:82
  164.8 9.5 %collective-permute-start.6 = (bf16[1920,128]{0,1:T(8,128)(2,1)S(1)}, bf16[1920,128]{0,1:T(8,128)(2,1)S(1)}, u32[]{:S(2)}, u32[]{:S(2)}) collective-permute-start(bf16[1920,128]{0,1:T(8,128)(2,1)S(1)} %copy-done.6), channel_id=1, source_target_pairs={{1,2},{2,1},{5,6},{6,5},{9,10},{10,9},{13,14},{14,13},{17,18},{18,... | collective-permute-start | bytes 1474568 | tf_op jit(solution)/shard_map/ppermute | solution.py:82
  165.7 13.9 %collective-permute-start.9 = (bf16[1920,128]{0,1:T(8,128)(2,1)S(1)}, bf16[1920,128]{0,1:T(8,128)(2,1)S(1)}, u32[]{:S(2)}, u32[]{:S(2)}) collective-permute-start(bf16[1920,128]{0,1:T(8,128)(2,1)S(1)} %fusion.58), channel_id=1, source_target_pairs={{2,3},{1,0},{6,7},{5,4},{10,11},{9,8},{14,15},{13,12},{18,19},{17,... | collective-permute-start | bytes 1474568 | tf_op jit(solution)/shard_map/ppermute | solution.py:82
  168.8 14.1 %collective-permute-start.33 = (bf16[1920,128]{0,1:T(8,128)(2,1)S(1)}, bf16[1920,128]{0,1:T(8,128)(2,1)}, u32[]{:S(2)}, u32[]{:S(2)}) collective-permute-start(bf16[1920,128]{0,1:T(8,128)(2,1)S(1)} %fusion.55), channel_id=1, source_target_pairs={{0,16},{16,0},{1,17},{17,1},{2,18},{18,2},{3,19},{19,3},{4,20},{20... | collective-permute-start | bytes 1474568 | tf_op jit(solution)/shard_map/ppermute | solution.py:15
  173.1 13.7 %collective-permute-start.35 = (bf16[1920,128]{0,1:T(8,128)(2,1)S(1)}, bf16[1920,128]{0,1:T(8,128)(2,1)S(1)}, u32[]{:S(2)}, u32[]{:S(2)}) collective-permute-start(bf16[1920,128]{0,1:T(8,128)(2,1)S(1)} %fusion.55), channel_id=1, source_target_pairs={{0,8},{4,12},{8,0},{12,4},{1,9},{5,13},{9,1},{13,5},{2,10},{6,14},... | collective-permute-start | bytes 1474568 | tf_op jit(solution)/shard_map/ppermute | solution.py:15
  179.9 14.2 %collective-permute-start.10 = (bf16[1920,128]{0,1:T(8,128)(2,1)S(1)}, bf16[1920,128]{0,1:T(8,128)(2,1)S(1)}, u32[]{:S(2)}, u32[]{:S(2)}) collective-permute-start(bf16[1920,128]{0,1:T(8,128)(2,1)S(1)} %fusion.61), channel_id=1, source_target_pairs={{0,16},{16,0},{1,17},{17,1},{2,18},{18,2},{3,19},{19,3},{4,20},{20... | collective-permute-start | bytes 1474568 | tf_op jit(solution)/shard_map/ppermute | solution.py:15
  181.6 14.0 %collective-permute-start.12 = (bf16[1920,128]{0,1:T(8,128)(2,1)S(1)}, bf16[1920,128]{0,1:T(8,128)(2,1)S(1)}, u32[]{:S(2)}, u32[]{:S(2)}) collective-permute-start(bf16[1920,128]{0,1:T(8,128)(2,1)S(1)} %fusion.61), channel_id=1, source_target_pairs={{0,8},{4,12},{8,0},{12,4},{1,9},{5,13},{9,1},{13,5},{2,10},{6,14},... | collective-permute-start | bytes 1474568 | tf_op jit(solution)/shard_map/ppermute | solution.py:15
  184.2 24.6 %collective-permute-start.34 = (bf16[1920,256]{0,1:T(8,128)(2,1)S(1)}, bf16[1920,256]{0,1:T(8,128)(2,1)S(1)}, u32[]{:S(2)}, u32[]{:S(2)}) collective-permute-start(bf16[1920,256]{0,1:T(8,128)(2,1)S(1)} %pad_maximum_fusion.1), channel_id=1, source_target_pairs={{0,4},{4,0},{8,12},{12,8},{1,5},{5,1},{9,13},{13,9},{2,6},{6,2},{1... | collective-permute-start | bytes 2949128 | tf_op jit(solution)/shard_map/ppermute | solution.py:15
  186.8 15.2 %collective-permute-start.36 = (bf16[1920,128]{0,1:T(8,128)(2,1)S(1)}, bf16[1920,128]{0,1:T(8,128)(2,1)S(1)}, u32[]{:S(2)}, u32[]{:S(2)}) collective-permute-start(bf16[1920,128]{0,1:T(8,128)(2,1)S(1)} %collective-permute-done.35), channel_id=1, source_target_pairs={{0,16},{16,0},{1,17},{17,1},{2,18},{18,2},{3,19},{19,3},{4,20},{20... | collective-permute-start | bytes 1474568 | tf_op jit(solution)/shard_map/ppermute | solution.py:15
  194.2 19.6 %collective-permute-start.11 = (bf16[1920,256]{0,1:T(8,128)(2,1)S(1)}, bf16[1920,256]{0,1:T(8,128)(2,1)S(1)}, u32[]{:S(2)}, u32[]{:S(2)}) collective-permute-start(bf16[1920,256]{0,1:T(8,128)(2,1)S(1)} %pad_maximum_fusion), channel_id=1, source_target_pairs={{0,4},{4,0},{8,12},{12,8},{1,5},{5,1},{9,13},{13,9},{2,6},{6,2},{1... | collective-permute-start | bytes 2949128 | tf_op jit(solution)/shard_map/ppermute | solution.py:15
  194.3 13.6 %collective-permute-start.13 = (bf16[1920,128]{0,1:T(8,128)(2,1)S(1)}, bf16[1920,128]{0,1:T(8,128)(2,1)S(1)}, u32[]{:S(2)}, u32[]{:S(2)}) collective-permute-start(bf16[1920,128]{0,1:T(8,128)(2,1)S(1)} %collective-permute-done.10), channel_id=1, source_target_pairs={{0,8},{4,12},{8,0},{12,4},{1,9},{5,13},{9,1},{13,5},{2,10},{6,14},... | collective-permute-start | bytes 1474568 | tf_op jit(solution)/shard_map/ppermute | solution.py:15
  202.1 14.2 %collective-permute-start.37 = (bf16[1920,256]{0,1:T(8,128)(2,1)S(1)}, bf16[1920,256]{0,1:T(8,128)(2,1)S(1)}, u32[]{:S(2)}, u32[]{:S(2)}) collective-permute-start(bf16[1920,256]{0,1:T(8,128)(2,1)S(1)} %constant_dynamic-update-slice_fusion.2), channel_id=1, source_target_pairs={{0,4},{4,0},{8,12},{12,8},{1,5},{5,1},{9,13},{13,9},{2,6},{6,2},{1... | collective-permute-start | bytes 2949128 | tf_op jit(solution)/shard_map/ppermute | solution.py:15
  208.7 14.3 %collective-permute-start.14 = (bf16[1920,256]{0,1:T(8,128)(2,1)}, bf16[1920,256]{0,1:T(8,128)(2,1)}, u32[]{:S(2)}, u32[]{:S(2)}) collective-permute-start(bf16[1920,256]{0,1:T(8,128)(2,1)} %constant_dynamic-update-slice_fusion), channel_id=1, source_target_pairs={{0,4},{4,0},{8,12},{12,8},{1,5},{5,1},{9,13},{13,9},{2,6},{6,2},{1... | collective-permute-start | bytes 2949128 | tf_op jit(solution)/shard_map/ppermute | solution.py:15
  220.7 13.7 %collective-permute-start.38 = (bf16[12,48,256]{2,1,0:T(8,128)(2,1)S(1)}, bf16[12,48,256]{2,1,0:T(8,128)(2,1)S(1)}, u32[]{:S(2)}, u32[]{:S(2)}) collective-permute-start(bf16[12,48,256]{2,1,0:T(8,128)(2,1)S(1)} %reshape.163), channel_id=1, source_target_pairs={{0,1},{1,2},{2,3},{3,0},{4,5},{5,6},{6,7},{7,4},{8,9},{9,10},{10,1... | collective-permute-start | bytes 884744 | tf_op jit(solution)/shard_map/ppermute | solution.py:11
  232.5 11.0 %collective-permute-start.18 = (bf16[12,48,256]{2,1,0:T(8,128)(2,1)S(1)}, bf16[12,48,256]{2,1,0:T(8,128)(2,1)S(1)}, u32[]{:S(2)}, u32[]{:S(2)}) collective-permute-start(bf16[12,48,256]{2,1,0:T(8,128)(2,1)S(1)} %reshape.160), channel_id=1, source_target_pairs={{0,1},{1,2},{2,3},{3,0},{4,5},{5,6},{6,7},{7,4},{8,9},{9,10},{10,1... | collective-permute-start | bytes 884744 | tf_op jit(solution)/shard_map/ppermute | solution.py:11
  243.6 21.4 %collective-permute-start.19 = (bf16[12,48,256]{2,1,0:T(8,128)(2,1)S(1)}, bf16[12,48,256]{2,1,0:T(8,128)(2,1)S(1)}, u32[]{:S(2)}, u32[]{:S(2)}) collective-permute-start(bf16[12,48,256]{2,1,0:T(8,128)(2,1)S(1)} %get-tuple-element.37), channel_id=1, source_target_pairs={{0,2},{1,3},{2,0},{3,1},{4,6},{5,7},{6,4},{7,5},{8,10},{9,11},{10,... | collective-permute-start | bytes 884744 | tf_op jit(solution)/shard_map/ppermute | solution.py:11
  243.7 27.5 %collective-permute-start.39 = (bf16[12,48,256]{2,1,0:T(8,128)(2,1)S(1)}, bf16[12,48,256]{2,1,0:T(8,128)(2,1)S(1)}, u32[]{:S(2)}, u32[]{:S(2)}) collective-permute-start(bf16[12,48,256]{2,1,0:T(8,128)(2,1)S(1)} %get-tuple-element.38), channel_id=1, source_target_pairs={{0,2},{1,3},{2,0},{3,1},{4,6},{5,7},{6,4},{7,5},{8,10},{9,11},{10,... | collective-permute-start | bytes 884744 | tf_op jit(solution)/shard_map/ppermute | solution.py:11
  272.0 3.9 %collective-permute-start.40 = (bf16[4,48,2,1,128]{4,2,1,0,3:T(2,128)(2,1)S(1)}, bf16[4,48,2,1,128]{4,2,1,0,3:T(2,128)(2,1)S(1)}, u32[]{:S(2)}, u32[]{:S(2)}) collective-permute-start(bf16[4,48,2,1,128]{4,2,1,0,3:T(2,128)(2,1)S(1)} %squeeze.61), channel_id=1, source_target_pairs={{0,4},{4,0},{8,12},{12,8},{1,5},{5,1},{9,13},{13,9},{2,6},{6,2},{1... | collective-permute-start | bytes 294920 | tf_op jit(solution)/shard_map/ppermute | solution.py:15
  272.2 5.7 %collective-permute-start.41 = (bf16[4,48,2,1,128]{4,2,1,0,3:T(2,128)(2,1)S(1)}, bf16[4,48,2,1,128]{4,2,1,0,3:T(2,128)(2,1)S(1)}, u32[]{:S(2)}, u32[]{:S(2)}) collective-permute-start(bf16[4,48,2,1,128]{4,2,1,0,3:T(2,128)(2,1)S(1)} %squeeze.62), channel_id=1, source_target_pairs={{0,8},{4,12},{8,0},{12,4},{1,9},{5,13},{9,1},{13,5},{2,10},{6,14},... | collective-permute-start | bytes 294920 | tf_op jit(solution)/shard_map/ppermute | solution.py:15
  272.7 6.5 %collective-permute-start.42 = (bf16[4,48,2,1,128]{4,2,1,0,3:T(2,128)(2,1)S(1)}, bf16[4,48,2,1,128]{4,2,1,0,3:T(2,128)(2,1)S(1)}, u32[]{:S(2)}, u32[]{:S(2)}) collective-permute-start(bf16[4,48,2,1,128]{4,2,1,0,3:T(2,128)(2,1)S(1)} %squeeze.63), channel_id=1, source_target_pairs={{0,12},{4,8},{8,4},{12,0},{1,13},{5,9},{9,5},{13,1},{2,14},{6,10},... | collective-permute-start | bytes 294920 | tf_op jit(solution)/shard_map/ppermute | solution.py:15
  274.9 4.2 %collective-permute-start.20 = (bf16[4,48,2,1,128]{4,2,1,0,3:T(2,128)(2,1)S(1)}, bf16[4,48,2,1,128]{4,2,1,0,3:T(2,128)(2,1)S(1)}, u32[]{:S(2)}, u32[]{:S(2)}) collective-permute-start(bf16[4,48,2,1,128]{4,2,1,0,3:T(2,128)(2,1)S(1)} %squeeze.57), channel_id=1, source_target_pairs={{0,4},{4,0},{8,12},{12,8},{1,5},{5,1},{9,13},{13,9},{2,6},{6,2},{1... | collective-permute-start | bytes 294920 | tf_op jit(solution)/shard_map/ppermute | solution.py:15
  275.4 6.6 %collective-permute-start.21 = (bf16[4,48,2,1,128]{4,2,1,0,3:T(2,128)(2,1)S(1)}, bf16[4,48,2,1,128]{4,2,1,0,3:T(2,128)(2,1)S(1)}, u32[]{:S(2)}, u32[]{:S(2)}) collective-permute-start(bf16[4,48,2,1,128]{4,2,1,0,3:T(2,128)(2,1)S(1)} %squeeze.58), channel_id=1, source_target_pairs={{0,8},{4,12},{8,0},{12,4},{1,9},{5,13},{9,1},{13,5},{2,10},{6,14},... | collective-permute-start | bytes 294920 | tf_op jit(solution)/shard_map/ppermute | solution.py:15
  275.9 7.4 %collective-permute-start.22 = (bf16[4,48,2,1,128]{4,2,1,0,3:T(2,128)(2,1)S(1)}, bf16[4,48,2,1,128]{4,2,1,0,3:T(2,128)(2,1)S(1)}, u32[]{:S(2)}, u32[]{:S(2)}) collective-permute-start(bf16[4,48,2,1,128]{4,2,1,0,3:T(2,128)(2,1)S(1)} %squeeze.59), channel_id=1, source_target_pairs={{0,12},{4,8},{8,4},{12,0},{1,13},{5,9},{9,5},{13,1},{2,14},{6,10},... | collective-permute-start | bytes 294920 | tf_op jit(solution)/shard_map/ppermute | solution.py:15
  (13 other events, 153.2 us)

commit v2 on v1

--- a/solution.py
+++ b/solution.py
@@ -71,25 +71,6 @@
     return gathered_rows[None, None]
 
 
-block_order = ((3, 2, 1, 0), (3, 2, 0, 1), (0, 1, 3, 2), (0, 1, 2, 3))
-inward = [(0, 1), (3, 2)]
-across = [(1, 2), (2, 1)]
-outward = [(2, 3), (1, 0)]
-
-
-def sum_over_planes(block):
-    def send(value, pairs):
-        return lax.ppermute(value.astype(jnp.bfloat16), "head", pairs).astype(jnp.float32)
-
-    first_in = send(block(0), inward)
-    second_in = send(block(1), inward)
-    third_in = send(block(2), inward)
-    first_across = send(block(0) + first_in, across)
-    second_across = send(block(1) + second_in, across)
-    first_out = send(block(2) + first_across, outward)
-    return (block(3) + third_in + second_across + first_out).astype(jnp.bfloat16)
-
-
 def product_plan(
     features, proj_weight, proj_bias, kv_weight, key_gain, tile_map, tile_count, decode_owner
 ):
@@ -97,18 +78,18 @@
     token_rows = tile_slots * shard_len
     depth = proj_weight.shape[0]
     layers, head_dim = key_gain.shape
+    width = layers * head_dim
     most_tiles = tile_map.shape[1]
     group, tile, head = (lax.axis_index(name) for name in ("groups", "tile", "head"))
+    first_core, first_chip = tile % 2 == 0, tile < 2
+    at_end = (head == 0) | (head == 3)
     feature_rows = features.reshape(token_rows, feature_width)
     feature_parts = [
         lax.dynamic_slice_in_dim(feature_rows, (tile ^ r) * depth, depth, axis=1) for r in range(4)
     ]
+
     flip = [(t * 4 + h, h * 4 + t) for t in range(4) for h in range(4)]
-
-    def turned(shard):
-        return lax.ppermute(shard, ("tile", "head"), flip)
-
-    bias_rows = turned(proj_bias)
+    bias_rows = lax.ppermute(proj_bias, ("tile", "head"), flip)
     bias_part = add_columns(bias_rows[None], kv_weight)
     bias_part = bias_part + swapped(bias_part, "tile", 1)
     bias_part = bias_part + swapped(bias_part, "tile", 2)
@@ -120,46 +101,72 @@
     selector = jnp.einsum("rd,rjs->djs", owned_by, matched.astype(jnp.float32))
     selector = selector.astype(jnp.bfloat16).reshape(4 * most_tiles, tile_slots)
 
-    order = jnp.array(block_order, jnp.int32)[head]
-    per_head = kv_weight.reshape(-1, 2, layers, 2, head_dim)
-    mine = lax.dynamic_index_in_dim(per_head, group, axis=1, keepdims=False)
-    width = layers * head_dim
+    rounds = [
+        [
+            (t * 4 + h, (t // 2 * 2 + (h ^ h // 2) % 2) * 4 + t % 2 + 2 * ((h // 2) ^ j))
+            for t in range(4)
+            for h in range(4)
+        ]
+        for j in range(2)
+    ]
+    half = kv_weight.shape[0] // 2
     routed = []
     for part in range(2):
-        block_0 = turned(mine[:, :, part].reshape(-1, width))
-        block_2 = swapped(block_0, "tile", 2)
-        near = jnp.concatenate([block_0, swapped(block_0, "tile", 1)], axis=1)
-        far = jnp.concatenate([block_2, swapped(block_2, "tile", 1)], axis=1)
-        near_product = add_columns(proj_weight, near)
-        far_product = add_columns(proj_weight, far)
+        column = (group * 2 + part) * head_dim
+        mine = lax.dynamic_slice_in_dim(kv_weight, column, head_dim, axis=1)
+        stays = lax.dynamic_slice_in_dim(mine, tile // 2 * half, half, axis=0)
+        leaves = lax.dynamic_slice_in_dim(mine, half - tile // 2 * half, half, axis=0)
+        comes = swapped(leaves, "tile", 2)
+        pieces = []
+        for j in range(2):
+            own_rows = tile // 2 == (head // 2) ^ j
+            pieces.append(
+                lax.ppermute(jnp.where(own_rows, stays, comes), ("tile", "head"), rounds[j])
+            )
+        near_half = jnp.concatenate(pieces, axis=1)
+        other_half = swapped(near_half, "tile", 2)
+        near = jnp.concatenate(
+            [
+                jnp.where(first_chip, near_half, other_half),
+                jnp.where(first_chip, other_half, near_half),
+            ],
+            axis=0,
+        )
+        far = swapped(near, "tile", 1)
+        far_leaves = at_end == first_core
+        outer = add_columns(proj_weight, jnp.where(far_leaves, far, near)).astype(jnp.bfloat16)
+        pair_sum = add_columns(proj_weight, jnp.where(far_leaves, near, far))
+        pair_sum = pair_sum + swapped(outer, "head", 1).astype(jnp.float32)
+        mirrored = swapped(pair_sum[:, width:].astype(jnp.bfloat16), "head", 3)
+        own = (pair_sum[:, :width] + mirrored.astype(jnp.float32)).astype(jnp.bfloat16)
 
-        def block(k):
-            which = order[k] ^ tile
-            from_near = lax.dynamic_slice_in_dim(near_product, which % 2 * width, width, axis=1)
-            from_far = lax.dynamic_slice_in_dim(far_product, which % 2 * width, width, axis=1)
-            return jnp.where(which >= 2, from_far, from_near)
-
-        own = sum_over_planes(block)
         across_x, across_y = swapped(own, "tile", 2), swapped(own, "groups", 1)
         diagonal = swapped(across_y, "tile", 2) if part == 0 else swapped(across_x, "groups", 1)
-        rows_0 = jnp.concatenate([own, across_y], axis=1)
-        rows_2 = jnp.concatenate([across_x, diagonal], axis=1)
+
+        def both_heads(ours, theirs):
+            left, right = jnp.where(group == 0, ours, theirs), jnp.where(group == 0, theirs, ours)
+            return lax.optimization_barrier(jnp.concatenate([left, right], axis=1))
+
+        rows_0, rows_2 = both_heads(own, across_y), both_heads(across_x, diagonal)
         rows = [rows_0, swapped(rows_0, "tile", 1), rows_2, swapped(rows_2, "tile", 1)]
         total = sum(add_columns(feature_parts[r], rows[r]) for r in range(4))
-        total = total.reshape(token_rows, 2, layers, head_dim)
-        total = jnp.where(group == 0, total, total[:, ::-1]) + bias_part[None, :, :, part]
-        if part == 0:
-            inv_rms = lax.rsqrt(jnp.mean(total * total, axis=-1, keepdims=True) + eps_norm)
-            total = total * inv_rms * key_gain[None, None]
-        rolled = total.astype(jnp.bfloat16).reshape(tile_slots, shard_len, 2 * width)
+        finished = []
+        for k in range(2):
+            entries = total[:, k * width : (k + 1) * width].reshape(token_rows, layers, head_dim)
+            entries = entries + bias_part[k, :, part][None]
+            if part == 0:
+                squares = jnp.mean(entries * entries, axis=-1, keepdims=True)
+                entries = entries * lax.rsqrt(squares + eps_norm) * key_gain[None]
+            finished.append(entries.reshape(token_rows, width).astype(jnp.bfloat16))
+        rolled = jnp.concatenate(finished, axis=1).reshape(tile_slots, shard_len, 2 * width)
         for stride in (1, 2):
             odd = (turn_of // stride % 2 == 1)[:, None, None]
             rolled = jnp.where(odd, shifted_2(rolled, "head", stride), rolled)
         outgoing = add_columns(selector, rolled.reshape(tile_slots, -1)).astype(jnp.bfloat16)
         outgoing = outgoing.reshape(4, most_tiles, shard_len, 2, layers, head_dim)
         arrived = [outgoing[0]] + [swapped(outgoing[r], "tile", r) for r in (1, 2, 3)]
-        even = [jnp.where(tile % 2 == 0, arrived[r], arrived[r ^ 1]) for r in range(4)]
-        ranked = [jnp.where(tile < 2, even[r], even[r ^ 2]) for r in range(4)]
+        even = [jnp.where(first_core, arrived[r], arrived[r ^ 1]) for r in range(4)]
+        ranked = [jnp.where(first_chip, even[r], even[r ^ 2]) for r in range(4)]
         routed.append(jnp.stack(ranked, axis=1))
     cache = jnp.stack(routed, axis=-2)
     return cache.reshape(1, 1, most_tiles * 4 * shard_len, 4 * layers, head_dim)

time: 290 us -> 251 us (0.87)
  starting transfers between devices: 120 us -> 66.5 us
  waiting for transfers between devices: 105 us -> 139 us
  local copies, waits for them, and re-layouts: 15.2 us -> 5.52 us
  other arithmetic: 14.5 us -> 11.3 us
  matrix products: 30.6 us -> 27.7 us
    ppermute x24 -> x28, waiting for transfers between devices: 25.7 us -> 89.5 us  [swapped(): lax.ppermute(shard, axis, [(i, i ^ bit) for i in range(lax.axis_size(axis...]
    ppermute x15 -> x5, waiting for transfers between devices: 45.5 us -> 13.1 us  [the longest x4 13.1 us: product_plan(): lax.ppermute(jnp.where(own_rows, stays, comes), ('tile', 'head'), rounds[j])]
    ppermute x15 -> x5, starting transfers between devices: 41.6 us -> 9.87 us  [the longest x4 9.04 us: product_plan(): lax.ppermute(jnp.where(own_rows, stays, comes), ('tile', 'head'), rounds[j])]
    ppermute x24 -> x28, starting transfers between devices: 71.6 us -> 46.4 us  [swapped(): lax.ppermute(shard, axis, [(i, i ^ bit) for i in range(lax.axis_size(axis...]
    convert_element_type x10 -> x4, other arithmetic: 8.75 us -> 0.44 us  [the longest x2 0.27 us: product_plan(): finished.append(entries.reshape(token_rows, width).astype(jnp.bfloat16))]
    select_n x0 -> x7, other arithmetic: none -> 4.09 us  [the longest x2 1.83 us: product_plan(): jnp.where(own_rows, stays, comes)]
    rev x2 -> x0, local copies, waits for them, and re-layouts: 3.78 us -> none  [product_plan(): total[:, ::-1]]
    reshape x5 -> x0, local copies, waits for them, and re-layouts: 3.54 us -> none  [the longest x1 2.55 us: product_plan(): per_head = kv_weight.reshape(-1, 2, layers, 2, head_dim)]
  transfers between devices with their start and end apart: 43 -> 37, of which waited for: 18 -> 22; matrix products, arithmetic and copies ran while one was open for 17% -> 13% of each run, Pallas kernels for 0% -> 0%
where the time goes in v2:
time: 251 us
  waiting for transfers between devices  139 us (55%)
  starting transfers between devices  66.5 us (26%)
  matrix products  27.7 us (11%)
  other arithmetic  11.3 us (5%)
  local copies, waits for them, and re-layouts  5.52 us (2%)
    ppermute x28, waiting for transfers between devices, swapped(): lax.ppermute(shard, axis, [(i, i ^ bit) for i in range(lax.axis_size(axis...  89.5 us
    ppermute x28, starting transfers between devices, swapped(): lax.ppermute(shard, axis, [(i, i ^ bit) for i in range(lax.axis_size(axis...  46.4 us
    ppermute x4, waiting for transfers between devices, shifted_2(): lax.ppermute(shard, axis, [(i, (i + by) % count) for i in range(count)])  36.1 us
    dot_general x15, matrix products, add_columns(): return jnp.dot(operand, portion, preferred_element_type=jnp.float32)  27.5 us
    ppermute x4, waiting for transfers between devices, product_plan(): lax.ppermute(jnp.where(own_rows, stays, comes), ('tile', 'head'), rounds[j])  13.1 us
    ppermute x4, starting transfers between devices, shifted_2(): lax.ppermute(shard, axis, [(i, (i + by) % count) for i in range(count)])  10.3 us
    ppermute x4, starting transfers between devices, product_plan(): lax.ppermute(jnp.where(own_rows, stays, comes), ('tile', 'head'), rounds[j])  9.04 us
  transfers between devices with their start and end apart: 37, of which 22 were waited for; matrix products, arithmetic and copies ran while one was open for 13% of the time, Pallas kernels for 0%

profile of v2, /device:TPU:0, one launch (start us, length us, event | category | flops | bytes accessed | tf_op | source)
XLA Modules:
  0.0 250.6 jit_solution(14645570261724667880)
XLA Ops:
  0.0 1.4 dynamic_slice.28
  1.4 3.0 %collective-permute-start = (bf16[1024,128]{1,0:T(8,128)(2,1)S(1)}, bf16[1024,128]{1,0:T(8,128)(2,1)S(1)}, u32[]{:S(2)}, u32[]{:S(2)}) collective-permute-start(bf16[1024,128]{1,0:T(8,128)(2,1)S(1)} %dynamic_slice.28), channel_id=1, source_target_pairs={{0,8},{4,12},{8,0},{12,4},{1,9},{5,13},{9,1},{13,5},{2,10},{6,14},... | collective-permute-start | bytes 786440 | tf_op jit(solution)/shard_map/ppermute | solution.py:15
  4.4 6.3 %collective-permute-done = bf16[1024,128]{1,0:T(8,128)(2,1)S(1)} collective-permute-done((bf16[1024,128]{1,0:T(8,128)(2,1)S(1)}, bf16[1024,128]{1,0:T(8,128)(2,1)S(1)}, u32[]{:S(2)}, u32[]{:S(2)}) %collective-permute-start) | collective-permute-done | bytes 262176 | tf_op jit(solution)/shard_map/ppermute | solution.py:15
  10.7 1.6 broadcast_select_fusion.17
  12.3 1.8 collective-permute-start.20
  14.8 3.9 %collective-permute-start.2 = (bf16[1024,128]{1,0:T(8,128)(2,1)S(1)}, bf16[1024,128]{1,0:T(8,128)(2,1)S(1)}, u32[]{:S(2)}, u32[]{:S(2)}) collective-permute-start(bf16[1024,128]{1,0:T(8,128)(2,1)S(1)} %get-tuple-element.7), channel_id=1, source_target_pairs={{0,2},{1,6},{2,4},{3,0},{4,3},{5,7},{6,5},{7,1},{8,10},{9,14},{10,... | collective-permute-start | bytes 786440 | tf_op jit(solution)/shard_map/ppermute | solution.py:124
  18.7 1.2 collective-permute-done.20
  20.8 3.8 %collective-permute-start.22 = (bf16[1024,128]{1,0:T(8,128)(2,1)S(1)}, bf16[1024,128]{1,0:T(8,128)(2,1)S(1)}, u32[]{:S(2)}, u32[]{:S(2)}) collective-permute-start(bf16[1024,128]{1,0:T(8,128)(2,1)S(1)} %get-tuple-element.9), channel_id=1, source_target_pairs={{0,2},{1,6},{2,4},{3,0},{4,3},{5,7},{6,5},{7,1},{8,10},{9,14},{10,... | collective-permute-start | bytes 786440 | tf_op jit(solution)/shard_map/ppermute | solution.py:124
  24.7 6.9 %collective-permute-done.2 = bf16[1024,128]{1,0:T(8,128)(2,1)S(1)} collective-permute-done((bf16[1024,128]{1,0:T(8,128)(2,1)S(1)}, bf16[1024,128]{1,0:T(8,128)(2,1)S(1)}, u32[]{:S(2)}, u32[]{:S(2)}) %collective-permute-start.2) | collective-permute-done | bytes 262176 | tf_op jit(solution)/shard_map/ppermute | solution.py:124
  31.8 6.2 %collective-permute-done.22 = bf16[1024,128]{1,0:T(8,128)(2,1)S(1)} collective-permute-done((bf16[1024,128]{1,0:T(8,128)(2,1)S(1)}, bf16[1024,128]{1,0:T(8,128)(2,1)S(1)}, u32[]{:S(2)}, u32[]{:S(2)}) %collective-permute-start.22) | collective-permute-done | bytes 262176 | tf_op jit(solution)/shard_map/ppermute | solution.py:124
  38.7 2.3 collective-permute-done.3
  41.0 12.1 %collective-permute-done.23 = bf16[1024,256]{1,0:T(8,128)(2,1)} collective-permute-done((bf16[1024,256]{1,0:T(8,128)(2,1)S(1)}, bf16[1024,256]{1,0:T(8,128)(2,1)}, u32[]{:S(2)}, u32[]{:S(2)}) %collective-permute-start.23) | collective-permute-done | bytes 524320 | tf_op jit(solution)/shard_map/ppermute | solution.py:15
  53.1 1.7 broadcast_select_fusion.1
  54.7 1.1 pad_maximum_fusion.1
  55.9 4.6 %collective-permute-start.24 = (bf16[2048,256]{1,0:T(8,128)(2,1)}, bf16[2048,256]{1,0:T(8,128)(2,1)}, u32[]{:S(2)}, u32[]{:S(2)}) collective-permute-start(bf16[2048,256]{1,0:T(8,128)(2,1)} %pad_maximum_fusion.1), channel_id=1, source_target_pairs={{0,4},{4,0},{8,12},{12,8},{1,5},{5,1},{9,13},{13,9},{2,6},{6,2},{1... | collective-permute-start | bytes 3145736 | tf_op jit(solution)/shard_map/ppermute | solution.py:15
  62.4 4.1 %collective-permute-start.4 = (bf16[2048,256]{1,0:T(8,128)(2,1)}, bf16[2048,256]{1,0:T(8,128)(2,1)}, u32[]{:S(2)}, u32[]{:S(2)}) collective-permute-start(bf16[2048,256]{1,0:T(8,128)(2,1)} %pad_maximum_fusion), channel_id=1, source_target_pairs={{0,4},{4,0},{8,12},{12,8},{1,5},{5,1},{9,13},{13,9},{2,6},{6,2},{1... | collective-permute-start | bytes 3145736 | tf_op jit(solution)/shard_map/ppermute | solution.py:15
  66.9 1.9 collective-permute-done.13
  68.8 3.3 %collective-permute-start.14 = (f32[1,512]{1,0:T(1,128)S(1)}, f32[1,512]{1,0:T(1,128)S(1)}, u32[]{:S(2)}, u32[]{:S(2)}) collective-permute-start(f32[1,512]{1,0:T(1,128)S(1)} %add.192), channel_id=1, source_target_pairs={{0,8},{4,12},{8,0},{12,4},{1,9},{5,13},{9,1},{13,5},{2,10},{6,14},... | collective-permute-start | bytes 6152 | tf_op jit(solution)/shard_map/ppermute | solution.py:15
  72.1 7.2 %fusion.3 = bf16[1920,256]{0,1:T(8,128)(2,1)} fusion(bf16[1920,2048]{1,0:T(8,128)(2,1)} %param.9, bf16[2048,256]{1,0:T(8,128)(2,1)} %collective-permute-done.24, pred[]{:T(512)S(6)} %eq.94, bf16[1024,256]{1,0:T(8,128)(2,1)} %copy-done.3, bf16[1024,256]{1,0:T(8,128)(2,1)} %copy-done.1), kind=kOutput, calls=%fused_computation.9 | convolution fusion | flops 2016378880 | bytes 10944513 | tf_op jit(solution)/shard_map/dot_general | solution.py:19
  79.5 4.7 %fusion.2 = bf16[1920,256]{0,1:T(8,128)(2,1)} fusion(bf16[1920,2048]{1,0:T(8,128)(2,1)S(1)} %bitcast.110, bf16[2048,256]{1,0:T(8,128)(2,1)} %collective-permute-done.4, pred[]{:T(512)S(6)} %eq.94, bf16[1024,256]{1,0:T(8,128)(2,1)S(1)} %get-tuple-element.56, bf16[1024,256]{1,0:T(8,128)(2,1)S(1)} %get-tuple-element.57), kind=kOutput, calls=%fused_computation.8 | convolution fusion | flops 2016378880 | bytes 10944513 | tf_op jit(solution)/shard_map/dot_general | solution.py:19
  84.9 19.4 %collective-permute-done.25 = bf16[1920,256]{0,1:T(8,128)(2,1)} collective-permute-done((bf16[1920,256]{0,1:T(8,128)(2,1)}, bf16[1920,256]{0,1:T(8,128)(2,1)}, u32[]{:S(2)}, u32[]{:S(2)}) %collective-permute-start.25) | collective-permute-done | bytes 983072 | tf_op jit(solution)/shard_map/ppermute | solution.py:15
  104.4 5.8 %fusion.1 = f32[1920,256]{0,1:T(8,128)S(1)} fusion(bf16[1920,2048]{1,0:T(8,128)(2,1)} %param.9, bf16[1920,256]{0,1:T(8,128)(2,1)} %collective-permute-done.25, bf16[2048,256]{1,0:T(8,128)(2,1)} %collective-permute-done.24, pred[]{:T(512)S(6)} %eq.94, bf16[1024,256]{1,0:T(8,128)(2,1)S(1)} %copy-done.4, bf16[1024,256]{1,0:T(8,128)(2,1)S(1)} %copy-done.2), kind=kOutput, calls=%fused_computation.5 | convolution fusion | flops 2016870400 | bytes 12910593 | tf_op jit(solution)/shard_map/dot_general | solution.py:19
  110.3 2.2 collective-permute-start.26
  112.5 11.6 %collective-permute-done.5 = bf16[1920,256]{0,1:T(8,128)(2,1)S(1)} collective-permute-done((bf16[1920,256]{0,1:T(8,128)(2,1)}, bf16[1920,256]{0,1:T(8,128)(2,1)S(1)}, u32[]{:S(2)}, u32[]{:S(2)}) %collective-permute-start.5) | collective-permute-done | bytes 983072 | tf_op jit(solution)/shard_map/ppermute | solution.py:15
  124.1 2.4 fusion
  126.6 2.8 %collective-permute-start.6 = (bf16[1920,128]{0,1:T(8,128)(2,1)S(1)}, bf16[1920,128]{0,1:T(8,128)(2,1)S(1)}, u32[]{:S(2)}, u32[]{:S(2)}) collective-permute-start(bf16[1920,128]{0,1:T(8,128)(2,1)S(1)} %slice.139), channel_id=1, source_target_pairs={{0,3},{1,2},{2,1},{3,0},{4,7},{5,6},{6,5},{7,4},{8,11},{9,10},{10,... | collective-permute-start | bytes 1474568 | tf_op jit(solution)/shard_map/ppermute | solution.py:15
  129.4 7.9 %collective-permute-done.26 = bf16[1920,128]{0,1:T(8,128)(2,1)S(1)} collective-permute-done((bf16[1920,128]{0,1:T(8,128)(2,1)S(1)}, bf16[1920,128]{0,1:T(8,128)(2,1)S(1)}, u32[]{:S(2)}, u32[]{:S(2)}) %collective-permute-start.26) | collective-permute-done | bytes 491552 | tf_op jit(solution)/shard_map/ppermute | solution.py:15
  137.4 1.5 collective-permute-start.27
  138.9 3.9 %collective-permute-start.29 = (bf16[1920,128]{0,1:T(8,128)(2,1)S(1)}, bf16[1920,128]{0,1:T(8,128)(2,1)S(1)}, u32[]{:S(2)}, u32[]{:S(2)}) collective-permute-start(bf16[1920,128]{0,1:T(8,128)(2,1)S(1)} %fusion.46), channel_id=1, source_target_pairs={{0,8},{4,12},{8,0},{12,4},{1,9},{5,13},{9,1},{13,5},{2,10},{6,14},... | collective-permute-start | bytes 1474568 | tf_op jit(solution)/shard_map/ppermute | solution.py:15
  142.8 4.6 %collective-permute-done.6 = bf16[1920,128]{0,1:T(8,128)(2,1)S(1)} collective-permute-done((bf16[1920,128]{0,1:T(8,128)(2,1)S(1)}, bf16[1920,128]{0,1:T(8,128)(2,1)S(1)}, u32[]{:S(2)}, u32[]{:S(2)}) %collective-permute-start.6) | collective-permute-done | bytes 491552 | tf_op jit(solution)/shard_map/ppermute | solution.py:15
  147.5 1.5 collective-permute-start.7
  149.0 5.5 %collective-permute-start.9 = (bf16[1920,128]{0,1:T(8,128)(2,1)S(1)}, bf16[1920,128]{0,1:T(8,128)(2,1)S(1)}, u32[]{:S(2)}, u32[]{:S(2)}) collective-permute-start(bf16[1920,128]{0,1:T(8,128)(2,1)S(1)} %fusion.47), channel_id=1, source_target_pairs={{0,8},{4,12},{8,0},{12,4},{1,9},{5,13},{9,1},{13,5},{2,10},{6,14},... | collective-permute-start | bytes 1474568 | tf_op jit(solution)/shard_map/ppermute | solution.py:15
  155.5 6.2 %collective-permute-done.7 = bf16[1920,128]{0,1:T(8,128)(2,1)S(1)} collective-permute-done((bf16[1920,128]{0,1:T(8,128)(2,1)S(1)}, bf16[1920,128]{0,1:T(8,128)(2,1)S(1)}, u32[]{:S(2)}, u32[]{:S(2)}) %collective-permute-start.7) | collective-permute-done | bytes 491552 | tf_op jit(solution)/shard_map/ppermute | solution.py:15
  162.0 5.6 %collective-permute-start.10 = (bf16[1920,128]{0,1:T(8,128)(2,1)S(1)}, bf16[1920,128]{0,1:T(8,128)(2,1)S(1)}, u32[]{:S(2)}, u32[]{:S(2)}) collective-permute-start(bf16[1920,128]{0,1:T(8,128)(2,1)S(1)} %collective-permute-done.7), channel_id=1, source_target_pairs={{0,8},{4,12},{8,0},{12,4},{1,9},{5,13},{9,1},{13,5},{2,10},{6,14},... | collective-permute-start | bytes 1474568 | tf_op jit(solution)/shard_map/ppermute | solution.py:15
  167.6 3.3 %collective-permute-done.30 = bf16[1920,128]{0,1:T(8,128)(2,1)S(1)} collective-permute-done((bf16[1920,128]{0,1:T(8,128)(2,1)S(1)}, bf16[1920,128]{0,1:T(8,128)(2,1)S(1)}, u32[]{:S(2)}, u32[]{:S(2)}) %collective-permute-start.30) | collective-permute-done | bytes 491552 | tf_op jit(solution)/shard_map/ppermute | solution.py:15
  171.3 8.0 %collective-permute-done.10 = bf16[1920,128]{0,1:T(8,128)(2,1)S(1)} collective-permute-done((bf16[1920,128]{0,1:T(8,128)(2,1)S(1)}, bf16[1920,128]{0,1:T(8,128)(2,1)S(1)}, u32[]{:S(2)}, u32[]{:S(2)}) %collective-permute-start.10) | collective-permute-done | bytes 491552 | tf_op jit(solution)/shard_map/ppermute | solution.py:15
  184.7 7.2 %collective-permute-start.32 = (bf16[12,48,256]{2,1,0:T(8,128)(2,1)S(1)}, bf16[12,48,256]{2,1,0:T(8,128)(2,1)S(1)}, u32[]{:S(2)}, u32[]{:S(2)}) collective-permute-start(bf16[12,48,256]{2,1,0:T(8,128)(2,1)S(1)} %pad_maximum_fusion.8), channel_id=1, source_target_pairs={{0,1},{1,2},{2,3},{3,0},{4,5},{5,6},{6,7},{7,4},{8,9},{9,10},{10,1... | collective-permute-start | bytes 884744 | tf_op jit(solution)/shard_map/ppermute | solution.py:11
  194.4 4.9 %collective-permute-done.32 = bf16[12,48,256]{2,1,0:T(8,128)(2,1)S(1)} collective-permute-done((bf16[12,48,256]{2,1,0:T(8,128)(2,1)S(1)}, bf16[12,48,256]{2,1,0:T(8,128)(2,1)S(1)}, u32[]{:S(2)}, u32[]{:S(2)}) %collective-permute-start.32) | collective-permute-done | bytes 294944 | tf_op jit(solution)/shard_map/ppermute | solution.py:11
  199.3 5.9 %collective-permute-done.15 = bf16[12,48,256]{2,1,0:T(8,128)(2,1)S(1)} collective-permute-done((bf16[12,48,256]{2,1,0:T(8,128)(2,1)S(1)}, bf16[12,48,256]{2,1,0:T(8,128)(2,1)S(1)}, u32[]{:S(2)}, u32[]{:S(2)}) %collective-permute-start.15) | collective-permute-done | bytes 294944 | tf_op jit(solution)/shard_map/ppermute | solution.py:11
  205.5 2.3 collective-permute-start.16
  208.7 20.3 %collective-permute-done.16 = bf16[12,48,256]{2,1,0:T(8,128)(2,1)S(1)} collective-permute-done((bf16[12,48,256]{2,1,0:T(8,128)(2,1)S(1)}, bf16[12,48,256]{2,1,0:T(8,128)(2,1)S(1)}, u32[]{:S(2)}, u32[]{:S(2)}) %collective-permute-start.16) | collective-permute-done | bytes 294944 | tf_op jit(solution)/shard_map/ppermute | solution.py:11
  229.1 5.0 %collective-permute-done.33 = bf16[12,48,256]{2,1,0:T(8,128)(2,1)S(1)} collective-permute-done((bf16[12,48,256]{2,1,0:T(8,128)(2,1)S(1)}, bf16[12,48,256]{2,1,0:T(8,128)(2,1)S(1)}, u32[]{:S(2)}, u32[]{:S(2)}) %collective-permute-start.33) | collective-permute-done | bytes 294944 | tf_op jit(solution)/shard_map/ppermute | solution.py:11
  235.8 1.3 collective-permute-start.19
  240.7 1.3 collective-permute-done.19
  243.1 1.8 collective-permute-done.35
  244.9 1.3 collective-permute-done.36
  247.3 1.1 pad_maximum_fusion.6
  248.5 2.1 copy.19
  (144 shorter events, 24.0 us)
Async XLA Ops:
  0.0 19.9 %copy-start = (bf16[2048,512]{1,0:T(8,128)(2,1)S(1)}, bf16[2048,512]{1,0:T(8,128)(2,1)}, u32[]{:S(2)}) copy-start(bf16[2048,512]{1,0:T(8,128)(2,1)} %param.11) | copy-start | bytes 6291460
  1.4 9.3 %collective-permute-start = (bf16[1024,128]{1,0:T(8,128)(2,1)S(1)}, bf16[1024,128]{1,0:T(8,128)(2,1)S(1)}, u32[]{:S(2)}, u32[]{:S(2)}) collective-permute-start(bf16[1024,128]{1,0:T(8,128)(2,1)S(1)} %dynamic_slice.28), channel_id=1, source_target_pairs={{0,8},{4,12},{8,0},{12,4},{1,9},{5,13},{9,1},{13,5},{2,10},{6,14},... | collective-permute-start | bytes 786440 | tf_op jit(solution)/shard_map/ppermute | solution.py:15
  12.3 7.6 %collective-permute-start.20 = (bf16[1024,128]{1,0:T(8,128)(2,1)S(1)}, bf16[1024,128]{1,0:T(8,128)(2,1)S(1)}, u32[]{:S(2)}, u32[]{:S(2)}) collective-permute-start(bf16[1024,128]{1,0:T(8,128)(2,1)S(1)} %get-tuple-element.11), channel_id=1, source_target_pairs={{0,8},{4,12},{8,0},{12,4},{1,9},{5,13},{9,1},{13,5},{2,10},{6,14},... | collective-permute-start | bytes 786440 | tf_op jit(solution)/shard_map/ppermute | solution.py:15
  14.1 10.5 %collective-permute-start.1 = (bf16[1024,128]{1,0:T(8,128)(2,1)S(1)}, bf16[1024,128]{1,0:T(8,128)(2,1)S(1)}, u32[]{:S(2)}, u32[]{:S(2)}) collective-permute-start(bf16[1024,128]{1,0:T(8,128)(2,1)S(1)} %get-tuple-element.8), channel_id=1, source_target_pairs={{0,0},{1,4},{2,6},{3,2},{4,1},{5,5},{6,7},{7,3},{8,8},{9,12},{10,1... | collective-permute-start | bytes 786440 | tf_op jit(solution)/shard_map/ppermute | solution.py:124
  14.8 16.8 %collective-permute-start.2 = (bf16[1024,128]{1,0:T(8,128)(2,1)S(1)}, bf16[1024,128]{1,0:T(8,128)(2,1)S(1)}, u32[]{:S(2)}, u32[]{:S(2)}) collective-permute-start(bf16[1024,128]{1,0:T(8,128)(2,1)S(1)} %get-tuple-element.7), channel_id=1, source_target_pairs={{0,2},{1,6},{2,4},{3,0},{4,3},{5,7},{6,5},{7,1},{8,10},{9,14},{10,... | collective-permute-start | bytes 786440 | tf_op jit(solution)/shard_map/ppermute | solution.py:124
  20.1 11.6 %collective-permute-start.21 = (bf16[1024,128]{1,0:T(8,128)(2,1)S(1)}, bf16[1024,128]{1,0:T(8,128)(2,1)S(1)}, u32[]{:S(2)}, u32[]{:S(2)}) collective-permute-start(bf16[1024,128]{1,0:T(8,128)(2,1)S(1)} %get-tuple-element.10), channel_id=1, source_target_pairs={{0,0},{1,4},{2,6},{3,2},{4,1},{5,5},{6,7},{7,3},{8,8},{9,12},{10,1... | collective-permute-start | bytes 786440 | tf_op jit(solution)/shard_map/ppermute | solution.py:124
  20.8 17.2 %collective-permute-start.22 = (bf16[1024,128]{1,0:T(8,128)(2,1)S(1)}, bf16[1024,128]{1,0:T(8,128)(2,1)S(1)}, u32[]{:S(2)}, u32[]{:S(2)}) collective-permute-start(bf16[1024,128]{1,0:T(8,128)(2,1)S(1)} %get-tuple-element.9), channel_id=1, source_target_pairs={{0,2},{1,6},{2,4},{3,0},{4,3},{5,7},{6,5},{7,1},{8,10},{9,14},{10,... | collective-permute-start | bytes 786440 | tf_op jit(solution)/shard_map/ppermute | solution.py:124
  31.6 9.4 %copy-start.5 = (bf16[1024,256]{1,0:T(8,128)(2,1)}, bf16[1024,256]{1,0:T(8,128)(2,1)S(1)}, u32[]{:S(2)}) copy-start(bf16[1024,256]{1,0:T(8,128)(2,1)S(1)} %constant_dynamic-update-slice_fusion) | copy-start | bytes 1572868
  31.6 9.4 %collective-permute-start.3 = (bf16[1024,256]{1,0:T(8,128)(2,1)S(1)}, bf16[1024,256]{1,0:T(8,128)(2,1)}, u32[]{:S(2)}, u32[]{:S(2)}) collective-permute-start(bf16[1024,256]{1,0:T(8,128)(2,1)S(1)} %constant_dynamic-update-slice_fusion), channel_id=1, source_target_pairs={{0,8},{4,12},{8,0},{12,4},{1,9},{5,13},{9,1},{13,5},{2,10},{6,14},... | collective-permute-start | bytes 1572872 | tf_op jit(solution)/shard_map/ppermute | solution.py:15
  38.1 15.0 %collective-permute-start.23 = (bf16[1024,256]{1,0:T(8,128)(2,1)S(1)}, bf16[1024,256]{1,0:T(8,128)(2,1)}, u32[]{:S(2)}, u32[]{:S(2)}) collective-permute-start(bf16[1024,256]{1,0:T(8,128)(2,1)S(1)} %constant_dynamic-update-slice_fusion.2), channel_id=1, source_target_pairs={{0,8},{4,12},{8,0},{12,4},{1,9},{5,13},{9,1},{13,5},{2,10},{6,14},... | collective-permute-start | bytes 1572872 | tf_op jit(solution)/shard_map/ppermute | solution.py:15
  55.9 16.2 %collective-permute-start.24 = (bf16[2048,256]{1,0:T(8,128)(2,1)}, bf16[2048,256]{1,0:T(8,128)(2,1)}, u32[]{:S(2)}, u32[]{:S(2)}) collective-permute-start(bf16[2048,256]{1,0:T(8,128)(2,1)} %pad_maximum_fusion.1), channel_id=1, source_target_pairs={{0,4},{4,0},{8,12},{12,8},{1,5},{5,1},{9,13},{13,9},{2,6},{6,2},{1... | collective-permute-start | bytes 3145736 | tf_op jit(solution)/shard_map/ppermute | solution.py:15
  60.5 0.8 collective-permute-start.12
  62.4 17.1 %collective-permute-start.4 = (bf16[2048,256]{1,0:T(8,128)(2,1)}, bf16[2048,256]{1,0:T(8,128)(2,1)}, u32[]{:S(2)}, u32[]{:S(2)}) collective-permute-start(bf16[2048,256]{1,0:T(8,128)(2,1)} %pad_maximum_fusion), channel_id=1, source_target_pairs={{0,4},{4,0},{8,12},{12,8},{1,5},{5,1},{9,13},{13,9},{2,6},{6,2},{1... | collective-permute-start | bytes 3145736 | tf_op jit(solution)/shard_map/ppermute | solution.py:15
  66.8 1.9 collective-permute-start.13
  68.8 10.7 %slice-start.3 = ((s8[7864320]{0:T(1024)(128)(4,1)}), s8[4194304]{0:T(1024)(128)(4,1)S(1)}, s32[]{:S(2)}) async-start(s8[7864320]{0:T(1024)(128)(4,1)} %bitcast.109), calls=%async_computation.3 | async-start | bytes 8388608
  68.8 10.7 %slice-start.4 = ((s8[7864320]{0:T(1024)(128)(4,1)}), s8[3670016]{0:T(1024)(128)(4,1)S(1)}, s32[]{:S(2)}) async-start(s8[7864320]{0:T(1024)(128)(4,1)} %bitcast.109), calls=%async_computation.4 | async-start | bytes 7340032
  68.8 16.1 %collective-permute-start.14 = (f32[1,512]{1,0:T(1,128)S(1)}, f32[1,512]{1,0:T(1,128)S(1)}, u32[]{:S(2)}, u32[]{:S(2)}) collective-permute-start(f32[1,512]{1,0:T(1,128)S(1)} %add.192), channel_id=1, source_target_pairs={{0,8},{4,12},{8,0},{12,4},{1,9},{5,13},{9,1},{13,5},{2,10},{6,14},... | collective-permute-start | bytes 6152 | tf_op jit(solution)/shard_map/ppermute | solution.py:15
  79.3 25.1 %copy-start.2 = (bf16[1024,256]{1,0:T(8,128)(2,1)S(1)}, bf16[1024,256]{1,0:T(8,128)(2,1)}, u32[]{:S(2)}) copy-start(bf16[1024,256]{1,0:T(8,128)(2,1)} %copy-done.1) | copy-start | bytes 1572868
  79.3 25.1 %copy-start.4 = (bf16[1024,256]{1,0:T(8,128)(2,1)S(1)}, bf16[1024,256]{1,0:T(8,128)(2,1)}, u32[]{:S(2)}) copy-start(bf16[1024,256]{1,0:T(8,128)(2,1)} %copy-done.3) | copy-start | bytes 1572868
  79.3 25.0 %collective-permute-start.25 = (bf16[1920,256]{0,1:T(8,128)(2,1)}, bf16[1920,256]{0,1:T(8,128)(2,1)}, u32[]{:S(2)}, u32[]{:S(2)}) collective-permute-start(bf16[1920,256]{0,1:T(8,128)(2,1)} %fusion.3), channel_id=1, source_target_pairs={{0,1},{1,0},{2,3},{3,2},{4,5},{5,4},{6,7},{7,6},{8,9},{9,8},{10,11... | collective-permute-start | bytes 2949128 | tf_op jit(solution)/shard_map/ppermute | solution.py:15
  84.2 39.9 %collective-permute-start.5 = (bf16[1920,256]{0,1:T(8,128)(2,1)}, bf16[1920,256]{0,1:T(8,128)(2,1)S(1)}, u32[]{:S(2)}, u32[]{:S(2)}) collective-permute-start(bf16[1920,256]{0,1:T(8,128)(2,1)} %fusion.2), channel_id=1, source_target_pairs={{0,1},{1,0},{2,3},{3,2},{4,5},{5,4},{6,7},{7,6},{8,9},{9,8},{10,11... | collective-permute-start | bytes 2949128 | tf_op jit(solution)/shard_map/ppermute | solution.py:15
  84.9 39.2 %slice-start.5 = ((s8[7864320]{0:T(1024)(128)(4,1)}), s8[4194304]{0:T(1024)(128)(4,1)S(1)}, s32[]{:S(2)}) async-start(s8[7864320]{0:T(1024)(128)(4,1)} %bitcast.111), calls=%async_computation.5 | async-start | bytes 8388608
  84.9 39.2 %slice-start.6 = ((s8[7864320]{0:T(1024)(128)(4,1)}), s8[3670016]{0:T(1024)(128)(4,1)S(1)}, s32[]{:S(2)}) async-start(s8[7864320]{0:T(1024)(128)(4,1)} %bitcast.111), calls=%async_computation.6 | async-start | bytes 7340032
  110.3 27.0 %collective-permute-start.26 = (bf16[1920,128]{0,1:T(8,128)(2,1)S(1)}, bf16[1920,128]{0,1:T(8,128)(2,1)S(1)}, u32[]{:S(2)}, u32[]{:S(2)}) collective-permute-start(bf16[1920,128]{0,1:T(8,128)(2,1)S(1)} %slice.138), channel_id=1, source_target_pairs={{0,3},{1,2},{2,1},{3,0},{4,7},{5,6},{6,5},{7,4},{8,11},{9,10},{10,... | collective-permute-start | bytes 1474568 | tf_op jit(solution)/shard_map/ppermute | solution.py:15
  124.1 55.6 %slice-start = ((s8[8847360]{0:T(1024)(128)(4,1)}), s8[458752]{0:T(1024)(128)(4,1)S(1)}, s32[]{:S(2)}) async-start(s8[8847360]{0:T(1024)(128)(4,1)} %bitcast.99), calls=%async_computation | async-start | bytes 917504
  124.1 55.6 %slice-start.1 = ((s8[8847360]{0:T(1024)(128)(4,1)}), s8[4194304]{0:T(1024)(128)(4,1)S(1)}, s32[]{:S(2)}) async-start(s8[8847360]{0:T(1024)(128)(4,1)} %bitcast.99), calls=%async_computation.1 | async-start | bytes 8388608
  126.6 20.8 %collective-permute-start.6 = (bf16[1920,128]{0,1:T(8,128)(2,1)S(1)}, bf16[1920,128]{0,1:T(8,128)(2,1)S(1)}, u32[]{:S(2)}, u32[]{:S(2)}) collective-permute-start(bf16[1920,128]{0,1:T(8,128)(2,1)S(1)} %slice.139), channel_id=1, source_target_pairs={{0,3},{1,2},{2,1},{3,0},{4,7},{5,6},{6,5},{7,4},{8,11},{9,10},{10,... | collective-permute-start | bytes 1474568 | tf_op jit(solution)/shard_map/ppermute | solution.py:15
  137.4 17.1 %collective-permute-start.27 = (bf16[1920,128]{0,1:T(8,128)(2,1)S(1)}, bf16[1920,128]{0,1:T(8,128)(2,1)S(1)}, u32[]{:S(2)}, u32[]{:S(2)}) collective-permute-start(bf16[1920,128]{0,1:T(8,128)(2,1)S(1)} %fusion.46), channel_id=1, source_target_pairs={{0,16},{16,0},{1,17},{17,1},{2,18},{18,2},{3,19},{19,3},{4,20},{20... | collective-permute-start | bytes 1474568 | tf_op jit(solution)/shard_map/ppermute | solution.py:15
  138.9 15.9 %collective-permute-start.29 = (bf16[1920,128]{0,1:T(8,128)(2,1)S(1)}, bf16[1920,128]{0,1:T(8,128)(2,1)S(1)}, u32[]{:S(2)}, u32[]{:S(2)}) collective-permute-start(bf16[1920,128]{0,1:T(8,128)(2,1)S(1)} %fusion.46), channel_id=1, source_target_pairs={{0,8},{4,12},{8,0},{12,4},{1,9},{5,13},{9,1},{13,5},{2,10},{6,14},... | collective-permute-start | bytes 1474568 | tf_op jit(solution)/shard_map/ppermute | solution.py:15
  147.5 14.2 %collective-permute-start.7 = (bf16[1920,128]{0,1:T(8,128)(2,1)S(1)}, bf16[1920,128]{0,1:T(8,128)(2,1)S(1)}, u32[]{:S(2)}, u32[]{:S(2)}) collective-permute-start(bf16[1920,128]{0,1:T(8,128)(2,1)S(1)} %fusion.47), channel_id=1, source_target_pairs={{0,16},{16,0},{1,17},{17,1},{2,18},{18,2},{3,19},{19,3},{4,20},{20... | collective-permute-start | bytes 1474568 | tf_op jit(solution)/shard_map/ppermute | solution.py:15
  149.0 22.3 %collective-permute-start.9 = (bf16[1920,128]{0,1:T(8,128)(2,1)S(1)}, bf16[1920,128]{0,1:T(8,128)(2,1)S(1)}, u32[]{:S(2)}, u32[]{:S(2)}) collective-permute-start(bf16[1920,128]{0,1:T(8,128)(2,1)S(1)} %fusion.47), channel_id=1, source_target_pairs={{0,8},{4,12},{8,0},{12,4},{1,9},{5,13},{9,1},{13,5},{2,10},{6,14},... | collective-permute-start | bytes 1474568 | tf_op jit(solution)/shard_map/ppermute | solution.py:15
  154.6 25.0 %slice-start.2 = ((s8[8847360]{0:T(1024)(128)(4,1)}), s8[4194304]{0:T(1024)(128)(4,1)S(1)}, s32[]{:S(2)}) async-start(s8[8847360]{0:T(1024)(128)(4,1)} %bitcast.99), calls=%async_computation.2 | async-start | bytes 8388608
  154.7 24.9 %collective-permute-start.28 = (bf16[1920,256]{0,1:T(8,128)(2,1)S(1)}, bf16[1920,256]{0,1:T(8,128)(2,1)S(1)}, u32[]{:S(2)}, u32[]{:S(2)}) collective-permute-start(bf16[1920,256]{0,1:T(8,128)(2,1)S(1)} %pad_maximum_fusion.4), channel_id=1, source_target_pairs={{0,4},{4,0},{8,12},{12,8},{1,5},{5,1},{9,13},{13,9},{2,6},{6,2},{1... | collective-permute-start | bytes 2949128 | tf_op jit(solution)/shard_map/ppermute | solution.py:15
  154.8 16.0 %collective-permute-start.30 = (bf16[1920,128]{0,1:T(8,128)(2,1)S(1)}, bf16[1920,128]{0,1:T(8,128)(2,1)S(1)}, u32[]{:S(2)}, u32[]{:S(2)}) collective-permute-start(bf16[1920,128]{0,1:T(8,128)(2,1)S(1)} %collective-permute-done.29), channel_id=1, source_target_pairs={{0,16},{16,0},{1,17},{17,1},{2,18},{18,2},{3,19},{19,3},{4,20},{20... | collective-permute-start | bytes 1474568 | tf_op jit(solution)/shard_map/ppermute | solution.py:15
  161.9 18.6 %collective-permute-start.8 = (bf16[1920,256]{0,1:T(8,128)(2,1)S(1)}, bf16[1920,256]{0,1:T(8,128)(2,1)S(1)}, u32[]{:S(2)}, u32[]{:S(2)}) collective-permute-start(bf16[1920,256]{0,1:T(8,128)(2,1)S(1)} %pad_maximum_fusion.2), channel_id=1, source_target_pairs={{0,4},{4,0},{8,12},{12,8},{1,5},{5,1},{9,13},{13,9},{2,6},{6,2},{1... | collective-permute-start | bytes 2949128 | tf_op jit(solution)/shard_map/ppermute | solution.py:15
  162.0 17.4 %collective-permute-start.10 = (bf16[1920,128]{0,1:T(8,128)(2,1)S(1)}, bf16[1920,128]{0,1:T(8,128)(2,1)S(1)}, u32[]{:S(2)}, u32[]{:S(2)}) collective-permute-start(bf16[1920,128]{0,1:T(8,128)(2,1)S(1)} %collective-permute-done.7), channel_id=1, source_target_pairs={{0,8},{4,12},{8,0},{12,4},{1,9},{5,13},{9,1},{13,5},{2,10},{6,14},... | collective-permute-start | bytes 1474568 | tf_op jit(solution)/shard_map/ppermute | solution.py:15
  171.2 11.7 %collective-permute-start.31 = (bf16[1920,256]{0,1:T(8,128)(2,1)S(1)}, bf16[1920,256]{0,1:T(8,128)(2,1)S(1)}, u32[]{:S(2)}, u32[]{:S(2)}) collective-permute-start(bf16[1920,256]{0,1:T(8,128)(2,1)S(1)} %pad_maximum_fusion.5), channel_id=1, source_target_pairs={{0,4},{4,0},{8,12},{12,8},{1,5},{5,1},{9,13},{13,9},{2,6},{6,2},{1... | collective-permute-start | bytes 2949128 | tf_op jit(solution)/shard_map/ppermute | solution.py:15
  179.5 12.4 %collective-permute-start.11 = (bf16[1920,256]{0,1:T(8,128)(2,1)S(1)}, bf16[1920,256]{0,1:T(8,128)(2,1)S(1)}, u32[]{:S(2)}, u32[]{:S(2)}) collective-permute-start(bf16[1920,256]{0,1:T(8,128)(2,1)S(1)} %pad_maximum_fusion.3), channel_id=1, source_target_pairs={{0,4},{4,0},{8,12},{12,8},{1,5},{5,1},{9,13},{13,9},{2,6},{6,2},{1... | collective-permute-start | bytes 2949128 | tf_op jit(solution)/shard_map/ppermute | solution.py:15
  184.7 14.5 %collective-permute-start.32 = (bf16[12,48,256]{2,1,0:T(8,128)(2,1)S(1)}, bf16[12,48,256]{2,1,0:T(8,128)(2,1)S(1)}, u32[]{:S(2)}, u32[]{:S(2)}) collective-permute-start(bf16[12,48,256]{2,1,0:T(8,128)(2,1)S(1)} %pad_maximum_fusion.8), channel_id=1, source_target_pairs={{0,1},{1,2},{2,3},{3,0},{4,5},{5,6},{6,7},{7,4},{8,9},{9,10},{10,1... | collective-permute-start | bytes 884744 | tf_op jit(solution)/shard_map/ppermute | solution.py:11
  194.2 11.0 %collective-permute-start.15 = (bf16[12,48,256]{2,1,0:T(8,128)(2,1)S(1)}, bf16[12,48,256]{2,1,0:T(8,128)(2,1)S(1)}, u32[]{:S(2)}, u32[]{:S(2)}) collective-permute-start(bf16[12,48,256]{2,1,0:T(8,128)(2,1)S(1)} %pad_maximum_fusion.7), channel_id=1, source_target_pairs={{0,1},{1,2},{2,3},{3,0},{4,5},{5,6},{6,7},{7,4},{8,9},{9,10},{10,1... | collective-permute-start | bytes 884744 | tf_op jit(solution)/shard_map/ppermute | solution.py:11
  205.5 23.5 %collective-permute-start.16 = (bf16[12,48,256]{2,1,0:T(8,128)(2,1)S(1)}, bf16[12,48,256]{2,1,0:T(8,128)(2,1)S(1)}, u32[]{:S(2)}, u32[]{:S(2)}) collective-permute-start(bf16[12,48,256]{2,1,0:T(8,128)(2,1)S(1)} %get-tuple-element.50), channel_id=1, source_target_pairs={{0,2},{1,3},{2,0},{3,1},{4,6},{5,7},{6,4},{7,5},{8,10},{9,11},{10,... | collective-permute-start | bytes 884744 | tf_op jit(solution)/shard_map/ppermute | solution.py:11
  207.8 26.3 %collective-permute-start.33 = (bf16[12,48,256]{2,1,0:T(8,128)(2,1)S(1)}, bf16[12,48,256]{2,1,0:T(8,128)(2,1)S(1)}, u32[]{:S(2)}, u32[]{:S(2)}) collective-permute-start(bf16[12,48,256]{2,1,0:T(8,128)(2,1)S(1)} %get-tuple-element.51), channel_id=1, source_target_pairs={{0,2},{1,3},{2,0},{3,1},{4,6},{5,7},{6,4},{7,5},{8,10},{9,11},{10,... | collective-permute-start | bytes 884744 | tf_op jit(solution)/shard_map/ppermute | solution.py:11
  234.8 4.4 %collective-permute-start.17 = (bf16[4,48,2,1,128]{4,2,1,0,3:T(2,128)(2,1)S(1)}, bf16[4,48,2,1,128]{4,2,1,0,3:T(2,128)(2,1)S(1)}, u32[]{:S(2)}, u32[]{:S(2)}) collective-permute-start(bf16[4,48,2,1,128]{4,2,1,0,3:T(2,128)(2,1)S(1)} %squeeze.25), channel_id=1, source_target_pairs={{0,4},{4,0},{8,12},{12,8},{1,5},{5,1},{9,13},{13,9},{2,6},{6,2},{1... | collective-permute-start | bytes 294920 | tf_op jit(solution)/shard_map/ppermute | solution.py:15
  235.0 5.7 %collective-permute-start.18 = (bf16[4,48,2,1,128]{4,2,1,0,3:T(2,128)(2,1)S(1)}, bf16[4,48,2,1,128]{4,2,1,0,3:T(2,128)(2,1)S(1)}, u32[]{:S(2)}, u32[]{:S(2)}) collective-permute-start(bf16[4,48,2,1,128]{4,2,1,0,3:T(2,128)(2,1)S(1)} %squeeze.26), channel_id=1, source_target_pairs={{0,8},{4,12},{8,0},{12,4},{1,9},{5,13},{9,1},{13,5},{2,10},{6,14},... | collective-permute-start | bytes 294920 | tf_op jit(solution)/shard_map/ppermute | solution.py:15
  235.8 6.2 %collective-permute-start.19 = (bf16[4,48,2,1,128]{4,2,1,0,3:T(2,128)(2,1)S(1)}, bf16[4,48,2,1,128]{4,2,1,0,3:T(2,128)(2,1)S(1)}, u32[]{:S(2)}, u32[]{:S(2)}) collective-permute-start(bf16[4,48,2,1,128]{4,2,1,0,3:T(2,128)(2,1)S(1)} %squeeze.27), channel_id=1, source_target_pairs={{0,12},{4,8},{8,4},{12,0},{1,13},{5,9},{9,5},{13,1},{2,14},{6,10},... | collective-permute-start | bytes 294920 | tf_op jit(solution)/shard_map/ppermute | solution.py:15
  237.9 5.2 %collective-permute-start.34 = (bf16[4,48,2,1,128]{4,2,1,0,3:T(2,128)(2,1)S(1)}, bf16[4,48,2,1,128]{4,2,1,0,3:T(2,128)(2,1)S(1)}, u32[]{:S(2)}, u32[]{:S(2)}) collective-permute-start(bf16[4,48,2,1,128]{4,2,1,0,3:T(2,128)(2,1)S(1)} %squeeze.29), channel_id=1, source_target_pairs={{0,4},{4,0},{8,12},{12,8},{1,5},{5,1},{9,13},{13,9},{2,6},{6,2},{1... | collective-permute-start | bytes 294920 | tf_op jit(solution)/shard_map/ppermute | solution.py:15
  238.4 6.5 %collective-permute-start.35 = (bf16[4,48,2,1,128]{4,2,1,0,3:T(2,128)(2,1)S(1)}, bf16[4,48,2,1,128]{4,2,1,0,3:T(2,128)(2,1)S(1)}, u32[]{:S(2)}, u32[]{:S(2)}) collective-permute-start(bf16[4,48,2,1,128]{4,2,1,0,3:T(2,128)(2,1)S(1)} %squeeze.30), channel_id=1, source_target_pairs={{0,8},{4,12},{8,0},{12,4},{1,9},{5,13},{9,1},{13,5},{2,10},{6,14},... | collective-permute-start | bytes 294920 | tf_op jit(solution)/shard_map/ppermute | solution.py:15
  239.3 6.9 %collective-permute-start.36 = (bf16[4,48,2,1,128]{4,2,1,0,3:T(2,128)(2,1)S(1)}, bf16[4,48,2,1,128]{4,2,1,0,3:T(2,128)(2,1)S(1)}, u32[]{:S(2)}, u32[]{:S(2)}) collective-permute-start(bf16[4,48,2,1,128]{4,2,1,0,3:T(2,128)(2,1)S(1)} %squeeze.31), channel_id=1, source_target_pairs={{0,12},{4,8},{8,4},{12,0},{1,13},{5,9},{9,5},{13,1},{2,14},{6,10},... | collective-permute-start | bytes 294920 | tf_op jit(solution)/shard_map/ppermute | solution.py:15
  (8 other events, 41.6 us)

commit v3 on v2

--- a/solution.py
+++ b/solution.py
@@ -71,6 +71,10 @@
     return gathered_rows[None, None]
 
 
+def after(value, before):
+    return value if before is None else lax.optimization_barrier((value, before))[0]
+
+
 def product_plan(
     features, proj_weight, proj_bias, kv_weight, key_gain, tile_map, tile_count, decode_owner
 ):
@@ -110,46 +114,49 @@
         for j in range(2)
     ]
     half = kv_weight.shape[0] // 2
-    routed = []
-    for part in range(2):
+
+    def cross_chips(part, before):
         column = (group * 2 + part) * head_dim
         mine = lax.dynamic_slice_in_dim(kv_weight, column, head_dim, axis=1)
         stays = lax.dynamic_slice_in_dim(mine, tile // 2 * half, half, axis=0)
         leaves = lax.dynamic_slice_in_dim(mine, half - tile // 2 * half, half, axis=0)
-        comes = swapped(leaves, "tile", 2)
+        return stays, swapped(after(leaves, before), "tile", 2)
+
+    def cross_planes(stays, comes, before):
         pieces = []
         for j in range(2):
             own_rows = tile // 2 == (head // 2) ^ j
-            pieces.append(
-                lax.ppermute(jnp.where(own_rows, stays, comes), ("tile", "head"), rounds[j])
-            )
-        near_half = jnp.concatenate(pieces, axis=1)
+            piece = after(jnp.where(own_rows, stays, comes), before)
+            pieces.append(lax.ppermute(piece, ("tile", "head"), rounds[j]))
+        return jnp.concatenate(pieces, axis=1)
+
+    def within_plane(near_half):
         other_half = swapped(near_half, "tile", 2)
-        near = jnp.concatenate(
-            [
-                jnp.where(first_chip, near_half, other_half),
-                jnp.where(first_chip, other_half, near_half),
-            ],
-            axis=0,
-        )
-        far = swapped(near, "tile", 1)
+        top = jnp.where(first_chip, near_half, other_half)
+        bottom = jnp.where(first_chip, other_half, near_half)
+        near = jnp.concatenate([top, bottom], axis=0)
+        return near, swapped(near, "tile", 1)
+
+    def sum_over_planes(near, far, before):
         far_leaves = at_end == first_core
         outer = add_columns(proj_weight, jnp.where(far_leaves, far, near)).astype(jnp.bfloat16)
         pair_sum = add_columns(proj_weight, jnp.where(far_leaves, near, far))
-        pair_sum = pair_sum + swapped(outer, "head", 1).astype(jnp.float32)
+        pair_sum = pair_sum + swapped(after(outer, before), "head", 1).astype(jnp.float32)
         mirrored = swapped(pair_sum[:, width:].astype(jnp.bfloat16), "head", 3)
-        own = (pair_sum[:, :width] + mirrored.astype(jnp.float32)).astype(jnp.bfloat16)
-
+        return (pair_sum[:, :width] + mirrored.astype(jnp.float32)).astype(jnp.bfloat16)
+
+    def both_heads(ours, theirs):
+        left, right = jnp.where(group == 0, ours, theirs), jnp.where(group == 0, theirs, ours)
+        return lax.optimization_barrier(jnp.concatenate([left, right], axis=1))
+
+    def times_features(own, part):
         across_x, across_y = swapped(own, "tile", 2), swapped(own, "groups", 1)
         diagonal = swapped(across_y, "tile", 2) if part == 0 else swapped(across_x, "groups", 1)
-
-        def both_heads(ours, theirs):
-            left, right = jnp.where(group == 0, ours, theirs), jnp.where(group == 0, theirs, ours)
-            return lax.optimization_barrier(jnp.concatenate([left, right], axis=1))
-
         rows_0, rows_2 = both_heads(own, across_y), both_heads(across_x, diagonal)
         rows = [rows_0, swapped(rows_0, "tile", 1), rows_2, swapped(rows_2, "tile", 1)]
-        total = sum(add_columns(feature_parts[r], rows[r]) for r in range(4))
+        return sum(add_columns(feature_parts[r], rows[r]) for r in range(4))
+
+    def finish(total, part):
         finished = []
         for k in range(2):
             entries = total[:, k * width : (k + 1) * width].reshape(token_rows, layers, head_dim)
@@ -158,7 +165,10 @@
                 squares = jnp.mean(entries * entries, axis=-1, keepdims=True)
                 entries = entries * lax.rsqrt(squares + eps_norm) * key_gain[None]
             finished.append(entries.reshape(token_rows, width).astype(jnp.bfloat16))
-        rolled = jnp.concatenate(finished, axis=1).reshape(tile_slots, shard_len, 2 * width)
+        return jnp.concatenate(finished, axis=1).reshape(tile_slots, shard_len, 2 * width)
+
+    def route(rolled, before):
+        rolled = after(rolled, before)
         for stride in (1, 2):
             odd = (turn_of // stride % 2 == 1)[:, None, None]
             rolled = jnp.where(odd, shifted_2(rolled, "head", stride), rolled)
@@ -167,8 +177,21 @@
         arrived = [outgoing[0]] + [swapped(outgoing[r], "tile", r) for r in (1, 2, 3)]
         even = [jnp.where(first_core, arrived[r], arrived[r ^ 1]) for r in range(4)]
         ranked = [jnp.where(first_chip, even[r], even[r ^ 2]) for r in range(4)]
-        routed.append(jnp.stack(ranked, axis=1))
-    cache = jnp.stack(routed, axis=-2)
+        return jnp.stack(ranked, axis=1), rolled
+
+    key_stays, key_comes = cross_chips(0, None)
+    value_stays, value_comes = cross_chips(1, key_comes)
+    key_half = cross_planes(key_stays, key_comes, None)
+    value_half = cross_planes(value_stays, value_comes, key_half)
+    key_near, key_far = within_plane(key_half)
+    value_near, value_far = within_plane(after(value_half, key_near))
+    key_own = sum_over_planes(key_near, key_far, None)
+    value_own = sum_over_planes(value_near, value_far, key_own)
+    keys = finish(times_features(key_own, 0), 0)
+    values = finish(times_features(value_own, 1), 1)
+    routed_keys, keys = route(keys, value_own)
+    routed_values, _ = route(values, keys)
+    cache = jnp.stack([routed_keys, routed_values], axis=-2)
     return cache.reshape(1, 1, most_tiles * 4 * shard_len, 4 * layers, head_dim)
 
 

time: 251 us -> 274 us (1.092)
  starting transfers between devices: 66.5 us -> 82 us
  waiting for transfers between devices: 139 us -> 148 us
    ppermute x28, starting transfers between devices: 46.4 us -> 55.5 us  [swapped(): lax.ppermute(shard, axis, [(i, i ^ bit) for i in range(lax.axis_size(axis...]
    ppermute x4, waiting for transfers between devices: 13.1 us -> 21.8 us  [cross_planes(): pieces.append(lax.ppermute(piece, ('tile', 'head'), rounds[j]))]
    ppermute x4, starting transfers between devices: 10.3 us -> 18.2 us  [shifted_2(): lax.ppermute(shard, axis, [(i, (i + by) % count) for i in range(count)])]
  transfers between devices with their start and end apart: 37 -> 37, of which waited for: 22 -> 20; matrix products, arithmetic and copies ran while one was open for 13% -> 11% of each run, Pallas kernels for 0% -> 0%
where the time goes in v3:
time: 274 us
  waiting for transfers between devices  148 us (54%)
  starting transfers between devices  82 us (30%)
  matrix products  27.5 us (10%)
  other arithmetic  8.7 us (3%)
  local copies, waits for them, and re-layouts  6.85 us (2%)
    ppermute x28, waiting for transfers between devices, swapped(): lax.ppermute(shard, axis, [(i, i ^ bit) for i in range(lax.axis_size(axis...  87.9 us
    ppermute x28, starting transfers between devices, swapped(): lax.ppermute(shard, axis, [(i, i ^ bit) for i in range(lax.axis_size(axis...  55.5 us
    ppermute x4, waiting for transfers between devices, shifted_2(): lax.ppermute(shard, axis, [(i, (i + by) % count) for i in range(count)])  37.9 us
    dot_general x15, matrix products, add_columns(): return jnp.dot(operand, portion, preferred_element_type=jnp.float32)  27.3 us
    ppermute x4, waiting for transfers between devices, cross_planes(): pieces.append(lax.ppermute(piece, ('tile', 'head'), rounds[j]))  21.8 us
    ppermute x4, starting transfers between devices, shifted_2(): lax.ppermute(shard, axis, [(i, (i + by) % count) for i in range(count)])  18.2 us
    ppermute x4, starting transfers between devices, cross_planes(): pieces.append(lax.ppermute(piece, ('tile', 'head'), rounds[j]))  7.5 us
  transfers between devices with their start and end apart: 37, of which 20 were waited for; matrix products, arithmetic and copies ran while one was open for 11% of the time, Pallas kernels for 0%

profile of v3, /device:TPU:0, one launch (start us, length us, event | category | flops | bytes accessed | tf_op | source)
XLA Modules:
  0.0 273.5 jit_solution(6901482527089800752)
XLA Ops:
  0.0 1.6 fusion.77
  1.6 3.1 %collective-permute-start = (bf16[1024,128]{1,0:T(8,128)(2,1)S(1)}, bf16[1024,128]{1,0:T(8,128)(2,1)S(1)}, u32[]{:S(2)}, u32[]{:S(2)}) collective-permute-start(bf16[1024,128]{1,0:T(8,128)(2,1)S(1)} %get-tuple-element.27), channel_id=1, source_target_pairs={{0,8},{4,12},{8,0},{12,4},{1,9},{5,13},{9,1},{13,5},{2,10},{6,14},... | collective-permute-start | bytes 786440 | tf_op jit(solution)/shard_map/ppermute | solution.py:15
  4.6 6.3 %collective-permute-done = bf16[1024,128]{1,0:T(8,128)(2,1)S(1)} collective-permute-done((bf16[1024,128]{1,0:T(8,128)(2,1)S(1)}, bf16[1024,128]{1,0:T(8,128)(2,1)S(1)}, u32[]{:S(2)}, u32[]{:S(2)}) %collective-permute-start) | collective-permute-done | bytes 262176 | tf_op jit(solution)/shard_map/ppermute | solution.py:15
  10.9 1.7 collective-permute-start.15
  12.7 5.8 %collective-permute-done.15 = bf16[1024,128]{1,0:T(8,128)(2,1)S(1)} collective-permute-done((bf16[1024,128]{1,0:T(8,128)(2,1)S(1)}, bf16[1024,128]{1,0:T(8,128)(2,1)S(1)}, u32[]{:S(2)}, u32[]{:S(2)}) %collective-permute-start.15) | collective-permute-done | bytes 262176 | tf_op jit(solution)/shard_map/ppermute | solution.py:15
  18.4 1.7 broadcast_select_fusion.18
  20.8 3.7 %collective-permute-start.2 = (bf16[1024,128]{1,0:T(8,128)(2,1)S(1)}, bf16[1024,128]{1,0:T(8,128)(2,1)S(1)}, u32[]{:S(2)}, u32[]{:S(2)}) collective-permute-start(bf16[1024,128]{1,0:T(8,128)(2,1)S(1)} %get-tuple-element.26), channel_id=1, source_target_pairs={{0,2},{1,6},{2,4},{3,0},{4,3},{5,7},{6,5},{7,1},{8,10},{9,14},{10,... | collective-permute-start | bytes 786440 | tf_op jit(solution)/shard_map/ppermute | solution.py:130
  24.6 10.8 %collective-permute-done.2 = bf16[1024,128]{1,0:T(8,128)(2,1)S(1)} collective-permute-done((bf16[1024,128]{1,0:T(8,128)(2,1)S(1)}, bf16[1024,128]{1,0:T(8,128)(2,1)S(1)}, u32[]{:S(2)}, u32[]{:S(2)}) %collective-permute-start.2) | collective-permute-done | bytes 262176 | tf_op jit(solution)/shard_map/ppermute | solution.py:130
  35.5 1.6 collective-permute-start.3
  37.1 12.7 %collective-permute-done.3 = bf16[1024,256]{1,0:T(8,128)(2,1)S(1)} collective-permute-done((bf16[1024,256]{1,0:T(8,128)(2,1)S(1)}, bf16[1024,256]{1,0:T(8,128)(2,1)S(1)}, u32[]{:S(2)}, u32[]{:S(2)}) %collective-permute-start.3) | collective-permute-done | bytes 524320 | tf_op jit(solution)/shard_map/ppermute | solution.py:15
  50.7 2.4 collective-permute-start.17
  53.1 11.0 %collective-permute-done.17 = bf16[1024,128]{1,0:T(8,128)(2,1)S(1)} collective-permute-done((bf16[1024,128]{1,0:T(8,128)(2,1)S(1)}, bf16[1024,128]{1,0:T(8,128)(2,1)S(1)}, u32[]{:S(2)}, u32[]{:S(2)}) %collective-permute-start.17) | collective-permute-done | bytes 262176 | tf_op jit(solution)/shard_map/ppermute | solution.py:130
  64.2 1.6 collective-permute-start.18
  65.7 6.7 %fusion.2 = bf16[1920,256]{0,1:T(8,128)(2,1)S(1)} fusion(bf16[1920,2048]{1,0:T(8,128)(2,1)} %param.9, bf16[2048,256]{1,0:T(8,128)(2,1)} %collective-permute-done.4, pred[]{:T(512)S(6)} %eq.94, bf16[1024,256]{1,0:T(8,128)(2,1)S(1)} %get-tuple-element.32, bf16[1024,256]{1,0:T(8,128)(2,1)S(1)} %get-tuple-element.31), kind=kOutput, calls=%fused_computation.8 | convolution fusion | flops 2016378880 | bytes 10944513 | tf_op jit(solution)/shard_map/dot_general | solution.py:19
  72.5 1.8 collective-permute-start.5
  75.6 22.0 %collective-permute-start.13 = (f32[1,512]{1,0:T(1,128)S(1)}, f32[1,512]{1,0:T(1,128)S(1)}, u32[]{:S(2)}, u32[]{:S(2)}) collective-permute-start(f32[1,512]{1,0:T(1,128)S(1)} %fusion.80), channel_id=1, source_target_pairs={{0,4},{4,0},{8,12},{12,8},{1,5},{5,1},{9,13},{13,9},{2,6},{6,2},{1... | collective-permute-start | bytes 6152 | tf_op jit(solution)/shard_map/ppermute | solution.py:15
  97.9 2.5 fusion
  100.3 1.3 copy-done.1
  101.7 1.6 collective-permute-start.6
  104.0 3.0 %collective-permute-done.14 = f32[1,512]{1,0:T(1,128)S(1)} collective-permute-done((f32[1,512]{1,0:T(1,128)S(1)}, f32[1,512]{1,0:T(1,128)S(1)}, u32[]{:S(2)}, u32[]{:S(2)}) %collective-permute-start.14) | collective-permute-done | bytes 2080 | tf_op jit(solution)/shard_map/ppermute | solution.py:15
  107.0 10.0 %collective-permute-done.6 = bf16[1920,128]{0,1:T(8,128)(2,1)S(1)} collective-permute-done((bf16[1920,128]{0,1:T(8,128)(2,1)S(1)}, bf16[1920,128]{0,1:T(8,128)(2,1)S(1)}, u32[]{:S(2)}, u32[]{:S(2)}) %collective-permute-start.6) | collective-permute-done | bytes 491552 | tf_op jit(solution)/shard_map/ppermute | solution.py:15
  117.1 1.5 fusion.47
  118.5 1.4 collective-permute-start.7
  119.9 6.0 %fusion.3 = bf16[1920,256]{0,1:T(8,128)(2,1)S(1)} fusion(bf16[1920,2048]{1,0:T(8,128)(2,1)} %param.9, bf16[2048,256]{1,0:T(8,128)(2,1)} %collective-permute-done.19, pred[]{:T(512)S(6)} %eq.94, bf16[1024,256]{1,0:T(8,128)(2,1)S(1)} %get-tuple-element.30, bf16[1024,256]{1,0:T(8,128)(2,1)S(1)} %get-tuple-element.29), kind=kOutput, calls=%fused_computation.9 | convolution fusion | flops 2016378880 | bytes 10944513 | tf_op jit(solution)/shard_map/dot_general | solution.py:19
  126.9 10.3 %collective-permute-start.20 = (bf16[1920,256]{0,1:T(8,128)(2,1)S(1)}, bf16[1920,256]{0,1:T(8,128)(2,1)}, u32[]{:S(2)}, u32[]{:S(2)}) collective-permute-start(bf16[1920,256]{0,1:T(8,128)(2,1)S(1)} %fusion.3), channel_id=1, source_target_pairs={{0,1},{1,0},{2,3},{3,2},{4,5},{5,4},{6,7},{7,6},{8,9},{9,8},{10,11... | collective-permute-start | bytes 2949128 | tf_op jit(solution)/shard_map/ppermute | solution.py:15
  137.5 2.4 collective-permute-done.9
  139.9 9.7 %collective-permute-done.10 = bf16[1920,128]{0,1:T(8,128)(2,1)S(1)} collective-permute-done((bf16[1920,128]{0,1:T(8,128)(2,1)S(1)}, bf16[1920,128]{0,1:T(8,128)(2,1)S(1)}, u32[]{:S(2)}, u32[]{:S(2)}) %collective-permute-start.10) | collective-permute-done | bytes 491552 | tf_op jit(solution)/shard_map/ppermute | solution.py:15
  149.9 8.0 %collective-permute-done.20 = bf16[1920,256]{0,1:T(8,128)(2,1)} collective-permute-done((bf16[1920,256]{0,1:T(8,128)(2,1)S(1)}, bf16[1920,256]{0,1:T(8,128)(2,1)}, u32[]{:S(2)}, u32[]{:S(2)}) %collective-permute-start.20) | collective-permute-done | bytes 983072 | tf_op jit(solution)/shard_map/ppermute | solution.py:15
  157.8 3.6 %fusion.1 = f32[1920,256]{0,1:T(8,128)S(1)} fusion(bf16[1920,2048]{1,0:T(8,128)(2,1)S(1)} %bitcast.108, bf16[1920,256]{0,1:T(8,128)(2,1)} %collective-permute-done.20, bf16[2048,256]{1,0:T(8,128)(2,1)} %collective-permute-done.19, pred[]{:T(512)S(6)} %eq.94, bf16[1024,256]{1,0:T(8,128)(2,1)S(1)} %get-tuple-element.30, ...), kind=kOutput, calls=%fused_computation.5 | convolution fusion | flops 2016870400 | bytes 12910593 | tf_op jit(solution)/shard_map/dot_general | solution.py:19
  161.5 1.3 collective-permute-start.21
  162.8 2.0 fusion.14
  165.7 9.3 %collective-permute-done.21 = bf16[1920,128]{0,1:T(8,128)(2,1)S(1)} collective-permute-done((bf16[1920,128]{0,1:T(8,128)(2,1)S(1)}, bf16[1920,128]{0,1:T(8,128)(2,1)S(1)}, u32[]{:S(2)}, u32[]{:S(2)}) %collective-permute-start.21) | collective-permute-done | bytes 491552 | tf_op jit(solution)/shard_map/ppermute | solution.py:15
  175.0 1.0 collective-permute-start.27
  178.6 7.6 %collective-permute-done.29 = bf16[1920,128]{0,1:T(8,128)(2,1)S(1)} collective-permute-done((bf16[1920,128]{0,1:T(8,128)(2,1)S(1)}, bf16[1920,128]{0,1:T(8,128)(2,1)S(1)}, u32[]{:S(2)}, u32[]{:S(2)}) %collective-permute-start.29) | collective-permute-done | bytes 491552 | tf_op jit(solution)/shard_map/ppermute | solution.py:15
  186.2 1.2 collective-permute-start.30
  187.9 8.3 %collective-permute-done.30 = bf16[1920,128]{0,1:T(8,128)(2,1)S(1)} collective-permute-done((bf16[1920,128]{0,1:T(8,128)(2,1)S(1)}, bf16[1920,128]{0,1:T(8,128)(2,1)S(1)}, u32[]{:S(2)}, u32[]{:S(2)}) %collective-permute-start.30) | collective-permute-done | bytes 491552 | tf_op jit(solution)/shard_map/ppermute | solution.py:15
  200.9 15.8 %collective-permute-start.22 = (bf16[12,48,256]{2,1,0:T(8,128)(2,1)S(1)}, bf16[12,48,256]{2,1,0:T(8,128)(2,1)S(1)}, u32[]{:S(2)}, u32[]{:S(2)}) collective-permute-start(bf16[12,48,256]{2,1,0:T(8,128)(2,1)S(1)} %pad_maximum_fusion.8), channel_id=1, source_target_pairs={{0,1},{1,2},{2,3},{3,0},{4,5},{5,6},{6,7},{7,4},{8,9},{9,10},{10,1... | collective-permute-start | bytes 884744 | tf_op jit(solution)/shard_map/ppermute | solution.py:11
  216.8 6.4 %collective-permute-done.22 = bf16[12,48,256]{2,1,0:T(8,128)(2,1)S(1)} collective-permute-done((bf16[12,48,256]{2,1,0:T(8,128)(2,1)S(1)}, bf16[12,48,256]{2,1,0:T(8,128)(2,1)S(1)}, u32[]{:S(2)}, u32[]{:S(2)}) %collective-permute-start.22) | collective-permute-done | bytes 294944 | tf_op jit(solution)/shard_map/ppermute | solution.py:11
  223.3 2.3 collective-permute-start.23
  225.9 12.9 %collective-permute-done.23 = bf16[12,48,256]{2,1,0:T(8,128)(2,1)S(1)} collective-permute-done((bf16[12,48,256]{2,1,0:T(8,128)(2,1)S(1)}, bf16[12,48,256]{2,1,0:T(8,128)(2,1)S(1)}, u32[]{:S(2)}, u32[]{:S(2)}) %collective-permute-start.23) | collective-permute-done | bytes 294944 | tf_op jit(solution)/shard_map/ppermute | solution.py:11
  240.7 1.2 collective-permute-start.26
  242.0 6.3 %collective-permute-done.32 = bf16[12,48,256]{2,1,0:T(8,128)(2,1)S(1)} collective-permute-done((bf16[12,48,256]{2,1,0:T(8,128)(2,1)S(1)}, bf16[12,48,256]{2,1,0:T(8,128)(2,1)S(1)}, u32[]{:S(2)}, u32[]{:S(2)}) %collective-permute-start.32) | collective-permute-done | bytes 294944 | tf_op jit(solution)/shard_map/ppermute | solution.py:11
  249.0 12.2 %collective-permute-done.33 = bf16[12,48,256]{2,1,0:T(8,128)(2,1)S(1)} collective-permute-done((bf16[12,48,256]{2,1,0:T(8,128)(2,1)S(1)}, bf16[12,48,256]{2,1,0:T(8,128)(2,1)S(1)}, u32[]{:S(2)}, u32[]{:S(2)}) %collective-permute-start.33) | collective-permute-done | bytes 294944 | tf_op jit(solution)/shard_map/ppermute | solution.py:11
  263.0 1.3 collective-permute-start.36
  265.1 2.7 collective-permute-done.35
  267.9 1.3 collective-permute-done.36
  270.3 1.1 pad_maximum_fusion.6
  271.4 2.1 copy.19
  (134 shorter events, 20.8 us)
Async XLA Ops:
  1.6 9.4 %collective-permute-start = (bf16[1024,128]{1,0:T(8,128)(2,1)S(1)}, bf16[1024,128]{1,0:T(8,128)(2,1)S(1)}, u32[]{:S(2)}, u32[]{:S(2)}) collective-permute-start(bf16[1024,128]{1,0:T(8,128)(2,1)S(1)} %get-tuple-element.27), channel_id=1, source_target_pairs={{0,8},{4,12},{8,0},{12,4},{1,9},{5,13},{9,1},{13,5},{2,10},{6,14},... | collective-permute-start | bytes 786440 | tf_op jit(solution)/shard_map/ppermute | solution.py:15
  10.9 7.5 %collective-permute-start.15 = (bf16[1024,128]{1,0:T(8,128)(2,1)S(1)}, bf16[1024,128]{1,0:T(8,128)(2,1)S(1)}, u32[]{:S(2)}, u32[]{:S(2)}) collective-permute-start(bf16[1024,128]{1,0:T(8,128)(2,1)S(1)} %get-tuple-element.12), channel_id=1, source_target_pairs={{0,8},{4,12},{8,0},{12,4},{1,9},{5,13},{9,1},{13,5},{2,10},{6,14},... | collective-permute-start | bytes 786440 | tf_op jit(solution)/shard_map/ppermute | solution.py:15
  20.2 4.4 %collective-permute-start.1 = (bf16[1024,128]{1,0:T(8,128)(2,1)S(1)}, bf16[1024,128]{1,0:T(8,128)(2,1)S(1)}, u32[]{:S(2)}, u32[]{:S(2)}) collective-permute-start(bf16[1024,128]{1,0:T(8,128)(2,1)S(1)} %get-tuple-element.25), channel_id=1, source_target_pairs={{0,0},{1,4},{2,6},{3,2},{4,1},{5,5},{6,7},{7,3},{8,8},{9,12},{10,1... | collective-permute-start | bytes 786440 | tf_op jit(solution)/shard_map/ppermute | solution.py:130
  20.8 14.6 %collective-permute-start.2 = (bf16[1024,128]{1,0:T(8,128)(2,1)S(1)}, bf16[1024,128]{1,0:T(8,128)(2,1)S(1)}, u32[]{:S(2)}, u32[]{:S(2)}) collective-permute-start(bf16[1024,128]{1,0:T(8,128)(2,1)S(1)} %get-tuple-element.26), channel_id=1, source_target_pairs={{0,2},{1,6},{2,4},{3,0},{4,3},{5,7},{6,5},{7,1},{8,10},{9,14},{10,... | collective-permute-start | bytes 786440 | tf_op jit(solution)/shard_map/ppermute | solution.py:130
  35.5 14.2 %collective-permute-start.3 = (bf16[1024,256]{1,0:T(8,128)(2,1)S(1)}, bf16[1024,256]{1,0:T(8,128)(2,1)S(1)}, u32[]{:S(2)}, u32[]{:S(2)}) collective-permute-start(bf16[1024,256]{1,0:T(8,128)(2,1)S(1)} %constant_dynamic-update-slice_fusion), channel_id=1, source_target_pairs={{0,8},{4,12},{8,0},{12,4},{1,9},{5,13},{9,1},{13,5},{2,10},{6,14},... | collective-permute-start | bytes 1572872 | tf_op jit(solution)/shard_map/ppermute | solution.py:15
  49.9 15.8 %collective-permute-start.4 = (bf16[2048,256]{1,0:T(8,128)(2,1)S(1)}, bf16[2048,256]{1,0:T(8,128)(2,1)}, u32[]{:S(2)}, u32[]{:S(2)}) collective-permute-start(bf16[2048,256]{1,0:T(8,128)(2,1)S(1)} %pad_maximum_fusion), channel_id=1, source_target_pairs={{0,4},{4,0},{8,12},{12,8},{1,5},{5,1},{9,13},{13,9},{2,6},{6,2},{1... | collective-permute-start | bytes 3145736 | tf_op jit(solution)/shard_map/ppermute | solution.py:15
  50.0 3.1 %collective-permute-start.16 = (bf16[1024,128]{1,0:T(8,128)(2,1)S(1)}, bf16[1024,128]{1,0:T(8,128)(2,1)S(1)}, u32[]{:S(2)}, u32[]{:S(2)}) collective-permute-start(bf16[1024,128]{1,0:T(8,128)(2,1)S(1)} %get-tuple-element.13), channel_id=1, source_target_pairs={{0,0},{1,4},{2,6},{3,2},{4,1},{5,5},{6,7},{7,3},{8,8},{9,12},{10,1... | collective-permute-start | bytes 786440 | tf_op jit(solution)/shard_map/ppermute | solution.py:130
  50.7 13.4 %collective-permute-start.17 = (bf16[1024,128]{1,0:T(8,128)(2,1)S(1)}, bf16[1024,128]{1,0:T(8,128)(2,1)S(1)}, u32[]{:S(2)}, u32[]{:S(2)}) collective-permute-start(bf16[1024,128]{1,0:T(8,128)(2,1)S(1)} %get-tuple-element.14), channel_id=1, source_target_pairs={{0,2},{1,6},{2,4},{3,0},{4,3},{5,7},{6,5},{7,1},{8,10},{9,14},{10,... | collective-permute-start | bytes 786440 | tf_op jit(solution)/shard_map/ppermute | solution.py:130
  64.1 33.8 %slice-start.3 = ((s8[7864320]{0:T(1024)(128)(4,1)}), s8[4194304]{0:T(1024)(128)(4,1)S(1)}, s32[]{:S(2)}) async-start(s8[7864320]{0:T(1024)(128)(4,1)} %bitcast.105), calls=%async_computation.3 | async-start | bytes 8388608
  64.1 10.2 %copy-start.5 = (bf16[2048]{0:T(1024)(128)(2,1)S(1)}, bf16[2048]{0:T(1024)(128)(2,1)}, u32[]{:S(2)}) copy-start(bf16[2048]{0:T(1024)(128)(2,1)} %param.10) | copy-start | bytes 12292
  64.2 11.0 %copy-start = (bf16[2048,512]{1,0:T(8,128)(2,1)S(1)}, bf16[2048,512]{1,0:T(8,128)(2,1)}, u32[]{:S(2)}) copy-start(bf16[2048,512]{1,0:T(8,128)(2,1)} %param.11) | copy-start | bytes 6291460
  64.2 33.7 %slice-start.4 = ((s8[7864320]{0:T(1024)(128)(4,1)}), s8[3670016]{0:T(1024)(128)(4,1)S(1)}, s32[]{:S(2)}) async-start(s8[7864320]{0:T(1024)(128)(4,1)} %bitcast.105), calls=%async_computation.4 | async-start | bytes 7340032
  64.2 33.4 %collective-permute-start.18 = (bf16[1024,256]{1,0:T(8,128)(2,1)S(1)}, bf16[1024,256]{1,0:T(8,128)(2,1)S(1)}, u32[]{:S(2)}, u32[]{:S(2)}) collective-permute-start(bf16[1024,256]{1,0:T(8,128)(2,1)S(1)} %pad_maximum_fusion.7), channel_id=1, source_target_pairs={{0,8},{4,12},{8,0},{12,4},{1,9},{5,13},{9,1},{13,5},{2,10},{6,14},... | collective-permute-start | bytes 1572872 | tf_op jit(solution)/shard_map/ppermute | solution.py:15
  72.5 25.4 %collective-permute-start.5 = (bf16[1920,256]{0,1:T(8,128)(2,1)S(1)}, bf16[1920,256]{0,1:T(8,128)(2,1)S(1)}, u32[]{:S(2)}, u32[]{:S(2)}) collective-permute-start(bf16[1920,256]{0,1:T(8,128)(2,1)S(1)} %fusion.2), channel_id=1, source_target_pairs={{0,1},{1,0},{2,3},{3,2},{4,5},{5,4},{6,7},{7,6},{8,9},{9,8},{10,11... | collective-permute-start | bytes 2949128 | tf_op jit(solution)/shard_map/ppermute | solution.py:15
  74.3 0.8 collective-permute-start.12
  75.6 27.8 %collective-permute-start.13 = (f32[1,512]{1,0:T(1,128)S(1)}, f32[1,512]{1,0:T(1,128)S(1)}, u32[]{:S(2)}, u32[]{:S(2)}) collective-permute-start(f32[1,512]{1,0:T(1,128)S(1)} %fusion.80), channel_id=1, source_target_pairs={{0,4},{4,0},{8,12},{12,8},{1,5},{5,1},{9,13},{13,9},{2,6},{6,2},{1... | collective-permute-start | bytes 6152 | tf_op jit(solution)/shard_map/ppermute | solution.py:15
  97.7 6.2 %copy-start.6 = (s32[4]{0:T(128)S(1)}, s32[4]{0:T(128)}, u32[]{:S(2)}) copy-start(s32[4]{0:T(128)} %param.14) | copy-start | bytes 52
  97.7 6.2 %copy-start.2 = (s32[4,4]{1,0:T(4,128)S(1)}, s32[4,4]{1,0:T(4,128)}, u32[]{:S(2)}) copy-start(s32[4,4]{1,0:T(4,128)} %param.13) | copy-start | bytes 196
  97.8 22.2 %collective-permute-start.19 = (bf16[2048,256]{1,0:T(8,128)(2,1)S(1)}, bf16[2048,256]{1,0:T(8,128)(2,1)}, u32[]{:S(2)}, u32[]{:S(2)}) collective-permute-start(bf16[2048,256]{1,0:T(8,128)(2,1)S(1)} %pad_maximum_fusion.1), channel_id=1, source_target_pairs={{0,4},{4,0},{8,12},{12,8},{1,5},{5,1},{9,13},{13,9},{2,6},{6,2},{1... | collective-permute-start | bytes 3145736 | tf_op jit(solution)/shard_map/ppermute | solution.py:15
  101.7 15.4 %collective-permute-start.6 = (bf16[1920,128]{0,1:T(8,128)(2,1)S(1)}, bf16[1920,128]{0,1:T(8,128)(2,1)S(1)}, u32[]{:S(2)}, u32[]{:S(2)}) collective-permute-start(bf16[1920,128]{0,1:T(8,128)(2,1)S(1)} %slice.139), channel_id=1, source_target_pairs={{0,3},{1,2},{2,1},{3,0},{4,7},{5,6},{6,5},{7,4},{8,11},{9,10},{10,... | collective-permute-start | bytes 1474568 | tf_op jit(solution)/shard_map/ppermute | solution.py:15
  103.4 3.7 %collective-permute-start.14 = (f32[1,512]{1,0:T(1,128)S(1)}, f32[1,512]{1,0:T(1,128)S(1)}, u32[]{:S(2)}, u32[]{:S(2)}) collective-permute-start(f32[1,512]{1,0:T(1,128)S(1)} %add.192), channel_id=1, source_target_pairs={{0,8},{4,12},{8,0},{12,4},{1,9},{5,13},{9,1},{13,5},{2,10},{6,14},... | collective-permute-start | bytes 6152 | tf_op jit(solution)/shard_map/ppermute | solution.py:15
  117.1 40.7 %slice-start.5 = ((s8[7864320]{0:T(1024)(128)(4,1)}), s8[4194304]{0:T(1024)(128)(4,1)S(1)}, s32[]{:S(2)}) async-start(s8[7864320]{0:T(1024)(128)(4,1)} %bitcast.107), calls=%async_computation.5 | async-start | bytes 8388608
  118.5 39.3 %slice-start.6 = ((s8[7864320]{0:T(1024)(128)(4,1)}), s8[3670016]{0:T(1024)(128)(4,1)S(1)}, s32[]{:S(2)}) async-start(s8[7864320]{0:T(1024)(128)(4,1)} %bitcast.107), calls=%async_computation.6 | async-start | bytes 7340032
  118.5 18.6 %collective-permute-start.7 = (bf16[1920,128]{0,1:T(8,128)(2,1)S(1)}, bf16[1920,128]{0,1:T(8,128)(2,1)S(1)}, u32[]{:S(2)}, u32[]{:S(2)}) collective-permute-start(bf16[1920,128]{0,1:T(8,128)(2,1)S(1)} %fusion.47), channel_id=1, source_target_pairs={{0,16},{16,0},{1,17},{17,1},{2,18},{18,2},{3,19},{19,3},{4,20},{20... | collective-permute-start | bytes 1474568 | tf_op jit(solution)/shard_map/ppermute | solution.py:15
  125.9 14.0 %collective-permute-start.9 = (bf16[1920,128]{0,1:T(8,128)(2,1)S(1)}, bf16[1920,128]{0,1:T(8,128)(2,1)S(1)}, u32[]{:S(2)}, u32[]{:S(2)}) collective-permute-start(bf16[1920,128]{0,1:T(8,128)(2,1)S(1)} %fusion.47), channel_id=1, source_target_pairs={{0,8},{4,12},{8,0},{12,4},{1,9},{5,13},{9,1},{13,5},{2,10},{6,14},... | collective-permute-start | bytes 1474568 | tf_op jit(solution)/shard_map/ppermute | solution.py:15
  126.9 31.0 %collective-permute-start.20 = (bf16[1920,256]{0,1:T(8,128)(2,1)S(1)}, bf16[1920,256]{0,1:T(8,128)(2,1)}, u32[]{:S(2)}, u32[]{:S(2)}) collective-permute-start(bf16[1920,256]{0,1:T(8,128)(2,1)S(1)} %fusion.3), channel_id=1, source_target_pairs={{0,1},{1,0},{2,3},{3,2},{4,5},{5,4},{6,7},{7,6},{8,9},{9,8},{10,11... | collective-permute-start | bytes 2949128 | tf_op jit(solution)/shard_map/ppermute | solution.py:15
  137.1 12.4 %collective-permute-start.10 = (bf16[1920,128]{0,1:T(8,128)(2,1)S(1)}, bf16[1920,128]{0,1:T(8,128)(2,1)S(1)}, u32[]{:S(2)}, u32[]{:S(2)}) collective-permute-start(bf16[1920,128]{0,1:T(8,128)(2,1)S(1)} %collective-permute-done.7), channel_id=1, source_target_pairs={{0,8},{4,12},{8,0},{12,4},{1,9},{5,13},{9,1},{13,5},{2,10},{6,14},... | collective-permute-start | bytes 1474568 | tf_op jit(solution)/shard_map/ppermute | solution.py:15
  137.4 25.4 %collective-permute-start.8 = (bf16[1920,256]{0,1:T(8,128)(2,1)S(1)}, bf16[1920,256]{0,1:T(8,128)(2,1)}, u32[]{:S(2)}, u32[]{:S(2)}) collective-permute-start(bf16[1920,256]{0,1:T(8,128)(2,1)S(1)} %pad_maximum_fusion.2), channel_id=1, source_target_pairs={{0,4},{4,0},{8,12},{12,8},{1,5},{5,1},{9,13},{13,9},{2,6},{6,2},{1... | collective-permute-start | bytes 2949128 | tf_op jit(solution)/shard_map/ppermute | solution.py:15
  149.7 13.1 %slice-start = ((s8[8847360]{0:T(1024)(128)(4,1)}), s8[4194304]{0:T(1024)(128)(4,1)S(1)}, s32[]{:S(2)}) async-start(s8[8847360]{0:T(1024)(128)(4,1)} %bitcast.95), calls=%async_computation | async-start | bytes 8388608
  149.8 13.0 %slice-start.1 = ((s8[8847360]{0:T(1024)(128)(4,1)}), s8[4194304]{0:T(1024)(128)(4,1)S(1)}, s32[]{:S(2)}) async-start(s8[8847360]{0:T(1024)(128)(4,1)} %bitcast.95), calls=%async_computation.1 | async-start | bytes 8388608
  149.8 13.0 %slice-start.2 = ((s8[8847360]{0:T(1024)(128)(4,1)}), s8[458752]{0:T(1024)(128)(4,1)S(1)}, s32[]{:S(2)}) async-start(s8[8847360]{0:T(1024)(128)(4,1)} %bitcast.95), calls=%async_computation.2 | async-start | bytes 917504
  149.8 26.9 %collective-permute-start.11 = (bf16[1920,256]{0,1:T(8,128)(2,1)S(1)}, bf16[1920,256]{0,1:T(8,128)(2,1)S(1)}, u32[]{:S(2)}, u32[]{:S(2)}) collective-permute-start(bf16[1920,256]{0,1:T(8,128)(2,1)S(1)} %pad_maximum_fusion.3), channel_id=1, source_target_pairs={{0,4},{4,0},{8,12},{12,8},{1,5},{5,1},{9,13},{13,9},{2,6},{6,2},{1... | collective-permute-start | bytes 2949128 | tf_op jit(solution)/shard_map/ppermute | solution.py:15
  161.5 13.4 %collective-permute-start.21 = (bf16[1920,128]{0,1:T(8,128)(2,1)S(1)}, bf16[1920,128]{0,1:T(8,128)(2,1)S(1)}, u32[]{:S(2)}, u32[]{:S(2)}) collective-permute-start(bf16[1920,128]{0,1:T(8,128)(2,1)S(1)} %slice.138), channel_id=1, source_target_pairs={{0,3},{1,2},{2,1},{3,0},{4,7},{5,6},{6,5},{7,4},{8,11},{9,10},{10,... | collective-permute-start | bytes 1474568 | tf_op jit(solution)/shard_map/ppermute | solution.py:15
  175.0 12.3 %collective-permute-start.27 = (bf16[1920,128]{0,1:T(8,128)(2,1)S(1)}, bf16[1920,128]{0,1:T(8,128)(2,1)S(1)}, u32[]{:S(2)}, u32[]{:S(2)}) collective-permute-start(bf16[1920,128]{0,1:T(8,128)(2,1)S(1)} %fusion.46), channel_id=1, source_target_pairs={{0,16},{16,0},{1,17},{17,1},{2,18},{18,2},{3,19},{19,3},{4,20},{20... | collective-permute-start | bytes 1474568 | tf_op jit(solution)/shard_map/ppermute | solution.py:15
  176.0 10.2 %collective-permute-start.29 = (bf16[1920,128]{0,1:T(8,128)(2,1)S(1)}, bf16[1920,128]{0,1:T(8,128)(2,1)S(1)}, u32[]{:S(2)}, u32[]{:S(2)}) collective-permute-start(bf16[1920,128]{0,1:T(8,128)(2,1)S(1)} %fusion.46), channel_id=1, source_target_pairs={{0,8},{4,12},{8,0},{12,4},{1,9},{5,13},{9,1},{13,5},{2,10},{6,14},... | collective-permute-start | bytes 1474568 | tf_op jit(solution)/shard_map/ppermute | solution.py:15
  186.2 10.0 %collective-permute-start.30 = (bf16[1920,128]{0,1:T(8,128)(2,1)S(1)}, bf16[1920,128]{0,1:T(8,128)(2,1)S(1)}, u32[]{:S(2)}, u32[]{:S(2)}) collective-permute-start(bf16[1920,128]{0,1:T(8,128)(2,1)S(1)} %collective-permute-done.29), channel_id=1, source_target_pairs={{0,16},{16,0},{1,17},{17,1},{2,18},{18,2},{3,19},{19,3},{4,20},{20... | collective-permute-start | bytes 1474568 | tf_op jit(solution)/shard_map/ppermute | solution.py:15
  187.6 8.9 %collective-permute-start.28 = (bf16[1920,256]{0,1:T(8,128)(2,1)S(1)}, bf16[1920,256]{0,1:T(8,128)(2,1)S(1)}, u32[]{:S(2)}, u32[]{:S(2)}) collective-permute-start(bf16[1920,256]{0,1:T(8,128)(2,1)S(1)} %pad_maximum_fusion.4), channel_id=1, source_target_pairs={{0,4},{4,0},{8,12},{12,8},{1,5},{5,1},{9,13},{13,9},{2,6},{6,2},{1... | collective-permute-start | bytes 2949128 | tf_op jit(solution)/shard_map/ppermute | solution.py:15
  196.4 2.6 collective-permute-start.31
  200.9 22.3 %collective-permute-start.22 = (bf16[12,48,256]{2,1,0:T(8,128)(2,1)S(1)}, bf16[12,48,256]{2,1,0:T(8,128)(2,1)S(1)}, u32[]{:S(2)}, u32[]{:S(2)}) collective-permute-start(bf16[12,48,256]{2,1,0:T(8,128)(2,1)S(1)} %pad_maximum_fusion.8), channel_id=1, source_target_pairs={{0,1},{1,2},{2,3},{3,0},{4,5},{5,6},{6,7},{7,4},{8,9},{9,10},{10,1... | collective-permute-start | bytes 884744 | tf_op jit(solution)/shard_map/ppermute | solution.py:11
  223.3 15.5 %collective-permute-start.23 = (bf16[12,48,256]{2,1,0:T(8,128)(2,1)S(1)}, bf16[12,48,256]{2,1,0:T(8,128)(2,1)S(1)}, u32[]{:S(2)}, u32[]{:S(2)}) collective-permute-start(bf16[12,48,256]{2,1,0:T(8,128)(2,1)S(1)} %broadcast_select_fusion.13), channel_id=1, source_target_pairs={{0,2},{1,3},{2,0},{3,1},{4,6},{5,7},{6,4},{7,5},{8,10},{9,11},{10,... | collective-permute-start | bytes 884744 | tf_op jit(solution)/shard_map/ppermute | solution.py:11
  239.1 9.1 %collective-permute-start.32 = (bf16[12,48,256]{2,1,0:T(8,128)(2,1)S(1)}, bf16[12,48,256]{2,1,0:T(8,128)(2,1)S(1)}, u32[]{:S(2)}, u32[]{:S(2)}) collective-permute-start(bf16[12,48,256]{2,1,0:T(8,128)(2,1)S(1)} %pad_maximum_fusion.9), channel_id=1, source_target_pairs={{0,1},{1,2},{2,3},{3,0},{4,5},{5,6},{6,7},{7,4},{8,9},{9,10},{10,1... | collective-permute-start | bytes 884744 | tf_op jit(solution)/shard_map/ppermute | solution.py:11
  239.7 8.9 %collective-permute-start.24 = (bf16[4,48,2,1,128]{4,2,1,0,3:T(2,128)(2,1)S(1)}, bf16[4,48,2,1,128]{4,2,1,0,3:T(2,128)(2,1)S(1)}, u32[]{:S(2)}, u32[]{:S(2)}) collective-permute-start(bf16[4,48,2,1,128]{4,2,1,0,3:T(2,128)(2,1)S(1)} %squeeze.25), channel_id=1, source_target_pairs={{0,4},{4,0},{8,12},{12,8},{1,5},{5,1},{9,13},{13,9},{2,6},{6,2},{1... | collective-permute-start | bytes 294920 | tf_op jit(solution)/shard_map/ppermute | solution.py:15
  239.9 8.7 %collective-permute-start.25 = (bf16[4,48,2,1,128]{4,2,1,0,3:T(2,128)(2,1)S(1)}, bf16[4,48,2,1,128]{4,2,1,0,3:T(2,128)(2,1)S(1)}, u32[]{:S(2)}, u32[]{:S(2)}) collective-permute-start(bf16[4,48,2,1,128]{4,2,1,0,3:T(2,128)(2,1)S(1)} %squeeze.26), channel_id=1, source_target_pairs={{0,8},{4,12},{8,0},{12,4},{1,9},{5,13},{9,1},{13,5},{2,10},{6,14},... | collective-permute-start | bytes 294920 | tf_op jit(solution)/shard_map/ppermute | solution.py:15
  240.7 7.8 %collective-permute-start.26 = (bf16[4,48,2,1,128]{4,2,1,0,3:T(2,128)(2,1)S(1)}, bf16[4,48,2,1,128]{4,2,1,0,3:T(2,128)(2,1)S(1)}, u32[]{:S(2)}, u32[]{:S(2)}) collective-permute-start(bf16[4,48,2,1,128]{4,2,1,0,3:T(2,128)(2,1)S(1)} %squeeze.27), channel_id=1, source_target_pairs={{0,12},{4,8},{8,4},{12,0},{1,13},{5,9},{9,5},{13,1},{2,14},{6,10},... | collective-permute-start | bytes 294920 | tf_op jit(solution)/shard_map/ppermute | solution.py:15
  248.4 12.9 %collective-permute-start.33 = (bf16[12,48,256]{2,1,0:T(8,128)(2,1)S(1)}, bf16[12,48,256]{2,1,0:T(8,128)(2,1)S(1)}, u32[]{:S(2)}, u32[]{:S(2)}) collective-permute-start(bf16[12,48,256]{2,1,0:T(8,128)(2,1)S(1)} %broadcast_select_fusion.12), channel_id=1, source_target_pairs={{0,2},{1,3},{2,0},{3,1},{4,6},{5,7},{6,4},{7,5},{8,10},{9,11},{10,... | collective-permute-start | bytes 884744 | tf_op jit(solution)/shard_map/ppermute | solution.py:11
  262.0 3.1 %collective-permute-start.34 = (bf16[4,48,2,1,128]{4,2,1,0,3:T(2,128)(2,1)S(1)}, bf16[4,48,2,1,128]{4,2,1,0,3:T(2,128)(2,1)S(1)}, u32[]{:S(2)}, u32[]{:S(2)}) collective-permute-start(bf16[4,48,2,1,128]{4,2,1,0,3:T(2,128)(2,1)S(1)} %squeeze.29), channel_id=1, source_target_pairs={{0,4},{4,0},{8,12},{12,8},{1,5},{5,1},{9,13},{13,9},{2,6},{6,2},{1... | collective-permute-start | bytes 294920 | tf_op jit(solution)/shard_map/ppermute | solution.py:15
  262.2 5.7 %collective-permute-start.35 = (bf16[4,48,2,1,128]{4,2,1,0,3:T(2,128)(2,1)S(1)}, bf16[4,48,2,1,128]{4,2,1,0,3:T(2,128)(2,1)S(1)}, u32[]{:S(2)}, u32[]{:S(2)}) collective-permute-start(bf16[4,48,2,1,128]{4,2,1,0,3:T(2,128)(2,1)S(1)} %squeeze.30), channel_id=1, source_target_pairs={{0,8},{4,12},{8,0},{12,4},{1,9},{5,13},{9,1},{13,5},{2,10},{6,14},... | collective-permute-start | bytes 294920 | tf_op jit(solution)/shard_map/ppermute | solution.py:15
  263.0 6.2 %collective-permute-start.36 = (bf16[4,48,2,1,128]{4,2,1,0,3:T(2,128)(2,1)S(1)}, bf16[4,48,2,1,128]{4,2,1,0,3:T(2,128)(2,1)S(1)}, u32[]{:S(2)}, u32[]{:S(2)}) collective-permute-start(bf16[4,48,2,1,128]{4,2,1,0,3:T(2,128)(2,1)S(1)} %squeeze.31), channel_id=1, source_target_pairs={{0,12},{4,8},{8,4},{12,0},{1,13},{5,9},{9,5},{13,1},{2,14},{6,10},... | collective-permute-start | bytes 294920 | tf_op jit(solution)/shard_map/ppermute | solution.py:15
  (3 other events, 7.7 us)

commit v4 on v3

--- a/solution.py
+++ b/solution.py
@@ -115,13 +115,6 @@
     ]
     half = kv_weight.shape[0] // 2
 
-    def cross_chips(part, before):
-        column = (group * 2 + part) * head_dim
-        mine = lax.dynamic_slice_in_dim(kv_weight, column, head_dim, axis=1)
-        stays = lax.dynamic_slice_in_dim(mine, tile // 2 * half, half, axis=0)
-        leaves = lax.dynamic_slice_in_dim(mine, half - tile // 2 * half, half, axis=0)
-        return stays, swapped(after(leaves, before), "tile", 2)
-
     def cross_planes(stays, comes, before):
         pieces = []
         for j in range(2):
@@ -130,28 +123,41 @@
             pieces.append(lax.ppermute(piece, ("tile", "head"), rounds[j]))
         return jnp.concatenate(pieces, axis=1)
 
-    def within_plane(near_half):
-        other_half = swapped(near_half, "tile", 2)
+    def whole_rows(near_half, other_half):
         top = jnp.where(first_chip, near_half, other_half)
         bottom = jnp.where(first_chip, other_half, near_half)
-        near = jnp.concatenate([top, bottom], axis=0)
-        return near, swapped(near, "tile", 1)
-
-    def sum_over_planes(near, far, before):
-        far_leaves = at_end == first_core
-        outer = add_columns(proj_weight, jnp.where(far_leaves, far, near)).astype(jnp.bfloat16)
-        pair_sum = add_columns(proj_weight, jnp.where(far_leaves, near, far))
-        pair_sum = pair_sum + swapped(after(outer, before), "head", 1).astype(jnp.float32)
+        return jnp.concatenate([top, bottom], axis=0)
+
+    far_leaves = at_end == first_core
+
+    def products(near, far):
+        leaves = add_columns(proj_weight, jnp.where(far_leaves, far, near)).astype(jnp.bfloat16)
+        stays = after(jnp.where(far_leaves, near, far), leaves)
+        return leaves, add_columns(proj_weight, stays)
+
+    def mirror_sum(pair_sum):
         mirrored = swapped(pair_sum[:, width:].astype(jnp.bfloat16), "head", 3)
         return (pair_sum[:, :width] + mirrored.astype(jnp.float32)).astype(jnp.bfloat16)
+
+    def other_chips(own):
+        diagonal = [
+            ((g * 4 + t) * 4 + h, ((1 - g) * 4 + (t ^ 2)) * 4 + h)
+            for g in range(2)
+            for t in range(4)
+            for h in range(4)
+        ]
+        return (
+            swapped(own, "tile", 2),
+            swapped(own, "groups", 1),
+            lax.ppermute(own, ("groups", "tile", "head"), diagonal),
+        )
 
     def both_heads(ours, theirs):
         left, right = jnp.where(group == 0, ours, theirs), jnp.where(group == 0, theirs, ours)
         return lax.optimization_barrier(jnp.concatenate([left, right], axis=1))
 
-    def times_features(own, part):
-        across_x, across_y = swapped(own, "tile", 2), swapped(own, "groups", 1)
-        diagonal = swapped(across_y, "tile", 2) if part == 0 else swapped(across_x, "groups", 1)
+    def times_features(own, others):
+        across_x, across_y, diagonal = others
         rows_0, rows_2 = both_heads(own, across_y), both_heads(across_x, diagonal)
         rows = [rows_0, swapped(rows_0, "tile", 1), rows_2, swapped(rows_2, "tile", 1)]
         return sum(add_columns(feature_parts[r], rows[r]) for r in range(4))
@@ -179,17 +185,28 @@
         ranked = [jnp.where(first_chip, even[r], even[r ^ 2]) for r in range(4)]
         return jnp.stack(ranked, axis=1), rolled
 
-    key_stays, key_comes = cross_chips(0, None)
-    value_stays, value_comes = cross_chips(1, key_comes)
-    key_half = cross_planes(key_stays, key_comes, None)
-    value_half = cross_planes(value_stays, value_comes, key_half)
-    key_near, key_far = within_plane(key_half)
-    value_near, value_far = within_plane(after(value_half, key_near))
-    key_own = sum_over_planes(key_near, key_far, None)
-    value_own = sum_over_planes(value_near, value_far, key_own)
-    keys = finish(times_features(key_own, 0), 0)
-    values = finish(times_features(value_own, 1), 1)
+    mine = lax.dynamic_slice_in_dim(kv_weight, group * 2 * head_dim, 2 * head_dim, axis=1)
+    stays = lax.dynamic_slice_in_dim(mine, tile // 2 * half, half, axis=0)
+    leaves = lax.dynamic_slice_in_dim(mine, half - tile // 2 * half, half, axis=0)
+    comes = swapped(leaves, "tile", 2)
+    key_half = cross_planes(stays[:, :width], comes[:, :width], None)
+    key_half = after(key_half, bias_part)
+    value_half = cross_planes(stays[:, width:], comes[:, width:], key_half)
+    key_near = whole_rows(key_half, swapped(key_half, "tile", 2))
+    key_near = after(key_near, value_half)
+    key_leaves, key_stays = products(key_near, swapped(key_near, "tile", 1))
+    value_other = after(swapped(value_half, "tile", 2), key_stays)
+    value_near = whole_rows(value_half, value_other)
+    value_leaves, value_stays = products(value_near, swapped(value_near, "tile", 1))
+    key_comes = after(swapped(key_leaves, "head", 1), value_stays)
+    key_own = mirror_sum(key_stays + key_comes.astype(jnp.float32))
+    key_others = other_chips(key_own)
+    value_comes = after(swapped(after(value_leaves, key_own), "head", 1), key_others)
+    value_pair = value_stays + value_comes.astype(jnp.float32)
+    value_own = mirror_sum(value_pair)
+    keys = finish(times_features(after(key_own, value_pair), key_others), 0)
     routed_keys, keys = route(keys, value_own)
+    values = finish(times_features(value_own, other_chips(value_own)), 1)
     routed_values, _ = route(values, keys)
     cache = jnp.stack([routed_keys, routed_values], axis=-2)
     return cache.reshape(1, 1, most_tiles * 4 * shard_len, 4 * layers, head_dim)

time: 274 us -> 255 us (0.931)
  starting transfers between devices: 82 us -> 61.1 us
  waiting for transfers between devices: 148 us -> 155 us
  matrix products: 27.5 us -> 23.3 us
    ppermute x28 -> x25, starting transfers between devices: 55.5 us -> 33.2 us  [swapped(): lax.ppermute(shard, axis, [(i, i ^ bit) for i in range(lax.axis_size(axis...]
    ppermute x0 -> x2, waiting for transfers between devices: none -> 20 us  [other_chips(): lax.ppermute(own, ('groups', 'tile', 'head'), diagonal)]
    ppermute x4, waiting for transfers between devices: 21.8 us -> 14.3 us  [cross_planes(): pieces.append(lax.ppermute(piece, ('tile', 'head'), rounds[j]))]
    ppermute x28 -> x25, waiting for transfers between devices: 87.9 us -> 82.1 us  [swapped(): lax.ppermute(shard, axis, [(i, i ^ bit) for i in range(lax.axis_size(axis...]
    ppermute x4, starting transfers between devices: 18.2 us -> 12.8 us  [shifted_2(): lax.ppermute(shard, axis, [(i, (i + by) % count) for i in range(count)])]
    ppermute x0 -> x2, starting transfers between devices: none -> 4.27 us  [other_chips(): lax.ppermute(own, ('groups', 'tile', 'head'), diagonal)]
    dot_general x15, matrix products: 27.3 us -> 23.1 us  [add_columns(): return jnp.dot(operand, portion, preferred_element_type=jnp.float32)]
  transfers between devices with their start and end apart: 37 -> 36, of which waited for: 20 -> 23; matrix products, arithmetic and copies ran while one was open for 11% -> 11% of each run, Pallas kernels for 0% -> 0%
where the time goes in v4:
time: 255 us
  waiting for transfers between devices  155 us (61%)
  starting transfers between devices  61.1 us (24%)
  matrix products  23.3 us (9%)
  other arithmetic  9.25 us (4%)
  local copies, waits for them, and re-layouts  5.74 us (2%)
    ppermute x25, waiting for transfers between devices, swapped(): lax.ppermute(shard, axis, [(i, i ^ bit) for i in range(lax.axis_size(axis...  82.1 us
    ppermute x4, waiting for transfers between devices, shifted_2(): lax.ppermute(shard, axis, [(i, (i + by) % count) for i in range(count)])  38.8 us
    ppermute x25, starting transfers between devices, swapped(): lax.ppermute(shard, axis, [(i, i ^ bit) for i in range(lax.axis_size(axis...  33.2 us
    dot_general x15, matrix products, add_columns(): return jnp.dot(operand, portion, preferred_element_type=jnp.float32)  23.1 us
    ppermute x2, waiting for transfers between devices, other_chips(): lax.ppermute(own, ('groups', 'tile', 'head'), diagonal)  20 us
    ppermute x4, waiting for transfers between devices, cross_planes(): pieces.append(lax.ppermute(piece, ('tile', 'head'), rounds[j]))  14.3 us
    ppermute x4, starting transfers between devices, shifted_2(): lax.ppermute(shard, axis, [(i, (i + by) % count) for i in range(count)])  12.8 us
    ppermute x4, starting transfers between devices, cross_planes(): pieces.append(lax.ppermute(piece, ('tile', 'head'), rounds[j]))  9.56 us
  transfers between devices with their start and end apart: 36, of which 23 were waited for; matrix products, arithmetic and copies ran while one was open for 11% of the time, Pallas kernels for 0%

profile of v4, /device:TPU:0, one launch (start us, length us, event | category | flops | bytes accessed | tf_op | source)
XLA Modules:
  0.0 255.2 jit_solution(3855430141670817821)
XLA Ops:
  0.0 1.6 dynamic_slice.21
  1.6 3.0 %collective-permute-start = (bf16[1024,256]{1,0:T(8,128)(2,1)S(1)}, bf16[1024,256]{1,0:T(8,128)(2,1)S(1)}, u32[]{:S(2)}, u32[]{:S(2)}) collective-permute-start(bf16[1024,256]{1,0:T(8,128)(2,1)S(1)} %dynamic_slice.21), channel_id=1, source_target_pairs={{0,8},{4,12},{8,0},{12,4},{1,9},{5,13},{9,1},{13,5},{2,10},{6,14},... | collective-permute-start | bytes 1572872 | tf_op jit(solution)/shard_map/ppermute | solution.py:15
  4.6 1.3 collective-permute-start.3
  5.9 10.6 %collective-permute-done = bf16[1024,256]{1,0:T(8,128)(2,1)S(1)} collective-permute-done((bf16[1024,256]{1,0:T(8,128)(2,1)S(1)}, bf16[1024,256]{1,0:T(8,128)(2,1)S(1)}, u32[]{:S(2)}, u32[]{:S(2)}) %collective-permute-start) | collective-permute-done | bytes 524320 | tf_op jit(solution)/shard_map/ppermute | solution.py:15
  16.5 1.7 broadcast_select_fusion.18
  18.9 4.2 %collective-permute-start.2 = (bf16[1024,128]{1,0:T(8,128)(2,1)S(1)}, bf16[1024,128]{1,0:T(8,128)(2,1)S(1)}, u32[]{:S(2)}, u32[]{:S(2)}) collective-permute-start(bf16[1024,128]{1,0:T(8,128)(2,1)S(1)} %get-tuple-element.36), channel_id=1, source_target_pairs={{0,2},{1,6},{2,4},{3,0},{4,3},{5,7},{6,5},{7,1},{8,10},{9,14},{10,... | collective-permute-start | bytes 786440 | tf_op jit(solution)/shard_map/ppermute | solution.py:123
  23.5 1.6 collective-permute-start.4
  25.9 1.3 collective-permute-start.5
  27.3 2.2 collective-permute-done.5
  29.5 4.5 %collective-permute-done.2 = bf16[1024,128]{1,0:T(8,128)(2,1)S(1)} collective-permute-done((bf16[1024,128]{1,0:T(8,128)(2,1)S(1)}, bf16[1024,128]{1,0:T(8,128)(2,1)S(1)}, u32[]{:S(2)}, u32[]{:S(2)}) %collective-permute-start.2) | collective-permute-done | bytes 262176 | tf_op jit(solution)/shard_map/ppermute | solution.py:123
  34.1 1.3 collective-permute-start.6
  36.1 4.0 %collective-permute-start.8 = (bf16[1024,128]{1,0:T(8,128)(2,1)S(1)}, bf16[1024,128]{1,0:T(8,128)(2,1)S(1)}, u32[]{:S(2)}, u32[]{:S(2)}) collective-permute-start(bf16[1024,128]{1,0:T(8,128)(2,1)S(1)} %get-tuple-element.20), channel_id=1, source_target_pairs={{0,2},{1,6},{2,4},{3,0},{4,3},{5,7},{6,5},{7,1},{8,10},{9,14},{10,... | collective-permute-start | bytes 786440 | tf_op jit(solution)/shard_map/ppermute | solution.py:123
  40.2 9.7 %collective-permute-done.8 = bf16[1024,128]{1,0:T(8,128)(2,1)S(1)} collective-permute-done((bf16[1024,128]{1,0:T(8,128)(2,1)S(1)}, bf16[1024,128]{1,0:T(8,128)(2,1)S(1)}, u32[]{:S(2)}, u32[]{:S(2)}) %collective-permute-start.8) | collective-permute-done | bytes 262176 | tf_op jit(solution)/shard_map/ppermute | solution.py:123
  50.1 4.0 %collective-permute-start.9 = (bf16[2048,256]{1,0:T(8,128)(2,1)S(1)}, bf16[2048,256]{1,0:T(8,128)(2,1)S(1)}, u32[]{:S(2)}, u32[]{:S(2)}) collective-permute-start(bf16[2048,256]{1,0:T(8,128)(2,1)S(1)} %pad_maximum_fusion), channel_id=1, source_target_pairs={{0,4},{4,0},{8,12},{12,8},{1,5},{5,1},{9,13},{13,9},{2,6},{6,2},{1... | collective-permute-start | bytes 3145736 | tf_op jit(solution)/shard_map/ppermute | solution.py:15
  54.8 1.6 collective-permute-done.9
  56.6 5.8 %fusion = bf16[1920,256]{0,1:T(8,128)(2,1)S(1)} fusion(bf16[1920,2048]{1,0:T(8,128)(2,1)} %param.9, bf16[2048,256]{1,0:T(8,128)(2,1)S(1)} %collective-permute-done.9, bf16[2048,256]{1,0:T(8,128)(2,1)S(1)} %pad_maximum_fusion, pred[]{:T(512)S(6)} %eq.93), kind=kOutput, calls=%fused_computation.6 | convolution fusion | flops 2014281728 | bytes 10944513 | tf_op jit(solution)/shard_map/dot_general | solution.py:19
  62.4 2.4 convolution_bitcast_fusion.1
  64.8 3.3 %collective-permute-done.11 = bf16[1024,256]{1,0:T(8,128)(2,1)S(1)} collective-permute-done((bf16[1024,256]{1,0:T(8,128)(2,1)S(1)}, bf16[1024,256]{1,0:T(8,128)(2,1)S(1)}, u32[]{:S(2)}, u32[]{:S(2)}) %collective-permute-start.11) | collective-permute-done | bytes 524320 | tf_op jit(solution)/shard_map/ppermute | solution.py:15
  69.0 2.1 collective-permute-done.12
  71.0 3.3 %fusion.1 = bf16[1920,256]{0,1:T(8,128)(2,1)} fusion(bf16[1920,2048]{1,0:T(8,128)(2,1)S(1)} %bitcast.104, bf16[2048,256]{1,0:T(8,128)(2,1)S(1)} %collective-permute-done.12, pred[]{:T(512)S(6)} %eq.93, bf16[1024,256]{1,0:T(8,128)(2,1)S(1)} %get-tuple-element.38, bf16[1024,256]{1,0:T(8,128)(2,1)S(1)} %get-tuple-element.37), kind=kOutput, calls=%fused_computation.7 | convolution fusion | flops 2016378880 | bytes 10944513 | tf_op jit(solution)/shard_map/dot_general | solution.py:19
  74.6 2.5 convolution_bitcast_fusion
  77.1 15.5 %collective-permute-done.10 = bf16[1920,256]{0,1:T(8,128)(2,1)S(1)} collective-permute-done((bf16[1920,256]{0,1:T(8,128)(2,1)S(1)}, bf16[1920,256]{0,1:T(8,128)(2,1)S(1)}, u32[]{:S(2)}, u32[]{:S(2)}) %collective-permute-start.10) | collective-permute-done | bytes 983072 | tf_op jit(solution)/shard_map/ppermute | solution.py:15
  92.8 1.8 collective-permute-start.13
  94.7 12.9 %collective-permute-done.13 = bf16[1920,128]{0,1:T(8,128)(2,1)S(1)} collective-permute-done((bf16[1920,128]{0,1:T(8,128)(2,1)S(1)}, bf16[1920,128]{0,1:T(8,128)(2,1)S(1)}, u32[]{:S(2)}, u32[]{:S(2)}) %collective-permute-start.13) | collective-permute-done | bytes 491552 | tf_op jit(solution)/shard_map/ppermute | solution.py:15
  108.4 2.1 collective-permute-start.17
  110.6 9.1 %collective-permute-start.14 = (bf16[1920,256]{0,1:T(8,128)(2,1)}, bf16[1920,256]{0,1:T(8,128)(2,1)S(1)}, u32[]{:S(2)}, u32[]{:S(2)}) collective-permute-start(bf16[1920,256]{0,1:T(8,128)(2,1)} %fusion.1), channel_id=1, source_target_pairs={{0,1},{1,0},{2,3},{3,2},{4,5},{5,4},{6,7},{7,6},{8,9},{9,8},{10,11... | collective-permute-start | bytes 2949128 | tf_op jit(solution)/shard_map/ppermute | solution.py:15
  120.6 1.4 collective-permute-done.15
  122.0 9.1 %collective-permute-done.17 = bf16[1920,128]{0,1:T(8,128)(2,1)} collective-permute-done((bf16[1920,128]{0,1:T(8,128)(2,1)S(1)}, bf16[1920,128]{0,1:T(8,128)(2,1)}, u32[]{:S(2)}, u32[]{:S(2)}) %collective-permute-start.17) | collective-permute-done | bytes 491552 | tf_op jit(solution)/shard_map/ppermute | solution.py:152
  131.2 1.3 broadcast_select_fusion.11
  132.4 7.9 %collective-permute-done.16 = bf16[1920,128]{0,1:T(8,128)(2,1)S(1)} collective-permute-done((bf16[1920,128]{0,1:T(8,128)(2,1)S(1)}, bf16[1920,128]{0,1:T(8,128)(2,1)S(1)}, u32[]{:S(2)}, u32[]{:S(2)}) %collective-permute-start.16) | collective-permute-done | bytes 491552 | tf_op jit(solution)/shard_map/ppermute | solution.py:15
  140.6 2.2 collective-permute-start.20
  143.1 2.6 %fusion.8 = f32[576,256]{1,0:T(8,128)S(1)} fusion(bf16[1920,256]{0,1:T(8,128)(2,1)S(1)} %pad_maximum_fusion.3, bf16[576,7680]{1,0:T(8,128)(2,1)} %bitcast.93, s32[]{:T(128)S(6)} %select_n.318), kind=kOutput, calls=%fused_computation.16 | convolution fusion | flops 566231040 | bytes 3784708 | tf_op jit(solution)/shard_map/dot_general | solution.py:19
  145.7 8.8 %collective-permute-done.20 = bf16[1920,128]{0,1:T(8,128)(2,1)S(1)} collective-permute-done((bf16[1920,128]{0,1:T(8,128)(2,1)S(1)}, bf16[1920,128]{0,1:T(8,128)(2,1)S(1)}, u32[]{:S(2)}, u32[]{:S(2)}) %collective-permute-start.20) | collective-permute-done | bytes 491552 | tf_op jit(solution)/shard_map/ppermute | solution.py:15
  156.3 2.1 collective-permute-start.29
  158.5 7.2 %collective-permute-done.26 = bf16[1920,128]{0,1:T(8,128)(2,1)S(1)} collective-permute-done((bf16[1920,128]{0,1:T(8,128)(2,1)S(1)}, bf16[1920,128]{0,1:T(8,128)(2,1)S(1)}, u32[]{:S(2)}, u32[]{:S(2)}) %collective-permute-start.26) | collective-permute-done | bytes 491552 | tf_op jit(solution)/shard_map/ppermute | solution.py:15
  165.9 3.8 %collective-permute-done.28 = bf16[1920,128]{0,1:T(8,128)(2,1)S(1)} collective-permute-done((bf16[1920,128]{0,1:T(8,128)(2,1)S(1)}, bf16[1920,128]{0,1:T(8,128)(2,1)S(1)}, u32[]{:S(2)}, u32[]{:S(2)}) %collective-permute-start.28) | collective-permute-done | bytes 491552 | tf_op jit(solution)/shard_map/ppermute | solution.py:15
  169.7 10.9 %collective-permute-done.29 = bf16[1920,128]{0,1:T(8,128)(2,1)S(1)} collective-permute-done((bf16[1920,128]{0,1:T(8,128)(2,1)S(1)}, bf16[1920,128]{0,1:T(8,128)(2,1)S(1)}, u32[]{:S(2)}, u32[]{:S(2)}) %collective-permute-start.29) | collective-permute-done | bytes 491552 | tf_op jit(solution)/shard_map/ppermute | solution.py:152
  187.2 8.9 %collective-permute-start.21 = (bf16[12,48,256]{2,1,0:T(8,128)(2,1)S(1)}, bf16[12,48,256]{2,1,0:T(8,128)(2,1)S(1)}, u32[]{:S(2)}, u32[]{:S(2)}) collective-permute-start(bf16[12,48,256]{2,1,0:T(8,128)(2,1)S(1)} %pad_maximum_fusion.8), channel_id=1, source_target_pairs={{0,1},{1,2},{2,3},{3,0},{4,5},{5,6},{6,7},{7,4},{8,9},{9,10},{10,1... | collective-permute-start | bytes 884744 | tf_op jit(solution)/shard_map/ppermute | solution.py:11
  196.2 6.8 %collective-permute-done.21 = bf16[12,48,256]{2,1,0:T(8,128)(2,1)S(1)} collective-permute-done((bf16[12,48,256]{2,1,0:T(8,128)(2,1)S(1)}, bf16[12,48,256]{2,1,0:T(8,128)(2,1)S(1)}, u32[]{:S(2)}, u32[]{:S(2)}) %collective-permute-start.21) | collective-permute-done | bytes 294944 | tf_op jit(solution)/shard_map/ppermute | solution.py:11
  203.1 3.5 %collective-permute-start.22 = (bf16[12,48,256]{2,1,0:T(8,128)(2,1)S(1)}, bf16[12,48,256]{2,1,0:T(8,128)(2,1)S(1)}, u32[]{:S(2)}, u32[]{:S(2)}) collective-permute-start(bf16[12,48,256]{2,1,0:T(8,128)(2,1)S(1)} %broadcast_select_fusion.15), channel_id=1, source_target_pairs={{0,2},{1,3},{2,0},{3,1},{4,6},{5,7},{6,4},{7,5},{8,10},{9,11},{10,... | collective-permute-start | bytes 884744 | tf_op jit(solution)/shard_map/ppermute | solution.py:11
  206.9 13.0 %collective-permute-done.22 = bf16[12,48,256]{2,1,0:T(8,128)(2,1)S(1)} collective-permute-done((bf16[12,48,256]{2,1,0:T(8,128)(2,1)S(1)}, bf16[12,48,256]{2,1,0:T(8,128)(2,1)S(1)}, u32[]{:S(2)}, u32[]{:S(2)}) %collective-permute-start.22) | collective-permute-done | bytes 294944 | tf_op jit(solution)/shard_map/ppermute | solution.py:11
  221.9 1.3 collective-permute-start.25
  223.2 7.0 %collective-permute-done.31 = bf16[12,48,256]{2,1,0:T(8,128)(2,1)S(1)} collective-permute-done((bf16[12,48,256]{2,1,0:T(8,128)(2,1)S(1)}, bf16[12,48,256]{2,1,0:T(8,128)(2,1)S(1)}, u32[]{:S(2)}, u32[]{:S(2)}) %collective-permute-start.31) | collective-permute-done | bytes 294944 | tf_op jit(solution)/shard_map/ppermute | solution.py:11
  231.0 12.0 %collective-permute-done.32 = bf16[12,48,256]{2,1,0:T(8,128)(2,1)S(1)} collective-permute-done((bf16[12,48,256]{2,1,0:T(8,128)(2,1)S(1)}, bf16[12,48,256]{2,1,0:T(8,128)(2,1)S(1)}, u32[]{:S(2)}, u32[]{:S(2)}) %collective-permute-start.32) | collective-permute-done | bytes 294944 | tf_op jit(solution)/shard_map/ppermute | solution.py:11
  244.7 1.3 collective-permute-start.35
  246.9 2.7 %collective-permute-done.34 = bf16[4,48,2,1,128]{4,2,1,0,3:T(2,128)(2,1)S(1)} collective-permute-done((bf16[4,48,2,1,128]{4,2,1,0,3:T(2,128)(2,1)S(1)}, bf16[4,48,2,1,128]{4,2,1,0,3:T(2,128)(2,1)S(1)}, u32[]{:S(2)}, u32[]{:S(2)}) %collective-permute-start.34) | collective-permute-done | bytes 98336 | tf_op jit(solution)/shard_map/ppermute | solution.py:15
  249.6 1.3 collective-permute-done.35
  253.1 2.1 copy.19
  (127 shorter events, 23.6 us)
Async XLA Ops:
  0.0 23.2 %copy-start = (bf16[2048,512]{1,0:T(8,128)(2,1)S(1)}, bf16[2048,512]{1,0:T(8,128)(2,1)}, u32[]{:S(2)}) copy-start(bf16[2048,512]{1,0:T(8,128)(2,1)} %param.11) | copy-start | bytes 6291460
  1.6 14.9 %collective-permute-start = (bf16[1024,256]{1,0:T(8,128)(2,1)S(1)}, bf16[1024,256]{1,0:T(8,128)(2,1)S(1)}, u32[]{:S(2)}, u32[]{:S(2)}) collective-permute-start(bf16[1024,256]{1,0:T(8,128)(2,1)S(1)} %dynamic_slice.21), channel_id=1, source_target_pairs={{0,8},{4,12},{8,0},{12,4},{1,9},{5,13},{9,1},{13,5},{2,10},{6,14},... | collective-permute-start | bytes 1572872 | tf_op jit(solution)/shard_map/ppermute | solution.py:15
  4.6 1.3 collective-permute-start.3
  18.2 11.3 %collective-permute-start.1 = (bf16[1024,128]{1,0:T(8,128)(2,1)S(1)}, bf16[1024,128]{1,0:T(8,128)(2,1)S(1)}, u32[]{:S(2)}, u32[]{:S(2)}) collective-permute-start(bf16[1024,128]{1,0:T(8,128)(2,1)S(1)} %get-tuple-element.35), channel_id=1, source_target_pairs={{0,0},{1,4},{2,6},{3,2},{4,1},{5,5},{6,7},{7,3},{8,8},{9,12},{10,1... | collective-permute-start | bytes 786440 | tf_op jit(solution)/shard_map/ppermute | solution.py:123
  18.9 15.1 %collective-permute-start.2 = (bf16[1024,128]{1,0:T(8,128)(2,1)S(1)}, bf16[1024,128]{1,0:T(8,128)(2,1)S(1)}, u32[]{:S(2)}, u32[]{:S(2)}) collective-permute-start(bf16[1024,128]{1,0:T(8,128)(2,1)S(1)} %get-tuple-element.36), channel_id=1, source_target_pairs={{0,2},{1,6},{2,4},{3,0},{4,3},{5,7},{6,5},{7,1},{8,10},{9,14},{10,... | collective-permute-start | bytes 786440 | tf_op jit(solution)/shard_map/ppermute | solution.py:123
  23.5 2.4 collective-permute-start.4
  25.9 3.6 %collective-permute-start.5 = (f32[1,512]{1,0:T(1,128)S(1)}, f32[1,512]{1,0:T(1,128)S(1)}, u32[]{:S(2)}, u32[]{:S(2)}) collective-permute-start(f32[1,512]{1,0:T(1,128)S(1)} %add.172), channel_id=1, source_target_pairs={{0,8},{4,12},{8,0},{12,4},{1,9},{5,13},{9,1},{13,5},{2,10},{6,14},... | collective-permute-start | bytes 6152 | tf_op jit(solution)/shard_map/ppermute | solution.py:15
  34.1 15.9 %collective-permute-start.6 = (bf16[1024,256]{1,0:T(8,128)(2,1)S(1)}, bf16[1024,256]{1,0:T(8,128)(2,1)S(1)}, u32[]{:S(2)}, u32[]{:S(2)}) collective-permute-start(bf16[1024,256]{1,0:T(8,128)(2,1)S(1)} %pad_maximum_fusion.7), channel_id=1, source_target_pairs={{0,8},{4,12},{8,0},{12,4},{1,9},{5,13},{9,1},{13,5},{2,10},{6,14},... | collective-permute-start | bytes 1572872 | tf_op jit(solution)/shard_map/ppermute | solution.py:15
  35.4 4.7 %collective-permute-start.7 = (bf16[1024,128]{1,0:T(8,128)(2,1)S(1)}, bf16[1024,128]{1,0:T(8,128)(2,1)S(1)}, u32[]{:S(2)}, u32[]{:S(2)}) collective-permute-start(bf16[1024,128]{1,0:T(8,128)(2,1)S(1)} %get-tuple-element.19), channel_id=1, source_target_pairs={{0,0},{1,4},{2,6},{3,2},{4,1},{5,5},{6,7},{7,3},{8,8},{9,12},{10,1... | collective-permute-start | bytes 786440 | tf_op jit(solution)/shard_map/ppermute | solution.py:123
  36.1 13.8 %collective-permute-start.8 = (bf16[1024,128]{1,0:T(8,128)(2,1)S(1)}, bf16[1024,128]{1,0:T(8,128)(2,1)S(1)}, u32[]{:S(2)}, u32[]{:S(2)}) collective-permute-start(bf16[1024,128]{1,0:T(8,128)(2,1)S(1)} %get-tuple-element.20), channel_id=1, source_target_pairs={{0,2},{1,6},{2,4},{3,0},{4,3},{5,7},{6,5},{7,1},{8,10},{9,14},{10,... | collective-permute-start | bytes 786440 | tf_op jit(solution)/shard_map/ppermute | solution.py:123
  50.1 6.3 %collective-permute-start.9 = (bf16[2048,256]{1,0:T(8,128)(2,1)S(1)}, bf16[2048,256]{1,0:T(8,128)(2,1)S(1)}, u32[]{:S(2)}, u32[]{:S(2)}) collective-permute-start(bf16[2048,256]{1,0:T(8,128)(2,1)S(1)} %pad_maximum_fusion), channel_id=1, source_target_pairs={{0,4},{4,0},{8,12},{12,8},{1,5},{5,1},{9,13},{13,9},{2,6},{6,2},{1... | collective-permute-start | bytes 3145736 | tf_op jit(solution)/shard_map/ppermute | solution.py:15
  54.2 13.9 %collective-permute-start.11 = (bf16[1024,256]{1,0:T(8,128)(2,1)S(1)}, bf16[1024,256]{1,0:T(8,128)(2,1)S(1)}, u32[]{:S(2)}, u32[]{:S(2)}) collective-permute-start(bf16[1024,256]{1,0:T(8,128)(2,1)S(1)} %constant_dynamic-update-slice_fusion), channel_id=1, source_target_pairs={{0,8},{4,12},{8,0},{12,4},{1,9},{5,13},{9,1},{13,5},{2,10},{6,14},... | collective-permute-start | bytes 1572872 | tf_op jit(solution)/shard_map/ppermute | solution.py:15
  56.4 5.9 %slice-start.3 = ((s8[7864320]{0:T(1024)(128)(4,1)}), s8[4194304]{0:T(1024)(128)(4,1)S(1)}, s32[]{:S(2)}) async-start(s8[7864320]{0:T(1024)(128)(4,1)} %bitcast.103), calls=%async_computation.3 | async-start | bytes 8388608
  56.6 5.8 %slice-start.4 = ((s8[7864320]{0:T(1024)(128)(4,1)}), s8[3670016]{0:T(1024)(128)(4,1)S(1)}, s32[]{:S(2)}) async-start(s8[7864320]{0:T(1024)(128)(4,1)} %bitcast.103), calls=%async_computation.4 | async-start | bytes 7340032
  68.3 2.7 %collective-permute-start.12 = (bf16[2048,256]{1,0:T(8,128)(2,1)S(1)}, bf16[2048,256]{1,0:T(8,128)(2,1)S(1)}, u32[]{:S(2)}, u32[]{:S(2)}) collective-permute-start(bf16[2048,256]{1,0:T(8,128)(2,1)S(1)} %pad_maximum_fusion.1), channel_id=1, source_target_pairs={{0,4},{4,0},{8,12},{12,8},{1,5},{5,1},{9,13},{13,9},{2,6},{6,2},{1... | collective-permute-start | bytes 3145736 | tf_op jit(solution)/shard_map/ppermute | solution.py:15
  68.4 24.2 %collective-permute-start.10 = (bf16[1920,256]{0,1:T(8,128)(2,1)S(1)}, bf16[1920,256]{0,1:T(8,128)(2,1)S(1)}, u32[]{:S(2)}, u32[]{:S(2)}) collective-permute-start(bf16[1920,256]{0,1:T(8,128)(2,1)S(1)} %fusion), channel_id=1, source_target_pairs={{0,1},{1,0},{2,3},{3,2},{4,5},{5,4},{6,7},{7,6},{8,9},{9,8},{10,11... | collective-permute-start | bytes 2949128 | tf_op jit(solution)/shard_map/ppermute | solution.py:15
  92.7 27.0 %copy-start.4 = (s32[4]{0:T(128)S(1)}, s32[4]{0:T(128)}, u32[]{:S(2)}) copy-start(s32[4]{0:T(128)} %param.14) | copy-start | bytes 52
  92.7 27.0 %copy-start.1 = (s32[4,4]{1,0:T(4,128)S(1)}, s32[4,4]{1,0:T(4,128)}, u32[]{:S(2)}) copy-start(s32[4,4]{1,0:T(4,128)} %param.13) | copy-start | bytes 196
  92.7 27.1 %copy-start.3 = (s32[4]{0:T(128)S(1)}, s32[4]{0:T(128)}, u32[]{:S(2)}) copy-start(s32[4]{0:T(128)} %param.15) | copy-start | bytes 52
  92.8 14.8 %collective-permute-start.13 = (bf16[1920,128]{0,1:T(8,128)(2,1)S(1)}, bf16[1920,128]{0,1:T(8,128)(2,1)S(1)}, u32[]{:S(2)}, u32[]{:S(2)}) collective-permute-start(bf16[1920,128]{0,1:T(8,128)(2,1)S(1)} %slice.161), channel_id=1, source_target_pairs={{0,3},{1,2},{2,1},{3,0},{4,7},{5,6},{6,5},{7,4},{8,11},{9,10},{10,... | collective-permute-start | bytes 1474568 | tf_op jit(solution)/shard_map/ppermute | solution.py:15
  107.7 14.3 %collective-permute-start.15 = (bf16[1920,128]{0,1:T(8,128)(2,1)S(1)}, bf16[1920,128]{0,1:T(8,128)(2,1)}, u32[]{:S(2)}, u32[]{:S(2)}) collective-permute-start(bf16[1920,128]{0,1:T(8,128)(2,1)S(1)} %fusion.41), channel_id=1, source_target_pairs={{0,8},{4,12},{8,0},{12,4},{1,9},{5,13},{9,1},{13,5},{2,10},{6,14},... | collective-permute-start | bytes 1474568 | tf_op jit(solution)/shard_map/ppermute | solution.py:15
  108.4 22.7 %collective-permute-start.17 = (bf16[1920,128]{0,1:T(8,128)(2,1)S(1)}, bf16[1920,128]{0,1:T(8,128)(2,1)}, u32[]{:S(2)}, u32[]{:S(2)}) collective-permute-start(bf16[1920,128]{0,1:T(8,128)(2,1)S(1)} %fusion.41), channel_id=1, source_target_pairs={{0,24},{1,25},{2,26},{3,27},{4,28},{5,29},{6,30},{7,31},{8,16},{9,... | collective-permute-start | bytes 1474568 | tf_op jit(solution)/shard_map/ppermute | solution.py:152
  110.6 29.8 %collective-permute-start.14 = (bf16[1920,256]{0,1:T(8,128)(2,1)}, bf16[1920,256]{0,1:T(8,128)(2,1)S(1)}, u32[]{:S(2)}, u32[]{:S(2)}) collective-permute-start(bf16[1920,256]{0,1:T(8,128)(2,1)} %fusion.1), channel_id=1, source_target_pairs={{0,1},{1,0},{2,3},{3,2},{4,5},{5,4},{6,7},{7,6},{8,9},{9,8},{10,11... | collective-permute-start | bytes 2949128 | tf_op jit(solution)/shard_map/ppermute | solution.py:15
  119.9 20.5 %collective-permute-start.16 = (bf16[1920,128]{0,1:T(8,128)(2,1)S(1)}, bf16[1920,128]{0,1:T(8,128)(2,1)S(1)}, u32[]{:S(2)}, u32[]{:S(2)}) collective-permute-start(bf16[1920,128]{0,1:T(8,128)(2,1)S(1)} %fusion.41), channel_id=1, source_target_pairs={{0,16},{16,0},{1,17},{17,1},{2,18},{18,2},{3,19},{19,3},{4,20},{20... | collective-permute-start | bytes 1474568 | tf_op jit(solution)/shard_map/ppermute | solution.py:15
  140.6 13.9 %collective-permute-start.20 = (bf16[1920,128]{0,1:T(8,128)(2,1)S(1)}, bf16[1920,128]{0,1:T(8,128)(2,1)S(1)}, u32[]{:S(2)}, u32[]{:S(2)}) collective-permute-start(bf16[1920,128]{0,1:T(8,128)(2,1)S(1)} %slice.160), channel_id=1, source_target_pairs={{0,3},{1,2},{2,1},{3,0},{4,7},{5,6},{6,5},{7,4},{8,11},{9,10},{10,... | collective-permute-start | bytes 1474568 | tf_op jit(solution)/shard_map/ppermute | solution.py:15
  142.8 39.7 %collective-permute-start.19 = (bf16[1920,256]{0,1:T(8,128)(2,1)S(1)}, bf16[1920,256]{0,1:T(8,128)(2,1)S(1)}, u32[]{:S(2)}, u32[]{:S(2)}) collective-permute-start(bf16[1920,256]{0,1:T(8,128)(2,1)S(1)} %pad_maximum_fusion.3), channel_id=1, source_target_pairs={{0,4},{4,0},{8,12},{12,8},{1,5},{5,1},{9,13},{13,9},{2,6},{6,2},{1... | collective-permute-start | bytes 2949128 | tf_op jit(solution)/shard_map/ppermute | solution.py:15
  142.9 37.9 %slice-start = ((s8[8847360]{0:T(1024)(128)(4,1)}), s8[4194304]{0:T(1024)(128)(4,1)S(1)}, s32[]{:S(2)}) async-start(s8[8847360]{0:T(1024)(128)(4,1)} %bitcast.94), calls=%async_computation | async-start | bytes 8388608
  142.9 37.9 %slice-start.1 = ((s8[8847360]{0:T(1024)(128)(4,1)}), s8[458752]{0:T(1024)(128)(4,1)S(1)}, s32[]{:S(2)}) async-start(s8[8847360]{0:T(1024)(128)(4,1)} %bitcast.94), calls=%async_computation.1 | async-start | bytes 917504
  154.6 11.1 %collective-permute-start.26 = (bf16[1920,128]{0,1:T(8,128)(2,1)S(1)}, bf16[1920,128]{0,1:T(8,128)(2,1)S(1)}, u32[]{:S(2)}, u32[]{:S(2)}) collective-permute-start(bf16[1920,128]{0,1:T(8,128)(2,1)S(1)} %fusion.40), channel_id=1, source_target_pairs={{0,16},{16,0},{1,17},{17,1},{2,18},{18,2},{3,19},{19,3},{4,20},{20... | collective-permute-start | bytes 1474568 | tf_op jit(solution)/shard_map/ppermute | solution.py:15
  155.5 25.3 %slice-start.2 = ((s8[8847360]{0:T(1024)(128)(4,1)}), s8[4194304]{0:T(1024)(128)(4,1)S(1)}, s32[]{:S(2)}) async-start(s8[8847360]{0:T(1024)(128)(4,1)} %bitcast.94), calls=%async_computation.2 | async-start | bytes 8388608
  155.5 25.3 %collective-permute-start.18 = (bf16[1920,256]{0,1:T(8,128)(2,1)S(1)}, bf16[1920,256]{0,1:T(8,128)(2,1)S(1)}, u32[]{:S(2)}, u32[]{:S(2)}) collective-permute-start(bf16[1920,256]{0,1:T(8,128)(2,1)S(1)} %pad_maximum_fusion.2), channel_id=1, source_target_pairs={{0,4},{4,0},{8,12},{12,8},{1,5},{5,1},{9,13},{13,9},{2,6},{6,2},{1... | collective-permute-start | bytes 2949128 | tf_op jit(solution)/shard_map/ppermute | solution.py:15
  155.6 14.1 %collective-permute-start.28 = (bf16[1920,128]{0,1:T(8,128)(2,1)S(1)}, bf16[1920,128]{0,1:T(8,128)(2,1)S(1)}, u32[]{:S(2)}, u32[]{:S(2)}) collective-permute-start(bf16[1920,128]{0,1:T(8,128)(2,1)S(1)} %fusion.40), channel_id=1, source_target_pairs={{0,8},{4,12},{8,0},{12,4},{1,9},{5,13},{9,1},{13,5},{2,10},{6,14},... | collective-permute-start | bytes 1474568 | tf_op jit(solution)/shard_map/ppermute | solution.py:15
  156.3 24.2 %collective-permute-start.29 = (bf16[1920,128]{0,1:T(8,128)(2,1)S(1)}, bf16[1920,128]{0,1:T(8,128)(2,1)S(1)}, u32[]{:S(2)}, u32[]{:S(2)}) collective-permute-start(bf16[1920,128]{0,1:T(8,128)(2,1)S(1)} %fusion.40), channel_id=1, source_target_pairs={{0,24},{1,25},{2,26},{3,27},{4,28},{5,29},{6,30},{7,31},{8,16},{9,... | collective-permute-start | bytes 1474568 | tf_op jit(solution)/shard_map/ppermute | solution.py:152
  165.8 18.6 %collective-permute-start.27 = (bf16[1920,256]{0,1:T(8,128)(2,1)S(1)}, bf16[1920,256]{0,1:T(8,128)(2,1)S(1)}, u32[]{:S(2)}, u32[]{:S(2)}) collective-permute-start(bf16[1920,256]{0,1:T(8,128)(2,1)S(1)} %pad_maximum_fusion.4), channel_id=1, source_target_pairs={{0,4},{4,0},{8,12},{12,8},{1,5},{5,1},{9,13},{13,9},{2,6},{6,2},{1... | collective-permute-start | bytes 2949128 | tf_op jit(solution)/shard_map/ppermute | solution.py:15
  180.7 5.4 %collective-permute-start.30 = (bf16[1920,256]{0,1:T(8,128)(2,1)S(1)}, bf16[1920,256]{0,1:T(8,128)(2,1)S(1)}, u32[]{:S(2)}, u32[]{:S(2)}) collective-permute-start(bf16[1920,256]{0,1:T(8,128)(2,1)S(1)} %pad_maximum_fusion.5), channel_id=1, source_target_pairs={{0,4},{4,0},{8,12},{12,8},{1,5},{5,1},{9,13},{13,9},{2,6},{6,2},{1... | collective-permute-start | bytes 2949128 | tf_op jit(solution)/shard_map/ppermute | solution.py:15
  186.1 0.8 copy-start.2
  187.2 15.8 %collective-permute-start.21 = (bf16[12,48,256]{2,1,0:T(8,128)(2,1)S(1)}, bf16[12,48,256]{2,1,0:T(8,128)(2,1)S(1)}, u32[]{:S(2)}, u32[]{:S(2)}) collective-permute-start(bf16[12,48,256]{2,1,0:T(8,128)(2,1)S(1)} %pad_maximum_fusion.8), channel_id=1, source_target_pairs={{0,1},{1,2},{2,3},{3,0},{4,5},{5,6},{6,7},{7,4},{8,9},{9,10},{10,1... | collective-permute-start | bytes 884744 | tf_op jit(solution)/shard_map/ppermute | solution.py:11
  203.1 16.7 %collective-permute-start.22 = (bf16[12,48,256]{2,1,0:T(8,128)(2,1)S(1)}, bf16[12,48,256]{2,1,0:T(8,128)(2,1)S(1)}, u32[]{:S(2)}, u32[]{:S(2)}) collective-permute-start(bf16[12,48,256]{2,1,0:T(8,128)(2,1)S(1)} %broadcast_select_fusion.15), channel_id=1, source_target_pairs={{0,2},{1,3},{2,0},{3,1},{4,6},{5,7},{6,4},{7,5},{8,10},{9,11},{10,... | collective-permute-start | bytes 884744 | tf_op jit(solution)/shard_map/ppermute | solution.py:11
  220.1 10.1 %collective-permute-start.31 = (bf16[12,48,256]{2,1,0:T(8,128)(2,1)S(1)}, bf16[12,48,256]{2,1,0:T(8,128)(2,1)S(1)}, u32[]{:S(2)}, u32[]{:S(2)}) collective-permute-start(bf16[12,48,256]{2,1,0:T(8,128)(2,1)S(1)} %pad_maximum_fusion.9), channel_id=1, source_target_pairs={{0,1},{1,2},{2,3},{3,0},{4,5},{5,6},{6,7},{7,4},{8,9},{9,10},{10,1... | collective-permute-start | bytes 884744 | tf_op jit(solution)/shard_map/ppermute | solution.py:11
  220.9 9.6 %collective-permute-start.23 = (bf16[4,48,2,1,128]{4,2,1,0,3:T(2,128)(2,1)S(1)}, bf16[4,48,2,1,128]{4,2,1,0,3:T(2,128)(2,1)S(1)}, u32[]{:S(2)}, u32[]{:S(2)}) collective-permute-start(bf16[4,48,2,1,128]{4,2,1,0,3:T(2,128)(2,1)S(1)} %squeeze.25), channel_id=1, source_target_pairs={{0,4},{4,0},{8,12},{12,8},{1,5},{5,1},{9,13},{13,9},{2,6},{6,2},{1... | collective-permute-start | bytes 294920 | tf_op jit(solution)/shard_map/ppermute | solution.py:15
  221.1 9.5 %collective-permute-start.24 = (bf16[4,48,2,1,128]{4,2,1,0,3:T(2,128)(2,1)S(1)}, bf16[4,48,2,1,128]{4,2,1,0,3:T(2,128)(2,1)S(1)}, u32[]{:S(2)}, u32[]{:S(2)}) collective-permute-start(bf16[4,48,2,1,128]{4,2,1,0,3:T(2,128)(2,1)S(1)} %squeeze.26), channel_id=1, source_target_pairs={{0,8},{4,12},{8,0},{12,4},{1,9},{5,13},{9,1},{13,5},{2,10},{6,14},... | collective-permute-start | bytes 294920 | tf_op jit(solution)/shard_map/ppermute | solution.py:15
  221.9 8.7 %collective-permute-start.25 = (bf16[4,48,2,1,128]{4,2,1,0,3:T(2,128)(2,1)S(1)}, bf16[4,48,2,1,128]{4,2,1,0,3:T(2,128)(2,1)S(1)}, u32[]{:S(2)}, u32[]{:S(2)}) collective-permute-start(bf16[4,48,2,1,128]{4,2,1,0,3:T(2,128)(2,1)S(1)} %squeeze.27), channel_id=1, source_target_pairs={{0,12},{4,8},{8,4},{12,0},{1,13},{5,9},{9,5},{13,1},{2,14},{6,10},... | collective-permute-start | bytes 294920 | tf_op jit(solution)/shard_map/ppermute | solution.py:15
  230.4 12.6 %collective-permute-start.32 = (bf16[12,48,256]{2,1,0:T(8,128)(2,1)S(1)}, bf16[12,48,256]{2,1,0:T(8,128)(2,1)S(1)}, u32[]{:S(2)}, u32[]{:S(2)}) collective-permute-start(bf16[12,48,256]{2,1,0:T(8,128)(2,1)S(1)} %broadcast_select_fusion.14), channel_id=1, source_target_pairs={{0,2},{1,3},{2,0},{3,1},{4,6},{5,7},{6,4},{7,5},{8,10},{9,11},{10,... | collective-permute-start | bytes 884744 | tf_op jit(solution)/shard_map/ppermute | solution.py:11
  243.7 3.1 %collective-permute-start.33 = (bf16[4,48,2,1,128]{4,2,1,0,3:T(2,128)(2,1)S(1)}, bf16[4,48,2,1,128]{4,2,1,0,3:T(2,128)(2,1)S(1)}, u32[]{:S(2)}, u32[]{:S(2)}) collective-permute-start(bf16[4,48,2,1,128]{4,2,1,0,3:T(2,128)(2,1)S(1)} %squeeze.29), channel_id=1, source_target_pairs={{0,4},{4,0},{8,12},{12,8},{1,5},{5,1},{9,13},{13,9},{2,6},{6,2},{1... | collective-permute-start | bytes 294920 | tf_op jit(solution)/shard_map/ppermute | solution.py:15
  243.9 5.7 %collective-permute-start.34 = (bf16[4,48,2,1,128]{4,2,1,0,3:T(2,128)(2,1)S(1)}, bf16[4,48,2,1,128]{4,2,1,0,3:T(2,128)(2,1)S(1)}, u32[]{:S(2)}, u32[]{:S(2)}) collective-permute-start(bf16[4,48,2,1,128]{4,2,1,0,3:T(2,128)(2,1)S(1)} %squeeze.30), channel_id=1, source_target_pairs={{0,8},{4,12},{8,0},{12,4},{1,9},{5,13},{9,1},{13,5},{2,10},{6,14},... | collective-permute-start | bytes 294920 | tf_op jit(solution)/shard_map/ppermute | solution.py:15
  244.7 6.2 %collective-permute-start.35 = (bf16[4,48,2,1,128]{4,2,1,0,3:T(2,128)(2,1)S(1)}, bf16[4,48,2,1,128]{4,2,1,0,3:T(2,128)(2,1)S(1)}, u32[]{:S(2)}, u32[]{:S(2)}) collective-permute-start(bf16[4,48,2,1,128]{4,2,1,0,3:T(2,128)(2,1)S(1)} %squeeze.31), channel_id=1, source_target_pairs={{0,12},{4,8},{8,4},{12,0},{1,13},{5,9},{9,5},{13,1},{2,14},{6,10},... | collective-permute-start | bytes 294920 | tf_op jit(solution)/shard_map/ppermute | solution.py:15

commit v5 on v4

--- a/solution.py
+++ b/solution.py
@@ -173,42 +173,53 @@
             finished.append(entries.reshape(token_rows, width).astype(jnp.bfloat16))
         return jnp.concatenate(finished, axis=1).reshape(tile_slots, shard_len, 2 * width)
 
-    def route(rolled, before):
-        rolled = after(rolled, before)
-        for stride in (1, 2):
-            odd = (turn_of // stride % 2 == 1)[:, None, None]
-            rolled = jnp.where(odd, shifted_2(rolled, "head", stride), rolled)
+    def roll(rolled, stride):
+        odd = (turn_of // stride % 2 == 1)[:, None, None]
+        return jnp.where(odd, shifted_2(rolled, "head", stride), rolled)
+
+    def to_owners(rolled):
         outgoing = add_columns(selector, rolled.reshape(tile_slots, -1)).astype(jnp.bfloat16)
         outgoing = outgoing.reshape(4, most_tiles, shard_len, 2, layers, head_dim)
         arrived = [outgoing[0]] + [swapped(outgoing[r], "tile", r) for r in (1, 2, 3)]
         even = [jnp.where(first_core, arrived[r], arrived[r ^ 1]) for r in range(4)]
         ranked = [jnp.where(first_chip, even[r], even[r ^ 2]) for r in range(4)]
-        return jnp.stack(ranked, axis=1), rolled
-
-    mine = lax.dynamic_slice_in_dim(kv_weight, group * 2 * head_dim, 2 * head_dim, axis=1)
-    stays = lax.dynamic_slice_in_dim(mine, tile // 2 * half, half, axis=0)
-    leaves = lax.dynamic_slice_in_dim(mine, half - tile // 2 * half, half, axis=0)
-    comes = swapped(leaves, "tile", 2)
-    key_half = cross_planes(stays[:, :width], comes[:, :width], None)
-    key_half = after(key_half, bias_part)
-    value_half = cross_planes(stays[:, width:], comes[:, width:], key_half)
-    key_near = whole_rows(key_half, swapped(key_half, "tile", 2))
-    key_near = after(key_near, value_half)
+        return jnp.stack(ranked, axis=1)
+
+    column = group * 2 * head_dim
+    key_mine = lax.dynamic_slice_in_dim(kv_weight, column, head_dim, axis=1)
+    value_mine = lax.dynamic_slice_in_dim(kv_weight, column + head_dim, head_dim, axis=1)
+    to_plane = [
+        (t * 4 + h, (h // 2 * 2 + (h ^ h // 2) % 2) * 4 + t) for t in range(4) for h in range(4)
+    ]
+    key_block = after(lax.ppermute(key_mine, ("tile", "head"), to_plane), bias_part)
+    stays = lax.dynamic_slice_in_dim(value_mine, tile // 2 * half, half, axis=0)
+    leaves = lax.dynamic_slice_in_dim(value_mine, half - tile // 2 * half, half, axis=0)
+    value_half = cross_planes(stays, swapped(leaves, "tile", 2), key_block)
+    key_other = swapped(key_block, "tile", 2)
+    kept_first = tile // 2 == head // 2
+    key_near = jnp.concatenate(
+        [jnp.where(kept_first, key_block, key_other), jnp.where(kept_first, key_other, key_block)],
+        axis=1,
+    )
     key_leaves, key_stays = products(key_near, swapped(key_near, "tile", 1))
+    value_half = after(value_half, key_leaves)
     value_other = after(swapped(value_half, "tile", 2), key_stays)
     value_near = whole_rows(value_half, value_other)
     value_leaves, value_stays = products(value_near, swapped(value_near, "tile", 1))
     key_comes = after(swapped(key_leaves, "head", 1), value_stays)
     key_own = mirror_sum(key_stays + key_comes.astype(jnp.float32))
+    value_comes = swapped(after(value_leaves, key_comes), "head", 1)
     key_others = other_chips(key_own)
-    value_comes = after(swapped(after(value_leaves, key_own), "head", 1), key_others)
+    value_comes = after(value_comes, key_others)
     value_pair = value_stays + value_comes.astype(jnp.float32)
     value_own = mirror_sum(value_pair)
     keys = finish(times_features(after(key_own, value_pair), key_others), 0)
-    routed_keys, keys = route(keys, value_own)
-    values = finish(times_features(value_own, other_chips(value_own)), 1)
-    routed_values, _ = route(values, keys)
-    cache = jnp.stack([routed_keys, routed_values], axis=-2)
+    keys = roll(after(keys, value_own), 1)
+    value_others = other_chips(value_own)
+    values = finish(times_features(after(value_own, keys), value_others), 1)
+    keys = roll(keys, 2)
+    values = roll(roll(after(values, keys), 1), 2)
+    cache = jnp.stack([to_owners(keys), to_owners(values)], axis=-2)
     return cache.reshape(1, 1, most_tiles * 4 * shard_len, 4 * layers, head_dim)
 
 

time: 255 us -> 277 us (1.086)
  starting transfers between devices: 61.1 us -> 88.5 us
  waiting for transfers between devices: 155 us -> 142 us
  other arithmetic: 9.25 us -> 12.3 us
  matrix products: 23.3 us -> 26.1 us
    ppermute x4, starting transfers between devices: 12.8 us -> 30.1 us  [shifted_2(): lax.ppermute(shard, axis, [(i, (i + by) % count) for i in range(count)])]
    ppermute x25, starting transfers between devices: 33.2 us -> 48.8 us  [swapped(): lax.ppermute(shard, axis, [(i, i ^ bit) for i in range(lax.axis_size(axis...]
    ppermute x2, waiting for transfers between devices: 20 us -> 7.84 us  [other_chips(): lax.ppermute(own, ('groups', 'tile', 'head'), diagonal)]
    ppermute x4 -> x2, starting transfers between devices: 9.56 us -> 3.66 us  [cross_planes(): pieces.append(lax.ppermute(piece, ('tile', 'head'), rounds[j]))]
    ppermute x25, waiting for transfers between devices: 82.1 us -> 86.3 us  [swapped(): lax.ppermute(shard, axis, [(i, i ^ bit) for i in range(lax.axis_size(axis...]
    dot_general x15, matrix products: 23.1 us -> 25.9 us  [add_columns(): return jnp.dot(operand, portion, preferred_element_type=jnp.float32)]
    ppermute x4 -> x2, waiting for transfers between devices: 14.3 us -> 11.5 us  [cross_planes(): pieces.append(lax.ppermute(piece, ('tile', 'head'), rounds[j]))]
  transfers between devices with their start and end apart: 36 -> 35, of which waited for: 23 -> 20; matrix products, arithmetic and copies ran while one was open for 11% -> 11% of each run, Pallas kernels for 0% -> 0%
where the time goes in v5:
time: 277 us; the launch traced here: 276 us
  waiting for transfers between devices  142 us (51%)
  starting transfers between devices  88.5 us (32%)
  matrix products  26.1 us (9%)
  other arithmetic  12.3 us (4%)
  local copies, waits for them, and re-layouts  6.19 us (2%)
    ppermute x25, waiting for transfers between devices, swapped(): lax.ppermute(shard, axis, [(i, i ^ bit) for i in range(lax.axis_size(axis...  86.3 us
    ppermute x25, starting transfers between devices, swapped(): lax.ppermute(shard, axis, [(i, i ^ bit) for i in range(lax.axis_size(axis...  48.8 us
    ppermute x4, waiting for transfers between devices, shifted_2(): lax.ppermute(shard, axis, [(i, (i + by) % count) for i in range(count)])  36.9 us
    ppermute x4, starting transfers between devices, shifted_2(): lax.ppermute(shard, axis, [(i, (i + by) % count) for i in range(count)])  30.1 us
    dot_general x15, matrix products, add_columns(): return jnp.dot(operand, portion, preferred_element_type=jnp.float32)  25.9 us
    ppermute x2, waiting for transfers between devices, cross_planes(): pieces.append(lax.ppermute(piece, ('tile', 'head'), rounds[j]))  11.5 us
    ppermute x2, waiting for transfers between devices, other_chips(): lax.ppermute(own, ('groups', 'tile', 'head'), diagonal)  7.84 us
  transfers between devices with their start and end apart: 35, of which 20 were waited for; matrix products, arithmetic and copies ran while one was open for 11% of the time, Pallas kernels for 0%

profile of v5, /device:TPU:0, one launch (start us, length us, event | category | flops | bytes accessed | tf_op | source)
XLA Modules:
  0.0 276.1 jit_solution(7733718268423748487)
XLA Ops:
  0.0 1.1 constant_dynamic-slice_fusion
  1.8 1.3 collective-permute-start.1
  3.1 2.0 fusion.73
  5.1 13.5 %collective-permute-start.2 = (f32[1,512]{1,0:T(1,128)S(1)}, f32[1,512]{1,0:T(1,128)S(1)}, u32[]{:S(2)}, u32[]{:S(2)}) collective-permute-start(f32[1,512]{1,0:T(1,128)S(1)} %fusion.73), channel_id=1, source_target_pairs={{0,4},{4,0},{8,12},{12,8},{1,5},{5,1},{9,13},{13,9},{2,6},{6,2},{1... | collective-permute-start | bytes 6152 | tf_op jit(solution)/shard_map/ppermute | solution.py:15
  19.5 16.6 %collective-permute-start.3 = (f32[1,512]{1,0:T(1,128)S(1)}, f32[1,512]{1,0:T(1,128)S(1)}, u32[]{:S(2)}, u32[]{:S(2)}) collective-permute-start(f32[1,512]{1,0:T(1,128)S(1)} %add.178), channel_id=1, source_target_pairs={{0,8},{4,12},{8,0},{12,4},{1,9},{5,13},{9,1},{13,5},{2,10},{6,14},... | collective-permute-start | bytes 6152 | tf_op jit(solution)/shard_map/ppermute | solution.py:15
  36.0 1.6 collective-permute-done.3
  37.6 2.1 collective-permute-start.4
  39.7 11.1 %collective-permute-done.4 = bf16[2048,128]{1,0:T(8,128)(2,1)S(1)} collective-permute-done((bf16[2048,128]{1,0:T(8,128)(2,1)S(1)}, bf16[2048,128]{1,0:T(8,128)(2,1)S(1)}, u32[]{:S(2)}, u32[]{:S(2)}) %collective-permute-start.4) | collective-permute-done | bytes 524320 | tf_op jit(solution)/shard_map/ppermute | solution.py:15
  51.1 1.3 dynamic_slice.25
  52.4 1.8 collective-permute-start.7
  54.2 7.0 %collective-permute-done.7 = bf16[1024,128]{1,0:T(8,128)(2,1)} collective-permute-done((bf16[1024,128]{1,0:T(8,128)(2,1)S(1)}, bf16[1024,128]{1,0:T(8,128)(2,1)}, u32[]{:S(2)}, u32[]{:S(2)}) %collective-permute-start.7) | collective-permute-done | bytes 262176 | tf_op jit(solution)/shard_map/ppermute | solution.py:15
  61.2 2.1 broadcast_select_fusion.19
  63.3 3.6 %collective-permute-start.8 = (bf16[1024,128]{1,0:T(8,128)(2,1)}, bf16[1024,128]{1,0:T(8,128)(2,1)}, u32[]{:S(2)}, u32[]{:S(2)}) collective-permute-start(bf16[1024,128]{1,0:T(8,128)(2,1)} %get-tuple-element.21), channel_id=1, source_target_pairs={{0,0},{1,4},{2,6},{3,2},{4,1},{5,5},{6,7},{7,3},{8,8},{9,12},{10,1... | collective-permute-start | bytes 786440 | tf_op jit(solution)/shard_map/ppermute | solution.py:123
  66.9 11.5 %collective-permute-done.9 = bf16[1024,128]{1,0:T(8,128)(2,1)} collective-permute-done((bf16[1024,128]{1,0:T(8,128)(2,1)S(1)}, bf16[1024,128]{1,0:T(8,128)(2,1)}, u32[]{:S(2)}, u32[]{:S(2)}) %collective-permute-start.9) | collective-permute-done | bytes 262176 | tf_op jit(solution)/shard_map/ppermute | solution.py:123
  78.4 1.1 pad_maximum_fusion.7
  79.9 5.8 %fusion = bf16[1920,256]{0,1:T(8,128)(2,1)S(1)} fusion(bf16[1920,2048]{1,0:T(8,128)(2,1)} %param.9, bf16[2048,256]{1,0:T(8,128)(2,1)S(1)} %collective-permute-done.5, pred[]{:T(512)S(6)} %eq.92, bf16[2048,128]{1,0:T(8,128)(2,1)S(1)} %get-tuple-element.40, bf16[2048,128]{1,0:T(8,128)(2,1)S(1)} %get-tuple-element.39), kind=kOutput, calls=%fused_computation.6 | convolution fusion | flops 2016378880 | bytes 10944513 | tf_op jit(solution)/shard_map/dot_general | solution.py:19
  86.3 2.4 convolution_bitcast_fusion.1
  88.7 11.1 %collective-permute-done.10 = bf16[1024,256]{1,0:T(8,128)(2,1)S(1)} collective-permute-done((bf16[1024,256]{1,0:T(8,128)(2,1)S(1)}, bf16[1024,256]{1,0:T(8,128)(2,1)S(1)}, u32[]{:S(2)}, u32[]{:S(2)}) %collective-permute-start.10) | collective-permute-done | bytes 524320 | tf_op jit(solution)/shard_map/ppermute | solution.py:15
  100.6 1.6 collective-permute-start.6
  102.9 3.3 %fusion.1 = bf16[1920,256]{0,1:T(8,128)(2,1)} fusion(bf16[1920,2048]{1,0:T(8,128)(2,1)S(1)} %bitcast.104, bf16[2048,256]{1,0:T(8,128)(2,1)S(1)} %collective-permute-done.11, pred[]{:T(512)S(6)} %eq.92, bf16[1024,256]{1,0:T(8,128)(2,1)S(1)} %get-tuple-element.38, bf16[1024,256]{1,0:T(8,128)(2,1)S(1)} %get-tuple-element.37), kind=kOutput, calls=%fused_computation.7 | convolution fusion | flops 2016378880 | bytes 10944513 | tf_op jit(solution)/shard_map/dot_general | solution.py:19
  106.5 3.8 %convolution_bitcast_fusion = f32[1920,256]{0,1:T(8,128)} fusion(bf16[2048,256]{1,0:T(8,128)(2,1)S(1)} %broadcast_select_fusion, bf16[1920,2048]{1,0:T(8,128)(2,1)S(1)} %bitcast.104), kind=kOutput, calls=%fused_computation.2 | convolution fusion | flops 2013265920 | bytes 10878976 | tf_op jit(solution)/shard_map/dot_general | solution.py:19
  110.3 14.3 %collective-permute-done.6 = bf16[1920,256]{0,1:T(8,128)(2,1)S(1)} collective-permute-done((bf16[1920,256]{0,1:T(8,128)(2,1)S(1)}, bf16[1920,256]{0,1:T(8,128)(2,1)S(1)}, u32[]{:S(2)}, u32[]{:S(2)}) %collective-permute-start.6) | collective-permute-done | bytes 983072 | tf_op jit(solution)/shard_map/ppermute | solution.py:15
  124.8 1.0 collective-permute-start.12
  127.0 14.0 %collective-permute-done.12 = bf16[1920,128]{0,1:T(8,128)(2,1)} collective-permute-done((bf16[1920,128]{0,1:T(8,128)(2,1)S(1)}, bf16[1920,128]{0,1:T(8,128)(2,1)}, u32[]{:S(2)}, u32[]{:S(2)}) %collective-permute-start.12) | collective-permute-done | bytes 491552 | tf_op jit(solution)/shard_map/ppermute | solution.py:15
  140.9 1.1 fusion.41
  142.8 2.1 collective-permute-start.16
  145.8 10.5 %collective-permute-done.14 = bf16[1920,128]{0,1:T(8,128)(2,1)} collective-permute-done((bf16[1920,128]{0,1:T(8,128)(2,1)S(1)}, bf16[1920,128]{0,1:T(8,128)(2,1)}, u32[]{:S(2)}, u32[]{:S(2)}) %collective-permute-start.14) | collective-permute-done | bytes 491552 | tf_op jit(solution)/shard_map/ppermute | solution.py:15
  156.4 7.4 %collective-permute-done.16 = bf16[1920,128]{0,1:T(8,128)(2,1)} collective-permute-done((bf16[1920,128]{0,1:T(8,128)(2,1)S(1)}, bf16[1920,128]{0,1:T(8,128)(2,1)}, u32[]{:S(2)}, u32[]{:S(2)}) %collective-permute-start.16) | collective-permute-done | bytes 491552 | tf_op jit(solution)/shard_map/ppermute | solution.py:152
  163.7 1.4 broadcast_select_fusion.11
  165.9 1.7 collective-permute-start.19
  167.9 2.5 fusion.8
  170.5 11.0 %collective-permute-done.19 = bf16[1920,128]{0,1:T(8,128)(2,1)S(1)} collective-permute-done((bf16[1920,128]{0,1:T(8,128)(2,1)S(1)}, bf16[1920,128]{0,1:T(8,128)(2,1)S(1)}, u32[]{:S(2)}, u32[]{:S(2)}) %collective-permute-start.19) | collective-permute-done | bytes 491552 | tf_op jit(solution)/shard_map/ppermute | solution.py:15
  182.4 1.0 collective-permute-start.27
  183.4 1.8 collective-permute-start.28
  188.2 17.4 %collective-permute-start.20 = (bf16[12,48,256]{2,1,0:T(8,128)(2,1)S(1)}, bf16[12,48,256]{2,1,0:T(8,128)(2,1)S(1)}, u32[]{:S(2)}, u32[]{:S(2)}) collective-permute-start(bf16[12,48,256]{2,1,0:T(8,128)(2,1)S(1)} %pad_maximum_fusion.8), channel_id=1, source_target_pairs={{0,1},{1,2},{2,3},{3,0},{4,5},{5,6},{6,7},{7,4},{8,9},{9,10},{10,1... | collective-permute-start | bytes 884744 | tf_op jit(solution)/shard_map/ppermute | solution.py:11
  206.1 5.1 %collective-permute-done.20 = bf16[12,48,256]{2,1,0:T(8,128)(2,1)S(1)} collective-permute-done((bf16[12,48,256]{2,1,0:T(8,128)(2,1)S(1)}, bf16[12,48,256]{2,1,0:T(8,128)(2,1)S(1)}, u32[]{:S(2)}, u32[]{:S(2)}) %collective-permute-start.20) | collective-permute-done | bytes 294944 | tf_op jit(solution)/shard_map/ppermute | solution.py:11
  211.3 11.7 %collective-permute-start.21 = (bf16[12,48,256]{2,1,0:T(8,128)(2,1)S(1)}, bf16[12,48,256]{2,1,0:T(8,128)(2,1)S(1)}, u32[]{:S(2)}, u32[]{:S(2)}) collective-permute-start(bf16[12,48,256]{2,1,0:T(8,128)(2,1)S(1)} %broadcast_select_fusion.15), channel_id=1, source_target_pairs={{0,2},{1,3},{2,0},{3,1},{4,6},{5,7},{6,4},{7,5},{8,10},{9,11},{10,... | collective-permute-start | bytes 884744 | tf_op jit(solution)/shard_map/ppermute | solution.py:11
  224.7 10.5 %collective-permute-done.21 = bf16[12,48,256]{2,1,0:T(8,128)(2,1)S(1)} collective-permute-done((bf16[12,48,256]{2,1,0:T(8,128)(2,1)S(1)}, bf16[12,48,256]{2,1,0:T(8,128)(2,1)S(1)}, u32[]{:S(2)}, u32[]{:S(2)}) %collective-permute-start.21) | collective-permute-done | bytes 294944 | tf_op jit(solution)/shard_map/ppermute | solution.py:11
  238.3 1.0 collective-permute-start.30
  239.7 1.1 collective-permute-start.23
  240.9 0.9 collective-permute-start.24
  241.8 7.5 %collective-permute-done.30 = bf16[12,48,256]{2,1,0:T(8,128)(2,1)S(1)} collective-permute-done((bf16[12,48,256]{2,1,0:T(8,128)(2,1)S(1)}, bf16[12,48,256]{2,1,0:T(8,128)(2,1)S(1)}, u32[]{:S(2)}, u32[]{:S(2)}) %collective-permute-start.30) | collective-permute-done | bytes 294944 | tf_op jit(solution)/shard_map/ppermute | solution.py:11
  250.0 13.8 %collective-permute-done.31 = bf16[12,48,256]{2,1,0:T(8,128)(2,1)S(1)} collective-permute-done((bf16[12,48,256]{2,1,0:T(8,128)(2,1)S(1)}, bf16[12,48,256]{2,1,0:T(8,128)(2,1)S(1)}, u32[]{:S(2)}, u32[]{:S(2)}) %collective-permute-start.31) | collective-permute-done | bytes 294944 | tf_op jit(solution)/shard_map/ppermute | solution.py:11
  264.8 1.1 collective-permute-start.33
  267.8 2.7 collective-permute-done.33
  270.5 1.3 collective-permute-done.34
  272.9 1.1 pad_maximum_fusion.6
  274.0 2.1 copy.19
  (124 shorter events, 23.1 us)
Async XLA Ops:
  1.1 36.5 %collective-permute-start = (bf16[2048,128]{1,0:T(8,128)(2,1)S(1)}, bf16[2048,128]{1,0:T(8,128)(2,1)S(1)}, u32[]{:S(2)}, u32[]{:S(2)}) collective-permute-start(bf16[2048,128]{1,0:T(8,128)(2,1)S(1)} %constant_dynamic-slice_fusion), channel_id=1, source_target_pairs={{0,0},{1,4},{2,12},{3,8},{4,1},{5,5},{6,13},{7,9},{8,2},{9,6},{10,... | collective-permute-start | bytes 1572872 | tf_op jit(solution)/shard_map/ppermute | solution.py:194
  1.8 1.4 collective-permute-start.1
  5.1 14.4 %collective-permute-start.2 = (f32[1,512]{1,0:T(1,128)S(1)}, f32[1,512]{1,0:T(1,128)S(1)}, u32[]{:S(2)}, u32[]{:S(2)}) collective-permute-start(f32[1,512]{1,0:T(1,128)S(1)} %fusion.73), channel_id=1, source_target_pairs={{0,4},{4,0},{8,12},{12,8},{1,5},{5,1},{9,13},{13,9},{2,6},{6,2},{1... | collective-permute-start | bytes 6152 | tf_op jit(solution)/shard_map/ppermute | solution.py:15
  19.5 18.1 %collective-permute-start.3 = (f32[1,512]{1,0:T(1,128)S(1)}, f32[1,512]{1,0:T(1,128)S(1)}, u32[]{:S(2)}, u32[]{:S(2)}) collective-permute-start(f32[1,512]{1,0:T(1,128)S(1)} %add.178), channel_id=1, source_target_pairs={{0,8},{4,12},{8,0},{12,4},{1,9},{5,13},{9,1},{13,5},{2,10},{6,14},... | collective-permute-start | bytes 6152 | tf_op jit(solution)/shard_map/ppermute | solution.py:15
  37.6 13.2 %collective-permute-start.4 = (bf16[2048,128]{1,0:T(8,128)(2,1)S(1)}, bf16[2048,128]{1,0:T(8,128)(2,1)S(1)}, u32[]{:S(2)}, u32[]{:S(2)}) collective-permute-start(bf16[2048,128]{1,0:T(8,128)(2,1)S(1)} %collective-permute-done), channel_id=1, source_target_pairs={{0,8},{4,12},{8,0},{12,4},{1,9},{5,13},{9,1},{13,5},{2,10},{6,14},... | collective-permute-start | bytes 1572872 | tf_op jit(solution)/shard_map/ppermute | solution.py:15
  51.0 28.5 %collective-permute-start.5 = (bf16[2048,256]{1,0:T(8,128)(2,1)S(1)}, bf16[2048,256]{1,0:T(8,128)(2,1)S(1)}, u32[]{:S(2)}, u32[]{:S(2)}) collective-permute-start(bf16[2048,256]{1,0:T(8,128)(2,1)S(1)} %pad_maximum_fusion), channel_id=1, source_target_pairs={{0,4},{4,0},{8,12},{12,8},{1,5},{5,1},{9,13},{13,9},{2,6},{6,2},{1... | collective-permute-start | bytes 3145736 | tf_op jit(solution)/shard_map/ppermute | solution.py:15
  52.4 8.9 %collective-permute-start.7 = (bf16[1024,128]{1,0:T(8,128)(2,1)S(1)}, bf16[1024,128]{1,0:T(8,128)(2,1)}, u32[]{:S(2)}, u32[]{:S(2)}) collective-permute-start(bf16[1024,128]{1,0:T(8,128)(2,1)S(1)} %dynamic_slice.25), channel_id=1, source_target_pairs={{0,8},{4,12},{8,0},{12,4},{1,9},{5,13},{9,1},{13,5},{2,10},{6,14},... | collective-permute-start | bytes 786440 | tf_op jit(solution)/shard_map/ppermute | solution.py:15
  63.3 3.7 %collective-permute-start.8 = (bf16[1024,128]{1,0:T(8,128)(2,1)}, bf16[1024,128]{1,0:T(8,128)(2,1)}, u32[]{:S(2)}, u32[]{:S(2)}) collective-permute-start(bf16[1024,128]{1,0:T(8,128)(2,1)} %get-tuple-element.21), channel_id=1, source_target_pairs={{0,0},{1,4},{2,6},{3,2},{4,1},{5,5},{6,7},{7,3},{8,8},{9,12},{10,1... | collective-permute-start | bytes 786440 | tf_op jit(solution)/shard_map/ppermute | solution.py:123
  66.9 11.6 %collective-permute-start.9 = (bf16[1024,128]{1,0:T(8,128)(2,1)S(1)}, bf16[1024,128]{1,0:T(8,128)(2,1)}, u32[]{:S(2)}, u32[]{:S(2)}) collective-permute-start(bf16[1024,128]{1,0:T(8,128)(2,1)S(1)} %get-tuple-element.22), channel_id=1, source_target_pairs={{0,2},{1,6},{2,4},{3,0},{4,3},{5,7},{6,5},{7,1},{8,10},{9,14},{10,... | collective-permute-start | bytes 786440 | tf_op jit(solution)/shard_map/ppermute | solution.py:123
  79.5 6.8 %slice-start.3 = ((s8[7864320]{0:T(1024)(128)(4,1)}), s8[4194304]{0:T(1024)(128)(4,1)S(1)}, s32[]{:S(2)}) async-start(s8[7864320]{0:T(1024)(128)(4,1)} %bitcast.103), calls=%async_computation.3 | async-start | bytes 8388608
  79.9 6.5 %slice-start.4 = ((s8[7864320]{0:T(1024)(128)(4,1)}), s8[3670016]{0:T(1024)(128)(4,1)S(1)}, s32[]{:S(2)}) async-start(s8[7864320]{0:T(1024)(128)(4,1)} %bitcast.103), calls=%async_computation.4 | async-start | bytes 7340032
  85.7 14.1 %collective-permute-start.10 = (bf16[1024,256]{1,0:T(8,128)(2,1)S(1)}, bf16[1024,256]{1,0:T(8,128)(2,1)S(1)}, u32[]{:S(2)}, u32[]{:S(2)}) collective-permute-start(bf16[1024,256]{1,0:T(8,128)(2,1)S(1)} %pad_maximum_fusion.7), channel_id=1, source_target_pairs={{0,8},{4,12},{8,0},{12,4},{1,9},{5,13},{9,1},{13,5},{2,10},{6,14},... | collective-permute-start | bytes 1572872 | tf_op jit(solution)/shard_map/ppermute | solution.py:15
  100.0 2.9 %collective-permute-start.11 = (bf16[2048,256]{1,0:T(8,128)(2,1)S(1)}, bf16[2048,256]{1,0:T(8,128)(2,1)S(1)}, u32[]{:S(2)}, u32[]{:S(2)}) collective-permute-start(bf16[2048,256]{1,0:T(8,128)(2,1)S(1)} %pad_maximum_fusion.1), channel_id=1, source_target_pairs={{0,4},{4,0},{8,12},{12,8},{1,5},{5,1},{9,13},{13,9},{2,6},{6,2},{1... | collective-permute-start | bytes 3145736 | tf_op jit(solution)/shard_map/ppermute | solution.py:15
  100.6 23.9 %collective-permute-start.6 = (bf16[1920,256]{0,1:T(8,128)(2,1)S(1)}, bf16[1920,256]{0,1:T(8,128)(2,1)S(1)}, u32[]{:S(2)}, u32[]{:S(2)}) collective-permute-start(bf16[1920,256]{0,1:T(8,128)(2,1)S(1)} %fusion), channel_id=1, source_target_pairs={{0,1},{1,0},{2,3},{3,2},{4,5},{5,4},{6,7},{7,6},{8,9},{9,8},{10,11... | collective-permute-start | bytes 2949128 | tf_op jit(solution)/shard_map/ppermute | solution.py:15
  110.2 15.5 %copy-start.4 = (s32[4]{0:T(128)S(1)}, s32[4]{0:T(128)}, u32[]{:S(2)}) copy-start(s32[4]{0:T(128)} %param.14) | copy-start | bytes 52
  110.2 15.5 %copy-start.1 = (s32[4,4]{1,0:T(4,128)S(1)}, s32[4,4]{1,0:T(4,128)}, u32[]{:S(2)}) copy-start(s32[4,4]{1,0:T(4,128)} %param.13) | copy-start | bytes 196
  110.3 15.6 %copy-start.3 = (s32[4]{0:T(128)S(1)}, s32[4]{0:T(128)}, u32[]{:S(2)}) copy-start(s32[4]{0:T(128)} %param.15) | copy-start | bytes 52
  124.8 16.1 %collective-permute-start.12 = (bf16[1920,128]{0,1:T(8,128)(2,1)S(1)}, bf16[1920,128]{0,1:T(8,128)(2,1)}, u32[]{:S(2)}, u32[]{:S(2)}) collective-permute-start(bf16[1920,128]{0,1:T(8,128)(2,1)S(1)} %slice.139), channel_id=1, source_target_pairs={{0,3},{1,2},{2,1},{3,0},{4,7},{5,6},{6,5},{7,4},{8,11},{9,10},{10,... | collective-permute-start | bytes 1474568 | tf_op jit(solution)/shard_map/ppermute | solution.py:15
  126.1 39.2 %collective-permute-start.13 = (bf16[1920,256]{0,1:T(8,128)(2,1)}, bf16[1920,256]{0,1:T(8,128)(2,1)S(1)}, u32[]{:S(2)}, u32[]{:S(2)}) collective-permute-start(bf16[1920,256]{0,1:T(8,128)(2,1)} %fusion.1), channel_id=1, source_target_pairs={{0,1},{1,0},{2,3},{3,2},{4,5},{5,4},{6,7},{7,6},{8,9},{9,8},{10,11... | collective-permute-start | bytes 2949128 | tf_op jit(solution)/shard_map/ppermute | solution.py:15
  142.0 23.2 %copy-start = (f32[1920,256]{0,1:T(8,128)S(1)}, f32[1920,256]{0,1:T(8,128)}, u32[]{:S(2)}) copy-start(f32[1920,256]{0,1:T(8,128)} %convolution_bitcast_fusion) | copy-start | bytes 5898244
  142.0 14.3 %collective-permute-start.14 = (bf16[1920,128]{0,1:T(8,128)(2,1)S(1)}, bf16[1920,128]{0,1:T(8,128)(2,1)}, u32[]{:S(2)}, u32[]{:S(2)}) collective-permute-start(bf16[1920,128]{0,1:T(8,128)(2,1)S(1)} %fusion.41), channel_id=1, source_target_pairs={{0,8},{4,12},{8,0},{12,4},{1,9},{5,13},{9,1},{13,5},{2,10},{6,14},... | collective-permute-start | bytes 1474568 | tf_op jit(solution)/shard_map/ppermute | solution.py:15
  142.8 20.9 %collective-permute-start.16 = (bf16[1920,128]{0,1:T(8,128)(2,1)S(1)}, bf16[1920,128]{0,1:T(8,128)(2,1)}, u32[]{:S(2)}, u32[]{:S(2)}) collective-permute-start(bf16[1920,128]{0,1:T(8,128)(2,1)S(1)} %fusion.41), channel_id=1, source_target_pairs={{0,24},{1,25},{2,26},{3,27},{4,28},{5,29},{6,30},{7,31},{8,16},{9,... | collective-permute-start | bytes 1474568 | tf_op jit(solution)/shard_map/ppermute | solution.py:152
  145.1 20.2 %collective-permute-start.15 = (bf16[1920,128]{0,1:T(8,128)(2,1)S(1)}, bf16[1920,128]{0,1:T(8,128)(2,1)S(1)}, u32[]{:S(2)}, u32[]{:S(2)}) collective-permute-start(bf16[1920,128]{0,1:T(8,128)(2,1)S(1)} %fusion.41), channel_id=1, source_target_pairs={{0,16},{16,0},{1,17},{17,1},{2,18},{18,2},{3,19},{19,3},{4,20},{20... | collective-permute-start | bytes 1474568 | tf_op jit(solution)/shard_map/ppermute | solution.py:15
  163.7 21.4 %slice-start = ((s8[8847360]{0:T(1024)(128)(4,1)}), s8[4194304]{0:T(1024)(128)(4,1)S(1)}, s32[]{:S(2)}) async-start(s8[8847360]{0:T(1024)(128)(4,1)} %bitcast.94), calls=%async_computation | async-start | bytes 8388608
  165.4 19.7 %slice-start.1 = ((s8[8847360]{0:T(1024)(128)(4,1)}), s8[4194304]{0:T(1024)(128)(4,1)S(1)}, s32[]{:S(2)}) async-start(s8[8847360]{0:T(1024)(128)(4,1)} %bitcast.94), calls=%async_computation.1 | async-start | bytes 8388608
  165.8 19.3 %collective-permute-start.17 = (bf16[1920,256]{0,1:T(8,128)(2,1)S(1)}, bf16[1920,256]{0,1:T(8,128)(2,1)S(1)}, u32[]{:S(2)}, u32[]{:S(2)}) collective-permute-start(bf16[1920,256]{0,1:T(8,128)(2,1)S(1)} %pad_maximum_fusion.2), channel_id=1, source_target_pairs={{0,4},{4,0},{8,12},{12,8},{1,5},{5,1},{9,13},{13,9},{2,6},{6,2},{1... | collective-permute-start | bytes 2949128 | tf_op jit(solution)/shard_map/ppermute | solution.py:15
  165.9 15.5 %collective-permute-start.19 = (bf16[1920,128]{0,1:T(8,128)(2,1)S(1)}, bf16[1920,128]{0,1:T(8,128)(2,1)S(1)}, u32[]{:S(2)}, u32[]{:S(2)}) collective-permute-start(bf16[1920,128]{0,1:T(8,128)(2,1)S(1)} %slice.138), channel_id=1, source_target_pairs={{0,3},{1,2},{2,1},{3,0},{4,7},{5,6},{6,5},{7,4},{8,11},{9,10},{10,... | collective-permute-start | bytes 1474568 | tf_op jit(solution)/shard_map/ppermute | solution.py:15
  167.7 19.1 %collective-permute-start.18 = (bf16[1920,256]{0,1:T(8,128)(2,1)S(1)}, bf16[1920,256]{0,1:T(8,128)(2,1)S(1)}, u32[]{:S(2)}, u32[]{:S(2)}) collective-permute-start(bf16[1920,256]{0,1:T(8,128)(2,1)S(1)} %pad_maximum_fusion.3), channel_id=1, source_target_pairs={{0,4},{4,0},{8,12},{12,8},{1,5},{5,1},{9,13},{13,9},{2,6},{6,2},{1... | collective-permute-start | bytes 2949128 | tf_op jit(solution)/shard_map/ppermute | solution.py:15
  167.9 17.2 %slice-start.2 = ((s8[8847360]{0:T(1024)(128)(4,1)}), s8[458752]{0:T(1024)(128)(4,1)S(1)}, s32[]{:S(2)}) async-start(s8[8847360]{0:T(1024)(128)(4,1)} %bitcast.94), calls=%async_computation.2 | async-start | bytes 917504
  181.6 41.4 %collective-permute-start.25 = (bf16[1920,128]{0,1:T(8,128)(2,1)S(1)}, bf16[1920,128]{0,1:T(8,128)(2,1)S(1)}, u32[]{:S(2)}, u32[]{:S(2)}) collective-permute-start(bf16[1920,128]{0,1:T(8,128)(2,1)S(1)} %fusion.40), channel_id=1, source_target_pairs={{0,16},{16,0},{1,17},{17,1},{2,18},{18,2},{3,19},{19,3},{4,20},{20... | collective-permute-start | bytes 1474568 | tf_op jit(solution)/shard_map/ppermute | solution.py:15
  182.4 23.2 %collective-permute-start.27 = (bf16[1920,128]{0,1:T(8,128)(2,1)S(1)}, bf16[1920,128]{0,1:T(8,128)(2,1)S(1)}, u32[]{:S(2)}, u32[]{:S(2)}) collective-permute-start(bf16[1920,128]{0,1:T(8,128)(2,1)S(1)} %fusion.40), channel_id=1, source_target_pairs={{0,8},{4,12},{8,0},{12,4},{1,9},{5,13},{9,1},{13,5},{2,10},{6,14},... | collective-permute-start | bytes 1474568 | tf_op jit(solution)/shard_map/ppermute | solution.py:15
  183.4 22.7 %collective-permute-start.28 = (bf16[1920,128]{0,1:T(8,128)(2,1)S(1)}, bf16[1920,128]{0,1:T(8,128)(2,1)S(1)}, u32[]{:S(2)}, u32[]{:S(2)}) collective-permute-start(bf16[1920,128]{0,1:T(8,128)(2,1)S(1)} %fusion.40), channel_id=1, source_target_pairs={{0,24},{1,25},{2,26},{3,27},{4,28},{5,29},{6,30},{7,31},{8,16},{9,... | collective-permute-start | bytes 1474568 | tf_op jit(solution)/shard_map/ppermute | solution.py:152
  186.8 1.1 copy-start.2
  188.2 23.0 %collective-permute-start.20 = (bf16[12,48,256]{2,1,0:T(8,128)(2,1)S(1)}, bf16[12,48,256]{2,1,0:T(8,128)(2,1)S(1)}, u32[]{:S(2)}, u32[]{:S(2)}) collective-permute-start(bf16[12,48,256]{2,1,0:T(8,128)(2,1)S(1)} %pad_maximum_fusion.8), channel_id=1, source_target_pairs={{0,1},{1,2},{2,3},{3,0},{4,5},{5,6},{6,7},{7,4},{8,9},{9,10},{10,1... | collective-permute-start | bytes 884744 | tf_op jit(solution)/shard_map/ppermute | solution.py:11
  211.3 23.9 %collective-permute-start.21 = (bf16[12,48,256]{2,1,0:T(8,128)(2,1)S(1)}, bf16[12,48,256]{2,1,0:T(8,128)(2,1)S(1)}, u32[]{:S(2)}, u32[]{:S(2)}) collective-permute-start(bf16[12,48,256]{2,1,0:T(8,128)(2,1)S(1)} %broadcast_select_fusion.15), channel_id=1, source_target_pairs={{0,2},{1,3},{2,0},{3,1},{4,6},{5,7},{6,4},{7,5},{8,10},{9,11},{10,... | collective-permute-start | bytes 884744 | tf_op jit(solution)/shard_map/ppermute | solution.py:11
  223.2 12.5 %collective-permute-start.26 = (bf16[1920,256]{0,1:T(8,128)(2,1)S(1)}, bf16[1920,256]{0,1:T(8,128)(2,1)S(1)}, u32[]{:S(2)}, u32[]{:S(2)}) collective-permute-start(bf16[1920,256]{0,1:T(8,128)(2,1)S(1)} %pad_maximum_fusion.4), channel_id=1, source_target_pairs={{0,4},{4,0},{8,12},{12,8},{1,5},{5,1},{9,13},{13,9},{2,6},{6,2},{1... | collective-permute-start | bytes 2949128 | tf_op jit(solution)/shard_map/ppermute | solution.py:15
  223.3 14.0 %collective-permute-start.29 = (bf16[1920,256]{0,1:T(8,128)(2,1)S(1)}, bf16[1920,256]{0,1:T(8,128)(2,1)S(1)}, u32[]{:S(2)}, u32[]{:S(2)}) collective-permute-start(bf16[1920,256]{0,1:T(8,128)(2,1)S(1)} %pad_maximum_fusion.5), channel_id=1, source_target_pairs={{0,4},{4,0},{8,12},{12,8},{1,5},{5,1},{9,13},{13,9},{2,6},{6,2},{1... | collective-permute-start | bytes 2949128 | tf_op jit(solution)/shard_map/ppermute | solution.py:15
  238.3 11.0 %collective-permute-start.30 = (bf16[12,48,256]{2,1,0:T(8,128)(2,1)S(1)}, bf16[12,48,256]{2,1,0:T(8,128)(2,1)S(1)}, u32[]{:S(2)}, u32[]{:S(2)}) collective-permute-start(bf16[12,48,256]{2,1,0:T(8,128)(2,1)S(1)} %pad_maximum_fusion.9), channel_id=1, source_target_pairs={{0,1},{1,2},{2,3},{3,0},{4,5},{5,6},{6,7},{7,4},{8,9},{9,10},{10,1... | collective-permute-start | bytes 884744 | tf_op jit(solution)/shard_map/ppermute | solution.py:11
  239.5 10.1 %collective-permute-start.22 = (bf16[4,48,2,1,128]{4,2,1,0,3:T(2,128)(2,1)S(1)}, bf16[4,48,2,1,128]{4,2,1,0,3:T(2,128)(2,1)S(1)}, u32[]{:S(2)}, u32[]{:S(2)}) collective-permute-start(bf16[4,48,2,1,128]{4,2,1,0,3:T(2,128)(2,1)S(1)} %squeeze.25), channel_id=1, source_target_pairs={{0,4},{4,0},{8,12},{12,8},{1,5},{5,1},{9,13},{13,9},{2,6},{6,2},{1... | collective-permute-start | bytes 294920 | tf_op jit(solution)/shard_map/ppermute | solution.py:15
  239.7 9.9 %collective-permute-start.23 = (bf16[4,48,2,1,128]{4,2,1,0,3:T(2,128)(2,1)S(1)}, bf16[4,48,2,1,128]{4,2,1,0,3:T(2,128)(2,1)S(1)}, u32[]{:S(2)}, u32[]{:S(2)}) collective-permute-start(bf16[4,48,2,1,128]{4,2,1,0,3:T(2,128)(2,1)S(1)} %squeeze.26), channel_id=1, source_target_pairs={{0,8},{4,12},{8,0},{12,4},{1,9},{5,13},{9,1},{13,5},{2,10},{6,14},... | collective-permute-start | bytes 294920 | tf_op jit(solution)/shard_map/ppermute | solution.py:15
  240.9 8.7 %collective-permute-start.24 = (bf16[4,48,2,1,128]{4,2,1,0,3:T(2,128)(2,1)S(1)}, bf16[4,48,2,1,128]{4,2,1,0,3:T(2,128)(2,1)S(1)}, u32[]{:S(2)}, u32[]{:S(2)}) collective-permute-start(bf16[4,48,2,1,128]{4,2,1,0,3:T(2,128)(2,1)S(1)} %squeeze.27), channel_id=1, source_target_pairs={{0,12},{4,8},{8,4},{12,0},{1,13},{5,9},{9,5},{13,1},{2,14},{6,10},... | collective-permute-start | bytes 294920 | tf_op jit(solution)/shard_map/ppermute | solution.py:15
  249.4 14.5 %collective-permute-start.31 = (bf16[12,48,256]{2,1,0:T(8,128)(2,1)S(1)}, bf16[12,48,256]{2,1,0:T(8,128)(2,1)S(1)}, u32[]{:S(2)}, u32[]{:S(2)}) collective-permute-start(bf16[12,48,256]{2,1,0:T(8,128)(2,1)S(1)} %broadcast_select_fusion.14), channel_id=1, source_target_pairs={{0,2},{1,3},{2,0},{3,1},{4,6},{5,7},{6,4},{7,5},{8,10},{9,11},{10,... | collective-permute-start | bytes 884744 | tf_op jit(solution)/shard_map/ppermute | solution.py:11
  264.6 3.1 %collective-permute-start.32 = (bf16[4,48,2,1,128]{4,2,1,0,3:T(2,128)(2,1)S(1)}, bf16[4,48,2,1,128]{4,2,1,0,3:T(2,128)(2,1)S(1)}, u32[]{:S(2)}, u32[]{:S(2)}) collective-permute-start(bf16[4,48,2,1,128]{4,2,1,0,3:T(2,128)(2,1)S(1)} %squeeze.29), channel_id=1, source_target_pairs={{0,4},{4,0},{8,12},{12,8},{1,5},{5,1},{9,13},{13,9},{2,6},{6,2},{1... | collective-permute-start | bytes 294920 | tf_op jit(solution)/shard_map/ppermute | solution.py:15
  264.8 5.7 %collective-permute-start.33 = (bf16[4,48,2,1,128]{4,2,1,0,3:T(2,128)(2,1)S(1)}, bf16[4,48,2,1,128]{4,2,1,0,3:T(2,128)(2,1)S(1)}, u32[]{:S(2)}, u32[]{:S(2)}) collective-permute-start(bf16[4,48,2,1,128]{4,2,1,0,3:T(2,128)(2,1)S(1)} %squeeze.30), channel_id=1, source_target_pairs={{0,8},{4,12},{8,0},{12,4},{1,9},{5,13},{9,1},{13,5},{2,10},{6,14},... | collective-permute-start | bytes 294920 | tf_op jit(solution)/shard_map/ppermute | solution.py:15
  266.0 5.7 %collective-permute-start.34 = (bf16[4,48,2,1,128]{4,2,1,0,3:T(2,128)(2,1)S(1)}, bf16[4,48,2,1,128]{4,2,1,0,3:T(2,128)(2,1)S(1)}, u32[]{:S(2)}, u32[]{:S(2)}) collective-permute-start(bf16[4,48,2,1,128]{4,2,1,0,3:T(2,128)(2,1)S(1)} %squeeze.31), channel_id=1, source_target_pairs={{0,12},{4,8},{8,4},{12,0},{1,13},{5,9},{9,5},{13,1},{2,14},{6,10},... | collective-permute-start | bytes 294920 | tf_op jit(solution)/shard_map/ppermute | solution.py:15

commit v6 on v0

--- a/solution.py
+++ b/solution.py
@@ -11,11 +11,24 @@
     return lax.ppermute(shard, axis, [(i, (i + by) % count) for i in range(count)])
 
 
+def swapped(shard, axis, bit):
+    return lax.ppermute(shard, axis, [(i, i ^ bit) for i in range(lax.axis_size(axis))])
+
+
 def add_columns(operand, portion):
     return jnp.dot(operand, portion, preferred_element_type=jnp.float32)
 
 
-def on_device(
+def routing(tile_map, tile_count, decode_owner, tile_slots, head_groups):
+    most_tiles = tile_map.shape[1]
+    owner_tile = decode_owner // head_groups
+    owner_turn = decode_owner % head_groups
+    usable = jnp.arange(most_tiles)[None, :] < tile_count[:, None]
+    matched = (tile_map[:, :, None] == jnp.arange(tile_slots)[None, None, :]) & usable[:, :, None]
+    return owner_tile, owner_turn, matched
+
+
+def gather_plan(
     features, proj_weight, proj_bias, kv_weight, key_gain, tile_map, tile_count, decode_owner
 ):
     tile_slots, shard_len, feature_width = features.shape
@@ -37,16 +50,13 @@
     tile_ranks = lax.axis_size("tile")
     head_groups = lax.axis_size("head")
     most_tiles = tile_map.shape[1]
-    owner_tile = decode_owner // head_groups
-    owner_turn = decode_owner % head_groups
+    owner_tile, owner_turn, matched = routing(
+        tile_map, tile_count, decode_owner, tile_slots, head_groups
+    )
     owned_by = (owner_tile[:, None] == jnp.arange(tile_ranks)[None, :]).astype(jnp.float32)
-    usable = jnp.arange(most_tiles)[None, :] < tile_count[:, None]
-    matched = (
-        (tile_map[:, :, None] == jnp.arange(tile_slots)[None, None, :]) & usable[:, :, None]
-    ).astype(jnp.float32)
-    selector = jnp.einsum("rd,rjs->jds", owned_by, matched).astype(jnp.bfloat16)
-    selector = selector.reshape(most_tiles * tile_ranks, tile_slots)
-    outgoing = jnp.dot(selector, per_tile, preferred_element_type=jnp.float32).astype(jnp.bfloat16)
+    selector = jnp.einsum("rd,rjs->jds", owned_by, matched.astype(jnp.float32))
+    selector = selector.astype(jnp.bfloat16).reshape(most_tiles * tile_ranks, tile_slots)
+    outgoing = add_columns(selector, per_tile).astype(jnp.bfloat16)
     outgoing = outgoing.reshape(most_tiles, tile_ranks, shard_len, kv_width)
     arrived = lax.all_to_all(outgoing, "tile", split_axis=1, concat_axis=1, tiled=True)
     gathered_rows = arrived.reshape(
@@ -59,6 +69,176 @@
         gathered_rows = jnp.where(my_turn // stride % 2 == 1, shifted, gathered_rows)
         stride = stride * 2
     return gathered_rows[None, None]
+
+
+def product_plan(
+    features, proj_weight, proj_bias, kv_weight, key_gain, tile_map, tile_count, decode_owner
+):
+    tile_slots, shard_len, feature_width = features.shape
+    token_rows = tile_slots * shard_len
+    depth = proj_weight.shape[0]
+    layers, head_dim = key_gain.shape
+    width = layers * head_dim
+    most_tiles = tile_map.shape[1]
+    group, tile, head = (lax.axis_index(name) for name in ("groups", "tile", "head"))
+    first_core, first_chip = tile % 2 == 0, tile < 2
+    at_end = (head == 0) | (head == 3)
+    feature_rows = features.reshape(token_rows, feature_width)
+    step = lax.optimization_barrier
+
+    def moved(shard, target):
+        pairs = []
+        for t in range(4):
+            for h in range(4):
+                to_tile, to_head = target(t, h)
+                pairs.append((t * 4 + h, to_tile * 4 + to_head))
+        return lax.ppermute(shard, ("tile", "head"), pairs)
+
+    def outer_core(h):
+        return (h ^ h // 2) % 2
+
+    def times_features(rows, r):
+        columns = lax.dynamic_slice_in_dim(feature_rows, (tile ^ r) * depth, depth, axis=1)
+        return add_columns(columns, rows)
+
+    def put_first(condition, one, other, axis):
+        return jnp.concatenate(
+            [jnp.where(condition, one, other), jnp.where(condition, other, one)], axis=axis
+        )
+
+    def both_heads(ours, theirs):
+        return put_first(group == 0, ours, theirs, 1)
+
+    def products(near, far):
+        near_product, far_product = add_columns(proj_weight, near), add_columns(proj_weight, far)
+        near_kept = at_end == first_core
+        kept = jnp.where(near_kept, near_product, far_product)
+        sent = jnp.where(near_kept, far_product, near_product)
+        parts = [sent[:, width:], kept[:, width:], sent[:, :width]]
+        return kept[:, :width], [part.astype(jnp.bfloat16) for part in parts]
+
+    def exchange(parts):
+        return [swapped(part, "head", bit) for part, bit in zip(parts, (2, 3, 1))]
+
+    def summed(kept, arrived):
+        total = kept
+        for block in arrived:
+            total = total + block.astype(jnp.float32)
+        return total.astype(jnp.bfloat16)
+
+    def finish(total, part):
+        finished = []
+        for k in range(2):
+            entries = total[:, k * width : (k + 1) * width].reshape(token_rows, layers, head_dim)
+            entries = entries + bias_part[k, :, part][None]
+            if part == 0:
+                squares = jnp.mean(entries * entries, axis=-1, keepdims=True)
+                entries = entries * lax.rsqrt(squares + eps_norm) * key_gain[None]
+            finished.append(entries.reshape(token_rows, width).astype(jnp.bfloat16))
+        return jnp.concatenate(finished, axis=1).reshape(tile_slots, shard_len, 2 * width)
+
+    owner_tile, owner_turn, matched = routing(tile_map, tile_count, decode_owner, tile_slots, 4)
+    turn_of = jnp.sum(jnp.where(matched, owner_turn[:, None, None], 0), axis=(0, 1))
+    owned_by = (owner_tile[:, None] == (tile ^ jnp.arange(4))[None, :]).astype(jnp.float32)
+    selector = jnp.einsum("rd,rjs->djs", owned_by, matched.astype(jnp.float32))
+    selector = selector.astype(jnp.bfloat16).reshape(4 * most_tiles, tile_slots)
+
+    def rolled(rows, shifted, stride):
+        odd = (turn_of // stride % 2 == 1)[:, None, None]
+        return jnp.where(odd, shifted, rows)
+
+    def outgoing(rows):
+        picked = add_columns(selector, rows.reshape(tile_slots, -1)).astype(jnp.bfloat16)
+        picked = picked.reshape(4, most_tiles, shard_len, 2, layers, head_dim)
+        return [picked[r] for r in range(4)]
+
+    def to_owners(picked):
+        return [picked[0]] + [swapped(picked[r], "tile", r) for r in (1, 2, 3)]
+
+    def in_order(arrived):
+        even = [jnp.where(first_core, arrived[r], arrived[r ^ 1]) for r in range(4)]
+        ranked = [jnp.where(first_chip, even[r], even[r ^ 2]) for r in range(4)]
+        return jnp.stack(ranked, axis=1)
+
+    column, half = group * 2 * head_dim, kv_weight.shape[0] // 2
+    key_mine = lax.dynamic_slice_in_dim(kv_weight, column, head_dim, axis=1)
+    value_mine = lax.dynamic_slice_in_dim(kv_weight, column + head_dim, head_dim, axis=1)
+    stays = lax.dynamic_slice_in_dim(value_mine, tile // 2 * half, half, axis=0)
+    leaves = lax.dynamic_slice_in_dim(value_mine, half - tile // 2 * half, half, axis=0)
+    bias_rows = moved(proj_bias, lambda t, h: (h, t))
+    key_block = moved(key_mine, lambda t, h: (h // 2 * 2 + outer_core(h), t))
+    comes = swapped(leaves, "tile", 2)
+    bias_rows, key_block, comes, stays = step((bias_rows, key_block, comes, stays))
+
+    value_pieces = []
+    for j in range(2):
+        piece = jnp.where(tile // 2 == (head // 2) ^ j, stays, comes)
+        value_pieces.append(
+            moved(piece, lambda t, h: (t // 2 * 2 + outer_core(h), t % 2 + 2 * ((h // 2) ^ j)))
+        )
+    key_other = swapped(key_block, "tile", 2)
+    bias_part = add_columns(bias_rows[None], kv_weight)
+    value_pieces, key_block, key_other, bias_part = step(
+        (value_pieces, key_block, key_other, bias_part)
+    )
+
+    key_near = put_first(tile // 2 == head // 2, key_block, key_other, 1)
+    value_half = jnp.concatenate(value_pieces, axis=1)
+    key_near, value_half = step((key_near, value_half))
+    key_kept, key_parts = products(key_near, swapped(key_near, "tile", 1))
+    bias_part = bias_part + swapped(bias_part, "tile", 1)
+    key_kept, key_parts, value_half, bias_part = step((key_kept, key_parts, value_half, bias_part))
+
+    key_arrived = exchange(key_parts)
+    value_other = swapped(value_half, "tile", 2)
+    bias_part = bias_part + swapped(bias_part, "tile", 2)
+    value_near = put_first(first_chip, value_half, value_other, 0)
+    value_kept, value_parts = products(value_near, swapped(value_near, "tile", 1))
+    key_kept, key_arrived, value_kept, value_parts, bias_part = step(
+        (key_kept, key_arrived, value_kept, value_parts, bias_part)
+    )
+    bias_part = bias_part.reshape(2, layers, 2, head_dim)
+
+    value_arrived = exchange(value_parts)
+    own = summed(key_kept, key_arrived)
+    across_x, across_y = step((swapped(own, "tile", 2), swapped(own, "groups", 1)))
+    rows_0 = step(both_heads(own, across_y))
+    rows_1, diagonal = step((swapped(rows_0, "tile", 1), swapped(across_y, "tile", 2)))
+    rows_2 = step(both_heads(across_x, diagonal))
+    total = times_features(rows_0, 0) + times_features(rows_1, 1)
+    total = total + times_features(rows_2, 2) + times_features(swapped(rows_2, "tile", 1), 3)
+    keys = finish(total, 0)
+    keys, value_kept, value_arrived = step((keys, value_kept, value_arrived))
+
+    own = summed(value_kept, value_arrived)
+    own, across_x, across_y, shifted, keys = step(
+        (
+            own,
+            swapped(own, "tile", 2),
+            swapped(own, "groups", 1),
+            shifted_2(keys, "head", 1),
+            keys,
+        )
+    )
+
+    keys = rolled(keys, shifted, 1)
+    rows_0, keys = step((both_heads(own, across_y), keys))
+    shifted, diagonal = shifted_2(keys, "head", 2), swapped(across_x, "groups", 1)
+    total = times_features(rows_0, 0) + times_features(swapped(rows_0, "tile", 1), 1)
+    rows_2 = step(both_heads(across_x, diagonal))
+    total = total + times_features(rows_2, 2) + times_features(swapped(rows_2, "tile", 1), 3)
+    values = finish(total, 1)
+    shifted, values, keys = step((shifted, values, keys))
+
+    picked = outgoing(rolled(keys, shifted, 2))
+    arrived, shifted, values = step((to_owners(picked), shifted_2(values, "head", 1), values))
+
+    values = rolled(values, shifted, 1)
+    key_cache, shifted, values = step((in_order(arrived), shifted_2(values, "head", 2), values))
+
+    value_cache = in_order(to_owners(outgoing(rolled(values, shifted, 2))))
+    cache = jnp.stack([key_cache, value_cache], axis=-2)
+    return cache.reshape(1, 1, most_tiles * 4 * shard_len, 4 * layers, head_dim)
 
 
 def solution(mesh):
@@ -72,8 +252,9 @@
         P("groups"),
         P("groups"),
     )
+    sizes = tuple(mesh.shape[name] for name in ("groups", "tile", "head"))
     return jax.shard_map(
-        on_device,
+        product_plan if sizes == (2, 4, 4) else gather_plan,
         mesh=mesh,
         in_specs=placed,
         out_specs=P(("groups", "tile"), "head", None, None, None),

time: 524 us -> 281 us (0.54)
  waiting for transfers between devices: 448 us -> 152 us
  starting transfers between devices: 0.21 us -> 76.4 us
  between operations: 15.9 us -> 0.86 us
  blocking collectives: 14.2 us -> 0 us
  local copies, waits for them, and re-layouts: 2.39 us -> 10.8 us
    all_gather x3 -> x0, waiting for transfers between devices: 395 us -> none  [the longest x1 193 us: on_device(): weight_cols = lax.all_gather(proj_weight, 'tile', axis=0, tiled=True)]
    ppermute x0 -> x33, waiting for transfers between devices: none -> 121 us  [the longest x29 113 us: swapped(): lax.ppermute(shard, axis, [(i, i ^ bit) for i in range(lax.axis_size(axis...]
    ppermute x0 -> x33, starting transfers between devices: none -> 53.5 us  [the longest x29 51.4 us: swapped(): lax.ppermute(shard, axis, [(i, i ^ bit) for i in range(lax.axis_size(axis...]
    dot_general x3 -> x1, matrix products: 26.3 us -> 0.19 us  [product_plan(): selector = jnp.einsum('rd,rjs->djs', owned_by, matched.astype(jnp.float32))]
    ppermute x2 -> x4, starting transfers between devices: 0.13 us -> 22.9 us  [shifted_2(): lax.ppermute(shard, axis, [(i, (i + by) % count) for i in range(count)])]
    dot_general x1 -> x15, matrix products: 10 us -> 32.3 us  [add_columns(): return jnp.dot(operand, portion, preferred_element_type=jnp.float32)]
    ppermute x2 -> x4, waiting for transfers between devices: 52 us -> 30.4 us  [shifted_2(): lax.ppermute(shard, axis, [(i, (i + by) % count) for i in range(count)])]
    all_to_all x1 -> x0, blocking collectives: 14.2 us -> none  [on_device(): lax.all_to_all(outgoing, 'tile', split_axis=1, concat_axis=1, tiled=True)]
  transfers between devices with their start and end apart: 5 -> 37, of which waited for: 5 -> 20; matrix products, arithmetic and copies ran while one was open for 5% -> 13% of each run, Pallas kernels for 0% -> 0%
where the time goes in v6:
time: 281 us; the launch traced here: 280 us
  waiting for transfers between devices  152 us (54%)
  starting transfers between devices  76.4 us (27%)
  matrix products  32.5 us (12%)
  local copies, waits for them, and re-layouts  10.8 us (4%)
  other arithmetic  7.95 us (3%)
    ppermute x29, waiting for transfers between devices, swapped(): lax.ppermute(shard, axis, [(i, i ^ bit) for i in range(lax.axis_size(axis...  113 us
    ppermute x29, starting transfers between devices, swapped(): lax.ppermute(shard, axis, [(i, i ^ bit) for i in range(lax.axis_size(axis...  51.4 us
    dot_general x15, matrix products, add_columns(): return jnp.dot(operand, portion, preferred_element_type=jnp.float32)  32.3 us
    ppermute x4, waiting for transfers between devices, shifted_2(): lax.ppermute(shard, axis, [(i, (i + by) % count) for i in range(count)])  30.4 us
    ppermute x4, starting transfers between devices, shifted_2(): lax.ppermute(shard, axis, [(i, (i + by) % count) for i in range(count)])  22.9 us
    ppermute x4, waiting for transfers between devices, moved(): return lax.ppermute(shard, ('tile', 'head'), pairs)  8.25 us
  transfers between devices with their start and end apart: 37, of which 20 were waited for; matrix products, arithmetic and copies ran while one was open for 13% of the time, Pallas kernels for 0%

profile of v6, /device:TPU:0, one launch (start us, length us, event | category | flops | bytes accessed | tf_op | source)
XLA Modules:
  0.0 280.5 jit_solution(14328755845998127434)
XLA Ops:
  0.0 1.2 constant_dynamic-slice_fusion
  2.0 2.3 fusion.66
  4.2 6.7 %collective-permute-start.2 = (bf16[1024,128]{1,0:T(8,128)(2,1)}, bf16[1024,128]{1,0:T(8,128)(2,1)}, u32[]{:S(2)}, u32[]{:S(2)}) collective-permute-start(bf16[1024,128]{1,0:T(8,128)(2,1)} %get-tuple-element.116), channel_id=1, source_target_pairs={{0,8},{4,12},{8,0},{12,4},{1,9},{5,13},{9,1},{13,5},{2,10},{6,14},... | collective-permute-start | bytes 786440 | tf_op jit(solution)/shard_map/ppermute | solution.py:15
  11.6 11.7 %collective-permute-done.2 = bf16[1024,128]{1,0:T(8,128)(2,1)} collective-permute-done((bf16[1024,128]{1,0:T(8,128)(2,1)}, bf16[1024,128]{1,0:T(8,128)(2,1)}, u32[]{:S(2)}, u32[]{:S(2)}) %collective-permute-start.2) | collective-permute-done | bytes 262176 | tf_op jit(solution)/shard_map/ppermute | solution.py:15
  23.3 9.8 %collective-permute-start.5 = (bf16[2048,128]{1,0:T(8,128)(2,1)S(1)}, bf16[2048,128]{1,0:T(8,128)(2,1)S(1)}, u32[]{:S(2)}, u32[]{:S(2)}) collective-permute-start(bf16[2048,128]{1,0:T(8,128)(2,1)S(1)} %collective-permute-done.1), channel_id=1, source_target_pairs={{0,8},{4,12},{8,0},{12,4},{1,9},{5,13},{9,1},{13,5},{2,10},{6,14},... | collective-permute-start | bytes 1572872 | tf_op jit(solution)/shard_map/ppermute | solution.py:15
  35.3 8.2 %collective-permute-done.4 = bf16[1024,128]{1,0:T(8,128)(2,1)S(1)} collective-permute-done((bf16[1024,128]{1,0:T(8,128)(2,1)S(1)}, bf16[1024,128]{1,0:T(8,128)(2,1)S(1)}, u32[]{:S(2)}, u32[]{:S(2)}) %collective-permute-start.4) | collective-permute-done | bytes 262176 | tf_op jit(solution)/shard_map/ppermute | solution.py:95
  43.5 1.5 collective-permute-done.5
  45.3 2.1 collective-permute-start.6
  47.4 5.6 %fusion.72 = f32[256,1920]{1,0:T(8,128)S(1)} fusion(bf16[2048,256]{1,0:T(8,128)(2,1)S(1)} %pad_maximum_fusion, bf16[1920,2048]{1,0:T(8,128)(2,1)} %param.9), kind=kOutput, calls=%fused_computation.148 | convolution fusion | flops 2013265920 | bytes 10878976 | tf_op jit(solution)/shard_map/dot_general | solution.py:19
  53.1 5.7 %fusion.73 = f32[256,1920]{1,0:T(8,128)S(1)} fusion(bf16[2048,256]{1,0:T(8,128)(2,1)S(1)} %collective-permute-done.6, bf16[1920,2048]{1,0:T(8,128)(2,1)} %param.9), kind=kOutput, calls=%fused_computation.149 | convolution fusion | flops 2013265920 | bytes 10878976 | tf_op jit(solution)/shard_map/dot_general | solution.py:19
  59.4 1.1 copy-done.1
  61.6 13.2 %collective-permute-done.11 = bf16[1024,256]{1,0:T(8,128)(2,1)S(1)} collective-permute-done((bf16[1024,256]{1,0:T(8,128)(2,1)S(1)}, bf16[1024,256]{1,0:T(8,128)(2,1)S(1)}, u32[]{:S(2)}, u32[]{:S(2)}) %collective-permute-start.11) | collective-permute-done | bytes 524320 | tf_op jit(solution)/shard_map/ppermute | solution.py:15
  77.9 1.7 collective-permute-start.10
  79.6 5.8 %fusion.65 = f32[256,1920]{1,0:T(8,128)S(1)} fusion(bf16[1920,2048]{1,0:T(8,128)(2,1)} %param.9, bf16[1024,256]{1,0:T(8,128)(2,1)S(1)} %get-tuple-element.118, bf16[1024,256]{1,0:T(8,128)(2,1)S(1)} %get-tuple-element.117), kind=kOutput, calls=%fused_computation.141 | convolution fusion | flops 2015363072 | bytes 10878976 | tf_op jit(solution)/shard_map/dot_general | solution.py:19
  85.5 2.4 fusion.74
  90.6 20.0 %collective-permute-done.8 = bf16[1920,128]{0,1:T(8,128)(2,1)S(1)} collective-permute-done((bf16[1920,128]{0,1:T(8,128)(2,1)S(1)}, bf16[1920,128]{0,1:T(8,128)(2,1)S(1)}, u32[]{:S(2)}, u32[]{:S(2)}) %collective-permute-start.8) | collective-permute-done | bytes 491552 | tf_op jit(solution)/shard_map/ppermute | solution.py:15
  110.6 1.3 collective-permute-done.10
  112.3 1.6 collective-permute-start.15
  113.9 1.7 collective-permute-start.14
  115.5 8.9 %collective-permute-done.15 = bf16[1920,128]{0,1:T(8,128)(2,1)S(1)} collective-permute-done((bf16[1920,128]{0,1:T(8,128)(2,1)S(1)}, bf16[1920,128]{0,1:T(8,128)(2,1)S(1)}, u32[]{:S(2)}, u32[]{:S(2)}) %collective-permute-start.15) | collective-permute-done | bytes 491552 | tf_op jit(solution)/shard_map/ppermute | solution.py:15
  124.5 1.2 collective-permute-done.14
  126.0 1.8 collective-permute-start.17
  127.8 11.8 %collective-permute-done.17 = bf16[1920,128]{0,1:T(8,128)(2,1)S(1)} collective-permute-done((bf16[1920,128]{0,1:T(8,128)(2,1)S(1)}, bf16[1920,128]{0,1:T(8,128)(2,1)S(1)}, u32[]{:S(2)}, u32[]{:S(2)}) %collective-permute-start.17) | collective-permute-done | bytes 491552 | tf_op jit(solution)/shard_map/ppermute | solution.py:15
  140.0 12.0 %collective-permute-start.19 = (bf16[1920,128]{0,1:T(8,128)(2,1)}, bf16[1920,128]{0,1:T(8,128)(2,1)S(1)}, u32[]{:S(2)}, u32[]{:S(2)}) collective-permute-start(bf16[1920,128]{0,1:T(8,128)(2,1)} %get-tuple-element.86), channel_id=1, source_target_pairs={{0,2},{1,3},{2,0},{3,1},{4,6},{5,7},{6,4},{7,5},{8,10},{9,11},{10,... | collective-permute-start | bytes 1474568 | tf_op jit(solution)/shard_map/ppermute | solution.py:15
  152.0 1.3 collective-permute-start.20
  153.3 2.6 fusion.14
  155.9 2.6 fusion.6
  158.5 2.7 fusion.2
  162.6 22.7 %collective-permute-done.19 = bf16[1920,128]{0,1:T(8,128)(2,1)S(1)} collective-permute-done((bf16[1920,128]{0,1:T(8,128)(2,1)}, bf16[1920,128]{0,1:T(8,128)(2,1)S(1)}, u32[]{:S(2)}, u32[]{:S(2)}) %collective-permute-start.19) | collective-permute-done | bytes 491552 | tf_op jit(solution)/shard_map/ppermute | solution.py:15
  185.4 1.1 collective-permute-done.21
  187.3 1.7 collective-permute-start.22
  189.0 16.1 %collective-permute-start.24 = (bf16[12,48,256]{2,1,0:T(8,128)(2,1)S(1)}, bf16[12,48,256]{2,1,0:T(8,128)(2,1)S(1)}, u32[]{:S(2)}, u32[]{:S(2)}) collective-permute-start(bf16[12,48,256]{2,1,0:T(8,128)(2,1)S(1)} %pad_maximum_fusion.9), channel_id=1, source_target_pairs={{0,1},{1,2},{2,3},{3,0},{4,5},{5,6},{6,7},{7,4},{8,9},{9,10},{10,1... | collective-permute-start | bytes 884744 | tf_op jit(solution)/shard_map/ppermute | solution.py:11
  205.3 5.6 %collective-permute-done.24 = bf16[12,48,256]{2,1,0:T(8,128)(2,1)S(1)} collective-permute-done((bf16[12,48,256]{2,1,0:T(8,128)(2,1)S(1)}, bf16[12,48,256]{2,1,0:T(8,128)(2,1)S(1)}, u32[]{:S(2)}, u32[]{:S(2)}) %collective-permute-start.24) | collective-permute-done | bytes 294944 | tf_op jit(solution)/shard_map/ppermute | solution.py:11
  211.0 1.5 collective-permute-start.27
  212.7 9.8 %collective-permute-done.27 = bf16[1920,128]{0,1:T(8,128)(2,1)S(1)} collective-permute-done((bf16[1920,128]{0,1:T(8,128)(2,1)S(1)}, bf16[1920,128]{0,1:T(8,128)(2,1)S(1)}, u32[]{:S(2)}, u32[]{:S(2)}) %collective-permute-start.27) | collective-permute-done | bytes 491552 | tf_op jit(solution)/shard_map/ppermute | solution.py:15
  223.6 4.7 %collective-permute-start.25 = (bf16[12,48,256]{2,1,0:T(8,128)(2,1)S(1)}, bf16[12,48,256]{2,1,0:T(8,128)(2,1)S(1)}, u32[]{:S(2)}, u32[]{:S(2)}) collective-permute-start(bf16[12,48,256]{2,1,0:T(8,128)(2,1)S(1)} %broadcast_select_fusion.13), channel_id=1, source_target_pairs={{0,2},{1,3},{2,0},{3,1},{4,6},{5,7},{6,4},{7,5},{8,10},{9,11},{10,... | collective-permute-start | bytes 884744 | tf_op jit(solution)/shard_map/ppermute | solution.py:11
  231.7 10.1 %collective-permute-done.25 = bf16[12,48,256]{2,1,0:T(8,128)(2,1)S(1)} collective-permute-done((bf16[12,48,256]{2,1,0:T(8,128)(2,1)S(1)}, bf16[12,48,256]{2,1,0:T(8,128)(2,1)S(1)}, u32[]{:S(2)}, u32[]{:S(2)}) %collective-permute-start.25) | collective-permute-done | bytes 294944 | tf_op jit(solution)/shard_map/ppermute | solution.py:11
  243.6 1.8 collective-permute-start.30
  245.6 3.6 %collective-permute-done.30 = bf16[4,48,2,1,128]{4,2,1,0,3:T(2,128)(2,1)S(1)} collective-permute-done((bf16[4,48,2,1,128]{4,2,1,0,3:T(2,128)(2,1)S(1)}, bf16[4,48,2,1,128]{4,2,1,0,3:T(2,128)(2,1)S(1)}, u32[]{:S(2)}, u32[]{:S(2)}) %collective-permute-start.30) | collective-permute-done | bytes 98336 | tf_op jit(solution)/shard_map/ppermute | solution.py:15
  249.2 1.3 collective-permute-done.31
  250.5 2.1 collective-permute-done.32
  252.7 1.4 collective-permute-start.33
  255.2 12.6 %collective-permute-done.33 = bf16[12,48,256]{2,1,0:T(8,128)(2,1)S(1)} collective-permute-done((bf16[12,48,256]{2,1,0:T(8,128)(2,1)S(1)}, bf16[12,48,256]{2,1,0:T(8,128)(2,1)S(1)}, u32[]{:S(2)}, u32[]{:S(2)}) %collective-permute-start.33) | collective-permute-done | bytes 294944 | tf_op jit(solution)/shard_map/ppermute | solution.py:11
  268.9 1.8 collective-permute-start.36
  271.1 2.7 collective-permute-done.36
  273.8 2.3 collective-permute-done.35
  277.3 1.1 pad_maximum_fusion.6
  278.4 2.1 copy.19
  (140 shorter events, 24.8 us)
Async XLA Ops:
  0.0 34.9 %copy-start.2 = (bf16[2048,512]{1,0:T(8,128)(2,1)S(1)}, bf16[2048,512]{1,0:T(8,128)(2,1)}, u32[]{:S(2)}) copy-start(bf16[2048,512]{1,0:T(8,128)(2,1)} %param.11) | copy-start | bytes 6291460
  0.0 10.9 %copy-start.6 = (bf16[2048]{0:T(1024)(128)(2,1)S(1)}, bf16[2048]{0:T(1024)(128)(2,1)}, u32[]{:S(2)}) copy-start(bf16[2048]{0:T(1024)(128)(2,1)} %param.10) | copy-start | bytes 12292
  1.2 22.1 %collective-permute-start.1 = (bf16[2048,128]{1,0:T(8,128)(2,1)S(1)}, bf16[2048,128]{1,0:T(8,128)(2,1)S(1)}, u32[]{:S(2)}, u32[]{:S(2)}) collective-permute-start(bf16[2048,128]{1,0:T(8,128)(2,1)S(1)} %constant_dynamic-slice_fusion), channel_id=1, source_target_pairs={{0,0},{1,4},{2,12},{3,8},{4,1},{5,5},{6,13},{7,9},{8,2},{9,6},{10,... | collective-permute-start | bytes 1572872 | tf_op jit(solution)/shard_map/ppermute | solution.py:95
  4.2 19.1 %collective-permute-start.2 = (bf16[1024,128]{1,0:T(8,128)(2,1)}, bf16[1024,128]{1,0:T(8,128)(2,1)}, u32[]{:S(2)}, u32[]{:S(2)}) collective-permute-start(bf16[1024,128]{1,0:T(8,128)(2,1)} %get-tuple-element.116), channel_id=1, source_target_pairs={{0,8},{4,12},{8,0},{12,4},{1,9},{5,13},{9,1},{13,5},{2,10},{6,14},... | collective-permute-start | bytes 786440 | tf_op jit(solution)/shard_map/ppermute | solution.py:15
  11.0 0.7 collective-permute-start
  23.3 21.7 %collective-permute-start.5 = (bf16[2048,128]{1,0:T(8,128)(2,1)S(1)}, bf16[2048,128]{1,0:T(8,128)(2,1)S(1)}, u32[]{:S(2)}, u32[]{:S(2)}) collective-permute-start(bf16[2048,128]{1,0:T(8,128)(2,1)S(1)} %collective-permute-done.1), channel_id=1, source_target_pairs={{0,8},{4,12},{8,0},{12,4},{1,9},{5,13},{9,1},{13,5},{2,10},{6,14},... | collective-permute-start | bytes 1572872 | tf_op jit(solution)/shard_map/ppermute | solution.py:15
  34.1 9.4 %collective-permute-start.4 = (bf16[1024,128]{1,0:T(8,128)(2,1)S(1)}, bf16[1024,128]{1,0:T(8,128)(2,1)S(1)}, u32[]{:S(2)}, u32[]{:S(2)}) collective-permute-start(bf16[1024,128]{1,0:T(8,128)(2,1)S(1)} %get-tuple-element.137), channel_id=1, source_target_pairs={{0,2},{1,6},{2,4},{3,0},{4,3},{5,7},{6,5},{7,1},{8,10},{9,14},{10,... | collective-permute-start | bytes 786440 | tf_op jit(solution)/shard_map/ppermute | solution.py:95
  34.2 9.3 %collective-permute-start.3 = (bf16[1024,128]{1,0:T(8,128)(2,1)S(1)}, bf16[1024,128]{1,0:T(8,128)(2,1)S(1)}, u32[]{:S(2)}, u32[]{:S(2)}) collective-permute-start(bf16[1024,128]{1,0:T(8,128)(2,1)S(1)} %get-tuple-element.138), channel_id=1, source_target_pairs={{0,0},{1,4},{2,6},{3,2},{4,1},{5,5},{6,7},{7,3},{8,8},{9,12},{10,1... | collective-permute-start | bytes 786440 | tf_op jit(solution)/shard_map/ppermute | solution.py:95
  45.3 7.8 %collective-permute-start.6 = (bf16[2048,256]{1,0:T(8,128)(2,1)S(1)}, bf16[2048,256]{1,0:T(8,128)(2,1)S(1)}, u32[]{:S(2)}, u32[]{:S(2)}) collective-permute-start(bf16[2048,256]{1,0:T(8,128)(2,1)S(1)} %pad_maximum_fusion), channel_id=1, source_target_pairs={{0,4},{4,0},{8,12},{12,8},{1,5},{5,1},{9,13},{13,9},{2,6},{6,2},{1... | collective-permute-start | bytes 3145736 | tf_op jit(solution)/shard_map/ppermute | solution.py:15
  47.3 5.7 %collective-permute-start.7 = (f32[1,512]{1,0:T(1,128)S(1)}, f32[1,512]{1,0:T(1,128)S(1)}, u32[]{:S(2)}, u32[]{:S(2)}) collective-permute-start(f32[1,512]{1,0:T(1,128)S(1)} %fusion.71), channel_id=1, source_target_pairs={{0,4},{4,0},{8,12},{12,8},{1,5},{5,1},{9,13},{13,9},{2,6},{6,2},{1... | collective-permute-start | bytes 6152 | tf_op jit(solution)/shard_map/ppermute | solution.py:15
  60.5 14.3 %collective-permute-start.11 = (bf16[1024,256]{1,0:T(8,128)(2,1)S(1)}, bf16[1024,256]{1,0:T(8,128)(2,1)S(1)}, u32[]{:S(2)}, u32[]{:S(2)}) collective-permute-start(bf16[1024,256]{1,0:T(8,128)(2,1)S(1)} %pad_maximum_fusion.7), channel_id=1, source_target_pairs={{0,8},{4,12},{8,0},{12,4},{1,9},{5,13},{9,1},{13,5},{2,10},{6,14},... | collective-permute-start | bytes 1572872 | tf_op jit(solution)/shard_map/ppermute | solution.py:15
  74.9 10.6 %slice-start.5 = ((s8[7864320]{0:T(1024)(128)(4,1)}), s8[4194304]{0:T(1024)(128)(4,1)S(1)}, s32[]{:S(2)}) async-start(s8[7864320]{0:T(1024)(128)(4,1)} %bitcast.104), calls=%async_computation.5 | async-start | bytes 8388608
  75.0 10.5 %collective-permute-start.12 = (bf16[2048,256]{1,0:T(8,128)(2,1)S(1)}, bf16[2048,256]{1,0:T(8,128)(2,1)S(1)}, u32[]{:S(2)}, u32[]{:S(2)}) collective-permute-start(bf16[2048,256]{1,0:T(8,128)(2,1)S(1)} %pad_maximum_fusion.1), channel_id=1, source_target_pairs={{0,4},{4,0},{8,12},{12,8},{1,5},{5,1},{9,13},{13,9},{2,6},{6,2},{1... | collective-permute-start | bytes 3145736 | tf_op jit(solution)/shard_map/ppermute | solution.py:15
  75.0 4.6 %collective-permute-start.13 = (f32[1,512]{1,0:T(1,128)S(1)}, f32[1,512]{1,0:T(1,128)S(1)}, u32[]{:S(2)}, u32[]{:S(2)}) collective-permute-start(f32[1,512]{1,0:T(1,128)S(1)} %add.191), channel_id=1, source_target_pairs={{0,8},{4,12},{8,0},{12,4},{1,9},{5,13},{9,1},{13,5},{2,10},{6,14},... | collective-permute-start | bytes 6152 | tf_op jit(solution)/shard_map/ppermute | solution.py:15
  76.1 34.4 %collective-permute-start.8 = (bf16[1920,128]{0,1:T(8,128)(2,1)S(1)}, bf16[1920,128]{0,1:T(8,128)(2,1)S(1)}, u32[]{:S(2)}, u32[]{:S(2)}) collective-permute-start(bf16[1920,128]{0,1:T(8,128)(2,1)S(1)} %get-tuple-element.71), channel_id=1, source_target_pairs={{0,2},{1,3},{2,0},{3,1},{4,6},{5,7},{6,4},{7,5},{8,10},{9,11},{10,... | collective-permute-start | bytes 1474568 | tf_op jit(solution)/shard_map/ppermute | solution.py:15
  76.8 33.7 %collective-permute-start.9 = (bf16[1920,128]{0,1:T(8,128)(2,1)S(1)}, bf16[1920,128]{0,1:T(8,128)(2,1)S(1)}, u32[]{:S(2)}, u32[]{:S(2)}) collective-permute-start(bf16[1920,128]{0,1:T(8,128)(2,1)S(1)} %slice.157), channel_id=1, source_target_pairs={{0,3},{1,2},{2,1},{3,0},{4,7},{5,6},{6,5},{7,4},{8,11},{9,10},{10,... | collective-permute-start | bytes 1474568 | tf_op jit(solution)/shard_map/ppermute | solution.py:15
  77.9 34.0 %collective-permute-start.10 = (bf16[1920,128]{0,1:T(8,128)(2,1)S(1)}, bf16[1920,128]{0,1:T(8,128)(2,1)S(1)}, u32[]{:S(2)}, u32[]{:S(2)}) collective-permute-start(bf16[1920,128]{0,1:T(8,128)(2,1)S(1)} %get-tuple-element.73), channel_id=1, source_target_pairs={{0,1},{1,0},{2,3},{3,2},{4,5},{5,4},{6,7},{7,6},{8,9},{9,8},{10,11... | collective-permute-start | bytes 1474568 | tf_op jit(solution)/shard_map/ppermute | solution.py:15
  79.6 5.9 %slice-start.6 = ((s8[7864320]{0:T(1024)(128)(4,1)}), s8[3670016]{0:T(1024)(128)(4,1)S(1)}, s32[]{:S(2)}) async-start(s8[7864320]{0:T(1024)(128)(4,1)} %bitcast.104), calls=%async_computation.6 | async-start | bytes 7340032
  89.5 22.3 %slice-start.1 = ((f32[1920,256]{0,1:T(8,128)}), f32[1920,128]{0,1:T(8,128)S(1)}, s32[]{:S(2)}) async-start(f32[1920,256]{0,1:T(8,128)} %copy-done.1), calls=%async_computation.1 | async-start | bytes 1966080 | tf_op jit(solution)/shard_map/slice | solution.py:118
  112.3 12.2 %collective-permute-start.15 = (bf16[1920,128]{0,1:T(8,128)(2,1)S(1)}, bf16[1920,128]{0,1:T(8,128)(2,1)S(1)}, u32[]{:S(2)}, u32[]{:S(2)}) collective-permute-start(bf16[1920,128]{0,1:T(8,128)(2,1)S(1)} %add_convert_fusion.1), channel_id=1, source_target_pairs={{0,16},{16,0},{1,17},{17,1},{2,18},{18,2},{3,19},{19,3},{4,20},{20... | collective-permute-start | bytes 1474568 | tf_op jit(solution)/shard_map/ppermute | solution.py:15
  113.9 11.8 %collective-permute-start.14 = (bf16[1920,128]{0,1:T(8,128)(2,1)S(1)}, bf16[1920,128]{0,1:T(8,128)(2,1)S(1)}, u32[]{:S(2)}, u32[]{:S(2)}) collective-permute-start(bf16[1920,128]{0,1:T(8,128)(2,1)S(1)} %add_convert_fusion.1), channel_id=1, source_target_pairs={{0,8},{4,12},{8,0},{12,4},{1,9},{5,13},{9,1},{13,5},{2,10},{6,14},... | collective-permute-start | bytes 1474568 | tf_op jit(solution)/shard_map/ppermute | solution.py:15
  125.9 14.0 %copy-start.3 = (s32[4,4]{1,0:T(4,128)S(1)}, s32[4,4]{1,0:T(4,128)}, u32[]{:S(2)}) copy-start(s32[4,4]{1,0:T(4,128)} %param.13) | copy-start | bytes 196
  125.9 14.1 %copy-start.5 = (s32[4]{0:T(128)S(1)}, s32[4]{0:T(128)}, u32[]{:S(2)}) copy-start(s32[4]{0:T(128)} %param.15) | copy-start | bytes 52
  125.9 13.7 %collective-permute-start.16 = (bf16[1920,256]{0,1:T(8,128)(2,1)S(1)}, bf16[1920,256]{0,1:T(8,128)(2,1)S(1)}, u32[]{:S(2)}, u32[]{:S(2)}) collective-permute-start(bf16[1920,256]{0,1:T(8,128)(2,1)S(1)} %pad_maximum_fusion.2), channel_id=1, source_target_pairs={{0,4},{4,0},{8,12},{12,8},{1,5},{5,1},{9,13},{13,9},{2,6},{6,2},{1... | collective-permute-start | bytes 2949128 | tf_op jit(solution)/shard_map/ppermute | solution.py:15
  126.0 13.6 %collective-permute-start.17 = (bf16[1920,128]{0,1:T(8,128)(2,1)S(1)}, bf16[1920,128]{0,1:T(8,128)(2,1)S(1)}, u32[]{:S(2)}, u32[]{:S(2)}) collective-permute-start(bf16[1920,128]{0,1:T(8,128)(2,1)S(1)} %collective-permute-done.15), channel_id=1, source_target_pairs={{0,8},{4,12},{8,0},{12,4},{1,9},{5,13},{9,1},{13,5},{2,10},{6,14},... | collective-permute-start | bytes 1474568 | tf_op jit(solution)/shard_map/ppermute | solution.py:15
  139.7 21.5 %slice-start.2 = ((s8[8847360]{0:T(1024)(128)(4,1)}), s8[458752]{0:T(1024)(128)(4,1)S(1)}, s32[]{:S(2)}) async-start(s8[8847360]{0:T(1024)(128)(4,1)} %bitcast.84), calls=%async_computation.2 | async-start | bytes 917504
  139.8 18.7 %collective-permute-start.18 = (bf16[1920,256]{0,1:T(8,128)(2,1)S(1)}, bf16[1920,256]{0,1:T(8,128)(2,1)}, u32[]{:S(2)}, u32[]{:S(2)}) collective-permute-start(bf16[1920,256]{0,1:T(8,128)(2,1)S(1)} %pad_maximum_fusion.3), channel_id=1, source_target_pairs={{0,4},{4,0},{8,12},{12,8},{1,5},{5,1},{9,13},{13,9},{2,6},{6,2},{1... | collective-permute-start | bytes 2949128 | tf_op jit(solution)/shard_map/ppermute | solution.py:15
  140.0 45.4 %collective-permute-start.19 = (bf16[1920,128]{0,1:T(8,128)(2,1)}, bf16[1920,128]{0,1:T(8,128)(2,1)S(1)}, u32[]{:S(2)}, u32[]{:S(2)}) collective-permute-start(bf16[1920,128]{0,1:T(8,128)(2,1)} %get-tuple-element.86), channel_id=1, source_target_pairs={{0,2},{1,3},{2,0},{3,1},{4,6},{5,7},{6,4},{7,5},{8,10},{9,11},{10,... | collective-permute-start | bytes 1474568 | tf_op jit(solution)/shard_map/ppermute | solution.py:15
  152.0 33.4 %collective-permute-start.20 = (bf16[1920,128]{0,1:T(8,128)(2,1)}, bf16[1920,128]{0,1:T(8,128)(2,1)S(1)}, u32[]{:S(2)}, u32[]{:S(2)}) collective-permute-start(bf16[1920,128]{0,1:T(8,128)(2,1)} %slice.156), channel_id=1, source_target_pairs={{0,3},{1,2},{2,1},{3,0},{4,7},{5,6},{6,5},{7,4},{8,11},{9,10},{10,... | collective-permute-start | bytes 1474568 | tf_op jit(solution)/shard_map/ppermute | solution.py:15
  153.2 33.2 %collective-permute-start.21 = (bf16[1920,128]{0,1:T(8,128)(2,1)}, bf16[1920,128]{0,1:T(8,128)(2,1)S(1)}, u32[]{:S(2)}, u32[]{:S(2)}) collective-permute-start(bf16[1920,128]{0,1:T(8,128)(2,1)} %get-tuple-element.88), channel_id=1, source_target_pairs={{0,1},{1,0},{2,3},{3,2},{4,5},{5,4},{6,7},{7,6},{8,9},{9,8},{10,11... | collective-permute-start | bytes 1474568 | tf_op jit(solution)/shard_map/ppermute | solution.py:15
  153.2 7.9 %slice-start.3 = ((s8[8847360]{0:T(1024)(128)(4,1)}), s8[4194304]{0:T(1024)(128)(4,1)S(1)}, s32[]{:S(2)}) async-start(s8[8847360]{0:T(1024)(128)(4,1)} %bitcast.84), calls=%async_computation.3 | async-start | bytes 8388608
  162.1 24.4 %slice-start = ((f32[1920,256]{0,1:T(8,128)}), f32[1920,128]{0,1:T(8,128)S(1)}, s32[]{:S(2)}) async-start(f32[1920,256]{0,1:T(8,128)} %copy-done), calls=%async_computation | async-start | bytes 1966080 | tf_op jit(solution)/shard_map/slice | solution.py:118
  162.3 26.7 %copy-start.7 = (s32[4]{0:T(128)S(1)}, s32[4]{0:T(128)}, u32[]{:S(2)}) copy-start(s32[4]{0:T(128)} %param.14) | copy-start | bytes 52
  186.7 24.2 %collective-permute-start.23 = (bf16[1920,128]{0,1:T(8,128)(2,1)S(1)}, bf16[1920,128]{0,1:T(8,128)(2,1)S(1)}, u32[]{:S(2)}, u32[]{:S(2)}) collective-permute-start(bf16[1920,128]{0,1:T(8,128)(2,1)S(1)} %add_convert_fusion), channel_id=1, source_target_pairs={{0,16},{16,0},{1,17},{17,1},{2,18},{18,2},{3,19},{19,3},{4,20},{20... | collective-permute-start | bytes 1474568 | tf_op jit(solution)/shard_map/ppermute | solution.py:15
  187.3 23.7 %collective-permute-start.22 = (bf16[1920,128]{0,1:T(8,128)(2,1)S(1)}, bf16[1920,128]{0,1:T(8,128)(2,1)S(1)}, u32[]{:S(2)}, u32[]{:S(2)}) collective-permute-start(bf16[1920,128]{0,1:T(8,128)(2,1)S(1)} %add_convert_fusion), channel_id=1, source_target_pairs={{0,8},{4,12},{8,0},{12,4},{1,9},{5,13},{9,1},{13,5},{2,10},{6,14},... | collective-permute-start | bytes 1474568 | tf_op jit(solution)/shard_map/ppermute | solution.py:15
  189.0 21.9 %collective-permute-start.24 = (bf16[12,48,256]{2,1,0:T(8,128)(2,1)S(1)}, bf16[12,48,256]{2,1,0:T(8,128)(2,1)S(1)}, u32[]{:S(2)}, u32[]{:S(2)}) collective-permute-start(bf16[12,48,256]{2,1,0:T(8,128)(2,1)S(1)} %pad_maximum_fusion.9), channel_id=1, source_target_pairs={{0,1},{1,2},{2,3},{3,0},{4,5},{5,6},{6,7},{7,4},{8,9},{9,10},{10,1... | collective-permute-start | bytes 884744 | tf_op jit(solution)/shard_map/ppermute | solution.py:11
  211.0 11.5 %collective-permute-start.27 = (bf16[1920,128]{0,1:T(8,128)(2,1)S(1)}, bf16[1920,128]{0,1:T(8,128)(2,1)S(1)}, u32[]{:S(2)}, u32[]{:S(2)}) collective-permute-start(bf16[1920,128]{0,1:T(8,128)(2,1)S(1)} %collective-permute-done.22), channel_id=1, source_target_pairs={{0,16},{16,0},{1,17},{17,1},{2,18},{18,2},{3,19},{19,3},{4,20},{20... | collective-permute-start | bytes 1474568 | tf_op jit(solution)/shard_map/ppermute | solution.py:15
  222.7 7.3 %collective-permute-start.28 = (bf16[1920,256]{0,1:T(8,128)(2,1)S(1)}, bf16[1920,256]{0,1:T(8,128)(2,1)S(1)}, u32[]{:S(2)}, u32[]{:S(2)}) collective-permute-start(bf16[1920,256]{0,1:T(8,128)(2,1)S(1)} %pad_maximum_fusion.5), channel_id=1, source_target_pairs={{0,4},{4,0},{8,12},{12,8},{1,5},{5,1},{9,13},{13,9},{2,6},{6,2},{1... | collective-permute-start | bytes 2949128 | tf_op jit(solution)/shard_map/ppermute | solution.py:15
  222.9 7.9 %collective-permute-start.26 = (bf16[1920,256]{0,1:T(8,128)(2,1)S(1)}, bf16[1920,256]{0,1:T(8,128)(2,1)S(1)}, u32[]{:S(2)}, u32[]{:S(2)}) collective-permute-start(bf16[1920,256]{0,1:T(8,128)(2,1)S(1)} %pad_maximum_fusion.4), channel_id=1, source_target_pairs={{0,4},{4,0},{8,12},{12,8},{1,5},{5,1},{9,13},{13,9},{2,6},{6,2},{1... | collective-permute-start | bytes 2949128 | tf_op jit(solution)/shard_map/ppermute | solution.py:15
  223.6 18.2 %collective-permute-start.25 = (bf16[12,48,256]{2,1,0:T(8,128)(2,1)S(1)}, bf16[12,48,256]{2,1,0:T(8,128)(2,1)S(1)}, u32[]{:S(2)}, u32[]{:S(2)}) collective-permute-start(bf16[12,48,256]{2,1,0:T(8,128)(2,1)S(1)} %broadcast_select_fusion.13), channel_id=1, source_target_pairs={{0,2},{1,3},{2,0},{3,1},{4,6},{5,7},{6,4},{7,5},{8,10},{9,11},{10,... | collective-permute-start | bytes 884744 | tf_op jit(solution)/shard_map/ppermute | solution.py:11
  242.1 10.5 %collective-permute-start.32 = (bf16[12,48,256]{2,1,0:T(8,128)(2,1)S(1)}, bf16[12,48,256]{2,1,0:T(8,128)(2,1)S(1)}, u32[]{:S(2)}, u32[]{:S(2)}) collective-permute-start(bf16[12,48,256]{2,1,0:T(8,128)(2,1)S(1)} %pad_maximum_fusion.10), channel_id=1, source_target_pairs={{0,1},{1,2},{2,3},{3,0},{4,5},{5,6},{6,7},{7,4},{8,9},{9,10},{10,1... | collective-permute-start | bytes 884744 | tf_op jit(solution)/shard_map/ppermute | solution.py:11
  243.5 2.1 collective-permute-start.29
  243.6 5.6 %collective-permute-start.30 = (bf16[4,48,2,1,128]{4,2,1,0,3:T(2,128)(2,1)S(1)}, bf16[4,48,2,1,128]{4,2,1,0,3:T(2,128)(2,1)S(1)}, u32[]{:S(2)}, u32[]{:S(2)}) collective-permute-start(bf16[4,48,2,1,128]{4,2,1,0,3:T(2,128)(2,1)S(1)} %squeeze.26), channel_id=1, source_target_pairs={{0,8},{4,12},{8,0},{12,4},{1,9},{5,13},{9,1},{13,5},{2,10},{6,14},... | collective-permute-start | bytes 294920 | tf_op jit(solution)/shard_map/ppermute | solution.py:15
  245.4 5.1 %collective-permute-start.31 = (bf16[4,48,2,1,128]{4,2,1,0,3:T(2,128)(2,1)S(1)}, bf16[4,48,2,1,128]{4,2,1,0,3:T(2,128)(2,1)S(1)}, u32[]{:S(2)}, u32[]{:S(2)}) collective-permute-start(bf16[4,48,2,1,128]{4,2,1,0,3:T(2,128)(2,1)S(1)} %squeeze.27), channel_id=1, source_target_pairs={{0,12},{4,8},{8,4},{12,0},{1,13},{5,9},{9,5},{13,1},{2,14},{6,10},... | collective-permute-start | bytes 294920 | tf_op jit(solution)/shard_map/ppermute | solution.py:15
  252.7 15.1 %collective-permute-start.33 = (bf16[12,48,256]{2,1,0:T(8,128)(2,1)S(1)}, bf16[12,48,256]{2,1,0:T(8,128)(2,1)S(1)}, u32[]{:S(2)}, u32[]{:S(2)}) collective-permute-start(bf16[12,48,256]{2,1,0:T(8,128)(2,1)S(1)} %broadcast_select_fusion.12), channel_id=1, source_target_pairs={{0,2},{1,3},{2,0},{3,1},{4,6},{5,7},{6,4},{7,5},{8,10},{9,11},{10,... | collective-permute-start | bytes 884744 | tf_op jit(solution)/shard_map/ppermute | solution.py:11
  268.8 2.3 collective-permute-start.34
  268.9 5.0 %collective-permute-start.36 = (bf16[4,48,2,1,128]{4,2,1,0,3:T(2,128)(2,1)S(1)}, bf16[4,48,2,1,128]{4,2,1,0,3:T(2,128)(2,1)S(1)}, u32[]{:S(2)}, u32[]{:S(2)}) collective-permute-start(bf16[4,48,2,1,128]{4,2,1,0,3:T(2,128)(2,1)S(1)} %squeeze.31), channel_id=1, source_target_pairs={{0,12},{4,8},{8,4},{12,0},{1,13},{5,9},{9,5},{13,1},{2,14},{6,10},... | collective-permute-start | bytes 294920 | tf_op jit(solution)/shard_map/ppermute | solution.py:15
  270.7 5.4 %collective-permute-start.35 = (bf16[4,48,2,1,128]{4,2,1,0,3:T(2,128)(2,1)S(1)}, bf16[4,48,2,1,128]{4,2,1,0,3:T(2,128)(2,1)S(1)}, u32[]{:S(2)}, u32[]{:S(2)}) collective-permute-start(bf16[4,48,2,1,128]{4,2,1,0,3:T(2,128)(2,1)S(1)} %squeeze.30), channel_id=1, source_target_pairs={{0,8},{4,12},{8,0},{12,4},{1,9},{5,13},{9,1},{13,5},{2,10},{6,14},... | collective-permute-start | bytes 294920 | tf_op jit(solution)/shard_map/ppermute | solution.py:15
  (4 other events, 9.2 us)

commit v7 on v6

--- a/solution.py
+++ b/solution.py
@@ -110,21 +110,24 @@
         return put_first(group == 0, ours, theirs, 1)
 
     def products(near, far):
-        near_product, far_product = add_columns(proj_weight, near), add_columns(proj_weight, far)
+        both = add_columns(proj_weight, jnp.concatenate([near, far], axis=1))
+        near_0, near_1, far_0, far_1 = (both[:, k * width : (k + 1) * width] for k in range(4))
         near_kept = at_end == first_core
-        kept = jnp.where(near_kept, near_product, far_product)
-        sent = jnp.where(near_kept, far_product, near_product)
-        parts = [sent[:, width:], kept[:, width:], sent[:, :width]]
-        return kept[:, :width], [part.astype(jnp.bfloat16) for part in parts]
-
-    def exchange(parts):
-        return [swapped(part, "head", bit) for part, bit in zip(parts, (2, 3, 1))]
-
-    def summed(kept, arrived):
-        total = kept
-        for block in arrived:
-            total = total + block.astype(jnp.float32)
-        return total.astype(jnp.bfloat16)
+        return (
+            jnp.where(first_core, near_1, far_1).astype(jnp.bfloat16),
+            jnp.where(first_core, far_1, near_1),
+            jnp.where(near_kept, far_0, near_0),
+            jnp.where(near_kept, near_0, far_0),
+        )
+
+    def neighbours(block):
+        return swapped(block.astype(jnp.bfloat16), "head", 1)
+
+    def middle(block):
+        return moved(block.astype(jnp.bfloat16), lambda t, h: (t, (0, 2, 1, 3)[h]))
+
+    def plus(block, arrived):
+        return block.astype(jnp.float32) + arrived.astype(jnp.float32)
 
     def finish(total, part):
         finished = []
@@ -185,56 +188,77 @@
     key_near = put_first(tile // 2 == head // 2, key_block, key_other, 1)
     value_half = jnp.concatenate(value_pieces, axis=1)
     key_near, value_half = step((key_near, value_half))
-    key_kept, key_parts = products(key_near, swapped(key_near, "tile", 1))
+    first, second, third, own = products(key_near, swapped(key_near, "tile", 1))
     bias_part = bias_part + swapped(bias_part, "tile", 1)
-    key_kept, key_parts, value_half, bias_part = step((key_kept, key_parts, value_half, bias_part))
-
-    key_arrived = exchange(key_parts)
-    value_other = swapped(value_half, "tile", 2)
-    bias_part = bias_part + swapped(bias_part, "tile", 2)
+    first, second, third, own, value_half, bias_part = step(
+        (first, second, third, own, value_half, bias_part)
+    )
+
+    in_1, value_other, bias_other = step(
+        (neighbours(first), swapped(value_half, "tile", 2), swapped(bias_part, "tile", 2))
+    )
+    bias_part = (bias_part + bias_other).reshape(2, layers, 2, head_dim)
+
     value_near = put_first(first_chip, value_half, value_other, 0)
-    value_kept, value_parts = products(value_near, swapped(value_near, "tile", 1))
-    key_kept, key_arrived, value_kept, value_parts, bias_part = step(
-        (key_kept, key_arrived, value_kept, value_parts, bias_part)
-    )
-    bias_part = bias_part.reshape(2, layers, 2, head_dim)
-
-    value_arrived = exchange(value_parts)
-    own = summed(key_kept, key_arrived)
-    across_x, across_y = step((swapped(own, "tile", 2), swapped(own, "groups", 1)))
-    rows_0 = step(both_heads(own, across_y))
-    rows_1, diagonal = step((swapped(rows_0, "tile", 1), swapped(across_y, "tile", 2)))
-    rows_2 = step(both_heads(across_x, diagonal))
+    relayed = plus(first, in_1).astype(jnp.bfloat16)
+    value_near, relayed = step((value_near, relayed))
+    in_2, across_2 = neighbours(second), middle(relayed)
+    value_products = products(value_near, swapped(value_near, "tile", 1))
+    in_2, across_2, value_products = step((in_2, across_2, value_products))
+
+    relayed = jnp.where(at_end, third, plus(third, across_2)).astype(jnp.bfloat16)
+    in_3, across_3 = step((neighbours(relayed), middle(plus(second, in_2))))
+    own = plus(own, in_3) + jnp.where(at_end, 0.0, across_3.astype(jnp.float32))
+    own = own.astype(jnp.bfloat16)
+
+    first, second, third, value_own = value_products
+    in_1, across_x, across_y = step(
+        (neighbours(first), swapped(own, "tile", 2), swapped(own, "groups", 1))
+    )
+
+    rows_0, relayed = step((both_heads(own, across_y), plus(first, in_1).astype(jnp.bfloat16)))
+    in_2, across_2, diagonal, rows_1 = step(
+        (
+            neighbours(second),
+            middle(relayed),
+            swapped(across_y, "tile", 2),
+            swapped(rows_0, "tile", 1),
+        )
+    )
+
+    relayed = jnp.where(at_end, third, plus(third, across_2)).astype(jnp.bfloat16)
+    rows_2, relayed = step((both_heads(across_x, diagonal), relayed))
+    in_3, across_3 = neighbours(relayed), middle(plus(second, in_2))
     total = times_features(rows_0, 0) + times_features(rows_1, 1)
     total = total + times_features(rows_2, 2) + times_features(swapped(rows_2, "tile", 1), 3)
     keys = finish(total, 0)
-    keys, value_kept, value_arrived = step((keys, value_kept, value_arrived))
-
-    own = summed(value_kept, value_arrived)
-    own, across_x, across_y, shifted, keys = step(
+    in_3, across_3, keys = step((in_3, across_3, keys))
+    own = plus(value_own, in_3) + jnp.where(at_end, 0.0, across_3.astype(jnp.float32))
+    own = own.astype(jnp.bfloat16)
+
+    shifted, across_x, across_y = step(
+        (shifted_2(keys, "head", 1), swapped(own, "tile", 2), swapped(own, "groups", 1))
+    )
+
+    rows_0, keys = step((both_heads(own, across_y), rolled(keys, shifted, 1)))
+    shifted, diagonal, rows_1 = step(
         (
-            own,
-            swapped(own, "tile", 2),
-            swapped(own, "groups", 1),
-            shifted_2(keys, "head", 1),
-            keys,
-        )
-    )
-
-    keys = rolled(keys, shifted, 1)
-    rows_0, keys = step((both_heads(own, across_y), keys))
-    shifted, diagonal = shifted_2(keys, "head", 2), swapped(across_x, "groups", 1)
-    total = times_features(rows_0, 0) + times_features(swapped(rows_0, "tile", 1), 1)
-    rows_2 = step(both_heads(across_x, diagonal))
+            shifted_2(keys, "head", 2),
+            swapped(across_x, "groups", 1),
+            swapped(rows_0, "tile", 1),
+        )
+    )
+
+    rows_2, keys = step((both_heads(across_x, diagonal), rolled(keys, shifted, 2)))
+    total = times_features(rows_0, 0) + times_features(rows_1, 1)
     total = total + times_features(rows_2, 2) + times_features(swapped(rows_2, "tile", 1), 3)
     values = finish(total, 1)
-    shifted, values, keys = step((shifted, values, keys))
-
-    picked = outgoing(rolled(keys, shifted, 2))
-    arrived, shifted, values = step((to_owners(picked), shifted_2(values, "head", 1), values))
-
-    values = rolled(values, shifted, 1)
-    key_cache, shifted, values = step((in_order(arrived), shifted_2(values, "head", 2), values))
+    picked, values = step((outgoing(keys), values))
+
+    arrived, shifted = step((to_owners(picked), shifted_2(values, "head", 1)))
+
+    values = step(rolled(values, shifted, 1))
+    key_cache, shifted = step((in_order(arrived), shifted_2(values, "head", 2)))
 
     value_cache = in_order(to_owners(outgoing(rolled(values, shifted, 2))))
     cache = jnp.stack([key_cache, value_cache], axis=-2)

time: 281 us -> 247 us (0.88)
  waiting for transfers between devices: 152 us -> 131 us
  starting transfers between devices: 76.4 us -> 56.5 us
  other arithmetic: 7.95 us -> 18.6 us
  local copies, waits for them, and re-layouts: 10.8 us -> 7.24 us
    ppermute x29, waiting for transfers between devices: 113 us -> 80.9 us  [swapped(): lax.ppermute(shard, axis, [(i, i ^ bit) for i in range(lax.axis_size(axis...]
    ppermute x4, starting transfers between devices: 22.9 us -> 1.73 us  [shifted_2(): lax.ppermute(shard, axis, [(i, (i + by) % count) for i in range(count)])]
    ppermute x4, waiting for transfers between devices: 30.4 us -> 40.8 us  [shifted_2(): lax.ppermute(shard, axis, [(i, (i + by) % count) for i in range(count)])]
    ppermute x4 -> x8, starting transfers between devices: 2.08 us -> 11.6 us  [moved(): return lax.ppermute(shard, ('tile', 'head'), pairs)]
    ppermute x29, starting transfers between devices: 51.4 us -> 43.1 us  [swapped(): lax.ppermute(shard, axis, [(i, i ^ bit) for i in range(lax.axis_size(axis...]
    convert_element_type x2 -> x12, other arithmetic: 0.67 us -> 6.25 us  [the longest x1 1.96 us: product_plan(): plus(first, in_1).astype(jnp.bfloat16)]
    ppermute x4 -> x8, waiting for transfers between devices: 8.25 us -> 9.03 us  [moved(): return lax.ppermute(shard, ('tile', 'head'), pairs)]
    dot_general x15 -> x13, matrix products: 32.3 us -> 31.8 us  [add_columns(): return jnp.dot(operand, portion, preferred_element_type=jnp.float32)]
  transfers between devices with their start and end apart: 37 -> 41, of which waited for: 20 -> 25; matrix products, arithmetic and copies ran while one was open for 13% -> 12% of each run, Pallas kernels for 0% -> 0%
where the time goes in v7:
time: 247 us; the launch traced here: 246 us
  waiting for transfers between devices  131 us (53%)
  starting transfers between devices  56.5 us (23%)
  matrix products  32 us (13%)
  other arithmetic  18.6 us (8%)
  local copies, waits for them, and re-layouts  7.24 us (3%)
    ppermute x29, waiting for transfers between devices, swapped(): lax.ppermute(shard, axis, [(i, i ^ bit) for i in range(lax.axis_size(axis...  80.9 us
    ppermute x29, starting transfers between devices, swapped(): lax.ppermute(shard, axis, [(i, i ^ bit) for i in range(lax.axis_size(axis...  43.1 us
    ppermute x4, waiting for transfers between devices, shifted_2(): lax.ppermute(shard, axis, [(i, (i + by) % count) for i in range(count)])  40.8 us
    dot_general x13, matrix products, add_columns(): return jnp.dot(operand, portion, preferred_element_type=jnp.float32)  31.8 us
    ppermute x8, starting transfers between devices, moved(): return lax.ppermute(shard, ('tile', 'head'), pairs)  11.6 us
    ppermute x8, waiting for transfers between devices, moved(): return lax.ppermute(shard, ('tile', 'head'), pairs)  9.03 us
  transfers between devices with their start and end apart: 41, of which 25 were waited for; matrix products, arithmetic and copies ran while one was open for 12% of the time, Pallas kernels for 0%

profile of v7, /device:TPU:0, one launch (start us, length us, event | category | flops | bytes accessed | tf_op | source)
XLA Modules:
  0.0 245.8 jit_solution(2634712356482974122)
XLA Ops:
  0.0 1.2 constant_dynamic-slice_fusion
  2.0 2.3 fusion.73
  4.2 6.7 %collective-permute-start.2 = (bf16[1024,128]{1,0:T(8,128)(2,1)}, bf16[1024,128]{1,0:T(8,128)(2,1)}, u32[]{:S(2)}, u32[]{:S(2)}) collective-permute-start(bf16[1024,128]{1,0:T(8,128)(2,1)} %get-tuple-element.146), channel_id=1, source_target_pairs={{0,8},{4,12},{8,0},{12,4},{1,9},{5,13},{9,1},{13,5},{2,10},{6,14},... | collective-permute-start | bytes 786440 | tf_op jit(solution)/shard_map/ppermute | solution.py:15
  10.9 1.3 collective-permute-start
  12.3 11.0 %collective-permute-done.2 = bf16[1024,128]{1,0:T(8,128)(2,1)} collective-permute-done((bf16[1024,128]{1,0:T(8,128)(2,1)}, bf16[1024,128]{1,0:T(8,128)(2,1)}, u32[]{:S(2)}, u32[]{:S(2)}) %collective-permute-start.2) | collective-permute-done | bytes 262176 | tf_op jit(solution)/shard_map/ppermute | solution.py:15
  23.3 9.8 %collective-permute-start.5 = (bf16[2048,128]{1,0:T(8,128)(2,1)S(1)}, bf16[2048,128]{1,0:T(8,128)(2,1)S(1)}, u32[]{:S(2)}, u32[]{:S(2)}) collective-permute-start(bf16[2048,128]{1,0:T(8,128)(2,1)S(1)} %collective-permute-done.1), channel_id=1, source_target_pairs={{0,8},{4,12},{8,0},{12,4},{1,9},{5,13},{9,1},{13,5},{2,10},{6,14},... | collective-permute-start | bytes 1572872 | tf_op jit(solution)/shard_map/ppermute | solution.py:15
  34.7 1.4 collective-permute-start.4
  36.5 9.0 %collective-permute-done.4 = bf16[1024,128]{1,0:T(8,128)(2,1)S(1)} collective-permute-done((bf16[1024,128]{1,0:T(8,128)(2,1)S(1)}, bf16[1024,128]{1,0:T(8,128)(2,1)S(1)}, u32[]{:S(2)}, u32[]{:S(2)}) %collective-permute-start.4) | collective-permute-done | bytes 262176 | tf_op jit(solution)/shard_map/ppermute | solution.py:95
  45.8 4.2 %collective-permute-start.6 = (bf16[2048,256]{1,0:T(8,128)(2,1)S(1)}, bf16[2048,256]{1,0:T(8,128)(2,1)}, u32[]{:S(2)}, u32[]{:S(2)}) collective-permute-start(bf16[2048,256]{1,0:T(8,128)(2,1)S(1)} %pad_maximum_fusion), channel_id=1, source_target_pairs={{0,4},{4,0},{8,12},{12,8},{1,5},{5,1},{9,13},{13,9},{2,6},{6,2},{1... | collective-permute-start | bytes 3145736 | tf_op jit(solution)/shard_map/ppermute | solution.py:15
  50.1 2.1 collective-permute-done.7
  52.4 7.4 %convolution_bitcast_fusion.1 = f32[1920,512]{0,1:T(8,128)S(1)} fusion(bf16[1920,2048]{1,0:T(8,128)(2,1)} %param.9, bf16[2048,256]{1,0:T(8,128)(2,1)} %collective-permute-done.6, bf16[2048,256]{1,0:T(8,128)(2,1)S(1)} %pad_maximum_fusion), kind=kOutput, calls=%fused_computation.3 | convolution fusion | flops 4030726144 | bytes 13893632 | tf_op jit(solution)/shard_map/dot_general | solution.py:19
  59.9 1.5 slice_select_fusion.3
  61.4 1.8 collective-permute-start.10
  63.7 12.0 %collective-permute-done.11 = f32[1,512]{1,0:T(1,128)S(1)} collective-permute-done((f32[1,512]{1,0:T(1,128)S(1)}, f32[1,512]{1,0:T(1,128)S(1)}, u32[]{:S(2)}, u32[]{:S(2)}) %collective-permute-start.11) | collective-permute-done | bytes 2080 | tf_op jit(solution)/shard_map/ppermute | solution.py:15
  78.0 1.3 collective-permute-done.13
  79.4 7.1 %convolution_bitcast_fusion = f32[1920,512]{0,1:T(8,128)S(1)} fusion(bf16[1920,2048]{1,0:T(8,128)(2,1)} %param.9, bf16[2048,256]{1,0:T(8,128)(2,1)S(1)} %collective-permute-done.13, bf16[2048,256]{1,0:T(8,128)(2,1)S(1)} %pad_maximum_fusion.1), kind=kOutput, calls=%fused_computation.2 | convolution fusion | flops 4030726144 | bytes 13893632 | tf_op jit(solution)/shard_map/dot_general | solution.py:19
  86.5 1.2 slice_select_fusion
  87.8 2.7 %collective-permute-done.8 = bf16[1920,128]{0,1:T(8,128)(2,1)S(1)} collective-permute-done((bf16[1920,128]{0,1:T(8,128)(2,1)S(1)}, bf16[1920,128]{0,1:T(8,128)(2,1)S(1)}, u32[]{:S(2)}, u32[]{:S(2)}) %collective-permute-start.8) | collective-permute-done | bytes 491552 | tf_op jit(solution)/shard_map/ppermute | solution.py:15
  91.4 5.7 %collective-permute-start.15 = (bf16[1920,128]{0,1:T(8,128)(2,1)S(1)}, bf16[1920,128]{0,1:T(8,128)(2,1)S(1)}, u32[]{:S(2)}, u32[]{:S(2)}) collective-permute-start(bf16[1920,128]{0,1:T(8,128)(2,1)S(1)} %fusion.40), channel_id=1, source_target_pairs={{0,1},{1,0},{2,3},{3,2},{4,5},{5,4},{6,7},{7,6},{8,9},{9,8},{10,11... | collective-permute-start | bytes 1474568 | tf_op jit(solution)/shard_map/ppermute | solution.py:15
  97.2 12.1 %collective-permute-done.15 = bf16[1920,128]{0,1:T(8,128)(2,1)S(1)} collective-permute-done((bf16[1920,128]{0,1:T(8,128)(2,1)S(1)}, bf16[1920,128]{0,1:T(8,128)(2,1)S(1)}, u32[]{:S(2)}, u32[]{:S(2)}) %collective-permute-start.15) | collective-permute-done | bytes 491552 | tf_op jit(solution)/shard_map/ppermute | solution.py:15
  110.5 1.5 collective-permute-start.18
  112.0 6.2 %collective-permute-done.14 = bf16[1920,128]{0,1:T(8,128)(2,1)} collective-permute-done((bf16[1920,128]{0,1:T(8,128)(2,1)S(1)}, bf16[1920,128]{0,1:T(8,128)(2,1)}, u32[]{:S(2)}, u32[]{:S(2)}) %collective-permute-start.14) | collective-permute-done | bytes 491552 | tf_op jit(solution)/shard_map/ppermute | solution.py:15
  118.2 1.2 collective-permute-done.17
  120.3 2.0 add_convert_fusion.2
  125.3 1.5 collective-permute-start.19
  126.7 5.2 %collective-permute-start.20 = (bf16[1920,128]{0,1:T(8,128)(2,1)}, bf16[1920,128]{0,1:T(8,128)(2,1)}, u32[]{:S(2)}, u32[]{:S(2)}) collective-permute-start(bf16[1920,128]{0,1:T(8,128)(2,1)} %add_convert_fusion.2), channel_id=1, source_target_pairs={{0,0},{1,2},{2,1},{3,3},{4,4},{5,6},{6,5},{7,7},{8,8},{9,10},{10,9... | collective-permute-start | bytes 1474568 | tf_op jit(solution)/shard_map/ppermute | solution.py:95
  133.1 6.1 %collective-permute-done.19 = bf16[1920,128]{0,1:T(8,128)(2,1)} collective-permute-done((bf16[1920,128]{0,1:T(8,128)(2,1)}, bf16[1920,128]{0,1:T(8,128)(2,1)}, u32[]{:S(2)}, u32[]{:S(2)}) %collective-permute-start.19) | collective-permute-done | bytes 491552 | tf_op jit(solution)/shard_map/ppermute | solution.py:15
  139.2 6.4 %collective-permute-done.21 = bf16[1920,128]{0,1:T(8,128)(2,1)} collective-permute-done((bf16[1920,128]{0,1:T(8,128)(2,1)}, bf16[1920,128]{0,1:T(8,128)(2,1)}, u32[]{:S(2)}, u32[]{:S(2)}) %collective-permute-start.21) | collective-permute-done | bytes 491552 | tf_op jit(solution)/shard_map/ppermute | solution.py:15
  145.7 1.3 fusion.41
  147.0 1.2 broadcast_select_fusion.9
  148.4 2.8 %fusion.20 = f32[576,256]{1,0:T(8,128)S(1)} fusion(bf16[1920,256]{0,1:T(8,128)(2,1)} %pad_maximum_fusion.2, bf16[576,7680]{1,0:T(8,128)(2,1)} %bitcast.72, s32[]{:T(128)S(6)} %select_n.361), kind=kOutput, calls=%fused_computation.24 | convolution fusion | flops 566231040 | bytes 3784708 | tf_op jit(solution)/shard_map/dot_general | solution.py:19
  151.2 1.2 add_convert_fusion.1
  153.6 2.4 fusion.12
  157.0 2.0 fusion.37
  159.6 7.4 %collective-permute-done.23 = bf16[1920,128]{0,1:T(8,128)(2,1)S(1)} collective-permute-done((bf16[1920,128]{0,1:T(8,128)(2,1)S(1)}, bf16[1920,128]{0,1:T(8,128)(2,1)S(1)}, u32[]{:S(2)}, u32[]{:S(2)}) %collective-permute-start.23) | collective-permute-done | bytes 491552 | tf_op jit(solution)/shard_map/ppermute | solution.py:15
  168.2 1.5 collective-permute-start.28
  170.2 9.4 %collective-permute-done.26 = bf16[12,48,256]{2,1,0:T(8,128)(2,1)S(1)} collective-permute-done((bf16[12,48,256]{2,1,0:T(8,128)(2,1)S(1)}, bf16[12,48,256]{2,1,0:T(8,128)(2,1)S(1)}, u32[]{:S(2)}, u32[]{:S(2)}) %collective-permute-start.26) | collective-permute-done | bytes 294944 | tf_op jit(solution)/shard_map/ppermute | solution.py:11
  181.1 1.6 collective-permute-start.30
  184.8 14.0 %collective-permute-done.29 = bf16[12,48,256]{2,1,0:T(8,128)(2,1)S(1)} collective-permute-done((bf16[12,48,256]{2,1,0:T(8,128)(2,1)S(1)}, bf16[12,48,256]{2,1,0:T(8,128)(2,1)S(1)}, u32[]{:S(2)}, u32[]{:S(2)}) %collective-permute-start.29) | collective-permute-done | bytes 294944 | tf_op jit(solution)/shard_map/ppermute | solution.py:11
  200.2 2.4 fusion.10
  202.7 2.7 %fusion.6 = f32[576,256]{1,0:T(8,128)S(1)} fusion(bf16[1920,256]{0,1:T(8,128)(2,1)} %collective-permute-done.32, bf16[576,7680]{1,0:T(8,128)(2,1)} %bitcast.75, s32[]{:T(128)S(6)} %select_n.364), kind=kOutput, calls=%fused_computation.10 | convolution fusion | flops 566231040 | bytes 3784708 | tf_op jit(solution)/shard_map/dot_general | solution.py:19
  205.3 2.5 %fusion.31 = f32[576,256]{1,0:T(8,128)S(1)} fusion(f32[576,256]{1,0:T(8,128)S(1)} %fusion.6, f32[576,256]{1,0:T(8,128)S(1)} %fusion.10, f32[576,256]{1,0:T(8,128)S(1)} %fusion.18, bf16[1920,256]{0,1:T(8,128)(2,1)S(1)} %collective-permute-done.31, bf16[576,7680]{1,0:T(8,128)(2,1)} %bitcast.76, s32[]{:T(128)S(6)} %select_n.362), kind=kOutput, calls=%fused_computation.31 | convolution fusion | flops 566673408 | bytes 5554180 | tf_op jit(solution)/shard_map/dot_general | solution.py:19
  210.2 4.1 %collective-permute-done.34 = bf16[4,48,2,1,128]{4,2,1,0,3:T(2,128)(2,1)S(1)} collective-permute-done((bf16[4,48,2,1,128]{4,2,1,0,3:T(2,128)(2,1)S(1)}, bf16[4,48,2,1,128]{4,2,1,0,3:T(2,128)(2,1)S(1)}, u32[]{:S(2)}, u32[]{:S(2)}) %collective-permute-start.34) | collective-permute-done | bytes 98336 | tf_op jit(solution)/shard_map/ppermute | solution.py:15
  214.9 4.5 %collective-permute-done.36 = bf16[12,48,256]{2,1,0:T(8,128)(2,1)S(1)} collective-permute-done((bf16[12,48,256]{2,1,0:T(8,128)(2,1)S(1)}, bf16[12,48,256]{2,1,0:T(8,128)(2,1)S(1)}, u32[]{:S(2)}, u32[]{:S(2)}) %collective-permute-start.36) | collective-permute-done | bytes 294944 | tf_op jit(solution)/shard_map/ppermute | solution.py:11
  220.7 12.8 %collective-permute-done.37 = bf16[12,48,256]{2,1,0:T(8,128)(2,1)S(1)} collective-permute-done((bf16[12,48,256]{2,1,0:T(8,128)(2,1)S(1)}, bf16[12,48,256]{2,1,0:T(8,128)(2,1)S(1)}, u32[]{:S(2)}, u32[]{:S(2)}) %collective-permute-start.37) | collective-permute-done | bytes 294944 | tf_op jit(solution)/shard_map/ppermute | solution.py:11
  236.7 3.4 %collective-permute-done.39 = bf16[4,48,2,1,128]{4,2,1,0,3:T(2,128)(2,1)S(1)} collective-permute-done((bf16[4,48,2,1,128]{4,2,1,0,3:T(2,128)(2,1)S(1)}, bf16[4,48,2,1,128]{4,2,1,0,3:T(2,128)(2,1)S(1)}, u32[]{:S(2)}, u32[]{:S(2)}) %collective-permute-start.39) | collective-permute-done | bytes 98336 | tf_op jit(solution)/shard_map/ppermute | solution.py:15
  240.1 1.3 collective-permute-done.40
  243.7 2.1 copy.19
  (145 shorter events, 32.5 us)
Async XLA Ops:
  0.0 36.2 %copy-start = (bf16[2048,512]{1,0:T(8,128)(2,1)S(1)}, bf16[2048,512]{1,0:T(8,128)(2,1)}, u32[]{:S(2)}) copy-start(bf16[2048,512]{1,0:T(8,128)(2,1)} %param.11) | copy-start | bytes 6291460
  1.2 22.1 %collective-permute-start.1 = (bf16[2048,128]{1,0:T(8,128)(2,1)S(1)}, bf16[2048,128]{1,0:T(8,128)(2,1)S(1)}, u32[]{:S(2)}, u32[]{:S(2)}) collective-permute-start(bf16[2048,128]{1,0:T(8,128)(2,1)S(1)} %constant_dynamic-slice_fusion), channel_id=1, source_target_pairs={{0,0},{1,4},{2,12},{3,8},{4,1},{5,5},{6,13},{7,9},{8,2},{9,6},{10,... | collective-permute-start | bytes 1572872 | tf_op jit(solution)/shard_map/ppermute | solution.py:95
  4.2 19.1 %collective-permute-start.2 = (bf16[1024,128]{1,0:T(8,128)(2,1)}, bf16[1024,128]{1,0:T(8,128)(2,1)}, u32[]{:S(2)}, u32[]{:S(2)}) collective-permute-start(bf16[1024,128]{1,0:T(8,128)(2,1)} %get-tuple-element.146), channel_id=1, source_target_pairs={{0,8},{4,12},{8,0},{12,4},{1,9},{5,13},{9,1},{13,5},{2,10},{6,14},... | collective-permute-start | bytes 786440 | tf_op jit(solution)/shard_map/ppermute | solution.py:15
  10.9 1.3 collective-permute-start
  23.3 22.3 %collective-permute-start.5 = (bf16[2048,128]{1,0:T(8,128)(2,1)S(1)}, bf16[2048,128]{1,0:T(8,128)(2,1)S(1)}, u32[]{:S(2)}, u32[]{:S(2)}) collective-permute-start(bf16[2048,128]{1,0:T(8,128)(2,1)S(1)} %collective-permute-done.1), channel_id=1, source_target_pairs={{0,8},{4,12},{8,0},{12,4},{1,9},{5,13},{9,1},{13,5},{2,10},{6,14},... | collective-permute-start | bytes 1572872 | tf_op jit(solution)/shard_map/ppermute | solution.py:15
  34.0 2.5 %collective-permute-start.3 = (bf16[1024,128]{1,0:T(8,128)(2,1)S(1)}, bf16[1024,128]{1,0:T(8,128)(2,1)S(1)}, u32[]{:S(2)}, u32[]{:S(2)}) collective-permute-start(bf16[1024,128]{1,0:T(8,128)(2,1)S(1)} %get-tuple-element.164), channel_id=1, source_target_pairs={{0,0},{1,4},{2,6},{3,2},{4,1},{5,5},{6,7},{7,3},{8,8},{9,12},{10,1... | collective-permute-start | bytes 786440 | tf_op jit(solution)/shard_map/ppermute | solution.py:95
  34.7 10.8 %collective-permute-start.4 = (bf16[1024,128]{1,0:T(8,128)(2,1)S(1)}, bf16[1024,128]{1,0:T(8,128)(2,1)S(1)}, u32[]{:S(2)}, u32[]{:S(2)}) collective-permute-start(bf16[1024,128]{1,0:T(8,128)(2,1)S(1)} %get-tuple-element.163), channel_id=1, source_target_pairs={{0,2},{1,6},{2,4},{3,0},{4,3},{5,7},{6,5},{7,1},{8,10},{9,14},{10,... | collective-permute-start | bytes 786440 | tf_op jit(solution)/shard_map/ppermute | solution.py:95
  45.8 6.6 %collective-permute-start.6 = (bf16[2048,256]{1,0:T(8,128)(2,1)S(1)}, bf16[2048,256]{1,0:T(8,128)(2,1)}, u32[]{:S(2)}, u32[]{:S(2)}) collective-permute-start(bf16[2048,256]{1,0:T(8,128)(2,1)S(1)} %pad_maximum_fusion), channel_id=1, source_target_pairs={{0,4},{4,0},{8,12},{12,8},{1,5},{5,1},{9,13},{13,9},{2,6},{6,2},{1... | collective-permute-start | bytes 3145736 | tf_op jit(solution)/shard_map/ppermute | solution.py:15
  50.0 2.2 collective-permute-start.7
  61.4 15.0 %collective-permute-start.10 = (bf16[1024,256]{1,0:T(8,128)(2,1)S(1)}, bf16[1024,256]{1,0:T(8,128)(2,1)S(1)}, u32[]{:S(2)}, u32[]{:S(2)}) collective-permute-start(bf16[1024,256]{1,0:T(8,128)(2,1)S(1)} %pad_maximum_fusion.7), channel_id=1, source_target_pairs={{0,8},{4,12},{8,0},{12,4},{1,9},{5,13},{9,1},{13,5},{2,10},{6,14},... | collective-permute-start | bytes 1572872 | tf_op jit(solution)/shard_map/ppermute | solution.py:15
  63.2 13.2 %collective-permute-start.9 = (bf16[1920,128]{0,1:T(8,128)(2,1)S(1)}, bf16[1920,128]{0,1:T(8,128)(2,1)S(1)}, u32[]{:S(2)}, u32[]{:S(2)}) collective-permute-start(bf16[1920,128]{0,1:T(8,128)(2,1)S(1)} %select_convert_fusion.1), channel_id=1, source_target_pairs={{0,1},{1,0},{2,3},{3,2},{4,5},{5,4},{6,7},{7,6},{8,9},{9,8},{10,11... | collective-permute-start | bytes 1474568 | tf_op jit(solution)/shard_map/ppermute | solution.py:15
  63.6 12.0 %collective-permute-start.11 = (f32[1,512]{1,0:T(1,128)S(1)}, f32[1,512]{1,0:T(1,128)S(1)}, u32[]{:S(2)}, u32[]{:S(2)}) collective-permute-start(f32[1,512]{1,0:T(1,128)S(1)} %add.200), channel_id=1, source_target_pairs={{0,8},{4,12},{8,0},{12,4},{1,9},{5,13},{9,1},{13,5},{2,10},{6,14},... | collective-permute-start | bytes 6152 | tf_op jit(solution)/shard_map/ppermute | solution.py:15
  76.6 2.7 %collective-permute-start.13 = (bf16[2048,256]{1,0:T(8,128)(2,1)S(1)}, bf16[2048,256]{1,0:T(8,128)(2,1)S(1)}, u32[]{:S(2)}, u32[]{:S(2)}) collective-permute-start(bf16[2048,256]{1,0:T(8,128)(2,1)S(1)} %pad_maximum_fusion.1), channel_id=1, source_target_pairs={{0,4},{4,0},{8,12},{12,8},{1,5},{5,1},{9,13},{13,9},{2,6},{6,2},{1... | collective-permute-start | bytes 3145736 | tf_op jit(solution)/shard_map/ppermute | solution.py:15
  76.8 13.7 %collective-permute-start.8 = (bf16[1920,128]{0,1:T(8,128)(2,1)S(1)}, bf16[1920,128]{0,1:T(8,128)(2,1)S(1)}, u32[]{:S(2)}, u32[]{:S(2)}) collective-permute-start(bf16[1920,128]{0,1:T(8,128)(2,1)S(1)} %convert_element_type.113), channel_id=1, source_target_pairs={{0,1},{1,0},{2,3},{3,2},{4,5},{5,4},{6,7},{7,6},{8,9},{9,8},{10,11... | collective-permute-start | bytes 1474568 | tf_op jit(solution)/shard_map/ppermute | solution.py:15
  77.3 13.1 %collective-permute-start.12 = (bf16[1920,128]{0,1:T(8,128)(2,1)S(1)}, bf16[1920,128]{0,1:T(8,128)(2,1)S(1)}, u32[]{:S(2)}, u32[]{:S(2)}) collective-permute-start(bf16[1920,128]{0,1:T(8,128)(2,1)S(1)} %add_convert_fusion.5), channel_id=1, source_target_pairs={{0,0},{1,2},{2,1},{3,3},{4,4},{5,6},{6,5},{7,7},{8,8},{9,10},{10,9... | collective-permute-start | bytes 1474568 | tf_op jit(solution)/shard_map/ppermute | solution.py:95
  87.8 21.4 %copy-start.2 = (f32[1920,128]{0,1:T(8,128)S(1)}, f32[1920,128]{0,1:T(8,128)}, u32[]{:S(2)}) copy-start(f32[1920,128]{0,1:T(8,128)} %get-tuple-element.91) | copy-start | bytes 2949124
  90.6 6.6 %collective-permute-start.16 = (bf16[1920,128]{0,1:T(8,128)(2,1)S(1)}, bf16[1920,128]{0,1:T(8,128)(2,1)S(1)}, u32[]{:S(2)}, u32[]{:S(2)}) collective-permute-start(bf16[1920,128]{0,1:T(8,128)(2,1)S(1)} %add_convert_fusion.4), channel_id=1, source_target_pairs={{0,0},{1,2},{2,1},{3,3},{4,4},{5,6},{6,5},{7,7},{8,8},{9,10},{10,9... | collective-permute-start | bytes 1474568 | tf_op jit(solution)/shard_map/ppermute | solution.py:95
  91.4 17.8 %collective-permute-start.15 = (bf16[1920,128]{0,1:T(8,128)(2,1)S(1)}, bf16[1920,128]{0,1:T(8,128)(2,1)S(1)}, u32[]{:S(2)}, u32[]{:S(2)}) collective-permute-start(bf16[1920,128]{0,1:T(8,128)(2,1)S(1)} %fusion.40), channel_id=1, source_target_pairs={{0,1},{1,0},{2,3},{3,2},{4,5},{5,4},{6,7},{7,6},{8,9},{9,8},{10,11... | collective-permute-start | bytes 1474568 | tf_op jit(solution)/shard_map/ppermute | solution.py:15
  97.1 21.1 %collective-permute-start.14 = (bf16[1920,128]{0,1:T(8,128)(2,1)S(1)}, bf16[1920,128]{0,1:T(8,128)(2,1)}, u32[]{:S(2)}, u32[]{:S(2)}) collective-permute-start(bf16[1920,128]{0,1:T(8,128)(2,1)S(1)} %select_convert_fusion), channel_id=1, source_target_pairs={{0,1},{1,0},{2,3},{3,2},{4,5},{5,4},{6,7},{7,6},{8,9},{9,8},{10,11... | collective-permute-start | bytes 1474568 | tf_op jit(solution)/shard_map/ppermute | solution.py:15
  109.4 10.0 %collective-permute-start.17 = (bf16[1920,128]{0,1:T(8,128)(2,1)S(1)}, bf16[1920,128]{0,1:T(8,128)(2,1)S(1)}, u32[]{:S(2)}, u32[]{:S(2)}) collective-permute-start(bf16[1920,128]{0,1:T(8,128)(2,1)S(1)} %add_convert_fusion.3), channel_id=1, source_target_pairs={{0,8},{4,12},{8,0},{12,4},{1,9},{5,13},{9,1},{13,5},{2,10},{6,14},... | collective-permute-start | bytes 1474568 | tf_op jit(solution)/shard_map/ppermute | solution.py:15
  110.5 9.8 %collective-permute-start.18 = (bf16[1920,128]{0,1:T(8,128)(2,1)S(1)}, bf16[1920,128]{0,1:T(8,128)(2,1)}, u32[]{:S(2)}, u32[]{:S(2)}) collective-permute-start(bf16[1920,128]{0,1:T(8,128)(2,1)S(1)} %add_convert_fusion.3), channel_id=1, source_target_pairs={{0,16},{16,0},{1,17},{17,1},{2,18},{18,2},{3,19},{19,3},{4,20},{20... | collective-permute-start | bytes 1474568 | tf_op jit(solution)/shard_map/ppermute | solution.py:15
  123.4 9.7 %copy-start.8 = (s32[4]{0:T(128)S(1)}, s32[4]{0:T(128)}, u32[]{:S(2)}) copy-start(s32[4]{0:T(128)} %param.15) | copy-start | bytes 52
  123.4 22.3 %copy-start.1 = (f32[1920,128]{0,1:T(8,128)S(1)}, f32[1920,128]{0,1:T(8,128)}, u32[]{:S(2)}) copy-start(f32[1920,128]{0,1:T(8,128)} %get-tuple-element.104) | copy-start | bytes 2949124
  124.4 22.5 %copy-start.5 = (bf16[1920,128]{0,1:T(8,128)(2,1)S(1)}, bf16[1920,128]{0,1:T(8,128)(2,1)}, u32[]{:S(2)}) copy-start(bf16[1920,128]{0,1:T(8,128)(2,1)} %copy-done.4) | copy-start | bytes 1474564
  124.4 21.2 %collective-permute-start.22 = (bf16[1920,256]{0,1:T(8,128)(2,1)}, bf16[1920,256]{0,1:T(8,128)(2,1)}, u32[]{:S(2)}, u32[]{:S(2)}) collective-permute-start(bf16[1920,256]{0,1:T(8,128)(2,1)} %pad_maximum_fusion.2), channel_id=1, source_target_pairs={{0,4},{4,0},{8,12},{12,8},{1,5},{5,1},{9,13},{13,9},{2,6},{6,2},{1... | collective-permute-start | bytes 2949128 | tf_op jit(solution)/shard_map/ppermute | solution.py:15
  125.3 13.9 %collective-permute-start.19 = (bf16[1920,128]{0,1:T(8,128)(2,1)}, bf16[1920,128]{0,1:T(8,128)(2,1)}, u32[]{:S(2)}, u32[]{:S(2)}) collective-permute-start(bf16[1920,128]{0,1:T(8,128)(2,1)} %convert_element_type.125), channel_id=1, source_target_pairs={{0,1},{1,0},{2,3},{3,2},{4,5},{5,4},{6,7},{7,6},{8,9},{9,8},{10,11... | collective-permute-start | bytes 1474568 | tf_op jit(solution)/shard_map/ppermute | solution.py:15
  126.7 12.5 %collective-permute-start.20 = (bf16[1920,128]{0,1:T(8,128)(2,1)}, bf16[1920,128]{0,1:T(8,128)(2,1)}, u32[]{:S(2)}, u32[]{:S(2)}) collective-permute-start(bf16[1920,128]{0,1:T(8,128)(2,1)} %add_convert_fusion.2), channel_id=1, source_target_pairs={{0,0},{1,2},{2,1},{3,3},{4,4},{5,6},{6,5},{7,7},{8,8},{9,10},{10,9... | collective-permute-start | bytes 1474568 | tf_op jit(solution)/shard_map/ppermute | solution.py:95
  132.0 13.7 %collective-permute-start.21 = (bf16[1920,128]{0,1:T(8,128)(2,1)}, bf16[1920,128]{0,1:T(8,128)(2,1)}, u32[]{:S(2)}, u32[]{:S(2)}) collective-permute-start(bf16[1920,128]{0,1:T(8,128)(2,1)} %collective-permute-done.18), channel_id=1, source_target_pairs={{0,8},{4,12},{8,0},{12,4},{1,9},{5,13},{9,1},{13,5},{2,10},{6,14},... | collective-permute-start | bytes 1474568 | tf_op jit(solution)/shard_map/ppermute | solution.py:15
  145.7 10.4 %slice-start = ((s8[8847360]{0:T(1024)(128)(4,1)}), s8[4194304]{0:T(1024)(128)(4,1)S(1)}, s32[]{:S(2)}) async-start(s8[8847360]{0:T(1024)(128)(4,1)} %bitcast.77), calls=%async_computation | async-start | bytes 8388608
  148.3 7.8 %collective-permute-start.25 = (bf16[1920,256]{0,1:T(8,128)(2,1)S(1)}, bf16[1920,256]{0,1:T(8,128)(2,1)S(1)}, u32[]{:S(2)}, u32[]{:S(2)}) collective-permute-start(bf16[1920,256]{0,1:T(8,128)(2,1)S(1)} %pad_maximum_fusion.3), channel_id=1, source_target_pairs={{0,4},{4,0},{8,12},{12,8},{1,5},{5,1},{9,13},{13,9},{2,6},{6,2},{1... | collective-permute-start | bytes 2949128 | tf_op jit(solution)/shard_map/ppermute | solution.py:15
  152.4 7.1 %collective-permute-start.24 = (bf16[1920,128]{0,1:T(8,128)(2,1)S(1)}, bf16[1920,128]{0,1:T(8,128)(2,1)S(1)}, u32[]{:S(2)}, u32[]{:S(2)}) collective-permute-start(bf16[1920,128]{0,1:T(8,128)(2,1)S(1)} %add_convert_fusion.1), channel_id=1, source_target_pairs={{0,0},{1,2},{2,1},{3,3},{4,4},{5,6},{6,5},{7,7},{8,8},{9,10},{10,9... | collective-permute-start | bytes 1474568 | tf_op jit(solution)/shard_map/ppermute | solution.py:95
  153.3 13.7 %collective-permute-start.23 = (bf16[1920,128]{0,1:T(8,128)(2,1)S(1)}, bf16[1920,128]{0,1:T(8,128)(2,1)S(1)}, u32[]{:S(2)}, u32[]{:S(2)}) collective-permute-start(bf16[1920,128]{0,1:T(8,128)(2,1)S(1)} %fusion.41), channel_id=1, source_target_pairs={{0,1},{1,0},{2,3},{3,2},{4,5},{5,4},{6,7},{7,6},{8,9},{9,8},{10,11... | collective-permute-start | bytes 1474568 | tf_op jit(solution)/shard_map/ppermute | solution.py:15
  159.0 10.8 %copy-start.9 = (s32[4]{0:T(128)S(1)}, s32[4]{0:T(128)}, u32[]{:S(2)}) copy-start(s32[4]{0:T(128)} %param.14) | copy-start | bytes 52
  167.2 12.9 %collective-permute-start.27 = (bf16[1920,128]{0,1:T(8,128)(2,1)S(1)}, bf16[1920,128]{0,1:T(8,128)(2,1)S(1)}, u32[]{:S(2)}, u32[]{:S(2)}) collective-permute-start(bf16[1920,128]{0,1:T(8,128)(2,1)S(1)} %add_convert_fusion), channel_id=1, source_target_pairs={{0,8},{4,12},{8,0},{12,4},{1,9},{5,13},{9,1},{13,5},{2,10},{6,14},... | collective-permute-start | bytes 1474568 | tf_op jit(solution)/shard_map/ppermute | solution.py:15
  168.2 12.5 %collective-permute-start.28 = (bf16[1920,128]{0,1:T(8,128)(2,1)S(1)}, bf16[1920,128]{0,1:T(8,128)(2,1)S(1)}, u32[]{:S(2)}, u32[]{:S(2)}) collective-permute-start(bf16[1920,128]{0,1:T(8,128)(2,1)S(1)} %add_convert_fusion), channel_id=1, source_target_pairs={{0,16},{16,0},{1,17},{17,1},{2,18},{18,2},{3,19},{19,3},{4,20},{20... | collective-permute-start | bytes 1474568 | tf_op jit(solution)/shard_map/ppermute | solution.py:15
  169.8 9.9 %collective-permute-start.26 = (bf16[12,48,256]{2,1,0:T(8,128)(2,1)S(1)}, bf16[12,48,256]{2,1,0:T(8,128)(2,1)S(1)}, u32[]{:S(2)}, u32[]{:S(2)}) collective-permute-start(bf16[12,48,256]{2,1,0:T(8,128)(2,1)S(1)} %pad_maximum_fusion.9), channel_id=1, source_target_pairs={{0,1},{1,2},{2,3},{3,0},{4,5},{5,6},{6,7},{7,4},{8,9},{9,10},{10,1... | collective-permute-start | bytes 884744 | tf_op jit(solution)/shard_map/ppermute | solution.py:11
  181.0 17.7 %collective-permute-start.31 = (bf16[1920,256]{0,1:T(8,128)(2,1)S(1)}, bf16[1920,256]{0,1:T(8,128)(2,1)S(1)}, u32[]{:S(2)}, u32[]{:S(2)}) collective-permute-start(bf16[1920,256]{0,1:T(8,128)(2,1)S(1)} %pad_maximum_fusion.4), channel_id=1, source_target_pairs={{0,4},{4,0},{8,12},{12,8},{1,5},{5,1},{9,13},{13,9},{2,6},{6,2},{1... | collective-permute-start | bytes 2949128 | tf_op jit(solution)/shard_map/ppermute | solution.py:15
  181.1 17.6 %collective-permute-start.30 = (bf16[1920,128]{0,1:T(8,128)(2,1)S(1)}, bf16[1920,128]{0,1:T(8,128)(2,1)S(1)}, u32[]{:S(2)}, u32[]{:S(2)}) collective-permute-start(bf16[1920,128]{0,1:T(8,128)(2,1)S(1)} %collective-permute-done.27), channel_id=1, source_target_pairs={{0,16},{16,0},{1,17},{17,1},{2,18},{18,2},{3,19},{19,3},{4,20},{20... | collective-permute-start | bytes 1474568 | tf_op jit(solution)/shard_map/ppermute | solution.py:15
  182.7 16.1 %collective-permute-start.29 = (bf16[12,48,256]{2,1,0:T(8,128)(2,1)S(1)}, bf16[12,48,256]{2,1,0:T(8,128)(2,1)S(1)}, u32[]{:S(2)}, u32[]{:S(2)}) collective-permute-start(bf16[12,48,256]{2,1,0:T(8,128)(2,1)S(1)} %broadcast_select_fusion.15), channel_id=1, source_target_pairs={{0,2},{1,3},{2,0},{3,1},{4,6},{5,7},{6,4},{7,5},{8,10},{9,11},{10,... | collective-permute-start | bytes 884744 | tf_op jit(solution)/shard_map/ppermute | solution.py:11
  199.1 3.6 %collective-permute-start.32 = (bf16[1920,256]{0,1:T(8,128)(2,1)S(1)}, bf16[1920,256]{0,1:T(8,128)(2,1)}, u32[]{:S(2)}, u32[]{:S(2)}) collective-permute-start(bf16[1920,256]{0,1:T(8,128)(2,1)S(1)} %pad_maximum_fusion.5), channel_id=1, source_target_pairs={{0,4},{4,0},{8,12},{12,8},{1,5},{5,1},{9,13},{13,9},{2,6},{6,2},{1... | collective-permute-start | bytes 2949128 | tf_op jit(solution)/shard_map/ppermute | solution.py:15
  207.9 11.5 %collective-permute-start.36 = (bf16[12,48,256]{2,1,0:T(8,128)(2,1)S(1)}, bf16[12,48,256]{2,1,0:T(8,128)(2,1)S(1)}, u32[]{:S(2)}, u32[]{:S(2)}) collective-permute-start(bf16[12,48,256]{2,1,0:T(8,128)(2,1)S(1)} %pad_maximum_fusion.10), channel_id=1, source_target_pairs={{0,1},{1,2},{2,3},{3,0},{4,5},{5,6},{6,7},{7,4},{8,9},{9,10},{10,1... | collective-permute-start | bytes 884744 | tf_op jit(solution)/shard_map/ppermute | solution.py:11
  208.2 2.0 collective-permute-start.33
  208.7 5.5 %collective-permute-start.34 = (bf16[4,48,2,1,128]{4,2,1,0,3:T(2,128)(2,1)S(1)}, bf16[4,48,2,1,128]{4,2,1,0,3:T(2,128)(2,1)S(1)}, u32[]{:S(2)}, u32[]{:S(2)}) collective-permute-start(bf16[4,48,2,1,128]{4,2,1,0,3:T(2,128)(2,1)S(1)} %squeeze.26), channel_id=1, source_target_pairs={{0,8},{4,12},{8,0},{12,4},{1,9},{5,13},{9,1},{13,5},{2,10},{6,14},... | collective-permute-start | bytes 294920 | tf_op jit(solution)/shard_map/ppermute | solution.py:15
  209.8 5.1 %collective-permute-start.35 = (bf16[4,48,2,1,128]{4,2,1,0,3:T(2,128)(2,1)S(1)}, bf16[4,48,2,1,128]{4,2,1,0,3:T(2,128)(2,1)S(1)}, u32[]{:S(2)}, u32[]{:S(2)}) collective-permute-start(bf16[4,48,2,1,128]{4,2,1,0,3:T(2,128)(2,1)S(1)} %squeeze.27), channel_id=1, source_target_pairs={{0,12},{4,8},{8,4},{12,0},{1,13},{5,9},{9,5},{13,1},{2,14},{6,10},... | collective-permute-start | bytes 294920 | tf_op jit(solution)/shard_map/ppermute | solution.py:15
  219.5 14.0 %collective-permute-start.37 = (bf16[12,48,256]{2,1,0:T(8,128)(2,1)S(1)}, bf16[12,48,256]{2,1,0:T(8,128)(2,1)S(1)}, u32[]{:S(2)}, u32[]{:S(2)}) collective-permute-start(bf16[12,48,256]{2,1,0:T(8,128)(2,1)S(1)} %broadcast_select_fusion.14), channel_id=1, source_target_pairs={{0,2},{1,3},{2,0},{3,1},{4,6},{5,7},{6,4},{7,5},{8,10},{9,11},{10,... | collective-permute-start | bytes 884744 | tf_op jit(solution)/shard_map/ppermute | solution.py:11
  234.3 2.4 collective-permute-start.38
  234.5 5.7 %collective-permute-start.39 = (bf16[4,48,2,1,128]{4,2,1,0,3:T(2,128)(2,1)S(1)}, bf16[4,48,2,1,128]{4,2,1,0,3:T(2,128)(2,1)S(1)}, u32[]{:S(2)}, u32[]{:S(2)}) collective-permute-start(bf16[4,48,2,1,128]{4,2,1,0,3:T(2,128)(2,1)S(1)} %squeeze.30), channel_id=1, source_target_pairs={{0,8},{4,12},{8,0},{12,4},{1,9},{5,13},{9,1},{13,5},{2,10},{6,14},... | collective-permute-start | bytes 294920 | tf_op jit(solution)/shard_map/ppermute | solution.py:15
  235.6 5.8 %collective-permute-start.40 = (bf16[4,48,2,1,128]{4,2,1,0,3:T(2,128)(2,1)S(1)}, bf16[4,48,2,1,128]{4,2,1,0,3:T(2,128)(2,1)S(1)}, u32[]{:S(2)}, u32[]{:S(2)}) collective-permute-start(bf16[4,48,2,1,128]{4,2,1,0,3:T(2,128)(2,1)S(1)} %squeeze.31), channel_id=1, source_target_pairs={{0,12},{4,8},{8,4},{12,0},{1,13},{5,9},{9,5},{13,1},{2,14},{6,10},... | collective-permute-start | bytes 294920 | tf_op jit(solution)/shard_map/ppermute | solution.py:15
  (6 other events, 31.0 us)

commit v8 on v7

--- a/solution.py
+++ b/solution.py
@@ -113,21 +113,28 @@
         both = add_columns(proj_weight, jnp.concatenate([near, far], axis=1))
         near_0, near_1, far_0, far_1 = (both[:, k * width : (k + 1) * width] for k in range(4))
         near_kept = at_end == first_core
-        return (
-            jnp.where(first_core, near_1, far_1).astype(jnp.bfloat16),
-            jnp.where(first_core, far_1, near_1),
+        parts = (
+            jnp.where(near_kept, far_1, near_1),
+            jnp.where(near_kept, near_1, far_1),
             jnp.where(near_kept, far_0, near_0),
-            jnp.where(near_kept, near_0, far_0),
-        )
-
-    def neighbours(block):
-        return swapped(block.astype(jnp.bfloat16), "head", 1)
-
-    def middle(block):
-        return moved(block.astype(jnp.bfloat16), lambda t, h: (t, (0, 2, 1, 3)[h]))
-
-    def plus(block, arrived):
-        return block.astype(jnp.float32) + arrived.astype(jnp.float32)
+        )
+        own = jnp.where(near_kept, near_0, far_0)
+        return own, tuple(part.astype(jnp.bfloat16) for part in parts)
+
+    def exchange(parts):
+        return tuple(swapped(part, "head", bit) for part, bit in zip(parts, (2, 3, 1)))
+
+    def summed(own, arrived):
+        for block in arrived:
+            own = own + block.astype(jnp.float32)
+        return own.astype(jnp.bfloat16)
+
+    once = jnp.minimum(jnp.max(tile_count), 1)
+
+    def in_loop(chain, given):
+        shapes = jax.eval_shape(chain, given)[1]
+        empty = jax.tree.map(lambda x: jnp.zeros(x.shape, x.dtype), shapes)
+        return lax.fori_loop(0, once, lambda _, carry: chain(carry[0]), (given, empty))[1]
 
     def finish(total, part):
         finished = []
@@ -164,77 +171,58 @@
         return jnp.stack(ranked, axis=1)
 
     column, half = group * 2 * head_dim, kv_weight.shape[0] // 2
-    key_mine = lax.dynamic_slice_in_dim(kv_weight, column, head_dim, axis=1)
-    value_mine = lax.dynamic_slice_in_dim(kv_weight, column + head_dim, head_dim, axis=1)
-    stays = lax.dynamic_slice_in_dim(value_mine, tile // 2 * half, half, axis=0)
-    leaves = lax.dynamic_slice_in_dim(value_mine, half - tile // 2 * half, half, axis=0)
+
+    def to_planes(part):
+        mine = lax.dynamic_slice_in_dim(kv_weight, column + part * head_dim, head_dim, axis=1)
+        return (
+            moved(mine[:half], lambda t, h: (h // 2 * 2 + outer_core(h), t)),
+            moved(mine[half:], lambda t, h: ((1 - h // 2) * 2 + outer_core(h), t)),
+        )
+
+    def across(rows):
+        return swapped(jnp.concatenate(rows, axis=0), "tile", 2)
+
+    def with_other(rows, other):
+        one = jnp.concatenate([rows[0], other[half:]], axis=0)
+        two = jnp.concatenate([other[:half], rows[1]], axis=0)
+        return put_first(tile // 2 == head // 2, one, two, 1)
+
     bias_rows = moved(proj_bias, lambda t, h: (h, t))
-    key_block = moved(key_mine, lambda t, h: (h // 2 * 2 + outer_core(h), t))
-    comes = swapped(leaves, "tile", 2)
-    bias_rows, key_block, comes, stays = step((bias_rows, key_block, comes, stays))
-
-    value_pieces = []
-    for j in range(2):
-        piece = jnp.where(tile // 2 == (head // 2) ^ j, stays, comes)
-        value_pieces.append(
-            moved(piece, lambda t, h: (t // 2 * 2 + outer_core(h), t % 2 + 2 * ((h // 2) ^ j)))
-        )
-    key_other = swapped(key_block, "tile", 2)
+    bias_rows, key_rows = step((bias_rows, to_planes(0)))
+
     bias_part = add_columns(bias_rows[None], kv_weight)
-    value_pieces, key_block, key_other, bias_part = step(
-        (value_pieces, key_block, key_other, bias_part)
-    )
-
-    key_near = put_first(tile // 2 == head // 2, key_block, key_other, 1)
-    value_half = jnp.concatenate(value_pieces, axis=1)
-    key_near, value_half = step((key_near, value_half))
-    first, second, third, own = products(key_near, swapped(key_near, "tile", 1))
+    value_rows, key_rows, key_other, bias_part = step(
+        (to_planes(1), key_rows, across(key_rows), bias_part)
+    )
+
+    key_near = step(with_other(key_rows, key_other))
+    own, parts = products(key_near, swapped(key_near, "tile", 1))
     bias_part = bias_part + swapped(bias_part, "tile", 1)
-    first, second, third, own, value_half, bias_part = step(
-        (first, second, third, own, value_half, bias_part)
-    )
-
-    in_1, value_other, bias_other = step(
-        (neighbours(first), swapped(value_half, "tile", 2), swapped(bias_part, "tile", 2))
-    )
-    bias_part = (bias_part + bias_other).reshape(2, layers, 2, head_dim)
-
-    value_near = put_first(first_chip, value_half, value_other, 0)
-    relayed = plus(first, in_1).astype(jnp.bfloat16)
-    value_near, relayed = step((value_near, relayed))
-    in_2, across_2 = neighbours(second), middle(relayed)
-    value_products = products(value_near, swapped(value_near, "tile", 1))
-    in_2, across_2, value_products = step((in_2, across_2, value_products))
-
-    relayed = jnp.where(at_end, third, plus(third, across_2)).astype(jnp.bfloat16)
-    in_3, across_3 = step((neighbours(relayed), middle(plus(second, in_2))))
-    own = plus(own, in_3) + jnp.where(at_end, 0.0, across_3.astype(jnp.float32))
-    own = own.astype(jnp.bfloat16)
-
-    first, second, third, value_own = value_products
-    in_1, across_x, across_y = step(
-        (neighbours(first), swapped(own, "tile", 2), swapped(own, "groups", 1))
-    )
-
-    rows_0, relayed = step((both_heads(own, across_y), plus(first, in_1).astype(jnp.bfloat16)))
-    in_2, across_2, diagonal, rows_1 = step(
-        (
-            neighbours(second),
-            middle(relayed),
-            swapped(across_y, "tile", 2),
-            swapped(rows_0, "tile", 1),
-        )
-    )
-
-    relayed = jnp.where(at_end, third, plus(third, across_2)).astype(jnp.bfloat16)
-    rows_2, relayed = step((both_heads(across_x, diagonal), relayed))
-    in_3, across_3 = neighbours(relayed), middle(plus(second, in_2))
-    total = times_features(rows_0, 0) + times_features(rows_1, 1)
-    total = total + times_features(rows_2, 2) + times_features(swapped(rows_2, "tile", 1), 3)
-    keys = finish(total, 0)
-    in_3, across_3, keys = step((in_3, across_3, keys))
-    own = plus(value_own, in_3) + jnp.where(at_end, 0.0, across_3.astype(jnp.float32))
-    own = own.astype(jnp.bfloat16)
+    own, parts, value_rows, bias_part = step((own, parts, value_rows, bias_part))
+
+    def values_product(given):
+        rows, bias = given
+        other, bias_other = step((across(rows), swapped(bias, "tile", 2)))
+        near = step(with_other(rows, other))
+        given = (other[:half], other[half:]), bias_other
+        return given, (products(near, swapped(near, "tile", 1)), bias + bias_other)
+
+    arrived, beside = step((exchange(parts), in_loop(values_product, (value_rows, bias_part))))
+    own = summed(own, arrived)
+    (value_own, parts), bias_part = beside
+    bias_part = bias_part.reshape(2, layers, 2, head_dim)
+
+    def keys_product(own):
+        across_x, across_y = step((swapped(own, "tile", 2), swapped(own, "groups", 1)))
+        rows_0 = step(both_heads(own, across_y))
+        diagonal, rows_1 = step((swapped(across_y, "tile", 2), swapped(rows_0, "tile", 1)))
+        rows_2 = step(both_heads(across_x, diagonal))
+        total = times_features(rows_0, 0) + times_features(rows_1, 1)
+        total = total + times_features(rows_2, 2) + times_features(swapped(rows_2, "tile", 1), 3)
+        return across_x, finish(total, 0)
+
+    arrived, keys = step((exchange(parts), in_loop(keys_product, own)))
+    own = summed(value_own, arrived)
 
     shifted, across_x, across_y = step(
         (shifted_2(keys, "head", 1), swapped(own, "tile", 2), swapped(own, "groups", 1))

time: 247 us -> 252 us (1.020)
  local copies, waits for them, and re-layouts: 7.24 us -> 26.5 us
  waiting for transfers between devices: 131 us -> 115 us
  starting transfers between devices: 56.5 us -> 67.1 us
  matrix products: 32 us -> 26.7 us
  other arithmetic: 18.6 us -> 15.3 us
    ppermute x29 -> x28, waiting for transfers between devices: 80.9 us -> 48.9 us  [swapped(): lax.ppermute(shard, axis, [(i, i ^ bit) for i in range(lax.axis_size(axis...]
    ppermute x8 -> x5, waiting for transfers between devices: 9.03 us -> 30.8 us  [moved(): return lax.ppermute(shard, ('tile', 'head'), pairs)]
    ppermute x4, starting transfers between devices: 1.73 us -> 10.9 us  [shifted_2(): lax.ppermute(shard, axis, [(i, (i + by) % count) for i in range(count)])]
    ppermute x4, waiting for transfers between devices: 40.8 us -> 35.3 us  [shifted_2(): lax.ppermute(shard, axis, [(i, (i + by) % count) for i in range(count)])]
    dot_general x13, matrix products: 31.8 us -> 26.5 us  [add_columns(): return jnp.dot(operand, portion, preferred_element_type=jnp.float32)]
    dynamic_slice x2 -> x1, local copies, waits for them, and re-layouts: 3.48 us -> 7.24 us  [times_features(): lax.dynamic_slice_in_dim(feature_rows, (tile ^ r) * depth, depth, axis=1)]
    slice x0 -> x3, local copies, waits for them, and re-layouts: none -> 3.23 us  [the longest x1 2.14 us: to_planes(): mine[half:]]
    squeeze x8, local copies, waits for them, and re-layouts: 0.94 us -> 3.99 us  [outgoing(): return [picked[r] for r in range(4)]]
  transfers between devices with their start and end apart: 41 -> 37, of which waited for: 25 -> 18; matrix products, arithmetic and copies ran while one was open for 12% -> 17% of each run, Pallas kernels for 0% -> 0%
where the time goes in v8:
time: 252 us
  waiting for transfers between devices  115 us (46%)
  starting transfers between devices  67.1 us (27%)
  matrix products  26.7 us (11%)
  local copies, waits for them, and re-layouts  26.5 us (11%)
  other arithmetic  15.3 us (6%)
    ppermute x28, waiting for transfers between devices, swapped(): lax.ppermute(shard, axis, [(i, i ^ bit) for i in range(lax.axis_size(axis...  48.9 us
    ppermute x28, starting transfers between devices, swapped(): lax.ppermute(shard, axis, [(i, i ^ bit) for i in range(lax.axis_size(axis...  45.4 us
    ppermute x4, waiting for transfers between devices, shifted_2(): lax.ppermute(shard, axis, [(i, (i + by) % count) for i in range(count)])  35.3 us
    ppermute x5, waiting for transfers between devices, moved(): return lax.ppermute(shard, ('tile', 'head'), pairs)  30.8 us
    dot_general x13, matrix products, add_columns(): return jnp.dot(operand, portion, preferred_element_type=jnp.float32)  26.5 us
    ppermute x4, starting transfers between devices, shifted_2(): lax.ppermute(shard, axis, [(i, (i + by) % count) for i in range(count)])  10.9 us
    ppermute x5, starting transfers between devices, moved(): return lax.ppermute(shard, ('tile', 'head'), pairs)  10.8 us
    dynamic_slice x1, local copies, waits for them, and re-layouts, times_features(): lax.dynamic_slice_in_dim(feature_rows, (tile ^ r) * depth, depth, axis=1)  7.24 us
  transfers between devices with their start and end apart: 37, of which 18 were waited for; matrix products, arithmetic and copies ran while one was open for 17% of the time, Pallas kernels for 0%

profile of v8, /device:TPU:0, one launch (start us, length us, event | category | flops | bytes accessed | tf_op | source)
XLA Modules:
  0.0 251.9 jit_solution(8537281779039557102)
XLA Ops:
  0.0 2.1 fusion.31
  2.8 6.8 %collective-permute-start.12 = (bf16[1024,128]{1,0:T(8,128)(2,1)S(1)}, bf16[1024,128]{1,0:T(8,128)(2,1)S(1)}, u32[]{:S(2)}, u32[]{:S(2)}) collective-permute-start(bf16[1024,128]{1,0:T(8,128)(2,1)S(1)} %get-tuple-element.661), channel_id=1, source_target_pairs={{0,8},{1,12},{2,4},{3,0},{4,9},{5,13},{6,5},{7,1},{8,10},{9,14},{1... | collective-permute-start | bytes 786440 | tf_op jit(solution)/shard_map/ppermute | solution.py:95
  9.6 1.3 collective-permute-start.10
  10.9 11.7 %collective-permute-done.12 = bf16[1024,128]{1,0:T(8,128)(2,1)S(1)} collective-permute-done((bf16[1024,128]{1,0:T(8,128)(2,1)S(1)}, bf16[1024,128]{1,0:T(8,128)(2,1)S(1)}, u32[]{:S(2)}, u32[]{:S(2)}) %collective-permute-start.12) | collective-permute-done | bytes 262176 | tf_op jit(solution)/shard_map/ppermute | solution.py:95
  23.5 11.3 %collective-permute-start.13 = (bf16[2048,128]{1,0:T(8,128)(2,1)}, bf16[2048,128]{1,0:T(8,128)(2,1)}, u32[]{:S(2)}, u32[]{:S(2)}) collective-permute-start(bf16[2048,128]{1,0:T(8,128)(2,1)} %pad_maximum_fusion.11), channel_id=1, source_target_pairs={{0,8},{4,12},{8,0},{12,4},{1,9},{5,13},{9,1},{13,5},{2,10},{6,14},... | collective-permute-start | bytes 1572872 | tf_op jit(solution)/shard_map/ppermute | solution.py:15
  34.8 1.6 collective-permute-start.8
  37.1 19.1 %collective-permute-done.9 = bf16[1024,128]{1,0:T(8,128)(2,1)S(1)} collective-permute-done((bf16[1024,128]{1,0:T(8,128)(2,1)S(1)}, bf16[1024,128]{1,0:T(8,128)(2,1)S(1)}, u32[]{:S(2)}, u32[]{:S(2)}) %collective-permute-start.9) | collective-permute-done | bytes 262176 | tf_op jit(solution)/shard_map/ppermute | solution.py:95
  57.6 4.7 %collective-permute-start.14 = (bf16[2048,256]{1,0:T(8,128)(2,1)S(1)}, bf16[2048,256]{1,0:T(8,128)(2,1)S(1)}, u32[]{:S(2)}, u32[]{:S(2)}) collective-permute-start(bf16[2048,256]{1,0:T(8,128)(2,1)S(1)} %pad_maximum_fusion.7), channel_id=1, source_target_pairs={{0,4},{4,0},{8,12},{12,8},{1,5},{5,1},{9,13},{13,9},{2,6},{6,2},{1... | collective-permute-start | bytes 3145736 | tf_op jit(solution)/shard_map/ppermute | solution.py:15
  62.3 7.2 %constant_dynamic-slice_fusion.1 = (bf16[576,1920]{1,0:T(8,128)(2,1)}, bf16[576,1920]{1,0:T(8,128)(2,1)}, bf16[576,1920]{1,0:T(8,128)(2,1)}, bf16[576,1920]{1,0:T(8,128)(2,1)}) fusion(bf16[576,7680]{1,0:T(8,128)(2,1)} %bitcast.114, s32[]{:T(128)S(6)} %select_n.343, s32[]{:T(128)S(6)} %select_n.342, s32[]{:T(128)S(6)} %select_n.341, s32[]{:T(128)S(6)} %select_n.340), kind=kLoop, calls=%fused_computation.116 | loop fusion | bytes 17694736 | tf_op jit(solution)/shard_map/while/body/dynamic_slice | solution.py:101
  71.1 7.1 %convolution_bitcast_fusion.1 = f32[1920,512]{0,1:T(8,128)S(1)} fusion(bf16[1920,2048]{1,0:T(8,128)(2,1)} %param.13, bf16[2048,256]{1,0:T(8,128)(2,1)S(1)} %collective-permute-done.14, bf16[2048,256]{1,0:T(8,128)(2,1)S(1)} %pad_maximum_fusion.7), kind=kOutput, calls=%fused_computation.38 | convolution fusion | flops 4030726144 | bytes 13893632 | tf_op jit(solution)/shard_map/dot_general | solution.py:19
  78.3 1.2 select_convert_fusion.3
  79.7 1.3 collective-permute-start.17
  81.0 2.0 collective-permute-start.18
  87.1 26.5 %while.41 = (s32[]{:T(128)}, bf16[1024,128]{1,0:T(8,128)(2,1)S(1)}, bf16[1024,128]{1,0:T(8,128)(2,1)S(1)}, f32[1,512]{1,0:T(1,128)S(1)}, f32[1920,128]{0,1:T(8,1...) while((s32[]{:T(128)}, bf16[1024,128]{1,0:T(8,128)(2,1)S(1)}, ...), condition=%wide.region_2.3_spmd, body=%wide.region_1.2_spmd.sunk | while | flops 4037476864 | bytes 33933564 | solution.py:137
  87.3 1.9 collective-permute-start.1
  89.2 11.5 %collective-permute-done.1 = f32[1,512]{1,0:T(1,128)S(1)} collective-permute-done((f32[1,512]{1,0:T(1,128)S(1)}, f32[1,512]{1,0:T(1,128)S(1)}, u32[]{:S(2)}, u32[]{:S(2)}) %collective-permute-start.1) | collective-permute-done | bytes 2080 | tf_op jit(solution)/shard_map/while/body/ppermute | solution.py:15
  101.8 2.1 collective-permute-done.2
  103.9 7.4 %convolution_bitcast_fusion.3 = f32[1920,512]{0,1:T(8,128)S(1)} fusion(bf16[1920,2048]{1,0:T(8,128)(2,1)} %get-tuple-element.924, bf16[2048,256]{1,0:T(8,128)(2,1)} %collective-permute-done.2, bf16[2048,256]{1,0:T(8,128)(2,1)S(1)} %pad_maximum_fusion.22), kind=kOutput, calls=%fused_computation.clone.1 | convolution fusion | flops 4030726144 | bytes 13893632 | tf_op jit(solution)/shard_map/while/body/dot_general | solution.py:19
  112.4 1.2 select_convert_fusion.7
  114.1 1.6 collective-permute-done.18
  115.6 8.5 %collective-permute-start.19 = (bf16[1920,128]{0,1:T(8,128)(2,1)}, bf16[1920,128]{0,1:T(8,128)(2,1)}, u32[]{:S(2)}, u32[]{:S(2)}) collective-permute-start(bf16[1920,128]{0,1:T(8,128)(2,1)} %get-tuple-element.529), channel_id=1, source_target_pairs={{0,2},{1,3},{2,0},{3,1},{4,6},{5,7},{6,4},{7,5},{8,10},{9,11},{10,... | collective-permute-start | bytes 1474568 | tf_op jit(solution)/shard_map/ppermute | solution.py:15
  124.1 3.4 %collective-permute-start.20 = (bf16[1920,128]{0,1:T(8,128)(2,1)}, bf16[1920,128]{0,1:T(8,128)(2,1)}, u32[]{:S(2)}, u32[]{:S(2)}) collective-permute-start(bf16[1920,128]{0,1:T(8,128)(2,1)} %get-tuple-element.530), channel_id=1, source_target_pairs={{0,3},{1,2},{2,1},{3,0},{4,7},{5,6},{6,5},{7,4},{8,11},{9,10},{10,... | collective-permute-start | bytes 1474568 | tf_op jit(solution)/shard_map/ppermute | solution.py:15
  127.5 1.5 add_convert_fusion.1
  130.0 35.2 %while.42 = (s32[]{:T(128)}, bf16[1920,128]{1,0:T(8,128)(2,1)S(1)}, bf16[12,48,256]{2,1,0:T(8,128)(2,1)}, s32[]{:T(128)}, pred[]{:T(512)}, /*index=5*/bf16[576,1...) while((s32[]{:T(128)}, bf16[1920,128]{1,0:T(8,128)(2,1)S(1)}, ...), condition=%wide.region_6.7_spmd, body=%wide.region_3.6_spmd.sunk | while | flops 2271905024 | bytes 76995496 | solution.py:137
  130.1 1.2 collective-permute-start.3
  131.3 1.5 collective-permute-start.4
  132.8 10.0 %collective-permute-done.3 = bf16[1920,128]{1,0:T(8,128)(2,1)S(1)} collective-permute-done((bf16[1920,128]{1,0:T(8,128)(2,1)S(1)}, bf16[1920,128]{1,0:T(8,128)(2,1)S(1)}, u32[]{:S(2)}, u32[]{:S(2)}) %collective-permute-start.3) | collective-permute-done | bytes 491552 | tf_op jit(solution)/shard_map/while/body/ppermute | solution.py:15
  144.9 12.7 %collective-permute-done.5 = bf16[1920,128]{1,0:T(8,128)(2,1)S(1)} collective-permute-done((bf16[1920,128]{1,0:T(8,128)(2,1)S(1)}, bf16[1920,128]{1,0:T(8,128)(2,1)S(1)}, u32[]{:S(2)}, u32[]{:S(2)}) %collective-permute-start.5) | collective-permute-done | bytes 491552 | tf_op jit(solution)/shard_map/while/body/ppermute | solution.py:15
  159.4 2.1 convolution_add_fusion.8
  165.3 1.6 add_convert_fusion
  167.8 1.5 collective-permute-start.24
  169.4 5.8 %collective-permute-start.22 = (bf16[12,48,256]{2,1,0:T(8,128)(2,1)S(1)}, bf16[12,48,256]{2,1,0:T(8,128)(2,1)S(1)}, u32[]{:S(2)}, u32[]{:S(2)}) collective-permute-start(bf16[12,48,256]{2,1,0:T(8,128)(2,1)S(1)} %copy-done.10), channel_id=1, source_target_pairs={{0,1},{1,2},{2,3},{3,0},{4,5},{5,6},{6,7},{7,4},{8,9},{9,10},{10,1... | collective-permute-start | bytes 884744 | tf_op jit(solution)/shard_map/ppermute | solution.py:11
  175.3 5.6 %collective-permute-done.22 = bf16[12,48,256]{2,1,0:T(8,128)(2,1)S(1)} collective-permute-done((bf16[12,48,256]{2,1,0:T(8,128)(2,1)S(1)}, bf16[12,48,256]{2,1,0:T(8,128)(2,1)S(1)}, u32[]{:S(2)}, u32[]{:S(2)}) %collective-permute-start.22) | collective-permute-done | bytes 294944 | tf_op jit(solution)/shard_map/ppermute | solution.py:11
  181.7 1.5 collective-permute-start.26
  183.2 4.1 %collective-permute-start.25 = (bf16[12,48,256]{2,1,0:T(8,128)(2,1)S(1)}, bf16[12,48,256]{2,1,0:T(8,128)(2,1)S(1)}, u32[]{:S(2)}, u32[]{:S(2)}) collective-permute-start(bf16[12,48,256]{2,1,0:T(8,128)(2,1)S(1)} %broadcast_select_fusion.15), channel_id=1, source_target_pairs={{0,2},{1,3},{2,0},{3,1},{4,6},{5,7},{6,4},{7,5},{8,10},{9,11},{10,... | collective-permute-start | bytes 884744 | tf_op jit(solution)/shard_map/ppermute | solution.py:11
  187.4 1.6 fusion.37
  189.0 12.1 %collective-permute-done.25 = bf16[12,48,256]{2,1,0:T(8,128)(2,1)S(1)} collective-permute-done((bf16[12,48,256]{2,1,0:T(8,128)(2,1)S(1)}, bf16[12,48,256]{2,1,0:T(8,128)(2,1)S(1)}, u32[]{:S(2)}, u32[]{:S(2)}) %collective-permute-start.25) | collective-permute-done | bytes 294944 | tf_op jit(solution)/shard_map/ppermute | solution.py:11
  204.6 1.6 squeeze.27
  207.1 2.3 convolution_add_fusion.5
  211.1 2.0 convolution_add_fusion.3
  215.9 4.0 %collective-permute-done.30 = bf16[4,48,2,1,128]{4,2,1,0,3:T(2,128)(2,1)S(1)} collective-permute-done((bf16[4,48,2,1,128]{4,2,1,0,3:T(2,128)(2,1)S(1)}, bf16[4,48,2,1,128]{4,2,1,0,3:T(2,128)(2,1)S(1)}, u32[]{:S(2)}, u32[]{:S(2)}) %collective-permute-start.30) | collective-permute-done | bytes 98336 | tf_op jit(solution)/shard_map/ppermute | solution.py:15
  220.8 4.0 %collective-permute-done.32 = bf16[12,48,256]{2,1,0:T(8,128)(2,1)S(1)} collective-permute-done((bf16[12,48,256]{2,1,0:T(8,128)(2,1)S(1)}, bf16[12,48,256]{2,1,0:T(8,128)(2,1)S(1)}, u32[]{:S(2)}, u32[]{:S(2)}) %collective-permute-start.32) | collective-permute-done | bytes 294944 | tf_op jit(solution)/shard_map/ppermute | solution.py:11
  226.0 13.6 %collective-permute-done.33 = bf16[12,48,256]{2,1,0:T(8,128)(2,1)S(1)} collective-permute-done((bf16[12,48,256]{2,1,0:T(8,128)(2,1)S(1)}, bf16[12,48,256]{2,1,0:T(8,128)(2,1)S(1)}, u32[]{:S(2)}, u32[]{:S(2)}) %collective-permute-start.33) | collective-permute-done | bytes 294944 | tf_op jit(solution)/shard_map/ppermute | solution.py:11
  241.2 1.5 collective-permute-start.36
  242.8 3.4 %collective-permute-done.35 = bf16[4,48,2,1,128]{4,2,1,0,3:T(2,128)(2,1)S(1)} collective-permute-done((bf16[4,48,2,1,128]{4,2,1,0,3:T(2,128)(2,1)S(1)}, bf16[4,48,2,1,128]{4,2,1,0,3:T(2,128)(2,1)S(1)}, u32[]{:S(2)}, u32[]{:S(2)}) %collective-permute-start.35) | collective-permute-done | bytes 98336 | tf_op jit(solution)/shard_map/ppermute | solution.py:15
  246.3 1.3 collective-permute-done.36
  248.7 1.1 pad_maximum_fusion.10
  249.8 2.1 copy.21
  (157 shorter events, 35.7 us)
Async XLA Ops:
  0.0 36.8 %copy-start = (bf16[2048,512]{1,0:T(8,128)(2,1)S(1)}, bf16[2048,512]{1,0:T(8,128)(2,1)}, u32[]{:S(2)}) copy-start(bf16[2048,512]{1,0:T(8,128)(2,1)} %param.15) | copy-start | bytes 6291460
  2.1 8.8 %collective-permute-start.11 = (bf16[1024,128]{1,0:T(8,128)(2,1)S(1)}, bf16[1024,128]{1,0:T(8,128)(2,1)S(1)}, u32[]{:S(2)}, u32[]{:S(2)}) collective-permute-start(bf16[1024,128]{1,0:T(8,128)(2,1)S(1)} %get-tuple-element.662), channel_id=1, source_target_pairs={{0,0},{1,4},{2,12},{3,8},{4,1},{5,5},{6,13},{7,9},{8,2},{9,6},{10,... | collective-permute-start | bytes 786440 | tf_op jit(solution)/shard_map/ppermute | solution.py:95
  2.8 19.9 %collective-permute-start.12 = (bf16[1024,128]{1,0:T(8,128)(2,1)S(1)}, bf16[1024,128]{1,0:T(8,128)(2,1)S(1)}, u32[]{:S(2)}, u32[]{:S(2)}) collective-permute-start(bf16[1024,128]{1,0:T(8,128)(2,1)S(1)} %get-tuple-element.661), channel_id=1, source_target_pairs={{0,8},{1,12},{2,4},{3,0},{4,9},{5,13},{6,5},{7,1},{8,10},{9,14},{1... | collective-permute-start | bytes 786440 | tf_op jit(solution)/shard_map/ppermute | solution.py:95
  9.6 1.3 collective-permute-start.10
  23.5 32.7 %collective-permute-start.13 = (bf16[2048,128]{1,0:T(8,128)(2,1)}, bf16[2048,128]{1,0:T(8,128)(2,1)}, u32[]{:S(2)}, u32[]{:S(2)}) collective-permute-start(bf16[2048,128]{1,0:T(8,128)(2,1)} %pad_maximum_fusion.11), channel_id=1, source_target_pairs={{0,8},{4,12},{8,0},{12,4},{1,9},{5,13},{9,1},{13,5},{2,10},{6,14},... | collective-permute-start | bytes 1572872 | tf_op jit(solution)/shard_map/ppermute | solution.py:15
  34.8 2.4 collective-permute-start.8
  36.4 19.8 %collective-permute-start.9 = (bf16[1024,128]{1,0:T(8,128)(2,1)S(1)}, bf16[1024,128]{1,0:T(8,128)(2,1)S(1)}, u32[]{:S(2)}, u32[]{:S(2)}) collective-permute-start(bf16[1024,128]{1,0:T(8,128)(2,1)S(1)} %get-tuple-element.664), channel_id=1, source_target_pairs={{0,8},{1,12},{2,4},{3,0},{4,9},{5,13},{6,5},{7,1},{8,10},{9,14},{1... | collective-permute-start | bytes 786440 | tf_op jit(solution)/shard_map/ppermute | solution.py:95
  57.6 13.5 %collective-permute-start.14 = (bf16[2048,256]{1,0:T(8,128)(2,1)S(1)}, bf16[2048,256]{1,0:T(8,128)(2,1)S(1)}, u32[]{:S(2)}, u32[]{:S(2)}) collective-permute-start(bf16[2048,256]{1,0:T(8,128)(2,1)S(1)} %pad_maximum_fusion.7), channel_id=1, source_target_pairs={{0,4},{4,0},{8,12},{12,8},{1,5},{5,1},{9,13},{13,9},{2,6},{6,2},{1... | collective-permute-start | bytes 3145736 | tf_op jit(solution)/shard_map/ppermute | solution.py:15
  62.3 7.3 %copy-start.16 = (s32[4]{0:T(128)S(1)}, s32[4]{0:T(128)}, u32[]{:S(2)}) copy-start(s32[4]{0:T(128)} %param.19) | copy-start | bytes 52
  62.3 7.3 %copy-start.15 = (s32[4,4]{1,0:T(4,128)S(1)}, s32[4,4]{1,0:T(4,128)}, u32[]{:S(2)}) copy-start(s32[4,4]{1,0:T(4,128)} %param.17) | copy-start | bytes 196
  62.3 7.4 %copy-start.18 = (s32[4]{0:T(128)S(1)}, s32[4]{0:T(128)}, u32[]{:S(2)}) copy-start(s32[4]{0:T(128)} %param.18) | copy-start | bytes 52
  69.6 1.5 collective-permute-start.15
  79.5 34.6 %collective-permute-start.16 = (bf16[1920,128]{0,1:T(8,128)(2,1)}, bf16[1920,128]{0,1:T(8,128)(2,1)}, u32[]{:S(2)}, u32[]{:S(2)}) collective-permute-start(bf16[1920,128]{0,1:T(8,128)(2,1)} %get-tuple-element.518), channel_id=1, source_target_pairs={{0,2},{1,3},{2,0},{3,1},{4,6},{5,7},{6,4},{7,5},{8,10},{9,11},{10,... | collective-permute-start | bytes 1474568 | tf_op jit(solution)/shard_map/ppermute | solution.py:15
  79.7 34.4 %collective-permute-start.17 = (bf16[1920,128]{0,1:T(8,128)(2,1)}, bf16[1920,128]{0,1:T(8,128)(2,1)}, u32[]{:S(2)}, u32[]{:S(2)}) collective-permute-start(bf16[1920,128]{0,1:T(8,128)(2,1)} %get-tuple-element.519), channel_id=1, source_target_pairs={{0,3},{1,2},{2,1},{3,0},{4,7},{5,6},{6,5},{7,4},{8,11},{9,10},{10,... | collective-permute-start | bytes 1474568 | tf_op jit(solution)/shard_map/ppermute | solution.py:15
  81.0 34.6 %collective-permute-start.18 = (bf16[1920,128]{0,1:T(8,128)(2,1)}, bf16[1920,128]{0,1:T(8,128)(2,1)}, u32[]{:S(2)}, u32[]{:S(2)}) collective-permute-start(bf16[1920,128]{0,1:T(8,128)(2,1)} %get-tuple-element.520), channel_id=1, source_target_pairs={{0,1},{1,0},{2,3},{3,2},{4,5},{5,4},{6,7},{7,6},{8,9},{9,8},{10,11... | collective-permute-start | bytes 1474568 | tf_op jit(solution)/shard_map/ppermute | solution.py:15
  87.1 13.6 %collective-permute-start = (bf16[2048,128]{1,0:T(8,128)(2,1)S(1)}, bf16[2048,128]{1,0:T(8,128)(2,1)S(1)}, u32[]{:S(2)}, u32[]{:S(2)}) collective-permute-start(bf16[2048,128]{1,0:T(8,128)(2,1)S(1)} %pad_maximum_fusion.21), channel_id=1, source_target_pairs={{0,8},{4,12},{8,0},{12,4},{1,9},{5,13},{9,1},{13,5},{2,10},{6,14},... | collective-permute-start | bytes 1572872 | tf_op jit(solution)/shard_map/while/body/ppermute | solution.py:15
  87.3 13.4 %collective-permute-start.1 = (f32[1,512]{1,0:T(1,128)S(1)}, f32[1,512]{1,0:T(1,128)S(1)}, u32[]{:S(2)}, u32[]{:S(2)}) collective-permute-start(f32[1,512]{1,0:T(1,128)S(1)} %copy.36), channel_id=1, source_target_pairs={{0,8},{4,12},{8,0},{12,4},{1,9},{5,13},{9,1},{13,5},{2,10},{6,14},... | collective-permute-start | bytes 6152 | tf_op jit(solution)/shard_map/while/body/ppermute | solution.py:15
  101.1 2.9 %collective-permute-start.2 = (bf16[2048,256]{1,0:T(8,128)(2,1)S(1)}, bf16[2048,256]{1,0:T(8,128)(2,1)}, u32[]{:S(2)}, u32[]{:S(2)}) collective-permute-start(bf16[2048,256]{1,0:T(8,128)(2,1)S(1)} %pad_maximum_fusion.22), channel_id=1, source_target_pairs={{0,4},{4,0},{8,12},{12,8},{1,5},{5,1},{9,13},{13,9},{2,6},{6,2},{1... | collective-permute-start | bytes 3145736 | tf_op jit(solution)/shard_map/while/body/ppermute | solution.py:15
  113.6 16.4 %copy-start.13 = (f32[1,512]{1,0:T(1,128)S(1)}, f32[1,512]{1,0:T(1,128)}, u32[]{:S(2)}) copy-start(f32[1,512]{1,0:T(1,128)} %get-tuple-element.536) | copy-start | bytes 6148
  113.6 16.4 %copy-start.14 = (f32[1,128]{1,0:T(1,128)S(1)}, f32[1,128]{1,0:T(1,128)}, u32[]{:S(2)}) copy-start(f32[1,128]{1,0:T(1,128)} %param.16) | copy-start | bytes 1540
  115.6 49.6 %collective-permute-start.19 = (bf16[1920,128]{0,1:T(8,128)(2,1)}, bf16[1920,128]{0,1:T(8,128)(2,1)}, u32[]{:S(2)}, u32[]{:S(2)}) collective-permute-start(bf16[1920,128]{0,1:T(8,128)(2,1)} %get-tuple-element.529), channel_id=1, source_target_pairs={{0,2},{1,3},{2,0},{3,1},{4,6},{5,7},{6,4},{7,5},{8,10},{9,11},{10,... | collective-permute-start | bytes 1474568 | tf_op jit(solution)/shard_map/ppermute | solution.py:15
  124.1 41.2 %collective-permute-start.20 = (bf16[1920,128]{0,1:T(8,128)(2,1)}, bf16[1920,128]{0,1:T(8,128)(2,1)}, u32[]{:S(2)}, u32[]{:S(2)}) collective-permute-start(bf16[1920,128]{0,1:T(8,128)(2,1)} %get-tuple-element.530), channel_id=1, source_target_pairs={{0,3},{1,2},{2,1},{3,0},{4,7},{5,6},{6,5},{7,4},{8,11},{9,10},{10,... | collective-permute-start | bytes 1474568 | tf_op jit(solution)/shard_map/ppermute | solution.py:15
  127.5 37.8 %collective-permute-start.21 = (bf16[1920,128]{0,1:T(8,128)(2,1)}, bf16[1920,128]{0,1:T(8,128)(2,1)}, u32[]{:S(2)}, u32[]{:S(2)}) collective-permute-start(bf16[1920,128]{0,1:T(8,128)(2,1)} %get-tuple-element.531), channel_id=1, source_target_pairs={{0,1},{1,0},{2,3},{3,2},{4,5},{5,4},{6,7},{7,6},{8,9},{9,8},{10,11... | collective-permute-start | bytes 1474568 | tf_op jit(solution)/shard_map/ppermute | solution.py:15
  130.0 35.2 %copy-start.1 = (f32[1920,128]{0,1:T(8,128)S(1)}, f32[1920,128]{0,1:T(8,128)}, u32[]{:S(2)}) copy-start(f32[1920,128]{0,1:T(8,128)} %get-tuple-element.539) | copy-start | bytes 2949124
  130.1 12.7 %collective-permute-start.3 = (bf16[1920,128]{1,0:T(8,128)(2,1)S(1)}, bf16[1920,128]{1,0:T(8,128)(2,1)S(1)}, u32[]{:S(2)}, u32[]{:S(2)}) collective-permute-start(bf16[1920,128]{1,0:T(8,128)(2,1)S(1)} %copy.55), channel_id=1, source_target_pairs={{0,8},{4,12},{8,0},{12,4},{1,9},{5,13},{9,1},{13,5},{2,10},{6,14},... | collective-permute-start | bytes 1474568 | tf_op jit(solution)/shard_map/while/body/ppermute | solution.py:15
  131.3 12.4 %collective-permute-start.4 = (bf16[1920,128]{1,0:T(8,128)(2,1)S(1)}, bf16[1920,128]{1,0:T(8,128)(2,1)S(1)}, u32[]{:S(2)}, u32[]{:S(2)}) collective-permute-start(bf16[1920,128]{1,0:T(8,128)(2,1)S(1)} %copy.55), channel_id=1, source_target_pairs={{0,16},{16,0},{1,17},{17,1},{2,18},{18,2},{3,19},{19,3},{4,20},{20... | collective-permute-start | bytes 1474568 | tf_op jit(solution)/shard_map/while/body/ppermute | solution.py:15
  143.8 13.7 %collective-permute-start.6 = (bf16[1920,256]{1,0:T(8,128)(2,1)S(1)}, bf16[1920,256]{1,0:T(8,128)(2,1)}, u32[]{:S(2)}, u32[]{:S(2)}) collective-permute-start(bf16[1920,256]{1,0:T(8,128)(2,1)S(1)} %pad_maximum_fusion.23), channel_id=1, source_target_pairs={{0,4},{4,0},{8,12},{12,8},{1,5},{5,1},{9,13},{13,9},{2,6},{6,2},{1... | collective-permute-start | bytes 2949128 | tf_op jit(solution)/shard_map/while/body/ppermute | solution.py:15
  143.9 13.6 %collective-permute-start.5 = (bf16[1920,128]{1,0:T(8,128)(2,1)S(1)}, bf16[1920,128]{1,0:T(8,128)(2,1)S(1)}, u32[]{:S(2)}, u32[]{:S(2)}) collective-permute-start(bf16[1920,128]{1,0:T(8,128)(2,1)S(1)} %collective-permute-done.4), channel_id=1, source_target_pairs={{0,8},{4,12},{8,0},{12,4},{1,9},{5,13},{9,1},{13,5},{2,10},{6,14},... | collective-permute-start | bytes 1474568 | tf_op jit(solution)/shard_map/while/body/ppermute | solution.py:15
  144.9 12.9 %copy-start.8 = (bf16[576,1920]{1,0:T(8,128)(2,1)S(1)}, bf16[576,1920]{1,0:T(8,128)(2,1)}, u32[]{:S(2)}) copy-start(bf16[576,1920]{1,0:T(8,128)(2,1)} %get-tuple-element.955) | copy-start | bytes 6635524 | tf_op jit(solution)/shard_map/while
  157.7 4.7 %collective-permute-start.7 = (bf16[1920,256]{1,0:T(8,128)(2,1)S(1)}, bf16[1920,256]{1,0:T(8,128)(2,1)S(1)}, u32[]{:S(2)}, u32[]{:S(2)}) collective-permute-start(bf16[1920,256]{1,0:T(8,128)(2,1)S(1)} %pad_maximum_fusion.24), channel_id=1, source_target_pairs={{0,4},{4,0},{8,12},{12,8},{1,5},{5,1},{9,13},{13,9},{2,6},{6,2},{1... | collective-permute-start | bytes 2949128 | tf_op jit(solution)/shard_map/while/body/ppermute | solution.py:15
  165.2 4.1 %copy-start.10 = (bf16[12,48,256]{2,1,0:T(8,128)(2,1)S(1)}, bf16[12,48,256]{2,1,0:T(8,128)(2,1)}, u32[]{:S(2)}) copy-start(bf16[12,48,256]{2,1,0:T(8,128)(2,1)} %get-tuple-element.538) | copy-start | bytes 884740
  166.8 14.1 %collective-permute-start.23 = (bf16[1920,128]{0,1:T(8,128)(2,1)S(1)}, bf16[1920,128]{0,1:T(8,128)(2,1)S(1)}, u32[]{:S(2)}, u32[]{:S(2)}) collective-permute-start(bf16[1920,128]{0,1:T(8,128)(2,1)S(1)} %add_convert_fusion), channel_id=1, source_target_pairs={{0,8},{4,12},{8,0},{12,4},{1,9},{5,13},{9,1},{13,5},{2,10},{6,14},... | collective-permute-start | bytes 1474568 | tf_op jit(solution)/shard_map/ppermute | solution.py:15
  167.8 13.3 %collective-permute-start.24 = (bf16[1920,128]{0,1:T(8,128)(2,1)S(1)}, bf16[1920,128]{0,1:T(8,128)(2,1)S(1)}, u32[]{:S(2)}, u32[]{:S(2)}) collective-permute-start(bf16[1920,128]{0,1:T(8,128)(2,1)S(1)} %add_convert_fusion), channel_id=1, source_target_pairs={{0,16},{16,0},{1,17},{17,1},{2,18},{18,2},{3,19},{19,3},{4,20},{20... | collective-permute-start | bytes 1474568 | tf_op jit(solution)/shard_map/ppermute | solution.py:15
  169.4 11.6 %collective-permute-start.22 = (bf16[12,48,256]{2,1,0:T(8,128)(2,1)S(1)}, bf16[12,48,256]{2,1,0:T(8,128)(2,1)S(1)}, u32[]{:S(2)}, u32[]{:S(2)}) collective-permute-start(bf16[12,48,256]{2,1,0:T(8,128)(2,1)S(1)} %copy-done.10), channel_id=1, source_target_pairs={{0,1},{1,2},{2,3},{3,0},{4,5},{5,6},{6,7},{7,4},{8,9},{9,10},{10,1... | collective-permute-start | bytes 884744 | tf_op jit(solution)/shard_map/ppermute | solution.py:11
  175.3 12.1 %copy-start.9 = (bf16[576,1920]{1,0:T(8,128)(2,1)S(1)}, bf16[576,1920]{1,0:T(8,128)(2,1)}, u32[]{:S(2)}) copy-start(bf16[576,1920]{1,0:T(8,128)(2,1)} %get-tuple-element.978) | copy-start | bytes 6635524
  181.4 19.7 %collective-permute-start.27 = (bf16[1920,256]{0,1:T(8,128)(2,1)S(1)}, bf16[1920,256]{0,1:T(8,128)(2,1)S(1)}, u32[]{:S(2)}, u32[]{:S(2)}) collective-permute-start(bf16[1920,256]{0,1:T(8,128)(2,1)S(1)} %pad_maximum_fusion.8), channel_id=1, source_target_pairs={{0,4},{4,0},{8,12},{12,8},{1,5},{5,1},{9,13},{13,9},{2,6},{6,2},{1... | collective-permute-start | bytes 2949128 | tf_op jit(solution)/shard_map/ppermute | solution.py:15
  181.7 19.4 %collective-permute-start.26 = (bf16[1920,128]{0,1:T(8,128)(2,1)S(1)}, bf16[1920,128]{0,1:T(8,128)(2,1)S(1)}, u32[]{:S(2)}, u32[]{:S(2)}) collective-permute-start(bf16[1920,128]{0,1:T(8,128)(2,1)S(1)} %collective-permute-done.23), channel_id=1, source_target_pairs={{0,16},{16,0},{1,17},{17,1},{2,18},{18,2},{3,19},{19,3},{4,20},{20... | collective-permute-start | bytes 1474568 | tf_op jit(solution)/shard_map/ppermute | solution.py:15
  183.2 17.8 %collective-permute-start.25 = (bf16[12,48,256]{2,1,0:T(8,128)(2,1)S(1)}, bf16[12,48,256]{2,1,0:T(8,128)(2,1)S(1)}, u32[]{:S(2)}, u32[]{:S(2)}) collective-permute-start(bf16[12,48,256]{2,1,0:T(8,128)(2,1)S(1)} %broadcast_select_fusion.15), channel_id=1, source_target_pairs={{0,2},{1,3},{2,0},{3,1},{4,6},{5,7},{6,4},{7,5},{8,10},{9,11},{10,... | collective-permute-start | bytes 884744 | tf_op jit(solution)/shard_map/ppermute | solution.py:11
  202.2 4.9 %copy-start.7 = (bf16[576,1920]{1,0:T(8,128)(2,1)S(1)}, bf16[576,1920]{1,0:T(8,128)(2,1)}, u32[]{:S(2)}) copy-start(bf16[576,1920]{1,0:T(8,128)(2,1)} %get-tuple-element.977) | copy-start | bytes 6635524
  202.5 7.9 %collective-permute-start.28 = (bf16[1920,256]{0,1:T(8,128)(2,1)S(1)}, bf16[1920,256]{0,1:T(8,128)(2,1)}, u32[]{:S(2)}, u32[]{:S(2)}) collective-permute-start(bf16[1920,256]{0,1:T(8,128)(2,1)S(1)} %pad_maximum_fusion.9), channel_id=1, source_target_pairs={{0,4},{4,0},{8,12},{12,8},{1,5},{5,1},{9,13},{13,9},{2,6},{6,2},{1... | collective-permute-start | bytes 2949128 | tf_op jit(solution)/shard_map/ppermute | solution.py:15
  213.2 11.5 %collective-permute-start.32 = (bf16[12,48,256]{2,1,0:T(8,128)(2,1)S(1)}, bf16[12,48,256]{2,1,0:T(8,128)(2,1)S(1)}, u32[]{:S(2)}, u32[]{:S(2)}) collective-permute-start(bf16[12,48,256]{2,1,0:T(8,128)(2,1)S(1)} %pad_maximum_fusion.15), channel_id=1, source_target_pairs={{0,1},{1,2},{2,3},{3,0},{4,5},{5,6},{6,7},{7,4},{8,9},{9,10},{10,1... | collective-permute-start | bytes 884744 | tf_op jit(solution)/shard_map/ppermute | solution.py:11
  214.1 1.9 collective-permute-start.29
  214.3 5.6 %collective-permute-start.30 = (bf16[4,48,2,1,128]{4,2,1,0,3:T(2,128)(2,1)S(1)}, bf16[4,48,2,1,128]{4,2,1,0,3:T(2,128)(2,1)S(1)}, u32[]{:S(2)}, u32[]{:S(2)}) collective-permute-start(bf16[4,48,2,1,128]{4,2,1,0,3:T(2,128)(2,1)S(1)} %copy-done.11), channel_id=1, source_target_pairs={{0,8},{4,12},{8,0},{12,4},{1,9},{5,13},{9,1},{13,5},{2,10},{6,14},... | collective-permute-start | bytes 294920 | tf_op jit(solution)/shard_map/ppermute | solution.py:15
  215.1 5.6 %collective-permute-start.31 = (bf16[4,48,2,1,128]{4,2,1,0,3:T(2,128)(2,1)S(1)}, bf16[4,48,2,1,128]{4,2,1,0,3:T(2,128)(2,1)S(1)}, u32[]{:S(2)}, u32[]{:S(2)}) collective-permute-start(bf16[4,48,2,1,128]{4,2,1,0,3:T(2,128)(2,1)S(1)} %squeeze.29), channel_id=1, source_target_pairs={{0,12},{4,8},{8,4},{12,0},{1,13},{5,9},{9,5},{13,1},{2,14},{6,10},... | collective-permute-start | bytes 294920 | tf_op jit(solution)/shard_map/ppermute | solution.py:15
  224.8 14.8 %collective-permute-start.33 = (bf16[12,48,256]{2,1,0:T(8,128)(2,1)S(1)}, bf16[12,48,256]{2,1,0:T(8,128)(2,1)S(1)}, u32[]{:S(2)}, u32[]{:S(2)}) collective-permute-start(bf16[12,48,256]{2,1,0:T(8,128)(2,1)S(1)} %broadcast_select_fusion.14), channel_id=1, source_target_pairs={{0,2},{1,3},{2,0},{3,1},{4,6},{5,7},{6,4},{7,5},{8,10},{9,11},{10,... | collective-permute-start | bytes 884744 | tf_op jit(solution)/shard_map/ppermute | solution.py:11
  240.4 2.4 collective-permute-start.34
  240.6 5.7 %collective-permute-start.35 = (bf16[4,48,2,1,128]{4,2,1,0,3:T(2,128)(2,1)S(1)}, bf16[4,48,2,1,128]{4,2,1,0,3:T(2,128)(2,1)S(1)}, u32[]{:S(2)}, u32[]{:S(2)}) collective-permute-start(bf16[4,48,2,1,128]{4,2,1,0,3:T(2,128)(2,1)S(1)} %squeeze.32), channel_id=1, source_target_pairs={{0,8},{4,12},{8,0},{12,4},{1,9},{5,13},{9,1},{13,5},{2,10},{6,14},... | collective-permute-start | bytes 294920 | tf_op jit(solution)/shard_map/ppermute | solution.py:15
  241.2 6.4 %collective-permute-start.36 = (bf16[4,48,2,1,128]{4,2,1,0,3:T(2,128)(2,1)S(1)}, bf16[4,48,2,1,128]{4,2,1,0,3:T(2,128)(2,1)S(1)}, u32[]{:S(2)}, u32[]{:S(2)}) collective-permute-start(bf16[4,48,2,1,128]{4,2,1,0,3:T(2,128)(2,1)S(1)} %squeeze.33), channel_id=1, source_target_pairs={{0,12},{4,8},{8,4},{12,0},{1,13},{5,9},{9,5},{13,1},{2,14},{6,10},... | collective-permute-start | bytes 294920 | tf_op jit(solution)/shard_map/ppermute | solution.py:15
  (8 other events, 18.1 us)

commit v9 on v8

--- a/solution.py
+++ b/solution.py
@@ -97,9 +97,9 @@
     def outer_core(h):
         return (h ^ h // 2) % 2
 
-    def times_features(rows, r):
-        columns = lax.dynamic_slice_in_dim(feature_rows, (tile ^ r) * depth, depth, axis=1)
-        return add_columns(columns, rows)
+    feature_parts = [
+        lax.dynamic_slice_in_dim(feature_rows, (tile ^ r) * depth, depth, axis=1) for r in range(4)
+    ]
 
     def put_first(condition, one, other, axis):
         return jnp.concatenate(
@@ -131,10 +131,11 @@
 
     once = jnp.minimum(jnp.max(tile_count), 1)
 
-    def in_loop(chain, given):
-        shapes = jax.eval_shape(chain, given)[1]
-        empty = jax.tree.map(lambda x: jnp.zeros(x.shape, x.dtype), shapes)
+    def in_loop(chain, given, empty):
         return lax.fori_loop(0, once, lambda _, carry: chain(carry[0]), (given, empty))[1]
+
+    def times_features(rows, parts):
+        return sum(add_columns(parts[r], rows[r]) for r in range(4))
 
     def finish(total, part):
         finished = []
@@ -171,43 +172,52 @@
         return jnp.stack(ranked, axis=1)
 
     column, half = group * 2 * head_dim, kv_weight.shape[0] // 2
-
-    def to_planes(part):
-        mine = lax.dynamic_slice_in_dim(kv_weight, column + part * head_dim, head_dim, axis=1)
-        return (
-            moved(mine[:half], lambda t, h: (h // 2 * 2 + outer_core(h), t)),
-            moved(mine[half:], lambda t, h: ((1 - h // 2) * 2 + outer_core(h), t)),
-        )
-
-    def across(rows):
-        return swapped(jnp.concatenate(rows, axis=0), "tile", 2)
-
-    def with_other(rows, other):
-        one = jnp.concatenate([rows[0], other[half:]], axis=0)
-        two = jnp.concatenate([other[:half], rows[1]], axis=0)
-        return put_first(tile // 2 == head // 2, one, two, 1)
-
+    key_mine = lax.dynamic_slice_in_dim(kv_weight, column, head_dim, axis=1)
+    value_mine = lax.dynamic_slice_in_dim(kv_weight, column + head_dim, head_dim, axis=1)
+    stays = lax.dynamic_slice_in_dim(value_mine, tile // 2 * half, half, axis=0)
+    leaves = lax.dynamic_slice_in_dim(value_mine, half - tile // 2 * half, half, axis=0)
     bias_rows = moved(proj_bias, lambda t, h: (h, t))
-    bias_rows, key_rows = step((bias_rows, to_planes(0)))
-
+    key_block = moved(key_mine, lambda t, h: (h // 2 * 2 + outer_core(h), t))
+    comes = swapped(leaves, "tile", 2)
+    no_block = jnp.zeros((depth, width), jnp.float32)
+    no_terms = no_block, tuple(jnp.zeros((depth, width), jnp.bfloat16) for _ in range(3))
+    no_tokens = tuple(
+        jnp.zeros((tile_slots, shard_len, 2 * width), jnp.bfloat16) for _ in range(2)
+    )
+    bias_rows, key_block, comes, stays, feature_parts, no_terms, no_tokens, once = step(
+        (bias_rows, key_block, comes, stays, feature_parts, no_terms, no_tokens, once)
+    )
+
+    value_pieces = []
+    for j in range(2):
+        piece = jnp.where(tile // 2 == (head // 2) ^ j, stays, comes)
+        value_pieces.append(
+            moved(piece, lambda t, h: (t // 2 * 2 + outer_core(h), t % 2 + 2 * ((h // 2) ^ j)))
+        )
+    key_other = swapped(key_block, "tile", 2)
     bias_part = add_columns(bias_rows[None], kv_weight)
-    value_rows, key_rows, key_other, bias_part = step(
-        (to_planes(1), key_rows, across(key_rows), bias_part)
-    )
-
-    key_near = step(with_other(key_rows, key_other))
+    value_pieces, key_block, key_other, bias_part = step(
+        (value_pieces, key_block, key_other, bias_part)
+    )
+
+    key_near = put_first(tile // 2 == head // 2, key_block, key_other, 1)
+    value_half = jnp.concatenate(value_pieces, axis=1)
+    key_near, value_half = step((key_near, value_half))
     own, parts = products(key_near, swapped(key_near, "tile", 1))
     bias_part = bias_part + swapped(bias_part, "tile", 1)
-    own, parts, value_rows, bias_part = step((own, parts, value_rows, bias_part))
-
-    def values_product(given):
-        rows, bias = given
-        other, bias_other = step((across(rows), swapped(bias, "tile", 2)))
-        near = step(with_other(rows, other))
-        given = (other[:half], other[half:]), bias_other
-        return given, (products(near, swapped(near, "tile", 1)), bias + bias_other)
-
-    arrived, beside = step((exchange(parts), in_loop(values_product, (value_rows, bias_part))))
+    own, parts, value_half, bias_part = step((own, parts, value_half, bias_part))
+
+    def values_terms(given):
+        value_half, bias_part = given
+        other, bias_other = step((swapped(value_half, "tile", 2), swapped(bias_part, "tile", 2)))
+        near = step(put_first(first_chip, value_half, other, 0))
+        terms = products(near, swapped(near, "tile", 1))
+        return (other, bias_other), (terms, bias_part + bias_other)
+
+    empty = no_terms, bias_part
+    arrived, beside = step(
+        (exchange(parts), in_loop(values_terms, (value_half, bias_part), empty))
+    )
     own = summed(own, arrived)
     (value_own, parts), bias_part = beside
     bias_part = bias_part.reshape(2, layers, 2, head_dim)
@@ -217,39 +227,44 @@
         rows_0 = step(both_heads(own, across_y))
         diagonal, rows_1 = step((swapped(across_y, "tile", 2), swapped(rows_0, "tile", 1)))
         rows_2 = step(both_heads(across_x, diagonal))
-        total = times_features(rows_0, 0) + times_features(rows_1, 1)
-        total = total + times_features(rows_2, 2) + times_features(swapped(rows_2, "tile", 1), 3)
-        return across_x, finish(total, 0)
-
-    arrived, keys = step((exchange(parts), in_loop(keys_product, own)))
+        rows = [rows_0, rows_1, rows_2, swapped(rows_2, "tile", 1)]
+        return across_x, finish(times_features(rows, feature_parts), 0)
+
+    arrived, keys = step((exchange(parts), in_loop(keys_product, own, no_tokens[0])))
     own = summed(value_own, arrived)
 
     shifted, across_x, across_y = step(
         (shifted_2(keys, "head", 1), swapped(own, "tile", 2), swapped(own, "groups", 1))
     )
 
-    rows_0, keys = step((both_heads(own, across_y), rolled(keys, shifted, 1)))
-    shifted, diagonal, rows_1 = step(
-        (
-            shifted_2(keys, "head", 2),
-            swapped(across_x, "groups", 1),
-            swapped(rows_0, "tile", 1),
-        )
-    )
-
-    rows_2, keys = step((both_heads(across_x, diagonal), rolled(keys, shifted, 2)))
-    total = times_features(rows_0, 0) + times_features(rows_1, 1)
-    total = total + times_features(rows_2, 2) + times_features(swapped(rows_2, "tile", 1), 3)
-    values = finish(total, 1)
-    picked, values = step((outgoing(keys), values))
-
-    arrived, shifted = step((to_owners(picked), shifted_2(values, "head", 1)))
+    def values_product(given):
+        own, across_x, across_y = given
+        rows_0 = step(both_heads(own, across_y))
+        middle = depth // 2
+        upper, lower, rows_1 = step(
+            (
+                swapped(across_x[:middle], "groups", 1),
+                swapped(across_y[middle:], "tile", 2),
+                swapped(rows_0, "tile", 1),
+            )
+        )
+        rows_2 = step(both_heads(across_x, jnp.concatenate([upper, lower], axis=0)))
+        rows = [rows_0, rows_1, rows_2, swapped(rows_2, "tile", 1)]
+        total = times_features(rows, feature_parts)
+        return (across_y, own, across_x), finish(total, 1)
+
+    keys = step(rolled(keys, shifted, 1))
+    values = in_loop(values_product, (own, across_x, across_y), no_tokens[1])
+    shifted, values = step((shifted_2(keys, "head", 2), values))
+
+    picked = outgoing(rolled(keys, shifted, 2))
+    shifted, picked = step((shifted_2(values, "head", 1), picked))
 
     values = step(rolled(values, shifted, 1))
-    key_cache, shifted = step((in_order(arrived), shifted_2(values, "head", 2)))
+    arrived, shifted = step((to_owners(picked), shifted_2(values, "head", 2)))
 
     value_cache = in_order(to_owners(outgoing(rolled(values, shifted, 2))))
-    cache = jnp.stack([key_cache, value_cache], axis=-2)
+    cache = jnp.stack([in_order(arrived), value_cache], axis=-2)
     return cache.reshape(1, 1, most_tiles * 4 * shard_len, 4 * layers, head_dim)
 
 

time: 252 us -> 234 us (0.929)
  waiting for transfers between devices: 115 us -> 93.8 us
  other arithmetic: 15.3 us -> 19.8 us
  local copies, waits for them, and re-layouts: 26.5 us -> 29.4 us
  starting transfers between devices: 67.1 us -> 64.2 us
    ppermute x5 -> x4, waiting for transfers between devices: 30.8 us -> 9.02 us  [moved(): return lax.ppermute(shard, ('tile', 'head'), pairs)]
    ppermute x28 -> x30, waiting for transfers between devices: 48.9 us -> 63 us  [swapped(): lax.ppermute(shard, axis, [(i, i ^ bit) for i in range(lax.axis_size(axis...]
    ppermute x4, waiting for transfers between devices: 35.3 us -> 21.8 us  [shifted_2(): lax.ppermute(shard, axis, [(i, (i + by) % count) for i in range(count)])]
    ppermute x5 -> x4, starting transfers between devices: 10.8 us -> 4.12 us  [moved(): return lax.ppermute(shard, ('tile', 'head'), pairs)]
    ppermute x28 -> x30, starting transfers between devices: 45.4 us -> 51.2 us  [swapped(): lax.ppermute(shard, axis, [(i, i ^ bit) for i in range(lax.axis_size(axis...]
    dynamic_slice x1 -> x3, local copies, waits for them, and re-layouts: 7.24 us -> 10.6 us  [the longest x1 7.31 us: product_plan(): lax.dynamic_slice_in_dim(feature_rows, (tile ^ r) * depth, depth, axis=1)]
    optimization_barrier x1 -> x5, local copies, waits for them, and re-layouts: 0.01 us -> 3.33 us  [the longest x4 3.32 us: product_plan(): step((exchange(parts), in_loop(values_terms, (value_half, bias_part), emp...]
    squeeze x8, local copies, waits for them, and re-layouts: 3.99 us -> 0.94 us  [outgoing(): return [picked[r] for r in range(4)]]
  transfers between devices with their start and end apart: 37 -> 38, of which waited for: 18 -> 20; matrix products, arithmetic and copies ran while one was open for 17% -> 19% of each run, Pallas kernels for 0% -> 0%
where the time goes in v9:
time: 234 us; the launch traced here: 233 us
  waiting for transfers between devices  93.8 us (40%)
  starting transfers between devices  64.2 us (27%)
  local copies, waits for them, and re-layouts  29.4 us (13%)
  matrix products  24.3 us (10%)
  other arithmetic  19.8 us (8%)
    ppermute x30, waiting for transfers between devices, swapped(): lax.ppermute(shard, axis, [(i, i ^ bit) for i in range(lax.axis_size(axis...  63 us
    ppermute x30, starting transfers between devices, swapped(): lax.ppermute(shard, axis, [(i, i ^ bit) for i in range(lax.axis_size(axis...  51.2 us
    dot_general x13, matrix products, add_columns(): return jnp.dot(operand, portion, preferred_element_type=jnp.float32)  24.1 us
    ppermute x4, waiting for transfers between devices, shifted_2(): lax.ppermute(shard, axis, [(i, (i + by) % count) for i in range(count)])  21.8 us
    ppermute x4, waiting for transfers between devices, moved(): return lax.ppermute(shard, ('tile', 'head'), pairs)  9.02 us
    ppermute x4, starting transfers between devices, shifted_2(): lax.ppermute(shard, axis, [(i, (i + by) % count) for i in range(count)])  8.88 us
    dynamic_slice x1, local copies, waits for them, and re-layouts, product_plan(): lax.dynamic_slice_in_dim(feature_rows, (tile ^ r) * depth, depth, axis=1)  7.31 us
  transfers between devices with their start and end apart: 38, of which 20 were waited for; matrix products, arithmetic and copies ran while one was open for 19% of the time, Pallas kernels for 0%

profile of v9, /device:TPU:0, one launch (start us, length us, event | category | flops | bytes accessed | tf_op | source)
XLA Modules:
  0.0 233.2 jit_solution(4388378158817439560)
XLA Ops:
  1.8 2.3 fusion.31
  4.1 6.7 %collective-permute-start.14 = (bf16[1024,128]{1,0:T(8,128)(2,1)}, bf16[1024,128]{1,0:T(8,128)(2,1)}, u32[]{:S(2)}, u32[]{:S(2)}) collective-permute-start(bf16[1024,128]{1,0:T(8,128)(2,1)} %get-tuple-element.662), channel_id=1, source_target_pairs={{0,8},{4,12},{8,0},{12,4},{1,9},{5,13},{9,1},{13,5},{2,10},{6,14},... | collective-permute-start | bytes 786440 | tf_op jit(solution)/shard_map/ppermute | solution.py:15
  10.8 1.3 collective-permute-start.12
  12.1 7.3 %constant_dynamic-slice_fusion = (bf16[576,1920]{1,0:T(8,128)(2,1)}, bf16[576,1920]{1,0:T(8,128)(2,1)}, bf16[576,1920]{1,0:T(8,128)(2,1)}, bf16[576,1920]{1,0:T(8,128)(2,1)}) fusion(bf16[576,7680]{1,0:T(8,128)(2,1)} %bitcast.143, s32[]{:T(128)S(6)} %select_n.356, s32[]{:T(128)S(6)} %select_n.355, s32[]{:T(128)S(6)} %select_n.354, s32[]{:T(128)S(6)} %select_n.353), kind=kLoop, calls=%fused_computation.117 | loop fusion | bytes 17694736 | tf_op jit(solution)/shard_map/dynamic_slice | solution.py:101
  20.7 2.4 %collective-permute-done.14 = bf16[1024,128]{1,0:T(8,128)(2,1)} collective-permute-done((bf16[1024,128]{1,0:T(8,128)(2,1)}, bf16[1024,128]{1,0:T(8,128)(2,1)}, u32[]{:S(2)}, u32[]{:S(2)}) %collective-permute-start.14) | collective-permute-done | bytes 262176 | tf_op jit(solution)/shard_map/ppermute | solution.py:15
  23.1 9.8 %collective-permute-start.17 = (bf16[2048,128]{1,0:T(8,128)(2,1)S(1)}, bf16[2048,128]{1,0:T(8,128)(2,1)S(1)}, u32[]{:S(2)}, u32[]{:S(2)}) collective-permute-start(bf16[2048,128]{1,0:T(8,128)(2,1)S(1)} %collective-permute-done.13), channel_id=1, source_target_pairs={{0,8},{4,12},{8,0},{12,4},{1,9},{5,13},{9,1},{13,5},{2,10},{6,14},... | collective-permute-start | bytes 1572872 | tf_op jit(solution)/shard_map/ppermute | solution.py:15
  34.6 1.4 collective-permute-start.16
  36.4 9.0 %collective-permute-done.16 = bf16[1024,128]{1,0:T(8,128)(2,1)S(1)} collective-permute-done((bf16[1024,128]{1,0:T(8,128)(2,1)S(1)}, bf16[1024,128]{1,0:T(8,128)(2,1)S(1)}, u32[]{:S(2)}, u32[]{:S(2)}) %collective-permute-start.16) | collective-permute-done | bytes 262176 | tf_op jit(solution)/shard_map/ppermute | solution.py:95
  45.7 4.2 %collective-permute-start.18 = (bf16[2048,256]{1,0:T(8,128)(2,1)S(1)}, bf16[2048,256]{1,0:T(8,128)(2,1)S(1)}, u32[]{:S(2)}, u32[]{:S(2)}) collective-permute-start(bf16[2048,256]{1,0:T(8,128)(2,1)S(1)} %pad_maximum_fusion.7), channel_id=1, source_target_pairs={{0,4},{4,0},{8,12},{12,8},{1,5},{5,1},{9,13},{13,9},{2,6},{6,2},{1... | collective-permute-start | bytes 3145736 | tf_op jit(solution)/shard_map/ppermute | solution.py:15
  54.0 7.1 %convolution_bitcast_fusion.1 = f32[1920,512]{0,1:T(8,128)S(1)} fusion(bf16[1920,2048]{1,0:T(8,128)(2,1)} %param.15, bf16[2048,256]{1,0:T(8,128)(2,1)S(1)} %collective-permute-done.18, bf16[2048,256]{1,0:T(8,128)(2,1)S(1)} %pad_maximum_fusion.7), kind=kOutput, calls=%fused_computation.54 | convolution fusion | flops 4030726144 | bytes 13893632 | tf_op jit(solution)/shard_map/dot_general | solution.py:19
  62.9 1.5 collective-permute-start.20
  65.2 1.2 collective-permute-start.22
  67.5 26.0 %while.56 = (s32[]{:T(128)}, bf16[1024,256]{1,0:T(8,128)(2,1)S(1)}, f32[1,512]{1,0:T(1,128)S(1)}, f32[1920,128]{0,1:T(8,128)}, bf16[1920,128]{0,1:T(8,128)(2,1)}...) while((s32[]{:T(128)}, bf16[1024,256]{1,0:T(8,128)(2,1)S(1)}, ...), condition=%wide.region_3.4_spmd, body=%wide.region_2.3_spmd.sunk | while | flops 4034331136 | bytes 31836404 | solution.py:135
  67.5 1.8 collective-permute-start
  69.6 11.2 %collective-permute-done.1 = f32[1,512]{1,0:T(1,128)S(1)} collective-permute-done((f32[1,512]{1,0:T(1,128)S(1)}, f32[1,512]{1,0:T(1,128)S(1)}, u32[]{:S(2)}, u32[]{:S(2)}) %collective-permute-start.1) | collective-permute-done | bytes 2080 | tf_op jit(solution)/shard_map/while/body/ppermute | solution.py:15
  81.6 2.2 collective-permute-done.2
  83.8 7.4 %convolution_bitcast_fusion.3 = f32[1920,512]{0,1:T(8,128)S(1)} fusion(bf16[1920,2048]{1,0:T(8,128)(2,1)} %get-tuple-element.998, bf16[2048,256]{1,0:T(8,128)(2,1)} %collective-permute-done.2, bf16[2048,256]{1,0:T(8,128)(2,1)S(1)} %pad_maximum_fusion.17), kind=kOutput, calls=%fused_computation.clone.1 | convolution fusion | flops 4030726144 | bytes 13893632 | tf_op jit(solution)/shard_map/while/body/dot_general | solution.py:19
  91.1 1.2 select_convert_fusion.7
  93.5 4.5 %collective-permute-done.20 = bf16[1920,128]{0,1:T(8,128)(2,1)S(1)} collective-permute-done((bf16[1920,128]{0,1:T(8,128)(2,1)}, bf16[1920,128]{0,1:T(8,128)(2,1)S(1)}, u32[]{:S(2)}, u32[]{:S(2)}) %collective-permute-start.20) | collective-permute-done | bytes 491552 | tf_op jit(solution)/shard_map/ppermute | solution.py:15
  99.2 2.4 %add_convert_fusion.1 = bf16[1920,128]{0,1:T(8,128)(2,1)} fusion(bf16[1920,128]{0,1:T(8,128)(2,1)} %collective-permute-done.22, bf16[1920,128]{0,1:T(8,128)(2,1)} %collective-permute-done.21, f32[1920,128]{0,1:T(8,128)S(1)} %slice_select_fusion.1, bf16[1920,128]{0,1:T(8,128)(2,1)} %copy-done.17), kind=kLoop, calls=%fused_computation.61 | loop fusion | flops 1720320 | bytes 2949120 | tf_op jit(solution)/shard_map/convert_element_type | solution.py:130
  101.6 1.4 copy.23
  104.0 10.7 %collective-permute-start.23 = (bf16[1920,128]{1,0:T(8,128)(2,1)}, bf16[1920,128]{1,0:T(8,128)(2,1)}, u32[]{:S(2)}, u32[]{:S(2)}) collective-permute-start(bf16[1920,128]{1,0:T(8,128)(2,1)} %copy.20), channel_id=1, source_target_pairs={{0,2},{1,3},{2,0},{3,1},{4,6},{5,7},{6,4},{7,5},{8,10},{9,11},{10,... | collective-permute-start | bytes 1474568 | tf_op jit(solution)/shard_map/ppermute | solution.py:15
  115.7 1.6 collective-permute-start.24
  118.7 36.4 %while.57 = (s32[]{:T(128)}, bf16[1920,128]{1,0:T(8,128)(2,1)S(1)}, bf16[12,48,256]{2,1,0:T(8,128)(2,1)}, s32[]{:T(128)}, pred[]{:T(512)}, /*index=5*/bf16[576,1...) while((s32[]{:T(128)}, bf16[1920,128]{1,0:T(8,128)(2,1)S(1)}, ...), condition=%wide.region_7.8_spmd, body=%wide.region_4.7_spmd.sunk | while | flops 2271905024 | bytes 76995496 | solution.py:135
  118.9 2.2 collective-permute-start.3
  121.1 1.5 collective-permute-start.4
  122.7 9.3 %collective-permute-done.3 = bf16[1920,128]{1,0:T(8,128)(2,1)S(1)} collective-permute-done((bf16[1920,128]{1,0:T(8,128)(2,1)S(1)}, bf16[1920,128]{1,0:T(8,128)(2,1)S(1)}, u32[]{:S(2)}, u32[]{:S(2)}) %collective-permute-start.3) | collective-permute-done | bytes 491552 | tf_op jit(solution)/shard_map/while/body/ppermute | solution.py:15
  132.0 1.5 collective-permute-done.4
  134.2 13.2 %collective-permute-done.5 = bf16[1920,128]{1,0:T(8,128)(2,1)S(1)} collective-permute-done((bf16[1920,128]{1,0:T(8,128)(2,1)S(1)}, bf16[1920,128]{1,0:T(8,128)(2,1)S(1)}, u32[]{:S(2)}, u32[]{:S(2)}) %collective-permute-start.5) | collective-permute-done | bytes 491552 | tf_op jit(solution)/shard_map/while/body/ppermute | solution.py:15
  149.3 2.1 convolution_add_fusion.10
  155.1 1.6 add_convert_fusion
  157.2 1.5 collective-permute-start.28
  158.9 4.1 %collective-permute-start.26 = (bf16[12,48,256]{2,1,0:T(8,128)(2,1)S(1)}, bf16[12,48,256]{2,1,0:T(8,128)(2,1)S(1)}, u32[]{:S(2)}, u32[]{:S(2)}) collective-permute-start(bf16[12,48,256]{2,1,0:T(8,128)(2,1)S(1)} %copy-done.16), channel_id=1, source_target_pairs={{0,1},{1,2},{2,3},{3,0},{4,5},{5,6},{6,7},{7,4},{8,9},{9,10},{10,1... | collective-permute-start | bytes 884744 | tf_op jit(solution)/shard_map/ppermute | solution.py:11
  163.1 6.4 %collective-permute-done.26 = bf16[12,48,256]{2,1,0:T(8,128)(2,1)S(1)} collective-permute-done((bf16[12,48,256]{2,1,0:T(8,128)(2,1)S(1)}, bf16[12,48,256]{2,1,0:T(8,128)(2,1)S(1)}, u32[]{:S(2)}, u32[]{:S(2)}) %collective-permute-start.26) | collective-permute-done | bytes 294944 | tf_op jit(solution)/shard_map/ppermute | solution.py:11
  171.3 4.4 %collective-permute-start.29 = (bf16[12,48,256]{2,1,0:T(8,128)(2,1)}, bf16[12,48,256]{2,1,0:T(8,128)(2,1)}, u32[]{:S(2)}, u32[]{:S(2)}) collective-permute-start(bf16[12,48,256]{2,1,0:T(8,128)(2,1)} %broadcast_select_fusion.15), channel_id=1, source_target_pairs={{0,2},{1,3},{2,0},{3,1},{4,6},{5,7},{6,4},{7,5},{8,10},{9,11},{10,... | collective-permute-start | bytes 884744 | tf_op jit(solution)/shard_map/ppermute | solution.py:11
  175.8 19.0 %while.58 = (s32[]{:T(128)}, bf16[1920,128]{1,0:T(8,128)(2,1)S(1)}, bf16[1920,128]{1,0:T(8,128)(2,1)S(1)}, bf16[1920,128]{1,0:T(8,128)(2,1)S(1)}, bf16[12,48,256...) while((s32[]{:T(128)}, bf16[1920,128]{1,0:T(8,128)(2,1)S(1)}, ...), condition=%wide.region_9.10_spmd, body=%wide.region_8.9_spmd.sunk | while | flops 2271166464 | bytes 77368712 | solution.py:135
  177.8 1.5 collective-permute-start.8
  179.4 5.9 %collective-permute-done.9 = bf16[960,128]{1,0:T(8,128)(2,1)S(1)} collective-permute-done((bf16[960,128]{1,0:T(8,128)(2,1)}, bf16[960,128]{1,0:T(8,128)(2,1)S(1)}, u32[]{:S(2)}, u32[]{:S(2)}) %collective-permute-start.9) | collective-permute-done | bytes 245792 | tf_op jit(solution)/shard_map/while/body/ppermute | solution.py:15
  186.5 1.3 copy-done.13
  189.4 2.1 convolution_add_fusion.12
  197.3 9.3 %collective-permute-done.30 = bf16[12,48,256]{2,1,0:T(8,128)(2,1)S(1)} collective-permute-done((bf16[12,48,256]{2,1,0:T(8,128)(2,1)S(1)}, bf16[12,48,256]{2,1,0:T(8,128)(2,1)S(1)}, u32[]{:S(2)}, u32[]{:S(2)}) %collective-permute-start.30) | collective-permute-done | bytes 294944 | tf_op jit(solution)/shard_map/ppermute | solution.py:11
  206.9 1.7 collective-permute-start.32
  208.8 3.8 %collective-permute-done.32 = bf16[4,48,2,1,128]{4,2,1,0,3:T(2,128)(2,1)S(1)} collective-permute-done((bf16[4,48,2,1,128]{4,2,1,0,3:T(2,128)(2,1)S(1)}, bf16[4,48,2,1,128]{4,2,1,0,3:T(2,128)(2,1)S(1)}, u32[]{:S(2)}, u32[]{:S(2)}) %collective-permute-start.32) | collective-permute-done | bytes 98336 | tf_op jit(solution)/shard_map/ppermute | solution.py:15
  213.8 6.0 %collective-permute-done.34 = bf16[12,48,256]{2,1,0:T(8,128)(2,1)S(1)} collective-permute-done((bf16[12,48,256]{2,1,0:T(8,128)(2,1)S(1)}, bf16[12,48,256]{2,1,0:T(8,128)(2,1)S(1)}, u32[]{:S(2)}, u32[]{:S(2)}) %collective-permute-start.34) | collective-permute-done | bytes 294944 | tf_op jit(solution)/shard_map/ppermute | solution.py:11
  220.7 1.7 collective-permute-start.36
  222.9 3.3 %collective-permute-done.36 = bf16[4,48,2,1,128]{4,2,1,0,3:T(2,128)(2,1)S(1)} collective-permute-done((bf16[4,48,2,1,128]{4,2,1,0,3:T(2,128)(2,1)S(1)}, bf16[4,48,2,1,128]{4,2,1,0,3:T(2,128)(2,1)S(1)}, u32[]{:S(2)}, u32[]{:S(2)}) %collective-permute-start.36) | collective-permute-done | bytes 98336 | tf_op jit(solution)/shard_map/ppermute | solution.py:15
  226.3 1.5 collective-permute-done.37
  231.1 2.1 copy.29
  (185 shorter events, 44.7 us)
Async XLA Ops:
  1.1 22.1 %collective-permute-start.13 = (bf16[2048,128]{1,0:T(8,128)(2,1)S(1)}, bf16[2048,128]{1,0:T(8,128)(2,1)S(1)}, u32[]{:S(2)}, u32[]{:S(2)}) collective-permute-start(bf16[2048,128]{1,0:T(8,128)(2,1)S(1)} %constant_dynamic-slice_fusion.4), channel_id=1, source_target_pairs={{0,0},{1,4},{2,12},{3,8},{4,1},{5,5},{6,13},{7,9},{8,2},{9,6},{10,... | collective-permute-start | bytes 1572872 | tf_op jit(solution)/shard_map/ppermute | solution.py:95
  4.1 19.1 %collective-permute-start.14 = (bf16[1024,128]{1,0:T(8,128)(2,1)}, bf16[1024,128]{1,0:T(8,128)(2,1)}, u32[]{:S(2)}, u32[]{:S(2)}) collective-permute-start(bf16[1024,128]{1,0:T(8,128)(2,1)} %get-tuple-element.662), channel_id=1, source_target_pairs={{0,8},{4,12},{8,0},{12,4},{1,9},{5,13},{9,1},{13,5},{2,10},{6,14},... | collective-permute-start | bytes 786440 | tf_op jit(solution)/shard_map/ppermute | solution.py:15
  10.8 9.9 %collective-permute-start.12 = (bf16[2048]{0:T(1024)(128)(2,1)}, bf16[2048]{0:T(1024)(128)(2,1)S(1)}, u32[]{:S(2)}, u32[]{:S(2)}) collective-permute-start(bf16[2048]{0:T(1024)(128)(2,1)} %param.16), channel_id=1, source_target_pairs={{0,0},{1,4},{2,8},{3,12},{4,1},{5,5},{6,9},{7,13},{8,2},{9,6},{10,... | collective-permute-start | bytes 12296 | tf_op jit(solution)/shard_map/ppermute | solution.py:95
  12.1 23.9 %copy-start.2 = (bf16[2048,512]{1,0:T(8,128)(2,1)S(1)}, bf16[2048,512]{1,0:T(8,128)(2,1)}, u32[]{:S(2)}) copy-start(bf16[2048,512]{1,0:T(8,128)(2,1)} %param.17) | copy-start | bytes 6291460
  23.1 22.3 %collective-permute-start.17 = (bf16[2048,128]{1,0:T(8,128)(2,1)S(1)}, bf16[2048,128]{1,0:T(8,128)(2,1)S(1)}, u32[]{:S(2)}, u32[]{:S(2)}) collective-permute-start(bf16[2048,128]{1,0:T(8,128)(2,1)S(1)} %collective-permute-done.13), channel_id=1, source_target_pairs={{0,8},{4,12},{8,0},{12,4},{1,9},{5,13},{9,1},{13,5},{2,10},{6,14},... | collective-permute-start | bytes 1572872 | tf_op jit(solution)/shard_map/ppermute | solution.py:15
  33.9 2.5 %collective-permute-start.15 = (bf16[1024,128]{1,0:T(8,128)(2,1)S(1)}, bf16[1024,128]{1,0:T(8,128)(2,1)S(1)}, u32[]{:S(2)}, u32[]{:S(2)}) collective-permute-start(bf16[1024,128]{1,0:T(8,128)(2,1)S(1)} %get-tuple-element.666), channel_id=1, source_target_pairs={{0,0},{1,4},{2,6},{3,2},{4,1},{5,5},{6,7},{7,3},{8,8},{9,12},{10,1... | collective-permute-start | bytes 786440 | tf_op jit(solution)/shard_map/ppermute | solution.py:95
  34.6 10.8 %collective-permute-start.16 = (bf16[1024,128]{1,0:T(8,128)(2,1)S(1)}, bf16[1024,128]{1,0:T(8,128)(2,1)S(1)}, u32[]{:S(2)}, u32[]{:S(2)}) collective-permute-start(bf16[1024,128]{1,0:T(8,128)(2,1)S(1)} %get-tuple-element.665), channel_id=1, source_target_pairs={{0,2},{1,6},{2,4},{3,0},{4,3},{5,7},{6,5},{7,1},{8,10},{9,14},{10,... | collective-permute-start | bytes 786440 | tf_op jit(solution)/shard_map/ppermute | solution.py:95
  45.7 8.2 %collective-permute-start.18 = (bf16[2048,256]{1,0:T(8,128)(2,1)S(1)}, bf16[2048,256]{1,0:T(8,128)(2,1)S(1)}, u32[]{:S(2)}, u32[]{:S(2)}) collective-permute-start(bf16[2048,256]{1,0:T(8,128)(2,1)S(1)} %pad_maximum_fusion.7), channel_id=1, source_target_pairs={{0,4},{4,0},{8,12},{12,8},{1,5},{5,1},{9,13},{13,9},{2,6},{6,2},{1... | collective-permute-start | bytes 3145736 | tf_op jit(solution)/shard_map/ppermute | solution.py:15
  50.5 3.5 %collective-permute-start.19 = (f32[1,512]{1,0:T(1,128)S(1)}, f32[1,512]{1,0:T(1,128)S(1)}, u32[]{:S(2)}, u32[]{:S(2)}) collective-permute-start(f32[1,512]{1,0:T(1,128)S(1)} %fusion.36), channel_id=1, source_target_pairs={{0,4},{4,0},{8,12},{12,8},{1,5},{5,1},{9,13},{13,9},{2,6},{6,2},{1... | collective-permute-start | bytes 6152 | tf_op jit(solution)/shard_map/ppermute | solution.py:15
  51.5 9.5 %copy-start = (bf16[1920,128]{0,1:T(8,128)(2,1)}, bf16[1920,128]{0,1:T(8,128)(2,1)S(1)}, u32[]{:S(2)}) copy-start(bf16[1920,128]{0,1:T(8,128)(2,1)S(1)} %broadcast.226) | copy-start | bytes 1474564
  53.2 7.9 %copy-start.4 = (bf16[12,48,256]{2,1,0:T(8,128)(2,1)}, bf16[12,48,256]{2,1,0:T(8,128)(2,1)S(1)}, u32[]{:S(2)}) copy-start(bf16[12,48,256]{2,1,0:T(8,128)(2,1)S(1)} %broadcast.227) | copy-start | bytes 884740
  62.9 35.1 %collective-permute-start.20 = (bf16[1920,128]{0,1:T(8,128)(2,1)}, bf16[1920,128]{0,1:T(8,128)(2,1)S(1)}, u32[]{:S(2)}, u32[]{:S(2)}) collective-permute-start(bf16[1920,128]{0,1:T(8,128)(2,1)} %get-tuple-element.486), channel_id=1, source_target_pairs={{0,2},{1,3},{2,0},{3,1},{4,6},{5,7},{6,4},{7,5},{8,10},{9,11},{10,... | collective-permute-start | bytes 1474568 | tf_op jit(solution)/shard_map/ppermute | solution.py:15
  64.4 33.6 %collective-permute-start.21 = (bf16[1920,128]{0,1:T(8,128)(2,1)}, bf16[1920,128]{0,1:T(8,128)(2,1)}, u32[]{:S(2)}, u32[]{:S(2)}) collective-permute-start(bf16[1920,128]{0,1:T(8,128)(2,1)} %get-tuple-element.487), channel_id=1, source_target_pairs={{0,3},{1,2},{2,1},{3,0},{4,7},{5,6},{6,5},{7,4},{8,11},{9,10},{10,... | collective-permute-start | bytes 1474568 | tf_op jit(solution)/shard_map/ppermute | solution.py:15
  65.2 34.0 %collective-permute-start.22 = (bf16[1920,128]{0,1:T(8,128)(2,1)S(1)}, bf16[1920,128]{0,1:T(8,128)(2,1)}, u32[]{:S(2)}, u32[]{:S(2)}) collective-permute-start(bf16[1920,128]{0,1:T(8,128)(2,1)S(1)} %get-tuple-element.488), channel_id=1, source_target_pairs={{0,1},{1,0},{2,3},{3,2},{4,5},{5,4},{6,7},{7,6},{8,9},{9,8},{10,11... | collective-permute-start | bytes 1474568 | tf_op jit(solution)/shard_map/ppermute | solution.py:15
  67.5 13.3 %collective-permute-start = (bf16[1024,256]{1,0:T(8,128)(2,1)S(1)}, bf16[1024,256]{1,0:T(8,128)(2,1)S(1)}, u32[]{:S(2)}, u32[]{:S(2)}) collective-permute-start(bf16[1024,256]{1,0:T(8,128)(2,1)S(1)} %copy.42), channel_id=1, source_target_pairs={{0,8},{4,12},{8,0},{12,4},{1,9},{5,13},{9,1},{13,5},{2,10},{6,14},... | collective-permute-start | bytes 1572872 | tf_op jit(solution)/shard_map/while/body/ppermute | solution.py:15
  69.3 11.5 %collective-permute-start.1 = (f32[1,512]{1,0:T(1,128)S(1)}, f32[1,512]{1,0:T(1,128)S(1)}, u32[]{:S(2)}, u32[]{:S(2)}) collective-permute-start(f32[1,512]{1,0:T(1,128)S(1)} %copy.43), channel_id=1, source_target_pairs={{0,8},{4,12},{8,0},{12,4},{1,9},{5,13},{9,1},{13,5},{2,10},{6,14},... | collective-permute-start | bytes 6152 | tf_op jit(solution)/shard_map/while/body/ppermute | solution.py:15
  80.9 2.9 %collective-permute-start.2 = (bf16[2048,256]{1,0:T(8,128)(2,1)S(1)}, bf16[2048,256]{1,0:T(8,128)(2,1)}, u32[]{:S(2)}, u32[]{:S(2)}) collective-permute-start(bf16[2048,256]{1,0:T(8,128)(2,1)S(1)} %pad_maximum_fusion.17), channel_id=1, source_target_pairs={{0,4},{4,0},{8,12},{12,8},{1,5},{5,1},{9,13},{13,9},{2,6},{6,2},{1... | collective-permute-start | bytes 3145736 | tf_op jit(solution)/shard_map/while/body/ppermute | solution.py:15
  93.5 9.5 %copy-start.1 = (bf16[1920,128]{0,1:T(8,128)(2,1)S(1)}, bf16[1920,128]{0,1:T(8,128)(2,1)}, u32[]{:S(2)}) copy-start(bf16[1920,128]{0,1:T(8,128)(2,1)} %get-tuple-element.501) | copy-start | bytes 1474564
  99.2 15.5 %copy-start.14 = (bf16[1920,128]{0,1:T(8,128)(2,1)S(1)}, bf16[1920,128]{0,1:T(8,128)(2,1)}, u32[]{:S(2)}) copy-start(bf16[1920,128]{0,1:T(8,128)(2,1)} %get-tuple-element.502) | copy-start | bytes 1474564
  101.5 15.8 %copy-start.15 = (bf16[1920,128]{0,1:T(8,128)(2,1)S(1)}, bf16[1920,128]{0,1:T(8,128)(2,1)}, u32[]{:S(2)}) copy-start(bf16[1920,128]{0,1:T(8,128)(2,1)} %get-tuple-element.503) | copy-start | bytes 1474564
  101.6 16.8 %copy-start.3 = (f32[1920,128]{0,1:T(8,128)S(1)}, f32[1920,128]{0,1:T(8,128)}, u32[]{:S(2)}) copy-start(f32[1920,128]{0,1:T(8,128)} %get-tuple-element.516) | copy-start | bytes 2949124
  104.0 14.7 %copy-start.18 = (f32[1,512]{1,0:T(1,128)S(1)}, f32[1,512]{1,0:T(1,128)}, u32[]{:S(2)}) copy-start(f32[1,512]{1,0:T(1,128)} %get-tuple-element.513) | copy-start | bytes 6148
  104.0 14.7 %copy-start.19 = (f32[1,128]{1,0:T(1,128)S(1)}, f32[1,128]{1,0:T(1,128)}, u32[]{:S(2)}) copy-start(f32[1,128]{1,0:T(1,128)} %param.18) | copy-start | bytes 1540
  104.0 51.1 %collective-permute-start.23 = (bf16[1920,128]{1,0:T(8,128)(2,1)}, bf16[1920,128]{1,0:T(8,128)(2,1)}, u32[]{:S(2)}, u32[]{:S(2)}) collective-permute-start(bf16[1920,128]{1,0:T(8,128)(2,1)} %copy.20), channel_id=1, source_target_pairs={{0,2},{1,3},{2,0},{3,1},{4,6},{5,7},{6,4},{7,5},{8,10},{9,11},{10,... | collective-permute-start | bytes 1474568 | tf_op jit(solution)/shard_map/ppermute | solution.py:15
  115.7 39.4 %collective-permute-start.24 = (bf16[1920,128]{1,0:T(8,128)(2,1)}, bf16[1920,128]{1,0:T(8,128)(2,1)}, u32[]{:S(2)}, u32[]{:S(2)}) collective-permute-start(bf16[1920,128]{1,0:T(8,128)(2,1)} %copy.21), channel_id=1, source_target_pairs={{0,3},{1,2},{2,1},{3,0},{4,7},{5,6},{6,5},{7,4},{8,11},{9,10},{10,... | collective-permute-start | bytes 1474568 | tf_op jit(solution)/shard_map/ppermute | solution.py:15
  118.3 36.8 %collective-permute-start.25 = (bf16[1920,128]{1,0:T(8,128)(2,1)}, bf16[1920,128]{1,0:T(8,128)(2,1)}, u32[]{:S(2)}, u32[]{:S(2)}) collective-permute-start(bf16[1920,128]{1,0:T(8,128)(2,1)} %copy.22), channel_id=1, source_target_pairs={{0,1},{1,0},{2,3},{3,2},{4,5},{5,4},{6,7},{7,6},{8,9},{9,8},{10,11... | collective-permute-start | bytes 1474568 | tf_op jit(solution)/shard_map/ppermute | solution.py:15
  118.9 13.1 %collective-permute-start.3 = (bf16[1920,128]{1,0:T(8,128)(2,1)S(1)}, bf16[1920,128]{1,0:T(8,128)(2,1)S(1)}, u32[]{:S(2)}, u32[]{:S(2)}) collective-permute-start(bf16[1920,128]{1,0:T(8,128)(2,1)S(1)} %copy.61), channel_id=1, source_target_pairs={{0,8},{4,12},{8,0},{12,4},{1,9},{5,13},{9,1},{13,5},{2,10},{6,14},... | collective-permute-start | bytes 1474568 | tf_op jit(solution)/shard_map/while/body/ppermute | solution.py:15
  121.1 12.3 %collective-permute-start.4 = (bf16[1920,128]{1,0:T(8,128)(2,1)S(1)}, bf16[1920,128]{1,0:T(8,128)(2,1)S(1)}, u32[]{:S(2)}, u32[]{:S(2)}) collective-permute-start(bf16[1920,128]{1,0:T(8,128)(2,1)S(1)} %copy.61), channel_id=1, source_target_pairs={{0,16},{16,0},{1,17},{17,1},{2,18},{18,2},{3,19},{19,3},{4,20},{20... | collective-permute-start | bytes 1474568 | tf_op jit(solution)/shard_map/while/body/ppermute | solution.py:15
  133.6 13.7 %collective-permute-start.6 = (bf16[1920,256]{1,0:T(8,128)(2,1)S(1)}, bf16[1920,256]{1,0:T(8,128)(2,1)}, u32[]{:S(2)}, u32[]{:S(2)}) collective-permute-start(bf16[1920,256]{1,0:T(8,128)(2,1)S(1)} %pad_maximum_fusion.18), channel_id=1, source_target_pairs={{0,4},{4,0},{8,12},{12,8},{1,5},{5,1},{9,13},{13,9},{2,6},{6,2},{1... | collective-permute-start | bytes 2949128 | tf_op jit(solution)/shard_map/while/body/ppermute | solution.py:15
  133.7 13.6 %collective-permute-start.5 = (bf16[1920,128]{1,0:T(8,128)(2,1)S(1)}, bf16[1920,128]{1,0:T(8,128)(2,1)S(1)}, u32[]{:S(2)}, u32[]{:S(2)}) collective-permute-start(bf16[1920,128]{1,0:T(8,128)(2,1)S(1)} %collective-permute-done.4), channel_id=1, source_target_pairs={{0,8},{4,12},{8,0},{12,4},{1,9},{5,13},{9,1},{13,5},{2,10},{6,14},... | collective-permute-start | bytes 1474568 | tf_op jit(solution)/shard_map/while/body/ppermute | solution.py:15
  134.2 13.5 %copy-start.12 = (bf16[576,1920]{1,0:T(8,128)(2,1)S(1)}, bf16[576,1920]{1,0:T(8,128)(2,1)}, u32[]{:S(2)}) copy-start(bf16[576,1920]{1,0:T(8,128)(2,1)} %get-tuple-element.1029) | copy-start | bytes 6635524 | tf_op jit(solution)/shard_map/while
  147.6 4.7 %collective-permute-start.7 = (bf16[1920,256]{1,0:T(8,128)(2,1)S(1)}, bf16[1920,256]{1,0:T(8,128)(2,1)S(1)}, u32[]{:S(2)}, u32[]{:S(2)}) collective-permute-start(bf16[1920,256]{1,0:T(8,128)(2,1)S(1)} %pad_maximum_fusion.19), channel_id=1, source_target_pairs={{0,4},{4,0},{8,12},{12,8},{1,5},{5,1},{9,13},{13,9},{2,6},{6,2},{1... | collective-permute-start | bytes 2949128 | tf_op jit(solution)/shard_map/while/body/ppermute | solution.py:15
  156.7 13.7 %collective-permute-start.27 = (bf16[1920,128]{1,0:T(8,128)(2,1)S(1)}, bf16[1920,128]{1,0:T(8,128)(2,1)S(1)}, u32[]{:S(2)}, u32[]{:S(2)}) collective-permute-start(bf16[1920,128]{1,0:T(8,128)(2,1)S(1)} %add_convert_fusion), channel_id=1, source_target_pairs={{0,8},{4,12},{8,0},{12,4},{1,9},{5,13},{9,1},{13,5},{2,10},{6,14},... | collective-permute-start | bytes 1474568 | tf_op jit(solution)/shard_map/ppermute | solution.py:15
  157.2 13.3 %collective-permute-start.28 = (bf16[1920,128]{1,0:T(8,128)(2,1)S(1)}, bf16[1920,128]{1,0:T(8,128)(2,1)S(1)}, u32[]{:S(2)}, u32[]{:S(2)}) collective-permute-start(bf16[1920,128]{1,0:T(8,128)(2,1)S(1)} %add_convert_fusion), channel_id=1, source_target_pairs={{0,16},{16,0},{1,17},{17,1},{2,18},{18,2},{3,19},{19,3},{4,20},{20... | collective-permute-start | bytes 1474568 | tf_op jit(solution)/shard_map/ppermute | solution.py:15
  158.9 10.7 %collective-permute-start.26 = (bf16[12,48,256]{2,1,0:T(8,128)(2,1)S(1)}, bf16[12,48,256]{2,1,0:T(8,128)(2,1)S(1)}, u32[]{:S(2)}, u32[]{:S(2)}) collective-permute-start(bf16[12,48,256]{2,1,0:T(8,128)(2,1)S(1)} %copy-done.16), channel_id=1, source_target_pairs={{0,1},{1,2},{2,3},{3,0},{4,5},{5,6},{6,7},{7,4},{8,9},{9,10},{10,1... | collective-permute-start | bytes 884744 | tf_op jit(solution)/shard_map/ppermute | solution.py:11
  171.3 23.5 %collective-permute-start.29 = (bf16[12,48,256]{2,1,0:T(8,128)(2,1)}, bf16[12,48,256]{2,1,0:T(8,128)(2,1)}, u32[]{:S(2)}, u32[]{:S(2)}) collective-permute-start(bf16[12,48,256]{2,1,0:T(8,128)(2,1)} %broadcast_select_fusion.15), channel_id=1, source_target_pairs={{0,2},{1,3},{2,0},{3,1},{4,6},{5,7},{6,4},{7,5},{8,10},{9,11},{10,... | collective-permute-start | bytes 884744 | tf_op jit(solution)/shard_map/ppermute | solution.py:11
  176.0 10.1 %collective-permute-start.10 = (bf16[1920,256]{1,0:T(8,128)(2,1)S(1)}, bf16[1920,256]{1,0:T(8,128)(2,1)}, u32[]{:S(2)}, u32[]{:S(2)}) collective-permute-start(bf16[1920,256]{1,0:T(8,128)(2,1)S(1)} %pad_maximum_fusion.21), channel_id=1, source_target_pairs={{0,4},{4,0},{8,12},{12,8},{1,5},{5,1},{9,13},{13,9},{2,6},{6,2},{1... | collective-permute-start | bytes 2949128 | tf_op jit(solution)/shard_map/while/body/ppermute | solution.py:15
  176.8 8.6 %collective-permute-start.9 = (bf16[960,128]{1,0:T(8,128)(2,1)}, bf16[960,128]{1,0:T(8,128)(2,1)S(1)}, u32[]{:S(2)}, u32[]{:S(2)}) collective-permute-start(bf16[960,128]{1,0:T(8,128)(2,1)} %slice.211), channel_id=1, source_target_pairs={{0,8},{4,12},{8,0},{12,4},{1,9},{5,13},{9,1},{13,5},{2,10},{6,14},... | collective-permute-start | bytes 737288 | tf_op jit(solution)/shard_map/while/body/ppermute | solution.py:15
  177.8 8.3 %collective-permute-start.8 = (bf16[960,128]{1,0:T(8,128)(2,1)}, bf16[960,128]{1,0:T(8,128)(2,1)S(1)}, u32[]{:S(2)}, u32[]{:S(2)}) collective-permute-start(bf16[960,128]{1,0:T(8,128)(2,1)} %slice.210), channel_id=1, source_target_pairs={{0,16},{16,0},{1,17},{17,1},{2,18},{18,2},{3,19},{19,3},{4,20},{20... | collective-permute-start | bytes 737288 | tf_op jit(solution)/shard_map/while/body/ppermute | solution.py:15
  186.4 5.9 %collective-permute-start.11 = (bf16[1920,256]{1,0:T(8,128)(2,1)S(1)}, bf16[1920,256]{1,0:T(8,128)(2,1)S(1)}, u32[]{:S(2)}, u32[]{:S(2)}) collective-permute-start(bf16[1920,256]{1,0:T(8,128)(2,1)S(1)} %pad_maximum_fusion.22), channel_id=1, source_target_pairs={{0,4},{4,0},{8,12},{12,8},{1,5},{5,1},{9,13},{13,9},{2,6},{6,2},{1... | collective-permute-start | bytes 2949128 | tf_op jit(solution)/shard_map/while/body/ppermute | solution.py:15
  196.1 10.5 %collective-permute-start.30 = (bf16[12,48,256]{2,1,0:T(8,128)(2,1)S(1)}, bf16[12,48,256]{2,1,0:T(8,128)(2,1)S(1)}, u32[]{:S(2)}, u32[]{:S(2)}) collective-permute-start(bf16[12,48,256]{2,1,0:T(8,128)(2,1)S(1)} %copy-done.5), channel_id=1, source_target_pairs={{0,1},{1,2},{2,3},{3,0},{4,5},{5,6},{6,7},{7,4},{8,9},{9,10},{10,1... | collective-permute-start | bytes 884744 | tf_op jit(solution)/shard_map/ppermute | solution.py:11
  206.7 13.0 %collective-permute-start.34 = (bf16[12,48,256]{2,1,0:T(8,128)(2,1)S(1)}, bf16[12,48,256]{2,1,0:T(8,128)(2,1)S(1)}, u32[]{:S(2)}, u32[]{:S(2)}) collective-permute-start(bf16[12,48,256]{2,1,0:T(8,128)(2,1)S(1)} %broadcast_select_fusion.14), channel_id=1, source_target_pairs={{0,2},{1,3},{2,0},{3,1},{4,6},{5,7},{6,4},{7,5},{8,10},{9,11},{10,... | collective-permute-start | bytes 884744 | tf_op jit(solution)/shard_map/ppermute | solution.py:11
  206.8 1.9 collective-permute-start.31
  206.9 5.7 %collective-permute-start.32 = (bf16[4,48,2,1,128]{4,2,1,0,3:T(2,128)(2,1)S(1)}, bf16[4,48,2,1,128]{4,2,1,0,3:T(2,128)(2,1)S(1)}, u32[]{:S(2)}, u32[]{:S(2)}) collective-permute-start(bf16[4,48,2,1,128]{4,2,1,0,3:T(2,128)(2,1)S(1)} %squeeze.30), channel_id=1, source_target_pairs={{0,8},{4,12},{8,0},{12,4},{1,9},{5,13},{9,1},{13,5},{2,10},{6,14},... | collective-permute-start | bytes 294920 | tf_op jit(solution)/shard_map/ppermute | solution.py:15
  208.6 5.1 %collective-permute-start.33 = (bf16[4,48,2,1,128]{4,2,1,0,3:T(2,128)(2,1)S(1)}, bf16[4,48,2,1,128]{4,2,1,0,3:T(2,128)(2,1)S(1)}, u32[]{:S(2)}, u32[]{:S(2)}) collective-permute-start(bf16[4,48,2,1,128]{4,2,1,0,3:T(2,128)(2,1)S(1)} %squeeze.31), channel_id=1, source_target_pairs={{0,12},{4,8},{8,4},{12,0},{1,13},{5,9},{9,5},{13,1},{2,14},{6,10},... | collective-permute-start | bytes 294920 | tf_op jit(solution)/shard_map/ppermute | solution.py:15
  220.5 2.4 %collective-permute-start.35 = (bf16[4,48,2,1,128]{4,2,1,0,3:T(2,128)(2,1)S(1)}, bf16[4,48,2,1,128]{4,2,1,0,3:T(2,128)(2,1)S(1)}, u32[]{:S(2)}, u32[]{:S(2)}) collective-permute-start(bf16[4,48,2,1,128]{4,2,1,0,3:T(2,128)(2,1)S(1)} %squeeze.33), channel_id=1, source_target_pairs={{0,4},{4,0},{8,12},{12,8},{1,5},{5,1},{9,13},{13,9},{2,6},{6,2},{1... | collective-permute-start | bytes 294920 | tf_op jit(solution)/shard_map/ppermute | solution.py:15
  220.7 5.6 %collective-permute-start.36 = (bf16[4,48,2,1,128]{4,2,1,0,3:T(2,128)(2,1)S(1)}, bf16[4,48,2,1,128]{4,2,1,0,3:T(2,128)(2,1)S(1)}, u32[]{:S(2)}, u32[]{:S(2)}) collective-permute-start(bf16[4,48,2,1,128]{4,2,1,0,3:T(2,128)(2,1)S(1)} %squeeze.34), channel_id=1, source_target_pairs={{0,8},{4,12},{8,0},{12,4},{1,9},{5,13},{9,1},{13,5},{2,10},{6,14},... | collective-permute-start | bytes 294920 | tf_op jit(solution)/shard_map/ppermute | solution.py:15
  222.6 5.2 %collective-permute-start.37 = (bf16[4,48,2,1,128]{4,2,1,0,3:T(2,128)(2,1)S(1)}, bf16[4,48,2,1,128]{4,2,1,0,3:T(2,128)(2,1)S(1)}, u32[]{:S(2)}, u32[]{:S(2)}) collective-permute-start(bf16[4,48,2,1,128]{4,2,1,0,3:T(2,128)(2,1)S(1)} %squeeze.35), channel_id=1, source_target_pairs={{0,12},{4,8},{8,4},{12,0},{1,13},{5,9},{9,5},{13,1},{2,14},{6,10},... | collective-permute-start | bytes 294920 | tf_op jit(solution)/shard_map/ppermute | solution.py:15
  (16 other events, 51.4 us)

commit v10 on v9

--- a/solution.py
+++ b/solution.py
@@ -1,6 +1,8 @@
 import jax
 import jax.numpy as jnp
 from jax import lax
+from jax.experimental import pallas as pl
+from jax.experimental.pallas import tpu as pltpu
 from jax.sharding import PartitionSpec as P
 
 eps_norm = 1e-05
@@ -71,6 +73,51 @@
     return gathered_rows[None, None]
 
 
+def terms_body(choice, ours, others, near_ours, near_others, far_ours, far_others, own, *parts):
+    near = add_columns(ours[...], near_ours[...]) + add_columns(others[...], near_others[...])
+    far = add_columns(ours[...], far_ours[...]) + add_columns(others[...], far_others[...])
+    width = own.shape[1]
+    near_kept = choice[0] == 1
+    kept, sent = jnp.where(near_kept, near, far), jnp.where(near_kept, far, near)
+    own[...] = kept[:, :width]
+    blocks = (sent[:, width:], kept[:, width:], sent[:, :width])
+    for part, block in zip(parts, blocks):
+        part[...] = block.astype(part.dtype)
+
+
+def product_terms(choice, weight, near, far):
+    depth, rows = weight.shape
+    half, columns = rows // 2, near[0].shape[1]
+    width = columns // 2
+    tall = 240 if depth % 240 == 0 else depth
+    whole = pl.BlockSpec((half, columns), lambda i, choice: (0, 0))
+    narrow = pl.BlockSpec((tall, width), lambda i, choice: (i, 0))
+    shapes = [jax.ShapeDtypeStruct((depth, width), t) for t in (jnp.float32,) + 3 * (jnp.bfloat16,)]
+    return pl.pallas_call(
+        terms_body,
+        out_shape=shapes,
+        grid_spec=pltpu.PrefetchScalarGridSpec(
+            num_scalar_prefetch=1,
+            grid=(depth // tall,),
+            in_specs=[
+                pl.BlockSpec((tall, half), lambda i, choice: (i, choice[1])),
+                pl.BlockSpec((tall, half), lambda i, choice: (i, 1 - choice[1])),
+                whole,
+                whole,
+                whole,
+                whole,
+            ],
+            out_specs=[narrow] * 4,
+        ),
+        compiler_params=pltpu.CompilerParams(vmem_limit_bytes=32 * 1024 * 1024),
+        cost_estimate=pl.CostEstimate(
+            flops=4 * depth * rows * columns,
+            bytes_accessed=2 * depth * rows + 4 * rows * columns + 10 * depth * width,
+            transcendentals=0,
+        ),
+    )(choice, weight, weight, *near, *far)
+
+
 def product_plan(
     features, proj_weight, proj_bias, kv_weight, key_gain, tile_map, tile_count, decode_owner
 ):
@@ -109,17 +156,11 @@
     def both_heads(ours, theirs):
         return put_first(group == 0, ours, theirs, 1)
 
+    choice = jnp.stack([(at_end == first_core).astype(jnp.int32), head // 2])
+
     def products(near, far):
-        both = add_columns(proj_weight, jnp.concatenate([near, far], axis=1))
-        near_0, near_1, far_0, far_1 = (both[:, k * width : (k + 1) * width] for k in range(4))
-        near_kept = at_end == first_core
-        parts = (
-            jnp.where(near_kept, far_1, near_1),
-            jnp.where(near_kept, near_1, far_1),
-            jnp.where(near_kept, far_0, near_0),
-        )
-        own = jnp.where(near_kept, near_0, far_0)
-        return own, tuple(part.astype(jnp.bfloat16) for part in parts)
+        own, *parts = product_terms(choice, proj_weight, near, far)
+        return own, tuple(parts)
 
     def exchange(parts):
         return tuple(swapped(part, "head", bit) for part, bit in zip(parts, (2, 3, 1)))
@@ -172,51 +213,82 @@
         return jnp.stack(ranked, axis=1)
 
     column, half = group * 2 * head_dim, kv_weight.shape[0] // 2
-    key_mine = lax.dynamic_slice_in_dim(kv_weight, column, head_dim, axis=1)
-    value_mine = lax.dynamic_slice_in_dim(kv_weight, column + head_dim, head_dim, axis=1)
-    stays = lax.dynamic_slice_in_dim(value_mine, tile // 2 * half, half, axis=0)
-    leaves = lax.dynamic_slice_in_dim(value_mine, half - tile // 2 * half, half, axis=0)
+
+    def halves(part):
+        mine = lax.dynamic_slice_in_dim(kv_weight, column + part * head_dim, head_dim, axis=1)
+        ours = lax.dynamic_slice_in_dim(mine, tile // 2 * half, half, axis=0)
+        return ours, lax.dynamic_slice_in_dim(mine, half - tile // 2 * half, half, axis=0)
+
+    def ours_to_plane(rows):
+        return moved(rows, lambda t, h: (h // 2 * 2 + outer_core(h), t))
+
+    def others_to_plane(rows):
+        return moved(rows, lambda t, h: (h // 2 * 2 + outer_core(h), t ^ 2))
+
+    def both_blocks(rows, other):
+        return put_first(tile // 2 == head // 2, rows, other, 1)
+
+    key_ours, key_others = halves(0)
+    value_ours, value_others = halves(1)
     bias_rows = moved(proj_bias, lambda t, h: (h, t))
-    key_block = moved(key_mine, lambda t, h: (h // 2 * 2 + outer_core(h), t))
-    comes = swapped(leaves, "tile", 2)
-    no_block = jnp.zeros((depth, width), jnp.float32)
-    no_terms = no_block, tuple(jnp.zeros((depth, width), jnp.bfloat16) for _ in range(3))
+    key_ours = ours_to_plane(key_ours)
+    key_others, value_others = swapped(key_others, "tile", 2), swapped(value_others, "tile", 2)
+    no_terms = (
+        jnp.zeros((depth, width), jnp.float32),
+        tuple(jnp.full((depth, width), k, jnp.bfloat16) for k in range(3)),
+    )
     no_tokens = tuple(
-        jnp.zeros((tile_slots, shard_len, 2 * width), jnp.bfloat16) for _ in range(2)
-    )
-    bias_rows, key_block, comes, stays, feature_parts, no_terms, no_tokens, once = step(
-        (bias_rows, key_block, comes, stays, feature_parts, no_terms, no_tokens, once)
-    )
-
-    value_pieces = []
-    for j in range(2):
-        piece = jnp.where(tile // 2 == (head // 2) ^ j, stays, comes)
-        value_pieces.append(
-            moved(piece, lambda t, h: (t // 2 * 2 + outer_core(h), t % 2 + 2 * ((h // 2) ^ j)))
+        jnp.full((tile_slots, shard_len, 2 * width), k, jnp.bfloat16) for k in range(2)
+    )
+    bias_rows, key_ours, key_others, value_ours, value_others = step(
+        (bias_rows, key_ours, key_others, value_ours, value_others)
+    )
+
+    key_others, value_ours = others_to_plane(key_others), ours_to_plane(value_ours)
+    other = swapped(key_ours, "tile", 2)
+    bias_part = add_columns(bias_rows[None], kv_weight)
+    key_ours, key_others, value_ours, other, bias_part, feature_parts, no_terms, no_tokens, once = step(
+        (
+            key_ours,
+            key_others,
+            value_ours,
+            other,
+            bias_part,
+            feature_parts,
+            no_terms,
+            no_tokens,
+            once,
         )
-    key_other = swapped(key_block, "tile", 2)
-    bias_part = add_columns(bias_rows[None], kv_weight)
-    value_pieces, key_block, key_other, bias_part = step(
-        (value_pieces, key_block, key_other, bias_part)
-    )
-
-    key_near = put_first(tile // 2 == head // 2, key_block, key_other, 1)
-    value_half = jnp.concatenate(value_pieces, axis=1)
-    key_near, value_half = step((key_near, value_half))
-    own, parts = products(key_near, swapped(key_near, "tile", 1))
+    )
+
+    near_ours = step(both_blocks(key_ours, other))
+    value_others = others_to_plane(value_others)
+    other, far_ours = step((swapped(key_others, "tile", 2), swapped(near_ours, "tile", 1)))
+    near_others = step(both_blocks(key_others, other))
+    far_others = swapped(near_others, "tile", 1)
     bias_part = bias_part + swapped(bias_part, "tile", 1)
-    own, parts, value_half, bias_part = step((own, parts, value_half, bias_part))
+    own, parts = products((near_ours, near_others), (far_ours, far_others))
+    own, parts, value_ours, value_others, bias_part = step(
+        (own, parts, value_ours, value_others, bias_part)
+    )
 
     def values_terms(given):
-        value_half, bias_part = given
-        other, bias_other = step((swapped(value_half, "tile", 2), swapped(bias_part, "tile", 2)))
-        near = step(put_first(first_chip, value_half, other, 0))
-        terms = products(near, swapped(near, "tile", 1))
-        return (other, bias_other), (terms, bias_part + bias_other)
+        value_ours, value_others, bias_part = given
+        other_ours, other_others, bias_other = step(
+            (
+                swapped(value_ours, "tile", 2),
+                swapped(value_others, "tile", 2),
+                swapped(bias_part, "tile", 2),
+            )
+        )
+        near = both_blocks(value_ours, other_ours), both_blocks(value_others, other_others)
+        near = step(near)
+        terms = products(near, tuple(swapped(rows, "tile", 1) for rows in near))
+        return (other_ours, other_others, bias_other), (terms, bias_part + bias_other)
 
     empty = no_terms, bias_part
     arrived, beside = step(
-        (exchange(parts), in_loop(values_terms, (value_half, bias_part), empty))
+        (exchange(parts), in_loop(values_terms, (value_ours, value_others, bias_part), empty))
     )
     own = summed(own, arrived)
     (value_own, parts), bias_part = beside

time: 234 us -> 238 us (1.017)
  Pallas kernels: 0 us -> 19.8 us
  waiting for transfers between devices: 93.8 us -> 112 us
  matrix products: 24.3 us -> 9.92 us
  starting transfers between devices: 64.2 us -> 53.6 us
  other arithmetic: 19.8 us -> 13.2 us
    ppermute x30 -> x35, waiting for transfers between devices: 63 us -> 84.3 us  [swapped(): lax.ppermute(shard, axis, [(i, i ^ bit) for i in range(lax.axis_size(axis...]
    pallas_call x0 -> x2, Pallas kernels: none -> 19.8 us  [product_terms(): pl.pallas_call(terms_body, out_shape=shapes, grid_spec=pltpu.PrefetchScal...]
    dot_general x13 -> x11, matrix products: 24.1 us -> 9.73 us  [add_columns(): return jnp.dot(operand, portion, preferred_element_type=jnp.float32)]
    ppermute x30 -> x35, starting transfers between devices: 51.2 us -> 37.1 us  [swapped(): lax.ppermute(shard, axis, [(i, i ^ bit) for i in range(lax.axis_size(axis...]
    broadcast_in_dim x1 -> x6, local copies, waits for them, and re-layouts: 1.06 us -> 5.07 us  [the longest x3 2.56 us: product_plan(): jnp.full((depth, width), k, jnp.bfloat16)]
    optimization_barrier x5 -> x1, local copies, waits for them, and re-layouts: 3.33 us -> 0.01 us  [product_plan(): step((bias_rows, key_ours, key_others, value_ours, value_others))]
    ppermute x4 -> x5, waiting for transfers between devices: 9.02 us -> 6.25 us  [moved(): return lax.ppermute(shard, ('tile', 'head'), pairs)]
    convert_element_type x2 -> x0, other arithmetic: 2.4 us -> none  [products(): return (own, tuple((part.astype(jnp.bfloat16) for part in parts)))]
  transfers between devices with their start and end apart: 38 -> 44, of which waited for: 20 -> 22; matrix products, arithmetic and copies ran while one was open for 19% -> 13% of each run, Pallas kernels for 0% -> 8%
where the time goes in v10:
time: 238 us; the launch traced here: 237 us
  waiting for transfers between devices  112 us (47%)
  starting transfers between devices  53.6 us (23%)
  local copies, waits for them, and re-layouts  27.5 us (12%)
  Pallas kernels  19.8 us (8%)
  other arithmetic  13.2 us (6%)
  matrix products  9.92 us (4%)
    ppermute x35, waiting for transfers between devices, swapped(): lax.ppermute(shard, axis, [(i, i ^ bit) for i in range(lax.axis_size(axis...  84.3 us
    ppermute x35, starting transfers between devices, swapped(): lax.ppermute(shard, axis, [(i, i ^ bit) for i in range(lax.axis_size(axis...  37.1 us
    ppermute x4, waiting for transfers between devices, shifted_2(): lax.ppermute(shard, axis, [(i, (i + by) % count) for i in range(count)])  21.3 us
    pallas_call x2, Pallas kernels, product_terms(): pl.pallas_call(terms_body, out_shape=shapes, grid_spec=pltpu.PrefetchScal...  19.8 us
    ppermute x4, starting transfers between devices, shifted_2(): lax.ppermute(shard, axis, [(i, (i + by) % count) for i in range(count)])  10.6 us
    dot_general x11, matrix products, add_columns(): return jnp.dot(operand, portion, preferred_element_type=jnp.float32)  9.73 us
    dynamic_slice x1, local copies, waits for them, and re-layouts, product_plan(): lax.dynamic_slice_in_dim(feature_rows, (tile ^ r) * depth, depth, axis=1)  7.31 us
    ppermute x5, waiting for transfers between devices, moved(): return lax.ppermute(shard, ('tile', 'head'), pairs)  6.25 us
  transfers between devices with their start and end apart: 44, of which 22 were waited for; matrix products, arithmetic and copies ran while one was open for 13% of the time, Pallas kernels for 8%

profile of v10, /device:TPU:0, one launch (start us, length us, event | category | flops | bytes accessed | tf_op | source)
XLA Modules:
  0.0 237.3 jit_solution(3155461294928524752)
XLA Ops:
  0.0 2.2 fusion.23
  2.9 6.8 %collective-permute-start.16 = (bf16[1024,128]{1,0:T(8,128)(2,1)S(1)}, bf16[1024,128]{1,0:T(8,128)(2,1)}, u32[]{:S(2)}, u32[]{:S(2)}) collective-permute-start(bf16[1024,128]{1,0:T(8,128)(2,1)S(1)} %get-tuple-element.825), channel_id=1, source_target_pairs={{0,8},{4,12},{8,0},{12,4},{1,9},{5,13},{9,1},{13,5},{2,10},{6,14},... | collective-permute-start | bytes 786440 | tf_op jit(solution)/shard_map/ppermute | solution.py:17
  9.8 1.3 collective-permute-start.14
  11.1 7.3 %constant_dynamic-slice_fusion = (bf16[576,1920]{1,0:T(8,128)(2,1)}, bf16[576,1920]{1,0:T(8,128)(2,1)}, bf16[576,1920]{1,0:T(8,128)(2,1)}, bf16[576,1920]{1,0:T(8,128)(2,1)}) fusion(bf16[576,7680]{1,0:T(8,128)(2,1)} %bitcast.135, s32[]{:T(128)S(6)} %select_n.331, s32[]{:T(128)S(6)} %select_n.330, s32[]{:T(128)S(6)} %select_n.329, s32[]{:T(128)S(6)} %select_n.328), kind=kLoop, calls=%fused_computation.110 | loop fusion | bytes 17694736 | tf_op jit(solution)/shard_map/dynamic_slice | solution.py:148
  19.8 1.6 collective-permute-done.16
  21.4 5.6 %collective-permute-done.17 = bf16[1024,128]{1,0:T(8,128)(2,1)} collective-permute-done((bf16[1024,128]{1,0:T(8,128)(2,1)S(1)}, bf16[1024,128]{1,0:T(8,128)(2,1)}, u32[]{:S(2)}, u32[]{:S(2)}) %collective-permute-start.17) | collective-permute-done | bytes 262176 | tf_op jit(solution)/shard_map/ppermute | solution.py:17
  27.0 1.8 collective-permute-start.18
  29.5 2.8 %collective-permute-start.20 = (bf16[1024,128]{1,0:T(8,128)(2,1)S(1)}, bf16[1024,128]{1,0:T(8,128)(2,1)S(1)}, u32[]{:S(2)}, u32[]{:S(2)}) collective-permute-start(bf16[1024,128]{1,0:T(8,128)(2,1)S(1)} %collective-permute-done.15), channel_id=1, source_target_pairs={{0,8},{4,12},{8,0},{12,4},{1,9},{5,13},{9,1},{13,5},{2,10},{6,14},... | collective-permute-start | bytes 786440 | tf_op jit(solution)/shard_map/ppermute | solution.py:17
  32.6 6.2 %collective-permute-done.18 = bf16[1024,128]{1,0:T(8,128)(2,1)S(1)} collective-permute-done((bf16[1024,128]{1,0:T(8,128)(2,1)}, bf16[1024,128]{1,0:T(8,128)(2,1)S(1)}, u32[]{:S(2)}, u32[]{:S(2)}) %collective-permute-start.18) | collective-permute-done | bytes 262176 | tf_op jit(solution)/shard_map/ppermute | solution.py:142
  38.9 5.1 %collective-permute-done.20 = bf16[1024,128]{1,0:T(8,128)(2,1)S(1)} collective-permute-done((bf16[1024,128]{1,0:T(8,128)(2,1)S(1)}, bf16[1024,128]{1,0:T(8,128)(2,1)S(1)}, u32[]{:S(2)}, u32[]{:S(2)}) %collective-permute-start.20) | collective-permute-done | bytes 262176 | tf_op jit(solution)/shard_map/ppermute | solution.py:17
  44.9 2.2 collective-permute-start.21
  47.0 6.6 %collective-permute-done.21 = bf16[1024,128]{1,0:T(8,128)(2,1)S(1)} collective-permute-done((bf16[1024,128]{1,0:T(8,128)(2,1)S(1)}, bf16[1024,128]{1,0:T(8,128)(2,1)S(1)}, u32[]{:S(2)}, u32[]{:S(2)}) %collective-permute-start.21) | collective-permute-done | bytes 262176 | tf_op jit(solution)/shard_map/ppermute | solution.py:17
  54.4 1.5 collective-permute-start.24
  55.9 9.7 %shard_map.82 = (f32[1920,128]{1,0:T(8,128)S(1)}, bf16[1920,128]{1,0:T(8,128)(2,1)}, bf16[1920,128]{1,0:T(8,128)(2,1)}, bf16[1920,128]{1,0:T(8,128)(2,1)S(1)}) custom-call(s32[2]{0:T(128)S(1)} %pad_add_fusion.choice, bf16[1920,2048]{1,0:T(8,128)(2,1)} %others.1, bf16[1920,2048]{1,0:T(8,128)(2,1)} %others.1, ...), custom_call_target="tpu_custom_call" | custom-call | flops 4026531840 | bytes 12419072 | tf_op jit(solution)/shard_map/pallas_call | solution.py:96
  67.1 1.3 collective-permute-start.26
  68.4 2.3 collective-permute-start.27
  74.4 28.3 %while.59 = (s32[]{:T(128)}, bf16[1024,128]{1,0:T(8,128)(2,1)S(1)}, bf16[1024,128]{1,0:T(8,128)(2,1)}, f32[1,512]{1,0:T(1,128)S(1)}, f32[1920,128]{1,0:T(8,128)}...) while((s32[]{:T(128)}, bf16[1024,128]{1,0:T(8,128)(2,1)S(1)}, ...), condition=%wide.region_3.4_spmd, body=%wide.region_2.3_spmd.sunk | while | flops 4029153792 | bytes 25020776 | solution.py:176
  75.9 1.6 collective-permute-start.1
  77.9 11.4 %collective-permute-done.2 = f32[1,512]{1,0:T(1,128)S(1)} collective-permute-done((f32[1,512]{1,0:T(1,128)S(1)}, f32[1,512]{1,0:T(1,128)S(1)}, u32[]{:S(2)}, u32[]{:S(2)}) %collective-permute-start.2) | collective-permute-done | bytes 2080 | tf_op jit(solution)/shard_map/while/body/ppermute | solution.py:17
  92.6 10.1 %body.4 = (f32[1920,128]{1,0:T(8,128)}, bf16[1920,128]{1,0:T(8,128)(2,1)}, bf16[1920,128]{1,0:T(8,128)(2,1)}, bf16[1920,128]{1,0:T(8,128)(2,1)}) custom-call(s32[2]{0:T(128)S(1)} %get-tuple-element.1182.choice, bf16[1920,2048]{1,0:T(8,128)(2,1)} %get-tuple-element.1183.ours.others, bf16[1920,2048]{1,0:T(8,128)(2,1)} %get-tuple-element.1183.ours.others, ...), custom_call_target="tpu_custom_call" | custom-call | flops 4026531840 | bytes 12419072 | tf_op jit(solution)/shard_map/while/body/pallas_call | solution.py:96
  102.9 13.3 %collective-permute-done.28 = bf16[1920,128]{1,0:T(8,128)(2,1)S(1)} collective-permute-done((bf16[1920,128]{1,0:T(8,128)(2,1)}, bf16[1920,128]{1,0:T(8,128)(2,1)S(1)}, u32[]{:S(2)}, u32[]{:S(2)}) %collective-permute-start.28) | collective-permute-done | bytes 491552 | tf_op jit(solution)/shard_map/ppermute | solution.py:17
  117.3 1.6 collective-permute-start.30
  119.8 1.4 add_convert_fusion.1
  121.9 33.4 %while.60 = (s32[]{:T(128)}, bf16[1920,128]{1,0:T(8,128)(2,1)S(1)}, bf16[12,48,256]{2,1,0:T(8,128)(2,1)}, s32[]{:T(128)}, pred[]{:T(512)}, /*index=5*/bf16[576,1...) while((s32[]{:T(128)}, bf16[1920,128]{1,0:T(8,128)(2,1)S(1)}, ...), condition=%wide.region_7.8_spmd, body=%wide.region_4.7_spmd.sunk | while | flops 2271905024 | bytes 76995496 | solution.py:176
  122.3 1.3 collective-permute-start.6
  123.6 10.0 %collective-permute-done.5 = bf16[1920,128]{1,0:T(8,128)(2,1)S(1)} collective-permute-done((bf16[1920,128]{1,0:T(8,128)(2,1)S(1)}, bf16[1920,128]{1,0:T(8,128)(2,1)S(1)}, u32[]{:S(2)}, u32[]{:S(2)}) %collective-permute-start.5) | collective-permute-done | bytes 491552 | tf_op jit(solution)/shard_map/while/body/ppermute | solution.py:17
  134.0 1.7 collective-permute-start.7
  135.7 11.9 %collective-permute-done.7 = bf16[1920,128]{1,0:T(8,128)(2,1)S(1)} collective-permute-done((bf16[1920,128]{1,0:T(8,128)(2,1)S(1)}, bf16[1920,128]{1,0:T(8,128)(2,1)S(1)}, u32[]{:S(2)}, u32[]{:S(2)}) %collective-permute-start.7) | collective-permute-done | bytes 491552 | tf_op jit(solution)/shard_map/while/body/ppermute | solution.py:17
  149.5 2.1 convolution_add_fusion.10
  155.3 1.8 add_convert_fusion
  157.1 1.7 collective-permute-start.33
  158.8 1.4 collective-permute-start.34
  160.4 5.3 %collective-permute-start.32 = (bf16[12,48,256]{2,1,0:T(8,128)(2,1)S(1)}, bf16[12,48,256]{2,1,0:T(8,128)(2,1)S(1)}, u32[]{:S(2)}, u32[]{:S(2)}) collective-permute-start(bf16[12,48,256]{2,1,0:T(8,128)(2,1)S(1)} %copy-done.13), channel_id=1, source_target_pairs={{0,1},{1,2},{2,3},{3,0},{4,5},{5,6},{6,7},{7,4},{8,9},{9,10},{10,1... | collective-permute-start | bytes 884744 | tf_op jit(solution)/shard_map/ppermute | solution.py:13
  165.9 5.9 %collective-permute-done.32 = bf16[12,48,256]{2,1,0:T(8,128)(2,1)S(1)} collective-permute-done((bf16[12,48,256]{2,1,0:T(8,128)(2,1)S(1)}, bf16[12,48,256]{2,1,0:T(8,128)(2,1)S(1)}, u32[]{:S(2)}, u32[]{:S(2)}) %collective-permute-start.32) | collective-permute-done | bytes 294944 | tf_op jit(solution)/shard_map/ppermute | solution.py:13
  173.0 5.1 %collective-permute-start.35 = (bf16[12,48,256]{2,1,0:T(8,128)(2,1)}, bf16[12,48,256]{2,1,0:T(8,128)(2,1)}, u32[]{:S(2)}, u32[]{:S(2)}) collective-permute-start(bf16[12,48,256]{2,1,0:T(8,128)(2,1)} %broadcast_select_fusion.15), channel_id=1, source_target_pairs={{0,2},{1,3},{2,0},{3,1},{4,6},{5,7},{6,4},{7,5},{8,10},{9,11},{10,... | collective-permute-start | bytes 884744 | tf_op jit(solution)/shard_map/ppermute | solution.py:13
  178.9 20.4 %while.61 = (s32[]{:T(128)}, bf16[1920,128]{1,0:T(8,128)(2,1)S(1)}, bf16[1920,128]{1,0:T(8,128)(2,1)S(1)}, bf16[1920,128]{1,0:T(8,128)(2,1)S(1)}, bf16[12,48,256...) while((s32[]{:T(128)}, bf16[1920,128]{1,0:T(8,128)(2,1)S(1)}, ...), condition=%wide.region_9.10_spmd, body=%wide.region_8.9_spmd.sunk | while | flops 2271166464 | bytes 77368712 | solution.py:176
  179.9 1.7 collective-permute-start.11
  183.6 4.8 %collective-permute-done.11 = bf16[960,128]{1,0:T(8,128)(2,1)S(1)} collective-permute-done((bf16[960,128]{1,0:T(8,128)(2,1)}, bf16[960,128]{1,0:T(8,128)(2,1)S(1)}, u32[]{:S(2)}, u32[]{:S(2)}) %collective-permute-start.11) | collective-permute-done | bytes 245792 | tf_op jit(solution)/shard_map/while/body/ppermute | solution.py:17
  188.5 2.1 collective-permute-done.10
  190.9 1.3 copy-done.11
  193.8 2.1 convolution_add_fusion.12
  201.5 9.3 %collective-permute-done.36 = bf16[12,48,256]{2,1,0:T(8,128)(2,1)S(1)} collective-permute-done((bf16[12,48,256]{2,1,0:T(8,128)(2,1)S(1)}, bf16[12,48,256]{2,1,0:T(8,128)(2,1)S(1)}, u32[]{:S(2)}, u32[]{:S(2)}) %collective-permute-start.36) | collective-permute-done | bytes 294944 | tf_op jit(solution)/shard_map/ppermute | solution.py:13
  211.5 1.4 collective-permute-start.39
  213.0 3.8 %collective-permute-done.38 = bf16[4,48,2,1,128]{4,2,1,0,3:T(2,128)(2,1)S(1)} collective-permute-done((bf16[4,48,2,1,128]{4,2,1,0,3:T(2,128)(2,1)S(1)}, bf16[4,48,2,1,128]{4,2,1,0,3:T(2,128)(2,1)S(1)}, u32[]{:S(2)}, u32[]{:S(2)}) %collective-permute-start.38) | collective-permute-done | bytes 98336 | tf_op jit(solution)/shard_map/ppermute | solution.py:17
  218.0 6.0 %collective-permute-done.40 = bf16[12,48,256]{2,1,0:T(8,128)(2,1)S(1)} collective-permute-done((bf16[12,48,256]{2,1,0:T(8,128)(2,1)S(1)}, bf16[12,48,256]{2,1,0:T(8,128)(2,1)S(1)}, u32[]{:S(2)}, u32[]{:S(2)}) %collective-permute-start.40) | collective-permute-done | bytes 294944 | tf_op jit(solution)/shard_map/ppermute | solution.py:13
  225.5 1.6 collective-permute-start.43
  227.2 3.5 %collective-permute-done.42 = bf16[4,48,2,1,128]{4,2,1,0,3:T(2,128)(2,1)S(1)} collective-permute-done((bf16[4,48,2,1,128]{4,2,1,0,3:T(2,128)(2,1)S(1)}, bf16[4,48,2,1,128]{4,2,1,0,3:T(2,128)(2,1)S(1)}, u32[]{:S(2)}, u32[]{:S(2)}) %collective-permute-start.42) | collective-permute-done | bytes 98336 | tf_op jit(solution)/shard_map/ppermute | solution.py:17
  235.2 2.1 copy.19
  (176 shorter events, 44.0 us)
Async XLA Ops:
  2.2 17.5 %collective-permute-start.15 = (bf16[1024,128]{1,0:T(8,128)(2,1)S(1)}, bf16[1024,128]{1,0:T(8,128)(2,1)S(1)}, u32[]{:S(2)}, u32[]{:S(2)}) collective-permute-start(bf16[1024,128]{1,0:T(8,128)(2,1)S(1)} %get-tuple-element.826), channel_id=1, source_target_pairs={{0,0},{1,4},{2,12},{3,8},{4,1},{5,5},{6,13},{7,9},{8,2},{9,6},{10,... | collective-permute-start | bytes 786440 | tf_op jit(solution)/shard_map/ppermute | solution.py:142
  2.9 18.5 %collective-permute-start.16 = (bf16[1024,128]{1,0:T(8,128)(2,1)S(1)}, bf16[1024,128]{1,0:T(8,128)(2,1)}, u32[]{:S(2)}, u32[]{:S(2)}) collective-permute-start(bf16[1024,128]{1,0:T(8,128)(2,1)S(1)} %get-tuple-element.825), channel_id=1, source_target_pairs={{0,8},{4,12},{8,0},{12,4},{1,9},{5,13},{9,1},{13,5},{2,10},{6,14},... | collective-permute-start | bytes 786440 | tf_op jit(solution)/shard_map/ppermute | solution.py:17
  9.7 17.3 %collective-permute-start.17 = (bf16[1024,128]{1,0:T(8,128)(2,1)S(1)}, bf16[1024,128]{1,0:T(8,128)(2,1)}, u32[]{:S(2)}, u32[]{:S(2)}) collective-permute-start(bf16[1024,128]{1,0:T(8,128)(2,1)S(1)} %get-tuple-element.823), channel_id=1, source_target_pairs={{0,8},{4,12},{8,0},{12,4},{1,9},{5,13},{9,1},{13,5},{2,10},{6,14},... | collective-permute-start | bytes 786440 | tf_op jit(solution)/shard_map/ppermute | solution.py:17
  9.8 10.0 %collective-permute-start.14 = (bf16[2048]{0:T(1024)(128)(2,1)}, bf16[2048]{0:T(1024)(128)(2,1)S(1)}, u32[]{:S(2)}, u32[]{:S(2)}) collective-permute-start(bf16[2048]{0:T(1024)(128)(2,1)} %param.16), channel_id=1, source_target_pairs={{0,0},{1,4},{2,8},{3,12},{4,1},{5,5},{6,9},{7,13},{8,2},{9,6},{10,... | collective-permute-start | bytes 12296 | tf_op jit(solution)/shard_map/ppermute | solution.py:142
  11.1 21.1 %copy-start.3 = (bf16[2048,512]{1,0:T(8,128)(2,1)S(1)}, bf16[2048,512]{1,0:T(8,128)(2,1)}, u32[]{:S(2)}) copy-start(bf16[2048,512]{1,0:T(8,128)(2,1)} %param.17) | copy-start | bytes 6291460
  27.0 11.9 %collective-permute-start.18 = (bf16[1024,128]{1,0:T(8,128)(2,1)}, bf16[1024,128]{1,0:T(8,128)(2,1)S(1)}, u32[]{:S(2)}, u32[]{:S(2)}) collective-permute-start(bf16[1024,128]{1,0:T(8,128)(2,1)} %collective-permute-done.16), channel_id=1, source_target_pairs={{0,2},{1,6},{2,14},{3,10},{4,3},{5,7},{6,15},{7,11},{8,0},{9,4},{1... | collective-permute-start | bytes 786440 | tf_op jit(solution)/shard_map/ppermute | solution.py:142
  28.8 10.1 %collective-permute-start.19 = (bf16[1024,128]{1,0:T(8,128)(2,1)S(1)}, bf16[1024,128]{1,0:T(8,128)(2,1)S(1)}, u32[]{:S(2)}, u32[]{:S(2)}) collective-permute-start(bf16[1024,128]{1,0:T(8,128)(2,1)S(1)} %get-tuple-element.655), channel_id=1, source_target_pairs={{0,0},{1,4},{2,12},{3,8},{4,1},{5,5},{6,13},{7,9},{8,2},{9,6},{10,... | collective-permute-start | bytes 786440 | tf_op jit(solution)/shard_map/ppermute | solution.py:142
  29.5 14.5 %collective-permute-start.20 = (bf16[1024,128]{1,0:T(8,128)(2,1)S(1)}, bf16[1024,128]{1,0:T(8,128)(2,1)S(1)}, u32[]{:S(2)}, u32[]{:S(2)}) collective-permute-start(bf16[1024,128]{1,0:T(8,128)(2,1)S(1)} %collective-permute-done.15), channel_id=1, source_target_pairs={{0,8},{4,12},{8,0},{12,4},{1,9},{5,13},{9,1},{13,5},{2,10},{6,14},... | collective-permute-start | bytes 786440 | tf_op jit(solution)/shard_map/ppermute | solution.py:17
  44.1 9.5 %collective-permute-start.22 = (bf16[1024,256]{1,0:T(8,128)(2,1)S(1)}, bf16[1024,256]{1,0:T(8,128)(2,1)S(1)}, u32[]{:S(2)}, u32[]{:S(2)}) collective-permute-start(bf16[1024,256]{1,0:T(8,128)(2,1)S(1)} %pad_maximum_fusion.9.near_ours), channel_id=1, source_target_pairs={{0,4},{4,0},{8,12},{12,8},{1,5},{5,1},{9,13},{13,9},{2,6},{6,2},{1... | collective-permute-start | bytes 1572872 | tf_op jit(solution)/shard_map/ppermute | solution.py:17
  44.9 8.8 %collective-permute-start.21 = (bf16[1024,128]{1,0:T(8,128)(2,1)S(1)}, bf16[1024,128]{1,0:T(8,128)(2,1)S(1)}, u32[]{:S(2)}, u32[]{:S(2)}) collective-permute-start(bf16[1024,128]{1,0:T(8,128)(2,1)S(1)} %collective-permute-done.18), channel_id=1, source_target_pairs={{0,8},{4,12},{8,0},{12,4},{1,9},{5,13},{9,1},{13,5},{2,10},{6,14},... | collective-permute-start | bytes 786440 | tf_op jit(solution)/shard_map/ppermute | solution.py:17
  53.8 2.1 collective-permute-start.23
  53.9 2.0 collective-permute-start.25
  54.4 12.1 %collective-permute-start.24 = (bf16[1024,128]{1,0:T(8,128)(2,1)}, bf16[1024,128]{1,0:T(8,128)(2,1)S(1)}, u32[]{:S(2)}, u32[]{:S(2)}) collective-permute-start(bf16[1024,128]{1,0:T(8,128)(2,1)} %collective-permute-done.17), channel_id=1, source_target_pairs={{0,2},{1,6},{2,14},{3,10},{4,3},{5,7},{6,15},{7,11},{8,0},{9,4},{1... | collective-permute-start | bytes 786440 | tf_op jit(solution)/shard_map/ppermute | solution.py:142
  67.1 35.8 %collective-permute-start.26 = (bf16[1920,128]{1,0:T(8,128)(2,1)}, bf16[1920,128]{1,0:T(8,128)(2,1)}, u32[]{:S(2)}, u32[]{:S(2)}) collective-permute-start(bf16[1920,128]{1,0:T(8,128)(2,1)} %get-tuple-element.669), channel_id=1, source_target_pairs={{0,2},{1,3},{2,0},{3,1},{4,6},{5,7},{6,4},{7,5},{8,10},{9,11},{10,... | collective-permute-start | bytes 1474568 | tf_op jit(solution)/shard_map/ppermute | solution.py:17
  68.4 34.5 %collective-permute-start.27 = (bf16[1920,128]{1,0:T(8,128)(2,1)}, bf16[1920,128]{1,0:T(8,128)(2,1)}, u32[]{:S(2)}, u32[]{:S(2)}) collective-permute-start(bf16[1920,128]{1,0:T(8,128)(2,1)} %get-tuple-element.670), channel_id=1, source_target_pairs={{0,3},{1,2},{2,1},{3,0},{4,7},{5,6},{6,5},{7,4},{8,11},{9,10},{10,... | collective-permute-start | bytes 1474568 | tf_op jit(solution)/shard_map/ppermute | solution.py:17
  74.4 28.4 %copy-start.16 = (s32[4,4]{1,0:T(4,128)S(1)}, s32[4,4]{1,0:T(4,128)}, u32[]{:S(2)}) copy-start(s32[4,4]{1,0:T(4,128)} %param.19) | copy-start | bytes 196
  74.4 28.5 %copy-start.18 = (s32[4]{0:T(128)S(1)}, s32[4]{0:T(128)}, u32[]{:S(2)}) copy-start(s32[4]{0:T(128)} %param.21) | copy-start | bytes 52
  74.4 14.9 %collective-permute-start = (bf16[1024,128]{1,0:T(8,128)(2,1)S(1)}, bf16[1024,128]{1,0:T(8,128)(2,1)S(1)}, u32[]{:S(2)}, u32[]{:S(2)}) collective-permute-start(bf16[1024,128]{1,0:T(8,128)(2,1)S(1)} %copy.33), channel_id=1, source_target_pairs={{0,8},{4,12},{8,0},{12,4},{1,9},{5,13},{9,1},{13,5},{2,10},{6,14},... | collective-permute-start | bytes 786440 | tf_op jit(solution)/shard_map/while/body/ppermute | solution.py:17
  75.9 13.4 %collective-permute-start.1 = (bf16[1024,128]{1,0:T(8,128)(2,1)S(1)}, bf16[1024,128]{1,0:T(8,128)(2,1)S(1)}, u32[]{:S(2)}, u32[]{:S(2)}) collective-permute-start(bf16[1024,128]{1,0:T(8,128)(2,1)S(1)} %copy.34), channel_id=1, source_target_pairs={{0,8},{4,12},{8,0},{12,4},{1,9},{5,13},{9,1},{13,5},{2,10},{6,14},... | collective-permute-start | bytes 786440 | tf_op jit(solution)/shard_map/while/body/ppermute | solution.py:17
  77.4 11.8 %collective-permute-start.2 = (f32[1,512]{1,0:T(1,128)S(1)}, f32[1,512]{1,0:T(1,128)S(1)}, u32[]{:S(2)}, u32[]{:S(2)}) collective-permute-start(f32[1,512]{1,0:T(1,128)S(1)} %copy.35), channel_id=1, source_target_pairs={{0,8},{4,12},{8,0},{12,4},{1,9},{5,13},{9,1},{13,5},{2,10},{6,14},... | collective-permute-start | bytes 6152 | tf_op jit(solution)/shard_map/while/body/ppermute | solution.py:17
  90.0 1.9 collective-permute-start.3
  90.1 2.5 %collective-permute-start.4 = (bf16[1024,256]{1,0:T(8,128)(2,1)S(1)}, bf16[1024,256]{1,0:T(8,128)(2,1)S(1)}, u32[]{:S(2)}, u32[]{:S(2)}) collective-permute-start(bf16[1024,256]{1,0:T(8,128)(2,1)S(1)} %pad_maximum_fusion.20.near_others), channel_id=1, source_target_pairs={{0,4},{4,0},{8,12},{12,8},{1,5},{5,1},{9,13},{13,9},{2,6},{6,2},{1... | collective-permute-start | bytes 1572872 | tf_op jit(solution)/shard_map/while/body/ppermute | solution.py:17
  102.7 19.2 %copy-start.14 = (f32[1,512]{1,0:T(1,128)S(1)}, f32[1,512]{1,0:T(1,128)}, u32[]{:S(2)}) copy-start(f32[1,512]{1,0:T(1,128)} %get-tuple-element.697) | copy-start | bytes 6148
  102.7 13.6 %collective-permute-start.28 = (bf16[1920,128]{1,0:T(8,128)(2,1)}, bf16[1920,128]{1,0:T(8,128)(2,1)S(1)}, u32[]{:S(2)}, u32[]{:S(2)}) collective-permute-start(bf16[1920,128]{1,0:T(8,128)(2,1)} %copy-done), channel_id=1, source_target_pairs={{0,1},{1,0},{2,3},{3,2},{4,5},{5,4},{6,7},{7,6},{8,9},{9,8},{10,11... | collective-permute-start | bytes 1474568 | tf_op jit(solution)/shard_map/ppermute | solution.py:17
  116.3 39.1 %collective-permute-start.29 = (bf16[1920,128]{1,0:T(8,128)(2,1)}, bf16[1920,128]{1,0:T(8,128)(2,1)S(1)}, u32[]{:S(2)}, u32[]{:S(2)}) collective-permute-start(bf16[1920,128]{1,0:T(8,128)(2,1)} %get-tuple-element.685), channel_id=1, source_target_pairs={{0,2},{1,3},{2,0},{3,1},{4,6},{5,7},{6,4},{7,5},{8,10},{9,11},{10,... | collective-permute-start | bytes 1474568 | tf_op jit(solution)/shard_map/ppermute | solution.py:17
  117.3 38.0 %collective-permute-start.30 = (bf16[1920,128]{1,0:T(8,128)(2,1)}, bf16[1920,128]{1,0:T(8,128)(2,1)}, u32[]{:S(2)}, u32[]{:S(2)}) collective-permute-start(bf16[1920,128]{1,0:T(8,128)(2,1)} %get-tuple-element.686), channel_id=1, source_target_pairs={{0,3},{1,2},{2,1},{3,0},{4,7},{5,6},{6,5},{7,4},{8,11},{9,10},{10,... | collective-permute-start | bytes 1474568 | tf_op jit(solution)/shard_map/ppermute | solution.py:17
  118.9 36.4 %collective-permute-start.31 = (bf16[1920,128]{1,0:T(8,128)(2,1)}, bf16[1920,128]{1,0:T(8,128)(2,1)}, u32[]{:S(2)}, u32[]{:S(2)}) collective-permute-start(bf16[1920,128]{1,0:T(8,128)(2,1)} %get-tuple-element.687), channel_id=1, source_target_pairs={{0,1},{1,0},{2,3},{3,2},{4,5},{5,4},{6,7},{7,6},{8,9},{9,8},{10,11... | collective-permute-start | bytes 1474568 | tf_op jit(solution)/shard_map/ppermute | solution.py:17
  121.9 11.7 %collective-permute-start.5 = (bf16[1920,128]{1,0:T(8,128)(2,1)S(1)}, bf16[1920,128]{1,0:T(8,128)(2,1)S(1)}, u32[]{:S(2)}, u32[]{:S(2)}) collective-permute-start(bf16[1920,128]{1,0:T(8,128)(2,1)S(1)} %copy.54), channel_id=1, source_target_pairs={{0,8},{4,12},{8,0},{12,4},{1,9},{5,13},{9,1},{13,5},{2,10},{6,14},... | collective-permute-start | bytes 1474568 | tf_op jit(solution)/shard_map/while/body/ppermute | solution.py:17
  122.3 11.4 %collective-permute-start.6 = (bf16[1920,128]{1,0:T(8,128)(2,1)S(1)}, bf16[1920,128]{1,0:T(8,128)(2,1)S(1)}, u32[]{:S(2)}, u32[]{:S(2)}) collective-permute-start(bf16[1920,128]{1,0:T(8,128)(2,1)S(1)} %copy.54), channel_id=1, source_target_pairs={{0,16},{16,0},{1,17},{17,1},{2,18},{18,2},{3,19},{19,3},{4,20},{20... | collective-permute-start | bytes 1474568 | tf_op jit(solution)/shard_map/while/body/ppermute | solution.py:17
  133.9 13.7 %collective-permute-start.8 = (bf16[1920,256]{1,0:T(8,128)(2,1)S(1)}, bf16[1920,256]{1,0:T(8,128)(2,1)}, u32[]{:S(2)}, u32[]{:S(2)}) collective-permute-start(bf16[1920,256]{1,0:T(8,128)(2,1)S(1)} %pad_maximum_fusion.21), channel_id=1, source_target_pairs={{0,4},{4,0},{8,12},{12,8},{1,5},{5,1},{9,13},{13,9},{2,6},{6,2},{1... | collective-permute-start | bytes 2949128 | tf_op jit(solution)/shard_map/while/body/ppermute | solution.py:17
  134.0 13.6 %collective-permute-start.7 = (bf16[1920,128]{1,0:T(8,128)(2,1)S(1)}, bf16[1920,128]{1,0:T(8,128)(2,1)S(1)}, u32[]{:S(2)}, u32[]{:S(2)}) collective-permute-start(bf16[1920,128]{1,0:T(8,128)(2,1)S(1)} %collective-permute-done.6), channel_id=1, source_target_pairs={{0,8},{4,12},{8,0},{12,4},{1,9},{5,13},{9,1},{13,5},{2,10},{6,14},... | collective-permute-start | bytes 1474568 | tf_op jit(solution)/shard_map/while/body/ppermute | solution.py:17
  147.8 4.7 %collective-permute-start.9 = (bf16[1920,256]{1,0:T(8,128)(2,1)S(1)}, bf16[1920,256]{1,0:T(8,128)(2,1)S(1)}, u32[]{:S(2)}, u32[]{:S(2)}) collective-permute-start(bf16[1920,256]{1,0:T(8,128)(2,1)S(1)} %pad_maximum_fusion.22), channel_id=1, source_target_pairs={{0,4},{4,0},{8,12},{12,8},{1,5},{5,1},{9,13},{13,9},{2,6},{6,2},{1... | collective-permute-start | bytes 2949128 | tf_op jit(solution)/shard_map/while/body/ppermute | solution.py:17
  157.1 14.7 %collective-permute-start.33 = (bf16[1920,128]{1,0:T(8,128)(2,1)S(1)}, bf16[1920,128]{1,0:T(8,128)(2,1)S(1)}, u32[]{:S(2)}, u32[]{:S(2)}) collective-permute-start(bf16[1920,128]{1,0:T(8,128)(2,1)S(1)} %add_convert_fusion), channel_id=1, source_target_pairs={{0,8},{4,12},{8,0},{12,4},{1,9},{5,13},{9,1},{13,5},{2,10},{6,14},... | collective-permute-start | bytes 1474568 | tf_op jit(solution)/shard_map/ppermute | solution.py:17
  158.8 13.3 %collective-permute-start.34 = (bf16[1920,128]{1,0:T(8,128)(2,1)S(1)}, bf16[1920,128]{1,0:T(8,128)(2,1)S(1)}, u32[]{:S(2)}, u32[]{:S(2)}) collective-permute-start(bf16[1920,128]{1,0:T(8,128)(2,1)S(1)} %add_convert_fusion), channel_id=1, source_target_pairs={{0,16},{16,0},{1,17},{17,1},{2,18},{18,2},{3,19},{19,3},{4,20},{20... | collective-permute-start | bytes 1474568 | tf_op jit(solution)/shard_map/ppermute | solution.py:17
  160.4 11.3 %collective-permute-start.32 = (bf16[12,48,256]{2,1,0:T(8,128)(2,1)S(1)}, bf16[12,48,256]{2,1,0:T(8,128)(2,1)S(1)}, u32[]{:S(2)}, u32[]{:S(2)}) collective-permute-start(bf16[12,48,256]{2,1,0:T(8,128)(2,1)S(1)} %copy-done.13), channel_id=1, source_target_pairs={{0,1},{1,2},{2,3},{3,0},{4,5},{5,6},{6,7},{7,4},{8,9},{9,10},{10,1... | collective-permute-start | bytes 884744 | tf_op jit(solution)/shard_map/ppermute | solution.py:13
  173.0 26.2 %collective-permute-start.35 = (bf16[12,48,256]{2,1,0:T(8,128)(2,1)}, bf16[12,48,256]{2,1,0:T(8,128)(2,1)}, u32[]{:S(2)}, u32[]{:S(2)}) collective-permute-start(bf16[12,48,256]{2,1,0:T(8,128)(2,1)} %broadcast_select_fusion.15), channel_id=1, source_target_pairs={{0,2},{1,3},{2,0},{3,1},{4,6},{5,7},{6,4},{7,5},{8,10},{9,11},{10,... | collective-permute-start | bytes 884744 | tf_op jit(solution)/shard_map/ppermute | solution.py:13
  179.1 11.5 %collective-permute-start.12 = (bf16[1920,256]{1,0:T(8,128)(2,1)S(1)}, bf16[1920,256]{1,0:T(8,128)(2,1)}, u32[]{:S(2)}, u32[]{:S(2)}) collective-permute-start(bf16[1920,256]{1,0:T(8,128)(2,1)S(1)} %pad_maximum_fusion.24), channel_id=1, source_target_pairs={{0,4},{4,0},{8,12},{12,8},{1,5},{5,1},{9,13},{13,9},{2,6},{6,2},{1... | collective-permute-start | bytes 2949128 | tf_op jit(solution)/shard_map/while/body/ppermute | solution.py:17
  179.9 8.6 %collective-permute-start.11 = (bf16[960,128]{1,0:T(8,128)(2,1)}, bf16[960,128]{1,0:T(8,128)(2,1)S(1)}, u32[]{:S(2)}, u32[]{:S(2)}) collective-permute-start(bf16[960,128]{1,0:T(8,128)(2,1)} %slice.143), channel_id=1, source_target_pairs={{0,8},{4,12},{8,0},{12,4},{1,9},{5,13},{9,1},{13,5},{2,10},{6,14},... | collective-permute-start | bytes 737288 | tf_op jit(solution)/shard_map/while/body/ppermute | solution.py:17
  182.3 8.3 %collective-permute-start.10 = (bf16[960,128]{1,0:T(8,128)(2,1)}, bf16[960,128]{1,0:T(8,128)(2,1)S(1)}, u32[]{:S(2)}, u32[]{:S(2)}) collective-permute-start(bf16[960,128]{1,0:T(8,128)(2,1)} %slice.142), channel_id=1, source_target_pairs={{0,16},{16,0},{1,17},{17,1},{2,18},{18,2},{3,19},{19,3},{4,20},{20... | collective-permute-start | bytes 737288 | tf_op jit(solution)/shard_map/while/body/ppermute | solution.py:17
  190.8 5.9 %collective-permute-start.13 = (bf16[1920,256]{1,0:T(8,128)(2,1)S(1)}, bf16[1920,256]{1,0:T(8,128)(2,1)S(1)}, u32[]{:S(2)}, u32[]{:S(2)}) collective-permute-start(bf16[1920,256]{1,0:T(8,128)(2,1)S(1)} %pad_maximum_fusion.25), channel_id=1, source_target_pairs={{0,4},{4,0},{8,12},{12,8},{1,5},{5,1},{9,13},{13,9},{2,6},{6,2},{1... | collective-permute-start | bytes 2949128 | tf_op jit(solution)/shard_map/while/body/ppermute | solution.py:17
  200.6 10.3 %collective-permute-start.36 = (bf16[12,48,256]{2,1,0:T(8,128)(2,1)S(1)}, bf16[12,48,256]{2,1,0:T(8,128)(2,1)S(1)}, u32[]{:S(2)}, u32[]{:S(2)}) collective-permute-start(bf16[12,48,256]{2,1,0:T(8,128)(2,1)S(1)} %copy-done.12), channel_id=1, source_target_pairs={{0,1},{1,2},{2,3},{3,0},{4,5},{5,6},{6,7},{7,4},{8,9},{9,10},{10,1... | collective-permute-start | bytes 884744 | tf_op jit(solution)/shard_map/ppermute | solution.py:13
  211.0 13.0 %collective-permute-start.40 = (bf16[12,48,256]{2,1,0:T(8,128)(2,1)S(1)}, bf16[12,48,256]{2,1,0:T(8,128)(2,1)S(1)}, u32[]{:S(2)}, u32[]{:S(2)}) collective-permute-start(bf16[12,48,256]{2,1,0:T(8,128)(2,1)S(1)} %broadcast_select_fusion.14), channel_id=1, source_target_pairs={{0,2},{1,3},{2,0},{3,1},{4,6},{5,7},{6,4},{7,5},{8,10},{9,11},{10,... | collective-permute-start | bytes 884744 | tf_op jit(solution)/shard_map/ppermute | solution.py:13
  211.0 1.9 collective-permute-start.37
  211.1 5.7 %collective-permute-start.38 = (bf16[4,48,2,1,128]{4,2,1,0,3:T(2,128)(2,1)S(1)}, bf16[4,48,2,1,128]{4,2,1,0,3:T(2,128)(2,1)S(1)}, u32[]{:S(2)}, u32[]{:S(2)}) collective-permute-start(bf16[4,48,2,1,128]{4,2,1,0,3:T(2,128)(2,1)S(1)} %squeeze.30), channel_id=1, source_target_pairs={{0,8},{4,12},{8,0},{12,4},{1,9},{5,13},{9,1},{13,5},{2,10},{6,14},... | collective-permute-start | bytes 294920 | tf_op jit(solution)/shard_map/ppermute | solution.py:17
  211.5 6.4 %collective-permute-start.39 = (bf16[4,48,2,1,128]{4,2,1,0,3:T(2,128)(2,1)S(1)}, bf16[4,48,2,1,128]{4,2,1,0,3:T(2,128)(2,1)S(1)}, u32[]{:S(2)}, u32[]{:S(2)}) collective-permute-start(bf16[4,48,2,1,128]{4,2,1,0,3:T(2,128)(2,1)S(1)} %squeeze.31), channel_id=1, source_target_pairs={{0,12},{4,8},{8,4},{12,0},{1,13},{5,9},{9,5},{13,1},{2,14},{6,10},... | collective-permute-start | bytes 294920 | tf_op jit(solution)/shard_map/ppermute | solution.py:17
  224.8 2.4 %collective-permute-start.41 = (bf16[4,48,2,1,128]{4,2,1,0,3:T(2,128)(2,1)S(1)}, bf16[4,48,2,1,128]{4,2,1,0,3:T(2,128)(2,1)S(1)}, u32[]{:S(2)}, u32[]{:S(2)}) collective-permute-start(bf16[4,48,2,1,128]{4,2,1,0,3:T(2,128)(2,1)S(1)} %squeeze.33), channel_id=1, source_target_pairs={{0,4},{4,0},{8,12},{12,8},{1,5},{5,1},{9,13},{13,9},{2,6},{6,2},{1... | collective-permute-start | bytes 294920 | tf_op jit(solution)/shard_map/ppermute | solution.py:17
  225.0 5.7 %collective-permute-start.42 = (bf16[4,48,2,1,128]{4,2,1,0,3:T(2,128)(2,1)S(1)}, bf16[4,48,2,1,128]{4,2,1,0,3:T(2,128)(2,1)S(1)}, u32[]{:S(2)}, u32[]{:S(2)}) collective-permute-start(bf16[4,48,2,1,128]{4,2,1,0,3:T(2,128)(2,1)S(1)} %squeeze.34), channel_id=1, source_target_pairs={{0,8},{4,12},{8,0},{12,4},{1,9},{5,13},{9,1},{13,5},{2,10},{6,14},... | collective-permute-start | bytes 294920 | tf_op jit(solution)/shard_map/ppermute | solution.py:17
  225.5 6.4 %collective-permute-start.43 = (bf16[4,48,2,1,128]{4,2,1,0,3:T(2,128)(2,1)S(1)}, bf16[4,48,2,1,128]{4,2,1,0,3:T(2,128)(2,1)S(1)}, u32[]{:S(2)}, u32[]{:S(2)}) collective-permute-start(bf16[4,48,2,1,128]{4,2,1,0,3:T(2,128)(2,1)S(1)} %squeeze.35), channel_id=1, source_target_pairs={{0,12},{4,8},{8,4},{12,0},{1,13},{5,9},{9,5},{13,1},{2,14},{6,10},... | collective-permute-start | bytes 294920 | tf_op jit(solution)/shard_map/ppermute | solution.py:17
  (15 other events, 67.0 us)

commit v11 on v9

--- a/solution.py
+++ b/solution.py
@@ -1,6 +1,8 @@
 import jax
 import jax.numpy as jnp
 from jax import lax
+from jax.experimental import pallas as pl
+from jax.experimental.pallas import tpu as pltpu
 from jax.sharding import PartitionSpec as P
 
 eps_norm = 1e-05
@@ -71,6 +73,40 @@
     return gathered_rows[None, None]
 
 
+def terms_body(choice, weight, near, far, terms):
+    near_product = add_columns(weight[...], near[...])
+    far_product = add_columns(weight[...], far[...])
+    width = terms.shape[2]
+    terms[choice[0]] = near_product[:, :width].astype(terms.dtype)
+    terms[choice[1]] = near_product[:, width:].astype(terms.dtype)
+    terms[choice[2]] = far_product[:, :width].astype(terms.dtype)
+    terms[choice[3]] = far_product[:, width:].astype(terms.dtype)
+
+
+def product_terms(choice, weight, near, far):
+    depth, rows = weight.shape
+    columns = near.shape[1]
+    width = columns // 2
+    tall = 640 if depth % 640 == 0 else depth
+    whole = pl.BlockSpec((rows, columns), lambda i, choice: (0, 0))
+    return pl.pallas_call(
+        terms_body,
+        out_shape=jax.ShapeDtypeStruct((4, depth, width), jnp.bfloat16),
+        grid_spec=pltpu.PrefetchScalarGridSpec(
+            num_scalar_prefetch=1,
+            grid=(depth // tall,),
+            in_specs=[pl.BlockSpec((tall, rows), lambda i, choice: (i, 0)), whole, whole],
+            out_specs=pl.BlockSpec((4, tall, width), lambda i, choice: (0, i, 0)),
+        ),
+        compiler_params=pltpu.CompilerParams(vmem_limit_bytes=32 * 1024 * 1024),
+        cost_estimate=pl.CostEstimate(
+            flops=4 * depth * rows * columns,
+            bytes_accessed=2 * depth * rows + 4 * rows * columns + 8 * depth * width,
+            transcendentals=0,
+        ),
+    )(choice, weight, near, far)
+
+
 def product_plan(
     features, proj_weight, proj_bias, kv_weight, key_gain, tile_map, tile_count, decode_owner
 ):
@@ -82,7 +118,6 @@
     most_tiles = tile_map.shape[1]
     group, tile, head = (lax.axis_index(name) for name in ("groups", "tile", "head"))
     first_core, first_chip = tile % 2 == 0, tile < 2
-    at_end = (head == 0) | (head == 3)
     feature_rows = features.reshape(token_rows, feature_width)
     step = lax.optimization_barrier
 
@@ -109,25 +144,17 @@
     def both_heads(ours, theirs):
         return put_first(group == 0, ours, theirs, 1)
 
+    outer = jnp.where(head < 2, jnp.array([0, 3]), jnp.array([3, 0]))
+    inner = jnp.where(head < 2, jnp.array([1, 2]), jnp.array([2, 1]))
+    choice = jnp.where(
+        first_core, jnp.concatenate([outer, inner]), jnp.concatenate([inner, outer])
+    ).astype(jnp.int32)
+
     def products(near, far):
-        both = add_columns(proj_weight, jnp.concatenate([near, far], axis=1))
-        near_0, near_1, far_0, far_1 = (both[:, k * width : (k + 1) * width] for k in range(4))
-        near_kept = at_end == first_core
-        parts = (
-            jnp.where(near_kept, far_1, near_1),
-            jnp.where(near_kept, near_1, far_1),
-            jnp.where(near_kept, far_0, near_0),
-        )
-        own = jnp.where(near_kept, near_0, far_0)
-        return own, tuple(part.astype(jnp.bfloat16) for part in parts)
-
-    def exchange(parts):
-        return tuple(swapped(part, "head", bit) for part, bit in zip(parts, (2, 3, 1)))
-
-    def summed(own, arrived):
-        for block in arrived:
-            own = own + block.astype(jnp.float32)
-        return own.astype(jnp.bfloat16)
+        return product_terms(choice, proj_weight, near, far)
+
+    def summed(terms):
+        return lax.psum_scatter(terms, "head", scatter_dimension=0)
 
     once = jnp.minimum(jnp.max(tile_count), 1)
 
@@ -179,10 +206,9 @@
     bias_rows = moved(proj_bias, lambda t, h: (h, t))
     key_block = moved(key_mine, lambda t, h: (h // 2 * 2 + outer_core(h), t))
     comes = swapped(leaves, "tile", 2)
-    no_block = jnp.zeros((depth, width), jnp.float32)
-    no_terms = no_block, tuple(jnp.zeros((depth, width), jnp.bfloat16) for _ in range(3))
+    no_terms = jnp.zeros((4, depth, width), jnp.bfloat16)
     no_tokens = tuple(
-        jnp.zeros((tile_slots, shard_len, 2 * width), jnp.bfloat16) for _ in range(2)
+        jnp.full((tile_slots, shard_len, 2 * width), k, jnp.bfloat16) for k in range(2)
     )
     bias_rows, key_block, comes, stays, feature_parts, no_terms, no_tokens, once = step(
         (bias_rows, key_block, comes, stays, feature_parts, no_terms, no_tokens, once)
@@ -203,9 +229,9 @@
     key_near = put_first(tile // 2 == head // 2, key_block, key_other, 1)
     value_half = jnp.concatenate(value_pieces, axis=1)
     key_near, value_half = step((key_near, value_half))
-    own, parts = products(key_near, swapped(key_near, "tile", 1))
+    terms = products(key_near, swapped(key_near, "tile", 1))
     bias_part = bias_part + swapped(bias_part, "tile", 1)
-    own, parts, value_half, bias_part = step((own, parts, value_half, bias_part))
+    terms, value_half, bias_part = step((terms, value_half, bias_part))
 
     def values_terms(given):
         value_half, bias_part = given
@@ -215,11 +241,8 @@
         return (other, bias_other), (terms, bias_part + bias_other)
 
     empty = no_terms, bias_part
-    arrived, beside = step(
-        (exchange(parts), in_loop(values_terms, (value_half, bias_part), empty))
-    )
-    own = summed(own, arrived)
-    (value_own, parts), bias_part = beside
+    own, beside = step((summed(terms), in_loop(values_terms, (value_half, bias_part), empty)))
+    terms, bias_part = beside
     bias_part = bias_part.reshape(2, layers, 2, head_dim)
 
     def keys_product(own):
@@ -230,8 +253,7 @@
         rows = [rows_0, rows_1, rows_2, swapped(rows_2, "tile", 1)]
         return across_x, finish(times_features(rows, feature_parts), 0)
 
-    arrived, keys = step((exchange(parts), in_loop(keys_product, own, no_tokens[0])))
-    own = summed(value_own, arrived)
+    own, keys = step((summed(terms), in_loop(keys_product, own, no_tokens[0])))
 
     shifted, across_x, across_y = step(
         (shifted_2(keys, "head", 1), swapped(own, "tile", 2), swapped(own, "groups", 1))

time: 234 us -> 237 us (1.013)
  waiting for transfers between devices: 93.8 us -> 115 us
  starting transfers between devices: 64.2 us -> 43.6 us
  Pallas kernels: 0 us -> 16.5 us
  matrix products: 24.3 us -> 9.92 us
  between operations: 1.06 us -> 14.4 us
  other arithmetic: 19.8 us -> 13.1 us
  local copies, waits for them, and re-layouts: 29.4 us -> 23.6 us
    ppermute x30 -> x24, starting transfers between devices: 51.2 us -> 30.6 us  [swapped(): lax.ppermute(shard, axis, [(i, i ^ bit) for i in range(lax.axis_size(axis...]
    reduce_scatter x0 -> x2, waiting for transfers between devices: none -> 19.4 us  [summed(): return lax.psum_scatter(terms, 'head', scatter_dimension=0)]
    pallas_call x0 -> x2, Pallas kernels: none -> 16.5 us  [product_terms(): pl.pallas_call(terms_body, out_shape=jax.ShapeDtypeStruct((4, depth, widt...]
    dot_general x13 -> x11, matrix products: 24.1 us -> 9.73 us  [add_columns(): return jnp.dot(operand, portion, preferred_element_type=jnp.float32)]
    convert_element_type x4 -> x0, other arithmetic: 6.36 us -> none  [the longest x2 3.96 us: summed(): return own.astype(jnp.bfloat16)]
    ppermute x4, starting transfers between devices: 4.12 us -> 9.91 us  [moved(): return lax.ppermute(shard, ('tile', 'head'), pairs)]
    ppermute x4, starting transfers between devices: 8.88 us -> 3.12 us  [shifted_2(): lax.ppermute(shard, axis, [(i, (i + by) % count) for i in range(count)])]
    optimization_barrier x4 -> x0, local copies, waits for them, and re-layouts: 3.32 us -> none  [product_plan(): step((exchange(parts), in_loop(values_terms, (value_half, bias_part), emp...]
  transfers between devices with their start and end apart: 38 -> 34, of which waited for: 20 -> 20; matrix products, arithmetic and copies ran while one was open for 19% -> 14% of each run, Pallas kernels for 0% -> 4%
where the time goes in v11:
time: 237 us; the launch traced here: 236 us
  waiting for transfers between devices  115 us (49%)
  starting transfers between devices  43.6 us (18%)
  local copies, waits for them, and re-layouts  23.6 us (10%)
  Pallas kernels  16.5 us (7%)
  between operations  14.4 us (6%)
  other arithmetic  13.1 us (6%)
  matrix products  9.92 us (4%)
    ppermute x24, waiting for transfers between devices, swapped(): lax.ppermute(shard, axis, [(i, i ^ bit) for i in range(lax.axis_size(axis...  63.7 us
    ppermute x24, starting transfers between devices, swapped(): lax.ppermute(shard, axis, [(i, i ^ bit) for i in range(lax.axis_size(axis...  30.6 us
    ppermute x4, waiting for transfers between devices, shifted_2(): lax.ppermute(shard, axis, [(i, (i + by) % count) for i in range(count)])  22.6 us
    reduce_scatter x2, waiting for transfers between devices, summed(): return lax.psum_scatter(terms, 'head', scatter_dimension=0)  19.4 us
    pallas_call x2, Pallas kernels, product_terms(): pl.pallas_call(terms_body, out_shape=jax.ShapeDtypeStruct((4, depth, widt...  16.5 us
    ppermute x4, starting transfers between devices, moved(): return lax.ppermute(shard, ('tile', 'head'), pairs)  9.91 us
    dot_general x11, matrix products, add_columns(): return jnp.dot(operand, portion, preferred_element_type=jnp.float32)  9.73 us
    ppermute x4, waiting for transfers between devices, moved(): return lax.ppermute(shard, ('tile', 'head'), pairs)  8.73 us
  transfers between devices with their start and end apart: 34, of which 20 were waited for; matrix products, arithmetic and copies ran while one was open for 14% of the time, Pallas kernels for 4%

profile of v11, /device:TPU:0, one launch (start us, length us, event | category | flops | bytes accessed | tf_op | source)
XLA Modules:
  0.0 236.1 jit_solution(13389315886513490278)
XLA Ops:
  6.5 1.3 collective-permute-start.12
  9.7 2.3 fusion.23
  11.9 8.6 %collective-permute-start.14 = (bf16[1024,128]{1,0:T(8,128)(2,1)}, bf16[1024,128]{1,0:T(8,128)(2,1)}, u32[]{:S(2)}, u32[]{:S(2)}) collective-permute-start(bf16[1024,128]{1,0:T(8,128)(2,1)} %get-tuple-element.506), channel_id=1, source_target_pairs={{0,8},{4,12},{8,0},{12,4},{1,9},{5,13},{9,1},{13,5},{2,10},{6,14},... | collective-permute-start | bytes 786440 | tf_op jit(solution)/shard_map/ppermute | solution.py:17
  20.5 7.4 %constant_dynamic-slice_fusion = (bf16[576,1920]{1,0:T(8,128)(2,1)}, bf16[576,1920]{1,0:T(8,128)(2,1)}, bf16[576,1920]{1,0:T(8,128)(2,1)}, bf16[576,1920]{1,0:T(8,128)(2,1)}) fusion(bf16[576,7680]{1,0:T(8,128)(2,1)} %bitcast.139, s32[]{:T(128)S(6)} %select_n.324, s32[]{:T(128)S(6)} %select_n.323, s32[]{:T(128)S(6)} %select_n.322, s32[]{:T(128)S(6)} %select_n.321), kind=kLoop, calls=%fused_computation.98 | loop fusion | bytes 17694736 | tf_op jit(solution)/shard_map/dynamic_slice | solution.py:136
  29.3 5.3 %collective-permute-done.14 = bf16[1024,128]{1,0:T(8,128)(2,1)} collective-permute-done((bf16[1024,128]{1,0:T(8,128)(2,1)}, bf16[1024,128]{1,0:T(8,128)(2,1)}, u32[]{:S(2)}, u32[]{:S(2)}) %collective-permute-start.14) | collective-permute-done | bytes 262176 | tf_op jit(solution)/shard_map/ppermute | solution.py:17
  34.5 2.6 %collective-permute-start.17 = (bf16[2048,128]{1,0:T(8,128)(2,1)S(1)}, bf16[2048,128]{1,0:T(8,128)(2,1)S(1)}, u32[]{:S(2)}, u32[]{:S(2)}) collective-permute-start(bf16[2048,128]{1,0:T(8,128)(2,1)S(1)} %collective-permute-done.13), channel_id=1, source_target_pairs={{0,8},{4,12},{8,0},{12,4},{1,9},{5,13},{9,1},{13,5},{2,10},{6,14},... | collective-permute-start | bytes 1572872 | tf_op jit(solution)/shard_map/ppermute | solution.py:17
  38.8 7.2 %collective-permute-start.16 = (bf16[1024,128]{1,0:T(8,128)(2,1)S(1)}, bf16[1024,128]{1,0:T(8,128)(2,1)S(1)}, u32[]{:S(2)}, u32[]{:S(2)}) collective-permute-start(bf16[1024,128]{1,0:T(8,128)(2,1)S(1)} %get-tuple-element.509), channel_id=1, source_target_pairs={{0,2},{1,6},{2,4},{3,0},{4,3},{5,7},{6,5},{7,1},{8,10},{9,14},{10,... | collective-permute-start | bytes 786440 | tf_op jit(solution)/shard_map/ppermute | solution.py:130
  46.5 8.7 %collective-permute-done.16 = bf16[1024,128]{1,0:T(8,128)(2,1)S(1)} collective-permute-done((bf16[1024,128]{1,0:T(8,128)(2,1)S(1)}, bf16[1024,128]{1,0:T(8,128)(2,1)S(1)}, u32[]{:S(2)}, u32[]{:S(2)}) %collective-permute-start.16) | collective-permute-done | bytes 262176 | tf_op jit(solution)/shard_map/ppermute | solution.py:130
  55.5 3.8 %collective-permute-start.18 = (bf16[2048,256]{1,0:T(8,128)(2,1)S(1)}, bf16[2048,256]{1,0:T(8,128)(2,1)S(1)}, u32[]{:S(2)}, u32[]{:S(2)}) collective-permute-start(bf16[2048,256]{1,0:T(8,128)(2,1)S(1)} %pad_maximum_fusion.7.near), channel_id=1, source_target_pairs={{0,4},{4,0},{8,12},{12,8},{1,5},{5,1},{9,13},{13,9},{2,6},{6,2},{1... | collective-permute-start | bytes 3145736 | tf_op jit(solution)/shard_map/ppermute | solution.py:17
  59.6 2.0 collective-permute-done.19
  61.5 8.2 %shard_map.118 = bf16[4,1920,128]{2,1,0:T(8,128)(2,1)} custom-call(s32[4]{0:T(128)S(1)} %broadcast_select_fusion.36.choice, bf16[1920,2048]{1,0:T(8,128)(2,1)} %weight.1, bf16[2048,256]{1,0:T(8,128)(2,1)S(1)} %pad_maximum_fusion.7.near, bf16[2048,256]{1,0:T(8,128)(2,1)S(1)} %collective-permute-done.18.far), custom_call_target="tpu_custom_call" | custom-call | flops 4026531840 | bytes 11927552 | tf_op jit(solution)/shard_map/pallas_call | solution.py:92
  70.5 1.6 broadcast_in_dim.60
  72.1 25.5 %while.48 = (s32[]{:T(128)}, bf16[1024,256]{1,0:T(8,128)(2,1)S(1)}, f32[1,512]{1,0:T(1,128)S(1)}, bf16[4,1920,128]{2,1,0:T(8,128)(2,1)}, f32[1,512]{1,0:T(1,128)...) while((s32[]{:T(128)}, bf16[1024,256]{1,0:T(8,128)(2,1)S(1)}, ...), condition=%wide.region_4.5_spmd, body=%wide.region_3.4_spmd.sunk | while | flops 4029153792 | bytes 23480540 | solution.py:162
  72.2 1.8 collective-permute-start
  74.3 12.2 %collective-permute-done.1 = f32[1,512]{1,0:T(1,128)S(1)} collective-permute-done((f32[1,512]{1,0:T(1,128)S(1)}, f32[1,512]{1,0:T(1,128)S(1)}, u32[]{:S(2)}, u32[]{:S(2)}) %collective-permute-start.1) | collective-permute-done | bytes 2080 | tf_op jit(solution)/shard_map/while/body/ppermute | solution.py:17
  87.3 2.1 collective-permute-done.2.far
  89.3 8.3 %body.1 = bf16[4,1920,128]{2,1,0:T(8,128)(2,1)} custom-call(s32[4]{0:T(128)S(1)} %get-tuple-element.814.choice, bf16[1920,2048]{1,0:T(8,128)(2,1)} %get-tuple-element.815.weight, bf16[2048,256]{1,0:T(8,128)(2,1)S(1)} %pad_maximum_fusion.17.near, bf16[2048,256]{1,0:T(8,128)(2,1)S(1)} %collective-permute-done.2.far), custom_call_target="tpu_custom_call" | custom-call | flops 4026531840 | bytes 11927552 | tf_op jit(solution)/shard_map/while/body/pallas_call | solution.py:92
  97.6 13.3 %reduce-scatter.3.cloned.1.call-done = bf16[1,1920,128]{2,1,0:T(8,128)(2,1)} async-done(((bf16[4,1920,128]{2,1,0:T(8,128)(2,1)}), bf16[1,1920,128]{2,1,0:T(8,128)(2,1)}) %reduce-scatter.3.cloned.1.call-update) | async-done | bytes 491536 | tf_op jit(solution)/shard_map/reduce_scatter | solution.py:157
  112.0 35.7 %while.49 = (s32[]{:T(128)}, bf16[1920,128]{1,0:T(8,128)(2,1)S(1)}, bf16[12,48,256]{2,1,0:T(8,128)(2,1)}, s32[]{:T(128)}, pred[]{:T(512)}, /*index=5*/bf16[576,1...) while((s32[]{:T(128)}, bf16[1920,128]{1,0:T(8,128)(2,1)S(1)}, ...), condition=%wide.region_9.10_spmd, body=%wide.region_6.9_spmd.sunk | while | flops 2271905024 | bytes 76995496 | solution.py:162
  112.0 1.5 collective-permute-start.3
  113.6 1.5 collective-permute-start.4
  115.1 9.8 %collective-permute-done.3 = bf16[1920,128]{1,0:T(8,128)(2,1)S(1)} collective-permute-done((bf16[1920,128]{1,0:T(8,128)(2,1)S(1)}, bf16[1920,128]{1,0:T(8,128)(2,1)S(1)}, u32[]{:S(2)}, u32[]{:S(2)}) %collective-permute-start.3) | collective-permute-done | bytes 491552 | tf_op jit(solution)/shard_map/while/body/ppermute | solution.py:17
  124.9 1.2 collective-permute-done.4
  127.0 13.0 %collective-permute-done.5 = bf16[1920,128]{1,0:T(8,128)(2,1)S(1)} collective-permute-done((bf16[1920,128]{1,0:T(8,128)(2,1)S(1)}, bf16[1920,128]{1,0:T(8,128)(2,1)S(1)}, u32[]{:S(2)}, u32[]{:S(2)}) %collective-permute-start.5) | collective-permute-done | bytes 491552 | tf_op jit(solution)/shard_map/while/body/ppermute | solution.py:17
  141.9 2.1 convolution_add_fusion.10
  147.7 6.2 %reduce-scatter.5.cloned.1.call-done = bf16[1,1920,128]{2,1,0:T(8,128)(2,1)} async-done(((bf16[4,1920,128]{2,1,0:T(8,128)(2,1)}), bf16[1,1920,128]{2,1,0:T(8,128)(2,1)}) %reduce-scatter.5.cloned.1.call-update) | async-done | bytes 491536 | tf_op jit(solution)/shard_map/reduce_scatter | solution.py:157
  153.9 1.5 collective-permute-start.21
  155.4 1.5 collective-permute-start.22
  157.9 9.2 %collective-permute-done.20 = bf16[12,48,256]{2,1,0:T(8,128)(2,1)S(1)} collective-permute-done((bf16[12,48,256]{2,1,0:T(8,128)(2,1)}, bf16[12,48,256]{2,1,0:T(8,128)(2,1)S(1)}, u32[]{:S(2)}, u32[]{:S(2)}) %collective-permute-start.20) | collective-permute-done | bytes 294944 | tf_op jit(solution)/shard_map/ppermute | solution.py:13
  168.1 1.8 broadcast_select_fusion.15
  169.9 1.9 collective-permute-start.23
  172.5 19.9 %while.50 = (s32[]{:T(128)}, bf16[1920,128]{1,0:T(8,128)(2,1)}, bf16[1920,128]{1,0:T(8,128)(2,1)S(1)}, bf16[1920,128]{1,0:T(8,128)(2,1)S(1)}, bf16[12,48,256]{2,...) while((s32[]{:T(128)}, bf16[1920,128]{1,0:T(8,128)(2,1)}, ...), condition=%wide.region_11.12_spmd, body=%wide.region_10.11_spmd.sunk | while | flops 2271166464 | bytes 79334824 | solution.py:162
  173.8 1.5 collective-permute-start.8
  176.1 6.2 %collective-permute-done.8 = bf16[960,128]{1,0:T(8,128)(2,1)S(1)} collective-permute-done((bf16[960,128]{1,0:T(8,128)(2,1)S(1)}, bf16[960,128]{1,0:T(8,128)(2,1)S(1)}, u32[]{:S(2)}, u32[]{:S(2)}) %collective-permute-start.8) | collective-permute-done | bytes 245792 | tf_op jit(solution)/shard_map/while/body/ppermute | solution.py:17
  182.3 1.3 collective-permute-done.9
  183.9 1.3 copy-done.10
  187.0 2.1 convolution_add_fusion.12
  192.9 1.2 broadcast_select_fusion.13
  195.1 7.7 %collective-permute-done.24 = bf16[12,48,256]{2,1,0:T(8,128)(2,1)S(1)} collective-permute-done((bf16[12,48,256]{2,1,0:T(8,128)(2,1)}, bf16[12,48,256]{2,1,0:T(8,128)(2,1)S(1)}, u32[]{:S(2)}, u32[]{:S(2)}) %collective-permute-start.24) | collective-permute-done | bytes 294944 | tf_op jit(solution)/shard_map/ppermute | solution.py:13
  203.7 1.2 collective-permute-start.27
  205.0 3.8 %collective-permute-done.26 = bf16[4,48,2,1,128]{4,2,1,0,3:T(2,128)(2,1)S(1)} collective-permute-done((bf16[4,48,2,1,128]{4,2,1,0,3:T(2,128)(2,1)S(1)}, bf16[4,48,2,1,128]{4,2,1,0,3:T(2,128)(2,1)S(1)}, u32[]{:S(2)}, u32[]{:S(2)}) %collective-permute-start.26) | collective-permute-done | bytes 98336 | tf_op jit(solution)/shard_map/ppermute | solution.py:17
  208.8 1.2 collective-permute-done.27
  210.0 5.6 %collective-permute-done.28 = bf16[12,48,256]{2,1,0:T(8,128)(2,1)S(1)} collective-permute-done((bf16[12,48,256]{2,1,0:T(8,128)(2,1)S(1)}, bf16[12,48,256]{2,1,0:T(8,128)(2,1)S(1)}, u32[]{:S(2)}, u32[]{:S(2)}) %collective-permute-start.28) | collective-permute-done | bytes 294944 | tf_op jit(solution)/shard_map/ppermute | solution.py:13
  217.4 1.5 collective-permute-start.30
  219.1 2.0 collective-permute-done.31
  221.1 2.7 %collective-permute-done.30 = bf16[4,48,2,1,128]{4,2,1,0,3:T(2,128)(2,1)S(1)} collective-permute-done((bf16[4,48,2,1,128]{4,2,1,0,3:T(2,128)(2,1)S(1)}, bf16[4,48,2,1,128]{4,2,1,0,3:T(2,128)(2,1)S(1)}, u32[]{:S(2)}, u32[]{:S(2)}) %collective-permute-start.30) | collective-permute-done | bytes 98336 | tf_op jit(solution)/shard_map/ppermute | solution.py:17
  226.0 1.1 pad_maximum_fusion.8
  227.2 2.1 copy.23
  (156 shorter events, 30.9 us)
Async XLA Ops:
  6.5 104.3 %reduce-scatter.3.cloned.1.call-start = ((), (), s32[]{:S(2)}) async-start(), calls=%async_computation.2 | async-start | bytes 2457600 | tf_op jit(solution)/shard_map/reduce_scatter | solution.py:157
  6.5 22.7 %collective-permute-start.12 = (bf16[2048]{0:T(1024)(128)(2,1)}, bf16[2048]{0:T(1024)(128)(2,1)S(1)}, u32[]{:S(2)}, u32[]{:S(2)}) collective-permute-start(bf16[2048]{0:T(1024)(128)(2,1)} %param.20), channel_id=1, source_target_pairs={{0,0},{1,4},{2,8},{3,12},{4,1},{5,5},{6,9},{7,13},{8,2},{9,6},{10,... | collective-permute-start | bytes 12296 | tf_op jit(solution)/shard_map/ppermute | solution.py:130
  8.9 25.6 %collective-permute-start.13 = (bf16[2048,128]{1,0:T(8,128)(2,1)S(1)}, bf16[2048,128]{1,0:T(8,128)(2,1)S(1)}, u32[]{:S(2)}, u32[]{:S(2)}) collective-permute-start(bf16[2048,128]{1,0:T(8,128)(2,1)S(1)} %constant_dynamic-slice_fusion.4), channel_id=1, source_target_pairs={{0,0},{1,4},{2,12},{3,8},{4,1},{5,5},{6,13},{7,9},{8,2},{9,6},{10,... | collective-permute-start | bytes 1572872 | tf_op jit(solution)/shard_map/ppermute | solution.py:130
  11.9 22.6 %collective-permute-start.14 = (bf16[1024,128]{1,0:T(8,128)(2,1)}, bf16[1024,128]{1,0:T(8,128)(2,1)}, u32[]{:S(2)}, u32[]{:S(2)}) collective-permute-start(bf16[1024,128]{1,0:T(8,128)(2,1)} %get-tuple-element.506), channel_id=1, source_target_pairs={{0,8},{4,12},{8,0},{12,4},{1,9},{5,13},{9,1},{13,5},{2,10},{6,14},... | collective-permute-start | bytes 786440 | tf_op jit(solution)/shard_map/ppermute | solution.py:17
  20.5 7.4 %copy-start.17 = (s32[4]{0:T(128)S(1)}, s32[4]{0:T(128)}, u32[]{:S(2)}) copy-start(s32[4]{0:T(128)} %param.24) | copy-start | bytes 52
  20.5 25.5 %copy-start.2 = (bf16[2048,512]{1,0:T(8,128)(2,1)S(1)}, bf16[2048,512]{1,0:T(8,128)(2,1)}, u32[]{:S(2)}) copy-start(bf16[2048,512]{1,0:T(8,128)(2,1)} %param.21) | copy-start | bytes 6291460
  34.5 20.7 %collective-permute-start.17 = (bf16[2048,128]{1,0:T(8,128)(2,1)S(1)}, bf16[2048,128]{1,0:T(8,128)(2,1)S(1)}, u32[]{:S(2)}, u32[]{:S(2)}) collective-permute-start(bf16[2048,128]{1,0:T(8,128)(2,1)S(1)} %collective-permute-done.13), channel_id=1, source_target_pairs={{0,8},{4,12},{8,0},{12,4},{1,9},{5,13},{9,1},{13,5},{2,10},{6,14},... | collective-permute-start | bytes 1572872 | tf_op jit(solution)/shard_map/ppermute | solution.py:17
  38.1 8.3 %collective-permute-start.15 = (bf16[1024,128]{1,0:T(8,128)(2,1)S(1)}, bf16[1024,128]{1,0:T(8,128)(2,1)S(1)}, u32[]{:S(2)}, u32[]{:S(2)}) collective-permute-start(bf16[1024,128]{1,0:T(8,128)(2,1)S(1)} %get-tuple-element.510), channel_id=1, source_target_pairs={{0,0},{1,4},{2,6},{3,2},{4,1},{5,5},{6,7},{7,3},{8,8},{9,12},{10,1... | collective-permute-start | bytes 786440 | tf_op jit(solution)/shard_map/ppermute | solution.py:130
  38.8 16.3 %collective-permute-start.16 = (bf16[1024,128]{1,0:T(8,128)(2,1)S(1)}, bf16[1024,128]{1,0:T(8,128)(2,1)S(1)}, u32[]{:S(2)}, u32[]{:S(2)}) collective-permute-start(bf16[1024,128]{1,0:T(8,128)(2,1)S(1)} %get-tuple-element.509), channel_id=1, source_target_pairs={{0,2},{1,6},{2,4},{3,0},{4,3},{5,7},{6,5},{7,1},{8,10},{9,14},{10,... | collective-permute-start | bytes 786440 | tf_op jit(solution)/shard_map/ppermute | solution.py:130
  46.4 12.8 %copy-start.19 = (s32[2]{0:T(128)S(1)}, s32[2]{0:T(128)}, u32[]{:S(2)}) copy-start(s32[2]{0:T(128)} %constant.213.clone) | copy-start | bytes 28
  46.4 12.8 %copy-start.15 = (s32[2]{0:T(128)S(1)}, s32[2]{0:T(128)}, u32[]{:S(2)}) copy-start(s32[2]{0:T(128)} %constant.214.clone) | copy-start | bytes 28
  46.4 12.8 %copy-start.16 = (s32[2]{0:T(128)S(1)}, s32[2]{0:T(128)}, u32[]{:S(2)}) copy-start(s32[2]{0:T(128)} %constant.215.clone) | copy-start | bytes 28
  46.4 13.0 %copy-start.14 = (s32[4,4]{1,0:T(4,128)S(1)}, s32[4,4]{1,0:T(4,128)}, u32[]{:S(2)}) copy-start(s32[4,4]{1,0:T(4,128)} %param.23) | copy-start | bytes 196
  55.5 6.1 %collective-permute-start.18 = (bf16[2048,256]{1,0:T(8,128)(2,1)S(1)}, bf16[2048,256]{1,0:T(8,128)(2,1)S(1)}, u32[]{:S(2)}, u32[]{:S(2)}) collective-permute-start(bf16[2048,256]{1,0:T(8,128)(2,1)S(1)} %pad_maximum_fusion.7.near), channel_id=1, source_target_pairs={{0,4},{4,0},{8,12},{12,8},{1,5},{5,1},{9,13},{13,9},{2,6},{6,2},{1... | collective-permute-start | bytes 3145736 | tf_op jit(solution)/shard_map/ppermute | solution.py:17
  59.3 2.2 collective-permute-start.19
  61.5 8.3 %copy-start.18 = (s32[4]{0:T(128)S(1)}, s32[4]{0:T(128)}, u32[]{:S(2)}) copy-start(s32[4]{0:T(128)} %param.25) | copy-start | bytes 52
  69.8 84.1 %reduce-scatter.5.cloned.1.call-start = ((), (), s32[]{:S(2)}) async-start(), calls=%async_computation.3 | async-start | bytes 2457600 | tf_op jit(solution)/shard_map/reduce_scatter | solution.py:157
  72.2 14.3 %collective-permute-start = (bf16[1024,256]{1,0:T(8,128)(2,1)S(1)}, bf16[1024,256]{1,0:T(8,128)(2,1)S(1)}, u32[]{:S(2)}, u32[]{:S(2)}) collective-permute-start(bf16[1024,256]{1,0:T(8,128)(2,1)S(1)} %copy.33), channel_id=1, source_target_pairs={{0,8},{4,12},{8,0},{12,4},{1,9},{5,13},{9,1},{13,5},{2,10},{6,14},... | collective-permute-start | bytes 1572872 | tf_op jit(solution)/shard_map/while/body/ppermute | solution.py:17
  74.0 12.5 %collective-permute-start.1 = (f32[1,512]{1,0:T(1,128)S(1)}, f32[1,512]{1,0:T(1,128)S(1)}, u32[]{:S(2)}, u32[]{:S(2)}) collective-permute-start(f32[1,512]{1,0:T(1,128)S(1)} %copy.34), channel_id=1, source_target_pairs={{0,8},{4,12},{8,0},{12,4},{1,9},{5,13},{9,1},{13,5},{2,10},{6,14},... | collective-permute-start | bytes 6152 | tf_op jit(solution)/shard_map/while/body/ppermute | solution.py:17
  86.6 2.7 %collective-permute-start.2 = (bf16[2048,256]{1,0:T(8,128)(2,1)S(1)}, bf16[2048,256]{1,0:T(8,128)(2,1)S(1)}, u32[]{:S(2)}, u32[]{:S(2)}) collective-permute-start(bf16[2048,256]{1,0:T(8,128)(2,1)S(1)} %pad_maximum_fusion.17.near), channel_id=1, source_target_pairs={{0,4},{4,0},{8,12},{12,8},{1,5},{5,1},{9,13},{13,9},{2,6},{6,2},{1... | collective-permute-start | bytes 3145736 | tf_op jit(solution)/shard_map/while/body/ppermute | solution.py:17
  97.6 14.0 %copy-start.12 = (f32[1,512]{1,0:T(1,128)S(1)}, f32[1,512]{1,0:T(1,128)}, u32[]{:S(2)}) copy-start(f32[1,512]{1,0:T(1,128)} %get-tuple-element.394) | copy-start | bytes 6148
  97.6 14.0 %copy-start.13 = (f32[1,128]{1,0:T(1,128)S(1)}, f32[1,128]{1,0:T(1,128)}, u32[]{:S(2)}) copy-start(f32[1,128]{1,0:T(1,128)} %param.22) | copy-start | bytes 1540
  112.0 12.9 %collective-permute-start.3 = (bf16[1920,128]{1,0:T(8,128)(2,1)S(1)}, bf16[1920,128]{1,0:T(8,128)(2,1)S(1)}, u32[]{:S(2)}, u32[]{:S(2)}) collective-permute-start(bf16[1920,128]{1,0:T(8,128)(2,1)S(1)} %copy.46), channel_id=1, source_target_pairs={{0,8},{4,12},{8,0},{12,4},{1,9},{5,13},{9,1},{13,5},{2,10},{6,14},... | collective-permute-start | bytes 1474568 | tf_op jit(solution)/shard_map/while/body/ppermute | solution.py:17
  113.6 12.5 %collective-permute-start.4 = (bf16[1920,128]{1,0:T(8,128)(2,1)S(1)}, bf16[1920,128]{1,0:T(8,128)(2,1)S(1)}, u32[]{:S(2)}, u32[]{:S(2)}) collective-permute-start(bf16[1920,128]{1,0:T(8,128)(2,1)S(1)} %copy.46), channel_id=1, source_target_pairs={{0,16},{16,0},{1,17},{17,1},{2,18},{18,2},{3,19},{19,3},{4,20},{20... | collective-permute-start | bytes 1474568 | tf_op jit(solution)/shard_map/while/body/ppermute | solution.py:17
  126.3 13.7 %collective-permute-start.6 = (bf16[1920,256]{1,0:T(8,128)(2,1)S(1)}, bf16[1920,256]{1,0:T(8,128)(2,1)}, u32[]{:S(2)}, u32[]{:S(2)}) collective-permute-start(bf16[1920,256]{1,0:T(8,128)(2,1)S(1)} %pad_maximum_fusion.18), channel_id=1, source_target_pairs={{0,4},{4,0},{8,12},{12,8},{1,5},{5,1},{9,13},{13,9},{2,6},{6,2},{1... | collective-permute-start | bytes 2949128 | tf_op jit(solution)/shard_map/while/body/ppermute | solution.py:17
  126.4 13.6 %collective-permute-start.5 = (bf16[1920,128]{1,0:T(8,128)(2,1)S(1)}, bf16[1920,128]{1,0:T(8,128)(2,1)S(1)}, u32[]{:S(2)}, u32[]{:S(2)}) collective-permute-start(bf16[1920,128]{1,0:T(8,128)(2,1)S(1)} %collective-permute-done.4), channel_id=1, source_target_pairs={{0,8},{4,12},{8,0},{12,4},{1,9},{5,13},{9,1},{13,5},{2,10},{6,14},... | collective-permute-start | bytes 1474568 | tf_op jit(solution)/shard_map/while/body/ppermute | solution.py:17
  127.0 13.3 %copy-start.9 = (bf16[576,1920]{1,0:T(8,128)(2,1)S(1)}, bf16[576,1920]{1,0:T(8,128)(2,1)}, u32[]{:S(2)}) copy-start(bf16[576,1920]{1,0:T(8,128)(2,1)} %get-tuple-element.846) | copy-start | bytes 6635524 | tf_op jit(solution)/shard_map/while
  140.2 4.7 %collective-permute-start.7 = (bf16[1920,256]{1,0:T(8,128)(2,1)S(1)}, bf16[1920,256]{1,0:T(8,128)(2,1)S(1)}, u32[]{:S(2)}, u32[]{:S(2)}) collective-permute-start(bf16[1920,256]{1,0:T(8,128)(2,1)S(1)} %pad_maximum_fusion.19), channel_id=1, source_target_pairs={{0,4},{4,0},{8,12},{12,8},{1,5},{5,1},{9,13},{13,9},{2,6},{6,2},{1... | collective-permute-start | bytes 2949128 | tf_op jit(solution)/shard_map/while/body/ppermute | solution.py:17
  141.9 2.1 copy-start.5
  153.9 13.2 %collective-permute-start.21 = (bf16[1920,128]{1,0:T(8,128)(2,1)}, bf16[1920,128]{1,0:T(8,128)(2,1)S(1)}, u32[]{:S(2)}, u32[]{:S(2)}) collective-permute-start(bf16[1920,128]{1,0:T(8,128)(2,1)} %bitcast.131), channel_id=1, source_target_pairs={{0,8},{4,12},{8,0},{12,4},{1,9},{5,13},{9,1},{13,5},{2,10},{6,14},... | collective-permute-start | bytes 1474568 | tf_op jit(solution)/shard_map/ppermute | solution.py:17
  155.4 12.7 %collective-permute-start.22 = (bf16[1920,128]{1,0:T(8,128)(2,1)}, bf16[1920,128]{1,0:T(8,128)(2,1)S(1)}, u32[]{:S(2)}, u32[]{:S(2)}) collective-permute-start(bf16[1920,128]{1,0:T(8,128)(2,1)} %bitcast.132), channel_id=1, source_target_pairs={{0,16},{16,0},{1,17},{17,1},{2,18},{18,2},{3,19},{19,3},{4,20},{20... | collective-permute-start | bytes 1474568 | tf_op jit(solution)/shard_map/ppermute | solution.py:17
  157.0 10.0 %collective-permute-start.20 = (bf16[12,48,256]{2,1,0:T(8,128)(2,1)}, bf16[12,48,256]{2,1,0:T(8,128)(2,1)S(1)}, u32[]{:S(2)}, u32[]{:S(2)}) collective-permute-start(bf16[12,48,256]{2,1,0:T(8,128)(2,1)} %get-tuple-element.396), channel_id=1, source_target_pairs={{0,1},{1,2},{2,3},{3,0},{4,5},{5,6},{6,7},{7,4},{8,9},{9,10},{10,1... | collective-permute-start | bytes 884744 | tf_op jit(solution)/shard_map/ppermute | solution.py:13
  169.9 22.6 %collective-permute-start.23 = (bf16[12,48,256]{2,1,0:T(8,128)(2,1)}, bf16[12,48,256]{2,1,0:T(8,128)(2,1)}, u32[]{:S(2)}, u32[]{:S(2)}) collective-permute-start(bf16[12,48,256]{2,1,0:T(8,128)(2,1)} %broadcast_select_fusion.15), channel_id=1, source_target_pairs={{0,2},{1,3},{2,0},{3,1},{4,6},{5,7},{6,4},{7,5},{8,10},{9,11},{10,... | collective-permute-start | bytes 884744 | tf_op jit(solution)/shard_map/ppermute | solution.py:13
  173.7 9.8 %collective-permute-start.10 = (bf16[1920,256]{1,0:T(8,128)(2,1)S(1)}, bf16[1920,256]{1,0:T(8,128)(2,1)}, u32[]{:S(2)}, u32[]{:S(2)}) collective-permute-start(bf16[1920,256]{1,0:T(8,128)(2,1)S(1)} %pad_maximum_fusion.21), channel_id=1, source_target_pairs={{0,4},{4,0},{8,12},{12,8},{1,5},{5,1},{9,13},{13,9},{2,6},{6,2},{1... | collective-permute-start | bytes 2949128 | tf_op jit(solution)/shard_map/while/body/ppermute | solution.py:17
  173.8 8.4 %collective-permute-start.8 = (bf16[960,128]{1,0:T(8,128)(2,1)S(1)}, bf16[960,128]{1,0:T(8,128)(2,1)S(1)}, u32[]{:S(2)}, u32[]{:S(2)}) collective-permute-start(bf16[960,128]{1,0:T(8,128)(2,1)S(1)} %slice.142), channel_id=1, source_target_pairs={{0,16},{16,0},{1,17},{17,1},{2,18},{18,2},{3,19},{19,3},{4,20},{20... | collective-permute-start | bytes 737288 | tf_op jit(solution)/shard_map/while/body/ppermute | solution.py:17
  175.4 8.1 %collective-permute-start.9 = (bf16[960,128]{1,0:T(8,128)(2,1)S(1)}, bf16[960,128]{1,0:T(8,128)(2,1)S(1)}, u32[]{:S(2)}, u32[]{:S(2)}) collective-permute-start(bf16[960,128]{1,0:T(8,128)(2,1)S(1)} %slice.143), channel_id=1, source_target_pairs={{0,8},{4,12},{8,0},{12,4},{1,9},{5,13},{9,1},{13,5},{2,10},{6,14},... | collective-permute-start | bytes 737288 | tf_op jit(solution)/shard_map/while/body/ppermute | solution.py:17
  183.8 6.2 %collective-permute-start.11 = (bf16[1920,256]{1,0:T(8,128)(2,1)S(1)}, bf16[1920,256]{1,0:T(8,128)(2,1)S(1)}, u32[]{:S(2)}, u32[]{:S(2)}) collective-permute-start(bf16[1920,256]{1,0:T(8,128)(2,1)S(1)} %pad_maximum_fusion.22), channel_id=1, source_target_pairs={{0,4},{4,0},{8,12},{12,8},{1,5},{5,1},{9,13},{13,9},{2,6},{6,2},{1... | collective-permute-start | bytes 2949128 | tf_op jit(solution)/shard_map/while/body/ppermute | solution.py:17
  185.2 1.9 copy-start.8
  187.0 2.1 copy-start.6
  192.4 10.4 %collective-permute-start.24 = (bf16[12,48,256]{2,1,0:T(8,128)(2,1)}, bf16[12,48,256]{2,1,0:T(8,128)(2,1)S(1)}, u32[]{:S(2)}, u32[]{:S(2)}) collective-permute-start(bf16[12,48,256]{2,1,0:T(8,128)(2,1)} %get-tuple-element.403), channel_id=1, source_target_pairs={{0,1},{1,2},{2,3},{3,0},{4,5},{5,6},{6,7},{7,4},{8,9},{9,10},{10,1... | collective-permute-start | bytes 884744 | tf_op jit(solution)/shard_map/ppermute | solution.py:13
  192.9 10.0 %copy-start.11 = (bf16[12,48,256]{2,1,0:T(8,128)(2,1)S(1)}, bf16[12,48,256]{2,1,0:T(8,128)(2,1)}, u32[]{:S(2)}) copy-start(bf16[12,48,256]{2,1,0:T(8,128)(2,1)} %get-tuple-element.403) | copy-start | bytes 884740
  202.9 12.7 %collective-permute-start.28 = (bf16[12,48,256]{2,1,0:T(8,128)(2,1)S(1)}, bf16[12,48,256]{2,1,0:T(8,128)(2,1)S(1)}, u32[]{:S(2)}, u32[]{:S(2)}) collective-permute-start(bf16[12,48,256]{2,1,0:T(8,128)(2,1)S(1)} %broadcast_select_fusion.14), channel_id=1, source_target_pairs={{0,2},{1,3},{2,0},{3,1},{4,6},{5,7},{6,4},{7,5},{8,10},{9,11},{10,... | collective-permute-start | bytes 884744 | tf_op jit(solution)/shard_map/ppermute | solution.py:13
  203.0 1.9 collective-permute-start.25
  203.1 5.7 %collective-permute-start.26 = (bf16[4,48,2,1,128]{4,2,1,0,3:T(2,128)(2,1)S(1)}, bf16[4,48,2,1,128]{4,2,1,0,3:T(2,128)(2,1)S(1)}, u32[]{:S(2)}, u32[]{:S(2)}) collective-permute-start(bf16[4,48,2,1,128]{4,2,1,0,3:T(2,128)(2,1)S(1)} %squeeze.30), channel_id=1, source_target_pairs={{0,8},{4,12},{8,0},{12,4},{1,9},{5,13},{9,1},{13,5},{2,10},{6,14},... | collective-permute-start | bytes 294920 | tf_op jit(solution)/shard_map/ppermute | solution.py:17
  203.7 6.2 %collective-permute-start.27 = (bf16[4,48,2,1,128]{4,2,1,0,3:T(2,128)(2,1)S(1)}, bf16[4,48,2,1,128]{4,2,1,0,3:T(2,128)(2,1)S(1)}, u32[]{:S(2)}, u32[]{:S(2)}) collective-permute-start(bf16[4,48,2,1,128]{4,2,1,0,3:T(2,128)(2,1)S(1)} %squeeze.31), channel_id=1, source_target_pairs={{0,12},{4,8},{8,4},{12,0},{1,13},{5,9},{9,5},{13,1},{2,14},{6,10},... | collective-permute-start | bytes 294920 | tf_op jit(solution)/shard_map/ppermute | solution.py:17
  216.4 2.7 %collective-permute-start.29 = (bf16[4,48,2,1,128]{4,2,1,0,3:T(2,128)(2,1)S(1)}, bf16[4,48,2,1,128]{4,2,1,0,3:T(2,128)(2,1)S(1)}, u32[]{:S(2)}, u32[]{:S(2)}) collective-permute-start(bf16[4,48,2,1,128]{4,2,1,0,3:T(2,128)(2,1)S(1)} %squeeze.33), channel_id=1, source_target_pairs={{0,4},{4,0},{8,12},{12,8},{1,5},{5,1},{9,13},{13,9},{2,6},{6,2},{1... | collective-permute-start | bytes 294920 | tf_op jit(solution)/shard_map/ppermute | solution.py:17
  216.6 4.5 %collective-permute-start.31 = (bf16[4,48,2,1,128]{4,2,1,0,3:T(2,128)(2,1)S(1)}, bf16[4,48,2,1,128]{4,2,1,0,3:T(2,128)(2,1)S(1)}, u32[]{:S(2)}, u32[]{:S(2)}) collective-permute-start(bf16[4,48,2,1,128]{4,2,1,0,3:T(2,128)(2,1)S(1)} %squeeze.35), channel_id=1, source_target_pairs={{0,12},{4,8},{8,4},{12,0},{1,13},{5,9},{9,5},{13,1},{2,14},{6,10},... | collective-permute-start | bytes 294920 | tf_op jit(solution)/shard_map/ppermute | solution.py:17
  217.4 6.4 %collective-permute-start.30 = (bf16[4,48,2,1,128]{4,2,1,0,3:T(2,128)(2,1)S(1)}, bf16[4,48,2,1,128]{4,2,1,0,3:T(2,128)(2,1)S(1)}, u32[]{:S(2)}, u32[]{:S(2)}) collective-permute-start(bf16[4,48,2,1,128]{4,2,1,0,3:T(2,128)(2,1)S(1)} %squeeze.34), channel_id=1, source_target_pairs={{0,8},{4,12},{8,0},{12,4},{1,9},{5,13},{9,1},{13,5},{2,10},{6,14},... | collective-permute-start | bytes 294920 | tf_op jit(solution)/shard_map/ppermute | solution.py:17
  (6 other events, 8.7 us)
Sparse Core Ops, SparseCore 0:
  69.9 40.9 reduce-scatter.2
  113.2 40.6 reduce-scatter.4

commit v12 on v9

--- a/solution.py
+++ b/solution.py
@@ -1,6 +1,10 @@
+import functools
+
 import jax
 import jax.numpy as jnp
 from jax import lax
+from jax.experimental import pallas as pl
+from jax.experimental.pallas import tpu as pltpu
 from jax.sharding import PartitionSpec as P
 
 eps_norm = 1e-05
@@ -71,6 +75,82 @@
     return gathered_rows[None, None]
 
 
+scalars, vmem = pl.BlockSpec(memory_space=pltpu.SMEM), pl.BlockSpec(memory_space=pltpu.VMEM)
+kernel_memory = pltpu.CompilerParams(vmem_limit_bytes=40 * 1024 * 1024)
+
+
+def terms_body(choice, weight, near, far, own, *parts):
+    depth, width = own.shape
+    tall = 640 if depth % 640 == 0 else depth
+
+    @pl.loop(0, depth // tall)
+    def _(i):
+        rows = pl.ds(pl.multiple_of(i * tall, tall), tall)
+        near_product = add_columns(weight[rows, :], near[...])
+        far_product = add_columns(weight[rows, :], far[...])
+        near_kept = choice[0] == 1
+        kept = jnp.where(near_kept, near_product, far_product)
+        sent = jnp.where(near_kept, far_product, near_product)
+        own[rows, :] = kept[:, :width]
+        for part, block in zip(parts, (sent[:, width:], kept[:, width:], sent[:, :width])):
+            part[rows, :] = block.astype(part.dtype)
+
+
+def product_terms(choice, weight, near, far):
+    depth, rows = weight.shape
+    columns = near.shape[1]
+    width = columns // 2
+    return pl.pallas_call(
+        terms_body,
+        out_shape=[
+            jax.ShapeDtypeStruct((depth, width), dtype)
+            for dtype in (jnp.float32, jnp.bfloat16, jnp.bfloat16, jnp.bfloat16)
+        ],
+        in_specs=[scalars, vmem, vmem, vmem],
+        out_specs=[vmem] * 4,
+        compiler_params=kernel_memory,
+        cost_estimate=pl.CostEstimate(
+            flops=4 * depth * rows * columns,
+            bytes_accessed=2 * depth * rows + 4 * rows * columns + 10 * depth * width,
+            transcendentals=0,
+        ),
+    )(choice, weight, near, far)
+
+
+def tokens_body(normed, tile, features, bias, gain, *refs):
+    *parts, out, total = refs
+    depth, columns = parts[0].shape
+    for r, part in enumerate(parts):
+        start = pl.multiple_of((tile[0] ^ r) * depth, 128)
+        product = add_columns(features[:, pl.ds(start, depth)], part[...])
+        total[...] = product if r == 0 else total[...] + product
+    width = columns // 2
+    for k in range(2):
+        block = pl.ds(k * width, width)
+        entries = total[:, block] + bias[:, block]
+        if normed:
+            squares = jnp.mean(entries * entries, axis=-1, keepdims=True)
+            entries = entries * lax.rsqrt(squares + eps_norm) * gain[...]
+        out[:, block] = entries.astype(out.dtype)
+
+
+def token_entries(normed, tile, features, bias, gain, parts):
+    rows, columns = features.shape[0], parts[0].shape[1]
+    return pl.pallas_call(
+        functools.partial(tokens_body, normed),
+        out_shape=jax.ShapeDtypeStruct((rows, columns), jnp.bfloat16),
+        in_specs=[scalars] + [vmem] * 7,
+        out_specs=vmem,
+        scratch_shapes=[pltpu.VMEM((rows, columns), jnp.float32)],
+        compiler_params=kernel_memory,
+        cost_estimate=pl.CostEstimate(
+            flops=2 * rows * features.shape[1] * columns,
+            bytes_accessed=2 * features.shape[1] * (rows + columns) + 2 * rows * columns,
+            transcendentals=rows,
+        ),
+    )(tile, features, bias, gain, *parts)
+
+
 def product_plan(
     features, proj_weight, proj_bias, kv_weight, key_gain, tile_map, tile_count, decode_owner
 ):
@@ -97,10 +177,6 @@
     def outer_core(h):
         return (h ^ h // 2) % 2
 
-    feature_parts = [
-        lax.dynamic_slice_in_dim(feature_rows, (tile ^ r) * depth, depth, axis=1) for r in range(4)
-    ]
-
     def put_first(condition, one, other, axis):
         return jnp.concatenate(
             [jnp.where(condition, one, other), jnp.where(condition, other, one)], axis=axis
@@ -109,17 +185,11 @@
     def both_heads(ours, theirs):
         return put_first(group == 0, ours, theirs, 1)
 
+    choice = (at_end == first_core).astype(jnp.int32).reshape(1)
+
     def products(near, far):
-        both = add_columns(proj_weight, jnp.concatenate([near, far], axis=1))
-        near_0, near_1, far_0, far_1 = (both[:, k * width : (k + 1) * width] for k in range(4))
-        near_kept = at_end == first_core
-        parts = (
-            jnp.where(near_kept, far_1, near_1),
-            jnp.where(near_kept, near_1, far_1),
-            jnp.where(near_kept, far_0, near_0),
-        )
-        own = jnp.where(near_kept, near_0, far_0)
-        return own, tuple(part.astype(jnp.bfloat16) for part in parts)
+        own, *parts = product_terms(choice, proj_weight, near, far)
+        return own, tuple(parts)
 
     def exchange(parts):
         return tuple(swapped(part, "head", bit) for part, bit in zip(parts, (2, 3, 1)))
@@ -134,19 +204,10 @@
     def in_loop(chain, given, empty):
         return lax.fori_loop(0, once, lambda _, carry: chain(carry[0]), (given, empty))[1]
 
-    def times_features(rows, parts):
-        return sum(add_columns(parts[r], rows[r]) for r in range(4))
-
-    def finish(total, part):
-        finished = []
-        for k in range(2):
-            entries = total[:, k * width : (k + 1) * width].reshape(token_rows, layers, head_dim)
-            entries = entries + bias_part[k, :, part][None]
-            if part == 0:
-                squares = jnp.mean(entries * entries, axis=-1, keepdims=True)
-                entries = entries * lax.rsqrt(squares + eps_norm) * key_gain[None]
-            finished.append(entries.reshape(token_rows, width).astype(jnp.bfloat16))
-        return jnp.concatenate(finished, axis=1).reshape(tile_slots, shard_len, 2 * width)
+    def times_features(parts, part, bias_part):
+        bias = bias_part[:, :, part].reshape(1, 2 * width)
+        entries = token_entries(part == 0, tile.reshape(1), feature_rows, bias, key_gain, parts)
+        return entries.reshape(tile_slots, shard_len, 2 * width)
 
     owner_tile, owner_turn, matched = routing(tile_map, tile_count, decode_owner, tile_slots, 4)
     turn_of = jnp.sum(jnp.where(matched, owner_turn[:, None, None], 0), axis=(0, 1))
@@ -179,13 +240,15 @@
     bias_rows = moved(proj_bias, lambda t, h: (h, t))
     key_block = moved(key_mine, lambda t, h: (h // 2 * 2 + outer_core(h), t))
     comes = swapped(leaves, "tile", 2)
-    no_block = jnp.zeros((depth, width), jnp.float32)
-    no_terms = no_block, tuple(jnp.zeros((depth, width), jnp.bfloat16) for _ in range(3))
+    no_terms = (
+        jnp.zeros((depth, width), jnp.float32),
+        tuple(jnp.full((depth, width), k, jnp.bfloat16) for k in range(3)),
+    )
     no_tokens = tuple(
-        jnp.zeros((tile_slots, shard_len, 2 * width), jnp.bfloat16) for _ in range(2)
-    )
-    bias_rows, key_block, comes, stays, feature_parts, no_terms, no_tokens, once = step(
-        (bias_rows, key_block, comes, stays, feature_parts, no_terms, no_tokens, once)
+        jnp.full((tile_slots, shard_len, 2 * width), k, jnp.bfloat16) for k in range(2)
+    )
+    bias_rows, key_block, comes, stays, once = step(
+        (bias_rows, key_block, comes, stays, once)
     )
 
     value_pieces = []
@@ -228,7 +291,7 @@
         diagonal, rows_1 = step((swapped(across_y, "tile", 2), swapped(rows_0, "tile", 1)))
         rows_2 = step(both_heads(across_x, diagonal))
         rows = [rows_0, rows_1, rows_2, swapped(rows_2, "tile", 1)]
-        return across_x, finish(times_features(rows, feature_parts), 0)
+        return across_x, times_features(rows, 0, bias_part)
 
     arrived, keys = step((exchange(parts), in_loop(keys_product, own, no_tokens[0])))
     own = summed(value_own, arrived)
@@ -250,8 +313,7 @@
         )
         rows_2 = step(both_heads(across_x, jnp.concatenate([upper, lower], axis=0)))
         rows = [rows_0, rows_1, rows_2, swapped(rows_2, "tile", 1)]
-        total = times_features(rows, feature_parts)
-        return (across_y, own, across_x), finish(total, 1)
+        return (across_y, own, across_x), times_features(rows, 1, bias_part)
 
     keys = step(rolled(keys, shifted, 1))
     values = in_loop(values_product, (own, across_x, across_y), no_tokens[1])

time: 234 us -> 240 us (1.026)
  Pallas kernels: 0 us -> 32.4 us
  matrix products: 24.3 us -> 1.02 us
  waiting for transfers between devices: 93.8 us -> 106 us
  local copies, waits for them, and re-layouts: 29.4 us -> 21.2 us
  starting transfers between devices: 64.2 us -> 60.4 us
  other arithmetic: 19.8 us -> 17.1 us
    pallas_call x0 -> x4, Pallas kernels: none -> 32.4 us  [the longest x2 18.1 us: product_terms(): pl.pallas_call(terms_body, out_shape=[jax.ShapeDtypeStruct((depth, width)...]
    dot_general x13 -> x3, matrix products: 24.1 us -> 0.83 us  [add_columns(): return jnp.dot(operand, portion, preferred_element_type=jnp.float32)]
    ppermute x30, waiting for transfers between devices: 63 us -> 71.7 us  [swapped(): lax.ppermute(shard, axis, [(i, i ^ bit) for i in range(lax.axis_size(axis...]
    dynamic_slice x1 -> x0, local copies, waits for them, and re-layouts: 7.31 us -> none  [product_plan(): lax.dynamic_slice_in_dim(feature_rows, (tile ^ r) * depth, depth, axis=1)]
    broadcast_in_dim x1 -> x6, local copies, waits for them, and re-layouts: 1.06 us -> 5.08 us  [the longest x3 2.55 us: product_plan(): jnp.full((depth, width), k, jnp.bfloat16)]
    ppermute x4, starting transfers between devices: 8.88 us -> 5.49 us  [shifted_2(): lax.ppermute(shard, axis, [(i, (i + by) % count) for i in range(count)])]
    optimization_barrier x5 -> x1, local copies, waits for them, and re-layouts: 3.33 us -> 0.01 us  [product_plan(): step((bias_rows, key_block, comes, stays, once))]
    ppermute x4, waiting for transfers between devices: 21.8 us -> 25.1 us  [shifted_2(): lax.ppermute(shard, axis, [(i, (i + by) % count) for i in range(count)])]
  transfers between devices with their start and end apart: 38 -> 38, of which waited for: 20 -> 22; matrix products, arithmetic and copies ran while one was open for 19% -> 10% of each run, Pallas kernels for 0% -> 10%
where the time goes in v12:
time: 240 us; the launch traced here: 239 us
  waiting for transfers between devices  106 us (44%)
  starting transfers between devices  60.4 us (25%)
  Pallas kernels  32.4 us (14%)
  local copies, waits for them, and re-layouts  21.2 us (9%)
  other arithmetic  17.1 us (7%)
    ppermute x30, waiting for transfers between devices, swapped(): lax.ppermute(shard, axis, [(i, i ^ bit) for i in range(lax.axis_size(axis...  71.7 us
    ppermute x30, starting transfers between devices, swapped(): lax.ppermute(shard, axis, [(i, i ^ bit) for i in range(lax.axis_size(axis...  51.4 us
    ppermute x4, waiting for transfers between devices, shifted_2(): lax.ppermute(shard, axis, [(i, (i + by) % count) for i in range(count)])  25.1 us
    pallas_call x2, Pallas kernels, product_terms(): pl.pallas_call(terms_body, out_shape=[jax.ShapeDtypeStruct((depth, width)...  18.1 us
    pallas_call x2, Pallas kernels, token_entries(): pl.pallas_call(functools.partial(tokens_body, normed), out_shape=jax.Shap...  14.3 us
    ppermute x4, waiting for transfers between devices, moved(): return lax.ppermute(shard, ('tile', 'head'), pairs)  9.02 us
    ppermute x4, starting transfers between devices, shifted_2(): lax.ppermute(shard, axis, [(i, (i + by) % count) for i in range(count)])  5.49 us
  transfers between devices with their start and end apart: 38, of which 22 were waited for; matrix products, arithmetic and copies ran while one was open for 10% of the time, Pallas kernels for 10%

profile of v12, /device:TPU:0, one launch (start us, length us, event | category | flops | bytes accessed | tf_op | source)
XLA Modules:
  0.0 238.9 jit_solution(11065280192685253900)
XLA Ops:
  0.0 1.2 constant_dynamic-slice_fusion
  2.0 2.3 fusion.19
  4.2 6.7 %collective-permute-start.14 = (bf16[1024,128]{1,0:T(8,128)(2,1)}, bf16[1024,128]{1,0:T(8,128)(2,1)}, u32[]{:S(2)}, u32[]{:S(2)}) collective-permute-start(bf16[1024,128]{1,0:T(8,128)(2,1)} %get-tuple-element.509), channel_id=1, source_target_pairs={{0,8},{4,12},{8,0},{12,4},{1,9},{5,13},{9,1},{13,5},{2,10},{6,14},... | collective-permute-start | bytes 786440 | tf_op jit(solution)/shard_map/ppermute | solution.py:19
  12.9 10.5 %collective-permute-done.14 = bf16[1024,128]{1,0:T(8,128)(2,1)} collective-permute-done((bf16[1024,128]{1,0:T(8,128)(2,1)}, bf16[1024,128]{1,0:T(8,128)(2,1)}, u32[]{:S(2)}, u32[]{:S(2)}) %collective-permute-start.14) | collective-permute-done | bytes 262176 | tf_op jit(solution)/shard_map/ppermute | solution.py:19
  23.3 9.8 %collective-permute-start.17 = (bf16[2048,128]{1,0:T(8,128)(2,1)S(1)}, bf16[2048,128]{1,0:T(8,128)(2,1)S(1)}, u32[]{:S(2)}, u32[]{:S(2)}) collective-permute-start(bf16[2048,128]{1,0:T(8,128)(2,1)S(1)} %collective-permute-done.13), channel_id=1, source_target_pairs={{0,8},{4,12},{8,0},{12,4},{1,9},{5,13},{9,1},{13,5},{2,10},{6,14},... | collective-permute-start | bytes 1572872 | tf_op jit(solution)/shard_map/ppermute | solution.py:19
  34.7 1.4 collective-permute-start.16
  36.6 9.0 %collective-permute-done.16 = bf16[1024,128]{1,0:T(8,128)(2,1)S(1)} collective-permute-done((bf16[1024,128]{1,0:T(8,128)(2,1)S(1)}, bf16[1024,128]{1,0:T(8,128)(2,1)S(1)}, u32[]{:S(2)}, u32[]{:S(2)}) %collective-permute-start.16) | collective-permute-done | bytes 262176 | tf_op jit(solution)/shard_map/ppermute | solution.py:175
  46.6 4.2 %collective-permute-start.18 = (bf16[2048,256]{1,0:T(8,128)(2,1)S(1)}, bf16[2048,256]{1,0:T(8,128)(2,1)S(1)}, u32[]{:S(2)}, u32[]{:S(2)}) collective-permute-start(bf16[2048,256]{1,0:T(8,128)(2,1)S(1)} %pad_maximum_fusion.5.near), channel_id=1, source_target_pairs={{0,4},{4,0},{8,12},{12,8},{1,5},{5,1},{9,13},{13,9},{2,6},{6,2},{1... | collective-permute-start | bytes 3145736 | tf_op jit(solution)/shard_map/ppermute | solution.py:19
  51.4 1.7 collective-permute-done.19
  53.1 8.9 %shard_map.82 = (f32[1920,128]{1,0:T(8,128)S(1)}, bf16[1920,128]{1,0:T(8,128)(2,1)}, bf16[1920,128]{1,0:T(8,128)(2,1)}, bf16[1920,128]{1,0:T(8,128)(2,1)}) custom-call(s32[1]{0:T(128)} %bitcast.6.choice, bf16[1920,2048]{1,0:T(8,128)(2,1)} %weight.1, bf16[2048,256]{1,0:T(8,128)(2,1)S(1)} %pad_maximum_fusion.5.near, ...), custom_call_target="tpu_custom_call" | custom-call | flops 4026531840 | bytes 12419072 | tf_op jit(solution)/shard_map/pallas_call | solution.py:103
  62.6 1.5 collective-permute-start.20
  69.7 27.7 %while.54 = (s32[]{:T(128)}, bf16[1024,256]{1,0:T(8,128)(2,1)}, f32[1,512]{1,0:T(1,128)S(1)}, f32[1920,128]{1,0:T(8,128)}, bf16[1920,128]{1,0:T(8,128)(2,1)}, /*...) while((s32[]{:T(128)}, bf16[1024,256]{1,0:T(8,128)(2,1)}, ...), condition=%wide.region_3.4_spmd, body=%wide.region_2.3_spmd.sunk | while | flops 4029153792 | bytes 23972084 | solution.py:205
  70.7 1.7 collective-permute-start
  72.8 11.4 %collective-permute-done.1 = f32[1,512]{1,0:T(1,128)S(1)} collective-permute-done((f32[1,512]{1,0:T(1,128)S(1)}, f32[1,512]{1,0:T(1,128)S(1)}, u32[]{:S(2)}, u32[]{:S(2)}) %collective-permute-start.1) | collective-permute-done | bytes 2080 | tf_op jit(solution)/shard_map/while/body/ppermute | solution.py:19
  86.1 2.1 collective-permute-done.2.far
  88.2 9.2 %body.7 = (f32[1920,128]{1,0:T(8,128)}, bf16[1920,128]{1,0:T(8,128)(2,1)}, bf16[1920,128]{1,0:T(8,128)(2,1)}, bf16[1920,128]{1,0:T(8,128)(2,1)}) custom-call(s32[1]{0:T(128)} %get-tuple-element.804.choice, bf16[1920,2048]{1,0:T(8,128)(2,1)} %get-tuple-element.805.weight, bf16[2048,256]{1,0:T(8,128)(2,1)S(1)} %pad_maximum_fusion.13.near, ...), custom_call_target="tpu_custom_call" | custom-call | flops 4026531840 | bytes 12419072 | tf_op jit(solution)/shard_map/while/body/pallas_call | solution.py:103
  97.8 1.3 collective-permute-done.22
  99.7 10.7 %collective-permute-start.23 = (bf16[1920,128]{1,0:T(8,128)(2,1)}, bf16[1920,128]{1,0:T(8,128)(2,1)}, u32[]{:S(2)}, u32[]{:S(2)}) collective-permute-start(bf16[1920,128]{1,0:T(8,128)(2,1)} %get-tuple-element.384), channel_id=1, source_target_pairs={{0,2},{1,3},{2,0},{3,1},{4,6},{5,7},{6,4},{7,5},{8,10},{9,11},{10,... | collective-permute-start | bytes 1474568 | tf_op jit(solution)/shard_map/ppermute | solution.py:19
  110.4 1.4 collective-permute-start.24
  111.9 1.6 add_convert_fusion.1
  114.2 38.9 %while.55 = (s32[]{:T(128)}, bf16[1920,128]{1,0:T(8,128)(2,1)S(1)}, bf16[12,48,256]{2,1,0:T(8,128)(2,1)}, s32[]{:T(128)}, s32[]{:T(128)}, /*index=5*/f32[2,1,2,1...) while((s32[]{:T(128)}, bf16[1920,128]{1,0:T(8,128)(2,1)S(1)}, ...), condition=%wide.region_5.6_spmd, body=%wide.region_4.5_spmd.sunk | while | flops 2269839360 | bytes 35686704 | solution.py:205
  114.2 2.4 %collective-permute-start.3 = (bf16[1920,128]{1,0:T(8,128)(2,1)S(1)}, bf16[1920,128]{1,0:T(8,128)(2,1)S(1)}, u32[]{:S(2)}, u32[]{:S(2)}) collective-permute-start(bf16[1920,128]{1,0:T(8,128)(2,1)S(1)} %copy.53), channel_id=1, source_target_pairs={{0,8},{4,12},{8,0},{12,4},{1,9},{5,13},{9,1},{13,5},{2,10},{6,14},... | collective-permute-start | bytes 1474568 | tf_op jit(solution)/shard_map/while/body/ppermute | solution.py:19
  116.6 1.5 collective-permute-start.4
  118.1 9.4 %collective-permute-done.3 = bf16[1920,128]{1,0:T(8,128)(2,1)S(1)} collective-permute-done((bf16[1920,128]{1,0:T(8,128)(2,1)S(1)}, bf16[1920,128]{1,0:T(8,128)(2,1)S(1)}, u32[]{:S(2)}, u32[]{:S(2)}) %collective-permute-start.3) | collective-permute-done | bytes 491552 | tf_op jit(solution)/shard_map/while/body/ppermute | solution.py:19
  127.5 1.5 collective-permute-done.4
  129.7 13.2 %collective-permute-done.5 = bf16[1920,128]{1,0:T(8,128)(2,1)S(1)} collective-permute-done((bf16[1920,128]{1,0:T(8,128)(2,1)S(1)}, bf16[1920,128]{1,0:T(8,128)(2,1)S(1)}, u32[]{:S(2)}, u32[]{:S(2)}) %collective-permute-start.5) | collective-permute-done | bytes 491552 | tf_op jit(solution)/shard_map/while/body/ppermute | solution.py:19
  143.2 2.7 %collective-permute-done.7.refs_3_ = bf16[1920,256]{1,0:T(8,128)(2,1)} collective-permute-done((bf16[1920,256]{1,0:T(8,128)(2,1)S(1)}, bf16[1920,256]{1,0:T(8,128)(2,1)}, u32[]{:S(2)}, u32[]{:S(2)}) %collective-permute-start.7) | collective-permute-done | bytes 983072 | tf_op jit(solution)/shard_map/while/body/ppermute | solution.py:19
  145.8 7.2 %body.8 = bf16[576,256]{1,0:T(8,128)(2,1)} custom-call(s32[1]{0:T(128)} %bitcast.59.tile, bf16[576,7680]{1,0:T(8,128)(2,1)} %get-tuple-element.834.features, f32[1,256]{1,0:T(1,128)S(1)} %bitcast.66, f32[1,128]{1,0:T(1,128)S(1)} %get-tuple-element.835.gain, bf16[1920,256]{1,0:T(8,128)(2,1)S(1)} %pad_maximum_fusion.14.refs_0_, ...), custom_call_target="tpu_custom_call" | custom-call | flops 2264924160 | bytes 13074432 | tf_op jit(solution)/shard_map/while/body/pallas_call | solution.py:139
  153.0 2.7 %add_convert_fusion = bf16[1920,128]{1,0:T(8,128)(2,1)} fusion(bf16[1920,128]{1,0:T(8,128)(2,1)} %collective-permute-done.25, bf16[1920,128]{1,0:T(8,128)(2,1)} %collective-permute-done.24, f32[1920,128]{1,0:T(8,128)} %get-tuple-element.394, bf16[1920,128]{1,0:T(8,128)(2,1)} %collective-permute-done.23), kind=kLoop, calls=%fused_computation.21 | loop fusion | flops 1720320 | bytes 2949120 | tf_op jit(solution)/shard_map/convert_element_type | solution.py:200
  156.1 1.5 collective-permute-start.28
  157.8 2.2 collective-permute-start.26
  160.1 8.0 %collective-permute-done.26 = bf16[12,48,256]{2,1,0:T(8,128)(2,1)S(1)} collective-permute-done((bf16[12,48,256]{2,1,0:T(8,128)(2,1)S(1)}, bf16[12,48,256]{2,1,0:T(8,128)(2,1)S(1)}, u32[]{:S(2)}, u32[]{:S(2)}) %collective-permute-start.26) | collective-permute-done | bytes 294944 | tf_op jit(solution)/shard_map/ppermute | solution.py:15
  170.2 2.7 %collective-permute-start.29 = (bf16[12,48,256]{2,1,0:T(8,128)(2,1)}, bf16[12,48,256]{2,1,0:T(8,128)(2,1)}, u32[]{:S(2)}, u32[]{:S(2)}) collective-permute-start(bf16[12,48,256]{2,1,0:T(8,128)(2,1)} %broadcast_select_fusion.15), channel_id=1, source_target_pairs={{0,2},{1,3},{2,0},{3,1},{4,6},{5,7},{6,4},{7,5},{8,10},{9,11},{10,... | collective-permute-start | bytes 884744 | tf_op jit(solution)/shard_map/ppermute | solution.py:15
  173.7 24.9 %while.56 = (s32[]{:T(128)}, bf16[1920,128]{1,0:T(8,128)(2,1)}, bf16[1920,128]{1,0:T(8,128)(2,1)}, bf16[1920,128]{1,0:T(8,128)(2,1)}, bf16[12,48,256]{2,1,0:T(8,...) while((s32[]{:T(128)}, bf16[1920,128]{1,0:T(8,128)(2,1)}, ...), condition=%wide.region_7.8_spmd, body=%wide.region_6.7_spmd.sunk | while | flops 2269839360 | bytes 36669720 | solution.py:205
  177.5 1.6 collective-permute-start.8
  179.1 5.4 %collective-permute-done.9 = bf16[960,128]{1,0:T(8,128)(2,1)S(1)} collective-permute-done((bf16[960,128]{1,0:T(8,128)(2,1)S(1)}, bf16[960,128]{1,0:T(8,128)(2,1)S(1)}, u32[]{:S(2)}, u32[]{:S(2)}) %collective-permute-start.9) | collective-permute-done | bytes 245792 | tf_op jit(solution)/shard_map/while/body/ppermute | solution.py:19
  187.0 1.8 copy.71
  188.8 1.9 copy.70
  191.5 7.1 %body.9 = bf16[576,256]{1,0:T(8,128)(2,1)} custom-call(s32[1]{0:T(128)} %bitcast.62.tile, bf16[576,7680]{1,0:T(8,128)(2,1)} %get-tuple-element.870.features, f32[1,256]{1,0:T(1,128)S(1)} %bitcast.65, f32[1,128]{1,0:T(1,128)S(1)} %get-tuple-element.871.gain, bf16[1920,256]{1,0:T(8,128)(2,1)S(1)} %pad_maximum_fusion.16.refs_0_, ...), custom_call_target="tpu_custom_call" | custom-call | flops 2264924160 | bytes 13074432 | tf_op jit(solution)/shard_map/while/body/pallas_call | solution.py:139
  201.3 10.1 %collective-permute-done.30 = bf16[12,48,256]{2,1,0:T(8,128)(2,1)S(1)} collective-permute-done((bf16[12,48,256]{2,1,0:T(8,128)(2,1)S(1)}, bf16[12,48,256]{2,1,0:T(8,128)(2,1)S(1)}, u32[]{:S(2)}, u32[]{:S(2)}) %collective-permute-start.30) | collective-permute-done | bytes 294944 | tf_op jit(solution)/shard_map/ppermute | solution.py:15
  211.6 1.6 collective-permute-start.32
  213.5 3.8 %collective-permute-done.32 = bf16[4,48,2,1,128]{4,2,1,0,3:T(2,128)(2,1)S(1)} collective-permute-done((bf16[4,48,2,1,128]{4,2,1,0,3:T(2,128)(2,1)S(1)}, bf16[4,48,2,1,128]{4,2,1,0,3:T(2,128)(2,1)S(1)}, u32[]{:S(2)}, u32[]{:S(2)}) %collective-permute-start.32) | collective-permute-done | bytes 98336 | tf_op jit(solution)/shard_map/ppermute | solution.py:19
  217.3 1.2 collective-permute-done.33
  218.5 7.1 %collective-permute-done.34 = bf16[12,48,256]{2,1,0:T(8,128)(2,1)S(1)} collective-permute-done((bf16[12,48,256]{2,1,0:T(8,128)(2,1)S(1)}, bf16[12,48,256]{2,1,0:T(8,128)(2,1)S(1)}, u32[]{:S(2)}, u32[]{:S(2)}) %collective-permute-start.34) | collective-permute-done | bytes 294944 | tf_op jit(solution)/shard_map/ppermute | solution.py:15
  226.5 1.6 collective-permute-start.36
  228.7 3.4 %collective-permute-done.36 = bf16[4,48,2,1,128]{4,2,1,0,3:T(2,128)(2,1)S(1)} collective-permute-done((bf16[4,48,2,1,128]{4,2,1,0,3:T(2,128)(2,1)S(1)}, bf16[4,48,2,1,128]{4,2,1,0,3:T(2,128)(2,1)S(1)}, u32[]{:S(2)}, u32[]{:S(2)}) %collective-permute-start.36) | collective-permute-done | bytes 98336 | tf_op jit(solution)/shard_map/ppermute | solution.py:19
  232.2 1.3 collective-permute-done.37
  236.8 2.1 copy.21
  (128 shorter events, 36.5 us)
Async XLA Ops:
  0.0 36.2 %copy-start = (bf16[2048,512]{1,0:T(8,128)(2,1)S(1)}, bf16[2048,512]{1,0:T(8,128)(2,1)}, u32[]{:S(2)}) copy-start(bf16[2048,512]{1,0:T(8,128)(2,1)} %param.17) | copy-start | bytes 6291460
  0.0 10.9 %copy-start.5 = (bf16[2048]{0:T(1024)(128)(2,1)S(1)}, bf16[2048]{0:T(1024)(128)(2,1)}, u32[]{:S(2)}) copy-start(bf16[2048]{0:T(1024)(128)(2,1)} %param.16) | copy-start | bytes 12292
  0.0 11.6 %copy-start.6 = (s32[4]{0:T(128)S(1)}, s32[4]{0:T(128)}, u32[]{:S(2)}) copy-start(s32[4]{0:T(128)} %param.20) | copy-start | bytes 52
  1.2 22.1 %collective-permute-start.13 = (bf16[2048,128]{1,0:T(8,128)(2,1)S(1)}, bf16[2048,128]{1,0:T(8,128)(2,1)S(1)}, u32[]{:S(2)}, u32[]{:S(2)}) collective-permute-start(bf16[2048,128]{1,0:T(8,128)(2,1)S(1)} %constant_dynamic-slice_fusion), channel_id=1, source_target_pairs={{0,0},{1,4},{2,12},{3,8},{4,1},{5,5},{6,13},{7,9},{8,2},{9,6},{10,... | collective-permute-start | bytes 1572872 | tf_op jit(solution)/shard_map/ppermute | solution.py:175
  4.2 19.1 %collective-permute-start.14 = (bf16[1024,128]{1,0:T(8,128)(2,1)}, bf16[1024,128]{1,0:T(8,128)(2,1)}, u32[]{:S(2)}, u32[]{:S(2)}) collective-permute-start(bf16[1024,128]{1,0:T(8,128)(2,1)} %get-tuple-element.509), channel_id=1, source_target_pairs={{0,8},{4,12},{8,0},{12,4},{1,9},{5,13},{9,1},{13,5},{2,10},{6,14},... | collective-permute-start | bytes 786440 | tf_op jit(solution)/shard_map/ppermute | solution.py:19
  11.0 1.9 collective-permute-start.12
  23.3 22.3 %collective-permute-start.17 = (bf16[2048,128]{1,0:T(8,128)(2,1)S(1)}, bf16[2048,128]{1,0:T(8,128)(2,1)S(1)}, u32[]{:S(2)}, u32[]{:S(2)}) collective-permute-start(bf16[2048,128]{1,0:T(8,128)(2,1)S(1)} %collective-permute-done.13), channel_id=1, source_target_pairs={{0,8},{4,12},{8,0},{12,4},{1,9},{5,13},{9,1},{13,5},{2,10},{6,14},... | collective-permute-start | bytes 1572872 | tf_op jit(solution)/shard_map/ppermute | solution.py:19
  34.1 2.5 %collective-permute-start.15 = (bf16[1024,128]{1,0:T(8,128)(2,1)S(1)}, bf16[1024,128]{1,0:T(8,128)(2,1)S(1)}, u32[]{:S(2)}, u32[]{:S(2)}) collective-permute-start(bf16[1024,128]{1,0:T(8,128)(2,1)S(1)} %get-tuple-element.513), channel_id=1, source_target_pairs={{0,0},{1,4},{2,6},{3,2},{4,1},{5,5},{6,7},{7,3},{8,8},{9,12},{10,1... | collective-permute-start | bytes 786440 | tf_op jit(solution)/shard_map/ppermute | solution.py:175
  34.7 10.8 %collective-permute-start.16 = (bf16[1024,128]{1,0:T(8,128)(2,1)S(1)}, bf16[1024,128]{1,0:T(8,128)(2,1)S(1)}, u32[]{:S(2)}, u32[]{:S(2)}) collective-permute-start(bf16[1024,128]{1,0:T(8,128)(2,1)S(1)} %get-tuple-element.512), channel_id=1, source_target_pairs={{0,2},{1,6},{2,4},{3,0},{4,3},{5,7},{6,5},{7,1},{8,10},{9,14},{10,... | collective-permute-start | bytes 786440 | tf_op jit(solution)/shard_map/ppermute | solution.py:175
  46.4 4.4 %copy-start.7 = (s32[4]{0:T(128)S(1)}, s32[4]{0:T(128)}, u32[]{:S(2)}) copy-start(s32[4]{0:T(128)} %param.21) | copy-start | bytes 52
  46.4 4.8 %copy-start.4 = (s32[4,4]{1,0:T(4,128)S(1)}, s32[4,4]{1,0:T(4,128)}, u32[]{:S(2)}) copy-start(s32[4,4]{1,0:T(4,128)} %param.19) | copy-start | bytes 196
  46.6 6.5 %collective-permute-start.18 = (bf16[2048,256]{1,0:T(8,128)(2,1)S(1)}, bf16[2048,256]{1,0:T(8,128)(2,1)S(1)}, u32[]{:S(2)}, u32[]{:S(2)}) collective-permute-start(bf16[2048,256]{1,0:T(8,128)(2,1)S(1)} %pad_maximum_fusion.5.near), channel_id=1, source_target_pairs={{0,4},{4,0},{8,12},{12,8},{1,5},{5,1},{9,13},{13,9},{2,6},{6,2},{1... | collective-permute-start | bytes 3145736 | tf_op jit(solution)/shard_map/ppermute | solution.py:19
  50.8 2.3 collective-permute-start.19
  62.6 35.2 %collective-permute-start.20 = (bf16[1920,128]{1,0:T(8,128)(2,1)}, bf16[1920,128]{1,0:T(8,128)(2,1)}, u32[]{:S(2)}, u32[]{:S(2)}) collective-permute-start(bf16[1920,128]{1,0:T(8,128)(2,1)} %get-tuple-element.373), channel_id=1, source_target_pairs={{0,2},{1,3},{2,0},{3,1},{4,6},{5,7},{6,4},{7,5},{8,10},{9,11},{10,... | collective-permute-start | bytes 1474568 | tf_op jit(solution)/shard_map/ppermute | solution.py:19
  64.1 33.7 %collective-permute-start.21 = (bf16[1920,128]{1,0:T(8,128)(2,1)}, bf16[1920,128]{1,0:T(8,128)(2,1)}, u32[]{:S(2)}, u32[]{:S(2)}) collective-permute-start(bf16[1920,128]{1,0:T(8,128)(2,1)} %get-tuple-element.374), channel_id=1, source_target_pairs={{0,3},{1,2},{2,1},{3,0},{4,7},{5,6},{6,5},{7,4},{8,11},{9,10},{10,... | collective-permute-start | bytes 1474568 | tf_op jit(solution)/shard_map/ppermute | solution.py:19
  65.1 34.0 %collective-permute-start.22 = (bf16[1920,128]{1,0:T(8,128)(2,1)}, bf16[1920,128]{1,0:T(8,128)(2,1)}, u32[]{:S(2)}, u32[]{:S(2)}) collective-permute-start(bf16[1920,128]{1,0:T(8,128)(2,1)} %get-tuple-element.375), channel_id=1, source_target_pairs={{0,1},{1,0},{2,3},{3,2},{4,5},{5,4},{6,7},{7,6},{8,9},{9,8},{10,11... | collective-permute-start | bytes 1474568 | tf_op jit(solution)/shard_map/ppermute | solution.py:19
  70.7 13.5 %collective-permute-start = (bf16[1024,256]{1,0:T(8,128)(2,1)S(1)}, bf16[1024,256]{1,0:T(8,128)(2,1)}, u32[]{:S(2)}, u32[]{:S(2)}) collective-permute-start(bf16[1024,256]{1,0:T(8,128)(2,1)S(1)} %copy.34), channel_id=1, source_target_pairs={{0,8},{4,12},{8,0},{12,4},{1,9},{5,13},{9,1},{13,5},{2,10},{6,14},... | collective-permute-start | bytes 1572872 | tf_op jit(solution)/shard_map/while/body/ppermute | solution.py:19
  72.5 11.7 %collective-permute-start.1 = (f32[1,512]{1,0:T(1,128)S(1)}, f32[1,512]{1,0:T(1,128)S(1)}, u32[]{:S(2)}, u32[]{:S(2)}) collective-permute-start(f32[1,512]{1,0:T(1,128)S(1)} %copy.35), channel_id=1, source_target_pairs={{0,8},{4,12},{8,0},{12,4},{1,9},{5,13},{9,1},{13,5},{2,10},{6,14},... | collective-permute-start | bytes 6152 | tf_op jit(solution)/shard_map/while/body/ppermute | solution.py:19
  85.4 2.7 %collective-permute-start.2 = (bf16[2048,256]{1,0:T(8,128)(2,1)S(1)}, bf16[2048,256]{1,0:T(8,128)(2,1)S(1)}, u32[]{:S(2)}, u32[]{:S(2)}) collective-permute-start(bf16[2048,256]{1,0:T(8,128)(2,1)S(1)} %pad_maximum_fusion.13.near), channel_id=1, source_target_pairs={{0,4},{4,0},{8,12},{12,8},{1,5},{5,1},{9,13},{13,9},{2,6},{6,2},{1... | collective-permute-start | bytes 3145736 | tf_op jit(solution)/shard_map/while/body/ppermute | solution.py:19
  97.4 16.8 %copy-start.3 = (f32[1,128]{1,0:T(1,128)S(1)}, f32[1,128]{1,0:T(1,128)}, u32[]{:S(2)}) copy-start(f32[1,128]{1,0:T(1,128)} %param.18) | copy-start | bytes 1540
  99.7 53.3 %collective-permute-start.23 = (bf16[1920,128]{1,0:T(8,128)(2,1)}, bf16[1920,128]{1,0:T(8,128)(2,1)}, u32[]{:S(2)}, u32[]{:S(2)}) collective-permute-start(bf16[1920,128]{1,0:T(8,128)(2,1)} %get-tuple-element.384), channel_id=1, source_target_pairs={{0,2},{1,3},{2,0},{3,1},{4,6},{5,7},{6,4},{7,5},{8,10},{9,11},{10,... | collective-permute-start | bytes 1474568 | tf_op jit(solution)/shard_map/ppermute | solution.py:19
  110.4 42.6 %collective-permute-start.24 = (bf16[1920,128]{1,0:T(8,128)(2,1)}, bf16[1920,128]{1,0:T(8,128)(2,1)}, u32[]{:S(2)}, u32[]{:S(2)}) collective-permute-start(bf16[1920,128]{1,0:T(8,128)(2,1)} %get-tuple-element.385), channel_id=1, source_target_pairs={{0,3},{1,2},{2,1},{3,0},{4,7},{5,6},{6,5},{7,4},{8,11},{9,10},{10,... | collective-permute-start | bytes 1474568 | tf_op jit(solution)/shard_map/ppermute | solution.py:19
  111.9 41.2 %collective-permute-start.25 = (bf16[1920,128]{1,0:T(8,128)(2,1)}, bf16[1920,128]{1,0:T(8,128)(2,1)}, u32[]{:S(2)}, u32[]{:S(2)}) collective-permute-start(bf16[1920,128]{1,0:T(8,128)(2,1)} %get-tuple-element.386), channel_id=1, source_target_pairs={{0,1},{1,0},{2,3},{3,2},{4,5},{5,4},{6,7},{7,6},{8,9},{9,8},{10,11... | collective-permute-start | bytes 1474568 | tf_op jit(solution)/shard_map/ppermute | solution.py:19
  114.2 13.3 %collective-permute-start.3 = (bf16[1920,128]{1,0:T(8,128)(2,1)S(1)}, bf16[1920,128]{1,0:T(8,128)(2,1)S(1)}, u32[]{:S(2)}, u32[]{:S(2)}) collective-permute-start(bf16[1920,128]{1,0:T(8,128)(2,1)S(1)} %copy.53), channel_id=1, source_target_pairs={{0,8},{4,12},{8,0},{12,4},{1,9},{5,13},{9,1},{13,5},{2,10},{6,14},... | collective-permute-start | bytes 1474568 | tf_op jit(solution)/shard_map/while/body/ppermute | solution.py:19
  116.6 12.3 %collective-permute-start.4 = (bf16[1920,128]{1,0:T(8,128)(2,1)S(1)}, bf16[1920,128]{1,0:T(8,128)(2,1)S(1)}, u32[]{:S(2)}, u32[]{:S(2)}) collective-permute-start(bf16[1920,128]{1,0:T(8,128)(2,1)S(1)} %copy.53), channel_id=1, source_target_pairs={{0,16},{16,0},{1,17},{17,1},{2,18},{18,2},{3,19},{19,3},{4,20},{20... | collective-permute-start | bytes 1474568 | tf_op jit(solution)/shard_map/while/body/ppermute | solution.py:19
  129.2 13.7 %collective-permute-start.6 = (bf16[1920,256]{1,0:T(8,128)(2,1)S(1)}, bf16[1920,256]{1,0:T(8,128)(2,1)S(1)}, u32[]{:S(2)}, u32[]{:S(2)}) collective-permute-start(bf16[1920,256]{1,0:T(8,128)(2,1)S(1)} %pad_maximum_fusion.14.refs_0_), channel_id=1, source_target_pairs={{0,4},{4,0},{8,12},{12,8},{1,5},{5,1},{9,13},{13,9},{2,6},{6,2},{1... | collective-permute-start | bytes 2949128 | tf_op jit(solution)/shard_map/while/body/ppermute | solution.py:19
  129.2 13.6 %collective-permute-start.5 = (bf16[1920,128]{1,0:T(8,128)(2,1)S(1)}, bf16[1920,128]{1,0:T(8,128)(2,1)S(1)}, u32[]{:S(2)}, u32[]{:S(2)}) collective-permute-start(bf16[1920,128]{1,0:T(8,128)(2,1)S(1)} %collective-permute-done.4), channel_id=1, source_target_pairs={{0,8},{4,12},{8,0},{12,4},{1,9},{5,13},{9,1},{13,5},{2,10},{6,14},... | collective-permute-start | bytes 1474568 | tf_op jit(solution)/shard_map/while/body/ppermute | solution.py:19
  143.1 2.8 %collective-permute-start.7 = (bf16[1920,256]{1,0:T(8,128)(2,1)S(1)}, bf16[1920,256]{1,0:T(8,128)(2,1)}, u32[]{:S(2)}, u32[]{:S(2)}) collective-permute-start(bf16[1920,256]{1,0:T(8,128)(2,1)S(1)} %pad_maximum_fusion.15.refs_2_), channel_id=1, source_target_pairs={{0,4},{4,0},{8,12},{12,8},{1,5},{5,1},{9,13},{13,9},{2,6},{6,2},{1... | collective-permute-start | bytes 2949128 | tf_op jit(solution)/shard_map/while/body/ppermute | solution.py:19
  153.0 4.8 %copy-start.2 = (bf16[12,48,256]{2,1,0:T(8,128)(2,1)S(1)}, bf16[12,48,256]{2,1,0:T(8,128)(2,1)}, u32[]{:S(2)}) copy-start(bf16[12,48,256]{2,1,0:T(8,128)(2,1)} %get-tuple-element.393) | copy-start | bytes 884740
  155.7 13.6 %collective-permute-start.27 = (bf16[1920,128]{1,0:T(8,128)(2,1)}, bf16[1920,128]{1,0:T(8,128)(2,1)}, u32[]{:S(2)}, u32[]{:S(2)}) collective-permute-start(bf16[1920,128]{1,0:T(8,128)(2,1)} %add_convert_fusion), channel_id=1, source_target_pairs={{0,8},{4,12},{8,0},{12,4},{1,9},{5,13},{9,1},{13,5},{2,10},{6,14},... | collective-permute-start | bytes 1474568 | tf_op jit(solution)/shard_map/ppermute | solution.py:19
  156.1 13.3 %collective-permute-start.28 = (bf16[1920,128]{1,0:T(8,128)(2,1)}, bf16[1920,128]{1,0:T(8,128)(2,1)}, u32[]{:S(2)}, u32[]{:S(2)}) collective-permute-start(bf16[1920,128]{1,0:T(8,128)(2,1)} %add_convert_fusion), channel_id=1, source_target_pairs={{0,16},{16,0},{1,17},{17,1},{2,18},{18,2},{3,19},{19,3},{4,20},{20... | collective-permute-start | bytes 1474568 | tf_op jit(solution)/shard_map/ppermute | solution.py:19
  157.8 10.3 %collective-permute-start.26 = (bf16[12,48,256]{2,1,0:T(8,128)(2,1)S(1)}, bf16[12,48,256]{2,1,0:T(8,128)(2,1)S(1)}, u32[]{:S(2)}, u32[]{:S(2)}) collective-permute-start(bf16[12,48,256]{2,1,0:T(8,128)(2,1)S(1)} %copy-done.2), channel_id=1, source_target_pairs={{0,1},{1,2},{2,3},{3,0},{4,5},{5,6},{6,7},{7,4},{8,9},{9,10},{10,1... | collective-permute-start | bytes 884744 | tf_op jit(solution)/shard_map/ppermute | solution.py:15
  170.2 28.4 %collective-permute-start.29 = (bf16[12,48,256]{2,1,0:T(8,128)(2,1)}, bf16[12,48,256]{2,1,0:T(8,128)(2,1)}, u32[]{:S(2)}, u32[]{:S(2)}) collective-permute-start(bf16[12,48,256]{2,1,0:T(8,128)(2,1)} %broadcast_select_fusion.15), channel_id=1, source_target_pairs={{0,2},{1,3},{2,0},{3,1},{4,6},{5,7},{6,4},{7,5},{8,10},{9,11},{10,... | collective-permute-start | bytes 884744 | tf_op jit(solution)/shard_map/ppermute | solution.py:15
  175.9 9.7 %collective-permute-start.10 = (bf16[1920,256]{1,0:T(8,128)(2,1)S(1)}, bf16[1920,256]{1,0:T(8,128)(2,1)S(1)}, u32[]{:S(2)}, u32[]{:S(2)}) collective-permute-start(bf16[1920,256]{1,0:T(8,128)(2,1)S(1)} %pad_maximum_fusion.16.refs_0_), channel_id=1, source_target_pairs={{0,4},{4,0},{8,12},{12,8},{1,5},{5,1},{9,13},{13,9},{2,6},{6,2},{1... | collective-permute-start | bytes 2949128 | tf_op jit(solution)/shard_map/while/body/ppermute | solution.py:19
  176.0 8.4 %collective-permute-start.9 = (bf16[960,128]{1,0:T(8,128)(2,1)S(1)}, bf16[960,128]{1,0:T(8,128)(2,1)S(1)}, u32[]{:S(2)}, u32[]{:S(2)}) collective-permute-start(bf16[960,128]{1,0:T(8,128)(2,1)S(1)} %slice.83), channel_id=1, source_target_pairs={{0,8},{4,12},{8,0},{12,4},{1,9},{5,13},{9,1},{13,5},{2,10},{6,14},... | collective-permute-start | bytes 737288 | tf_op jit(solution)/shard_map/while/body/ppermute | solution.py:19
  177.5 8.1 %collective-permute-start.8 = (bf16[960,128]{1,0:T(8,128)(2,1)S(1)}, bf16[960,128]{1,0:T(8,128)(2,1)S(1)}, u32[]{:S(2)}, u32[]{:S(2)}) collective-permute-start(bf16[960,128]{1,0:T(8,128)(2,1)S(1)} %slice.82), channel_id=1, source_target_pairs={{0,16},{16,0},{1,17},{17,1},{2,18},{18,2},{3,19},{19,3},{4,20},{20... | collective-permute-start | bytes 737288 | tf_op jit(solution)/shard_map/while/body/ppermute | solution.py:19
  186.9 4.6 %collective-permute-start.11 = (bf16[1920,256]{1,0:T(8,128)(2,1)S(1)}, bf16[1920,256]{1,0:T(8,128)(2,1)}, u32[]{:S(2)}, u32[]{:S(2)}) collective-permute-start(bf16[1920,256]{1,0:T(8,128)(2,1)S(1)} %pad_maximum_fusion.17.refs_2_), channel_id=1, source_target_pairs={{0,4},{4,0},{8,12},{12,8},{1,5},{5,1},{9,13},{13,9},{2,6},{6,2},{1... | collective-permute-start | bytes 2949128 | tf_op jit(solution)/shard_map/while/body/ppermute | solution.py:19
  198.6 1.4 copy-start.1
  199.9 11.4 %collective-permute-start.30 = (bf16[12,48,256]{2,1,0:T(8,128)(2,1)S(1)}, bf16[12,48,256]{2,1,0:T(8,128)(2,1)S(1)}, u32[]{:S(2)}, u32[]{:S(2)}) collective-permute-start(bf16[12,48,256]{2,1,0:T(8,128)(2,1)S(1)} %copy-done.1), channel_id=1, source_target_pairs={{0,1},{1,2},{2,3},{3,0},{4,5},{5,6},{6,7},{7,4},{8,9},{9,10},{10,1... | collective-permute-start | bytes 884744 | tf_op jit(solution)/shard_map/ppermute | solution.py:15
  211.5 14.1 %collective-permute-start.34 = (bf16[12,48,256]{2,1,0:T(8,128)(2,1)S(1)}, bf16[12,48,256]{2,1,0:T(8,128)(2,1)S(1)}, u32[]{:S(2)}, u32[]{:S(2)}) collective-permute-start(bf16[12,48,256]{2,1,0:T(8,128)(2,1)S(1)} %broadcast_select_fusion.14), channel_id=1, source_target_pairs={{0,2},{1,3},{2,0},{3,1},{4,6},{5,7},{6,4},{7,5},{8,10},{9,11},{10,... | collective-permute-start | bytes 884744 | tf_op jit(solution)/shard_map/ppermute | solution.py:15
  211.6 1.9 collective-permute-start.31
  211.6 5.7 %collective-permute-start.32 = (bf16[4,48,2,1,128]{4,2,1,0,3:T(2,128)(2,1)S(1)}, bf16[4,48,2,1,128]{4,2,1,0,3:T(2,128)(2,1)S(1)}, u32[]{:S(2)}, u32[]{:S(2)}) collective-permute-start(bf16[4,48,2,1,128]{4,2,1,0,3:T(2,128)(2,1)S(1)} %squeeze.32), channel_id=1, source_target_pairs={{0,8},{4,12},{8,0},{12,4},{1,9},{5,13},{9,1},{13,5},{2,10},{6,14},... | collective-permute-start | bytes 294920 | tf_op jit(solution)/shard_map/ppermute | solution.py:19
  213.3 5.2 %collective-permute-start.33 = (bf16[4,48,2,1,128]{4,2,1,0,3:T(2,128)(2,1)S(1)}, bf16[4,48,2,1,128]{4,2,1,0,3:T(2,128)(2,1)S(1)}, u32[]{:S(2)}, u32[]{:S(2)}) collective-permute-start(bf16[4,48,2,1,128]{4,2,1,0,3:T(2,128)(2,1)S(1)} %squeeze.33), channel_id=1, source_target_pairs={{0,12},{4,8},{8,4},{12,0},{1,13},{5,9},{9,5},{13,1},{2,14},{6,10},... | collective-permute-start | bytes 294920 | tf_op jit(solution)/shard_map/ppermute | solution.py:19
  226.3 2.4 %collective-permute-start.35 = (bf16[4,48,2,1,128]{4,2,1,0,3:T(2,128)(2,1)S(1)}, bf16[4,48,2,1,128]{4,2,1,0,3:T(2,128)(2,1)S(1)}, u32[]{:S(2)}, u32[]{:S(2)}) collective-permute-start(bf16[4,48,2,1,128]{4,2,1,0,3:T(2,128)(2,1)S(1)} %squeeze.35), channel_id=1, source_target_pairs={{0,4},{4,0},{8,12},{12,8},{1,5},{5,1},{9,13},{13,9},{2,6},{6,2},{1... | collective-permute-start | bytes 294920 | tf_op jit(solution)/shard_map/ppermute | solution.py:19
  226.5 5.7 %collective-permute-start.36 = (bf16[4,48,2,1,128]{4,2,1,0,3:T(2,128)(2,1)S(1)}, bf16[4,48,2,1,128]{4,2,1,0,3:T(2,128)(2,1)S(1)}, u32[]{:S(2)}, u32[]{:S(2)}) collective-permute-start(bf16[4,48,2,1,128]{4,2,1,0,3:T(2,128)(2,1)S(1)} %squeeze.36), channel_id=1, source_target_pairs={{0,8},{4,12},{8,0},{12,4},{1,9},{5,13},{9,1},{13,5},{2,10},{6,14},... | collective-permute-start | bytes 294920 | tf_op jit(solution)/shard_map/ppermute | solution.py:19
  228.2 5.2 %collective-permute-start.37 = (bf16[4,48,2,1,128]{4,2,1,0,3:T(2,128)(2,1)S(1)}, bf16[4,48,2,1,128]{4,2,1,0,3:T(2,128)(2,1)S(1)}, u32[]{:S(2)}, u32[]{:S(2)}) collective-permute-start(bf16[4,48,2,1,128]{4,2,1,0,3:T(2,128)(2,1)S(1)} %squeeze.37), channel_id=1, source_target_pairs={{0,12},{4,8},{8,4},{12,0},{1,13},{5,9},{9,5},{13,1},{2,14},{6,10},... | collective-permute-start | bytes 294920 | tf_op jit(solution)/shard_map/ppermute | solution.py:19

commit v13 on v10

--- a/solution.py
+++ b/solution.py
@@ -89,7 +89,7 @@
     depth, rows = weight.shape
     half, columns = rows // 2, near[0].shape[1]
     width = columns // 2
-    tall = 240 if depth % 240 == 0 else depth
+    tall = 640 if depth % 640 == 0 else depth
     whole = pl.BlockSpec((half, columns), lambda i, choice: (0, 0))
     narrow = pl.BlockSpec((tall, width), lambda i, choice: (i, 0))
     shapes = [jax.ShapeDtypeStruct((depth, width), t) for t in (jnp.float32,) + 3 * (jnp.bfloat16,)]
@@ -144,10 +144,6 @@
     def outer_core(h):
         return (h ^ h // 2) % 2
 
-    feature_parts = [
-        lax.dynamic_slice_in_dim(feature_rows, (tile ^ r) * depth, depth, axis=1) for r in range(4)
-    ]
-
     def put_first(condition, one, other, axis):
         return jnp.concatenate(
             [jnp.where(condition, one, other), jnp.where(condition, other, one)], axis=axis
@@ -228,11 +224,16 @@
     def both_blocks(rows, other):
         return put_first(tile // 2 == head // 2, rows, other, 1)
 
-    key_ours, key_others = halves(0)
-    value_ours, value_others = halves(1)
-    bias_rows = moved(proj_bias, lambda t, h: (h, t))
-    key_ours = ours_to_plane(key_ours)
-    key_others, value_others = swapped(key_others, "tile", 2), swapped(value_others, "tile", 2)
+    ours = [halves(part)[0] for part in range(2)]
+    others = jnp.concatenate([halves(part)[1] for part in range(2)], axis=1)
+
+    def cross_x(given):
+        others, bias_rows = given
+        comes, bias_rows = step(
+            (swapped(others, "tile", 2), moved(bias_rows, lambda t, h: (h, t)))
+        )
+        return (comes, bias_rows), (comes, bias_rows)
+
     no_terms = (
         jnp.zeros((depth, width), jnp.float32),
         tuple(jnp.full((depth, width), k, jnp.bfloat16) for k in range(3)),
@@ -240,24 +241,30 @@
     no_tokens = tuple(
         jnp.full((tile_slots, shard_len, 2 * width), k, jnp.bfloat16) for k in range(2)
     )
-    bias_rows, key_ours, key_others, value_ours, value_others = step(
-        (bias_rows, key_ours, key_others, value_ours, value_others)
-    )
-
-    key_others, value_ours = others_to_plane(key_others), ours_to_plane(value_ours)
-    other = swapped(key_ours, "tile", 2)
+    empty = jnp.zeros_like(others), jnp.zeros_like(proj_bias)
+    key_ours, (comes, bias_rows), value_ours, feature_rows = step(
+        (
+            ours_to_plane(ours[0]),
+            in_loop(cross_x, (others, proj_bias), empty),
+            ours[1],
+            feature_rows,
+        )
+    )
+
+    key_others, value_others = comes[:, :width], comes[:, width:]
     bias_part = add_columns(bias_rows[None], kv_weight)
-    key_ours, key_others, value_ours, other, bias_part, feature_parts, no_terms, no_tokens, once = step(
+    feature_parts = [
+        lax.dynamic_slice_in_dim(feature_rows, (tile ^ r) * depth, depth, axis=1) for r in range(4)
+    ]
+    key_ours, key_others, value_ours, value_others, other, bias_part, feature_parts = step(
         (
             key_ours,
-            key_others,
-            value_ours,
-            other,
+            others_to_plane(key_others),
+            ours_to_plane(value_ours),
+            value_others,
+            swapped(key_ours, "tile", 2),
             bias_part,
             feature_parts,
-            no_terms,
-            no_tokens,
-            once,
         )
     )
 

time: 238 us -> 239 us (level)
  local copies, waits for them, and re-layouts: 27.5 us -> 32.1 us
  Pallas kernels: 19.8 us -> 16.1 us
    ppermute x5, waiting for transfers between devices: 6.25 us -> 0.01 us  [moved(): return lax.ppermute(shard, ('tile', 'head'), pairs)]
    ppermute x35 -> x34, waiting for transfers between devices: 84.3 us -> 90.1 us  [swapped(): lax.ppermute(shard, axis, [(i, i ^ bit) for i in range(lax.axis_size(axis...]
    pallas_call x2, Pallas kernels: 19.8 us -> 16.1 us  [product_terms(): pl.pallas_call(terms_body, out_shape=shapes, grid_spec=pltpu.PrefetchScal...]
    ppermute x35 -> x34, starting transfers between devices: 37.1 us -> 38.9 us  [swapped(): lax.ppermute(shard, axis, [(i, i ^ bit) for i in range(lax.axis_size(axis...]
    while x22 -> x28, local copies, waits for them, and re-layouts: 5.16 us -> 5.94 us
  transfers between devices with their start and end apart: 44 -> 43, of which waited for: 22 -> 20; matrix products, arithmetic and copies ran while one was open for 13% -> 14% of each run, Pallas kernels for 8% -> 7%
where the time goes in v13:
time: 239 us
  waiting for transfers between devices  111 us (46%)
  starting transfers between devices  54.4 us (23%)
  local copies, waits for them, and re-layouts  32.1 us (13%)
  Pallas kernels  16.1 us (7%)
  other arithmetic  13.3 us (6%)
  matrix products  9.94 us (4%)
    ppermute x34, waiting for transfers between devices, swapped(): lax.ppermute(shard, axis, [(i, i ^ bit) for i in range(lax.axis_size(axis...  90.1 us
    ppermute x34, starting transfers between devices, swapped(): lax.ppermute(shard, axis, [(i, i ^ bit) for i in range(lax.axis_size(axis...  38.9 us
    ppermute x4, waiting for transfers between devices, shifted_2(): lax.ppermute(shard, axis, [(i, (i + by) % count) for i in range(count)])  21.1 us
    pallas_call x2, Pallas kernels, product_terms(): pl.pallas_call(terms_body, out_shape=shapes, grid_spec=pltpu.PrefetchScal...  16.1 us
    ppermute x4, starting transfers between devices, shifted_2(): lax.ppermute(shard, axis, [(i, (i + by) % count) for i in range(count)])  10.6 us
    dot_general x11, matrix products, add_columns(): return jnp.dot(operand, portion, preferred_element_type=jnp.float32)  9.75 us
    dynamic_slice x1, local copies, waits for them, and re-layouts, product_plan(): lax.dynamic_slice_in_dim(feature_rows, (tile ^ r) * depth, depth, axis=1)  7.34 us
    while x28, local copies, waits for them, and re-layouts  5.94 us
  transfers between devices with their start and end apart: 43, of which 20 were waited for; matrix products, arithmetic and copies ran while one was open for 14% of the time, Pallas kernels for 7%

profile of v13, /device:TPU:0, one launch (start us, length us, event | category | flops | bytes accessed | tf_op | source)
XLA Modules:
  0.0 238.6 jit_solution(17005806877424179894)
XLA Ops:
  0.0 2.2 fusion.23
  5.7 23.5 %while.75 = (s32[]{:T(128)}, bf16[1024,256]{1,0:T(8,128)(2,1)S(1)}, bf16[2048]{0:T(1024)(128)(2,1)S(1)}, bf16[1024,256]{1,0:T(8,128)(2,1)}, bf16[2048]{0:T(1024)(128)(2,1)}, /*index=5*/s32[]{:T(128)}, s32[]{:T(128)}) while((s32[]{:T(128)}, bf16[1024,256]{1,0:T(8,128)(2,1)S(1)}, bf16[2048]{0:T(1024)(128)(2,1)S(1)}, ...), condition=%wide.region_3.4_spmd, body=%wide.region_2.3_spmd.sunk | while | flops 2 | bytes 5284053 | solution.py:172
  5.7 6.7 %collective-permute-start = (bf16[1024,256]{1,0:T(8,128)(2,1)S(1)}, bf16[1024,256]{1,0:T(8,128)(2,1)S(1)}, u32[]{:S(2)}, u32[]{:S(2)}) collective-permute-start(bf16[1024,256]{1,0:T(8,128)(2,1)S(1)} %get-tuple-element.1227), channel_id=1, source_target_pairs={{0,8},{4,12},{8,0},{12,4},{1,9},{5,13},{9,1},{13,5},{2,10},{6,14},... | collective-permute-start | bytes 1572872 | tf_op jit(solution)/shard_map/while/body/ppermute | solution.py:17
  13.1 15.3 %collective-permute-done = bf16[1024,256]{1,0:T(8,128)(2,1)S(1)} collective-permute-done((bf16[1024,256]{1,0:T(8,128)(2,1)S(1)}, bf16[1024,256]{1,0:T(8,128)(2,1)S(1)}, u32[]{:S(2)}, u32[]{:S(2)}) %collective-permute-start) | collective-permute-done | bytes 524320 | tf_op jit(solution)/shard_map/while/body/ppermute | solution.py:17
  29.3 1.8 fusion.24
  31.0 1.4 collective-permute-start.17
  33.1 2.8 %collective-permute-start.19 = (bf16[1024,128]{1,0:T(8,128)(2,1)S(1)}, bf16[1024,128]{1,0:T(8,128)(2,1)S(1)}, u32[]{:S(2)}, u32[]{:S(2)}) collective-permute-start(bf16[1024,128]{1,0:T(8,128)(2,1)S(1)} %collective-permute-done.16), channel_id=1, source_target_pairs={{0,8},{4,12},{8,0},{12,4},{1,9},{5,13},{9,1},{13,5},{2,10},{6,14},... | collective-permute-start | bytes 786440 | tf_op jit(solution)/shard_map/ppermute | solution.py:17
  36.6 7.3 %constant_dynamic-slice_fusion = (bf16[576,1920]{1,0:T(8,128)(2,1)}, bf16[576,1920]{1,0:T(8,128)(2,1)}, bf16[576,1920]{1,0:T(8,128)(2,1)}, bf16[576,1920]{1,0:T(8,128)(2,1)}) fusion(bf16[576,7680]{1,0:T(8,128)(2,1)} %bitcast.135, s32[]{:T(128)S(6)} %select_n.333, s32[]{:T(128)S(6)} %select_n.332, s32[]{:T(128)S(6)} %select_n.331, s32[]{:T(128)S(6)} %select_n.330), kind=kLoop, calls=%fused_computation.111 | loop fusion | bytes 17694736 | tf_op jit(solution)/shard_map/dynamic_slice | solution.py:257
  44.3 2.0 collective-permute-done.19
  46.4 2.1 collective-permute-start.21
  48.5 2.2 collective-permute-start.20
  50.7 6.5 %collective-permute-done.20 = bf16[1024,128]{1,0:T(8,128)(2,1)S(1)} collective-permute-done((bf16[1024,128]{1,0:T(8,128)(2,1)S(1)}, bf16[1024,128]{1,0:T(8,128)(2,1)S(1)}, u32[]{:S(2)}, u32[]{:S(2)}) %collective-permute-start.20) | collective-permute-done | bytes 262176 | tf_op jit(solution)/shard_map/ppermute | solution.py:17
  58.0 1.5 collective-permute-start.23
  59.5 7.9 %shard_map.82 = (f32[1920,128]{1,0:T(8,128)S(1)}, bf16[1920,128]{1,0:T(8,128)(2,1)}, bf16[1920,128]{1,0:T(8,128)(2,1)}, bf16[1920,128]{1,0:T(8,128)(2,1)S(1)}) custom-call(s32[2]{0:T(128)S(1)} %pad_add_fusion.choice, bf16[1920,2048]{1,0:T(8,128)(2,1)} %others.1, bf16[1920,2048]{1,0:T(8,128)(2,1)} %others.1, ...), custom_call_target="tpu_custom_call" | custom-call | flops 4026531840 | bytes 12419072 | tf_op jit(solution)/shard_map/pallas_call | solution.py:96
  68.9 1.3 collective-permute-start.25
  70.2 3.8 %collective-permute-start.26 = (bf16[1920,128]{1,0:T(8,128)(2,1)}, bf16[1920,128]{1,0:T(8,128)(2,1)}, u32[]{:S(2)}, u32[]{:S(2)}) collective-permute-start(bf16[1920,128]{1,0:T(8,128)(2,1)} %get-tuple-element.701), channel_id=1, source_target_pairs={{0,3},{1,2},{2,1},{3,0},{4,7},{5,6},{6,5},{7,4},{8,11},{9,10},{10,... | collective-permute-start | bytes 1474568 | tf_op jit(solution)/shard_map/ppermute | solution.py:17
  77.6 26.4 %while.76 = (s32[]{:T(128)}, bf16[1024,128]{1,0:T(8,128)(2,1)S(1)}, bf16[1024,128]{1,0:T(8,128)(2,1)}, f32[1,512]{1,0:T(1,128)S(1)}, f32[1920,128]{1,0:T(8,128)}...) while((s32[]{:T(128)}, bf16[1024,128]{1,0:T(8,128)(2,1)S(1)}, ...), condition=%wide.region_5.6_spmd, body=%wide.region_4.5_spmd.sunk | while | flops 4029153792 | bytes 25020776 | solution.py:172
  78.6 2.0 collective-permute-start.3
  80.7 11.5 %collective-permute-done.4 = f32[1,512]{1,0:T(1,128)S(1)} collective-permute-done((f32[1,512]{1,0:T(1,128)S(1)}, f32[1,512]{1,0:T(1,128)S(1)}, u32[]{:S(2)}, u32[]{:S(2)}) %collective-permute-start.4) | collective-permute-done | bytes 2080 | tf_op jit(solution)/shard_map/while/body/ppermute | solution.py:17
  95.7 8.2 %body.4 = (f32[1920,128]{1,0:T(8,128)}, bf16[1920,128]{1,0:T(8,128)(2,1)}, bf16[1920,128]{1,0:T(8,128)(2,1)}, bf16[1920,128]{1,0:T(8,128)(2,1)}) custom-call(s32[2]{0:T(128)S(1)} %get-tuple-element.1279.choice, bf16[1920,2048]{1,0:T(8,128)(2,1)} %get-tuple-element.1280.ours.others, bf16[1920,2048]{1,0:T(8,128)(2,1)} %get-tuple-element.1280.ours.others, ...), custom_call_target="tpu_custom_call" | custom-call | flops 4026531840 | bytes 12419072 | tf_op jit(solution)/shard_map/while/body/pallas_call | solution.py:96
  104.2 13.5 %collective-permute-done.27 = bf16[1920,128]{1,0:T(8,128)(2,1)S(1)} collective-permute-done((bf16[1920,128]{1,0:T(8,128)(2,1)}, bf16[1920,128]{1,0:T(8,128)(2,1)S(1)}, u32[]{:S(2)}, u32[]{:S(2)}) %collective-permute-start.27) | collective-permute-done | bytes 491552 | tf_op jit(solution)/shard_map/ppermute | solution.py:17
  117.8 2.6 %collective-permute-start.29 = (bf16[1920,128]{1,0:T(8,128)(2,1)}, bf16[1920,128]{1,0:T(8,128)(2,1)}, u32[]{:S(2)}, u32[]{:S(2)}) collective-permute-start(bf16[1920,128]{1,0:T(8,128)(2,1)} %get-tuple-element.712), channel_id=1, source_target_pairs={{0,3},{1,2},{2,1},{3,0},{4,7},{5,6},{6,5},{7,4},{8,11},{9,10},{10,... | collective-permute-start | bytes 1474568 | tf_op jit(solution)/shard_map/ppermute | solution.py:17
  121.2 1.4 add_convert_fusion.1
  123.4 33.6 %while.77 = (s32[]{:T(128)}, bf16[1920,128]{1,0:T(8,128)(2,1)S(1)}, bf16[12,48,256]{2,1,0:T(8,128)(2,1)}, s32[]{:T(128)}, pred[]{:T(512)}, /*index=5*/bf16[576,1...) while((s32[]{:T(128)}, bf16[1920,128]{1,0:T(8,128)(2,1)S(1)}, ...), condition=%wide.region_9.10_spmd, body=%wide.region_6.9_spmd.sunk | while | flops 2271905024 | bytes 76995496 | solution.py:172
  123.5 1.4 collective-permute-start.8
  124.9 10.4 %collective-permute-done.7 = bf16[1920,128]{1,0:T(8,128)(2,1)S(1)} collective-permute-done((bf16[1920,128]{1,0:T(8,128)(2,1)S(1)}, bf16[1920,128]{1,0:T(8,128)(2,1)S(1)}, u32[]{:S(2)}, u32[]{:S(2)}) %collective-permute-start.7) | collective-permute-done | bytes 491552 | tf_op jit(solution)/shard_map/while/body/ppermute | solution.py:17
  135.7 1.7 collective-permute-start.9
  137.4 11.9 %collective-permute-done.9 = bf16[1920,128]{1,0:T(8,128)(2,1)S(1)} collective-permute-done((bf16[1920,128]{1,0:T(8,128)(2,1)S(1)}, bf16[1920,128]{1,0:T(8,128)(2,1)S(1)}, u32[]{:S(2)}, u32[]{:S(2)}) %collective-permute-start.9) | collective-permute-done | bytes 491552 | tf_op jit(solution)/shard_map/while/body/ppermute | solution.py:17
  151.2 2.1 convolution_add_fusion.10
  157.0 1.8 add_convert_fusion
  158.8 1.7 collective-permute-start.32
  160.5 1.4 collective-permute-start.33
  162.1 5.2 %collective-permute-start.31 = (bf16[12,48,256]{2,1,0:T(8,128)(2,1)S(1)}, bf16[12,48,256]{2,1,0:T(8,128)(2,1)S(1)}, u32[]{:S(2)}, u32[]{:S(2)}) collective-permute-start(bf16[12,48,256]{2,1,0:T(8,128)(2,1)S(1)} %copy-done.14), channel_id=1, source_target_pairs={{0,1},{1,2},{2,3},{3,0},{4,5},{5,6},{6,7},{7,4},{8,9},{9,10},{10,1... | collective-permute-start | bytes 884744 | tf_op jit(solution)/shard_map/ppermute | solution.py:13
  167.4 6.0 %collective-permute-done.31 = bf16[12,48,256]{2,1,0:T(8,128)(2,1)S(1)} collective-permute-done((bf16[12,48,256]{2,1,0:T(8,128)(2,1)S(1)}, bf16[12,48,256]{2,1,0:T(8,128)(2,1)S(1)}, u32[]{:S(2)}, u32[]{:S(2)}) %collective-permute-start.31) | collective-permute-done | bytes 294944 | tf_op jit(solution)/shard_map/ppermute | solution.py:13
  174.7 4.9 %collective-permute-start.34 = (bf16[12,48,256]{2,1,0:T(8,128)(2,1)}, bf16[12,48,256]{2,1,0:T(8,128)(2,1)}, u32[]{:S(2)}, u32[]{:S(2)}) collective-permute-start(bf16[12,48,256]{2,1,0:T(8,128)(2,1)} %broadcast_select_fusion.15), channel_id=1, source_target_pairs={{0,2},{1,3},{2,0},{3,1},{4,6},{5,7},{6,4},{7,5},{8,10},{9,11},{10,... | collective-permute-start | bytes 884744 | tf_op jit(solution)/shard_map/ppermute | solution.py:13
  180.4 20.0 %while.78 = (s32[]{:T(128)}, bf16[1920,128]{1,0:T(8,128)(2,1)S(1)}, bf16[1920,128]{1,0:T(8,128)(2,1)S(1)}, bf16[1920,128]{1,0:T(8,128)(2,1)S(1)}, bf16[12,48,256...) while((s32[]{:T(128)}, bf16[1920,128]{1,0:T(8,128)(2,1)S(1)}, ...), condition=%wide.region_11.12_spmd, body=%wide.region_10.11_spmd.sunk | while | flops 2271166464 | bytes 77368712 | solution.py:172
  181.4 1.3 collective-permute-start.13
  183.4 1.4 collective-permute-start.12
  184.8 5.1 %collective-permute-done.13 = bf16[960,128]{1,0:T(8,128)(2,1)S(1)} collective-permute-done((bf16[960,128]{1,0:T(8,128)(2,1)}, bf16[960,128]{1,0:T(8,128)(2,1)S(1)}, u32[]{:S(2)}, u32[]{:S(2)}) %collective-permute-start.13) | collective-permute-done | bytes 245792 | tf_op jit(solution)/shard_map/while/body/ppermute | solution.py:17
  190.0 1.7 collective-permute-done.12
  192.1 1.3 copy-done.12
  195.0 2.1 convolution_add_fusion.12
  203.1 8.9 %collective-permute-done.35 = bf16[12,48,256]{2,1,0:T(8,128)(2,1)S(1)} collective-permute-done((bf16[12,48,256]{2,1,0:T(8,128)(2,1)S(1)}, bf16[12,48,256]{2,1,0:T(8,128)(2,1)S(1)}, u32[]{:S(2)}, u32[]{:S(2)}) %collective-permute-start.35) | collective-permute-done | bytes 294944 | tf_op jit(solution)/shard_map/ppermute | solution.py:13
  214.1 3.8 %collective-permute-done.37 = bf16[4,48,2,1,128]{4,2,1,0,3:T(2,128)(2,1)S(1)} collective-permute-done((bf16[4,48,2,1,128]{4,2,1,0,3:T(2,128)(2,1)S(1)}, bf16[4,48,2,1,128]{4,2,1,0,3:T(2,128)(2,1)S(1)}, u32[]{:S(2)}, u32[]{:S(2)}) %collective-permute-start.37) | collective-permute-done | bytes 98336 | tf_op jit(solution)/shard_map/ppermute | solution.py:17
  219.1 6.1 %collective-permute-done.39 = bf16[12,48,256]{2,1,0:T(8,128)(2,1)S(1)} collective-permute-done((bf16[12,48,256]{2,1,0:T(8,128)(2,1)S(1)}, bf16[12,48,256]{2,1,0:T(8,128)(2,1)S(1)}, u32[]{:S(2)}, u32[]{:S(2)}) %collective-permute-start.39) | collective-permute-done | bytes 294944 | tf_op jit(solution)/shard_map/ppermute | solution.py:13
  228.4 3.4 %collective-permute-done.41 = bf16[4,48,2,1,128]{4,2,1,0,3:T(2,128)(2,1)S(1)} collective-permute-done((bf16[4,48,2,1,128]{4,2,1,0,3:T(2,128)(2,1)S(1)}, bf16[4,48,2,1,128]{4,2,1,0,3:T(2,128)(2,1)S(1)}, u32[]{:S(2)}, u32[]{:S(2)}) %collective-permute-start.41) | collective-permute-done | bytes 98336 | tf_op jit(solution)/shard_map/ppermute | solution.py:17
  231.8 1.3 collective-permute-done.42
  236.5 2.1 copy.19
  (187 shorter events, 45.6 us)
Async XLA Ops:
  2.2 27.1 %collective-permute-start.16 = (bf16[1024,128]{1,0:T(8,128)(2,1)S(1)}, bf16[1024,128]{1,0:T(8,128)(2,1)S(1)}, u32[]{:S(2)}, u32[]{:S(2)}) collective-permute-start(bf16[1024,128]{1,0:T(8,128)(2,1)S(1)} %get-tuple-element.862), channel_id=1, source_target_pairs={{0,0},{1,4},{2,12},{3,8},{4,1},{5,5},{6,13},{7,9},{8,2},{9,6},{10,... | collective-permute-start | bytes 786440 | tf_op jit(solution)/shard_map/ppermute | solution.py:142
  5.7 22.7 %collective-permute-start = (bf16[1024,256]{1,0:T(8,128)(2,1)S(1)}, bf16[1024,256]{1,0:T(8,128)(2,1)S(1)}, u32[]{:S(2)}, u32[]{:S(2)}) collective-permute-start(bf16[1024,256]{1,0:T(8,128)(2,1)S(1)} %get-tuple-element.1227), channel_id=1, source_target_pairs={{0,8},{4,12},{8,0},{12,4},{1,9},{5,13},{9,1},{13,5},{2,10},{6,14},... | collective-permute-start | bytes 1572872 | tf_op jit(solution)/shard_map/while/body/ppermute | solution.py:17
  12.5 0.7 collective-permute-start.1
  13.1 15.4 %copy-start.15 = (bf16[2048]{0:T(1024)(128)(2,1)}, bf16[2048]{0:T(1024)(128)(2,1)S(1)}, u32[]{:S(2)}) copy-start(bf16[2048]{0:T(1024)(128)(2,1)S(1)} %collective-permute-done.1) | copy-start | bytes 12292 | tf_op jit(solution)/shard_map/while
  31.0 13.2 %collective-permute-start.17 = (bf16[1024,128]{1,0:T(8,128)(2,1)S(1)}, bf16[1024,128]{1,0:T(8,128)(2,1)S(1)}, u32[]{:S(2)}, u32[]{:S(2)}) collective-permute-start(bf16[1024,128]{1,0:T(8,128)(2,1)S(1)} %get-tuple-element.868), channel_id=1, source_target_pairs={{0,2},{1,6},{2,14},{3,10},{4,3},{5,7},{6,15},{7,11},{8,0},{9,4},{1... | collective-permute-start | bytes 786440 | tf_op jit(solution)/shard_map/ppermute | solution.py:142
  32.4 11.8 %collective-permute-start.18 = (bf16[1024,128]{1,0:T(8,128)(2,1)S(1)}, bf16[1024,128]{1,0:T(8,128)(2,1)S(1)}, u32[]{:S(2)}, u32[]{:S(2)}) collective-permute-start(bf16[1024,128]{1,0:T(8,128)(2,1)S(1)} %get-tuple-element.685), channel_id=1, source_target_pairs={{0,0},{1,4},{2,12},{3,8},{4,1},{5,5},{6,13},{7,9},{8,2},{9,6},{10,... | collective-permute-start | bytes 786440 | tf_op jit(solution)/shard_map/ppermute | solution.py:142
  33.1 13.2 %collective-permute-start.19 = (bf16[1024,128]{1,0:T(8,128)(2,1)S(1)}, bf16[1024,128]{1,0:T(8,128)(2,1)S(1)}, u32[]{:S(2)}, u32[]{:S(2)}) collective-permute-start(bf16[1024,128]{1,0:T(8,128)(2,1)S(1)} %collective-permute-done.16), channel_id=1, source_target_pairs={{0,8},{4,12},{8,0},{12,4},{1,9},{5,13},{9,1},{13,5},{2,10},{6,14},... | collective-permute-start | bytes 786440 | tf_op jit(solution)/shard_map/ppermute | solution.py:17
  46.4 10.8 %collective-permute-start.21 = (bf16[1024,256]{1,0:T(8,128)(2,1)S(1)}, bf16[1024,256]{1,0:T(8,128)(2,1)S(1)}, u32[]{:S(2)}, u32[]{:S(2)}) collective-permute-start(bf16[1024,256]{1,0:T(8,128)(2,1)S(1)} %pad_maximum_fusion.10.near_ours), channel_id=1, source_target_pairs={{0,4},{4,0},{8,12},{12,8},{1,5},{5,1},{9,13},{13,9},{2,6},{6,2},{1... | collective-permute-start | bytes 1572872 | tf_op jit(solution)/shard_map/ppermute | solution.py:17
  48.5 8.7 %collective-permute-start.20 = (bf16[1024,128]{1,0:T(8,128)(2,1)S(1)}, bf16[1024,128]{1,0:T(8,128)(2,1)S(1)}, u32[]{:S(2)}, u32[]{:S(2)}) collective-permute-start(bf16[1024,128]{1,0:T(8,128)(2,1)S(1)} %collective-permute-done.17), channel_id=1, source_target_pairs={{0,8},{4,12},{8,0},{12,4},{1,9},{5,13},{9,1},{13,5},{2,10},{6,14},... | collective-permute-start | bytes 786440 | tf_op jit(solution)/shard_map/ppermute | solution.py:17
  57.4 2.1 collective-permute-start.22
  57.5 2.0 collective-permute-start.24
  58.0 10.2 %collective-permute-start.23 = (bf16[1024,128]{1,0:T(8,128)(2,1)}, bf16[1024,128]{1,0:T(8,128)(2,1)S(1)}, u32[]{:S(2)}, u32[]{:S(2)}) collective-permute-start(bf16[1024,128]{1,0:T(8,128)(2,1)} %get-tuple-element.698), channel_id=1, source_target_pairs={{0,2},{1,6},{2,14},{3,10},{4,3},{5,7},{6,15},{7,11},{8,0},{9,4},{1... | collective-permute-start | bytes 786440 | tf_op jit(solution)/shard_map/ppermute | solution.py:142
  68.9 35.3 %collective-permute-start.25 = (bf16[1920,128]{1,0:T(8,128)(2,1)}, bf16[1920,128]{1,0:T(8,128)(2,1)}, u32[]{:S(2)}, u32[]{:S(2)}) collective-permute-start(bf16[1920,128]{1,0:T(8,128)(2,1)} %get-tuple-element.700), channel_id=1, source_target_pairs={{0,2},{1,3},{2,0},{3,1},{4,6},{5,7},{6,4},{7,5},{8,10},{9,11},{10,... | collective-permute-start | bytes 1474568 | tf_op jit(solution)/shard_map/ppermute | solution.py:17
  70.2 34.0 %collective-permute-start.26 = (bf16[1920,128]{1,0:T(8,128)(2,1)}, bf16[1920,128]{1,0:T(8,128)(2,1)}, u32[]{:S(2)}, u32[]{:S(2)}) collective-permute-start(bf16[1920,128]{1,0:T(8,128)(2,1)} %get-tuple-element.701), channel_id=1, source_target_pairs={{0,3},{1,2},{2,1},{3,0},{4,7},{5,6},{6,5},{7,4},{8,11},{9,10},{10,... | collective-permute-start | bytes 1474568 | tf_op jit(solution)/shard_map/ppermute | solution.py:17
  77.6 26.5 %copy-start.19 = (s32[4,4]{1,0:T(4,128)S(1)}, s32[4,4]{1,0:T(4,128)}, u32[]{:S(2)}) copy-start(s32[4,4]{1,0:T(4,128)} %param.21) | copy-start | bytes 196
  77.6 26.6 %copy-start.21 = (s32[4]{0:T(128)S(1)}, s32[4]{0:T(128)}, u32[]{:S(2)}) copy-start(s32[4]{0:T(128)} %param.23) | copy-start | bytes 52
  77.6 14.6 %collective-permute-start.2 = (bf16[1024,128]{1,0:T(8,128)(2,1)S(1)}, bf16[1024,128]{1,0:T(8,128)(2,1)S(1)}, u32[]{:S(2)}, u32[]{:S(2)}) collective-permute-start(bf16[1024,128]{1,0:T(8,128)(2,1)S(1)} %copy.48), channel_id=1, source_target_pairs={{0,8},{4,12},{8,0},{12,4},{1,9},{5,13},{9,1},{13,5},{2,10},{6,14},... | collective-permute-start | bytes 786440 | tf_op jit(solution)/shard_map/while/body/ppermute | solution.py:17
  78.6 13.6 %collective-permute-start.3 = (bf16[1024,128]{1,0:T(8,128)(2,1)S(1)}, bf16[1024,128]{1,0:T(8,128)(2,1)S(1)}, u32[]{:S(2)}, u32[]{:S(2)}) collective-permute-start(bf16[1024,128]{1,0:T(8,128)(2,1)S(1)} %copy.49), channel_id=1, source_target_pairs={{0,8},{4,12},{8,0},{12,4},{1,9},{5,13},{9,1},{13,5},{2,10},{6,14},... | collective-permute-start | bytes 786440 | tf_op jit(solution)/shard_map/while/body/ppermute | solution.py:17
  80.6 11.6 %collective-permute-start.4 = (f32[1,512]{1,0:T(1,128)S(1)}, f32[1,512]{1,0:T(1,128)S(1)}, u32[]{:S(2)}, u32[]{:S(2)}) collective-permute-start(f32[1,512]{1,0:T(1,128)S(1)} %copy.50), channel_id=1, source_target_pairs={{0,8},{4,12},{8,0},{12,4},{1,9},{5,13},{9,1},{13,5},{2,10},{6,14},... | collective-permute-start | bytes 6152 | tf_op jit(solution)/shard_map/while/body/ppermute | solution.py:17
  92.9 2.0 collective-permute-start.5
  93.4 2.3 collective-permute-start.6
  104.0 19.4 %copy-start.16 = (f32[1,512]{1,0:T(1,128)S(1)}, f32[1,512]{1,0:T(1,128)}, u32[]{:S(2)}) copy-start(f32[1,512]{1,0:T(1,128)} %get-tuple-element.722) | copy-start | bytes 6148
  104.0 19.4 %copy-start.17 = (f32[1,128]{1,0:T(1,128)S(1)}, f32[1,128]{1,0:T(1,128)}, u32[]{:S(2)}) copy-start(f32[1,128]{1,0:T(1,128)} %param.20) | copy-start | bytes 1540
  104.0 13.8 %collective-permute-start.27 = (bf16[1920,128]{1,0:T(8,128)(2,1)}, bf16[1920,128]{1,0:T(8,128)(2,1)S(1)}, u32[]{:S(2)}, u32[]{:S(2)}) collective-permute-start(bf16[1920,128]{1,0:T(8,128)(2,1)} %copy-done), channel_id=1, source_target_pairs={{0,1},{1,0},{2,3},{3,2},{4,5},{5,4},{6,7},{7,6},{8,9},{9,8},{10,11... | collective-permute-start | bytes 1474568 | tf_op jit(solution)/shard_map/ppermute | solution.py:17
  117.8 39.3 %collective-permute-start.28 = (bf16[1920,128]{1,0:T(8,128)(2,1)}, bf16[1920,128]{1,0:T(8,128)(2,1)S(1)}, u32[]{:S(2)}, u32[]{:S(2)}) collective-permute-start(bf16[1920,128]{1,0:T(8,128)(2,1)} %get-tuple-element.711), channel_id=1, source_target_pairs={{0,2},{1,3},{2,0},{3,1},{4,6},{5,7},{6,4},{7,5},{8,10},{9,11},{10,... | collective-permute-start | bytes 1474568 | tf_op jit(solution)/shard_map/ppermute | solution.py:17
  117.8 39.3 %collective-permute-start.29 = (bf16[1920,128]{1,0:T(8,128)(2,1)}, bf16[1920,128]{1,0:T(8,128)(2,1)}, u32[]{:S(2)}, u32[]{:S(2)}) collective-permute-start(bf16[1920,128]{1,0:T(8,128)(2,1)} %get-tuple-element.712), channel_id=1, source_target_pairs={{0,3},{1,2},{2,1},{3,0},{4,7},{5,6},{6,5},{7,4},{8,11},{9,10},{10,... | collective-permute-start | bytes 1474568 | tf_op jit(solution)/shard_map/ppermute | solution.py:17
  120.4 36.6 %collective-permute-start.30 = (bf16[1920,128]{1,0:T(8,128)(2,1)}, bf16[1920,128]{1,0:T(8,128)(2,1)}, u32[]{:S(2)}, u32[]{:S(2)}) collective-permute-start(bf16[1920,128]{1,0:T(8,128)(2,1)} %get-tuple-element.713), channel_id=1, source_target_pairs={{0,1},{1,0},{2,3},{3,2},{4,5},{5,4},{6,7},{7,6},{8,9},{9,8},{10,11... | collective-permute-start | bytes 1474568 | tf_op jit(solution)/shard_map/ppermute | solution.py:17
  123.4 11.9 %collective-permute-start.7 = (bf16[1920,128]{1,0:T(8,128)(2,1)S(1)}, bf16[1920,128]{1,0:T(8,128)(2,1)S(1)}, u32[]{:S(2)}, u32[]{:S(2)}) collective-permute-start(bf16[1920,128]{1,0:T(8,128)(2,1)S(1)} %copy.69), channel_id=1, source_target_pairs={{0,8},{4,12},{8,0},{12,4},{1,9},{5,13},{9,1},{13,5},{2,10},{6,14},... | collective-permute-start | bytes 1474568 | tf_op jit(solution)/shard_map/while/body/ppermute | solution.py:17
  123.5 11.9 %collective-permute-start.8 = (bf16[1920,128]{1,0:T(8,128)(2,1)S(1)}, bf16[1920,128]{1,0:T(8,128)(2,1)S(1)}, u32[]{:S(2)}, u32[]{:S(2)}) collective-permute-start(bf16[1920,128]{1,0:T(8,128)(2,1)S(1)} %copy.69), channel_id=1, source_target_pairs={{0,16},{16,0},{1,17},{17,1},{2,18},{18,2},{3,19},{19,3},{4,20},{20... | collective-permute-start | bytes 1474568 | tf_op jit(solution)/shard_map/while/body/ppermute | solution.py:17
  135.6 13.7 %collective-permute-start.10 = (bf16[1920,256]{1,0:T(8,128)(2,1)S(1)}, bf16[1920,256]{1,0:T(8,128)(2,1)}, u32[]{:S(2)}, u32[]{:S(2)}) collective-permute-start(bf16[1920,256]{1,0:T(8,128)(2,1)S(1)} %pad_maximum_fusion.22), channel_id=1, source_target_pairs={{0,4},{4,0},{8,12},{12,8},{1,5},{5,1},{9,13},{13,9},{2,6},{6,2},{1... | collective-permute-start | bytes 2949128 | tf_op jit(solution)/shard_map/while/body/ppermute | solution.py:17
  135.7 13.6 %collective-permute-start.9 = (bf16[1920,128]{1,0:T(8,128)(2,1)S(1)}, bf16[1920,128]{1,0:T(8,128)(2,1)S(1)}, u32[]{:S(2)}, u32[]{:S(2)}) collective-permute-start(bf16[1920,128]{1,0:T(8,128)(2,1)S(1)} %collective-permute-done.8), channel_id=1, source_target_pairs={{0,8},{4,12},{8,0},{12,4},{1,9},{5,13},{9,1},{13,5},{2,10},{6,14},... | collective-permute-start | bytes 1474568 | tf_op jit(solution)/shard_map/while/body/ppermute | solution.py:17
  149.5 4.7 %collective-permute-start.11 = (bf16[1920,256]{1,0:T(8,128)(2,1)S(1)}, bf16[1920,256]{1,0:T(8,128)(2,1)S(1)}, u32[]{:S(2)}, u32[]{:S(2)}) collective-permute-start(bf16[1920,256]{1,0:T(8,128)(2,1)S(1)} %pad_maximum_fusion.23), channel_id=1, source_target_pairs={{0,4},{4,0},{8,12},{12,8},{1,5},{5,1},{9,13},{13,9},{2,6},{6,2},{1... | collective-permute-start | bytes 2949128 | tf_op jit(solution)/shard_map/while/body/ppermute | solution.py:17
  158.8 14.7 %collective-permute-start.32 = (bf16[1920,128]{1,0:T(8,128)(2,1)S(1)}, bf16[1920,128]{1,0:T(8,128)(2,1)S(1)}, u32[]{:S(2)}, u32[]{:S(2)}) collective-permute-start(bf16[1920,128]{1,0:T(8,128)(2,1)S(1)} %add_convert_fusion), channel_id=1, source_target_pairs={{0,8},{4,12},{8,0},{12,4},{1,9},{5,13},{9,1},{13,5},{2,10},{6,14},... | collective-permute-start | bytes 1474568 | tf_op jit(solution)/shard_map/ppermute | solution.py:17
  160.5 13.3 %collective-permute-start.33 = (bf16[1920,128]{1,0:T(8,128)(2,1)S(1)}, bf16[1920,128]{1,0:T(8,128)(2,1)S(1)}, u32[]{:S(2)}, u32[]{:S(2)}) collective-permute-start(bf16[1920,128]{1,0:T(8,128)(2,1)S(1)} %add_convert_fusion), channel_id=1, source_target_pairs={{0,16},{16,0},{1,17},{17,1},{2,18},{18,2},{3,19},{19,3},{4,20},{20... | collective-permute-start | bytes 1474568 | tf_op jit(solution)/shard_map/ppermute | solution.py:17
  162.1 11.3 %collective-permute-start.31 = (bf16[12,48,256]{2,1,0:T(8,128)(2,1)S(1)}, bf16[12,48,256]{2,1,0:T(8,128)(2,1)S(1)}, u32[]{:S(2)}, u32[]{:S(2)}) collective-permute-start(bf16[12,48,256]{2,1,0:T(8,128)(2,1)S(1)} %copy-done.14), channel_id=1, source_target_pairs={{0,1},{1,2},{2,3},{3,0},{4,5},{5,6},{6,7},{7,4},{8,9},{9,10},{10,1... | collective-permute-start | bytes 884744 | tf_op jit(solution)/shard_map/ppermute | solution.py:13
  174.7 25.7 %collective-permute-start.34 = (bf16[12,48,256]{2,1,0:T(8,128)(2,1)}, bf16[12,48,256]{2,1,0:T(8,128)(2,1)}, u32[]{:S(2)}, u32[]{:S(2)}) collective-permute-start(bf16[12,48,256]{2,1,0:T(8,128)(2,1)} %broadcast_select_fusion.15), channel_id=1, source_target_pairs={{0,2},{1,3},{2,0},{3,1},{4,6},{5,7},{6,4},{7,5},{8,10},{9,11},{10,... | collective-permute-start | bytes 884744 | tf_op jit(solution)/shard_map/ppermute | solution.py:13
  180.6 11.1 %collective-permute-start.14 = (bf16[1920,256]{1,0:T(8,128)(2,1)S(1)}, bf16[1920,256]{1,0:T(8,128)(2,1)}, u32[]{:S(2)}, u32[]{:S(2)}) collective-permute-start(bf16[1920,256]{1,0:T(8,128)(2,1)S(1)} %pad_maximum_fusion.25), channel_id=1, source_target_pairs={{0,4},{4,0},{8,12},{12,8},{1,5},{5,1},{9,13},{13,9},{2,6},{6,2},{1... | collective-permute-start | bytes 2949128 | tf_op jit(solution)/shard_map/while/body/ppermute | solution.py:17
  181.4 8.6 %collective-permute-start.13 = (bf16[960,128]{1,0:T(8,128)(2,1)}, bf16[960,128]{1,0:T(8,128)(2,1)S(1)}, u32[]{:S(2)}, u32[]{:S(2)}) collective-permute-start(bf16[960,128]{1,0:T(8,128)(2,1)} %slice.153), channel_id=1, source_target_pairs={{0,8},{4,12},{8,0},{12,4},{1,9},{5,13},{9,1},{13,5},{2,10},{6,14},... | collective-permute-start | bytes 737288 | tf_op jit(solution)/shard_map/while/body/ppermute | solution.py:17
  183.4 8.3 %collective-permute-start.12 = (bf16[960,128]{1,0:T(8,128)(2,1)}, bf16[960,128]{1,0:T(8,128)(2,1)S(1)}, u32[]{:S(2)}, u32[]{:S(2)}) collective-permute-start(bf16[960,128]{1,0:T(8,128)(2,1)} %slice.152), channel_id=1, source_target_pairs={{0,16},{16,0},{1,17},{17,1},{2,18},{18,2},{3,19},{19,3},{4,20},{20... | collective-permute-start | bytes 737288 | tf_op jit(solution)/shard_map/while/body/ppermute | solution.py:17
  192.0 5.9 %collective-permute-start.15 = (bf16[1920,256]{1,0:T(8,128)(2,1)S(1)}, bf16[1920,256]{1,0:T(8,128)(2,1)S(1)}, u32[]{:S(2)}, u32[]{:S(2)}) collective-permute-start(bf16[1920,256]{1,0:T(8,128)(2,1)S(1)} %pad_maximum_fusion.26), channel_id=1, source_target_pairs={{0,4},{4,0},{8,12},{12,8},{1,5},{5,1},{9,13},{13,9},{2,6},{6,2},{1... | collective-permute-start | bytes 2949128 | tf_op jit(solution)/shard_map/while/body/ppermute | solution.py:17
  201.7 10.3 %collective-permute-start.35 = (bf16[12,48,256]{2,1,0:T(8,128)(2,1)S(1)}, bf16[12,48,256]{2,1,0:T(8,128)(2,1)S(1)}, u32[]{:S(2)}, u32[]{:S(2)}) collective-permute-start(bf16[12,48,256]{2,1,0:T(8,128)(2,1)S(1)} %copy-done.13), channel_id=1, source_target_pairs={{0,1},{1,2},{2,3},{3,0},{4,5},{5,6},{6,7},{7,4},{8,9},{9,10},{10,1... | collective-permute-start | bytes 884744 | tf_op jit(solution)/shard_map/ppermute | solution.py:13
  212.1 13.1 %collective-permute-start.39 = (bf16[12,48,256]{2,1,0:T(8,128)(2,1)S(1)}, bf16[12,48,256]{2,1,0:T(8,128)(2,1)S(1)}, u32[]{:S(2)}, u32[]{:S(2)}) collective-permute-start(bf16[12,48,256]{2,1,0:T(8,128)(2,1)S(1)} %broadcast_select_fusion.14), channel_id=1, source_target_pairs={{0,2},{1,3},{2,0},{3,1},{4,6},{5,7},{6,4},{7,5},{8,10},{9,11},{10,... | collective-permute-start | bytes 884744 | tf_op jit(solution)/shard_map/ppermute | solution.py:13
  212.2 1.9 collective-permute-start.36
  212.3 5.7 %collective-permute-start.37 = (bf16[4,48,2,1,128]{4,2,1,0,3:T(2,128)(2,1)S(1)}, bf16[4,48,2,1,128]{4,2,1,0,3:T(2,128)(2,1)S(1)}, u32[]{:S(2)}, u32[]{:S(2)}) collective-permute-start(bf16[4,48,2,1,128]{4,2,1,0,3:T(2,128)(2,1)S(1)} %squeeze.30), channel_id=1, source_target_pairs={{0,8},{4,12},{8,0},{12,4},{1,9},{5,13},{9,1},{13,5},{2,10},{6,14},... | collective-permute-start | bytes 294920 | tf_op jit(solution)/shard_map/ppermute | solution.py:17
  213.1 6.1 %collective-permute-start.38 = (bf16[4,48,2,1,128]{4,2,1,0,3:T(2,128)(2,1)S(1)}, bf16[4,48,2,1,128]{4,2,1,0,3:T(2,128)(2,1)S(1)}, u32[]{:S(2)}, u32[]{:S(2)}) collective-permute-start(bf16[4,48,2,1,128]{4,2,1,0,3:T(2,128)(2,1)S(1)} %squeeze.31), channel_id=1, source_target_pairs={{0,12},{4,8},{8,4},{12,0},{1,13},{5,9},{9,5},{13,1},{2,14},{6,10},... | collective-permute-start | bytes 294920 | tf_op jit(solution)/shard_map/ppermute | solution.py:17
  226.0 2.4 %collective-permute-start.40 = (bf16[4,48,2,1,128]{4,2,1,0,3:T(2,128)(2,1)S(1)}, bf16[4,48,2,1,128]{4,2,1,0,3:T(2,128)(2,1)S(1)}, u32[]{:S(2)}, u32[]{:S(2)}) collective-permute-start(bf16[4,48,2,1,128]{4,2,1,0,3:T(2,128)(2,1)S(1)} %squeeze.33), channel_id=1, source_target_pairs={{0,4},{4,0},{8,12},{12,8},{1,5},{5,1},{9,13},{13,9},{2,6},{6,2},{1... | collective-permute-start | bytes 294920 | tf_op jit(solution)/shard_map/ppermute | solution.py:17
  226.2 5.7 %collective-permute-start.41 = (bf16[4,48,2,1,128]{4,2,1,0,3:T(2,128)(2,1)S(1)}, bf16[4,48,2,1,128]{4,2,1,0,3:T(2,128)(2,1)S(1)}, u32[]{:S(2)}, u32[]{:S(2)}) collective-permute-start(bf16[4,48,2,1,128]{4,2,1,0,3:T(2,128)(2,1)S(1)} %squeeze.34), channel_id=1, source_target_pairs={{0,8},{4,12},{8,0},{12,4},{1,9},{5,13},{9,1},{13,5},{2,10},{6,14},... | collective-permute-start | bytes 294920 | tf_op jit(solution)/shard_map/ppermute | solution.py:17
  227.0 6.1 %collective-permute-start.42 = (bf16[4,48,2,1,128]{4,2,1,0,3:T(2,128)(2,1)S(1)}, bf16[4,48,2,1,128]{4,2,1,0,3:T(2,128)(2,1)S(1)}, u32[]{:S(2)}, u32[]{:S(2)}) collective-permute-start(bf16[4,48,2,1,128]{4,2,1,0,3:T(2,128)(2,1)S(1)} %squeeze.35), channel_id=1, source_target_pairs={{0,12},{4,8},{8,4},{12,0},{1,13},{5,9},{9,5},{13,1},{2,14},{6,10},... | collective-permute-start | bytes 294920 | tf_op jit(solution)/shard_map/ppermute | solution.py:17
  (17 other events, 58.7 us)

commit v14 on v11

--- a/solution.py
+++ b/solution.py
@@ -73,35 +73,55 @@
     return gathered_rows[None, None]
 
 
-def terms_body(choice, weight, near, far, terms):
+def terms_body(choice, weight, near, far, own, second, mirror, first, kept_rest):
     near_product = add_columns(weight[...], near[...])
     far_product = add_columns(weight[...], far[...])
-    width = terms.shape[2]
-    terms[choice[0]] = near_product[:, :width].astype(terms.dtype)
-    terms[choice[1]] = near_product[:, width:].astype(terms.dtype)
-    terms[choice[2]] = far_product[:, :width].astype(terms.dtype)
-    terms[choice[3]] = far_product[:, width:].astype(terms.dtype)
+    near_kept = choice[0] == 1
+    kept = jnp.where(near_kept, near_product, far_product)
+    sent = jnp.where(near_kept, far_product, near_product)
+    tall, width = weight.shape[0], own.shape[1]
+    i = pl.program_id(0)
+    rows = pl.ds(pl.multiple_of(i * tall, tall), tall)
+    first[rows, :] = sent[:, :width].astype(first.dtype)
+
+    @pl.when(i < 2)
+    def _():
+        own[rows, :] = kept[:, :width]
+        second[rows, :] = sent[:, width:].astype(second.dtype)
+        mirror[rows, :] = kept[:, width:].astype(mirror.dtype)
+
+    @pl.when(i == 2)
+    def _():
+        kept_rest[...] = kept
+        first[3 * tall :, :] = sent[:, width:].astype(first.dtype)
 
 
 def product_terms(choice, weight, near, far):
     depth, rows = weight.shape
     columns = near.shape[1]
-    width = columns // 2
-    tall = 640 if depth % 640 == 0 else depth
-    whole = pl.BlockSpec((rows, columns), lambda i, choice: (0, 0))
+    width, tall = columns // 2, depth // 3
+    wide, narrow = jnp.float32, jnp.bfloat16
+    shapes = [
+        jax.ShapeDtypeStruct((2 * tall, width), wide),
+        jax.ShapeDtypeStruct((2 * tall, width), narrow),
+        jax.ShapeDtypeStruct((2 * tall, width), narrow),
+        jax.ShapeDtypeStruct((4 * tall, width), narrow),
+        jax.ShapeDtypeStruct((tall, columns), wide),
+    ]
+    whole = [pl.BlockSpec(array.shape, lambda i, choice: (0, 0)) for array in (near, *shapes)]
     return pl.pallas_call(
         terms_body,
-        out_shape=jax.ShapeDtypeStruct((4, depth, width), jnp.bfloat16),
+        out_shape=shapes,
         grid_spec=pltpu.PrefetchScalarGridSpec(
             num_scalar_prefetch=1,
-            grid=(depth // tall,),
-            in_specs=[pl.BlockSpec((tall, rows), lambda i, choice: (i, 0)), whole, whole],
-            out_specs=pl.BlockSpec((4, tall, width), lambda i, choice: (0, i, 0)),
+            grid=(3,),
+            in_specs=[pl.BlockSpec((tall, rows), lambda i, choice: (i, 0)), whole[0], whole[0]],
+            out_specs=whole[1:],
         ),
         compiler_params=pltpu.CompilerParams(vmem_limit_bytes=32 * 1024 * 1024),
         cost_estimate=pl.CostEstimate(
             flops=4 * depth * rows * columns,
-            bytes_accessed=2 * depth * rows + 4 * rows * columns + 8 * depth * width,
+            bytes_accessed=2 * depth * rows + 4 * rows * columns + 10 * depth * width,
             transcendentals=0,
         ),
     )(choice, weight, near, far)
@@ -118,6 +138,7 @@
     most_tiles = tile_map.shape[1]
     group, tile, head = (lax.axis_index(name) for name in ("groups", "tile", "head"))
     first_core, first_chip = tile % 2 == 0, tile < 2
+    at_end = (head == 0) | (head == 3)
     feature_rows = features.reshape(token_rows, feature_width)
     step = lax.optimization_barrier
 
@@ -144,17 +165,30 @@
     def both_heads(ours, theirs):
         return put_first(group == 0, ours, theirs, 1)
 
-    outer = jnp.where(head < 2, jnp.array([0, 3]), jnp.array([3, 0]))
-    inner = jnp.where(head < 2, jnp.array([1, 2]), jnp.array([2, 1]))
-    choice = jnp.where(
-        first_core, jnp.concatenate([outer, inner]), jnp.concatenate([inner, outer])
-    ).astype(jnp.int32)
+    choice = (at_end == first_core).astype(jnp.int32).reshape(1)
 
     def products(near, far):
-        return product_terms(choice, proj_weight, near, far)
-
-    def summed(terms):
-        return lax.psum_scatter(terms, "head", scatter_dimension=0)
+        return tuple(product_terms(choice, proj_weight, near, far))
+
+    rest = depth // 3
+
+    def to_neighbour(block):
+        return swapped(block, "head", 1)
+
+    def over_middle(block):
+        return swapped(block, "head", 3)
+
+    def plus(block, *arrived):
+        for other in arrived:
+            block = block + other.astype(jnp.float32)
+        return block
+
+    def pair_sum(kept_rest, arrived):
+        return plus(kept_rest, jnp.concatenate([arrived[:rest], arrived[rest:]], axis=1))
+
+    def summed(own, arrived, pair, mirrored):
+        rows = [plus(own, *arrived), plus(pair[:, :width], mirrored)]
+        return jnp.concatenate([block.astype(jnp.bfloat16) for block in rows], axis=0)
 
     once = jnp.minimum(jnp.max(tile_count), 1)
 
@@ -206,12 +240,15 @@
     bias_rows = moved(proj_bias, lambda t, h: (h, t))
     key_block = moved(key_mine, lambda t, h: (h // 2 * 2 + outer_core(h), t))
     comes = swapped(leaves, "tile", 2)
-    no_terms = jnp.zeros((4, depth, width), jnp.bfloat16)
+    no_terms = tuple(
+        jnp.full(shape.shape, k, shape.dtype)
+        for k, shape in enumerate(jax.eval_shape(products, *[kv_weight[:, : 2 * width]] * 2))
+    )
     no_tokens = tuple(
         jnp.full((tile_slots, shard_len, 2 * width), k, jnp.bfloat16) for k in range(2)
     )
-    bias_rows, key_block, comes, stays, feature_parts, no_terms, no_tokens, once = step(
-        (bias_rows, key_block, comes, stays, feature_parts, no_terms, no_tokens, once)
+    bias_rows, key_block, comes, stays, once, feature_parts = step(
+        (bias_rows, key_block, comes, stays, once, feature_parts)
     )
 
     value_pieces = []
@@ -241,9 +278,30 @@
         return (other, bias_other), (terms, bias_part + bias_other)
 
     empty = no_terms, bias_part
-    own, beside = step((summed(terms), in_loop(values_terms, (value_half, bias_part), empty)))
-    terms, bias_part = beside
+    own, second, mirror, first, kept_rest = terms
+    second, mirror, first, (value_terms, bias_part) = step(
+        (
+            swapped(second, "head", 2),
+            over_middle(mirror),
+            to_neighbour(first),
+            in_loop(values_terms, (value_half, bias_part), empty),
+        )
+    )
     bias_part = bias_part.reshape(2, layers, 2, head_dim)
+
+    value_own, value_second, value_mirror, value_first, value_kept = value_terms
+    pair = pair_sum(kept_rest, first[2 * rest :])
+    pair, value_rest = step((pair, value_first[2 * rest :]))
+    mirrored, value_rest, value_first, value_second, value_mirror = step(
+        (
+            over_middle(pair[:, width:].astype(jnp.bfloat16)),
+            to_neighbour(value_rest),
+            value_first[: 2 * rest],
+            value_second,
+            value_mirror,
+        )
+    )
+    own = summed(own, (second, mirror, first[: 2 * rest]), pair, mirrored)
 
     def keys_product(own):
         across_x, across_y = step((swapped(own, "tile", 2), swapped(own, "groups", 1)))
@@ -253,7 +311,19 @@
         rows = [rows_0, rows_1, rows_2, swapped(rows_2, "tile", 1)]
         return across_x, finish(times_features(rows, feature_parts), 0)
 
-    own, keys = step((summed(terms), in_loop(keys_product, own, no_tokens[0])))
+    pair = pair_sum(value_kept, value_rest)
+    middle = jnp.concatenate([value_mirror, pair[:, width:].astype(jnp.bfloat16)], axis=0)
+    pair, middle = step((pair, middle))
+    second, middle, first, keys = step(
+        (
+            swapped(value_second, "head", 2),
+            over_middle(middle),
+            to_neighbour(value_first),
+            in_loop(keys_product, own, no_tokens[0]),
+        )
+    )
+    arrived = second, middle[: 2 * rest], first
+    own = summed(value_own, arrived, pair, middle[2 * rest :])
 
     shifted, across_x, across_y = step(
         (shifted_2(keys, "head", 1), swapped(own, "tile", 2), swapped(own, "groups", 1))
@@ -272,8 +342,7 @@
         )
         rows_2 = step(both_heads(across_x, jnp.concatenate([upper, lower], axis=0)))
         rows = [rows_0, rows_1, rows_2, swapped(rows_2, "tile", 1)]
-        total = times_features(rows, feature_parts)
-        return (across_y, own, across_x), finish(total, 1)
+        return (across_y, own, across_x), finish(times_features(rows, feature_parts), 1)
 
     keys = step(rolled(keys, shifted, 1))
     values = in_loop(values_product, (own, across_x, across_y), no_tokens[1])

time: 237 us -> 234 us (0.987)
  between operations: 14.4 us -> 1.09 us
  waiting for transfers between devices: 115 us -> 103 us
  starting transfers between devices: 43.6 us -> 54.9 us
  local copies, waits for them, and re-layouts: 23.6 us -> 30.1 us
  other arithmetic: 13.1 us -> 17.8 us
    reduce_scatter x2 -> x0, waiting for transfers between devices: 19.4 us -> none  [summed(): return lax.psum_scatter(terms, 'head', scatter_dimension=0)]
    ppermute x24 -> x32, starting transfers between devices: 30.6 us -> 46.9 us  [swapped(): lax.ppermute(shard, axis, [(i, i ^ bit) for i in range(lax.axis_size(axis...]
    ppermute x24 -> x32, waiting for transfers between devices: 63.7 us -> 69.9 us  [swapped(): lax.ppermute(shard, axis, [(i, i ^ bit) for i in range(lax.axis_size(axis...]
    ppermute x4, starting transfers between devices: 9.91 us -> 4.12 us  [moved(): return lax.ppermute(shard, ('tile', 'head'), pairs)]
    convert_element_type x0 -> x4, other arithmetic: none -> 3.78 us  [summed(): block.astype(jnp.bfloat16)]
    broadcast_in_dim x1 -> x5, local copies, waits for them, and re-layouts: 1.65 us -> 4.26 us  [product_plan(): jnp.full(shape.shape, k, shape.dtype)]
    while x22 -> x20, local copies, waits for them, and re-layouts: 4.95 us -> 4.67 us
  transfers between devices with their start and end apart: 34 -> 40, of which waited for: 20 -> 21; matrix products, arithmetic and copies ran while one was open for 14% -> 16% of each run, Pallas kernels for 4% -> 4%
where the time goes in v14:
time: 234 us
  waiting for transfers between devices  103 us (44%)
  starting transfers between devices  54.9 us (23%)
  local copies, waits for them, and re-layouts  30.1 us (13%)
  other arithmetic  17.8 us (8%)
  Pallas kernels  15.9 us (7%)
  matrix products  9.94 us (4%)
    ppermute x32, waiting for transfers between devices, swapped(): lax.ppermute(shard, axis, [(i, i ^ bit) for i in range(lax.axis_size(axis...  69.9 us
    ppermute x32, starting transfers between devices, swapped(): lax.ppermute(shard, axis, [(i, i ^ bit) for i in range(lax.axis_size(axis...  46.9 us
    ppermute x4, waiting for transfers between devices, shifted_2(): lax.ppermute(shard, axis, [(i, (i + by) % count) for i in range(count)])  24.6 us
    pallas_call x2, Pallas kernels, product_terms(): pl.pallas_call(terms_body, out_shape=shapes, grid_spec=pltpu.PrefetchScal...  15.9 us
    dot_general x11, matrix products, add_columns(): return jnp.dot(operand, portion, preferred_element_type=jnp.float32)  9.75 us
    ppermute x4, waiting for transfers between devices, moved(): return lax.ppermute(shard, ('tile', 'head'), pairs)  9.02 us
    dynamic_slice x1, local copies, waits for them, and re-layouts, product_plan(): lax.dynamic_slice_in_dim(feature_rows, (tile ^ r) * depth, depth, axis=1)  7.31 us
  transfers between devices with their start and end apart: 40, of which 21 were waited for; matrix products, arithmetic and copies ran while one was open for 16% of the time, Pallas kernels for 4%

profile of v14, /device:TPU:0, one launch (start us, length us, event | category | flops | bytes accessed | tf_op | source)
XLA Modules:
  0.0 233.5 jit_solution(17774546493912814041)
XLA Ops:
  1.8 2.3 fusion.23
  4.1 6.7 %collective-permute-start.14 = (bf16[1024,128]{1,0:T(8,128)(2,1)}, bf16[1024,128]{1,0:T(8,128)(2,1)}, u32[]{:S(2)}, u32[]{:S(2)}) collective-permute-start(bf16[1024,128]{1,0:T(8,128)(2,1)} %get-tuple-element.589), channel_id=1, source_target_pairs={{0,8},{4,12},{8,0},{12,4},{1,9},{5,13},{9,1},{13,5},{2,10},{6,14},... | collective-permute-start | bytes 786440 | tf_op jit(solution)/shard_map/ppermute | solution.py:17
  10.8 1.3 collective-permute-start.12
  12.1 7.3 %constant_dynamic-slice_fusion = (bf16[576,1920]{1,0:T(8,128)(2,1)}, bf16[576,1920]{1,0:T(8,128)(2,1)}, bf16[576,1920]{1,0:T(8,128)(2,1)}, bf16[576,1920]{1,0:T(8,128)(2,1)}) fusion(bf16[576,7680]{1,0:T(8,128)(2,1)} %bitcast.134, s32[]{:T(128)S(6)} %select_n.299, s32[]{:T(128)S(6)} %select_n.298, s32[]{:T(128)S(6)} %select_n.297, s32[]{:T(128)S(6)} %select_n.296), kind=kLoop, calls=%fused_computation.109 | loop fusion | bytes 17694736 | tf_op jit(solution)/shard_map/dynamic_slice | solution.py:157
  20.8 2.4 %collective-permute-done.14 = bf16[1024,128]{1,0:T(8,128)(2,1)} collective-permute-done((bf16[1024,128]{1,0:T(8,128)(2,1)}, bf16[1024,128]{1,0:T(8,128)(2,1)}, u32[]{:S(2)}, u32[]{:S(2)}) %collective-permute-start.14) | collective-permute-done | bytes 262176 | tf_op jit(solution)/shard_map/ppermute | solution.py:17
  23.1 9.8 %collective-permute-start.17 = (bf16[2048,128]{1,0:T(8,128)(2,1)S(1)}, bf16[2048,128]{1,0:T(8,128)(2,1)S(1)}, u32[]{:S(2)}, u32[]{:S(2)}) collective-permute-start(bf16[2048,128]{1,0:T(8,128)(2,1)S(1)} %collective-permute-done.13), channel_id=1, source_target_pairs={{0,8},{4,12},{8,0},{12,4},{1,9},{5,13},{9,1},{13,5},{2,10},{6,14},... | collective-permute-start | bytes 1572872 | tf_op jit(solution)/shard_map/ppermute | solution.py:17
  34.6 1.4 collective-permute-start.16
  36.4 9.0 %collective-permute-done.16 = bf16[1024,128]{1,0:T(8,128)(2,1)S(1)} collective-permute-done((bf16[1024,128]{1,0:T(8,128)(2,1)S(1)}, bf16[1024,128]{1,0:T(8,128)(2,1)S(1)}, u32[]{:S(2)}, u32[]{:S(2)}) %collective-permute-start.16) | collective-permute-done | bytes 262176 | tf_op jit(solution)/shard_map/ppermute | solution.py:151
  46.5 4.2 %collective-permute-start.18 = (bf16[2048,256]{1,0:T(8,128)(2,1)S(1)}, bf16[2048,256]{1,0:T(8,128)(2,1)S(1)}, u32[]{:S(2)}, u32[]{:S(2)}) collective-permute-start(bf16[2048,256]{1,0:T(8,128)(2,1)S(1)} %pad_maximum_fusion.7.near), channel_id=1, source_target_pairs={{0,4},{4,0},{8,12},{12,8},{1,5},{5,1},{9,13},{13,9},{2,6},{6,2},{1... | collective-permute-start | bytes 3145736 | tf_op jit(solution)/shard_map/ppermute | solution.py:17
  51.3 1.7 collective-permute-done.19
  53.0 7.7 %shard_map.82 = (f32[1280,128]{1,0:T(8,128)S(1)}, bf16[1280,128]{1,0:T(8,128)(2,1)}, bf16[1280,128]{1,0:T(8,128)(2,1)}, bf16[2560,128]{1,0:T(8,128)(2,1)}, f32[640,256]{1,0:T(8,128)S(1)}) custom-call(s32[1]{0:T(128)} %bitcast.11.choice, bf16[1920,2048]{1,0:T(8,128)(2,1)} %weight.1, bf16[2048,256]{1,0:T(8,128)(2,1)S(1)} %pad_maximum_fusion.7.near, ...), custom_call_target="tpu_custom_call" | custom-call | flops 4026531840 | bytes 12419072 | tf_op jit(solution)/shard_map/pallas_call | solution.py:112
  61.4 2.2 collective-permute-start.20
  63.6 2.1 collective-permute-start.21
  69.9 26.6 %while.56 = (s32[]{:T(128)}, bf16[1024,256]{1,0:T(8,128)(2,1)}, f32[1,512]{1,0:T(1,128)S(1)}, f32[1280,128]{1,0:T(8,128)}, bf16[1280,128]{1,0:T(8,128)(2,1)}, /*...) while((s32[]{:T(128)}, bf16[1024,256]{1,0:T(8,128)(2,1)}, ...), condition=%wide.region_3.4_spmd, body=%wide.region_2.3_spmd.sunk | while | flops 4029153792 | bytes 23972092 | solution.py:196
  71.0 1.7 collective-permute-start
  73.0 11.4 %collective-permute-done.1 = f32[1,512]{1,0:T(1,128)S(1)} collective-permute-done((f32[1,512]{1,0:T(1,128)S(1)}, f32[1,512]{1,0:T(1,128)S(1)}, u32[]{:S(2)}, u32[]{:S(2)}) %collective-permute-start.1) | collective-permute-done | bytes 2080 | tf_op jit(solution)/shard_map/while/body/ppermute | solution.py:17
  86.3 2.1 collective-permute-done.2.far
  88.4 8.2 %body.1 = (f32[1280,128]{1,0:T(8,128)}, bf16[1280,128]{1,0:T(8,128)(2,1)}, bf16[1280,128]{1,0:T(8,128)(2,1)}, bf16[2560,128]{1,0:T(8,128)(2,1)}, f32[640,256]{1,0:T(8,128)}) custom-call(s32[1]{0:T(128)} %get-tuple-element.941.choice, bf16[1920,2048]{1,0:T(8,128)(2,1)} %get-tuple-element.942.weight, bf16[2048,256]{1,0:T(8,128)(2,1)S(1)} %pad_maximum_fusion.20.near, ...), custom_call_target="tpu_custom_call" | custom-call | flops 4026531840 | bytes 12419072 | tf_op jit(solution)/shard_map/while/body/pallas_call | solution.py:112
  98.9 1.8 collective-permute-start.23
  102.0 5.9 %collective-permute-done.23 = bf16[640,128]{1,0:T(8,128)(2,1)S(1)} collective-permute-done((bf16[640,128]{1,0:T(8,128)(2,1)S(1)}, bf16[640,128]{1,0:T(8,128)(2,1)S(1)}, u32[]{:S(2)}, u32[]{:S(2)}) %collective-permute-start.23) | collective-permute-done | bytes 163872 | tf_op jit(solution)/shard_map/ppermute | solution.py:17
  107.8 5.8 %collective-permute-done.24 = bf16[1280,128]{1,0:T(8,128)(2,1)S(1)} collective-permute-done((bf16[1280,128]{1,0:T(8,128)(2,1)S(1)}, bf16[1280,128]{1,0:T(8,128)(2,1)S(1)}, u32[]{:S(2)}, u32[]{:S(2)}) %collective-permute-start.24) | collective-permute-done | bytes 327712 | tf_op jit(solution)/shard_map/ppermute | solution.py:17
  114.8 2.1 collective-permute-start.26
  116.9 2.3 collective-permute-start.27
  119.9 34.9 %while.57 = (s32[]{:T(128)}, bf16[1920,128]{1,0:T(8,128)(2,1)S(1)}, bf16[12,48,256]{2,1,0:T(8,128)(2,1)}, s32[]{:T(128)}, pred[]{:T(512)}, /*index=5*/bf16[576,1...) while((s32[]{:T(128)}, bf16[1920,128]{1,0:T(8,128)(2,1)S(1)}, ...), condition=%wide.region_7.8_spmd, body=%wide.region_4.7_spmd.sunk | while | flops 2271905024 | bytes 76995496 | solution.py:196
  120.0 1.7 collective-permute-start.3
  121.7 1.5 collective-permute-start.4
  123.3 8.7 %collective-permute-done.3 = bf16[1920,128]{1,0:T(8,128)(2,1)S(1)} collective-permute-done((bf16[1920,128]{1,0:T(8,128)(2,1)S(1)}, bf16[1920,128]{1,0:T(8,128)(2,1)S(1)}, u32[]{:S(2)}, u32[]{:S(2)}) %collective-permute-start.3) | collective-permute-done | bytes 491552 | tf_op jit(solution)/shard_map/while/body/ppermute | solution.py:17
  131.9 1.3 collective-permute-done.4
  134.0 13.2 %collective-permute-done.5 = bf16[1920,128]{1,0:T(8,128)(2,1)S(1)} collective-permute-done((bf16[1920,128]{1,0:T(8,128)(2,1)S(1)}, bf16[1920,128]{1,0:T(8,128)(2,1)S(1)}, u32[]{:S(2)}, u32[]{:S(2)}) %collective-permute-start.5) | collective-permute-done | bytes 491552 | tf_op jit(solution)/shard_map/while/body/ppermute | solution.py:17
  149.1 2.1 convolution_add_fusion.10
  156.0 1.3 add_convert_fusion
  157.9 1.5 collective-permute-start.30
  160.2 10.0 %collective-permute-done.28 = bf16[12,48,256]{2,1,0:T(8,128)(2,1)S(1)} collective-permute-done((bf16[12,48,256]{2,1,0:T(8,128)(2,1)S(1)}, bf16[12,48,256]{2,1,0:T(8,128)(2,1)S(1)}, u32[]{:S(2)}, u32[]{:S(2)}) %collective-permute-start.28) | collective-permute-done | bytes 294944 | tf_op jit(solution)/shard_map/ppermute | solution.py:13
  172.0 1.4 collective-permute-start.31
  174.2 20.3 %while.58 = (s32[]{:T(128)}, bf16[1920,128]{1,0:T(8,128)(2,1)S(1)}, bf16[1920,128]{1,0:T(8,128)(2,1)S(1)}, bf16[1920,128]{1,0:T(8,128)(2,1)S(1)}, bf16[12,48,256...) while((s32[]{:T(128)}, bf16[1920,128]{1,0:T(8,128)(2,1)S(1)}, ...), condition=%wide.region_9.10_spmd, body=%wide.region_8.9_spmd.sunk | while | flops 2271166464 | bytes 77368712 | solution.py:196
  175.2 1.7 collective-permute-start.9
  177.6 1.5 collective-permute-start.8
  179.1 4.6 %collective-permute-done.9 = bf16[960,128]{1,0:T(8,128)(2,1)S(1)} collective-permute-done((bf16[960,128]{1,0:T(8,128)(2,1)}, bf16[960,128]{1,0:T(8,128)(2,1)S(1)}, u32[]{:S(2)}, u32[]{:S(2)}) %collective-permute-start.9) | collective-permute-done | bytes 245792 | tf_op jit(solution)/shard_map/while/body/ppermute | solution.py:17
  183.7 2.1 collective-permute-done.8
  189.1 2.1 convolution_add_fusion.12
  195.9 1.8 collective-permute-start.32
  198.5 7.6 %collective-permute-done.32 = bf16[12,48,256]{2,1,0:T(8,128)(2,1)S(1)} collective-permute-done((bf16[12,48,256]{2,1,0:T(8,128)(2,1)S(1)}, bf16[12,48,256]{2,1,0:T(8,128)(2,1)S(1)}, u32[]{:S(2)}, u32[]{:S(2)}) %collective-permute-start.32) | collective-permute-done | bytes 294944 | tf_op jit(solution)/shard_map/ppermute | solution.py:13
  206.8 1.4 collective-permute-start.35
  208.3 3.8 %collective-permute-done.34 = bf16[4,48,2,1,128]{4,2,1,0,3:T(2,128)(2,1)S(1)} collective-permute-done((bf16[4,48,2,1,128]{4,2,1,0,3:T(2,128)(2,1)S(1)}, bf16[4,48,2,1,128]{4,2,1,0,3:T(2,128)(2,1)S(1)}, u32[]{:S(2)}, u32[]{:S(2)}) %collective-permute-start.34) | collective-permute-done | bytes 98336 | tf_op jit(solution)/shard_map/ppermute | solution.py:17
  213.3 6.9 %collective-permute-done.36 = bf16[12,48,256]{2,1,0:T(8,128)(2,1)S(1)} collective-permute-done((bf16[12,48,256]{2,1,0:T(8,128)(2,1)S(1)}, bf16[12,48,256]{2,1,0:T(8,128)(2,1)S(1)}, u32[]{:S(2)}, u32[]{:S(2)}) %collective-permute-start.36) | collective-permute-done | bytes 294944 | tf_op jit(solution)/shard_map/ppermute | solution.py:13
  221.7 1.6 collective-permute-start.39
  223.4 3.4 %collective-permute-done.38 = bf16[4,48,2,1,128]{4,2,1,0,3:T(2,128)(2,1)S(1)} collective-permute-done((bf16[4,48,2,1,128]{4,2,1,0,3:T(2,128)(2,1)S(1)}, bf16[4,48,2,1,128]{4,2,1,0,3:T(2,128)(2,1)S(1)}, u32[]{:S(2)}, u32[]{:S(2)}) %collective-permute-start.38) | collective-permute-done | bytes 98336 | tf_op jit(solution)/shard_map/ppermute | solution.py:17
  231.4 2.1 copy.19
  (181 shorter events, 49.3 us)
Async XLA Ops:
  1.1 22.1 %collective-permute-start.13 = (bf16[2048,128]{1,0:T(8,128)(2,1)S(1)}, bf16[2048,128]{1,0:T(8,128)(2,1)S(1)}, u32[]{:S(2)}, u32[]{:S(2)}) collective-permute-start(bf16[2048,128]{1,0:T(8,128)(2,1)S(1)} %constant_dynamic-slice_fusion.4), channel_id=1, source_target_pairs={{0,0},{1,4},{2,12},{3,8},{4,1},{5,5},{6,13},{7,9},{8,2},{9,6},{10,... | collective-permute-start | bytes 1572872 | tf_op jit(solution)/shard_map/ppermute | solution.py:151
  4.1 19.1 %collective-permute-start.14 = (bf16[1024,128]{1,0:T(8,128)(2,1)}, bf16[1024,128]{1,0:T(8,128)(2,1)}, u32[]{:S(2)}, u32[]{:S(2)}) collective-permute-start(bf16[1024,128]{1,0:T(8,128)(2,1)} %get-tuple-element.589), channel_id=1, source_target_pairs={{0,8},{4,12},{8,0},{12,4},{1,9},{5,13},{9,1},{13,5},{2,10},{6,14},... | collective-permute-start | bytes 786440 | tf_op jit(solution)/shard_map/ppermute | solution.py:17
  10.8 10.0 %collective-permute-start.12 = (bf16[2048]{0:T(1024)(128)(2,1)}, bf16[2048]{0:T(1024)(128)(2,1)S(1)}, u32[]{:S(2)}, u32[]{:S(2)}) collective-permute-start(bf16[2048]{0:T(1024)(128)(2,1)} %param.16), channel_id=1, source_target_pairs={{0,0},{1,4},{2,8},{3,12},{4,1},{5,5},{6,9},{7,13},{8,2},{9,6},{10,... | collective-permute-start | bytes 12296 | tf_op jit(solution)/shard_map/ppermute | solution.py:151
  12.1 7.3 %copy-start.18 = (s32[4]{0:T(128)S(1)}, s32[4]{0:T(128)}, u32[]{:S(2)}) copy-start(s32[4]{0:T(128)} %param.20) | copy-start | bytes 52
  12.1 23.9 %copy-start = (bf16[2048,512]{1,0:T(8,128)(2,1)S(1)}, bf16[2048,512]{1,0:T(8,128)(2,1)}, u32[]{:S(2)}) copy-start(bf16[2048,512]{1,0:T(8,128)(2,1)} %param.17) | copy-start | bytes 6291460
  23.1 22.3 %collective-permute-start.17 = (bf16[2048,128]{1,0:T(8,128)(2,1)S(1)}, bf16[2048,128]{1,0:T(8,128)(2,1)S(1)}, u32[]{:S(2)}, u32[]{:S(2)}) collective-permute-start(bf16[2048,128]{1,0:T(8,128)(2,1)S(1)} %collective-permute-done.13), channel_id=1, source_target_pairs={{0,8},{4,12},{8,0},{12,4},{1,9},{5,13},{9,1},{13,5},{2,10},{6,14},... | collective-permute-start | bytes 1572872 | tf_op jit(solution)/shard_map/ppermute | solution.py:17
  33.9 2.5 %collective-permute-start.15 = (bf16[1024,128]{1,0:T(8,128)(2,1)S(1)}, bf16[1024,128]{1,0:T(8,128)(2,1)S(1)}, u32[]{:S(2)}, u32[]{:S(2)}) collective-permute-start(bf16[1024,128]{1,0:T(8,128)(2,1)S(1)} %get-tuple-element.597), channel_id=1, source_target_pairs={{0,0},{1,4},{2,6},{3,2},{4,1},{5,5},{6,7},{7,3},{8,8},{9,12},{10,1... | collective-permute-start | bytes 786440 | tf_op jit(solution)/shard_map/ppermute | solution.py:151
  34.6 10.8 %collective-permute-start.16 = (bf16[1024,128]{1,0:T(8,128)(2,1)S(1)}, bf16[1024,128]{1,0:T(8,128)(2,1)S(1)}, u32[]{:S(2)}, u32[]{:S(2)}) collective-permute-start(bf16[1024,128]{1,0:T(8,128)(2,1)S(1)} %get-tuple-element.596), channel_id=1, source_target_pairs={{0,2},{1,6},{2,4},{3,0},{4,3},{5,7},{6,5},{7,1},{8,10},{9,14},{10,... | collective-permute-start | bytes 786440 | tf_op jit(solution)/shard_map/ppermute | solution.py:151
  46.5 6.5 %collective-permute-start.18 = (bf16[2048,256]{1,0:T(8,128)(2,1)S(1)}, bf16[2048,256]{1,0:T(8,128)(2,1)S(1)}, u32[]{:S(2)}, u32[]{:S(2)}) collective-permute-start(bf16[2048,256]{1,0:T(8,128)(2,1)S(1)} %pad_maximum_fusion.7.near), channel_id=1, source_target_pairs={{0,4},{4,0},{8,12},{12,8},{1,5},{5,1},{9,13},{13,9},{2,6},{6,2},{1... | collective-permute-start | bytes 3145736 | tf_op jit(solution)/shard_map/ppermute | solution.py:17
  50.7 2.3 collective-permute-start.19
  61.3 35.3 %collective-permute-start.22 = (bf16[2560,128]{1,0:T(8,128)(2,1)}, bf16[2560,128]{1,0:T(8,128)(2,1)}, u32[]{:S(2)}, u32[]{:S(2)}) collective-permute-start(bf16[2560,128]{1,0:T(8,128)(2,1)} %get-tuple-element.436), channel_id=1, source_target_pairs={{0,1},{1,0},{2,3},{3,2},{4,5},{5,4},{6,7},{7,6},{8,9},{9,8},{10,11... | collective-permute-start | bytes 1966088 | tf_op jit(solution)/shard_map/ppermute | solution.py:17
  61.4 35.2 %collective-permute-start.20 = (bf16[1280,128]{1,0:T(8,128)(2,1)}, bf16[1280,128]{1,0:T(8,128)(2,1)}, u32[]{:S(2)}, u32[]{:S(2)}) collective-permute-start(bf16[1280,128]{1,0:T(8,128)(2,1)} %get-tuple-element.434), channel_id=1, source_target_pairs={{0,2},{1,3},{2,0},{3,1},{4,6},{5,7},{6,4},{7,5},{8,10},{9,11},{10,... | collective-permute-start | bytes 983048 | tf_op jit(solution)/shard_map/ppermute | solution.py:17
  63.6 33.0 %collective-permute-start.21 = (bf16[1280,128]{1,0:T(8,128)(2,1)}, bf16[1280,128]{1,0:T(8,128)(2,1)}, u32[]{:S(2)}, u32[]{:S(2)}) collective-permute-start(bf16[1280,128]{1,0:T(8,128)(2,1)} %get-tuple-element.435), channel_id=1, source_target_pairs={{0,3},{1,2},{2,1},{3,0},{4,7},{5,6},{6,5},{7,4},{8,11},{9,10},{10,... | collective-permute-start | bytes 983048 | tf_op jit(solution)/shard_map/ppermute | solution.py:17
  71.0 13.5 %collective-permute-start = (bf16[1024,256]{1,0:T(8,128)(2,1)S(1)}, bf16[1024,256]{1,0:T(8,128)(2,1)}, u32[]{:S(2)}, u32[]{:S(2)}) collective-permute-start(bf16[1024,256]{1,0:T(8,128)(2,1)S(1)} %copy.33), channel_id=1, source_target_pairs={{0,8},{4,12},{8,0},{12,4},{1,9},{5,13},{9,1},{13,5},{2,10},{6,14},... | collective-permute-start | bytes 1572872 | tf_op jit(solution)/shard_map/while/body/ppermute | solution.py:17
  72.7 11.7 %collective-permute-start.1 = (f32[1,512]{1,0:T(1,128)S(1)}, f32[1,512]{1,0:T(1,128)S(1)}, u32[]{:S(2)}, u32[]{:S(2)}) collective-permute-start(f32[1,512]{1,0:T(1,128)S(1)} %copy.34), channel_id=1, source_target_pairs={{0,8},{4,12},{8,0},{12,4},{1,9},{5,13},{9,1},{13,5},{2,10},{6,14},... | collective-permute-start | bytes 6152 | tf_op jit(solution)/shard_map/while/body/ppermute | solution.py:17
  85.7 2.7 %collective-permute-start.2 = (bf16[2048,256]{1,0:T(8,128)(2,1)S(1)}, bf16[2048,256]{1,0:T(8,128)(2,1)S(1)}, u32[]{:S(2)}, u32[]{:S(2)}) collective-permute-start(bf16[2048,256]{1,0:T(8,128)(2,1)S(1)} %pad_maximum_fusion.20.near), channel_id=1, source_target_pairs={{0,4},{4,0},{8,12},{12,8},{1,5},{5,1},{9,13},{13,9},{2,6},{6,2},{1... | collective-permute-start | bytes 3145736 | tf_op jit(solution)/shard_map/while/body/ppermute | solution.py:17
  98.8 14.9 %copy-start.1 = (f32[640,256]{1,0:T(8,128)S(1)}, f32[640,256]{1,0:T(8,128)}, u32[]{:S(2)}) copy-start(f32[640,256]{1,0:T(8,128)} %get-tuple-element.453) | copy-start | bytes 1966084
  98.8 15.0 %copy-start.12 = (bf16[1280,128]{1,0:T(8,128)(2,1)S(1)}, bf16[1280,128]{1,0:T(8,128)(2,1)}, u32[]{:S(2)}) copy-start(bf16[1280,128]{1,0:T(8,128)(2,1)} %get-tuple-element.455) | copy-start | bytes 983044
  98.9 9.0 %collective-permute-start.23 = (bf16[640,128]{1,0:T(8,128)(2,1)S(1)}, bf16[640,128]{1,0:T(8,128)(2,1)S(1)}, u32[]{:S(2)}, u32[]{:S(2)}) collective-permute-start(bf16[640,128]{1,0:T(8,128)(2,1)S(1)} %slice.189), channel_id=1, source_target_pairs={{0,3},{1,2},{2,1},{3,0},{4,7},{5,6},{6,5},{7,4},{8,11},{9,10},{10,... | collective-permute-start | bytes 491528 | tf_op jit(solution)/shard_map/ppermute | solution.py:17
  100.6 13.0 %collective-permute-start.24 = (bf16[1280,128]{1,0:T(8,128)(2,1)S(1)}, bf16[1280,128]{1,0:T(8,128)(2,1)S(1)}, u32[]{:S(2)}, u32[]{:S(2)}) collective-permute-start(bf16[1280,128]{1,0:T(8,128)(2,1)S(1)} %get-tuple-element.449), channel_id=1, source_target_pairs={{0,1},{1,0},{2,3},{3,2},{4,5},{5,4},{6,7},{7,6},{8,9},{9,8},{10,11... | collective-permute-start | bytes 983048 | tf_op jit(solution)/shard_map/ppermute | solution.py:17
  113.7 6.3 %copy-start.15 = (f32[1,512]{1,0:T(1,128)S(1)}, f32[1,512]{1,0:T(1,128)}, u32[]{:S(2)}) copy-start(f32[1,512]{1,0:T(1,128)} %get-tuple-element.466) | copy-start | bytes 6148
  113.7 6.2 %copy-start.16 = (f32[1,128]{1,0:T(1,128)S(1)}, f32[1,128]{1,0:T(1,128)}, u32[]{:S(2)}) copy-start(f32[1,128]{1,0:T(1,128)} %param.18) | copy-start | bytes 1540
  114.8 40.1 %collective-permute-start.26 = (bf16[1920,128]{1,0:T(8,128)(2,1)}, bf16[1920,128]{1,0:T(8,128)(2,1)}, u32[]{:S(2)}, u32[]{:S(2)}) collective-permute-start(bf16[1920,128]{1,0:T(8,128)(2,1)} %pad_maximum_fusion.10), channel_id=1, source_target_pairs={{0,3},{1,2},{2,1},{3,0},{4,7},{5,6},{6,5},{7,4},{8,11},{9,10},{10,... | collective-permute-start | bytes 1474568 | tf_op jit(solution)/shard_map/ppermute | solution.py:17
  116.9 38.0 %collective-permute-start.25 = (bf16[1280,128]{1,0:T(8,128)(2,1)}, bf16[1280,128]{1,0:T(8,128)(2,1)}, u32[]{:S(2)}, u32[]{:S(2)}) collective-permute-start(bf16[1280,128]{1,0:T(8,128)(2,1)} %get-tuple-element.452), channel_id=1, source_target_pairs={{0,2},{1,3},{2,0},{3,1},{4,6},{5,7},{6,4},{7,5},{8,10},{9,11},{10,... | collective-permute-start | bytes 983048 | tf_op jit(solution)/shard_map/ppermute | solution.py:17
  116.9 38.0 %collective-permute-start.27 = (bf16[1280,128]{1,0:T(8,128)(2,1)S(1)}, bf16[1280,128]{1,0:T(8,128)(2,1)}, u32[]{:S(2)}, u32[]{:S(2)}) collective-permute-start(bf16[1280,128]{1,0:T(8,128)(2,1)S(1)} %get-tuple-element.457), channel_id=1, source_target_pairs={{0,1},{1,0},{2,3},{3,2},{4,5},{5,4},{6,7},{7,6},{8,9},{9,8},{10,11... | collective-permute-start | bytes 983048 | tf_op jit(solution)/shard_map/ppermute | solution.py:17
  119.9 36.1 %copy-start.2 = (f32[1280,128]{1,0:T(8,128)S(1)}, f32[1280,128]{1,0:T(8,128)}, u32[]{:S(2)}) copy-start(f32[1280,128]{1,0:T(8,128)} %get-tuple-element.469) | copy-start | bytes 1966084
  120.0 11.9 %collective-permute-start.3 = (bf16[1920,128]{1,0:T(8,128)(2,1)S(1)}, bf16[1920,128]{1,0:T(8,128)(2,1)S(1)}, u32[]{:S(2)}, u32[]{:S(2)}) collective-permute-start(bf16[1920,128]{1,0:T(8,128)(2,1)S(1)} %copy.54), channel_id=1, source_target_pairs={{0,8},{4,12},{8,0},{12,4},{1,9},{5,13},{9,1},{13,5},{2,10},{6,14},... | collective-permute-start | bytes 1474568 | tf_op jit(solution)/shard_map/while/body/ppermute | solution.py:17
  121.7 11.5 %collective-permute-start.4 = (bf16[1920,128]{1,0:T(8,128)(2,1)S(1)}, bf16[1920,128]{1,0:T(8,128)(2,1)S(1)}, u32[]{:S(2)}, u32[]{:S(2)}) collective-permute-start(bf16[1920,128]{1,0:T(8,128)(2,1)S(1)} %copy.54), channel_id=1, source_target_pairs={{0,16},{16,0},{1,17},{17,1},{2,18},{18,2},{3,19},{19,3},{4,20},{20... | collective-permute-start | bytes 1474568 | tf_op jit(solution)/shard_map/while/body/ppermute | solution.py:17
  133.5 13.7 %collective-permute-start.6 = (bf16[1920,256]{1,0:T(8,128)(2,1)S(1)}, bf16[1920,256]{1,0:T(8,128)(2,1)}, u32[]{:S(2)}, u32[]{:S(2)}) collective-permute-start(bf16[1920,256]{1,0:T(8,128)(2,1)S(1)} %pad_maximum_fusion.21), channel_id=1, source_target_pairs={{0,4},{4,0},{8,12},{12,8},{1,5},{5,1},{9,13},{13,9},{2,6},{6,2},{1... | collective-permute-start | bytes 2949128 | tf_op jit(solution)/shard_map/while/body/ppermute | solution.py:17
  133.5 13.6 %collective-permute-start.5 = (bf16[1920,128]{1,0:T(8,128)(2,1)S(1)}, bf16[1920,128]{1,0:T(8,128)(2,1)S(1)}, u32[]{:S(2)}, u32[]{:S(2)}) collective-permute-start(bf16[1920,128]{1,0:T(8,128)(2,1)S(1)} %collective-permute-done.4), channel_id=1, source_target_pairs={{0,8},{4,12},{8,0},{12,4},{1,9},{5,13},{9,1},{13,5},{2,10},{6,14},... | collective-permute-start | bytes 1474568 | tf_op jit(solution)/shard_map/while/body/ppermute | solution.py:17
  134.0 13.4 %copy-start.9 = (bf16[576,1920]{1,0:T(8,128)(2,1)S(1)}, bf16[576,1920]{1,0:T(8,128)(2,1)}, u32[]{:S(2)}) copy-start(bf16[576,1920]{1,0:T(8,128)(2,1)} %get-tuple-element.973) | copy-start | bytes 6635524 | tf_op jit(solution)/shard_map/while
  147.4 4.7 %collective-permute-start.7 = (bf16[1920,256]{1,0:T(8,128)(2,1)S(1)}, bf16[1920,256]{1,0:T(8,128)(2,1)S(1)}, u32[]{:S(2)}, u32[]{:S(2)}) collective-permute-start(bf16[1920,256]{1,0:T(8,128)(2,1)S(1)} %pad_maximum_fusion.22), channel_id=1, source_target_pairs={{0,4},{4,0},{8,12},{12,8},{1,5},{5,1},{9,13},{13,9},{2,6},{6,2},{1... | collective-permute-start | bytes 2949128 | tf_op jit(solution)/shard_map/while/body/ppermute | solution.py:17
  157.4 13.7 %collective-permute-start.29 = (bf16[1920,128]{1,0:T(8,128)(2,1)S(1)}, bf16[1920,128]{1,0:T(8,128)(2,1)S(1)}, u32[]{:S(2)}, u32[]{:S(2)}) collective-permute-start(bf16[1920,128]{1,0:T(8,128)(2,1)S(1)} %pad_maximum_fusion.12), channel_id=1, source_target_pairs={{0,8},{4,12},{8,0},{12,4},{1,9},{5,13},{9,1},{13,5},{2,10},{6,14},... | collective-permute-start | bytes 1474568 | tf_op jit(solution)/shard_map/ppermute | solution.py:17
  157.9 13.3 %collective-permute-start.30 = (bf16[1920,128]{1,0:T(8,128)(2,1)S(1)}, bf16[1920,128]{1,0:T(8,128)(2,1)S(1)}, u32[]{:S(2)}, u32[]{:S(2)}) collective-permute-start(bf16[1920,128]{1,0:T(8,128)(2,1)S(1)} %pad_maximum_fusion.12), channel_id=1, source_target_pairs={{0,16},{16,0},{1,17},{17,1},{2,18},{18,2},{3,19},{19,3},{4,20},{20... | collective-permute-start | bytes 1474568 | tf_op jit(solution)/shard_map/ppermute | solution.py:17
  159.6 10.7 %collective-permute-start.28 = (bf16[12,48,256]{2,1,0:T(8,128)(2,1)S(1)}, bf16[12,48,256]{2,1,0:T(8,128)(2,1)S(1)}, u32[]{:S(2)}, u32[]{:S(2)}) collective-permute-start(bf16[12,48,256]{2,1,0:T(8,128)(2,1)S(1)} %copy-done.14), channel_id=1, source_target_pairs={{0,1},{1,2},{2,3},{3,0},{4,5},{5,6},{6,7},{7,4},{8,9},{9,10},{10,1... | collective-permute-start | bytes 884744 | tf_op jit(solution)/shard_map/ppermute | solution.py:13
  172.0 22.5 %collective-permute-start.31 = (bf16[12,48,256]{2,1,0:T(8,128)(2,1)}, bf16[12,48,256]{2,1,0:T(8,128)(2,1)}, u32[]{:S(2)}, u32[]{:S(2)}) collective-permute-start(bf16[12,48,256]{2,1,0:T(8,128)(2,1)} %broadcast_select_fusion.15), channel_id=1, source_target_pairs={{0,2},{1,3},{2,0},{3,1},{4,6},{5,7},{6,4},{7,5},{8,10},{9,11},{10,... | collective-permute-start | bytes 884744 | tf_op jit(solution)/shard_map/ppermute | solution.py:13
  174.4 11.5 %collective-permute-start.10 = (bf16[1920,256]{1,0:T(8,128)(2,1)S(1)}, bf16[1920,256]{1,0:T(8,128)(2,1)}, u32[]{:S(2)}, u32[]{:S(2)}) collective-permute-start(bf16[1920,256]{1,0:T(8,128)(2,1)S(1)} %pad_maximum_fusion.24), channel_id=1, source_target_pairs={{0,4},{4,0},{8,12},{12,8},{1,5},{5,1},{9,13},{13,9},{2,6},{6,2},{1... | collective-permute-start | bytes 2949128 | tf_op jit(solution)/shard_map/while/body/ppermute | solution.py:17
  175.2 8.6 %collective-permute-start.9 = (bf16[960,128]{1,0:T(8,128)(2,1)}, bf16[960,128]{1,0:T(8,128)(2,1)S(1)}, u32[]{:S(2)}, u32[]{:S(2)}) collective-permute-start(bf16[960,128]{1,0:T(8,128)(2,1)} %slice.217), channel_id=1, source_target_pairs={{0,8},{4,12},{8,0},{12,4},{1,9},{5,13},{9,1},{13,5},{2,10},{6,14},... | collective-permute-start | bytes 737288 | tf_op jit(solution)/shard_map/while/body/ppermute | solution.py:17
  177.6 8.3 %collective-permute-start.8 = (bf16[960,128]{1,0:T(8,128)(2,1)}, bf16[960,128]{1,0:T(8,128)(2,1)S(1)}, u32[]{:S(2)}, u32[]{:S(2)}) collective-permute-start(bf16[960,128]{1,0:T(8,128)(2,1)} %slice.216), channel_id=1, source_target_pairs={{0,16},{16,0},{1,17},{17,1},{2,18},{18,2},{3,19},{19,3},{4,20},{20... | collective-permute-start | bytes 737288 | tf_op jit(solution)/shard_map/while/body/ppermute | solution.py:17
  186.1 5.9 %collective-permute-start.11 = (bf16[1920,256]{1,0:T(8,128)(2,1)S(1)}, bf16[1920,256]{1,0:T(8,128)(2,1)S(1)}, u32[]{:S(2)}, u32[]{:S(2)}) collective-permute-start(bf16[1920,256]{1,0:T(8,128)(2,1)S(1)} %pad_maximum_fusion.25), channel_id=1, source_target_pairs={{0,4},{4,0},{8,12},{12,8},{1,5},{5,1},{9,13},{13,9},{2,6},{6,2},{1... | collective-permute-start | bytes 2949128 | tf_op jit(solution)/shard_map/while/body/ppermute | solution.py:17
  195.9 10.3 %collective-permute-start.32 = (bf16[12,48,256]{2,1,0:T(8,128)(2,1)S(1)}, bf16[12,48,256]{2,1,0:T(8,128)(2,1)S(1)}, u32[]{:S(2)}, u32[]{:S(2)}) collective-permute-start(bf16[12,48,256]{2,1,0:T(8,128)(2,1)S(1)} %copy-done.13), channel_id=1, source_target_pairs={{0,1},{1,2},{2,3},{3,0},{4,5},{5,6},{6,7},{7,4},{8,9},{9,10},{10,1... | collective-permute-start | bytes 884744 | tf_op jit(solution)/shard_map/ppermute | solution.py:13
  206.2 14.0 %collective-permute-start.36 = (bf16[12,48,256]{2,1,0:T(8,128)(2,1)S(1)}, bf16[12,48,256]{2,1,0:T(8,128)(2,1)S(1)}, u32[]{:S(2)}, u32[]{:S(2)}) collective-permute-start(bf16[12,48,256]{2,1,0:T(8,128)(2,1)S(1)} %broadcast_select_fusion.14), channel_id=1, source_target_pairs={{0,2},{1,3},{2,0},{3,1},{4,6},{5,7},{6,4},{7,5},{8,10},{9,11},{10,... | collective-permute-start | bytes 884744 | tf_op jit(solution)/shard_map/ppermute | solution.py:13
  206.3 1.9 collective-permute-start.33
  206.4 5.7 %collective-permute-start.34 = (bf16[4,48,2,1,128]{4,2,1,0,3:T(2,128)(2,1)S(1)}, bf16[4,48,2,1,128]{4,2,1,0,3:T(2,128)(2,1)S(1)}, u32[]{:S(2)}, u32[]{:S(2)}) collective-permute-start(bf16[4,48,2,1,128]{4,2,1,0,3:T(2,128)(2,1)S(1)} %squeeze.30), channel_id=1, source_target_pairs={{0,8},{4,12},{8,0},{12,4},{1,9},{5,13},{9,1},{13,5},{2,10},{6,14},... | collective-permute-start | bytes 294920 | tf_op jit(solution)/shard_map/ppermute | solution.py:17
  206.8 6.4 %collective-permute-start.35 = (bf16[4,48,2,1,128]{4,2,1,0,3:T(2,128)(2,1)S(1)}, bf16[4,48,2,1,128]{4,2,1,0,3:T(2,128)(2,1)S(1)}, u32[]{:S(2)}, u32[]{:S(2)}) collective-permute-start(bf16[4,48,2,1,128]{4,2,1,0,3:T(2,128)(2,1)S(1)} %squeeze.31), channel_id=1, source_target_pairs={{0,12},{4,8},{8,4},{12,0},{1,13},{5,9},{9,5},{13,1},{2,14},{6,10},... | collective-permute-start | bytes 294920 | tf_op jit(solution)/shard_map/ppermute | solution.py:17
  221.0 2.4 %collective-permute-start.37 = (bf16[4,48,2,1,128]{4,2,1,0,3:T(2,128)(2,1)S(1)}, bf16[4,48,2,1,128]{4,2,1,0,3:T(2,128)(2,1)S(1)}, u32[]{:S(2)}, u32[]{:S(2)}) collective-permute-start(bf16[4,48,2,1,128]{4,2,1,0,3:T(2,128)(2,1)S(1)} %squeeze.33), channel_id=1, source_target_pairs={{0,4},{4,0},{8,12},{12,8},{1,5},{5,1},{9,13},{13,9},{2,6},{6,2},{1... | collective-permute-start | bytes 294920 | tf_op jit(solution)/shard_map/ppermute | solution.py:17
  221.2 5.7 %collective-permute-start.38 = (bf16[4,48,2,1,128]{4,2,1,0,3:T(2,128)(2,1)S(1)}, bf16[4,48,2,1,128]{4,2,1,0,3:T(2,128)(2,1)S(1)}, u32[]{:S(2)}, u32[]{:S(2)}) collective-permute-start(bf16[4,48,2,1,128]{4,2,1,0,3:T(2,128)(2,1)S(1)} %squeeze.34), channel_id=1, source_target_pairs={{0,8},{4,12},{8,0},{12,4},{1,9},{5,13},{9,1},{13,5},{2,10},{6,14},... | collective-permute-start | bytes 294920 | tf_op jit(solution)/shard_map/ppermute | solution.py:17
  221.7 6.4 %collective-permute-start.39 = (bf16[4,48,2,1,128]{4,2,1,0,3:T(2,128)(2,1)S(1)}, bf16[4,48,2,1,128]{4,2,1,0,3:T(2,128)(2,1)S(1)}, u32[]{:S(2)}, u32[]{:S(2)}) collective-permute-start(bf16[4,48,2,1,128]{4,2,1,0,3:T(2,128)(2,1)S(1)} %squeeze.35), channel_id=1, source_target_pairs={{0,12},{4,8},{8,4},{12,0},{1,13},{5,9},{9,5},{13,1},{2,14},{6,10},... | collective-permute-start | bytes 294920 | tf_op jit(solution)/shard_map/ppermute | solution.py:17
  (12 other events, 33.8 us)

commit v15 on v14

--- a/solution.py
+++ b/solution.py
@@ -73,7 +73,7 @@
     return gathered_rows[None, None]
 
 
-def terms_body(choice, weight, near, far, own, second, mirror, first, kept_rest):
+def terms_body(choice, weight, near, far, own, second, mirror, first, *kept_rest):
     near_product = add_columns(weight[...], near[...])
     far_product = add_columns(weight[...], far[...])
     near_kept = choice[0] == 1
@@ -84,30 +84,36 @@
     rows = pl.ds(pl.multiple_of(i * tall, tall), tall)
     first[rows, :] = sent[:, :width].astype(first.dtype)
 
-    @pl.when(i < 2)
-    def _():
+    def write_direct():
         own[rows, :] = kept[:, :width]
         second[rows, :] = sent[:, width:].astype(second.dtype)
         mirror[rows, :] = kept[:, width:].astype(mirror.dtype)
 
-    @pl.when(i == 2)
-    def _():
-        kept_rest[...] = kept
-        first[3 * tall :, :] = sent[:, width:].astype(first.dtype)
-
-
-def product_terms(choice, weight, near, far):
+    if len(kept_rest) == 0:
+        write_direct()
+    else:
+        pl.when(i < 2)(write_direct)
+
+        @pl.when(i == 2)
+        def _():
+            kept_rest[0][...] = kept
+            first[3 * tall :, :] = sent[:, width:].astype(first.dtype)
+
+
+def product_terms(choice, weight, near, far, all_direct):
     depth, rows = weight.shape
     columns = near.shape[1]
     width, tall = columns // 2, depth // 3
+    direct = depth if all_direct else 2 * tall
     wide, narrow = jnp.float32, jnp.bfloat16
     shapes = [
-        jax.ShapeDtypeStruct((2 * tall, width), wide),
-        jax.ShapeDtypeStruct((2 * tall, width), narrow),
-        jax.ShapeDtypeStruct((2 * tall, width), narrow),
-        jax.ShapeDtypeStruct((4 * tall, width), narrow),
-        jax.ShapeDtypeStruct((tall, columns), wide),
+        jax.ShapeDtypeStruct((direct, width), wide),
+        jax.ShapeDtypeStruct((direct, width), narrow),
+        jax.ShapeDtypeStruct((direct, width), narrow),
+        jax.ShapeDtypeStruct((2 * depth - direct, width), narrow),
     ]
+    if not all_direct:
+        shapes = shapes + [jax.ShapeDtypeStruct((tall, columns), wide)]
     whole = [pl.BlockSpec(array.shape, lambda i, choice: (0, 0)) for array in (near, *shapes)]
     return pl.pallas_call(
         terms_body,
@@ -167,8 +173,8 @@
 
     choice = (at_end == first_core).astype(jnp.int32).reshape(1)
 
-    def products(near, far):
-        return tuple(product_terms(choice, proj_weight, near, far))
+    def products(near, far, all_direct):
+        return tuple(product_terms(choice, proj_weight, near, far, all_direct))
 
     rest = depth // 3
 
@@ -182,13 +188,6 @@
         for other in arrived:
             block = block + other.astype(jnp.float32)
         return block
-
-    def pair_sum(kept_rest, arrived):
-        return plus(kept_rest, jnp.concatenate([arrived[:rest], arrived[rest:]], axis=1))
-
-    def summed(own, arrived, pair, mirrored):
-        rows = [plus(own, *arrived), plus(pair[:, :width], mirrored)]
-        return jnp.concatenate([block.astype(jnp.bfloat16) for block in rows], axis=0)
 
     once = jnp.minimum(jnp.max(tile_count), 1)
 
@@ -241,14 +240,14 @@
     key_block = moved(key_mine, lambda t, h: (h // 2 * 2 + outer_core(h), t))
     comes = swapped(leaves, "tile", 2)
     no_terms = tuple(
-        jnp.full(shape.shape, k, shape.dtype)
-        for k, shape in enumerate(jax.eval_shape(products, *[kv_weight[:, : 2 * width]] * 2))
+        jnp.full((depth, width), once + k, dtype)
+        for k, dtype in enumerate((jnp.float32, jnp.bfloat16, jnp.bfloat16, jnp.bfloat16))
     )
     no_tokens = tuple(
-        jnp.full((tile_slots, shard_len, 2 * width), k, jnp.bfloat16) for k in range(2)
-    )
-    bias_rows, key_block, comes, stays, once, feature_parts = step(
-        (bias_rows, key_block, comes, stays, once, feature_parts)
+        jnp.full((tile_slots, shard_len, 2 * width), once + k, jnp.bfloat16) for k in range(2)
+    )
+    bias_rows, key_block, comes, stays, once, feature_parts, no_terms, no_tokens = step(
+        (bias_rows, key_block, comes, stays, once, feature_parts, no_terms, no_tokens)
     )
 
     value_pieces = []
@@ -266,7 +265,7 @@
     key_near = put_first(tile // 2 == head // 2, key_block, key_other, 1)
     value_half = jnp.concatenate(value_pieces, axis=1)
     key_near, value_half = step((key_near, value_half))
-    terms = products(key_near, swapped(key_near, "tile", 1))
+    terms = products(key_near, swapped(key_near, "tile", 1), False)
     bias_part = bias_part + swapped(bias_part, "tile", 1)
     terms, value_half, bias_part = step((terms, value_half, bias_part))
 
@@ -274,7 +273,7 @@
         value_half, bias_part = given
         other, bias_other = step((swapped(value_half, "tile", 2), swapped(bias_part, "tile", 2)))
         near = step(put_first(first_chip, value_half, other, 0))
-        terms = products(near, swapped(near, "tile", 1))
+        terms = products(near, swapped(near, "tile", 1), True)
         return (other, bias_other), (terms, bias_part + bias_other)
 
     empty = no_terms, bias_part
@@ -289,47 +288,16 @@
     )
     bias_part = bias_part.reshape(2, layers, 2, head_dim)
 
-    value_own, value_second, value_mirror, value_first, value_kept = value_terms
-    pair = pair_sum(kept_rest, first[2 * rest :])
-    pair, value_rest = step((pair, value_first[2 * rest :]))
-    mirrored, value_rest, value_first, value_second, value_mirror = step(
-        (
-            over_middle(pair[:, width:].astype(jnp.bfloat16)),
-            to_neighbour(value_rest),
-            value_first[: 2 * rest],
-            value_second,
-            value_mirror,
-        )
-    )
-    own = summed(own, (second, mirror, first[: 2 * rest]), pair, mirrored)
-
-    def keys_product(own):
-        across_x, across_y = step((swapped(own, "tile", 2), swapped(own, "groups", 1)))
-        rows_0 = step(both_heads(own, across_y))
-        diagonal, rows_1 = step((swapped(across_y, "tile", 2), swapped(rows_0, "tile", 1)))
-        rows_2 = step(both_heads(across_x, diagonal))
-        rows = [rows_0, rows_1, rows_2, swapped(rows_2, "tile", 1)]
-        return across_x, finish(times_features(rows, feature_parts), 0)
-
-    pair = pair_sum(value_kept, value_rest)
-    middle = jnp.concatenate([value_mirror, pair[:, width:].astype(jnp.bfloat16)], axis=0)
-    pair, middle = step((pair, middle))
-    second, middle, first, keys = step(
-        (
-            swapped(value_second, "head", 2),
-            over_middle(middle),
-            to_neighbour(value_first),
-            in_loop(keys_product, own, no_tokens[0]),
-        )
-    )
-    arrived = second, middle[: 2 * rest], first
-    own = summed(value_own, arrived, pair, middle[2 * rest :])
-
-    shifted, across_x, across_y = step(
-        (shifted_2(keys, "head", 1), swapped(own, "tile", 2), swapped(own, "groups", 1))
-    )
-
-    def values_product(given):
+    direct = 2 * rest
+    arrived = jnp.concatenate([first[direct : 3 * rest], first[3 * rest :]], axis=1)
+    pair = plus(kept_rest, arrived)
+    pair, mirrored, value_terms = step(
+        (pair, over_middle(pair[:, width:].astype(jnp.bfloat16)), value_terms)
+    )
+    blocks = [plus(own, second, mirror, first[:direct]), plus(pair[:, :width], mirrored)]
+    own = jnp.concatenate([block.astype(jnp.bfloat16) for block in blocks], axis=0)
+
+    def rest_of_plane(given, part):
         own, across_x, across_y = given
         rows_0 = step(both_heads(own, across_y))
         middle = depth // 2
@@ -342,7 +310,30 @@
         )
         rows_2 = step(both_heads(across_x, jnp.concatenate([upper, lower], axis=0)))
         rows = [rows_0, rows_1, rows_2, swapped(rows_2, "tile", 1)]
-        return (across_y, own, across_x), finish(times_features(rows, feature_parts), 1)
+        return finish(times_features(rows, feature_parts), part)
+
+    def keys_product(own):
+        across_x, across_y = step((swapped(own, "tile", 2), swapped(own, "groups", 1)))
+        return across_x, rest_of_plane((own, across_x, across_y), 0)
+
+    value_own, second, mirror, first = value_terms
+    second, mirror, first, keys = step(
+        (
+            swapped(second, "head", 2),
+            over_middle(mirror),
+            to_neighbour(first),
+            in_loop(keys_product, own, no_tokens[0]),
+        )
+    )
+    own = plus(value_own, second, mirror, first).astype(jnp.bfloat16)
+
+    shifted, across_x, across_y = step(
+        (shifted_2(keys, "head", 1), swapped(own, "tile", 2), swapped(own, "groups", 1))
+    )
+
+    def values_product(given):
+        own, across_x, across_y = given
+        return (across_y, own, across_x), rest_of_plane(given, 1)
 
     keys = step(rolled(keys, shifted, 1))
     values = in_loop(values_product, (own, across_x, across_y), no_tokens[1])

time: 234 us -> 232 us (level)
  other arithmetic: 17.8 us -> 14.6 us
    ppermute x32, waiting for transfers between devices: 69.9 us -> 73.1 us  [swapped(): lax.ppermute(shard, axis, [(i, i ^ bit) for i in range(lax.axis_size(axis...]
    while x20 -> x23, local copies, waits for them, and re-layouts: 4.67 us -> 6.72 us
    broadcast_in_dim x7 -> x6, local copies, waits for them, and re-layouts: 5.72 us -> 5.06 us  [the longest x4 3.58 us: product_plan(): jnp.full((depth, width), once + k, dtype)]
  transfers between devices with their start and end apart: 40 -> 40, of which waited for: 21 -> 23; matrix products, arithmetic and copies ran while one was open for 16% -> 13% of each run, Pallas kernels for 4% -> 3%
where the time goes in v15:
time: 232 us
  waiting for transfers between devices  105 us (45%)
  starting transfers between devices  54.7 us (24%)
  local copies, waits for them, and re-layouts  30.3 us (13%)
  Pallas kernels  15.7 us (7%)
  other arithmetic  14.6 us (6%)
  matrix products  9.93 us (4%)
    ppermute x32, waiting for transfers between devices, swapped(): lax.ppermute(shard, axis, [(i, i ^ bit) for i in range(lax.axis_size(axis...  73.1 us
    ppermute x32, starting transfers between devices, swapped(): lax.ppermute(shard, axis, [(i, i ^ bit) for i in range(lax.axis_size(axis...  46.2 us
    ppermute x4, waiting for transfers between devices, shifted_2(): lax.ppermute(shard, axis, [(i, (i + by) % count) for i in range(count)])  23 us
    pallas_call x2, Pallas kernels, product_terms(): pl.pallas_call(terms_body, out_shape=shapes, grid_spec=pltpu.PrefetchScal...  15.7 us
    dot_general x11, matrix products, add_columns(): return jnp.dot(operand, portion, preferred_element_type=jnp.float32)  9.74 us
    ppermute x4, waiting for transfers between devices, moved(): return lax.ppermute(shard, ('tile', 'head'), pairs)  9.03 us
    dynamic_slice x1, local copies, waits for them, and re-layouts, product_plan(): lax.dynamic_slice_in_dim(feature_rows, (tile ^ r) * depth, depth, axis=1)  7.2 us
    while x23, local copies, waits for them, and re-layouts  6.72 us
  transfers between devices with their start and end apart: 40, of which 23 were waited for; matrix products, arithmetic and copies ran while one was open for 13% of the time, Pallas kernels for 3%

profile of v15, /device:TPU:0, one launch (start us, length us, event | category | flops | bytes accessed | tf_op | source)
XLA Modules:
  0.0 231.7 jit_solution(5288332877414971796)
XLA Ops:
  1.8 2.3 fusion.23
  4.1 6.7 %collective-permute-start.15 = (bf16[1024,128]{1,0:T(8,128)(2,1)}, bf16[1024,128]{1,0:T(8,128)(2,1)}, u32[]{:S(2)}, u32[]{:S(2)}) collective-permute-start(bf16[1024,128]{1,0:T(8,128)(2,1)} %get-tuple-element.585), channel_id=1, source_target_pairs={{0,8},{4,12},{8,0},{12,4},{1,9},{5,13},{9,1},{13,5},{2,10},{6,14},... | collective-permute-start | bytes 786440 | tf_op jit(solution)/shard_map/ppermute | solution.py:17
  10.8 1.3 collective-permute-start.13
  12.1 7.2 %constant_dynamic-slice_fusion = (bf16[576,1920]{1,0:T(8,128)(2,1)}, bf16[576,1920]{1,0:T(8,128)(2,1)}, bf16[576,1920]{1,0:T(8,128)(2,1)}, bf16[576,1920]{1,0:T(8,128)(2,1)}) fusion(bf16[576,7680]{1,0:T(8,128)(2,1)} %bitcast.134, s32[]{:T(128)S(6)} %select_n.299, s32[]{:T(128)S(6)} %select_n.298, s32[]{:T(128)S(6)} %select_n.297, s32[]{:T(128)S(6)} %select_n.296), kind=kLoop, calls=%fused_computation.106 | loop fusion | bytes 17694736 | tf_op jit(solution)/shard_map/dynamic_slice | solution.py:163
  20.7 2.5 %collective-permute-done.15 = bf16[1024,128]{1,0:T(8,128)(2,1)} collective-permute-done((bf16[1024,128]{1,0:T(8,128)(2,1)}, bf16[1024,128]{1,0:T(8,128)(2,1)}, u32[]{:S(2)}, u32[]{:S(2)}) %collective-permute-start.15) | collective-permute-done | bytes 262176 | tf_op jit(solution)/shard_map/ppermute | solution.py:17
  28.2 9.8 %collective-permute-start.18 = (bf16[2048,128]{1,0:T(8,128)(2,1)S(1)}, bf16[2048,128]{1,0:T(8,128)(2,1)S(1)}, u32[]{:S(2)}, u32[]{:S(2)}) collective-permute-start(bf16[2048,128]{1,0:T(8,128)(2,1)S(1)} %collective-permute-done.14), channel_id=1, source_target_pairs={{0,8},{4,12},{8,0},{12,4},{1,9},{5,13},{9,1},{13,5},{2,10},{6,14},... | collective-permute-start | bytes 1572872 | tf_op jit(solution)/shard_map/ppermute | solution.py:17
  39.6 1.4 collective-permute-start.17
  41.4 9.0 %collective-permute-done.17 = bf16[1024,128]{1,0:T(8,128)(2,1)S(1)} collective-permute-done((bf16[1024,128]{1,0:T(8,128)(2,1)S(1)}, bf16[1024,128]{1,0:T(8,128)(2,1)S(1)}, u32[]{:S(2)}, u32[]{:S(2)}) %collective-permute-start.17) | collective-permute-done | bytes 262176 | tf_op jit(solution)/shard_map/ppermute | solution.py:157
  51.5 4.1 %collective-permute-start.19 = (bf16[2048,256]{1,0:T(8,128)(2,1)S(1)}, bf16[2048,256]{1,0:T(8,128)(2,1)S(1)}, u32[]{:S(2)}, u32[]{:S(2)}) collective-permute-start(bf16[2048,256]{1,0:T(8,128)(2,1)S(1)} %pad_maximum_fusion.7.near), channel_id=1, source_target_pairs={{0,4},{4,0},{8,12},{12,8},{1,5},{5,1},{9,13},{13,9},{2,6},{6,2},{1... | collective-permute-start | bytes 3145736 | tf_op jit(solution)/shard_map/ppermute | solution.py:17
  55.7 2.2 collective-permute-done.20
  58.0 7.7 %shard_map.82 = (f32[1280,128]{1,0:T(8,128)S(1)}, bf16[1280,128]{1,0:T(8,128)(2,1)}, bf16[1280,128]{1,0:T(8,128)(2,1)}, bf16[2560,128]{1,0:T(8,128)(2,1)}, f32[640,256]{1,0:T(8,128)S(1)}) custom-call(s32[1]{0:T(128)} %bitcast.11.choice, bf16[1920,2048]{1,0:T(8,128)(2,1)} %weight.1, bf16[2048,256]{1,0:T(8,128)(2,1)S(1)} %pad_maximum_fusion.7.near, ...), custom_call_target="tpu_custom_call" | custom-call | flops 4026531840 | bytes 12419072 | tf_op jit(solution)/shard_map/pallas_call | solution.py:118
  66.3 2.2 collective-permute-start.21
  68.5 2.1 collective-permute-start.22
  70.6 26.0 %while.54 = (s32[]{:T(128)}, bf16[1024,256]{1,0:T(8,128)(2,1)}, f32[1,512]{1,0:T(1,128)S(1)}, f32[1920,128]{1,0:T(8,128)}, bf16[1920,128]{1,0:T(8,128)(2,1)}, /*...) while((s32[]{:T(128)}, bf16[1024,256]{1,0:T(8,128)(2,1)}, ...), condition=%wide.region_3.4_spmd, body=%wide.region_2.3_spmd.sunk | while | flops 4029153792 | bytes 26069264 | solution.py:195
  71.6 1.7 collective-permute-start
  73.7 11.4 %collective-permute-done.1 = f32[1,512]{1,0:T(1,128)S(1)} collective-permute-done((f32[1,512]{1,0:T(1,128)S(1)}, f32[1,512]{1,0:T(1,128)S(1)}, u32[]{:S(2)}, u32[]{:S(2)}) %collective-permute-start.1) | collective-permute-done | bytes 2080 | tf_op jit(solution)/shard_map/while/body/ppermute | solution.py:17
  86.5 2.1 collective-permute-done.2.far
  88.6 8.0 %body.1 = (f32[1920,128]{1,0:T(8,128)}, bf16[1920,128]{1,0:T(8,128)(2,1)}, bf16[1920,128]{1,0:T(8,128)(2,1)}, bf16[1920,128]{1,0:T(8,128)(2,1)}) custom-call(s32[1]{0:T(128)} %get-tuple-element.926.choice, bf16[1920,2048]{1,0:T(8,128)(2,1)} %get-tuple-element.927.weight, bf16[2048,256]{1,0:T(8,128)(2,1)S(1)} %pad_maximum_fusion.18.near, ...), custom_call_target="tpu_custom_call" | custom-call | flops 4026531840 | bytes 12419072 | tf_op jit(solution)/shard_map/while/body/pallas_call | solution.py:118
  96.6 1.9 collective-permute-done.22
  101.0 1.3 add_convert_fusion.1
  102.3 5.0 %collective-permute-done.24 = bf16[640,128]{1,0:T(8,128)(2,1)S(1)} collective-permute-done((bf16[640,128]{1,0:T(8,128)(2,1)S(1)}, bf16[640,128]{1,0:T(8,128)(2,1)S(1)}, u32[]{:S(2)}, u32[]{:S(2)}) %collective-permute-start.24) | collective-permute-done | bytes 163872 | tf_op jit(solution)/shard_map/ppermute | solution.py:17
  107.2 3.1 %collective-permute-start.25 = (bf16[1920,128]{1,0:T(8,128)(2,1)}, bf16[1920,128]{1,0:T(8,128)(2,1)}, u32[]{:S(2)}, u32[]{:S(2)}) collective-permute-start(bf16[1920,128]{1,0:T(8,128)(2,1)} %get-tuple-element.451), channel_id=1, source_target_pairs={{0,2},{1,3},{2,0},{3,1},{4,6},{5,7},{6,4},{7,5},{8,10},{9,11},{10,... | collective-permute-start | bytes 1474568 | tf_op jit(solution)/shard_map/ppermute | solution.py:17
  111.6 31.6 %while.55 = (s32[]{:T(128)}, bf16[1920,128]{1,0:T(8,128)(2,1)S(1)}, bf16[12,48,256]{2,1,0:T(8,128)(2,1)}, s32[]{:T(128)}, pred[]{:T(512)}, /*index=5*/bf16[576,1...) while((s32[]{:T(128)}, bf16[1920,128]{1,0:T(8,128)(2,1)S(1)}, ...), condition=%wide.region_7.8_spmd, body=%wide.region_4.7_spmd.sunk | while | flops 2271905024 | bytes 78961616 | solution.py:195
  111.7 2.0 collective-permute-start.3
  113.7 1.5 collective-permute-start.4
  115.2 7.5 %collective-permute-done.3 = bf16[1920,128]{1,0:T(8,128)(2,1)S(1)} collective-permute-done((bf16[1920,128]{1,0:T(8,128)(2,1)S(1)}, bf16[1920,128]{1,0:T(8,128)(2,1)S(1)}, u32[]{:S(2)}, u32[]{:S(2)}) %collective-permute-start.3) | collective-permute-done | bytes 491552 | tf_op jit(solution)/shard_map/while/body/ppermute | solution.py:17
  122.7 1.5 collective-permute-done.4
  124.5 1.6 collective-permute-start.5
  126.4 6.5 %collective-permute-done.5 = bf16[960,128]{1,0:T(8,128)(2,1)S(1)} collective-permute-done((bf16[960,128]{1,0:T(8,128)(2,1)S(1)}, bf16[960,128]{1,0:T(8,128)(2,1)S(1)}, u32[]{:S(2)}, u32[]{:S(2)}) %collective-permute-start.5) | collective-permute-done | bytes 245792 | tf_op jit(solution)/shard_map/while/body/ppermute | solution.py:17
  137.4 2.1 convolution_add_fusion.10
  143.8 12.3 %collective-permute-done.27 = bf16[1920,128]{1,0:T(8,128)(2,1)S(1)} collective-permute-done((bf16[1920,128]{1,0:T(8,128)(2,1)}, bf16[1920,128]{1,0:T(8,128)(2,1)S(1)}, u32[]{:S(2)}, u32[]{:S(2)}) %collective-permute-start.27) | collective-permute-done | bytes 491552 | tf_op jit(solution)/shard_map/ppermute | solution.py:17
  156.1 1.4 add_convert_fusion
  159.2 8.4 %collective-permute-done.28 = bf16[12,48,256]{2,1,0:T(8,128)(2,1)S(1)} collective-permute-done((bf16[12,48,256]{2,1,0:T(8,128)(2,1)S(1)}, bf16[12,48,256]{2,1,0:T(8,128)(2,1)S(1)}, u32[]{:S(2)}, u32[]{:S(2)}) %collective-permute-start.28) | collective-permute-done | bytes 294944 | tf_op jit(solution)/shard_map/ppermute | solution.py:13
  167.6 1.7 collective-permute-done.29
  170.1 2.5 %collective-permute-start.31 = (bf16[12,48,256]{2,1,0:T(8,128)(2,1)}, bf16[12,48,256]{2,1,0:T(8,128)(2,1)}, u32[]{:S(2)}, u32[]{:S(2)}) collective-permute-start(bf16[12,48,256]{2,1,0:T(8,128)(2,1)} %broadcast_select_fusion.15), channel_id=1, source_target_pairs={{0,2},{1,3},{2,0},{3,1},{4,6},{5,7},{6,4},{7,5},{8,10},{9,11},{10,... | collective-permute-start | bytes 884744 | tf_op jit(solution)/shard_map/ppermute | solution.py:13
  172.7 20.3 %while.56 = (s32[]{:T(128)}, bf16[1920,128]{1,0:T(8,128)(2,1)S(1)}, bf16[1920,128]{1,0:T(8,128)(2,1)S(1)}, bf16[1920,128]{1,0:T(8,128)(2,1)S(1)}, bf16[12,48,256...) while((s32[]{:T(128)}, bf16[1920,128]{1,0:T(8,128)(2,1)S(1)}, ...), condition=%wide.region_9.10_spmd, body=%wide.region_8.9_spmd.sunk | while | flops 2271166464 | bytes 77368712 | solution.py:195
  173.7 1.7 collective-permute-start.10
  176.8 5.4 %collective-permute-done.10 = bf16[960,128]{1,0:T(8,128)(2,1)S(1)} collective-permute-done((bf16[960,128]{1,0:T(8,128)(2,1)}, bf16[960,128]{1,0:T(8,128)(2,1)S(1)}, u32[]{:S(2)}, u32[]{:S(2)}) %collective-permute-start.10) | collective-permute-done | bytes 245792 | tf_op jit(solution)/shard_map/while/body/ppermute | solution.py:17
  182.3 2.1 collective-permute-done.9
  187.6 2.1 convolution_add_fusion.12
  194.4 1.5 collective-permute-start.32
  196.7 7.9 %collective-permute-done.32 = bf16[12,48,256]{2,1,0:T(8,128)(2,1)S(1)} collective-permute-done((bf16[12,48,256]{2,1,0:T(8,128)(2,1)S(1)}, bf16[12,48,256]{2,1,0:T(8,128)(2,1)S(1)}, u32[]{:S(2)}, u32[]{:S(2)}) %collective-permute-start.32) | collective-permute-done | bytes 294944 | tf_op jit(solution)/shard_map/ppermute | solution.py:13
  205.3 1.4 collective-permute-start.35
  206.8 3.8 %collective-permute-done.34 = bf16[4,48,2,1,128]{4,2,1,0,3:T(2,128)(2,1)S(1)} collective-permute-done((bf16[4,48,2,1,128]{4,2,1,0,3:T(2,128)(2,1)S(1)}, bf16[4,48,2,1,128]{4,2,1,0,3:T(2,128)(2,1)S(1)}, u32[]{:S(2)}, u32[]{:S(2)}) %collective-permute-start.34) | collective-permute-done | bytes 98336 | tf_op jit(solution)/shard_map/ppermute | solution.py:17
  211.8 6.6 %collective-permute-done.36 = bf16[12,48,256]{2,1,0:T(8,128)(2,1)S(1)} collective-permute-done((bf16[12,48,256]{2,1,0:T(8,128)(2,1)S(1)}, bf16[12,48,256]{2,1,0:T(8,128)(2,1)S(1)}, u32[]{:S(2)}, u32[]{:S(2)}) %collective-permute-start.36) | collective-permute-done | bytes 294944 | tf_op jit(solution)/shard_map/ppermute | solution.py:13
  219.9 1.5 collective-permute-start.39
  221.5 3.4 %collective-permute-done.38 = bf16[4,48,2,1,128]{4,2,1,0,3:T(2,128)(2,1)S(1)} collective-permute-done((bf16[4,48,2,1,128]{4,2,1,0,3:T(2,128)(2,1)S(1)}, bf16[4,48,2,1,128]{4,2,1,0,3:T(2,128)(2,1)S(1)}, u32[]{:S(2)}, u32[]{:S(2)}) %collective-permute-start.38) | collective-permute-done | bytes 98336 | tf_op jit(solution)/shard_map/ppermute | solution.py:17
  229.6 2.1 copy.19
  (173 shorter events, 48.8 us)
Async XLA Ops:
  1.1 22.1 %collective-permute-start.14 = (bf16[2048,128]{1,0:T(8,128)(2,1)S(1)}, bf16[2048,128]{1,0:T(8,128)(2,1)S(1)}, u32[]{:S(2)}, u32[]{:S(2)}) collective-permute-start(bf16[2048,128]{1,0:T(8,128)(2,1)S(1)} %constant_dynamic-slice_fusion.4), channel_id=1, source_target_pairs={{0,0},{1,4},{2,12},{3,8},{4,1},{5,5},{6,13},{7,9},{8,2},{9,6},{10,... | collective-permute-start | bytes 1572872 | tf_op jit(solution)/shard_map/ppermute | solution.py:157
  4.1 19.1 %collective-permute-start.15 = (bf16[1024,128]{1,0:T(8,128)(2,1)}, bf16[1024,128]{1,0:T(8,128)(2,1)}, u32[]{:S(2)}, u32[]{:S(2)}) collective-permute-start(bf16[1024,128]{1,0:T(8,128)(2,1)} %get-tuple-element.585), channel_id=1, source_target_pairs={{0,8},{4,12},{8,0},{12,4},{1,9},{5,13},{9,1},{13,5},{2,10},{6,14},... | collective-permute-start | bytes 786440 | tf_op jit(solution)/shard_map/ppermute | solution.py:17
  10.8 9.9 %collective-permute-start.13 = (bf16[2048]{0:T(1024)(128)(2,1)}, bf16[2048]{0:T(1024)(128)(2,1)S(1)}, u32[]{:S(2)}, u32[]{:S(2)}) collective-permute-start(bf16[2048]{0:T(1024)(128)(2,1)} %param.16), channel_id=1, source_target_pairs={{0,0},{1,4},{2,8},{3,12},{4,1},{5,5},{6,9},{7,13},{8,2},{9,6},{10,... | collective-permute-start | bytes 12296 | tf_op jit(solution)/shard_map/ppermute | solution.py:157
  12.1 7.2 %copy-start.16 = (s32[4]{0:T(128)S(1)}, s32[4]{0:T(128)}, u32[]{:S(2)}) copy-start(s32[4]{0:T(128)} %param.20) | copy-start | bytes 52
  19.3 21.7 %copy-start.1 = (bf16[2048,512]{1,0:T(8,128)(2,1)S(1)}, bf16[2048,512]{1,0:T(8,128)(2,1)}, u32[]{:S(2)}) copy-start(bf16[2048,512]{1,0:T(8,128)(2,1)} %param.17) | copy-start | bytes 6291460
  28.2 22.3 %collective-permute-start.18 = (bf16[2048,128]{1,0:T(8,128)(2,1)S(1)}, bf16[2048,128]{1,0:T(8,128)(2,1)S(1)}, u32[]{:S(2)}, u32[]{:S(2)}) collective-permute-start(bf16[2048,128]{1,0:T(8,128)(2,1)S(1)} %collective-permute-done.14), channel_id=1, source_target_pairs={{0,8},{4,12},{8,0},{12,4},{1,9},{5,13},{9,1},{13,5},{2,10},{6,14},... | collective-permute-start | bytes 1572872 | tf_op jit(solution)/shard_map/ppermute | solution.py:17
  39.0 2.5 %collective-permute-start.16 = (bf16[1024,128]{1,0:T(8,128)(2,1)S(1)}, bf16[1024,128]{1,0:T(8,128)(2,1)S(1)}, u32[]{:S(2)}, u32[]{:S(2)}) collective-permute-start(bf16[1024,128]{1,0:T(8,128)(2,1)S(1)} %get-tuple-element.591), channel_id=1, source_target_pairs={{0,0},{1,4},{2,6},{3,2},{4,1},{5,5},{6,7},{7,3},{8,8},{9,12},{10,1... | collective-permute-start | bytes 786440 | tf_op jit(solution)/shard_map/ppermute | solution.py:157
  39.6 10.8 %collective-permute-start.17 = (bf16[1024,128]{1,0:T(8,128)(2,1)S(1)}, bf16[1024,128]{1,0:T(8,128)(2,1)S(1)}, u32[]{:S(2)}, u32[]{:S(2)}) collective-permute-start(bf16[1024,128]{1,0:T(8,128)(2,1)S(1)} %get-tuple-element.590), channel_id=1, source_target_pairs={{0,2},{1,6},{2,4},{3,0},{4,3},{5,7},{6,5},{7,1},{8,10},{9,14},{10,... | collective-permute-start | bytes 786440 | tf_op jit(solution)/shard_map/ppermute | solution.py:157
  51.5 6.4 %collective-permute-start.19 = (bf16[2048,256]{1,0:T(8,128)(2,1)S(1)}, bf16[2048,256]{1,0:T(8,128)(2,1)S(1)}, u32[]{:S(2)}, u32[]{:S(2)}) collective-permute-start(bf16[2048,256]{1,0:T(8,128)(2,1)S(1)} %pad_maximum_fusion.7.near), channel_id=1, source_target_pairs={{0,4},{4,0},{8,12},{12,8},{1,5},{5,1},{9,13},{13,9},{2,6},{6,2},{1... | collective-permute-start | bytes 3145736 | tf_op jit(solution)/shard_map/ppermute | solution.py:17
  55.7 2.3 collective-permute-start.20
  66.2 32.3 %collective-permute-start.23 = (bf16[2560,128]{1,0:T(8,128)(2,1)}, bf16[2560,128]{1,0:T(8,128)(2,1)}, u32[]{:S(2)}, u32[]{:S(2)}) collective-permute-start(bf16[2560,128]{1,0:T(8,128)(2,1)} %get-tuple-element.433), channel_id=1, source_target_pairs={{0,1},{1,0},{2,3},{3,2},{4,5},{5,4},{6,7},{7,6},{8,9},{9,8},{10,11... | collective-permute-start | bytes 1966088 | tf_op jit(solution)/shard_map/ppermute | solution.py:17
  66.3 30.3 %collective-permute-start.21 = (bf16[1280,128]{1,0:T(8,128)(2,1)}, bf16[1280,128]{1,0:T(8,128)(2,1)}, u32[]{:S(2)}, u32[]{:S(2)}) collective-permute-start(bf16[1280,128]{1,0:T(8,128)(2,1)} %get-tuple-element.431), channel_id=1, source_target_pairs={{0,2},{1,3},{2,0},{3,1},{4,6},{5,7},{6,4},{7,5},{8,10},{9,11},{10,... | collective-permute-start | bytes 983048 | tf_op jit(solution)/shard_map/ppermute | solution.py:17
  68.5 30.1 %collective-permute-start.22 = (bf16[1280,128]{1,0:T(8,128)(2,1)}, bf16[1280,128]{1,0:T(8,128)(2,1)}, u32[]{:S(2)}, u32[]{:S(2)}) collective-permute-start(bf16[1280,128]{1,0:T(8,128)(2,1)} %get-tuple-element.432), channel_id=1, source_target_pairs={{0,3},{1,2},{2,1},{3,0},{4,7},{5,6},{6,5},{7,4},{8,11},{9,10},{10,... | collective-permute-start | bytes 983048 | tf_op jit(solution)/shard_map/ppermute | solution.py:17
  71.6 13.4 %collective-permute-start = (bf16[1024,256]{1,0:T(8,128)(2,1)S(1)}, bf16[1024,256]{1,0:T(8,128)(2,1)S(1)}, u32[]{:S(2)}, u32[]{:S(2)}) collective-permute-start(bf16[1024,256]{1,0:T(8,128)(2,1)S(1)} %copy.33), channel_id=1, source_target_pairs={{0,8},{4,12},{8,0},{12,4},{1,9},{5,13},{9,1},{13,5},{2,10},{6,14},... | collective-permute-start | bytes 1572872 | tf_op jit(solution)/shard_map/while/body/ppermute | solution.py:17
  73.4 11.6 %collective-permute-start.1 = (f32[1,512]{1,0:T(1,128)S(1)}, f32[1,512]{1,0:T(1,128)S(1)}, u32[]{:S(2)}, u32[]{:S(2)}) collective-permute-start(f32[1,512]{1,0:T(1,128)S(1)} %copy.34), channel_id=1, source_target_pairs={{0,8},{4,12},{8,0},{12,4},{1,9},{5,13},{9,1},{13,5},{2,10},{6,14},... | collective-permute-start | bytes 6152 | tf_op jit(solution)/shard_map/while/body/ppermute | solution.py:17
  85.9 2.7 %collective-permute-start.2 = (bf16[2048,256]{1,0:T(8,128)(2,1)S(1)}, bf16[2048,256]{1,0:T(8,128)(2,1)S(1)}, u32[]{:S(2)}, u32[]{:S(2)}) collective-permute-start(bf16[2048,256]{1,0:T(8,128)(2,1)S(1)} %pad_maximum_fusion.18.near), channel_id=1, source_target_pairs={{0,4},{4,0},{8,12},{12,8},{1,5},{5,1},{9,13},{13,9},{2,6},{6,2},{1... | collective-permute-start | bytes 3145736 | tf_op jit(solution)/shard_map/while/body/ppermute | solution.py:17
  99.6 12.0 %copy-start.13 = (f32[1,512]{1,0:T(1,128)S(1)}, f32[1,512]{1,0:T(1,128)}, u32[]{:S(2)}) copy-start(f32[1,512]{1,0:T(1,128)} %get-tuple-element.464) | copy-start | bytes 6148
  99.6 12.0 %copy-start.14 = (f32[1,128]{1,0:T(1,128)S(1)}, f32[1,128]{1,0:T(1,128)}, u32[]{:S(2)}) copy-start(f32[1,128]{1,0:T(1,128)} %param.18) | copy-start | bytes 1540
  99.7 7.6 %collective-permute-start.24 = (bf16[640,128]{1,0:T(8,128)(2,1)S(1)}, bf16[640,128]{1,0:T(8,128)(2,1)S(1)}, u32[]{:S(2)}, u32[]{:S(2)}) collective-permute-start(bf16[640,128]{1,0:T(8,128)(2,1)S(1)} %slice.157), channel_id=1, source_target_pairs={{0,3},{1,2},{2,1},{3,0},{4,7},{5,6},{6,5},{7,4},{8,11},{9,10},{10,... | collective-permute-start | bytes 491528 | tf_op jit(solution)/shard_map/ppermute | solution.py:17
  107.2 36.5 %collective-permute-start.25 = (bf16[1920,128]{1,0:T(8,128)(2,1)}, bf16[1920,128]{1,0:T(8,128)(2,1)}, u32[]{:S(2)}, u32[]{:S(2)}) collective-permute-start(bf16[1920,128]{1,0:T(8,128)(2,1)} %get-tuple-element.451), channel_id=1, source_target_pairs={{0,2},{1,3},{2,0},{3,1},{4,6},{5,7},{6,4},{7,5},{8,10},{9,11},{10,... | collective-permute-start | bytes 1474568 | tf_op jit(solution)/shard_map/ppermute | solution.py:17
  110.3 33.5 %collective-permute-start.26 = (bf16[1920,128]{1,0:T(8,128)(2,1)}, bf16[1920,128]{1,0:T(8,128)(2,1)}, u32[]{:S(2)}, u32[]{:S(2)}) collective-permute-start(bf16[1920,128]{1,0:T(8,128)(2,1)} %get-tuple-element.452), channel_id=1, source_target_pairs={{0,3},{1,2},{2,1},{3,0},{4,7},{5,6},{6,5},{7,4},{8,11},{9,10},{10,... | collective-permute-start | bytes 1474568 | tf_op jit(solution)/shard_map/ppermute | solution.py:17
  111.6 32.0 %copy-start.15 = (s32[4,4]{1,0:T(4,128)S(1)}, s32[4,4]{1,0:T(4,128)}, u32[]{:S(2)}) copy-start(s32[4,4]{1,0:T(4,128)} %param.19) | copy-start | bytes 196
  111.6 32.1 %copy-start.17 = (s32[4]{0:T(128)S(1)}, s32[4]{0:T(128)}, u32[]{:S(2)}) copy-start(s32[4]{0:T(128)} %param.21) | copy-start | bytes 52
  111.6 44.4 %copy-start.2 = (f32[1920,128]{1,0:T(8,128)S(1)}, f32[1920,128]{1,0:T(8,128)}, u32[]{:S(2)}) copy-start(f32[1920,128]{1,0:T(8,128)} %get-tuple-element.467) | copy-start | bytes 2949124
  111.7 11.0 %collective-permute-start.3 = (bf16[1920,128]{1,0:T(8,128)(2,1)S(1)}, bf16[1920,128]{1,0:T(8,128)(2,1)S(1)}, u32[]{:S(2)}, u32[]{:S(2)}) collective-permute-start(bf16[1920,128]{1,0:T(8,128)(2,1)S(1)} %copy.52), channel_id=1, source_target_pairs={{0,8},{4,12},{8,0},{12,4},{1,9},{5,13},{9,1},{13,5},{2,10},{6,14},... | collective-permute-start | bytes 1474568 | tf_op jit(solution)/shard_map/while/body/ppermute | solution.py:17
  113.7 10.5 %collective-permute-start.4 = (bf16[1920,128]{1,0:T(8,128)(2,1)S(1)}, bf16[1920,128]{1,0:T(8,128)(2,1)S(1)}, u32[]{:S(2)}, u32[]{:S(2)}) collective-permute-start(bf16[1920,128]{1,0:T(8,128)(2,1)S(1)} %copy.52), channel_id=1, source_target_pairs={{0,16},{16,0},{1,17},{17,1},{2,18},{18,2},{3,19},{19,3},{4,20},{20... | collective-permute-start | bytes 1474568 | tf_op jit(solution)/shard_map/while/body/ppermute | solution.py:17
  124.4 9.8 %collective-permute-start.7 = (bf16[1920,256]{1,0:T(8,128)(2,1)S(1)}, bf16[1920,256]{1,0:T(8,128)(2,1)}, u32[]{:S(2)}, u32[]{:S(2)}) collective-permute-start(bf16[1920,256]{1,0:T(8,128)(2,1)S(1)} %pad_maximum_fusion.19), channel_id=1, source_target_pairs={{0,4},{4,0},{8,12},{12,8},{1,5},{5,1},{9,13},{13,9},{2,6},{6,2},{1... | collective-permute-start | bytes 2949128 | tf_op jit(solution)/shard_map/while/body/ppermute | solution.py:17
  124.5 8.4 %collective-permute-start.5 = (bf16[960,128]{1,0:T(8,128)(2,1)S(1)}, bf16[960,128]{1,0:T(8,128)(2,1)S(1)}, u32[]{:S(2)}, u32[]{:S(2)}) collective-permute-start(bf16[960,128]{1,0:T(8,128)(2,1)S(1)} %slice.180), channel_id=1, source_target_pairs={{0,16},{16,0},{1,17},{17,1},{2,18},{18,2},{3,19},{19,3},{4,20},{20... | collective-permute-start | bytes 737288 | tf_op jit(solution)/shard_map/while/body/ppermute | solution.py:17
  126.1 8.1 %collective-permute-start.6 = (bf16[960,128]{1,0:T(8,128)(2,1)S(1)}, bf16[960,128]{1,0:T(8,128)(2,1)S(1)}, u32[]{:S(2)}, u32[]{:S(2)}) collective-permute-start(bf16[960,128]{1,0:T(8,128)(2,1)S(1)} %slice.181), channel_id=1, source_target_pairs={{0,8},{4,12},{8,0},{12,4},{1,9},{5,13},{9,1},{13,5},{2,10},{6,14},... | collective-permute-start | bytes 737288 | tf_op jit(solution)/shard_map/while/body/ppermute | solution.py:17
  134.4 5.9 %collective-permute-start.8 = (bf16[1920,256]{1,0:T(8,128)(2,1)S(1)}, bf16[1920,256]{1,0:T(8,128)(2,1)S(1)}, u32[]{:S(2)}, u32[]{:S(2)}) collective-permute-start(bf16[1920,256]{1,0:T(8,128)(2,1)S(1)} %pad_maximum_fusion.20), channel_id=1, source_target_pairs={{0,4},{4,0},{8,12},{12,8},{1,5},{5,1},{9,13},{13,9},{2,6},{6,2},{1... | collective-permute-start | bytes 2949128 | tf_op jit(solution)/shard_map/while/body/ppermute | solution.py:17
  143.2 15.5 %copy-start.12 = (bf16[12,48,256]{2,1,0:T(8,128)(2,1)S(1)}, bf16[12,48,256]{2,1,0:T(8,128)(2,1)}, u32[]{:S(2)}) copy-start(bf16[12,48,256]{2,1,0:T(8,128)(2,1)} %get-tuple-element.466) | copy-start | bytes 884740
  143.2 12.8 %collective-permute-start.27 = (bf16[1920,128]{1,0:T(8,128)(2,1)}, bf16[1920,128]{1,0:T(8,128)(2,1)S(1)}, u32[]{:S(2)}, u32[]{:S(2)}) collective-permute-start(bf16[1920,128]{1,0:T(8,128)(2,1)} %get-tuple-element.453), channel_id=1, source_target_pairs={{0,1},{1,0},{2,3},{3,2},{4,5},{5,4},{6,7},{7,6},{8,9},{9,8},{10,11... | collective-permute-start | bytes 1474568 | tf_op jit(solution)/shard_map/ppermute | solution.py:17
  157.5 11.8 %collective-permute-start.29 = (bf16[1920,128]{1,0:T(8,128)(2,1)S(1)}, bf16[1920,128]{1,0:T(8,128)(2,1)S(1)}, u32[]{:S(2)}, u32[]{:S(2)}) collective-permute-start(bf16[1920,128]{1,0:T(8,128)(2,1)S(1)} %add_convert_fusion), channel_id=1, source_target_pairs={{0,8},{4,12},{8,0},{12,4},{1,9},{5,13},{9,1},{13,5},{2,10},{6,14},... | collective-permute-start | bytes 1474568 | tf_op jit(solution)/shard_map/ppermute | solution.py:17
  157.9 11.4 %collective-permute-start.30 = (bf16[1920,128]{1,0:T(8,128)(2,1)S(1)}, bf16[1920,128]{1,0:T(8,128)(2,1)S(1)}, u32[]{:S(2)}, u32[]{:S(2)}) collective-permute-start(bf16[1920,128]{1,0:T(8,128)(2,1)S(1)} %add_convert_fusion), channel_id=1, source_target_pairs={{0,16},{16,0},{1,17},{17,1},{2,18},{18,2},{3,19},{19,3},{4,20},{20... | collective-permute-start | bytes 1474568 | tf_op jit(solution)/shard_map/ppermute | solution.py:17
  158.7 8.9 %collective-permute-start.28 = (bf16[12,48,256]{2,1,0:T(8,128)(2,1)S(1)}, bf16[12,48,256]{2,1,0:T(8,128)(2,1)S(1)}, u32[]{:S(2)}, u32[]{:S(2)}) collective-permute-start(bf16[12,48,256]{2,1,0:T(8,128)(2,1)S(1)} %copy-done.12), channel_id=1, source_target_pairs={{0,1},{1,2},{2,3},{3,0},{4,5},{5,6},{6,7},{7,4},{8,9},{9,10},{10,1... | collective-permute-start | bytes 884744 | tf_op jit(solution)/shard_map/ppermute | solution.py:13
  170.1 22.9 %collective-permute-start.31 = (bf16[12,48,256]{2,1,0:T(8,128)(2,1)}, bf16[12,48,256]{2,1,0:T(8,128)(2,1)}, u32[]{:S(2)}, u32[]{:S(2)}) collective-permute-start(bf16[12,48,256]{2,1,0:T(8,128)(2,1)} %broadcast_select_fusion.15), channel_id=1, source_target_pairs={{0,2},{1,3},{2,0},{3,1},{4,6},{5,7},{6,4},{7,5},{8,10},{9,11},{10,... | collective-permute-start | bytes 884744 | tf_op jit(solution)/shard_map/ppermute | solution.py:13
  172.9 11.4 %collective-permute-start.11 = (bf16[1920,256]{1,0:T(8,128)(2,1)S(1)}, bf16[1920,256]{1,0:T(8,128)(2,1)}, u32[]{:S(2)}, u32[]{:S(2)}) collective-permute-start(bf16[1920,256]{1,0:T(8,128)(2,1)S(1)} %pad_maximum_fusion.22), channel_id=1, source_target_pairs={{0,4},{4,0},{8,12},{12,8},{1,5},{5,1},{9,13},{13,9},{2,6},{6,2},{1... | collective-permute-start | bytes 2949128 | tf_op jit(solution)/shard_map/while/body/ppermute | solution.py:17
  173.7 8.6 %collective-permute-start.10 = (bf16[960,128]{1,0:T(8,128)(2,1)}, bf16[960,128]{1,0:T(8,128)(2,1)S(1)}, u32[]{:S(2)}, u32[]{:S(2)}) collective-permute-start(bf16[960,128]{1,0:T(8,128)(2,1)} %slice.185), channel_id=1, source_target_pairs={{0,8},{4,12},{8,0},{12,4},{1,9},{5,13},{9,1},{13,5},{2,10},{6,14},... | collective-permute-start | bytes 737288 | tf_op jit(solution)/shard_map/while/body/ppermute | solution.py:17
  176.1 8.3 %collective-permute-start.9 = (bf16[960,128]{1,0:T(8,128)(2,1)}, bf16[960,128]{1,0:T(8,128)(2,1)S(1)}, u32[]{:S(2)}, u32[]{:S(2)}) collective-permute-start(bf16[960,128]{1,0:T(8,128)(2,1)} %slice.184), channel_id=1, source_target_pairs={{0,16},{16,0},{1,17},{17,1},{2,18},{18,2},{3,19},{19,3},{4,20},{20... | collective-permute-start | bytes 737288 | tf_op jit(solution)/shard_map/while/body/ppermute | solution.py:17
  184.6 5.9 %collective-permute-start.12 = (bf16[1920,256]{1,0:T(8,128)(2,1)S(1)}, bf16[1920,256]{1,0:T(8,128)(2,1)S(1)}, u32[]{:S(2)}, u32[]{:S(2)}) collective-permute-start(bf16[1920,256]{1,0:T(8,128)(2,1)S(1)} %pad_maximum_fusion.23), channel_id=1, source_target_pairs={{0,4},{4,0},{8,12},{12,8},{1,5},{5,1},{9,13},{13,9},{2,6},{6,2},{1... | collective-permute-start | bytes 2949128 | tf_op jit(solution)/shard_map/while/body/ppermute | solution.py:17
  194.4 10.3 %collective-permute-start.32 = (bf16[12,48,256]{2,1,0:T(8,128)(2,1)S(1)}, bf16[12,48,256]{2,1,0:T(8,128)(2,1)S(1)}, u32[]{:S(2)}, u32[]{:S(2)}) collective-permute-start(bf16[12,48,256]{2,1,0:T(8,128)(2,1)S(1)} %copy-done.11), channel_id=1, source_target_pairs={{0,1},{1,2},{2,3},{3,0},{4,5},{5,6},{6,7},{7,4},{8,9},{9,10},{10,1... | collective-permute-start | bytes 884744 | tf_op jit(solution)/shard_map/ppermute | solution.py:13
  204.7 13.6 %collective-permute-start.36 = (bf16[12,48,256]{2,1,0:T(8,128)(2,1)S(1)}, bf16[12,48,256]{2,1,0:T(8,128)(2,1)S(1)}, u32[]{:S(2)}, u32[]{:S(2)}) collective-permute-start(bf16[12,48,256]{2,1,0:T(8,128)(2,1)S(1)} %broadcast_select_fusion.14), channel_id=1, source_target_pairs={{0,2},{1,3},{2,0},{3,1},{4,6},{5,7},{6,4},{7,5},{8,10},{9,11},{10,... | collective-permute-start | bytes 884744 | tf_op jit(solution)/shard_map/ppermute | solution.py:13
  204.8 1.9 collective-permute-start.33
  204.9 5.7 %collective-permute-start.34 = (bf16[4,48,2,1,128]{4,2,1,0,3:T(2,128)(2,1)S(1)}, bf16[4,48,2,1,128]{4,2,1,0,3:T(2,128)(2,1)S(1)}, u32[]{:S(2)}, u32[]{:S(2)}) collective-permute-start(bf16[4,48,2,1,128]{4,2,1,0,3:T(2,128)(2,1)S(1)} %squeeze.30), channel_id=1, source_target_pairs={{0,8},{4,12},{8,0},{12,4},{1,9},{5,13},{9,1},{13,5},{2,10},{6,14},... | collective-permute-start | bytes 294920 | tf_op jit(solution)/shard_map/ppermute | solution.py:17
  205.3 6.4 %collective-permute-start.35 = (bf16[4,48,2,1,128]{4,2,1,0,3:T(2,128)(2,1)S(1)}, bf16[4,48,2,1,128]{4,2,1,0,3:T(2,128)(2,1)S(1)}, u32[]{:S(2)}, u32[]{:S(2)}) collective-permute-start(bf16[4,48,2,1,128]{4,2,1,0,3:T(2,128)(2,1)S(1)} %squeeze.31), channel_id=1, source_target_pairs={{0,12},{4,8},{8,4},{12,0},{1,13},{5,9},{9,5},{13,1},{2,14},{6,10},... | collective-permute-start | bytes 294920 | tf_op jit(solution)/shard_map/ppermute | solution.py:17
  219.1 2.4 %collective-permute-start.37 = (bf16[4,48,2,1,128]{4,2,1,0,3:T(2,128)(2,1)S(1)}, bf16[4,48,2,1,128]{4,2,1,0,3:T(2,128)(2,1)S(1)}, u32[]{:S(2)}, u32[]{:S(2)}) collective-permute-start(bf16[4,48,2,1,128]{4,2,1,0,3:T(2,128)(2,1)S(1)} %squeeze.33), channel_id=1, source_target_pairs={{0,4},{4,0},{8,12},{12,8},{1,5},{5,1},{9,13},{13,9},{2,6},{6,2},{1... | collective-permute-start | bytes 294920 | tf_op jit(solution)/shard_map/ppermute | solution.py:17
  219.3 5.7 %collective-permute-start.38 = (bf16[4,48,2,1,128]{4,2,1,0,3:T(2,128)(2,1)S(1)}, bf16[4,48,2,1,128]{4,2,1,0,3:T(2,128)(2,1)S(1)}, u32[]{:S(2)}, u32[]{:S(2)}) collective-permute-start(bf16[4,48,2,1,128]{4,2,1,0,3:T(2,128)(2,1)S(1)} %squeeze.34), channel_id=1, source_target_pairs={{0,8},{4,12},{8,0},{12,4},{1,9},{5,13},{9,1},{13,5},{2,10},{6,14},... | collective-permute-start | bytes 294920 | tf_op jit(solution)/shard_map/ppermute | solution.py:17
  219.9 6.4 %collective-permute-start.39 = (bf16[4,48,2,1,128]{4,2,1,0,3:T(2,128)(2,1)S(1)}, bf16[4,48,2,1,128]{4,2,1,0,3:T(2,128)(2,1)S(1)}, u32[]{:S(2)}, u32[]{:S(2)}) collective-permute-start(bf16[4,48,2,1,128]{4,2,1,0,3:T(2,128)(2,1)S(1)} %squeeze.35), channel_id=1, source_target_pairs={{0,12},{4,8},{8,4},{12,0},{1,13},{5,9},{9,5},{13,1},{2,14},{6,10},... | collective-permute-start | bytes 294920 | tf_op jit(solution)/shard_map/ppermute | solution.py:17
  (10 other events, 16.2 us)

commit v16 on v14

--- a/solution.py
+++ b/solution.py
@@ -73,7 +73,7 @@
     return gathered_rows[None, None]
 
 
-def terms_body(choice, weight, near, far, own, second, mirror, first, kept_rest):
+def terms_body(choice, weight, near, far, own, second, mirror, kept_rest, first, *rest):
     near_product = add_columns(weight[...], near[...])
     far_product = add_columns(weight[...], far[...])
     near_kept = choice[0] == 1
@@ -81,33 +81,35 @@
     sent = jnp.where(near_kept, far_product, near_product)
     tall, width = weight.shape[0], own.shape[1]
     i = pl.program_id(0)
-    rows = pl.ds(pl.multiple_of(i * tall, tall), tall)
-    first[rows, :] = sent[:, :width].astype(first.dtype)
 
     @pl.when(i < 2)
     def _():
+        rows = pl.ds(pl.multiple_of(i * tall, tall), tall)
         own[rows, :] = kept[:, :width]
         second[rows, :] = sent[:, width:].astype(second.dtype)
         mirror[rows, :] = kept[:, width:].astype(mirror.dtype)
+        first[rows, :] = sent[:, :width].astype(first.dtype)
 
     @pl.when(i == 2)
     def _():
         kept_rest[...] = kept
-        first[3 * tall :, :] = sent[:, width:].astype(first.dtype)
-
-
-def product_terms(choice, weight, near, far):
+        target, start = (rest[0], 0) if rest else (first, 2 * tall)
+        target[start : start + tall, :] = sent[:, :width].astype(target.dtype)
+        target[start + tall :, :] = sent[:, width:].astype(target.dtype)
+
+
+def term_shapes(depth, width, joined):
+    tall, wide, narrow = depth // 3, jnp.float32, jnp.bfloat16
+    rows = [(2 * tall, wide), (2 * tall, narrow), (2 * tall, narrow), (tall, wide)]
+    rows = rows + ([(4 * tall, narrow)] if joined else [(2 * tall, narrow)] * 2)
+    return [jax.ShapeDtypeStruct((n, 2 * width if n == tall else width), t) for n, t in rows]
+
+
+def product_terms(choice, weight, near, far, joined):
     depth, rows = weight.shape
     columns = near.shape[1]
-    width, tall = columns // 2, depth // 3
-    wide, narrow = jnp.float32, jnp.bfloat16
-    shapes = [
-        jax.ShapeDtypeStruct((2 * tall, width), wide),
-        jax.ShapeDtypeStruct((2 * tall, width), narrow),
-        jax.ShapeDtypeStruct((2 * tall, width), narrow),
-        jax.ShapeDtypeStruct((4 * tall, width), narrow),
-        jax.ShapeDtypeStruct((tall, columns), wide),
-    ]
+    tall = depth // 3
+    shapes = term_shapes(depth, columns // 2, joined)
     whole = [pl.BlockSpec(array.shape, lambda i, choice: (0, 0)) for array in (near, *shapes)]
     return pl.pallas_call(
         terms_body,
@@ -121,10 +123,18 @@
         compiler_params=pltpu.CompilerParams(vmem_limit_bytes=32 * 1024 * 1024),
         cost_estimate=pl.CostEstimate(
             flops=4 * depth * rows * columns,
-            bytes_accessed=2 * depth * rows + 4 * rows * columns + 10 * depth * width,
+            bytes_accessed=2 * depth * rows + 4 * rows * columns + 5 * depth * columns,
             transcendentals=0,
         ),
     )(choice, weight, near, far)
+
+
+def blank_arrays(shapes):
+    return pl.pallas_call(
+        lambda *refs: None,
+        out_shape=shapes,
+        out_specs=[pl.BlockSpec(memory_space=pl.ANY)] * len(shapes),
+    )()
 
 
 def product_plan(
@@ -167,8 +177,8 @@
 
     choice = (at_end == first_core).astype(jnp.int32).reshape(1)
 
-    def products(near, far):
-        return tuple(product_terms(choice, proj_weight, near, far))
+    def products(near, far, joined):
+        return tuple(product_terms(choice, proj_weight, near, far, joined))
 
     rest = depth // 3
 
@@ -182,13 +192,6 @@
         for other in arrived:
             block = block + other.astype(jnp.float32)
         return block
-
-    def pair_sum(kept_rest, arrived):
-        return plus(kept_rest, jnp.concatenate([arrived[:rest], arrived[rest:]], axis=1))
-
-    def summed(own, arrived, pair, mirrored):
-        rows = [plus(own, *arrived), plus(pair[:, :width], mirrored)]
-        return jnp.concatenate([block.astype(jnp.bfloat16) for block in rows], axis=0)
 
     once = jnp.minimum(jnp.max(tile_count), 1)
 
@@ -215,9 +218,10 @@
     selector = jnp.einsum("rd,rjs->djs", owned_by, matched.astype(jnp.float32))
     selector = selector.astype(jnp.bfloat16).reshape(4 * most_tiles, tile_slots)
 
+    turned = [turn_of // stride % 2 == 1 for stride in (1, 2)]
+
     def rolled(rows, shifted, stride):
-        odd = (turn_of // stride % 2 == 1)[:, None, None]
-        return jnp.where(odd, shifted, rows)
+        return jnp.where(turned[stride - 1][:, None, None], shifted, rows)
 
     def outgoing(rows):
         picked = add_columns(selector, rows.reshape(tile_slots, -1)).astype(jnp.bfloat16)
@@ -233,40 +237,57 @@
         return jnp.stack(ranked, axis=1)
 
     column, half = group * 2 * head_dim, kv_weight.shape[0] // 2
-    key_mine = lax.dynamic_slice_in_dim(kv_weight, column, head_dim, axis=1)
-    value_mine = lax.dynamic_slice_in_dim(kv_weight, column + head_dim, head_dim, axis=1)
-    stays = lax.dynamic_slice_in_dim(value_mine, tile // 2 * half, half, axis=0)
-    leaves = lax.dynamic_slice_in_dim(value_mine, half - tile // 2 * half, half, axis=0)
+
+    def halves(part):
+        mine = lax.dynamic_slice_in_dim(kv_weight, column + part * head_dim, head_dim, axis=1)
+        ours = lax.dynamic_slice_in_dim(mine, tile // 2 * half, half, axis=0)
+        return ours, lax.dynamic_slice_in_dim(mine, half - tile // 2 * half, half, axis=0)
+
+    def to_planes(stays, comes):
+        pieces = []
+        for j in range(2):
+            piece = jnp.where(tile // 2 == (head // 2) ^ j, stays, comes)
+            pieces.append(
+                moved(piece, lambda t, h: (t // 2 * 2 + outer_core(h), t % 2 + 2 * ((h // 2) ^ j)))
+            )
+        return pieces
+
+    key_stays, key_leaves = halves(0)
     bias_rows = moved(proj_bias, lambda t, h: (h, t))
-    key_block = moved(key_mine, lambda t, h: (h // 2 * 2 + outer_core(h), t))
-    comes = swapped(leaves, "tile", 2)
-    no_terms = tuple(
-        jnp.full(shape.shape, k, shape.dtype)
-        for k, shape in enumerate(jax.eval_shape(products, *[kv_weight[:, : 2 * width]] * 2))
-    )
-    no_tokens = tuple(
-        jnp.full((tile_slots, shard_len, 2 * width), k, jnp.bfloat16) for k in range(2)
-    )
-    bias_rows, key_block, comes, stays, once, feature_parts = step(
-        (bias_rows, key_block, comes, stays, once, feature_parts)
-    )
-
-    value_pieces = []
-    for j in range(2):
-        piece = jnp.where(tile // 2 == (head // 2) ^ j, stays, comes)
-        value_pieces.append(
-            moved(piece, lambda t, h: (t // 2 * 2 + outer_core(h), t % 2 + 2 * ((h // 2) ^ j)))
-        )
-    key_other = swapped(key_block, "tile", 2)
+    key_stays, key_comes, bias_rows, once = step(
+        (key_stays, swapped(key_leaves, "tile", 2), bias_rows, once)
+    )
+
+    value_stays, value_leaves = halves(1)
+    tokens = jax.ShapeDtypeStruct((tile_slots, shard_len, 2 * width), jnp.bfloat16)
+    shapes = term_shapes(depth, width, False) + [tokens, tokens]
+    *no_terms, no_keys, no_values = blank_arrays(shapes)
     bias_part = add_columns(bias_rows[None], kv_weight)
-    value_pieces, key_block, key_other, bias_part = step(
-        (value_pieces, key_block, key_other, bias_part)
-    )
-
-    key_near = put_first(tile // 2 == head // 2, key_block, key_other, 1)
+    key_pieces, value_stays, value_comes, bias_part, turned, selector = step(
+        (
+            to_planes(key_stays, key_comes),
+            value_stays,
+            swapped(value_leaves, "tile", 2),
+            bias_part,
+            turned,
+            selector,
+        )
+    )
+
+    key_half = jnp.concatenate(key_pieces, axis=1)
+    key_half, key_other, value_pieces, feature_parts = step(
+        (
+            key_half,
+            swapped(key_half, "tile", 2),
+            to_planes(value_stays, value_comes),
+            feature_parts,
+        )
+    )
+
+    key_near = put_first(first_chip, key_half, key_other, 0)
     value_half = jnp.concatenate(value_pieces, axis=1)
     key_near, value_half = step((key_near, value_half))
-    terms = products(key_near, swapped(key_near, "tile", 1))
+    terms = products(key_near, swapped(key_near, "tile", 1), True)
     bias_part = bias_part + swapped(bias_part, "tile", 1)
     terms, value_half, bias_part = step((terms, value_half, bias_part))
 
@@ -274,11 +295,11 @@
         value_half, bias_part = given
         other, bias_other = step((swapped(value_half, "tile", 2), swapped(bias_part, "tile", 2)))
         near = step(put_first(first_chip, value_half, other, 0))
-        terms = products(near, swapped(near, "tile", 1))
+        terms = products(near, swapped(near, "tile", 1), False)
         return (other, bias_other), (terms, bias_part + bias_other)
 
-    empty = no_terms, bias_part
-    own, second, mirror, first, kept_rest = terms
+    empty = tuple(no_terms), bias_part
+    own, second, mirror, kept_rest, first = terms
     second, mirror, first, (value_terms, bias_part) = step(
         (
             swapped(second, "head", 2),
@@ -289,47 +310,27 @@
     )
     bias_part = bias_part.reshape(2, layers, 2, head_dim)
 
-    value_own, value_second, value_mirror, value_first, value_kept = value_terms
+    def pair_sum(kept_rest, arrived):
+        return plus(kept_rest, jnp.concatenate([arrived[:rest], arrived[rest:]], axis=1))
+
+    def summed(own, arrived, pair, mirrored):
+        blocks = [plus(own, *arrived), plus(pair[:, :width], mirrored)]
+        return jnp.concatenate([block.astype(jnp.bfloat16) for block in blocks], axis=0)
+
+    value_own, value_second, value_mirror, value_kept, value_first, value_rest = value_terms
     pair = pair_sum(kept_rest, first[2 * rest :])
-    pair, value_rest = step((pair, value_first[2 * rest :]))
-    mirrored, value_rest, value_first, value_second, value_mirror = step(
+    value_rest, mirrored, value_second, value_mirror, value_first = step(
         (
+            to_neighbour(value_rest),
             over_middle(pair[:, width:].astype(jnp.bfloat16)),
-            to_neighbour(value_rest),
-            value_first[: 2 * rest],
             value_second,
             value_mirror,
+            value_first,
         )
     )
     own = summed(own, (second, mirror, first[: 2 * rest]), pair, mirrored)
 
-    def keys_product(own):
-        across_x, across_y = step((swapped(own, "tile", 2), swapped(own, "groups", 1)))
-        rows_0 = step(both_heads(own, across_y))
-        diagonal, rows_1 = step((swapped(across_y, "tile", 2), swapped(rows_0, "tile", 1)))
-        rows_2 = step(both_heads(across_x, diagonal))
-        rows = [rows_0, rows_1, rows_2, swapped(rows_2, "tile", 1)]
-        return across_x, finish(times_features(rows, feature_parts), 0)
-
-    pair = pair_sum(value_kept, value_rest)
-    middle = jnp.concatenate([value_mirror, pair[:, width:].astype(jnp.bfloat16)], axis=0)
-    pair, middle = step((pair, middle))
-    second, middle, first, keys = step(
-        (
-            swapped(value_second, "head", 2),
-            over_middle(middle),
-            to_neighbour(value_first),
-            in_loop(keys_product, own, no_tokens[0]),
-        )
-    )
-    arrived = second, middle[: 2 * rest], first
-    own = summed(value_own, arrived, pair, middle[2 * rest :])
-
-    shifted, across_x, across_y = step(
-        (shifted_2(keys, "head", 1), swapped(own, "tile", 2), swapped(own, "groups", 1))
-    )
-
-    def values_product(given):
+    def rest_of_plane(given, part):
         own, across_x, across_y = given
         rows_0 = step(both_heads(own, across_y))
         middle = depth // 2
@@ -342,10 +343,39 @@
         )
         rows_2 = step(both_heads(across_x, jnp.concatenate([upper, lower], axis=0)))
         rows = [rows_0, rows_1, rows_2, swapped(rows_2, "tile", 1)]
-        return (across_y, own, across_x), finish(times_features(rows, feature_parts), 1)
+        return finish(times_features(rows, feature_parts), part)
+
+    def keys_product(own):
+        across_x, across_y = step((swapped(own, "tile", 2), swapped(own, "groups", 1)))
+        rows_0 = step(both_heads(own, across_y))
+        diagonal, rows_1 = step((swapped(across_y, "tile", 2), swapped(rows_0, "tile", 1)))
+        rows_2 = step(both_heads(across_x, diagonal))
+        rows = [rows_0, rows_1, rows_2, swapped(rows_2, "tile", 1)]
+        return across_x, finish(times_features(rows, feature_parts), 0)
+
+    pair = pair_sum(value_kept, value_rest)
+    middle = jnp.concatenate([value_mirror, pair[:, width:].astype(jnp.bfloat16)], axis=0)
+    pair, middle = step((pair, middle))
+    second, middle, first, keys = step(
+        (
+            swapped(value_second, "head", 2),
+            over_middle(middle),
+            to_neighbour(value_first),
+            in_loop(keys_product, own, no_keys),
+        )
+    )
+    own = summed(value_own, (second, middle[: 2 * rest], first), pair, middle[2 * rest :])
+
+    shifted, across_x, across_y = step(
+        (shifted_2(keys, "head", 1), swapped(own, "tile", 2), swapped(own, "groups", 1))
+    )
+
+    def values_product(given):
+        own, across_x, across_y = given
+        return (across_y, own, across_x), rest_of_plane(given, 1)
 
     keys = step(rolled(keys, shifted, 1))
-    values = in_loop(values_product, (own, across_x, across_y), no_tokens[1])
+    values = in_loop(values_product, (own, across_x, across_y), no_values)
     shifted, values = step((shifted_2(keys, "head", 2), values))
 
     picked = outgoing(rolled(keys, shifted, 2))

time: 234 us -> 227 us (0.970)
  local copies, waits for them, and re-layouts: 30.1 us -> 23.7 us
    ppermute x32 -> x33, starting transfers between devices: 46.9 us -> 39.8 us  [swapped(): lax.ppermute(shard, axis, [(i, i ^ bit) for i in range(lax.axis_size(axis...]
    broadcast_in_dim x7 -> x0, local copies, waits for them, and re-layouts: 5.72 us -> none  [the longest x5 4.26 us: product_plan(): jnp.full(shape.shape, k, shape.dtype)]
    ppermute x4 -> x5, starting transfers between devices: 4.12 us -> 8.97 us  [moved(): return lax.ppermute(shard, ('tile', 'head'), pairs)]
    ppermute x4 -> x5, waiting for transfers between devices: 9.02 us -> 11.6 us  [moved(): return lax.ppermute(shard, ('tile', 'head'), pairs)]
    ppermute x32 -> x33, waiting for transfers between devices: 69.9 us -> 67.9 us  [swapped(): lax.ppermute(shard, axis, [(i, i ^ bit) for i in range(lax.axis_size(axis...]
    while x20 -> x22, local copies, waits for them, and re-layouts: 4.67 us -> 5.41 us
  transfers between devices with their start and end apart: 40 -> 42, of which waited for: 21 -> 23; matrix products, arithmetic and copies ran while one was open for 16% -> 13% of each run, Pallas kernels for 4% -> 4%
where the time goes in v16:
time: 227 us; the launch traced here: 226 us
  waiting for transfers between devices  104 us (46%)
  starting transfers between devices  53.8 us (24%)
  local copies, waits for them, and re-layouts  23.7 us (10%)
  other arithmetic  17.9 us (8%)
  Pallas kernels  16.1 us (7%)
  matrix products  9.93 us (4%)
    ppermute x33, waiting for transfers between devices, swapped(): lax.ppermute(shard, axis, [(i, i ^ bit) for i in range(lax.axis_size(axis...  67.9 us
    ppermute x33, starting transfers between devices, swapped(): lax.ppermute(shard, axis, [(i, i ^ bit) for i in range(lax.axis_size(axis...  39.8 us
    ppermute x4, waiting for transfers between devices, shifted_2(): lax.ppermute(shard, axis, [(i, (i + by) % count) for i in range(count)])  24.1 us
    pallas_call x2, Pallas kernels, product_terms(): pl.pallas_call(terms_body, out_shape=shapes, grid_spec=pltpu.PrefetchScal...  16.1 us
    ppermute x5, waiting for transfers between devices, moved(): return lax.ppermute(shard, ('tile', 'head'), pairs)  11.6 us
    dot_general x11, matrix products, add_columns(): return jnp.dot(operand, portion, preferred_element_type=jnp.float32)  9.74 us
    ppermute x5, starting transfers between devices, moved(): return lax.ppermute(shard, ('tile', 'head'), pairs)  8.97 us
    dynamic_slice x1, local copies, waits for them, and re-layouts, product_plan(): lax.dynamic_slice_in_dim(feature_rows, (tile ^ r) * depth, depth, axis=1)  7.16 us
  transfers between devices with their start and end apart: 42, of which 23 were waited for; matrix products, arithmetic and copies ran while one was open for 13% of the time, Pallas kernels for 4%

profile of v16, /device:TPU:0, one launch (start us, length us, event | category | flops | bytes accessed | tf_op | source)
XLA Modules:
  0.0 226.4 jit_solution(3656019581872916367)
XLA Ops:
  0.0 2.3 %fusion.24 = (bf16[1024,128]{1,0:T(8,128)(2,1)S(1)}, bf16[1024,128]{1,0:T(8,128)(2,1)S(1)}, bf16[1024,128]{1,0:T(8,128)(2,1)S(1)}, bf16[1024,128]{1,0:T(8,128)(2,1)S(1)}) fusion(bf16[2048,512]{1,0:T(8,128)(2,1)} %param.17, s32[]{:T(128)S(6)} %select_n.287, s32[]{:T(128)S(6)} %select_n.292, s32[]{:T(128)S(6)} %select_n.283, s32[]{:T(128)S(6)} %select_n.285), kind=kLoop, calls=%fused_computation.130 | loop fusion | bytes 2097168 | tf_op jit(solution)/shard_map/dynamic_slice | solution.py:244
  2.3 3.0 %collective-permute-start.12 = (bf16[1024,128]{1,0:T(8,128)(2,1)S(1)}, bf16[1024,128]{1,0:T(8,128)(2,1)}, u32[]{:S(2)}, u32[]{:S(2)}) collective-permute-start(bf16[1024,128]{1,0:T(8,128)(2,1)S(1)} %get-tuple-element.625), channel_id=1, source_target_pairs={{0,8},{4,12},{8,0},{12,4},{1,9},{5,13},{9,1},{13,5},{2,10},{6,14},... | collective-permute-start | bytes 786440 | tf_op jit(solution)/shard_map/ppermute | solution.py:17
  5.3 1.3 collective-permute-start.13
  6.7 4.7 %collective-permute-start.16 = (bf16[1024,128]{1,0:T(8,128)(2,1)S(1)}, bf16[1024,128]{1,0:T(8,128)(2,1)S(1)}, u32[]{:S(2)}, u32[]{:S(2)}) collective-permute-start(bf16[1024,128]{1,0:T(8,128)(2,1)S(1)} %get-tuple-element.623), channel_id=1, source_target_pairs={{0,8},{4,12},{8,0},{12,4},{1,9},{5,13},{9,1},{13,5},{2,10},{6,14},... | collective-permute-start | bytes 786440 | tf_op jit(solution)/shard_map/ppermute | solution.py:17
  16.9 1.9 collective-permute-start.15
  19.2 10.9 %collective-permute-done.15 = bf16[1024,128]{1,0:T(8,128)(2,1)S(1)} collective-permute-done((bf16[1024,128]{1,0:T(8,128)(2,1)S(1)}, bf16[1024,128]{1,0:T(8,128)(2,1)S(1)}, u32[]{:S(2)}, u32[]{:S(2)}) %collective-permute-start.15) | collective-permute-done | bytes 262176 | tf_op jit(solution)/shard_map/ppermute | solution.py:161
  30.3 1.6 collective-permute-start.17
  32.6 4.3 %collective-permute-start.19 = (bf16[1024,128]{1,0:T(8,128)(2,1)S(1)}, bf16[1024,128]{1,0:T(8,128)(2,1)S(1)}, u32[]{:S(2)}, u32[]{:S(2)}) collective-permute-start(bf16[1024,128]{1,0:T(8,128)(2,1)S(1)} %get-tuple-element.631), channel_id=1, source_target_pairs={{0,2},{1,6},{2,4},{3,0},{4,3},{5,7},{6,5},{7,1},{8,10},{9,14},{10,... | collective-permute-start | bytes 786440 | tf_op jit(solution)/shard_map/ppermute | solution.py:161
  36.9 7.2 %constant_dynamic-slice_fusion = (bf16[576,1920]{1,0:T(8,128)(2,1)}, bf16[576,1920]{1,0:T(8,128)(2,1)}, bf16[576,1920]{1,0:T(8,128)(2,1)}, bf16[576,1920]{1,0:T(8,128)(2,1)}) fusion(bf16[576,7680]{1,0:T(8,128)(2,1)} %bitcast.134, s32[]{:T(128)S(6)} %select_n.305, s32[]{:T(128)S(6)} %select_n.304, s32[]{:T(128)S(6)} %select_n.303, s32[]{:T(128)S(6)} %select_n.302), kind=kLoop, calls=%fused_computation.121 | loop fusion | bytes 17694736 | tf_op jit(solution)/shard_map/dynamic_slice | solution.py:167
  45.9 5.0 %collective-permute-start.20 = (bf16[2048,256]{1,0:T(8,128)(2,1)S(1)}, bf16[2048,256]{1,0:T(8,128)(2,1)S(1)}, u32[]{:S(2)}, u32[]{:S(2)}) collective-permute-start(bf16[2048,256]{1,0:T(8,128)(2,1)S(1)} %pad_maximum_fusion.7.near), channel_id=1, source_target_pairs={{0,4},{4,0},{8,12},{12,8},{1,5},{5,1},{9,13},{13,9},{2,6},{6,2},{1... | collective-permute-start | bytes 3145736 | tf_op jit(solution)/shard_map/ppermute | solution.py:17
  51.1 2.2 collective-permute-done.21
  53.3 7.8 %shard_map.82 = (f32[1280,128]{1,0:T(8,128)S(1)}, bf16[1280,128]{1,0:T(8,128)(2,1)}, bf16[1280,128]{1,0:T(8,128)(2,1)}, f32[640,256]{1,0:T(8,128)S(1)}, bf16[2560,128]{1,0:T(8,128)(2,1)}) custom-call(s32[1]{0:T(128)} %bitcast.14.choice, bf16[1920,2048]{1,0:T(8,128)(2,1)} %weight.1, bf16[2048,256]{1,0:T(8,128)(2,1)S(1)} %pad_maximum_fusion.7.near, ...), custom_call_target="tpu_custom_call" | custom-call | flops 4026531840 | bytes 12419072 | tf_op jit(solution)/shard_map/pallas_call | solution.py:114
  62.0 1.9 collective-permute-start.22
  63.9 2.2 collective-permute-start.23
  66.1 26.3 %while.58 = (s32[]{:T(128)}, bf16[1024,256]{1,0:T(8,128)(2,1)}, f32[1,512]{1,0:T(1,128)S(1)}, f32[1280,128]{1,0:T(8,128)}, bf16[1280,128]{1,0:T(8,128)(2,1)}, /*...) while((s32[]{:T(128)}, bf16[1024,256]{1,0:T(8,128)(2,1)}, ...), condition=%wide.region_3.4_spmd, body=%wide.region_2.3_spmd.sunk | while | flops 4029153792 | bytes 26069280 | solution.py:199
  67.8 1.3 collective-permute-start.1
  69.1 11.4 %collective-permute-done.1 = f32[1,512]{1,0:T(1,128)S(1)} collective-permute-done((f32[1,512]{1,0:T(1,128)S(1)}, f32[1,512]{1,0:T(1,128)S(1)}, u32[]{:S(2)}, u32[]{:S(2)}) %collective-permute-start.1) | collective-permute-done | bytes 2080 | tf_op jit(solution)/shard_map/while/body/ppermute | solution.py:17
  82.1 2.1 collective-permute-done.2.far
  84.1 8.3 %body.1 = (f32[1280,128]{1,0:T(8,128)}, bf16[1280,128]{1,0:T(8,128)(2,1)}, bf16[1280,128]{1,0:T(8,128)(2,1)}, f32[640,256]{1,0:T(8,128)}, bf16[1280,128]{1,0:T(8,128)(2,1)}, /*index=5*/bf16[1280,128]{1,0:T(8,128)(2,1)}) custom-call(s32[1]{0:T(128)} %get-tuple-element.987.choice, bf16[1920,2048]{1,0:T(8,128)(2,1)} %get-tuple-element.988.weight, ...), custom_call_target="tpu_custom_call" | custom-call | flops 4026531840 | bytes 12419072 | tf_op jit(solution)/shard_map/while/body/pallas_call | solution.py:114
  92.4 1.7 collective-permute-done.23
  95.2 1.3 collective-permute-start.26
  97.6 1.3 add_convert_fusion.1
  98.9 5.2 %collective-permute-done.26 = bf16[640,128]{1,0:T(8,128)(2,1)S(1)} collective-permute-done((bf16[640,128]{1,0:T(8,128)(2,1)S(1)}, bf16[640,128]{1,0:T(8,128)(2,1)S(1)}, u32[]{:S(2)}, u32[]{:S(2)}) %collective-permute-start.26) | collective-permute-done | bytes 163872 | tf_op jit(solution)/shard_map/ppermute | solution.py:17
  104.2 4.7 %collective-permute-done.25 = bf16[1280,128]{1,0:T(8,128)(2,1)S(1)} collective-permute-done((bf16[1280,128]{1,0:T(8,128)(2,1)S(1)}, bf16[1280,128]{1,0:T(8,128)(2,1)S(1)}, u32[]{:S(2)}, u32[]{:S(2)}) %collective-permute-start.25) | collective-permute-done | bytes 327712 | tf_op jit(solution)/shard_map/ppermute | solution.py:17
  109.9 2.2 collective-permute-start.28
  112.1 2.2 collective-permute-start.29
  114.3 33.9 %while.59 = (s32[]{:T(128)}, bf16[1920,128]{1,0:T(8,128)(2,1)S(1)}, bf16[12,48,256]{2,1,0:T(8,128)(2,1)}, s32[]{:T(128)}, pred[]{:T(512)}, /*index=5*/bf16[576,1...) while((s32[]{:T(128)}, bf16[1920,128]{1,0:T(8,128)(2,1)S(1)}, ...), condition=%wide.region_7.8_spmd, body=%wide.region_4.7_spmd.sunk | while | flops 2271905024 | bytes 76995496 | solution.py:199
  115.3 1.4 collective-permute-start.4
  116.7 9.0 %collective-permute-done.3 = bf16[1920,128]{1,0:T(8,128)(2,1)S(1)} collective-permute-done((bf16[1920,128]{1,0:T(8,128)(2,1)S(1)}, bf16[1920,128]{1,0:T(8,128)(2,1)S(1)}, u32[]{:S(2)}, u32[]{:S(2)}) %collective-permute-start.3) | collective-permute-done | bytes 491552 | tf_op jit(solution)/shard_map/while/body/ppermute | solution.py:17
  127.8 12.7 %collective-permute-done.5 = bf16[1920,128]{1,0:T(8,128)(2,1)S(1)} collective-permute-done((bf16[1920,128]{1,0:T(8,128)(2,1)S(1)}, bf16[1920,128]{1,0:T(8,128)(2,1)S(1)}, u32[]{:S(2)}, u32[]{:S(2)}) %collective-permute-start.5) | collective-permute-done | bytes 491552 | tf_op jit(solution)/shard_map/while/body/ppermute | solution.py:17
  142.4 2.1 convolution_add_fusion.10
  149.2 1.4 add_convert_fusion
  151.6 1.4 collective-permute-start.32
  154.1 9.5 %collective-permute-done.30 = bf16[12,48,256]{2,1,0:T(8,128)(2,1)S(1)} collective-permute-done((bf16[12,48,256]{2,1,0:T(8,128)(2,1)S(1)}, bf16[12,48,256]{2,1,0:T(8,128)(2,1)S(1)}, u32[]{:S(2)}, u32[]{:S(2)}) %collective-permute-start.30) | collective-permute-done | bytes 294944 | tf_op jit(solution)/shard_map/ppermute | solution.py:13
  165.8 2.0 collective-permute-start.33
  167.8 19.5 %while.60 = (s32[]{:T(128)}, bf16[1920,128]{1,0:T(8,128)(2,1)S(1)}, bf16[1920,128]{1,0:T(8,128)(2,1)S(1)}, bf16[1920,128]{1,0:T(8,128)(2,1)S(1)}, bf16[12,48,256...) while((s32[]{:T(128)}, bf16[1920,128]{1,0:T(8,128)(2,1)S(1)}, ...), condition=%wide.region_9.10_spmd, body=%wide.region_8.9_spmd.sunk | while | flops 2271166464 | bytes 77368712 | solution.py:199
  170.4 1.4 collective-permute-start.8
  171.8 5.6 %collective-permute-done.9 = bf16[960,128]{1,0:T(8,128)(2,1)S(1)} collective-permute-done((bf16[960,128]{1,0:T(8,128)(2,1)}, bf16[960,128]{1,0:T(8,128)(2,1)S(1)}, u32[]{:S(2)}, u32[]{:S(2)}) %collective-permute-start.9) | collective-permute-done | bytes 245792 | tf_op jit(solution)/shard_map/while/body/ppermute | solution.py:17
  177.4 1.3 collective-permute-done.8
  179.1 1.3 copy-done.9
  182.0 2.1 convolution_add_fusion.12
  188.7 1.8 collective-permute-start.34
  191.4 7.6 %collective-permute-done.34 = bf16[12,48,256]{2,1,0:T(8,128)(2,1)S(1)} collective-permute-done((bf16[12,48,256]{2,1,0:T(8,128)(2,1)S(1)}, bf16[12,48,256]{2,1,0:T(8,128)(2,1)S(1)}, u32[]{:S(2)}, u32[]{:S(2)}) %collective-permute-start.34) | collective-permute-done | bytes 294944 | tf_op jit(solution)/shard_map/ppermute | solution.py:13
  201.1 3.8 %collective-permute-done.36 = bf16[4,48,2,1,128]{4,2,1,0,3:T(2,128)(2,1)S(1)} collective-permute-done((bf16[4,48,2,1,128]{4,2,1,0,3:T(2,128)(2,1)S(1)}, bf16[4,48,2,1,128]{4,2,1,0,3:T(2,128)(2,1)S(1)}, u32[]{:S(2)}, u32[]{:S(2)}) %collective-permute-start.36) | collective-permute-done | bytes 98336 | tf_op jit(solution)/shard_map/ppermute | solution.py:17
  206.1 6.9 %collective-permute-done.38 = bf16[12,48,256]{2,1,0:T(8,128)(2,1)S(1)} collective-permute-done((bf16[12,48,256]{2,1,0:T(8,128)(2,1)S(1)}, bf16[12,48,256]{2,1,0:T(8,128)(2,1)S(1)}, u32[]{:S(2)}, u32[]{:S(2)}) %collective-permute-start.38) | collective-permute-done | bytes 294944 | tf_op jit(solution)/shard_map/ppermute | solution.py:13
  216.2 3.5 %collective-permute-done.40 = bf16[4,48,2,1,128]{4,2,1,0,3:T(2,128)(2,1)S(1)} collective-permute-done((bf16[4,48,2,1,128]{4,2,1,0,3:T(2,128)(2,1)S(1)}, bf16[4,48,2,1,128]{4,2,1,0,3:T(2,128)(2,1)S(1)}, u32[]{:S(2)}, u32[]{:S(2)}) %collective-permute-start.40) | collective-permute-done | bytes 98336 | tf_op jit(solution)/shard_map/ppermute | solution.py:17
  219.7 1.3 collective-permute-done.41
  224.3 2.1 copy.19
  (176 shorter events, 48.8 us)
Async XLA Ops:
  0.0 18.8 %copy-start.1 = (bf16[2048,512]{1,0:T(8,128)(2,1)S(1)}, bf16[2048,512]{1,0:T(8,128)(2,1)}, u32[]{:S(2)}) copy-start(bf16[2048,512]{1,0:T(8,128)(2,1)} %param.17) | copy-start | bytes 6291460
  0.0 13.8 %copy-start.17 = (s32[4]{0:T(128)S(1)}, s32[4]{0:T(128)}, u32[]{:S(2)}) copy-start(s32[4]{0:T(128)} %param.20) | copy-start | bytes 52
  2.3 12.8 %collective-permute-start.12 = (bf16[1024,128]{1,0:T(8,128)(2,1)S(1)}, bf16[1024,128]{1,0:T(8,128)(2,1)}, u32[]{:S(2)}, u32[]{:S(2)}) collective-permute-start(bf16[1024,128]{1,0:T(8,128)(2,1)S(1)} %get-tuple-element.625), channel_id=1, source_target_pairs={{0,8},{4,12},{8,0},{12,4},{1,9},{5,13},{9,1},{13,5},{2,10},{6,14},... | collective-permute-start | bytes 786440 | tf_op jit(solution)/shard_map/ppermute | solution.py:17
  5.3 9.8 %collective-permute-start.13 = (bf16[2048]{0:T(1024)(128)(2,1)}, bf16[2048]{0:T(1024)(128)(2,1)S(1)}, u32[]{:S(2)}, u32[]{:S(2)}) collective-permute-start(bf16[2048]{0:T(1024)(128)(2,1)} %param.16), channel_id=1, source_target_pairs={{0,0},{1,4},{2,8},{3,12},{4,1},{5,5},{6,9},{7,13},{8,2},{9,6},{10,... | collective-permute-start | bytes 12296 | tf_op jit(solution)/shard_map/ppermute | solution.py:161
  6.7 12.5 %collective-permute-start.16 = (bf16[1024,128]{1,0:T(8,128)(2,1)S(1)}, bf16[1024,128]{1,0:T(8,128)(2,1)S(1)}, u32[]{:S(2)}, u32[]{:S(2)}) collective-permute-start(bf16[1024,128]{1,0:T(8,128)(2,1)S(1)} %get-tuple-element.623), channel_id=1, source_target_pairs={{0,8},{4,12},{8,0},{12,4},{1,9},{5,13},{9,1},{13,5},{2,10},{6,14},... | collective-permute-start | bytes 786440 | tf_op jit(solution)/shard_map/ppermute | solution.py:17
  16.2 3.0 %collective-permute-start.14 = (bf16[1024,128]{1,0:T(8,128)(2,1)S(1)}, bf16[1024,128]{1,0:T(8,128)(2,1)S(1)}, u32[]{:S(2)}, u32[]{:S(2)}) collective-permute-start(bf16[1024,128]{1,0:T(8,128)(2,1)S(1)} %get-tuple-element.634), channel_id=1, source_target_pairs={{0,0},{1,4},{2,6},{3,2},{4,1},{5,5},{6,7},{7,3},{8,8},{9,12},{10,1... | collective-permute-start | bytes 786440 | tf_op jit(solution)/shard_map/ppermute | solution.py:161
  16.9 13.3 %collective-permute-start.15 = (bf16[1024,128]{1,0:T(8,128)(2,1)S(1)}, bf16[1024,128]{1,0:T(8,128)(2,1)S(1)}, u32[]{:S(2)}, u32[]{:S(2)}) collective-permute-start(bf16[1024,128]{1,0:T(8,128)(2,1)S(1)} %get-tuple-element.633), channel_id=1, source_target_pairs={{0,2},{1,6},{2,4},{3,0},{4,3},{5,7},{6,5},{7,1},{8,10},{9,14},{10,... | collective-permute-start | bytes 786440 | tf_op jit(solution)/shard_map/ppermute | solution.py:161
  30.3 14.7 %collective-permute-start.17 = (bf16[1024,256]{1,0:T(8,128)(2,1)S(1)}, bf16[1024,256]{1,0:T(8,128)(2,1)S(1)}, u32[]{:S(2)}, u32[]{:S(2)}) collective-permute-start(bf16[1024,256]{1,0:T(8,128)(2,1)S(1)} %constant_dynamic-update-slice_fusion.2), channel_id=1, source_target_pairs={{0,8},{4,12},{8,0},{12,4},{1,9},{5,13},{9,1},{13,5},{2,10},{6,14},... | collective-permute-start | bytes 1572872 | tf_op jit(solution)/shard_map/ppermute | solution.py:17
  31.9 12.2 %collective-permute-start.18 = (bf16[1024,128]{1,0:T(8,128)(2,1)S(1)}, bf16[1024,128]{1,0:T(8,128)(2,1)S(1)}, u32[]{:S(2)}, u32[]{:S(2)}) collective-permute-start(bf16[1024,128]{1,0:T(8,128)(2,1)S(1)} %get-tuple-element.632), channel_id=1, source_target_pairs={{0,0},{1,4},{2,6},{3,2},{4,1},{5,5},{6,7},{7,3},{8,8},{9,12},{10,1... | collective-permute-start | bytes 786440 | tf_op jit(solution)/shard_map/ppermute | solution.py:161
  32.6 12.2 %collective-permute-start.19 = (bf16[1024,128]{1,0:T(8,128)(2,1)S(1)}, bf16[1024,128]{1,0:T(8,128)(2,1)S(1)}, u32[]{:S(2)}, u32[]{:S(2)}) collective-permute-start(bf16[1024,128]{1,0:T(8,128)(2,1)S(1)} %get-tuple-element.631), channel_id=1, source_target_pairs={{0,2},{1,6},{2,4},{3,0},{4,3},{5,7},{6,5},{7,1},{8,10},{9,14},{10,... | collective-permute-start | bytes 786440 | tf_op jit(solution)/shard_map/ppermute | solution.py:161
  45.9 7.3 %collective-permute-start.20 = (bf16[2048,256]{1,0:T(8,128)(2,1)S(1)}, bf16[2048,256]{1,0:T(8,128)(2,1)S(1)}, u32[]{:S(2)}, u32[]{:S(2)}) collective-permute-start(bf16[2048,256]{1,0:T(8,128)(2,1)S(1)} %pad_maximum_fusion.7.near), channel_id=1, source_target_pairs={{0,4},{4,0},{8,12},{12,8},{1,5},{5,1},{9,13},{13,9},{2,6},{6,2},{1... | collective-permute-start | bytes 3145736 | tf_op jit(solution)/shard_map/ppermute | solution.py:17
  51.0 2.3 %collective-permute-start.21 = (f32[1,512]{1,0:T(1,128)S(1)}, f32[1,512]{1,0:T(1,128)S(1)}, u32[]{:S(2)}, u32[]{:S(2)}) collective-permute-start(f32[1,512]{1,0:T(1,128)S(1)} %fusion.31), channel_id=1, source_target_pairs={{0,4},{4,0},{8,12},{12,8},{1,5},{5,1},{9,13},{13,9},{2,6},{6,2},{1... | collective-permute-start | bytes 6152 | tf_op jit(solution)/shard_map/ppermute | solution.py:17
  61.7 32.4 %collective-permute-start.24 = (bf16[2560,128]{1,0:T(8,128)(2,1)}, bf16[2560,128]{1,0:T(8,128)(2,1)}, u32[]{:S(2)}, u32[]{:S(2)}) collective-permute-start(bf16[2560,128]{1,0:T(8,128)(2,1)} %get-tuple-element.458), channel_id=1, source_target_pairs={{0,1},{1,0},{2,3},{3,2},{4,5},{5,4},{6,7},{7,6},{8,9},{9,8},{10,11... | collective-permute-start | bytes 1966088 | tf_op jit(solution)/shard_map/ppermute | solution.py:17
  62.0 30.4 %collective-permute-start.22 = (bf16[1280,128]{1,0:T(8,128)(2,1)}, bf16[1280,128]{1,0:T(8,128)(2,1)}, u32[]{:S(2)}, u32[]{:S(2)}) collective-permute-start(bf16[1280,128]{1,0:T(8,128)(2,1)} %get-tuple-element.456), channel_id=1, source_target_pairs={{0,2},{1,3},{2,0},{3,1},{4,6},{5,7},{6,4},{7,5},{8,10},{9,11},{10,... | collective-permute-start | bytes 983048 | tf_op jit(solution)/shard_map/ppermute | solution.py:17
  63.9 30.2 %collective-permute-start.23 = (bf16[1280,128]{1,0:T(8,128)(2,1)}, bf16[1280,128]{1,0:T(8,128)(2,1)}, u32[]{:S(2)}, u32[]{:S(2)}) collective-permute-start(bf16[1280,128]{1,0:T(8,128)(2,1)} %get-tuple-element.457), channel_id=1, source_target_pairs={{0,3},{1,2},{2,1},{3,0},{4,7},{5,6},{6,5},{7,4},{8,11},{9,10},{10,... | collective-permute-start | bytes 983048 | tf_op jit(solution)/shard_map/ppermute | solution.py:17
  67.1 13.4 %collective-permute-start = (bf16[1024,256]{1,0:T(8,128)(2,1)S(1)}, bf16[1024,256]{1,0:T(8,128)(2,1)S(1)}, u32[]{:S(2)}, u32[]{:S(2)}) collective-permute-start(bf16[1024,256]{1,0:T(8,128)(2,1)S(1)} %copy.35), channel_id=1, source_target_pairs={{0,8},{4,12},{8,0},{12,4},{1,9},{5,13},{9,1},{13,5},{2,10},{6,14},... | collective-permute-start | bytes 1572872 | tf_op jit(solution)/shard_map/while/body/ppermute | solution.py:17
  67.8 12.7 %collective-permute-start.1 = (f32[1,512]{1,0:T(1,128)S(1)}, f32[1,512]{1,0:T(1,128)S(1)}, u32[]{:S(2)}, u32[]{:S(2)}) collective-permute-start(f32[1,512]{1,0:T(1,128)S(1)} %copy.36), channel_id=1, source_target_pairs={{0,8},{4,12},{8,0},{12,4},{1,9},{5,13},{9,1},{13,5},{2,10},{6,14},... | collective-permute-start | bytes 6152 | tf_op jit(solution)/shard_map/while/body/ppermute | solution.py:17
  81.4 2.7 %collective-permute-start.2 = (bf16[2048,256]{1,0:T(8,128)(2,1)S(1)}, bf16[2048,256]{1,0:T(8,128)(2,1)S(1)}, u32[]{:S(2)}, u32[]{:S(2)}) collective-permute-start(bf16[2048,256]{1,0:T(8,128)(2,1)S(1)} %pad_maximum_fusion.20.near), channel_id=1, source_target_pairs={{0,4},{4,0},{8,12},{12,8},{1,5},{5,1},{9,13},{13,9},{2,6},{6,2},{1... | collective-permute-start | bytes 3145736 | tf_op jit(solution)/shard_map/while/body/ppermute | solution.py:17
  95.1 13.8 %copy-start.10 = (f32[640,256]{1,0:T(8,128)S(1)}, f32[640,256]{1,0:T(8,128)}, u32[]{:S(2)}) copy-start(f32[640,256]{1,0:T(8,128)} %get-tuple-element.482) | copy-start | bytes 1966084
  95.2 13.9 %copy-start.11 = (bf16[1280,128]{1,0:T(8,128)(2,1)S(1)}, bf16[1280,128]{1,0:T(8,128)(2,1)}, u32[]{:S(2)}) copy-start(bf16[1280,128]{1,0:T(8,128)(2,1)} %get-tuple-element.484) | copy-start | bytes 983044
  95.2 9.0 %collective-permute-start.26 = (bf16[640,128]{1,0:T(8,128)(2,1)S(1)}, bf16[640,128]{1,0:T(8,128)(2,1)S(1)}, u32[]{:S(2)}, u32[]{:S(2)}) collective-permute-start(bf16[640,128]{1,0:T(8,128)(2,1)S(1)} %slice.184), channel_id=1, source_target_pairs={{0,3},{1,2},{2,1},{3,0},{4,7},{5,6},{6,5},{7,4},{8,11},{9,10},{10,... | collective-permute-start | bytes 491528 | tf_op jit(solution)/shard_map/ppermute | solution.py:17
  96.5 12.3 %collective-permute-start.25 = (bf16[1280,128]{1,0:T(8,128)(2,1)S(1)}, bf16[1280,128]{1,0:T(8,128)(2,1)S(1)}, u32[]{:S(2)}, u32[]{:S(2)}) collective-permute-start(bf16[1280,128]{1,0:T(8,128)(2,1)S(1)} %copy-done.16), channel_id=1, source_target_pairs={{0,1},{1,0},{2,3},{3,2},{4,5},{5,4},{6,7},{7,6},{8,9},{9,8},{10,11... | collective-permute-start | bytes 983048 | tf_op jit(solution)/shard_map/ppermute | solution.py:17
  108.9 5.4 %copy-start.14 = (f32[1,512]{1,0:T(1,128)S(1)}, f32[1,512]{1,0:T(1,128)}, u32[]{:S(2)}) copy-start(f32[1,512]{1,0:T(1,128)} %get-tuple-element.496) | copy-start | bytes 6148
  109.9 38.3 %collective-permute-start.28 = (bf16[1920,128]{1,0:T(8,128)(2,1)}, bf16[1920,128]{1,0:T(8,128)(2,1)}, u32[]{:S(2)}, u32[]{:S(2)}) collective-permute-start(bf16[1920,128]{1,0:T(8,128)(2,1)} %pad_maximum_fusion.10), channel_id=1, source_target_pairs={{0,3},{1,2},{2,1},{3,0},{4,7},{5,6},{6,5},{7,4},{8,11},{9,10},{10,... | collective-permute-start | bytes 1474568 | tf_op jit(solution)/shard_map/ppermute | solution.py:17
  112.0 36.2 %collective-permute-start.27 = (bf16[1280,128]{1,0:T(8,128)(2,1)}, bf16[1280,128]{1,0:T(8,128)(2,1)S(1)}, u32[]{:S(2)}, u32[]{:S(2)}) collective-permute-start(bf16[1280,128]{1,0:T(8,128)(2,1)} %get-tuple-element.481), channel_id=1, source_target_pairs={{0,2},{1,3},{2,0},{3,1},{4,6},{5,7},{6,4},{7,5},{8,10},{9,11},{10,... | collective-permute-start | bytes 983048 | tf_op jit(solution)/shard_map/ppermute | solution.py:17
  112.1 36.2 %collective-permute-start.29 = (bf16[1280,128]{1,0:T(8,128)(2,1)}, bf16[1280,128]{1,0:T(8,128)(2,1)}, u32[]{:S(2)}, u32[]{:S(2)}) collective-permute-start(bf16[1280,128]{1,0:T(8,128)(2,1)} %get-tuple-element.486), channel_id=1, source_target_pairs={{0,1},{1,0},{2,3},{3,2},{4,5},{5,4},{6,7},{7,6},{8,9},{9,8},{10,11... | collective-permute-start | bytes 983048 | tf_op jit(solution)/shard_map/ppermute | solution.py:17
  114.4 11.3 %collective-permute-start.3 = (bf16[1920,128]{1,0:T(8,128)(2,1)S(1)}, bf16[1920,128]{1,0:T(8,128)(2,1)S(1)}, u32[]{:S(2)}, u32[]{:S(2)}) collective-permute-start(bf16[1920,128]{1,0:T(8,128)(2,1)S(1)} %copy.58), channel_id=1, source_target_pairs={{0,8},{4,12},{8,0},{12,4},{1,9},{5,13},{9,1},{13,5},{2,10},{6,14},... | collective-permute-start | bytes 1474568 | tf_op jit(solution)/shard_map/while/body/ppermute | solution.py:17
  115.3 11.3 %collective-permute-start.4 = (bf16[1920,128]{1,0:T(8,128)(2,1)S(1)}, bf16[1920,128]{1,0:T(8,128)(2,1)S(1)}, u32[]{:S(2)}, u32[]{:S(2)}) collective-permute-start(bf16[1920,128]{1,0:T(8,128)(2,1)S(1)} %copy.58), channel_id=1, source_target_pairs={{0,16},{16,0},{1,17},{17,1},{2,18},{18,2},{3,19},{19,3},{4,20},{20... | collective-permute-start | bytes 1474568 | tf_op jit(solution)/shard_map/while/body/ppermute | solution.py:17
  126.8 13.7 %collective-permute-start.6 = (bf16[1920,256]{1,0:T(8,128)(2,1)S(1)}, bf16[1920,256]{1,0:T(8,128)(2,1)}, u32[]{:S(2)}, u32[]{:S(2)}) collective-permute-start(bf16[1920,256]{1,0:T(8,128)(2,1)S(1)} %pad_maximum_fusion.21), channel_id=1, source_target_pairs={{0,4},{4,0},{8,12},{12,8},{1,5},{5,1},{9,13},{13,9},{2,6},{6,2},{1... | collective-permute-start | bytes 2949128 | tf_op jit(solution)/shard_map/while/body/ppermute | solution.py:17
  126.8 13.6 %collective-permute-start.5 = (bf16[1920,128]{1,0:T(8,128)(2,1)S(1)}, bf16[1920,128]{1,0:T(8,128)(2,1)S(1)}, u32[]{:S(2)}, u32[]{:S(2)}) collective-permute-start(bf16[1920,128]{1,0:T(8,128)(2,1)S(1)} %collective-permute-done.4), channel_id=1, source_target_pairs={{0,8},{4,12},{8,0},{12,4},{1,9},{5,13},{9,1},{13,5},{2,10},{6,14},... | collective-permute-start | bytes 1474568 | tf_op jit(solution)/shard_map/while/body/ppermute | solution.py:17
  127.8 12.9 %copy-start.8 = (bf16[576,1920]{1,0:T(8,128)(2,1)S(1)}, bf16[576,1920]{1,0:T(8,128)(2,1)}, u32[]{:S(2)}) copy-start(bf16[576,1920]{1,0:T(8,128)(2,1)} %get-tuple-element.1019) | copy-start | bytes 6635524 | tf_op jit(solution)/shard_map/while
  140.7 4.7 %collective-permute-start.7 = (bf16[1920,256]{1,0:T(8,128)(2,1)S(1)}, bf16[1920,256]{1,0:T(8,128)(2,1)S(1)}, u32[]{:S(2)}, u32[]{:S(2)}) collective-permute-start(bf16[1920,256]{1,0:T(8,128)(2,1)S(1)} %pad_maximum_fusion.22), channel_id=1, source_target_pairs={{0,4},{4,0},{8,12},{12,8},{1,5},{5,1},{9,13},{13,9},{2,6},{6,2},{1... | collective-permute-start | bytes 2949128 | tf_op jit(solution)/shard_map/while/body/ppermute | solution.py:17
  150.7 13.7 %collective-permute-start.31 = (bf16[1920,128]{1,0:T(8,128)(2,1)S(1)}, bf16[1920,128]{1,0:T(8,128)(2,1)S(1)}, u32[]{:S(2)}, u32[]{:S(2)}) collective-permute-start(bf16[1920,128]{1,0:T(8,128)(2,1)S(1)} %pad_maximum_fusion.12), channel_id=1, source_target_pairs={{0,8},{4,12},{8,0},{12,4},{1,9},{5,13},{9,1},{13,5},{2,10},{6,14},... | collective-permute-start | bytes 1474568 | tf_op jit(solution)/shard_map/ppermute | solution.py:17
  151.6 13.3 %collective-permute-start.32 = (bf16[1920,128]{1,0:T(8,128)(2,1)S(1)}, bf16[1920,128]{1,0:T(8,128)(2,1)S(1)}, u32[]{:S(2)}, u32[]{:S(2)}) collective-permute-start(bf16[1920,128]{1,0:T(8,128)(2,1)S(1)} %pad_maximum_fusion.12), channel_id=1, source_target_pairs={{0,16},{16,0},{1,17},{17,1},{2,18},{18,2},{3,19},{19,3},{4,20},{20... | collective-permute-start | bytes 1474568 | tf_op jit(solution)/shard_map/ppermute | solution.py:17
  153.0 10.6 %collective-permute-start.30 = (bf16[12,48,256]{2,1,0:T(8,128)(2,1)S(1)}, bf16[12,48,256]{2,1,0:T(8,128)(2,1)S(1)}, u32[]{:S(2)}, u32[]{:S(2)}) collective-permute-start(bf16[12,48,256]{2,1,0:T(8,128)(2,1)S(1)} %copy-done.13), channel_id=1, source_target_pairs={{0,1},{1,2},{2,3},{3,0},{4,5},{5,6},{6,7},{7,4},{8,9},{9,10},{10,1... | collective-permute-start | bytes 884744 | tf_op jit(solution)/shard_map/ppermute | solution.py:13
  165.8 21.6 %collective-permute-start.33 = (bf16[12,48,256]{2,1,0:T(8,128)(2,1)}, bf16[12,48,256]{2,1,0:T(8,128)(2,1)}, u32[]{:S(2)}, u32[]{:S(2)}) collective-permute-start(bf16[12,48,256]{2,1,0:T(8,128)(2,1)} %broadcast_select_fusion.15), channel_id=1, source_target_pairs={{0,2},{1,3},{2,0},{3,1},{4,6},{5,7},{6,4},{7,5},{8,10},{9,11},{10,... | collective-permute-start | bytes 884744 | tf_op jit(solution)/shard_map/ppermute | solution.py:13
  168.0 10.7 %collective-permute-start.10 = (bf16[1920,256]{1,0:T(8,128)(2,1)S(1)}, bf16[1920,256]{1,0:T(8,128)(2,1)}, u32[]{:S(2)}, u32[]{:S(2)}) collective-permute-start(bf16[1920,256]{1,0:T(8,128)(2,1)S(1)} %pad_maximum_fusion.24), channel_id=1, source_target_pairs={{0,4},{4,0},{8,12},{12,8},{1,5},{5,1},{9,13},{13,9},{2,6},{6,2},{1... | collective-permute-start | bytes 2949128 | tf_op jit(solution)/shard_map/while/body/ppermute | solution.py:17
  168.8 8.6 %collective-permute-start.9 = (bf16[960,128]{1,0:T(8,128)(2,1)}, bf16[960,128]{1,0:T(8,128)(2,1)S(1)}, u32[]{:S(2)}, u32[]{:S(2)}) collective-permute-start(bf16[960,128]{1,0:T(8,128)(2,1)} %slice.210), channel_id=1, source_target_pairs={{0,8},{4,12},{8,0},{12,4},{1,9},{5,13},{9,1},{13,5},{2,10},{6,14},... | collective-permute-start | bytes 737288 | tf_op jit(solution)/shard_map/while/body/ppermute | solution.py:17
  170.4 8.3 %collective-permute-start.8 = (bf16[960,128]{1,0:T(8,128)(2,1)}, bf16[960,128]{1,0:T(8,128)(2,1)S(1)}, u32[]{:S(2)}, u32[]{:S(2)}) collective-permute-start(bf16[960,128]{1,0:T(8,128)(2,1)} %slice.209), channel_id=1, source_target_pairs={{0,16},{16,0},{1,17},{17,1},{2,18},{18,2},{3,19},{19,3},{4,20},{20... | collective-permute-start | bytes 737288 | tf_op jit(solution)/shard_map/while/body/ppermute | solution.py:17
  179.0 5.9 %collective-permute-start.11 = (bf16[1920,256]{1,0:T(8,128)(2,1)S(1)}, bf16[1920,256]{1,0:T(8,128)(2,1)S(1)}, u32[]{:S(2)}, u32[]{:S(2)}) collective-permute-start(bf16[1920,256]{1,0:T(8,128)(2,1)S(1)} %pad_maximum_fusion.25), channel_id=1, source_target_pairs={{0,4},{4,0},{8,12},{12,8},{1,5},{5,1},{9,13},{13,9},{2,6},{6,2},{1... | collective-permute-start | bytes 2949128 | tf_op jit(solution)/shard_map/while/body/ppermute | solution.py:17
  188.7 10.3 %collective-permute-start.34 = (bf16[12,48,256]{2,1,0:T(8,128)(2,1)S(1)}, bf16[12,48,256]{2,1,0:T(8,128)(2,1)S(1)}, u32[]{:S(2)}, u32[]{:S(2)}) collective-permute-start(bf16[12,48,256]{2,1,0:T(8,128)(2,1)S(1)} %copy-done.12), channel_id=1, source_target_pairs={{0,1},{1,2},{2,3},{3,0},{4,5},{5,6},{6,7},{7,4},{8,9},{9,10},{10,1... | collective-permute-start | bytes 884744 | tf_op jit(solution)/shard_map/ppermute | solution.py:13
  199.1 13.9 %collective-permute-start.38 = (bf16[12,48,256]{2,1,0:T(8,128)(2,1)S(1)}, bf16[12,48,256]{2,1,0:T(8,128)(2,1)S(1)}, u32[]{:S(2)}, u32[]{:S(2)}) collective-permute-start(bf16[12,48,256]{2,1,0:T(8,128)(2,1)S(1)} %broadcast_select_fusion.14), channel_id=1, source_target_pairs={{0,2},{1,3},{2,0},{3,1},{4,6},{5,7},{6,4},{7,5},{8,10},{9,11},{10,... | collective-permute-start | bytes 884744 | tf_op jit(solution)/shard_map/ppermute | solution.py:13
  199.2 1.9 collective-permute-start.35
  199.3 5.7 %collective-permute-start.36 = (bf16[4,48,2,1,128]{4,2,1,0,3:T(2,128)(2,1)S(1)}, bf16[4,48,2,1,128]{4,2,1,0,3:T(2,128)(2,1)S(1)}, u32[]{:S(2)}, u32[]{:S(2)}) collective-permute-start(bf16[4,48,2,1,128]{4,2,1,0,3:T(2,128)(2,1)S(1)} %squeeze.30), channel_id=1, source_target_pairs={{0,8},{4,12},{8,0},{12,4},{1,9},{5,13},{9,1},{13,5},{2,10},{6,14},... | collective-permute-start | bytes 294920 | tf_op jit(solution)/shard_map/ppermute | solution.py:17
  200.5 5.6 %collective-permute-start.37 = (bf16[4,48,2,1,128]{4,2,1,0,3:T(2,128)(2,1)S(1)}, bf16[4,48,2,1,128]{4,2,1,0,3:T(2,128)(2,1)S(1)}, u32[]{:S(2)}, u32[]{:S(2)}) collective-permute-start(bf16[4,48,2,1,128]{4,2,1,0,3:T(2,128)(2,1)S(1)} %squeeze.31), channel_id=1, source_target_pairs={{0,12},{4,8},{8,4},{12,0},{1,13},{5,9},{9,5},{13,1},{2,14},{6,10},... | collective-permute-start | bytes 294920 | tf_op jit(solution)/shard_map/ppermute | solution.py:17
  213.8 2.4 %collective-permute-start.39 = (bf16[4,48,2,1,128]{4,2,1,0,3:T(2,128)(2,1)S(1)}, bf16[4,48,2,1,128]{4,2,1,0,3:T(2,128)(2,1)S(1)}, u32[]{:S(2)}, u32[]{:S(2)}) collective-permute-start(bf16[4,48,2,1,128]{4,2,1,0,3:T(2,128)(2,1)S(1)} %squeeze.33), channel_id=1, source_target_pairs={{0,4},{4,0},{8,12},{12,8},{1,5},{5,1},{9,13},{13,9},{2,6},{6,2},{1... | collective-permute-start | bytes 294920 | tf_op jit(solution)/shard_map/ppermute | solution.py:17
  214.0 5.7 %collective-permute-start.40 = (bf16[4,48,2,1,128]{4,2,1,0,3:T(2,128)(2,1)S(1)}, bf16[4,48,2,1,128]{4,2,1,0,3:T(2,128)(2,1)S(1)}, u32[]{:S(2)}, u32[]{:S(2)}) collective-permute-start(bf16[4,48,2,1,128]{4,2,1,0,3:T(2,128)(2,1)S(1)} %squeeze.34), channel_id=1, source_target_pairs={{0,8},{4,12},{8,0},{12,4},{1,9},{5,13},{9,1},{13,5},{2,10},{6,14},... | collective-permute-start | bytes 294920 | tf_op jit(solution)/shard_map/ppermute | solution.py:17
  215.4 5.6 %collective-permute-start.41 = (bf16[4,48,2,1,128]{4,2,1,0,3:T(2,128)(2,1)S(1)}, bf16[4,48,2,1,128]{4,2,1,0,3:T(2,128)(2,1)S(1)}, u32[]{:S(2)}, u32[]{:S(2)}) collective-permute-start(bf16[4,48,2,1,128]{4,2,1,0,3:T(2,128)(2,1)S(1)} %squeeze.35), channel_id=1, source_target_pairs={{0,12},{4,8},{8,4},{12,0},{1,13},{5,9},{9,5},{13,1},{2,14},{6,10},... | collective-permute-start | bytes 294920 | tf_op jit(solution)/shard_map/ppermute | solution.py:17
  (12 other events, 28.9 us)

commit v17 on v15

--- a/solution.py
+++ b/solution.py
@@ -100,20 +100,20 @@
             first[3 * tall :, :] = sent[:, width:].astype(first.dtype)
 
 
+def term_shapes(depth, width, all_direct):
+    direct, wide, narrow = depth if all_direct else depth // 3 * 2, jnp.float32, jnp.bfloat16
+    shapes = [((direct, width), t) for t in (wide, narrow, narrow)]
+    shapes = shapes + [((2 * depth - direct, width), narrow)]
+    if not all_direct:
+        shapes = shapes + [((depth // 3, 2 * width), wide)]
+    return [jax.ShapeDtypeStruct(*shape) for shape in shapes]
+
+
 def product_terms(choice, weight, near, far, all_direct):
     depth, rows = weight.shape
     columns = near.shape[1]
-    width, tall = columns // 2, depth // 3
-    direct = depth if all_direct else 2 * tall
-    wide, narrow = jnp.float32, jnp.bfloat16
-    shapes = [
-        jax.ShapeDtypeStruct((direct, width), wide),
-        jax.ShapeDtypeStruct((direct, width), narrow),
-        jax.ShapeDtypeStruct((direct, width), narrow),
-        jax.ShapeDtypeStruct((2 * depth - direct, width), narrow),
-    ]
-    if not all_direct:
-        shapes = shapes + [jax.ShapeDtypeStruct((tall, columns), wide)]
+    tall = depth // 3
+    shapes = term_shapes(depth, columns // 2, all_direct)
     whole = [pl.BlockSpec(array.shape, lambda i, choice: (0, 0)) for array in (near, *shapes)]
     return pl.pallas_call(
         terms_body,
@@ -127,10 +127,18 @@
         compiler_params=pltpu.CompilerParams(vmem_limit_bytes=32 * 1024 * 1024),
         cost_estimate=pl.CostEstimate(
             flops=4 * depth * rows * columns,
-            bytes_accessed=2 * depth * rows + 4 * rows * columns + 10 * depth * width,
+            bytes_accessed=2 * depth * rows + 4 * rows * columns + 5 * depth * columns,
             transcendentals=0,
         ),
     )(choice, weight, near, far)
+
+
+def blank_arrays(shapes):
+    return pl.pallas_call(
+        lambda *refs: None,
+        out_shape=shapes,
+        out_specs=[pl.BlockSpec(memory_space=pl.ANY)] * len(shapes),
+    )()
 
 
 def product_plan(
@@ -214,9 +222,10 @@
     selector = jnp.einsum("rd,rjs->djs", owned_by, matched.astype(jnp.float32))
     selector = selector.astype(jnp.bfloat16).reshape(4 * most_tiles, tile_slots)
 
+    turned = [turn_of // stride % 2 == 1 for stride in (1, 2)]
+
     def rolled(rows, shifted, stride):
-        odd = (turn_of // stride % 2 == 1)[:, None, None]
-        return jnp.where(odd, shifted, rows)
+        return jnp.where(turned[stride - 1][:, None, None], shifted, rows)
 
     def outgoing(rows):
         picked = add_columns(selector, rows.reshape(tile_slots, -1)).astype(jnp.bfloat16)
@@ -232,42 +241,51 @@
         return jnp.stack(ranked, axis=1)
 
     column, half = group * 2 * head_dim, kv_weight.shape[0] // 2
-    key_mine = lax.dynamic_slice_in_dim(kv_weight, column, head_dim, axis=1)
-    value_mine = lax.dynamic_slice_in_dim(kv_weight, column + head_dim, head_dim, axis=1)
-    stays = lax.dynamic_slice_in_dim(value_mine, tile // 2 * half, half, axis=0)
-    leaves = lax.dynamic_slice_in_dim(value_mine, half - tile // 2 * half, half, axis=0)
+
+    def halves(part):
+        mine = lax.dynamic_slice_in_dim(kv_weight, column + part * head_dim, head_dim, axis=1)
+        ours = lax.dynamic_slice_in_dim(mine, tile // 2 * half, half, axis=0)
+        return ours, lax.dynamic_slice_in_dim(mine, half - tile // 2 * half, half, axis=0)
+
+    def to_planes(stays, comes):
+        pieces = []
+        for j in range(2):
+            piece = jnp.where(tile // 2 == (head // 2) ^ j, stays, comes)
+            pieces.append(
+                moved(piece, lambda t, h: (t // 2 * 2 + outer_core(h), t % 2 + 2 * ((h // 2) ^ j)))
+            )
+        return pieces
+
+    key_stays, key_leaves = halves(0)
     bias_rows = moved(proj_bias, lambda t, h: (h, t))
-    key_block = moved(key_mine, lambda t, h: (h // 2 * 2 + outer_core(h), t))
-    comes = swapped(leaves, "tile", 2)
-    no_terms = tuple(
-        jnp.full((depth, width), once + k, dtype)
-        for k, dtype in enumerate((jnp.float32, jnp.bfloat16, jnp.bfloat16, jnp.bfloat16))
-    )
-    no_tokens = tuple(
-        jnp.full((tile_slots, shard_len, 2 * width), once + k, jnp.bfloat16) for k in range(2)
-    )
-    bias_rows, key_block, comes, stays, once, feature_parts, no_terms, no_tokens = step(
-        (bias_rows, key_block, comes, stays, once, feature_parts, no_terms, no_tokens)
-    )
-
-    value_pieces = []
-    for j in range(2):
-        piece = jnp.where(tile // 2 == (head // 2) ^ j, stays, comes)
-        value_pieces.append(
-            moved(piece, lambda t, h: (t // 2 * 2 + outer_core(h), t % 2 + 2 * ((h // 2) ^ j)))
-        )
-    key_other = swapped(key_block, "tile", 2)
+    key_stays, key_comes, bias_rows = step((key_stays, swapped(key_leaves, "tile", 2), bias_rows))
+
+    value_stays, value_leaves = halves(1)
+    tokens = jax.ShapeDtypeStruct((tile_slots, shard_len, 2 * width), jnp.bfloat16)
+    shapes = term_shapes(depth, width, True) + [tokens, tokens]
+    *no_terms, no_keys, no_values = blank_arrays(shapes)
     bias_part = add_columns(bias_rows[None], kv_weight)
-    value_pieces, key_block, key_other, bias_part = step(
-        (value_pieces, key_block, key_other, bias_part)
-    )
-
-    key_near = put_first(tile // 2 == head // 2, key_block, key_other, 1)
-    value_half = jnp.concatenate(value_pieces, axis=1)
-    key_near, value_half = step((key_near, value_half))
+    key_pieces, value_stays, value_comes, bias_part, once = step(
+        (
+            to_planes(key_stays, key_comes),
+            value_stays,
+            swapped(value_leaves, "tile", 2),
+            bias_part,
+            once,
+        )
+    )
+
+    key_half = jnp.concatenate(key_pieces, axis=1)
+    value_pieces = to_planes(value_stays, value_comes)
+    key_half, key_other, feature_parts = step(
+        (key_half, swapped(key_half, "tile", 2), feature_parts)
+    )
+
+    key_near = step(put_first(first_chip, key_half, key_other, 0))
     terms = products(key_near, swapped(key_near, "tile", 1), False)
     bias_part = bias_part + swapped(bias_part, "tile", 1)
-    terms, value_half, bias_part = step((terms, value_half, bias_part))
+    terms, value_pieces, bias_part = step((terms, value_pieces, bias_part))
+    value_half = jnp.concatenate(value_pieces, axis=1)
 
     def values_terms(given):
         value_half, bias_part = given
@@ -276,7 +294,7 @@
         terms = products(near, swapped(near, "tile", 1), True)
         return (other, bias_other), (terms, bias_part + bias_other)
 
-    empty = no_terms, bias_part
+    empty = tuple(no_terms), bias_part
     own, second, mirror, first, kept_rest = terms
     second, mirror, first, (value_terms, bias_part) = step(
         (
@@ -291,9 +309,9 @@
     direct = 2 * rest
     arrived = jnp.concatenate([first[direct : 3 * rest], first[3 * rest :]], axis=1)
     pair = plus(kept_rest, arrived)
-    pair, mirrored, value_terms = step(
-        (pair, over_middle(pair[:, width:].astype(jnp.bfloat16)), value_terms)
-    )
+    pair = step(pair)
+    mirrored = over_middle(pair[:, width:].astype(jnp.bfloat16))
+    pair, mirrored, value_terms = step((pair, mirrored, value_terms))
     blocks = [plus(own, second, mirror, first[:direct]), plus(pair[:, :width], mirrored)]
     own = jnp.concatenate([block.astype(jnp.bfloat16) for block in blocks], axis=0)
 
@@ -314,7 +332,11 @@
 
     def keys_product(own):
         across_x, across_y = step((swapped(own, "tile", 2), swapped(own, "groups", 1)))
-        return across_x, rest_of_plane((own, across_x, across_y), 0)
+        rows_0 = step(both_heads(own, across_y))
+        diagonal, rows_1 = step((swapped(across_y, "tile", 2), swapped(rows_0, "tile", 1)))
+        rows_2 = step(both_heads(across_x, diagonal))
+        rows = [rows_0, rows_1, rows_2, swapped(rows_2, "tile", 1)]
+        return across_x, finish(times_features(rows, feature_parts), 0)
 
     value_own, second, mirror, first = value_terms
     second, mirror, first, keys = step(
@@ -322,7 +344,7 @@
             swapped(second, "head", 2),
             over_middle(mirror),
             to_neighbour(first),
-            in_loop(keys_product, own, no_tokens[0]),
+            in_loop(keys_product, own, no_keys),
         )
     )
     own = plus(value_own, second, mirror, first).astype(jnp.bfloat16)
@@ -336,7 +358,7 @@
         return (across_y, own, across_x), rest_of_plane(given, 1)
 
     keys = step(rolled(keys, shifted, 1))
-    values = in_loop(values_product, (own, across_x, across_y), no_tokens[1])
+    values = in_loop(values_product, (own, across_x, across_y), no_values)
     shifted, values = step((shifted_2(keys, "head", 2), values))
 
     picked = outgoing(rolled(keys, shifted, 2))

time: 232 us -> 222 us (0.957)
  local copies, waits for them, and re-layouts: 30.3 us -> 22.9 us
  waiting for transfers between devices: 105 us -> 99 us
  starting transfers between devices: 54.7 us -> 57.2 us
    ppermute x32, starting transfers between devices: 46.2 us -> 34.2 us  [swapped(): lax.ppermute(shard, axis, [(i, i ^ bit) for i in range(lax.axis_size(axis...]
    ppermute x4, starting transfers between devices: 4.39 us -> 14 us  [shifted_2(): lax.ppermute(shard, axis, [(i, (i + by) % count) for i in range(count)])]
    ppermute x32, waiting for transfers between devices: 73.1 us -> 63.9 us  [swapped(): lax.ppermute(shard, axis, [(i, i ^ bit) for i in range(lax.axis_size(axis...]
    ppermute x4 -> x5, waiting for transfers between devices: 9.03 us -> 14.5 us  [moved(): return lax.ppermute(shard, ('tile', 'head'), pairs)]
    broadcast_in_dim x6 -> x0, local copies, waits for them, and re-layouts: 5.06 us -> none  [the longest x4 3.58 us: product_plan(): jnp.full((depth, width), once + k, dtype)]
    ppermute x4 -> x5, starting transfers between devices: 4.12 us -> 9.02 us  [moved(): return lax.ppermute(shard, ('tile', 'head'), pairs)]
    while x23 -> x20, local copies, waits for them, and re-layouts: 6.72 us -> 4.67 us
  transfers between devices with their start and end apart: 40 -> 41, of which waited for: 23 -> 18; matrix products, arithmetic and copies ran while one was open for 13% -> 13% of each run, Pallas kernels for 3% -> 7%
where the time goes in v17:
time: 222 us; the launch traced here: 221 us
  waiting for transfers between devices  99 us (45%)
  starting transfers between devices  57.2 us (26%)
  local copies, waits for them, and re-layouts  22.9 us (10%)
  Pallas kernels  15.7 us (7%)
  other arithmetic  14.9 us (7%)
  matrix products  9.94 us (4%)
    ppermute x32, waiting for transfers between devices, swapped(): lax.ppermute(shard, axis, [(i, i ^ bit) for i in range(lax.axis_size(axis...  63.9 us
    ppermute x32, starting transfers between devices, swapped(): lax.ppermute(shard, axis, [(i, i ^ bit) for i in range(lax.axis_size(axis...  34.2 us
    ppermute x4, waiting for transfers between devices, shifted_2(): lax.ppermute(shard, axis, [(i, (i + by) % count) for i in range(count)])  20.6 us
    pallas_call x2, Pallas kernels, product_terms(): pl.pallas_call(terms_body, out_shape=shapes, grid_spec=pltpu.PrefetchScal...  15.7 us
    ppermute x5, waiting for transfers between devices, moved(): return lax.ppermute(shard, ('tile', 'head'), pairs)  14.5 us
    ppermute x4, starting transfers between devices, shifted_2(): lax.ppermute(shard, axis, [(i, (i + by) % count) for i in range(count)])  14 us
    dot_general x11, matrix products, add_columns(): return jnp.dot(operand, portion, preferred_element_type=jnp.float32)  9.75 us
    ppermute x5, starting transfers between devices, moved(): return lax.ppermute(shard, ('tile', 'head'), pairs)  9.02 us
  transfers between devices with their start and end apart: 41, of which 18 were waited for; matrix products, arithmetic and copies ran while one was open for 13% of the time, Pallas kernels for 7%

profile of v17, /device:TPU:0, one launch (start us, length us, event | category | flops | bytes accessed | tf_op | source)
XLA Modules:
  0.0 221.2 jit_solution(13587485599280283539)
XLA Ops:
  0.0 3.0 %fusion.23 = (bf16[1024,128]{1,0:T(8,128)(2,1)S(1)}, bf16[1024,128]{1,0:T(8,128)(2,1)}, bf16[1024,128]{1,0:T(8,128)(2,1)S(1)}, bf16[1024,128]{1,0:T(8,128)(2,1)S(1)}) fusion(bf16[2048,512]{1,0:T(8,128)(2,1)} %param.17, s32[]{:T(128)S(6)} %select_n.304, s32[]{:T(128)S(6)} %select_n.309, s32[]{:T(128)S(6)} %select_n.300, s32[]{:T(128)S(6)} %select_n.302), kind=kLoop, calls=%fused_computation.124 | loop fusion | bytes 2097168 | tf_op jit(solution)/shard_map/dynamic_slice | solution.py:248
  3.0 2.9 %collective-permute-start.12 = (bf16[1024,128]{1,0:T(8,128)(2,1)S(1)}, bf16[1024,128]{1,0:T(8,128)(2,1)S(1)}, u32[]{:S(2)}, u32[]{:S(2)}) collective-permute-start(bf16[1024,128]{1,0:T(8,128)(2,1)S(1)} %get-tuple-element.585), channel_id=1, source_target_pairs={{0,8},{4,12},{8,0},{12,4},{1,9},{5,13},{9,1},{13,5},{2,10},{6,14},... | collective-permute-start | bytes 786440 | tf_op jit(solution)/shard_map/ppermute | solution.py:17
  6.0 1.3 collective-permute-start.13
  7.3 4.7 %collective-permute-start.16 = (bf16[1024,128]{1,0:T(8,128)(2,1)S(1)}, bf16[1024,128]{1,0:T(8,128)(2,1)S(1)}, u32[]{:S(2)}, u32[]{:S(2)}) collective-permute-start(bf16[1024,128]{1,0:T(8,128)(2,1)S(1)} %get-tuple-element.583), channel_id=1, source_target_pairs={{0,8},{4,12},{8,0},{12,4},{1,9},{5,13},{9,1},{13,5},{2,10},{6,14},... | collective-permute-start | bytes 786440 | tf_op jit(solution)/shard_map/ppermute | solution.py:17
  14.0 4.3 %collective-permute-start.15 = (bf16[1024,128]{1,0:T(8,128)(2,1)S(1)}, bf16[1024,128]{1,0:T(8,128)(2,1)S(1)}, u32[]{:S(2)}, u32[]{:S(2)}) collective-permute-start(bf16[1024,128]{1,0:T(8,128)(2,1)S(1)} %get-tuple-element.593), channel_id=1, source_target_pairs={{0,2},{1,6},{2,4},{3,0},{4,3},{5,7},{6,5},{7,1},{8,10},{9,14},{10,... | collective-permute-start | bytes 786440 | tf_op jit(solution)/shard_map/ppermute | solution.py:165
  18.8 10.8 %collective-permute-done.15 = bf16[1024,128]{1,0:T(8,128)(2,1)S(1)} collective-permute-done((bf16[1024,128]{1,0:T(8,128)(2,1)S(1)}, bf16[1024,128]{1,0:T(8,128)(2,1)S(1)}, u32[]{:S(2)}, u32[]{:S(2)}) %collective-permute-start.15) | collective-permute-done | bytes 262176 | tf_op jit(solution)/shard_map/ppermute | solution.py:165
  30.8 7.1 %constant_dynamic-slice_fusion = (bf16[576,1920]{1,0:T(8,128)(2,1)}, bf16[576,1920]{1,0:T(8,128)(2,1)}, bf16[576,1920]{1,0:T(8,128)(2,1)}, bf16[576,1920]{1,0:T(8,128)(2,1)}) fusion(bf16[576,7680]{1,0:T(8,128)(2,1)} %bitcast.134, s32[]{:T(128)S(6)} %select_n.313, s32[]{:T(128)S(6)} %select_n.312, s32[]{:T(128)S(6)} %select_n.311, s32[]{:T(128)S(6)} %select_n.310), kind=kLoop, calls=%fused_computation.115 | loop fusion | bytes 17694736 | tf_op jit(solution)/shard_map/dynamic_slice | solution.py:171
  38.0 5.8 %collective-permute-done.17 = bf16[1024,256]{1,0:T(8,128)(2,1)S(1)} collective-permute-done((bf16[1024,256]{1,0:T(8,128)(2,1)S(1)}, bf16[1024,256]{1,0:T(8,128)(2,1)S(1)}, u32[]{:S(2)}, u32[]{:S(2)}) %collective-permute-start.17) | collective-permute-done | bytes 524320 | tf_op jit(solution)/shard_map/ppermute | solution.py:17
  45.5 2.0 collective-permute-start.20
  47.6 7.7 %shard_map.82 = (f32[1280,128]{1,0:T(8,128)S(1)}, bf16[1280,128]{1,0:T(8,128)(2,1)}, bf16[1280,128]{1,0:T(8,128)(2,1)}, bf16[2560,128]{1,0:T(8,128)(2,1)}, f32[640,256]{1,0:T(8,128)S(1)}) custom-call(s32[1]{0:T(128)} %bitcast.11.choice, bf16[1920,2048]{1,0:T(8,128)(2,1)} %weight.1, bf16[2048,256]{1,0:T(8,128)(2,1)S(1)} %pad_maximum_fusion.7.near, ...), custom_call_target="tpu_custom_call" | custom-call | flops 4026531840 | bytes 12419072 | tf_op jit(solution)/shard_map/pallas_call | solution.py:118
  55.3 3.7 %collective-permute-done.20 = bf16[1024,128]{1,0:T(8,128)(2,1)S(1)} collective-permute-done((bf16[1024,128]{1,0:T(8,128)(2,1)S(1)}, bf16[1024,128]{1,0:T(8,128)(2,1)S(1)}, u32[]{:S(2)}, u32[]{:S(2)}) %collective-permute-start.20) | collective-permute-done | bytes 262176 | tf_op jit(solution)/shard_map/ppermute | solution.py:165
  61.1 2.8 %collective-permute-start.23 = (bf16[1280,128]{1,0:T(8,128)(2,1)}, bf16[1280,128]{1,0:T(8,128)(2,1)}, u32[]{:S(2)}, u32[]{:S(2)}) collective-permute-start(bf16[1280,128]{1,0:T(8,128)(2,1)} %get-tuple-element.430), channel_id=1, source_target_pairs={{0,3},{1,2},{2,1},{3,0},{4,7},{5,6},{6,5},{7,4},{8,11},{9,10},{10,... | collective-permute-start | bytes 983048 | tf_op jit(solution)/shard_map/ppermute | solution.py:17
  64.8 26.8 %while.54 = (s32[]{:T(128)}, bf16[1024,256]{1,0:T(8,128)(2,1)}, f32[1,512]{1,0:T(1,128)S(1)}, f32[1920,128]{1,0:T(8,128)}, bf16[1920,128]{1,0:T(8,128)(2,1)}, /*...) while((s32[]{:T(128)}, bf16[1024,256]{1,0:T(8,128)(2,1)}, ...), condition=%wide.region_3.4_spmd, body=%wide.region_2.3_spmd.sunk | while | flops 4029153792 | bytes 23972084 | solution.py:203
  66.5 1.3 collective-permute-start.1
  67.8 11.8 %collective-permute-done.1 = f32[1,512]{1,0:T(1,128)S(1)} collective-permute-done((f32[1,512]{1,0:T(1,128)S(1)}, f32[1,512]{1,0:T(1,128)S(1)}, u32[]{:S(2)}, u32[]{:S(2)}) %collective-permute-start.1) | collective-permute-done | bytes 2080 | tf_op jit(solution)/shard_map/while/body/ppermute | solution.py:17
  81.5 2.1 collective-permute-done.2.far
  83.6 8.0 %body.1 = (f32[1920,128]{1,0:T(8,128)}, bf16[1920,128]{1,0:T(8,128)(2,1)}, bf16[1920,128]{1,0:T(8,128)(2,1)}, bf16[1920,128]{1,0:T(8,128)(2,1)}) custom-call(s32[1]{0:T(128)} %get-tuple-element.927.choice, bf16[1920,2048]{1,0:T(8,128)(2,1)} %get-tuple-element.928.weight, bf16[2048,256]{1,0:T(8,128)(2,1)S(1)} %pad_maximum_fusion.18.near, ...), custom_call_target="tpu_custom_call" | custom-call | flops 4026531840 | bytes 12419072 | tf_op jit(solution)/shard_map/while/body/pallas_call | solution.py:118
  92.8 1.9 collective-permute-start.25
  94.6 1.3 add_convert_fusion.1
  96.0 5.0 %collective-permute-done.25 = bf16[640,128]{1,0:T(8,128)(2,1)S(1)} collective-permute-done((bf16[640,128]{1,0:T(8,128)(2,1)S(1)}, bf16[640,128]{1,0:T(8,128)(2,1)S(1)}, u32[]{:S(2)}, u32[]{:S(2)}) %collective-permute-start.25) | collective-permute-done | bytes 163872 | tf_op jit(solution)/shard_map/ppermute | solution.py:17
  101.0 3.1 %collective-permute-start.26 = (bf16[1920,128]{1,0:T(8,128)(2,1)}, bf16[1920,128]{1,0:T(8,128)(2,1)}, u32[]{:S(2)}, u32[]{:S(2)}) collective-permute-start(bf16[1920,128]{1,0:T(8,128)(2,1)} %get-tuple-element.450), channel_id=1, source_target_pairs={{0,2},{1,3},{2,0},{3,1},{4,6},{5,7},{6,4},{7,5},{8,10},{9,11},{10,... | collective-permute-start | bytes 1474568 | tf_op jit(solution)/shard_map/ppermute | solution.py:17
  104.1 1.3 collective-permute-start.27
  105.5 34.2 %while.55 = (s32[]{:T(128)}, bf16[1920,128]{1,0:T(8,128)(2,1)S(1)}, bf16[12,48,256]{2,1,0:T(8,128)(2,1)}, s32[]{:T(128)}, pred[]{:T(512)}, /*index=5*/bf16[576,1...) while((s32[]{:T(128)}, bf16[1920,128]{1,0:T(8,128)(2,1)S(1)}, ...), condition=%wide.region_7.8_spmd, body=%wide.region_4.7_spmd.sunk | while | flops 2271905024 | bytes 76995496 | solution.py:203
  105.5 1.5 collective-permute-start.3
  107.1 1.4 collective-permute-start.4
  108.4 8.5 %collective-permute-done.3 = bf16[1920,128]{1,0:T(8,128)(2,1)S(1)} collective-permute-done((bf16[1920,128]{1,0:T(8,128)(2,1)S(1)}, bf16[1920,128]{1,0:T(8,128)(2,1)S(1)}, u32[]{:S(2)}, u32[]{:S(2)}) %collective-permute-start.3) | collective-permute-done | bytes 491552 | tf_op jit(solution)/shard_map/while/body/ppermute | solution.py:17
  119.0 12.9 %collective-permute-done.5 = bf16[1920,128]{1,0:T(8,128)(2,1)S(1)} collective-permute-done((bf16[1920,128]{1,0:T(8,128)(2,1)S(1)}, bf16[1920,128]{1,0:T(8,128)(2,1)S(1)}, u32[]{:S(2)}, u32[]{:S(2)}) %collective-permute-start.5) | collective-permute-done | bytes 491552 | tf_op jit(solution)/shard_map/while/body/ppermute | solution.py:17
  133.9 2.1 convolution_add_fusion.10
  139.7 1.6 add_convert_fusion
  142.0 1.4 collective-permute-start.31
  143.6 8.5 %collective-permute-start.29 = (bf16[12,48,256]{2,1,0:T(8,128)(2,1)S(1)}, bf16[12,48,256]{2,1,0:T(8,128)(2,1)S(1)}, u32[]{:S(2)}, u32[]{:S(2)}) collective-permute-start(bf16[12,48,256]{2,1,0:T(8,128)(2,1)S(1)} %copy-done.12), channel_id=1, source_target_pairs={{0,1},{1,2},{2,3},{3,0},{4,5},{5,6},{6,7},{7,4},{8,9},{9,10},{10,1... | collective-permute-start | bytes 884744 | tf_op jit(solution)/shard_map/ppermute | solution.py:13
  152.2 5.6 %collective-permute-done.29 = bf16[12,48,256]{2,1,0:T(8,128)(2,1)S(1)} collective-permute-done((bf16[12,48,256]{2,1,0:T(8,128)(2,1)S(1)}, bf16[12,48,256]{2,1,0:T(8,128)(2,1)S(1)}, u32[]{:S(2)}, u32[]{:S(2)}) %collective-permute-start.29) | collective-permute-done | bytes 294944 | tf_op jit(solution)/shard_map/ppermute | solution.py:13
  158.6 4.3 %collective-permute-start.32 = (bf16[12,48,256]{2,1,0:T(8,128)(2,1)}, bf16[12,48,256]{2,1,0:T(8,128)(2,1)}, u32[]{:S(2)}, u32[]{:S(2)}) collective-permute-start(bf16[12,48,256]{2,1,0:T(8,128)(2,1)} %broadcast_select_fusion.15), channel_id=1, source_target_pairs={{0,2},{1,3},{2,0},{3,1},{4,6},{5,7},{6,4},{7,5},{8,10},{9,11},{10,... | collective-permute-start | bytes 884744 | tf_op jit(solution)/shard_map/ppermute | solution.py:13
  163.0 19.4 %while.56 = (s32[]{:T(128)}, bf16[1920,128]{1,0:T(8,128)(2,1)S(1)}, bf16[1920,128]{1,0:T(8,128)(2,1)S(1)}, bf16[1920,128]{1,0:T(8,128)(2,1)S(1)}, bf16[12,48,256...) while((s32[]{:T(128)}, bf16[1920,128]{1,0:T(8,128)(2,1)S(1)}, ...), condition=%wide.region_9.10_spmd, body=%wide.region_8.9_spmd.sunk | while | flops 2271166464 | bytes 77368712 | solution.py:203
  165.4 1.4 collective-permute-start.8
  166.8 5.8 %collective-permute-done.9 = bf16[960,128]{1,0:T(8,128)(2,1)S(1)} collective-permute-done((bf16[960,128]{1,0:T(8,128)(2,1)}, bf16[960,128]{1,0:T(8,128)(2,1)S(1)}, u32[]{:S(2)}, u32[]{:S(2)}) %collective-permute-start.9) | collective-permute-done | bytes 245792 | tf_op jit(solution)/shard_map/while/body/ppermute | solution.py:17
  174.0 1.3 copy-done.8
  176.9 2.1 convolution_add_fusion.12
  182.3 1.2 broadcast_select_fusion.13
  185.6 8.3 %collective-permute-done.33 = bf16[12,48,256]{2,1,0:T(8,128)(2,1)S(1)} collective-permute-done((bf16[12,48,256]{2,1,0:T(8,128)(2,1)S(1)}, bf16[12,48,256]{2,1,0:T(8,128)(2,1)S(1)}, u32[]{:S(2)}, u32[]{:S(2)}) %collective-permute-start.33) | collective-permute-done | bytes 294944 | tf_op jit(solution)/shard_map/ppermute | solution.py:13
  194.2 1.4 collective-permute-start.35
  196.1 3.8 %collective-permute-done.35 = bf16[4,48,2,1,128]{4,2,1,0,3:T(2,128)(2,1)S(1)} collective-permute-done((bf16[4,48,2,1,128]{4,2,1,0,3:T(2,128)(2,1)S(1)}, bf16[4,48,2,1,128]{4,2,1,0,3:T(2,128)(2,1)S(1)}, u32[]{:S(2)}, u32[]{:S(2)}) %collective-permute-start.35) | collective-permute-done | bytes 98336 | tf_op jit(solution)/shard_map/ppermute | solution.py:17
  199.9 1.2 collective-permute-done.36
  201.1 6.7 %collective-permute-done.37 = bf16[12,48,256]{2,1,0:T(8,128)(2,1)S(1)} collective-permute-done((bf16[12,48,256]{2,1,0:T(8,128)(2,1)S(1)}, bf16[12,48,256]{2,1,0:T(8,128)(2,1)S(1)}, u32[]{:S(2)}, u32[]{:S(2)}) %collective-permute-start.37) | collective-permute-done | bytes 294944 | tf_op jit(solution)/shard_map/ppermute | solution.py:13
  208.8 1.4 collective-permute-start.39
  211.0 3.4 %collective-permute-done.39 = bf16[4,48,2,1,128]{4,2,1,0,3:T(2,128)(2,1)S(1)} collective-permute-done((bf16[4,48,2,1,128]{4,2,1,0,3:T(2,128)(2,1)S(1)}, bf16[4,48,2,1,128]{4,2,1,0,3:T(2,128)(2,1)S(1)}, u32[]{:S(2)}, u32[]{:S(2)}) %collective-permute-start.39) | collective-permute-done | bytes 98336 | tf_op jit(solution)/shard_map/ppermute | solution.py:17
  214.4 1.3 collective-permute-done.40
  219.1 2.1 copy.19
  (172 shorter events, 38.3 us)
Async XLA Ops:
  0.0 18.4 %copy-start = (bf16[2048,512]{1,0:T(8,128)(2,1)S(1)}, bf16[2048,512]{1,0:T(8,128)(2,1)}, u32[]{:S(2)}) copy-start(bf16[2048,512]{1,0:T(8,128)(2,1)} %param.17) | copy-start | bytes 6291460
  0.0 12.0 %copy-start.18 = (s32[4]{0:T(128)S(1)}, s32[4]{0:T(128)}, u32[]{:S(2)}) copy-start(s32[4]{0:T(128)} %param.20) | copy-start | bytes 52
  3.0 10.3 %collective-permute-start.12 = (bf16[1024,128]{1,0:T(8,128)(2,1)S(1)}, bf16[1024,128]{1,0:T(8,128)(2,1)S(1)}, u32[]{:S(2)}, u32[]{:S(2)}) collective-permute-start(bf16[1024,128]{1,0:T(8,128)(2,1)S(1)} %get-tuple-element.585), channel_id=1, source_target_pairs={{0,8},{4,12},{8,0},{12,4},{1,9},{5,13},{9,1},{13,5},{2,10},{6,14},... | collective-permute-start | bytes 786440 | tf_op jit(solution)/shard_map/ppermute | solution.py:17
  6.0 7.3 %collective-permute-start.13 = (bf16[2048]{0:T(1024)(128)(2,1)}, bf16[2048]{0:T(1024)(128)(2,1)S(1)}, u32[]{:S(2)}, u32[]{:S(2)}) collective-permute-start(bf16[2048]{0:T(1024)(128)(2,1)} %param.16), channel_id=1, source_target_pairs={{0,0},{1,4},{2,8},{3,12},{4,1},{5,5},{6,9},{7,13},{8,2},{9,6},{10,... | collective-permute-start | bytes 12296 | tf_op jit(solution)/shard_map/ppermute | solution.py:165
  7.3 11.5 %collective-permute-start.16 = (bf16[1024,128]{1,0:T(8,128)(2,1)S(1)}, bf16[1024,128]{1,0:T(8,128)(2,1)S(1)}, u32[]{:S(2)}, u32[]{:S(2)}) collective-permute-start(bf16[1024,128]{1,0:T(8,128)(2,1)S(1)} %get-tuple-element.583), channel_id=1, source_target_pairs={{0,8},{4,12},{8,0},{12,4},{1,9},{5,13},{9,1},{13,5},{2,10},{6,14},... | collective-permute-start | bytes 786440 | tf_op jit(solution)/shard_map/ppermute | solution.py:17
  13.4 5.4 %collective-permute-start.14 = (bf16[1024,128]{1,0:T(8,128)(2,1)S(1)}, bf16[1024,128]{1,0:T(8,128)(2,1)S(1)}, u32[]{:S(2)}, u32[]{:S(2)}) collective-permute-start(bf16[1024,128]{1,0:T(8,128)(2,1)S(1)} %get-tuple-element.594), channel_id=1, source_target_pairs={{0,0},{1,4},{2,6},{3,2},{4,1},{5,5},{6,7},{7,3},{8,8},{9,12},{10,1... | collective-permute-start | bytes 786440 | tf_op jit(solution)/shard_map/ppermute | solution.py:165
  14.0 15.5 %collective-permute-start.15 = (bf16[1024,128]{1,0:T(8,128)(2,1)S(1)}, bf16[1024,128]{1,0:T(8,128)(2,1)S(1)}, u32[]{:S(2)}, u32[]{:S(2)}) collective-permute-start(bf16[1024,128]{1,0:T(8,128)(2,1)S(1)} %get-tuple-element.593), channel_id=1, source_target_pairs={{0,2},{1,6},{2,4},{3,0},{4,3},{5,7},{6,5},{7,1},{8,10},{9,14},{10,... | collective-permute-start | bytes 786440 | tf_op jit(solution)/shard_map/ppermute | solution.py:165
  18.8 19.2 %copy-start.13 = (bf16[1024,128]{1,0:T(8,128)(2,1)}, bf16[1024,128]{1,0:T(8,128)(2,1)S(1)}, u32[]{:S(2)}) copy-start(bf16[1024,128]{1,0:T(8,128)(2,1)S(1)} %collective-permute-done.16) | copy-start | bytes 786436
  29.7 14.1 %collective-permute-start.17 = (bf16[1024,256]{1,0:T(8,128)(2,1)S(1)}, bf16[1024,256]{1,0:T(8,128)(2,1)S(1)}, u32[]{:S(2)}, u32[]{:S(2)}) collective-permute-start(bf16[1024,256]{1,0:T(8,128)(2,1)S(1)} %constant_dynamic-update-slice_fusion.2), channel_id=1, source_target_pairs={{0,8},{4,12},{8,0},{12,4},{1,9},{5,13},{9,1},{13,5},{2,10},{6,14},... | collective-permute-start | bytes 1572872 | tf_op jit(solution)/shard_map/ppermute | solution.py:17
  44.0 3.6 %collective-permute-start.18 = (bf16[2048,256]{1,0:T(8,128)(2,1)S(1)}, bf16[2048,256]{1,0:T(8,128)(2,1)S(1)}, u32[]{:S(2)}, u32[]{:S(2)}) collective-permute-start(bf16[2048,256]{1,0:T(8,128)(2,1)S(1)} %pad_maximum_fusion.7.near), channel_id=1, source_target_pairs={{0,4},{4,0},{8,12},{12,8},{1,5},{5,1},{9,13},{13,9},{2,6},{6,2},{1... | collective-permute-start | bytes 3145736 | tf_op jit(solution)/shard_map/ppermute | solution.py:17
  44.2 3.3 %collective-permute-start.21 = (f32[1,512]{1,0:T(1,128)S(1)}, f32[1,512]{1,0:T(1,128)S(1)}, u32[]{:S(2)}, u32[]{:S(2)}) collective-permute-start(f32[1,512]{1,0:T(1,128)S(1)} %fusion.29), channel_id=1, source_target_pairs={{0,4},{4,0},{8,12},{12,8},{1,5},{5,1},{9,13},{13,9},{2,6},{6,2},{1... | collective-permute-start | bytes 6152 | tf_op jit(solution)/shard_map/ppermute | solution.py:17
  44.9 10.4 %collective-permute-start.19 = (bf16[1024,128]{1,0:T(8,128)(2,1)S(1)}, bf16[1024,128]{1,0:T(8,128)(2,1)S(1)}, u32[]{:S(2)}, u32[]{:S(2)}) collective-permute-start(bf16[1024,128]{1,0:T(8,128)(2,1)S(1)} %get-tuple-element.592), channel_id=1, source_target_pairs={{0,0},{1,4},{2,6},{3,2},{4,1},{5,5},{6,7},{7,3},{8,8},{9,12},{10,1... | collective-permute-start | bytes 786440 | tf_op jit(solution)/shard_map/ppermute | solution.py:165
  45.5 13.4 %collective-permute-start.20 = (bf16[1024,128]{1,0:T(8,128)(2,1)S(1)}, bf16[1024,128]{1,0:T(8,128)(2,1)S(1)}, u32[]{:S(2)}, u32[]{:S(2)}) collective-permute-start(bf16[1024,128]{1,0:T(8,128)(2,1)S(1)} %get-tuple-element.591), channel_id=1, source_target_pairs={{0,2},{1,6},{2,4},{3,0},{4,3},{5,7},{6,5},{7,1},{8,10},{9,14},{10,... | collective-permute-start | bytes 786440 | tf_op jit(solution)/shard_map/ppermute | solution.py:165
  59.5 32.1 %collective-permute-start.24 = (bf16[2560,128]{1,0:T(8,128)(2,1)}, bf16[2560,128]{1,0:T(8,128)(2,1)}, u32[]{:S(2)}, u32[]{:S(2)}) collective-permute-start(bf16[2560,128]{1,0:T(8,128)(2,1)} %get-tuple-element.431), channel_id=1, source_target_pairs={{0,1},{1,0},{2,3},{3,2},{4,5},{5,4},{6,7},{7,6},{8,9},{9,8},{10,11... | collective-permute-start | bytes 1966088 | tf_op jit(solution)/shard_map/ppermute | solution.py:17
  60.0 31.6 %collective-permute-start.22 = (bf16[1280,128]{1,0:T(8,128)(2,1)}, bf16[1280,128]{1,0:T(8,128)(2,1)}, u32[]{:S(2)}, u32[]{:S(2)}) collective-permute-start(bf16[1280,128]{1,0:T(8,128)(2,1)} %get-tuple-element.429), channel_id=1, source_target_pairs={{0,2},{1,3},{2,0},{3,1},{4,6},{5,7},{6,4},{7,5},{8,10},{9,11},{10,... | collective-permute-start | bytes 983048 | tf_op jit(solution)/shard_map/ppermute | solution.py:17
  61.1 30.6 %collective-permute-start.23 = (bf16[1280,128]{1,0:T(8,128)(2,1)}, bf16[1280,128]{1,0:T(8,128)(2,1)}, u32[]{:S(2)}, u32[]{:S(2)}) collective-permute-start(bf16[1280,128]{1,0:T(8,128)(2,1)} %get-tuple-element.430), channel_id=1, source_target_pairs={{0,3},{1,2},{2,1},{3,0},{4,7},{5,6},{6,5},{7,4},{8,11},{9,10},{10,... | collective-permute-start | bytes 983048 | tf_op jit(solution)/shard_map/ppermute | solution.py:17
  65.8 13.9 %collective-permute-start = (bf16[1024,256]{1,0:T(8,128)(2,1)S(1)}, bf16[1024,256]{1,0:T(8,128)(2,1)}, u32[]{:S(2)}, u32[]{:S(2)}) collective-permute-start(bf16[1024,256]{1,0:T(8,128)(2,1)S(1)} %copy.33), channel_id=1, source_target_pairs={{0,8},{4,12},{8,0},{12,4},{1,9},{5,13},{9,1},{13,5},{2,10},{6,14},... | collective-permute-start | bytes 1572872 | tf_op jit(solution)/shard_map/while/body/ppermute | solution.py:17
  66.5 13.1 %collective-permute-start.1 = (f32[1,512]{1,0:T(1,128)S(1)}, f32[1,512]{1,0:T(1,128)S(1)}, u32[]{:S(2)}, u32[]{:S(2)}) collective-permute-start(f32[1,512]{1,0:T(1,128)S(1)} %copy.34), channel_id=1, source_target_pairs={{0,8},{4,12},{8,0},{12,4},{1,9},{5,13},{9,1},{13,5},{2,10},{6,14},... | collective-permute-start | bytes 6152 | tf_op jit(solution)/shard_map/while/body/ppermute | solution.py:17
  80.9 2.7 %collective-permute-start.2 = (bf16[2048,256]{1,0:T(8,128)(2,1)S(1)}, bf16[2048,256]{1,0:T(8,128)(2,1)S(1)}, u32[]{:S(2)}, u32[]{:S(2)}) collective-permute-start(bf16[2048,256]{1,0:T(8,128)(2,1)S(1)} %pad_maximum_fusion.18.near), channel_id=1, source_target_pairs={{0,4},{4,0},{8,12},{12,8},{1,5},{5,1},{9,13},{13,9},{2,6},{6,2},{1... | collective-permute-start | bytes 3145736 | tf_op jit(solution)/shard_map/while/body/ppermute | solution.py:17
  92.7 12.7 %copy-start.15 = (f32[1,512]{1,0:T(1,128)S(1)}, f32[1,512]{1,0:T(1,128)}, u32[]{:S(2)}) copy-start(f32[1,512]{1,0:T(1,128)} %get-tuple-element.463) | copy-start | bytes 6148
  92.7 12.7 %copy-start.16 = (f32[1,128]{1,0:T(1,128)S(1)}, f32[1,128]{1,0:T(1,128)}, u32[]{:S(2)}) copy-start(f32[1,128]{1,0:T(1,128)} %param.18) | copy-start | bytes 1540
  92.8 8.2 %collective-permute-start.25 = (bf16[640,128]{1,0:T(8,128)(2,1)S(1)}, bf16[640,128]{1,0:T(8,128)(2,1)S(1)}, u32[]{:S(2)}, u32[]{:S(2)}) collective-permute-start(bf16[640,128]{1,0:T(8,128)(2,1)S(1)} %slice.147), channel_id=1, source_target_pairs={{0,3},{1,2},{2,1},{3,0},{4,7},{5,6},{6,5},{7,4},{8,11},{9,10},{10,... | collective-permute-start | bytes 491528 | tf_op jit(solution)/shard_map/ppermute | solution.py:17
  101.0 38.7 %collective-permute-start.26 = (bf16[1920,128]{1,0:T(8,128)(2,1)}, bf16[1920,128]{1,0:T(8,128)(2,1)}, u32[]{:S(2)}, u32[]{:S(2)}) collective-permute-start(bf16[1920,128]{1,0:T(8,128)(2,1)} %get-tuple-element.450), channel_id=1, source_target_pairs={{0,2},{1,3},{2,0},{3,1},{4,6},{5,7},{6,4},{7,5},{8,10},{9,11},{10,... | collective-permute-start | bytes 1474568 | tf_op jit(solution)/shard_map/ppermute | solution.py:17
  104.1 35.6 %collective-permute-start.27 = (bf16[1920,128]{1,0:T(8,128)(2,1)}, bf16[1920,128]{1,0:T(8,128)(2,1)}, u32[]{:S(2)}, u32[]{:S(2)}) collective-permute-start(bf16[1920,128]{1,0:T(8,128)(2,1)} %get-tuple-element.451), channel_id=1, source_target_pairs={{0,3},{1,2},{2,1},{3,0},{4,7},{5,6},{6,5},{7,4},{8,11},{9,10},{10,... | collective-permute-start | bytes 1474568 | tf_op jit(solution)/shard_map/ppermute | solution.py:17
  105.4 34.3 %collective-permute-start.28 = (bf16[1920,128]{1,0:T(8,128)(2,1)}, bf16[1920,128]{1,0:T(8,128)(2,1)}, u32[]{:S(2)}, u32[]{:S(2)}) collective-permute-start(bf16[1920,128]{1,0:T(8,128)(2,1)} %get-tuple-element.452), channel_id=1, source_target_pairs={{0,1},{1,0},{2,3},{3,2},{4,5},{5,4},{6,7},{7,6},{8,9},{9,8},{10,11... | collective-permute-start | bytes 1474568 | tf_op jit(solution)/shard_map/ppermute | solution.py:17
  105.5 34.2 %copy-start.10 = (f32[1920,128]{1,0:T(8,128)S(1)}, f32[1920,128]{1,0:T(8,128)}, u32[]{:S(2)}) copy-start(f32[1920,128]{1,0:T(8,128)} %get-tuple-element.466) | copy-start | bytes 2949124
  105.5 11.4 %collective-permute-start.3 = (bf16[1920,128]{1,0:T(8,128)(2,1)S(1)}, bf16[1920,128]{1,0:T(8,128)(2,1)S(1)}, u32[]{:S(2)}, u32[]{:S(2)}) collective-permute-start(bf16[1920,128]{1,0:T(8,128)(2,1)S(1)} %copy.52), channel_id=1, source_target_pairs={{0,8},{4,12},{8,0},{12,4},{1,9},{5,13},{9,1},{13,5},{2,10},{6,14},... | collective-permute-start | bytes 1474568 | tf_op jit(solution)/shard_map/while/body/ppermute | solution.py:17
  107.1 11.0 %collective-permute-start.4 = (bf16[1920,128]{1,0:T(8,128)(2,1)S(1)}, bf16[1920,128]{1,0:T(8,128)(2,1)S(1)}, u32[]{:S(2)}, u32[]{:S(2)}) collective-permute-start(bf16[1920,128]{1,0:T(8,128)(2,1)S(1)} %copy.52), channel_id=1, source_target_pairs={{0,16},{16,0},{1,17},{17,1},{2,18},{18,2},{3,19},{19,3},{4,20},{20... | collective-permute-start | bytes 1474568 | tf_op jit(solution)/shard_map/while/body/ppermute | solution.py:17
  118.2 13.7 %collective-permute-start.6 = (bf16[1920,256]{1,0:T(8,128)(2,1)S(1)}, bf16[1920,256]{1,0:T(8,128)(2,1)}, u32[]{:S(2)}, u32[]{:S(2)}) collective-permute-start(bf16[1920,256]{1,0:T(8,128)(2,1)S(1)} %pad_maximum_fusion.19), channel_id=1, source_target_pairs={{0,4},{4,0},{8,12},{12,8},{1,5},{5,1},{9,13},{13,9},{2,6},{6,2},{1... | collective-permute-start | bytes 2949128 | tf_op jit(solution)/shard_map/while/body/ppermute | solution.py:17
  118.3 13.6 %collective-permute-start.5 = (bf16[1920,128]{1,0:T(8,128)(2,1)S(1)}, bf16[1920,128]{1,0:T(8,128)(2,1)S(1)}, u32[]{:S(2)}, u32[]{:S(2)}) collective-permute-start(bf16[1920,128]{1,0:T(8,128)(2,1)S(1)} %collective-permute-done.4), channel_id=1, source_target_pairs={{0,8},{4,12},{8,0},{12,4},{1,9},{5,13},{9,1},{13,5},{2,10},{6,14},... | collective-permute-start | bytes 1474568 | tf_op jit(solution)/shard_map/while/body/ppermute | solution.py:17
  119.0 13.2 %copy-start.7 = (bf16[576,1920]{1,0:T(8,128)(2,1)S(1)}, bf16[576,1920]{1,0:T(8,128)(2,1)}, u32[]{:S(2)}) copy-start(bf16[576,1920]{1,0:T(8,128)(2,1)} %get-tuple-element.959) | copy-start | bytes 6635524 | tf_op jit(solution)/shard_map/while
  132.1 4.7 %collective-permute-start.7 = (bf16[1920,256]{1,0:T(8,128)(2,1)S(1)}, bf16[1920,256]{1,0:T(8,128)(2,1)S(1)}, u32[]{:S(2)}, u32[]{:S(2)}) collective-permute-start(bf16[1920,256]{1,0:T(8,128)(2,1)S(1)} %pad_maximum_fusion.20), channel_id=1, source_target_pairs={{0,4},{4,0},{8,12},{12,8},{1,5},{5,1},{9,13},{13,9},{2,6},{6,2},{1... | collective-permute-start | bytes 2949128 | tf_op jit(solution)/shard_map/while/body/ppermute | solution.py:17
  141.3 16.5 %collective-permute-start.30 = (bf16[1920,128]{1,0:T(8,128)(2,1)S(1)}, bf16[1920,128]{1,0:T(8,128)(2,1)S(1)}, u32[]{:S(2)}, u32[]{:S(2)}) collective-permute-start(bf16[1920,128]{1,0:T(8,128)(2,1)S(1)} %add_convert_fusion), channel_id=1, source_target_pairs={{0,8},{4,12},{8,0},{12,4},{1,9},{5,13},{9,1},{13,5},{2,10},{6,14},... | collective-permute-start | bytes 1474568 | tf_op jit(solution)/shard_map/ppermute | solution.py:17
  142.0 15.8 %collective-permute-start.31 = (bf16[1920,128]{1,0:T(8,128)(2,1)S(1)}, bf16[1920,128]{1,0:T(8,128)(2,1)S(1)}, u32[]{:S(2)}, u32[]{:S(2)}) collective-permute-start(bf16[1920,128]{1,0:T(8,128)(2,1)S(1)} %add_convert_fusion), channel_id=1, source_target_pairs={{0,16},{16,0},{1,17},{17,1},{2,18},{18,2},{3,19},{19,3},{4,20},{20... | collective-permute-start | bytes 1474568 | tf_op jit(solution)/shard_map/ppermute | solution.py:17
  143.6 14.2 %collective-permute-start.29 = (bf16[12,48,256]{2,1,0:T(8,128)(2,1)S(1)}, bf16[12,48,256]{2,1,0:T(8,128)(2,1)S(1)}, u32[]{:S(2)}, u32[]{:S(2)}) collective-permute-start(bf16[12,48,256]{2,1,0:T(8,128)(2,1)S(1)} %copy-done.12), channel_id=1, source_target_pairs={{0,1},{1,2},{2,3},{3,0},{4,5},{5,6},{6,7},{7,4},{8,9},{9,10},{10,1... | collective-permute-start | bytes 884744 | tf_op jit(solution)/shard_map/ppermute | solution.py:13
  158.6 23.7 %collective-permute-start.32 = (bf16[12,48,256]{2,1,0:T(8,128)(2,1)}, bf16[12,48,256]{2,1,0:T(8,128)(2,1)}, u32[]{:S(2)}, u32[]{:S(2)}) collective-permute-start(bf16[12,48,256]{2,1,0:T(8,128)(2,1)} %broadcast_select_fusion.15), channel_id=1, source_target_pairs={{0,2},{1,3},{2,0},{3,1},{4,6},{5,7},{6,4},{7,5},{8,10},{9,11},{10,... | collective-permute-start | bytes 884744 | tf_op jit(solution)/shard_map/ppermute | solution.py:13
  163.2 10.5 %collective-permute-start.10 = (bf16[1920,256]{1,0:T(8,128)(2,1)S(1)}, bf16[1920,256]{1,0:T(8,128)(2,1)}, u32[]{:S(2)}, u32[]{:S(2)}) collective-permute-start(bf16[1920,256]{1,0:T(8,128)(2,1)S(1)} %pad_maximum_fusion.22), channel_id=1, source_target_pairs={{0,4},{4,0},{8,12},{12,8},{1,5},{5,1},{9,13},{13,9},{2,6},{6,2},{1... | collective-permute-start | bytes 2949128 | tf_op jit(solution)/shard_map/while/body/ppermute | solution.py:17
  164.0 8.6 %collective-permute-start.9 = (bf16[960,128]{1,0:T(8,128)(2,1)}, bf16[960,128]{1,0:T(8,128)(2,1)S(1)}, u32[]{:S(2)}, u32[]{:S(2)}) collective-permute-start(bf16[960,128]{1,0:T(8,128)(2,1)} %slice.171), channel_id=1, source_target_pairs={{0,8},{4,12},{8,0},{12,4},{1,9},{5,13},{9,1},{13,5},{2,10},{6,14},... | collective-permute-start | bytes 737288 | tf_op jit(solution)/shard_map/while/body/ppermute | solution.py:17
  165.4 8.3 %collective-permute-start.8 = (bf16[960,128]{1,0:T(8,128)(2,1)}, bf16[960,128]{1,0:T(8,128)(2,1)S(1)}, u32[]{:S(2)}, u32[]{:S(2)}) collective-permute-start(bf16[960,128]{1,0:T(8,128)(2,1)} %slice.170), channel_id=1, source_target_pairs={{0,16},{16,0},{1,17},{17,1},{2,18},{18,2},{3,19},{19,3},{4,20},{20... | collective-permute-start | bytes 737288 | tf_op jit(solution)/shard_map/while/body/ppermute | solution.py:17
  173.9 5.9 %collective-permute-start.11 = (bf16[1920,256]{1,0:T(8,128)(2,1)S(1)}, bf16[1920,256]{1,0:T(8,128)(2,1)S(1)}, u32[]{:S(2)}, u32[]{:S(2)}) collective-permute-start(bf16[1920,256]{1,0:T(8,128)(2,1)S(1)} %pad_maximum_fusion.23), channel_id=1, source_target_pairs={{0,4},{4,0},{8,12},{12,8},{1,5},{5,1},{9,13},{13,9},{2,6},{6,2},{1... | collective-permute-start | bytes 2949128 | tf_op jit(solution)/shard_map/while/body/ppermute | solution.py:17
  183.7 10.3 %collective-permute-start.33 = (bf16[12,48,256]{2,1,0:T(8,128)(2,1)S(1)}, bf16[12,48,256]{2,1,0:T(8,128)(2,1)S(1)}, u32[]{:S(2)}, u32[]{:S(2)}) collective-permute-start(bf16[12,48,256]{2,1,0:T(8,128)(2,1)S(1)} %copy-done.11), channel_id=1, source_target_pairs={{0,1},{1,2},{2,3},{3,0},{4,5},{5,6},{6,7},{7,4},{8,9},{9,10},{10,1... | collective-permute-start | bytes 884744 | tf_op jit(solution)/shard_map/ppermute | solution.py:13
  194.1 13.7 %collective-permute-start.37 = (bf16[12,48,256]{2,1,0:T(8,128)(2,1)S(1)}, bf16[12,48,256]{2,1,0:T(8,128)(2,1)S(1)}, u32[]{:S(2)}, u32[]{:S(2)}) collective-permute-start(bf16[12,48,256]{2,1,0:T(8,128)(2,1)S(1)} %broadcast_select_fusion.14), channel_id=1, source_target_pairs={{0,2},{1,3},{2,0},{3,1},{4,6},{5,7},{6,4},{7,5},{8,10},{9,11},{10,... | collective-permute-start | bytes 884744 | tf_op jit(solution)/shard_map/ppermute | solution.py:13
  194.2 1.9 collective-permute-start.34
  194.2 5.7 %collective-permute-start.35 = (bf16[4,48,2,1,128]{4,2,1,0,3:T(2,128)(2,1)S(1)}, bf16[4,48,2,1,128]{4,2,1,0,3:T(2,128)(2,1)S(1)}, u32[]{:S(2)}, u32[]{:S(2)}) collective-permute-start(bf16[4,48,2,1,128]{4,2,1,0,3:T(2,128)(2,1)S(1)} %squeeze.30), channel_id=1, source_target_pairs={{0,8},{4,12},{8,0},{12,4},{1,9},{5,13},{9,1},{13,5},{2,10},{6,14},... | collective-permute-start | bytes 294920 | tf_op jit(solution)/shard_map/ppermute | solution.py:17
  195.7 5.4 %collective-permute-start.36 = (bf16[4,48,2,1,128]{4,2,1,0,3:T(2,128)(2,1)S(1)}, bf16[4,48,2,1,128]{4,2,1,0,3:T(2,128)(2,1)S(1)}, u32[]{:S(2)}, u32[]{:S(2)}) collective-permute-start(bf16[4,48,2,1,128]{4,2,1,0,3:T(2,128)(2,1)S(1)} %squeeze.31), channel_id=1, source_target_pairs={{0,12},{4,8},{8,4},{12,0},{1,13},{5,9},{9,5},{13,1},{2,14},{6,10},... | collective-permute-start | bytes 294920 | tf_op jit(solution)/shard_map/ppermute | solution.py:17
  208.6 2.4 %collective-permute-start.38 = (bf16[4,48,2,1,128]{4,2,1,0,3:T(2,128)(2,1)S(1)}, bf16[4,48,2,1,128]{4,2,1,0,3:T(2,128)(2,1)S(1)}, u32[]{:S(2)}, u32[]{:S(2)}) collective-permute-start(bf16[4,48,2,1,128]{4,2,1,0,3:T(2,128)(2,1)S(1)} %squeeze.33), channel_id=1, source_target_pairs={{0,4},{4,0},{8,12},{12,8},{1,5},{5,1},{9,13},{13,9},{2,6},{6,2},{1... | collective-permute-start | bytes 294920 | tf_op jit(solution)/shard_map/ppermute | solution.py:17
  208.8 5.7 %collective-permute-start.39 = (bf16[4,48,2,1,128]{4,2,1,0,3:T(2,128)(2,1)S(1)}, bf16[4,48,2,1,128]{4,2,1,0,3:T(2,128)(2,1)S(1)}, u32[]{:S(2)}, u32[]{:S(2)}) collective-permute-start(bf16[4,48,2,1,128]{4,2,1,0,3:T(2,128)(2,1)S(1)} %squeeze.34), channel_id=1, source_target_pairs={{0,8},{4,12},{8,0},{12,4},{1,9},{5,13},{9,1},{13,5},{2,10},{6,14},... | collective-permute-start | bytes 294920 | tf_op jit(solution)/shard_map/ppermute | solution.py:17
  210.3 5.4 %collective-permute-start.40 = (bf16[4,48,2,1,128]{4,2,1,0,3:T(2,128)(2,1)S(1)}, bf16[4,48,2,1,128]{4,2,1,0,3:T(2,128)(2,1)S(1)}, u32[]{:S(2)}, u32[]{:S(2)}) collective-permute-start(bf16[4,48,2,1,128]{4,2,1,0,3:T(2,128)(2,1)S(1)} %squeeze.35), channel_id=1, source_target_pairs={{0,12},{4,8},{8,4},{12,0},{1,13},{5,9},{9,5},{13,1},{2,14},{6,10},... | collective-permute-start | bytes 294920 | tf_op jit(solution)/shard_map/ppermute | solution.py:17
  (13 other events, 37.7 us)

commit v18 on v17

--- a/solution.py
+++ b/solution.py
@@ -141,6 +141,69 @@
     )()
 
 
+def pick_body(places, odd, rows, shifted, *pieces):
+    for d, piece in enumerate(pieces):
+        for j in range(piece.shape[0]):
+            place = places[d * piece.shape[0] + j]
+            found = place >= 0
+            place = jnp.maximum(place, 0)
+            moves = odd[place] == 1
+
+            @pl.when(jnp.logical_not(found))
+            def _():
+                piece[j] = jnp.zeros(piece.shape[1:], piece.dtype)
+
+            @pl.when(jnp.logical_and(found, moves))
+            def _():
+                piece[j] = shifted[place]
+
+            @pl.when(jnp.logical_and(found, jnp.logical_not(moves)))
+            def _():
+                piece[j] = rows[place]
+
+
+def picked_tiles(places, odd, rows, shifted):
+    scalars, vmem = pl.BlockSpec(memory_space=pltpu.SMEM), pl.BlockSpec(memory_space=pltpu.VMEM)
+    owners, most_tiles = places.shape
+    shape = jax.ShapeDtypeStruct((most_tiles, *rows.shape[1:]), rows.dtype)
+    return pl.pallas_call(
+        pick_body,
+        out_shape=[shape] * owners,
+        in_specs=[scalars, scalars, vmem, vmem],
+        out_specs=[vmem] * owners,
+    )(places.reshape(-1), odd, rows, shifted)
+
+
+def cache_body(tile, *refs):
+    *pieces, out = refs
+    width = out.shape[4]
+    for mine in range(4):
+
+        @pl.when(tile[0] == mine)
+        def _():
+            for source in range(4):
+                keys = pieces[mine ^ source][0].astype(jnp.float32)
+                values = pieces[4 + (mine ^ source)][0].astype(jnp.float32)
+                rows = [keys[:, :width], values[:, :width], keys[:, width:], values[:, width:]]
+                out[0, source] = jnp.stack(rows, axis=1).astype(out.dtype)
+
+
+def cache_rows(tile, keys, values):
+    most_tiles, shard_len, columns = keys[0].shape
+    piece = pl.BlockSpec((1, shard_len, columns), lambda j: (j, 0, 0))
+    shape = (most_tiles, 4, shard_len, 4, columns // 2)
+    return pl.pallas_call(
+        cache_body,
+        out_shape=jax.ShapeDtypeStruct(shape, jnp.bfloat16),
+        grid=(most_tiles,),
+        in_specs=[pl.BlockSpec(memory_space=pltpu.SMEM)] + [piece] * 8,
+        out_specs=pl.BlockSpec((1, *shape[1:]), lambda j: (j, 0, 0, 0, 0)),
+        cost_estimate=pl.CostEstimate(
+            flops=0, bytes_accessed=32 * most_tiles * shard_len * columns, transcendentals=0
+        ),
+    )(tile, *keys, *values)
+
+
 def product_plan(
     features, proj_weight, proj_bias, kv_weight, key_gain, tile_map, tile_count, decode_owner
 ):
@@ -218,27 +281,20 @@
 
     owner_tile, owner_turn, matched = routing(tile_map, tile_count, decode_owner, tile_slots, 4)
     turn_of = jnp.sum(jnp.where(matched, owner_turn[:, None, None], 0), axis=(0, 1))
-    owned_by = (owner_tile[:, None] == (tile ^ jnp.arange(4))[None, :]).astype(jnp.float32)
-    selector = jnp.einsum("rd,rjs->djs", owned_by, matched.astype(jnp.float32))
-    selector = selector.astype(jnp.bfloat16).reshape(4 * most_tiles, tile_slots)
-
+    usable = jnp.arange(most_tiles)[None, :] < tile_count[:, None]
+    owned_by = owner_tile[:, None] == (tile ^ jnp.arange(4))[None, :]
+    places = jnp.where(usable[:, None] & owned_by[:, :, None], tile_map[:, None], -1)
+    places = jnp.max(places, axis=0).astype(jnp.int32)
     turned = [turn_of // stride % 2 == 1 for stride in (1, 2)]
 
     def rolled(rows, shifted, stride):
         return jnp.where(turned[stride - 1][:, None, None], shifted, rows)
 
-    def outgoing(rows):
-        picked = add_columns(selector, rows.reshape(tile_slots, -1)).astype(jnp.bfloat16)
-        picked = picked.reshape(4, most_tiles, shard_len, 2, layers, head_dim)
-        return [picked[r] for r in range(4)]
+    def outgoing(rows, shifted):
+        return picked_tiles(places, turned[1].astype(jnp.int32), rows, shifted)
 
     def to_owners(picked):
         return [picked[0]] + [swapped(picked[r], "tile", r) for r in (1, 2, 3)]
-
-    def in_order(arrived):
-        even = [jnp.where(first_core, arrived[r], arrived[r ^ 1]) for r in range(4)]
-        ranked = [jnp.where(first_chip, even[r], even[r ^ 2]) for r in range(4)]
-        return jnp.stack(ranked, axis=1)
 
     column, half = group * 2 * head_dim, kv_weight.shape[0] // 2
 
@@ -284,7 +340,8 @@
     key_near = step(put_first(first_chip, key_half, key_other, 0))
     terms = products(key_near, swapped(key_near, "tile", 1), False)
     bias_part = bias_part + swapped(bias_part, "tile", 1)
-    terms, value_pieces, bias_part = step((terms, value_pieces, bias_part))
+    terms, bias_part = step((terms, bias_part))
+    value_pieces, bias_part = step((value_pieces, bias_part))
     value_half = jnp.concatenate(value_pieces, axis=1)
 
     def values_terms(given):
@@ -315,21 +372,6 @@
     blocks = [plus(own, second, mirror, first[:direct]), plus(pair[:, :width], mirrored)]
     own = jnp.concatenate([block.astype(jnp.bfloat16) for block in blocks], axis=0)
 
-    def rest_of_plane(given, part):
-        own, across_x, across_y = given
-        rows_0 = step(both_heads(own, across_y))
-        middle = depth // 2
-        upper, lower, rows_1 = step(
-            (
-                swapped(across_x[:middle], "groups", 1),
-                swapped(across_y[middle:], "tile", 2),
-                swapped(rows_0, "tile", 1),
-            )
-        )
-        rows_2 = step(both_heads(across_x, jnp.concatenate([upper, lower], axis=0)))
-        rows = [rows_0, rows_1, rows_2, swapped(rows_2, "tile", 1)]
-        return finish(times_features(rows, feature_parts), part)
-
     def keys_product(own):
         across_x, across_y = step((swapped(own, "tile", 2), swapped(own, "groups", 1)))
         rows_0 = step(both_heads(own, across_y))
@@ -355,20 +397,34 @@
 
     def values_product(given):
         own, across_x, across_y = given
-        return (across_y, own, across_x), rest_of_plane(given, 1)
+        rows_0 = step(both_heads(own, across_y))
+        middle = depth // 2
+        upper, lower, rows_1, total = step(
+            (
+                swapped(across_x[:middle], "groups", 1),
+                swapped(across_y[middle:], "tile", 2),
+                swapped(rows_0, "tile", 1),
+                add_columns(feature_parts[0], rows_0),
+            )
+        )
+        rows_2 = step(both_heads(across_x, jnp.concatenate([upper, lower], axis=0)))
+        rows = [None, rows_1, rows_2, swapped(rows_2, "tile", 1)]
+        for r in (1, 2, 3):
+            total = total + add_columns(feature_parts[r], rows[r])
+        return (across_y, own, across_x), finish(total, 1)
 
     keys = step(rolled(keys, shifted, 1))
     values = in_loop(values_product, (own, across_x, across_y), no_values)
     shifted, values = step((shifted_2(keys, "head", 2), values))
 
-    picked = outgoing(rolled(keys, shifted, 2))
+    picked = outgoing(keys, shifted)
     shifted, picked = step((shifted_2(values, "head", 1), picked))
 
     values = step(rolled(values, shifted, 1))
     arrived, shifted = step((to_owners(picked), shifted_2(values, "head", 2)))
 
-    value_cache = in_order(to_owners(outgoing(rolled(values, shifted, 2))))
-    cache = jnp.stack([in_order(arrived), value_cache], axis=-2)
+    value_pieces = to_owners(outgoing(values, shifted))
+    cache = cache_rows(tile.reshape(1), arrived, value_pieces)
     return cache.reshape(1, 1, most_tiles * 4 * shard_len, 4 * layers, head_dim)
 
 

time: 222 us -> 229 us (1.032)
  Pallas kernels: 15.7 us -> 23.9 us
  matrix products: 9.94 us -> 13.3 us
  local copies, waits for them, and re-layouts: 22.9 us -> 20.2 us
    pallas_call x0 -> x3, Pallas kernels: none -> 8.13 us  [the longest x2 4.28 us: picked_tiles(): pl.pallas_call(pick_body, out_shape=[shape] * owners, in_specs=[scalars,...]
    dot_general x11 -> x9, matrix products: 9.75 us -> 13.3 us  [add_columns(): return jnp.dot(operand, portion, preferred_element_type=jnp.float32)]
    another operation x4 -> x0, other arithmetic: 3.3 us -> none  [the longest x3 2.54 us: product_plan(): cache = jnp.stack([in_order(arrived), value_cache], axis=-2)]
  transfers between devices with their start and end apart: 41 -> 41, of which waited for: 18 -> 18; matrix products, arithmetic and copies ran while one was open for 13% -> 17% of each run, Pallas kernels for 7% -> 8%
where the time goes in v18:
time: 229 us; the launch traced here: 228 us
  waiting for transfers between devices  97.6 us (43%)
  starting transfers between devices  55.3 us (24%)
  Pallas kernels  23.9 us (10%)
  local copies, waits for them, and re-layouts  20.2 us (9%)
  other arithmetic  16.5 us (7%)
  matrix products  13.3 us (6%)
    ppermute x32, waiting for transfers between devices, swapped(): lax.ppermute(shard, axis, [(i, i ^ bit) for i in range(lax.axis_size(axis...  63 us
    ppermute x32, starting transfers between devices, swapped(): lax.ppermute(shard, axis, [(i, i ^ bit) for i in range(lax.axis_size(axis...  33.9 us
    ppermute x4, waiting for transfers between devices, shifted_2(): lax.ppermute(shard, axis, [(i, (i + by) % count) for i in range(count)])  20.2 us
    pallas_call x2, Pallas kernels, product_terms(): pl.pallas_call(terms_body, out_shape=shapes, grid_spec=pltpu.PrefetchScal...  15.7 us
    ppermute x5, waiting for transfers between devices, moved(): return lax.ppermute(shard, ('tile', 'head'), pairs)  14.4 us
    dot_general x9, matrix products, add_columns(): return jnp.dot(operand, portion, preferred_element_type=jnp.float32)  13.3 us
    ppermute x4, starting transfers between devices, shifted_2(): lax.ppermute(shard, axis, [(i, (i + by) % count) for i in range(count)])  12.4 us
    ppermute x5, starting transfers between devices, moved(): return lax.ppermute(shard, ('tile', 'head'), pairs)  9.05 us
  transfers between devices with their start and end apart: 41, of which 18 were waited for; matrix products, arithmetic and copies ran while one was open for 17% of the time, Pallas kernels for 8%

profile of v18, /device:TPU:0, one launch (start us, length us, event | category | flops | bytes accessed | tf_op | source)
XLA Modules:
  0.0 228.2 jit_solution(14586773684659128121)
XLA Ops:
  0.0 3.0 %fusion.6 = (bf16[1024,128]{1,0:T(8,128)(2,1)S(1)}, bf16[1024,128]{1,0:T(8,128)(2,1)}, bf16[1024,128]{1,0:T(8,128)(2,1)S(1)}, bf16[1024,128]{1,0:T(8,128)(2,1)S(1)}) fusion(bf16[2048,512]{1,0:T(8,128)(2,1)} %param.17, s32[]{:T(128)S(6)} %select_n.222, s32[]{:T(128)S(6)} %select_n.227, s32[]{:T(128)S(6)} %select_n.218, s32[]{:T(128)S(6)} %select_n.220), kind=kLoop, calls=%fused_computation.89 | loop fusion | bytes 2097168 | tf_op jit(solution)/shard_map/dynamic_slice | solution.py:304
  3.0 2.9 %collective-permute-start.12 = (bf16[1024,128]{1,0:T(8,128)(2,1)S(1)}, bf16[1024,128]{1,0:T(8,128)(2,1)S(1)}, u32[]{:S(2)}, u32[]{:S(2)}) collective-permute-start(bf16[1024,128]{1,0:T(8,128)(2,1)S(1)} %get-tuple-element.604), channel_id=1, source_target_pairs={{0,8},{4,12},{8,0},{12,4},{1,9},{5,13},{9,1},{13,5},{2,10},{6,14},... | collective-permute-start | bytes 786440 | tf_op jit(solution)/shard_map/ppermute | solution.py:17
  6.0 1.3 collective-permute-start.13
  7.3 4.7 %collective-permute-start.16 = (bf16[1024,128]{1,0:T(8,128)(2,1)S(1)}, bf16[1024,128]{1,0:T(8,128)(2,1)S(1)}, u32[]{:S(2)}, u32[]{:S(2)}) collective-permute-start(bf16[1024,128]{1,0:T(8,128)(2,1)S(1)} %get-tuple-element.602), channel_id=1, source_target_pairs={{0,8},{4,12},{8,0},{12,4},{1,9},{5,13},{9,1},{13,5},{2,10},{6,14},... | collective-permute-start | bytes 786440 | tf_op jit(solution)/shard_map/ppermute | solution.py:17
  14.0 4.3 %collective-permute-start.15 = (bf16[1024,128]{1,0:T(8,128)(2,1)S(1)}, bf16[1024,128]{1,0:T(8,128)(2,1)S(1)}, u32[]{:S(2)}, u32[]{:S(2)}) collective-permute-start(bf16[1024,128]{1,0:T(8,128)(2,1)S(1)} %get-tuple-element.612), channel_id=1, source_target_pairs={{0,2},{1,6},{2,4},{3,0},{4,3},{5,7},{6,5},{7,1},{8,10},{9,14},{10,... | collective-permute-start | bytes 786440 | tf_op jit(solution)/shard_map/ppermute | solution.py:228
  18.8 10.7 %collective-permute-done.15 = bf16[1024,128]{1,0:T(8,128)(2,1)S(1)} collective-permute-done((bf16[1024,128]{1,0:T(8,128)(2,1)S(1)}, bf16[1024,128]{1,0:T(8,128)(2,1)S(1)}, u32[]{:S(2)}, u32[]{:S(2)}) %collective-permute-start.15) | collective-permute-done | bytes 262176 | tf_op jit(solution)/shard_map/ppermute | solution.py:228
  30.8 7.1 %constant_dynamic-slice_fusion = (bf16[576,1920]{1,0:T(8,128)(2,1)}, bf16[576,1920]{1,0:T(8,128)(2,1)}, bf16[576,1920]{1,0:T(8,128)(2,1)}, bf16[576,1920]{1,0:T(8,128)(2,1)}) fusion(bf16[576,7680]{1,0:T(8,128)(2,1)} %bitcast.105, s32[]{:T(128)S(6)} %select_n.231, s32[]{:T(128)S(6)} %select_n.230, s32[]{:T(128)S(6)} %select_n.229, s32[]{:T(128)S(6)} %select_n.228), kind=kLoop, calls=%fused_computation.82 | loop fusion | bytes 17694736 | tf_op jit(solution)/shard_map/dynamic_slice | solution.py:234
  38.0 5.8 %collective-permute-done.17 = bf16[1024,256]{1,0:T(8,128)(2,1)S(1)} collective-permute-done((bf16[1024,256]{1,0:T(8,128)(2,1)S(1)}, bf16[1024,256]{1,0:T(8,128)(2,1)S(1)}, u32[]{:S(2)}, u32[]{:S(2)}) %collective-permute-start.17) | collective-permute-done | bytes 524320 | tf_op jit(solution)/shard_map/ppermute | solution.py:17
  45.5 2.0 collective-permute-start.24
  47.6 7.7 %shard_map.82 = (f32[1280,128]{1,0:T(8,128)S(1)}, bf16[1280,128]{1,0:T(8,128)(2,1)}, bf16[1280,128]{1,0:T(8,128)(2,1)}, bf16[2560,128]{1,0:T(8,128)(2,1)}, f32[640,256]{1,0:T(8,128)S(1)}) custom-call(s32[1]{0:T(128)} %bitcast.15.choice, bf16[1920,2048]{1,0:T(8,128)(2,1)} %weight.1, bf16[2048,256]{1,0:T(8,128)(2,1)S(1)} %pad_maximum_fusion.7.near, ...), custom_call_target="tpu_custom_call" | custom-call | flops 4026531840 | bytes 12419072 | tf_op jit(solution)/shard_map/pallas_call | solution.py:118
  55.3 3.7 %collective-permute-done.24 = bf16[1024,128]{1,0:T(8,128)(2,1)S(1)} collective-permute-done((bf16[1024,128]{1,0:T(8,128)(2,1)S(1)}, bf16[1024,128]{1,0:T(8,128)(2,1)S(1)}, u32[]{:S(2)}, u32[]{:S(2)}) %collective-permute-start.24) | collective-permute-done | bytes 262176 | tf_op jit(solution)/shard_map/ppermute | solution.py:228
  61.0 2.9 %collective-permute-start.21 = (bf16[1280,128]{1,0:T(8,128)(2,1)}, bf16[1280,128]{1,0:T(8,128)(2,1)}, u32[]{:S(2)}, u32[]{:S(2)}) collective-permute-start(bf16[1280,128]{1,0:T(8,128)(2,1)} %get-tuple-element.438), channel_id=1, source_target_pairs={{0,3},{1,2},{2,1},{3,0},{4,7},{5,6},{6,5},{7,4},{8,11},{9,10},{10,... | collective-permute-start | bytes 983048 | tf_op jit(solution)/shard_map/ppermute | solution.py:17
  64.8 26.9 %while.54 = (s32[]{:T(128)}, bf16[1024,256]{1,0:T(8,128)(2,1)}, f32[1,512]{1,0:T(1,128)S(1)}, f32[1920,128]{1,0:T(8,128)}, bf16[1920,128]{1,0:T(8,128)(2,1)}, /*...) while((s32[]{:T(128)}, bf16[1024,256]{1,0:T(8,128)(2,1)}, ...), condition=%wide.region_3.4_spmd, body=%wide.region_2.3_spmd.sunk | while | flops 4029153792 | bytes 23972084 | solution.py:266
  66.6 1.3 collective-permute-start.1
  67.9 11.8 %collective-permute-done.1 = f32[1,512]{1,0:T(1,128)S(1)} collective-permute-done((f32[1,512]{1,0:T(1,128)S(1)}, f32[1,512]{1,0:T(1,128)S(1)}, u32[]{:S(2)}, u32[]{:S(2)}) %collective-permute-start.1) | collective-permute-done | bytes 2080 | tf_op jit(solution)/shard_map/while/body/ppermute | solution.py:17
  81.6 2.1 collective-permute-done.2.far
  83.6 8.1 %body.1 = (f32[1920,128]{1,0:T(8,128)}, bf16[1920,128]{1,0:T(8,128)(2,1)}, bf16[1920,128]{1,0:T(8,128)(2,1)}, bf16[1920,128]{1,0:T(8,128)(2,1)}) custom-call(s32[1]{0:T(128)} %get-tuple-element.929.choice, bf16[1920,2048]{1,0:T(8,128)(2,1)} %get-tuple-element.930.weight, bf16[2048,256]{1,0:T(8,128)(2,1)S(1)} %pad_maximum_fusion.17.near, ...), custom_call_target="tpu_custom_call" | custom-call | flops 4026531840 | bytes 12419072 | tf_op jit(solution)/shard_map/while/body/pallas_call | solution.py:118
  92.9 1.9 collective-permute-start.25
  94.7 1.3 add_convert_fusion.1
  96.0 5.0 %collective-permute-done.25 = bf16[640,128]{1,0:T(8,128)(2,1)S(1)} collective-permute-done((bf16[640,128]{1,0:T(8,128)(2,1)S(1)}, bf16[640,128]{1,0:T(8,128)(2,1)S(1)}, u32[]{:S(2)}, u32[]{:S(2)}) %collective-permute-start.25) | collective-permute-done | bytes 163872 | tf_op jit(solution)/shard_map/ppermute | solution.py:17
  101.1 3.1 %collective-permute-start.26 = (bf16[1920,128]{1,0:T(8,128)(2,1)}, bf16[1920,128]{1,0:T(8,128)(2,1)}, u32[]{:S(2)}, u32[]{:S(2)}) collective-permute-start(bf16[1920,128]{1,0:T(8,128)(2,1)} %get-tuple-element.461), channel_id=1, source_target_pairs={{0,2},{1,3},{2,0},{3,1},{4,6},{5,7},{6,4},{7,5},{8,10},{9,11},{10,... | collective-permute-start | bytes 1474568 | tf_op jit(solution)/shard_map/ppermute | solution.py:17
  105.5 35.9 %while.55 = (s32[]{:T(128)}, bf16[1920,128]{1,0:T(8,128)(2,1)S(1)}, bf16[12,48,256]{2,1,0:T(8,128)(2,1)}, s32[]{:T(128)}, pred[]{:T(512)}, /*index=5*/bf16[576,1...) while((s32[]{:T(128)}, bf16[1920,128]{1,0:T(8,128)(2,1)S(1)}, ...), condition=%wide.region_7.8_spmd, body=%wide.region_4.7_spmd.sunk | while | flops 2271905024 | bytes 68148112 | solution.py:266
  105.6 1.5 collective-permute-start.3
  107.1 1.4 collective-permute-start.4
  108.5 8.5 %collective-permute-done.3 = bf16[1920,128]{1,0:T(8,128)(2,1)S(1)} collective-permute-done((bf16[1920,128]{1,0:T(8,128)(2,1)S(1)}, bf16[1920,128]{1,0:T(8,128)(2,1)S(1)}, u32[]{:S(2)}, u32[]{:S(2)}) %collective-permute-start.3) | collective-permute-done | bytes 491552 | tf_op jit(solution)/shard_map/while/body/ppermute | solution.py:17
  119.9 13.1 %collective-permute-done.5 = bf16[1920,128]{1,0:T(8,128)(2,1)} collective-permute-done((bf16[1920,128]{1,0:T(8,128)(2,1)S(1)}, bf16[1920,128]{1,0:T(8,128)(2,1)}, u32[]{:S(2)}, u32[]{:S(2)}) %collective-permute-start.5) | collective-permute-done | bytes 491552 | tf_op jit(solution)/shard_map/while/body/ppermute | solution.py:17
  134.3 2.1 fusion.55
  136.5 2.1 convolution_add_fusion.5
  141.5 1.9 add_convert_fusion
  144.1 1.4 collective-permute-start.31
  145.6 6.7 %collective-permute-start.29 = (bf16[12,48,256]{2,1,0:T(8,128)(2,1)S(1)}, bf16[12,48,256]{2,1,0:T(8,128)(2,1)S(1)}, u32[]{:S(2)}, u32[]{:S(2)}) collective-permute-start(bf16[12,48,256]{2,1,0:T(8,128)(2,1)S(1)} %copy-done.11), channel_id=1, source_target_pairs={{0,1},{1,2},{2,3},{3,0},{4,5},{5,6},{6,7},{7,4},{8,9},{9,10},{10,1... | collective-permute-start | bytes 884744 | tf_op jit(solution)/shard_map/ppermute | solution.py:13
  153.0 5.1 %collective-permute-done.29 = bf16[12,48,256]{2,1,0:T(8,128)(2,1)S(1)} collective-permute-done((bf16[12,48,256]{2,1,0:T(8,128)(2,1)S(1)}, bf16[12,48,256]{2,1,0:T(8,128)(2,1)S(1)}, u32[]{:S(2)}, u32[]{:S(2)}) %collective-permute-start.29) | collective-permute-done | bytes 294944 | tf_op jit(solution)/shard_map/ppermute | solution.py:13
  158.9 4.6 %collective-permute-start.32 = (bf16[12,48,256]{2,1,0:T(8,128)(2,1)}, bf16[12,48,256]{2,1,0:T(8,128)(2,1)}, u32[]{:S(2)}, u32[]{:S(2)}) collective-permute-start(bf16[12,48,256]{2,1,0:T(8,128)(2,1)} %broadcast_select_fusion.13.rows), channel_id=1, source_target_pairs={{0,2},{1,3},{2,0},{3,1},{4,6},{5,7},{6,4},{7,5},{8,10},{9,11},{10,... | collective-permute-start | bytes 884744 | tf_op jit(solution)/shard_map/ppermute | solution.py:13
  163.5 22.9 %while.56 = (s32[]{:T(128)}, bf16[1920,128]{1,0:T(8,128)(2,1)}, bf16[1920,128]{1,0:T(8,128)(2,1)S(1)}, bf16[1920,128]{1,0:T(8,128)(2,1)}, bf16[12,48,256]{2,1,0:...) while((s32[]{:T(128)}, bf16[1920,128]{1,0:T(8,128)(2,1)}, ...), condition=%wide.region_9.10_spmd, body=%wide.region_8.9_spmd.sunk | while | flops 2271166464 | bytes 69897640 | solution.py:266
  166.7 1.4 collective-permute-start.8
  168.2 1.6 convolution_bitcast_fusion.7
  169.8 4.6 %collective-permute-done.9 = bf16[960,128]{1,0:T(8,128)(2,1)S(1)} collective-permute-done((bf16[960,128]{1,0:T(8,128)(2,1)S(1)}, bf16[960,128]{1,0:T(8,128)(2,1)S(1)}, u32[]{:S(2)}, u32[]{:S(2)}) %collective-permute-start.9) | collective-permute-done | bytes 245792 | tf_op jit(solution)/shard_map/while/body/ppermute | solution.py:17
  179.7 2.8 %convolution_bitcast_fusion.8 = f32[576,256]{1,0:T(8,128)S(1)} fusion(bf16[576,1920]{1,0:T(8,128)(2,1)} %get-tuple-element.1003, bf16[1920,256]{1,0:T(8,128)(2,1)} %pad_maximum_fusion.22), kind=kOutput, calls=%fused_computation.25.clone.1 | convolution fusion | flops 566231040 | bytes 3784704 | tf_op jit(solution)/shard_map/while/body/dot_general | solution.py:21
  183.6 2.0 add_add_fusion.2
  188.2 2.2 shard_map.84
  190.3 7.5 %collective-permute-done.33 = bf16[12,48,256]{2,1,0:T(8,128)(2,1)S(1)} collective-permute-done((bf16[12,48,256]{2,1,0:T(8,128)(2,1)}, bf16[12,48,256]{2,1,0:T(8,128)(2,1)S(1)}, u32[]{:S(2)}, u32[]{:S(2)}) %collective-permute-start.33) | collective-permute-done | bytes 294944 | tf_op jit(solution)/shard_map/ppermute | solution.py:13
  199.0 1.4 collective-permute-start.35
  200.9 4.0 %collective-permute-done.35.refs_2_ = bf16[4,48,256]{2,1,0:T(8,128)(2,1)S(1)} collective-permute-done((bf16[4,48,256]{2,1,0:T(8,128)(2,1)}, bf16[4,48,256]{2,1,0:T(8,128)(2,1)S(1)}, u32[]{:S(2)}, u32[]{:S(2)}) %collective-permute-start.35) | collective-permute-done | bytes 98336 | tf_op jit(solution)/shard_map/ppermute | solution.py:17
  206.1 7.6 %collective-permute-done.37.shifted = bf16[12,48,256]{2,1,0:T(8,128)(2,1)S(1)} collective-permute-done((bf16[12,48,256]{2,1,0:T(8,128)(2,1)S(1)}, bf16[12,48,256]{2,1,0:T(8,128)(2,1)S(1)}, u32[]{:S(2)}, u32[]{:S(2)}) %collective-permute-start.37) | collective-permute-done | bytes 294944 | tf_op jit(solution)/shard_map/ppermute | solution.py:13
  214.5 2.1 shard_map.85
  216.6 1.4 collective-permute-start.39
  218.4 4.0 %collective-permute-done.39.refs_6_ = bf16[4,48,256]{2,1,0:T(8,128)(2,1)S(1)} collective-permute-done((bf16[4,48,256]{2,1,0:T(8,128)(2,1)}, bf16[4,48,256]{2,1,0:T(8,128)(2,1)S(1)}, u32[]{:S(2)}, u32[]{:S(2)}) %collective-permute-start.39) | collective-permute-done | bytes 98336 | tf_op jit(solution)/shard_map/ppermute | solution.py:17
  224.3 3.8 %shard_map.86 = bf16[4,4,48,4,128]{4,3,2,1,0:T(4,128)(2,1)} custom-call(s32[1]{0:T(128)} %bitcast.14.tile, bf16[4,48,256]{2,1,0:T(8,128)(2,1)} %get-tuple-element.497.refs_0_, bf16[4,48,256]{2,1,0:T(8,128)(2,1)} %copy-done.15, bf16[4,48,256]{2,1,0:T(8,128)(2,1)} %copy-done.16, bf16[4,48,256]{2,1,0:T(8,128)(2,1)} %copy-done.17, ...), custom_call_target="tpu_custom_call" | custom-call | bytes 1572864 | tf_op jit(solution)/shard_map/pallas_call | solution.py:195
  (167 shorter events, 41.2 us)
Async XLA Ops:
  0.0 18.4 %copy-start.3 = (bf16[2048,512]{1,0:T(8,128)(2,1)S(1)}, bf16[2048,512]{1,0:T(8,128)(2,1)}, u32[]{:S(2)}) copy-start(bf16[2048,512]{1,0:T(8,128)(2,1)} %param.17) | copy-start | bytes 6291460
  3.0 10.3 %collective-permute-start.12 = (bf16[1024,128]{1,0:T(8,128)(2,1)S(1)}, bf16[1024,128]{1,0:T(8,128)(2,1)S(1)}, u32[]{:S(2)}, u32[]{:S(2)}) collective-permute-start(bf16[1024,128]{1,0:T(8,128)(2,1)S(1)} %get-tuple-element.604), channel_id=1, source_target_pairs={{0,8},{4,12},{8,0},{12,4},{1,9},{5,13},{9,1},{13,5},{2,10},{6,14},... | collective-permute-start | bytes 786440 | tf_op jit(solution)/shard_map/ppermute | solution.py:17
  6.0 7.3 %collective-permute-start.13 = (bf16[2048]{0:T(1024)(128)(2,1)}, bf16[2048]{0:T(1024)(128)(2,1)S(1)}, u32[]{:S(2)}, u32[]{:S(2)}) collective-permute-start(bf16[2048]{0:T(1024)(128)(2,1)} %param.16), channel_id=1, source_target_pairs={{0,0},{1,4},{2,8},{3,12},{4,1},{5,5},{6,9},{7,13},{8,2},{9,6},{10,... | collective-permute-start | bytes 12296 | tf_op jit(solution)/shard_map/ppermute | solution.py:228
  7.3 11.5 %collective-permute-start.16 = (bf16[1024,128]{1,0:T(8,128)(2,1)S(1)}, bf16[1024,128]{1,0:T(8,128)(2,1)S(1)}, u32[]{:S(2)}, u32[]{:S(2)}) collective-permute-start(bf16[1024,128]{1,0:T(8,128)(2,1)S(1)} %get-tuple-element.602), channel_id=1, source_target_pairs={{0,8},{4,12},{8,0},{12,4},{1,9},{5,13},{9,1},{13,5},{2,10},{6,14},... | collective-permute-start | bytes 786440 | tf_op jit(solution)/shard_map/ppermute | solution.py:17
  13.3 5.5 %collective-permute-start.14 = (bf16[1024,128]{1,0:T(8,128)(2,1)S(1)}, bf16[1024,128]{1,0:T(8,128)(2,1)S(1)}, u32[]{:S(2)}, u32[]{:S(2)}) collective-permute-start(bf16[1024,128]{1,0:T(8,128)(2,1)S(1)} %get-tuple-element.613), channel_id=1, source_target_pairs={{0,0},{1,4},{2,6},{3,2},{4,1},{5,5},{6,7},{7,3},{8,8},{9,12},{10,1... | collective-permute-start | bytes 786440 | tf_op jit(solution)/shard_map/ppermute | solution.py:228
  14.0 15.5 %collective-permute-start.15 = (bf16[1024,128]{1,0:T(8,128)(2,1)S(1)}, bf16[1024,128]{1,0:T(8,128)(2,1)S(1)}, u32[]{:S(2)}, u32[]{:S(2)}) collective-permute-start(bf16[1024,128]{1,0:T(8,128)(2,1)S(1)} %get-tuple-element.612), channel_id=1, source_target_pairs={{0,2},{1,6},{2,4},{3,0},{4,3},{5,7},{6,5},{7,1},{8,10},{9,14},{10,... | collective-permute-start | bytes 786440 | tf_op jit(solution)/shard_map/ppermute | solution.py:228
  18.8 19.2 %copy-start.13 = (bf16[1024,128]{1,0:T(8,128)(2,1)}, bf16[1024,128]{1,0:T(8,128)(2,1)S(1)}, u32[]{:S(2)}) copy-start(bf16[1024,128]{1,0:T(8,128)(2,1)S(1)} %collective-permute-done.16) | copy-start | bytes 786436
  29.6 14.1 %collective-permute-start.17 = (bf16[1024,256]{1,0:T(8,128)(2,1)S(1)}, bf16[1024,256]{1,0:T(8,128)(2,1)S(1)}, u32[]{:S(2)}, u32[]{:S(2)}) collective-permute-start(bf16[1024,256]{1,0:T(8,128)(2,1)S(1)} %constant_dynamic-update-slice_fusion.2), channel_id=1, source_target_pairs={{0,8},{4,12},{8,0},{12,4},{1,9},{5,13},{9,1},{13,5},{2,10},{6,14},... | collective-permute-start | bytes 1572872 | tf_op jit(solution)/shard_map/ppermute | solution.py:17
  44.0 3.6 %collective-permute-start.18 = (bf16[2048,256]{1,0:T(8,128)(2,1)S(1)}, bf16[2048,256]{1,0:T(8,128)(2,1)S(1)}, u32[]{:S(2)}, u32[]{:S(2)}) collective-permute-start(bf16[2048,256]{1,0:T(8,128)(2,1)S(1)} %pad_maximum_fusion.7.near), channel_id=1, source_target_pairs={{0,4},{4,0},{8,12},{12,8},{1,5},{5,1},{9,13},{13,9},{2,6},{6,2},{1... | collective-permute-start | bytes 3145736 | tf_op jit(solution)/shard_map/ppermute | solution.py:17
  44.1 3.5 %collective-permute-start.19 = (f32[1,512]{1,0:T(1,128)S(1)}, f32[1,512]{1,0:T(1,128)S(1)}, u32[]{:S(2)}, u32[]{:S(2)}) collective-permute-start(f32[1,512]{1,0:T(1,128)S(1)} %fusion.9), channel_id=1, source_target_pairs={{0,4},{4,0},{8,12},{12,8},{1,5},{5,1},{9,13},{13,9},{2,6},{6,2},{1... | collective-permute-start | bytes 6152 | tf_op jit(solution)/shard_map/ppermute | solution.py:17
  44.9 10.4 %collective-permute-start.23 = (bf16[1024,128]{1,0:T(8,128)(2,1)S(1)}, bf16[1024,128]{1,0:T(8,128)(2,1)S(1)}, u32[]{:S(2)}, u32[]{:S(2)}) collective-permute-start(bf16[1024,128]{1,0:T(8,128)(2,1)S(1)} %get-tuple-element.611), channel_id=1, source_target_pairs={{0,0},{1,4},{2,6},{3,2},{4,1},{5,5},{6,7},{7,3},{8,8},{9,12},{10,1... | collective-permute-start | bytes 786440 | tf_op jit(solution)/shard_map/ppermute | solution.py:228
  45.5 13.4 %collective-permute-start.24 = (bf16[1024,128]{1,0:T(8,128)(2,1)S(1)}, bf16[1024,128]{1,0:T(8,128)(2,1)S(1)}, u32[]{:S(2)}, u32[]{:S(2)}) collective-permute-start(bf16[1024,128]{1,0:T(8,128)(2,1)S(1)} %get-tuple-element.610), channel_id=1, source_target_pairs={{0,2},{1,6},{2,4},{3,0},{4,3},{5,7},{6,5},{7,1},{8,10},{9,14},{10,... | collective-permute-start | bytes 786440 | tf_op jit(solution)/shard_map/ppermute | solution.py:228
  59.5 32.1 %collective-permute-start.22 = (bf16[2560,128]{1,0:T(8,128)(2,1)}, bf16[2560,128]{1,0:T(8,128)(2,1)}, u32[]{:S(2)}, u32[]{:S(2)}) collective-permute-start(bf16[2560,128]{1,0:T(8,128)(2,1)} %get-tuple-element.439), channel_id=1, source_target_pairs={{0,1},{1,0},{2,3},{3,2},{4,5},{5,4},{6,7},{7,6},{8,9},{9,8},{10,11... | collective-permute-start | bytes 1966088 | tf_op jit(solution)/shard_map/ppermute | solution.py:17
  60.1 31.6 %collective-permute-start.20 = (bf16[1280,128]{1,0:T(8,128)(2,1)}, bf16[1280,128]{1,0:T(8,128)(2,1)}, u32[]{:S(2)}, u32[]{:S(2)}) collective-permute-start(bf16[1280,128]{1,0:T(8,128)(2,1)} %get-tuple-element.437), channel_id=1, source_target_pairs={{0,2},{1,3},{2,0},{3,1},{4,6},{5,7},{6,4},{7,5},{8,10},{9,11},{10,... | collective-permute-start | bytes 983048 | tf_op jit(solution)/shard_map/ppermute | solution.py:17
  61.0 30.7 %collective-permute-start.21 = (bf16[1280,128]{1,0:T(8,128)(2,1)}, bf16[1280,128]{1,0:T(8,128)(2,1)}, u32[]{:S(2)}, u32[]{:S(2)}) collective-permute-start(bf16[1280,128]{1,0:T(8,128)(2,1)} %get-tuple-element.438), channel_id=1, source_target_pairs={{0,3},{1,2},{2,1},{3,0},{4,7},{5,6},{6,5},{7,4},{8,11},{9,10},{10,... | collective-permute-start | bytes 983048 | tf_op jit(solution)/shard_map/ppermute | solution.py:17
  65.8 13.9 %collective-permute-start = (bf16[1024,256]{1,0:T(8,128)(2,1)S(1)}, bf16[1024,256]{1,0:T(8,128)(2,1)}, u32[]{:S(2)}, u32[]{:S(2)}) collective-permute-start(bf16[1024,256]{1,0:T(8,128)(2,1)S(1)} %copy.20), channel_id=1, source_target_pairs={{0,8},{4,12},{8,0},{12,4},{1,9},{5,13},{9,1},{13,5},{2,10},{6,14},... | collective-permute-start | bytes 1572872 | tf_op jit(solution)/shard_map/while/body/ppermute | solution.py:17
  66.6 13.1 %collective-permute-start.1 = (f32[1,512]{1,0:T(1,128)S(1)}, f32[1,512]{1,0:T(1,128)S(1)}, u32[]{:S(2)}, u32[]{:S(2)}) collective-permute-start(f32[1,512]{1,0:T(1,128)S(1)} %copy.21), channel_id=1, source_target_pairs={{0,8},{4,12},{8,0},{12,4},{1,9},{5,13},{9,1},{13,5},{2,10},{6,14},... | collective-permute-start | bytes 6152 | tf_op jit(solution)/shard_map/while/body/ppermute | solution.py:17
  80.9 2.7 %collective-permute-start.2 = (bf16[2048,256]{1,0:T(8,128)(2,1)S(1)}, bf16[2048,256]{1,0:T(8,128)(2,1)S(1)}, u32[]{:S(2)}, u32[]{:S(2)}) collective-permute-start(bf16[2048,256]{1,0:T(8,128)(2,1)S(1)} %pad_maximum_fusion.17.near), channel_id=1, source_target_pairs={{0,4},{4,0},{8,12},{12,8},{1,5},{5,1},{9,13},{13,9},{2,6},{6,2},{1... | collective-permute-start | bytes 3145736 | tf_op jit(solution)/shard_map/while/body/ppermute | solution.py:17
  92.9 8.2 %collective-permute-start.25 = (bf16[640,128]{1,0:T(8,128)(2,1)S(1)}, bf16[640,128]{1,0:T(8,128)(2,1)S(1)}, u32[]{:S(2)}, u32[]{:S(2)}) collective-permute-start(bf16[640,128]{1,0:T(8,128)(2,1)S(1)} %slice.99), channel_id=1, source_target_pairs={{0,3},{1,2},{2,1},{3,0},{4,7},{5,6},{6,5},{7,4},{8,11},{9,10},{10,... | collective-permute-start | bytes 491528 | tf_op jit(solution)/shard_map/ppermute | solution.py:17
  101.1 40.4 %collective-permute-start.26 = (bf16[1920,128]{1,0:T(8,128)(2,1)}, bf16[1920,128]{1,0:T(8,128)(2,1)}, u32[]{:S(2)}, u32[]{:S(2)}) collective-permute-start(bf16[1920,128]{1,0:T(8,128)(2,1)} %get-tuple-element.461), channel_id=1, source_target_pairs={{0,2},{1,3},{2,0},{3,1},{4,6},{5,7},{6,4},{7,5},{8,10},{9,11},{10,... | collective-permute-start | bytes 1474568 | tf_op jit(solution)/shard_map/ppermute | solution.py:17
  104.2 37.3 %collective-permute-start.27 = (bf16[1920,128]{1,0:T(8,128)(2,1)}, bf16[1920,128]{1,0:T(8,128)(2,1)}, u32[]{:S(2)}, u32[]{:S(2)}) collective-permute-start(bf16[1920,128]{1,0:T(8,128)(2,1)} %get-tuple-element.462), channel_id=1, source_target_pairs={{0,3},{1,2},{2,1},{3,0},{4,7},{5,6},{6,5},{7,4},{8,11},{9,10},{10,... | collective-permute-start | bytes 1474568 | tf_op jit(solution)/shard_map/ppermute | solution.py:17
  105.4 36.1 %collective-permute-start.28 = (bf16[1920,128]{1,0:T(8,128)(2,1)}, bf16[1920,128]{1,0:T(8,128)(2,1)}, u32[]{:S(2)}, u32[]{:S(2)}) collective-permute-start(bf16[1920,128]{1,0:T(8,128)(2,1)} %get-tuple-element.463), channel_id=1, source_target_pairs={{0,1},{1,0},{2,3},{3,2},{4,5},{5,4},{6,7},{7,6},{8,9},{9,8},{10,11... | collective-permute-start | bytes 1474568 | tf_op jit(solution)/shard_map/ppermute | solution.py:17
  105.6 11.4 %collective-permute-start.3 = (bf16[1920,128]{1,0:T(8,128)(2,1)S(1)}, bf16[1920,128]{1,0:T(8,128)(2,1)S(1)}, u32[]{:S(2)}, u32[]{:S(2)}) collective-permute-start(bf16[1920,128]{1,0:T(8,128)(2,1)S(1)} %copy.39), channel_id=1, source_target_pairs={{0,8},{4,12},{8,0},{12,4},{1,9},{5,13},{9,1},{13,5},{2,10},{6,14},... | collective-permute-start | bytes 1474568 | tf_op jit(solution)/shard_map/while/body/ppermute | solution.py:17
  107.1 11.0 %collective-permute-start.4 = (bf16[1920,128]{1,0:T(8,128)(2,1)S(1)}, bf16[1920,128]{1,0:T(8,128)(2,1)S(1)}, u32[]{:S(2)}, u32[]{:S(2)}) collective-permute-start(bf16[1920,128]{1,0:T(8,128)(2,1)S(1)} %copy.39), channel_id=1, source_target_pairs={{0,16},{16,0},{1,17},{17,1},{2,18},{18,2},{3,19},{19,3},{4,20},{20... | collective-permute-start | bytes 1474568 | tf_op jit(solution)/shard_map/while/body/ppermute | solution.py:17
  119.2 13.7 %collective-permute-start.6 = (bf16[1920,256]{1,0:T(8,128)(2,1)}, bf16[1920,256]{1,0:T(8,128)(2,1)}, u32[]{:S(2)}, u32[]{:S(2)}) collective-permute-start(bf16[1920,256]{1,0:T(8,128)(2,1)} %pad_maximum_fusion.18), channel_id=1, source_target_pairs={{0,4},{4,0},{8,12},{12,8},{1,5},{5,1},{9,13},{13,9},{2,6},{6,2},{1... | collective-permute-start | bytes 2949128 | tf_op jit(solution)/shard_map/while/body/ppermute | solution.py:17
  119.2 13.7 %collective-permute-start.5 = (bf16[1920,128]{1,0:T(8,128)(2,1)S(1)}, bf16[1920,128]{1,0:T(8,128)(2,1)}, u32[]{:S(2)}, u32[]{:S(2)}) collective-permute-start(bf16[1920,128]{1,0:T(8,128)(2,1)S(1)} %collective-permute-done.4), channel_id=1, source_target_pairs={{0,8},{4,12},{8,0},{12,4},{1,9},{5,13},{9,1},{13,5},{2,10},{6,14},... | collective-permute-start | bytes 1474568 | tf_op jit(solution)/shard_map/while/body/ppermute | solution.py:17
  134.2 5.2 %collective-permute-start.7 = (bf16[1920,256]{1,0:T(8,128)(2,1)S(1)}, bf16[1920,256]{1,0:T(8,128)(2,1)S(1)}, u32[]{:S(2)}, u32[]{:S(2)}) collective-permute-start(bf16[1920,256]{1,0:T(8,128)(2,1)S(1)} %pad_maximum_fusion.19), channel_id=1, source_target_pairs={{0,4},{4,0},{8,12},{12,8},{1,5},{5,1},{9,13},{13,9},{2,6},{6,2},{1... | collective-permute-start | bytes 2949128 | tf_op jit(solution)/shard_map/while/body/ppermute | solution.py:17
  143.4 20.1 %copy-start.1 = (bf16[1920,128]{1,0:T(8,128)(2,1)}, bf16[1920,128]{1,0:T(8,128)(2,1)S(1)}, u32[]{:S(2)}) copy-start(bf16[1920,128]{1,0:T(8,128)(2,1)S(1)} %add_convert_fusion) | copy-start | bytes 1474564
  143.4 14.6 %collective-permute-start.30 = (bf16[1920,128]{1,0:T(8,128)(2,1)S(1)}, bf16[1920,128]{1,0:T(8,128)(2,1)S(1)}, u32[]{:S(2)}, u32[]{:S(2)}) collective-permute-start(bf16[1920,128]{1,0:T(8,128)(2,1)S(1)} %add_convert_fusion), channel_id=1, source_target_pairs={{0,8},{4,12},{8,0},{12,4},{1,9},{5,13},{9,1},{13,5},{2,10},{6,14},... | collective-permute-start | bytes 1474568 | tf_op jit(solution)/shard_map/ppermute | solution.py:17
  144.1 13.9 %collective-permute-start.31 = (bf16[1920,128]{1,0:T(8,128)(2,1)S(1)}, bf16[1920,128]{1,0:T(8,128)(2,1)}, u32[]{:S(2)}, u32[]{:S(2)}) collective-permute-start(bf16[1920,128]{1,0:T(8,128)(2,1)S(1)} %add_convert_fusion), channel_id=1, source_target_pairs={{0,16},{16,0},{1,17},{17,1},{2,18},{18,2},{3,19},{19,3},{4,20},{20... | collective-permute-start | bytes 1474568 | tf_op jit(solution)/shard_map/ppermute | solution.py:17
  145.6 12.5 %collective-permute-start.29 = (bf16[12,48,256]{2,1,0:T(8,128)(2,1)S(1)}, bf16[12,48,256]{2,1,0:T(8,128)(2,1)S(1)}, u32[]{:S(2)}, u32[]{:S(2)}) collective-permute-start(bf16[12,48,256]{2,1,0:T(8,128)(2,1)S(1)} %copy-done.11), channel_id=1, source_target_pairs={{0,1},{1,2},{2,3},{3,0},{4,5},{5,6},{6,7},{7,4},{8,9},{9,10},{10,1... | collective-permute-start | bytes 884744 | tf_op jit(solution)/shard_map/ppermute | solution.py:13
  158.9 27.5 %collective-permute-start.32 = (bf16[12,48,256]{2,1,0:T(8,128)(2,1)}, bf16[12,48,256]{2,1,0:T(8,128)(2,1)}, u32[]{:S(2)}, u32[]{:S(2)}) collective-permute-start(bf16[12,48,256]{2,1,0:T(8,128)(2,1)} %broadcast_select_fusion.13.rows), channel_id=1, source_target_pairs={{0,2},{1,3},{2,0},{3,1},{4,6},{5,7},{6,4},{7,5},{8,10},{9,11},{10,... | collective-permute-start | bytes 884744 | tf_op jit(solution)/shard_map/ppermute | solution.py:13
  165.9 9.0 %collective-permute-start.10 = (bf16[1920,256]{1,0:T(8,128)(2,1)S(1)}, bf16[1920,256]{1,0:T(8,128)(2,1)S(1)}, u32[]{:S(2)}, u32[]{:S(2)}) collective-permute-start(bf16[1920,256]{1,0:T(8,128)(2,1)S(1)} %pad_maximum_fusion.21), channel_id=1, source_target_pairs={{0,4},{4,0},{8,12},{12,8},{1,5},{5,1},{9,13},{13,9},{2,6},{6,2},{1... | collective-permute-start | bytes 2949128 | tf_op jit(solution)/shard_map/while/body/ppermute | solution.py:17
  166.0 8.4 %collective-permute-start.9 = (bf16[960,128]{1,0:T(8,128)(2,1)S(1)}, bf16[960,128]{1,0:T(8,128)(2,1)S(1)}, u32[]{:S(2)}, u32[]{:S(2)}) collective-permute-start(bf16[960,128]{1,0:T(8,128)(2,1)S(1)} %slice.115), channel_id=1, source_target_pairs={{0,8},{4,12},{8,0},{12,4},{1,9},{5,13},{9,1},{13,5},{2,10},{6,14},... | collective-permute-start | bytes 737288 | tf_op jit(solution)/shard_map/while/body/ppermute | solution.py:17
  166.7 8.1 %collective-permute-start.8 = (bf16[960,128]{1,0:T(8,128)(2,1)S(1)}, bf16[960,128]{1,0:T(8,128)(2,1)S(1)}, u32[]{:S(2)}, u32[]{:S(2)}) collective-permute-start(bf16[960,128]{1,0:T(8,128)(2,1)S(1)} %slice.114), channel_id=1, source_target_pairs={{0,16},{16,0},{1,17},{17,1},{2,18},{18,2},{3,19},{19,3},{4,20},{20... | collective-permute-start | bytes 737288 | tf_op jit(solution)/shard_map/while/body/ppermute | solution.py:17
  177.0 6.3 %collective-permute-start.11 = (bf16[1920,256]{1,0:T(8,128)(2,1)}, bf16[1920,256]{1,0:T(8,128)(2,1)}, u32[]{:S(2)}, u32[]{:S(2)}) collective-permute-start(bf16[1920,256]{1,0:T(8,128)(2,1)} %pad_maximum_fusion.22), channel_id=1, source_target_pairs={{0,4},{4,0},{8,12},{12,8},{1,5},{5,1},{9,13},{13,9},{2,6},{6,2},{1... | collective-permute-start | bytes 2949128 | tf_op jit(solution)/shard_map/while/body/ppermute | solution.py:17
  186.4 11.4 %collective-permute-start.33 = (bf16[12,48,256]{2,1,0:T(8,128)(2,1)}, bf16[12,48,256]{2,1,0:T(8,128)(2,1)S(1)}, u32[]{:S(2)}, u32[]{:S(2)}) collective-permute-start(bf16[12,48,256]{2,1,0:T(8,128)(2,1)} %get-tuple-element.486), channel_id=1, source_target_pairs={{0,1},{1,2},{2,3},{3,0},{4,5},{5,6},{6,7},{7,4},{8,9},{9,10},{10,1... | collective-permute-start | bytes 884744 | tf_op jit(solution)/shard_map/ppermute | solution.py:13
  198.9 14.9 %copy-start.9 = (bf16[12,48,256]{2,1,0:T(8,128)(2,1)}, bf16[12,48,256]{2,1,0:T(8,128)(2,1)S(1)}, u32[]{:S(2)}) copy-start(bf16[12,48,256]{2,1,0:T(8,128)(2,1)S(1)} %broadcast_select_fusion.12.rows) | copy-start | bytes 884740
  198.9 14.9 %collective-permute-start.37 = (bf16[12,48,256]{2,1,0:T(8,128)(2,1)S(1)}, bf16[12,48,256]{2,1,0:T(8,128)(2,1)S(1)}, u32[]{:S(2)}, u32[]{:S(2)}) collective-permute-start(bf16[12,48,256]{2,1,0:T(8,128)(2,1)S(1)} %broadcast_select_fusion.12.rows), channel_id=1, source_target_pairs={{0,2},{1,3},{2,0},{3,1},{4,6},{5,7},{6,4},{7,5},{8,10},{9,11},{10,... | collective-permute-start | bytes 884744 | tf_op jit(solution)/shard_map/ppermute | solution.py:13
  199.0 1.9 collective-permute-start.34
  199.0 5.9 %collective-permute-start.35 = (bf16[4,48,256]{2,1,0:T(8,128)(2,1)}, bf16[4,48,256]{2,1,0:T(8,128)(2,1)S(1)}, u32[]{:S(2)}, u32[]{:S(2)}) collective-permute-start(bf16[4,48,256]{2,1,0:T(8,128)(2,1)} %get-tuple-element.494), channel_id=1, source_target_pairs={{0,8},{4,12},{8,0},{12,4},{1,9},{5,13},{9,1},{13,5},{2,10},{6,14},... | collective-permute-start | bytes 294920 | tf_op jit(solution)/shard_map/ppermute | solution.py:17
  200.5 5.6 %collective-permute-start.36 = (bf16[4,48,256]{2,1,0:T(8,128)(2,1)}, bf16[4,48,256]{2,1,0:T(8,128)(2,1)S(1)}, u32[]{:S(2)}, u32[]{:S(2)}) collective-permute-start(bf16[4,48,256]{2,1,0:T(8,128)(2,1)} %get-tuple-element.495), channel_id=1, source_target_pairs={{0,12},{4,8},{8,4},{12,0},{1,13},{5,9},{9,5},{13,1},{2,14},{6,10},... | collective-permute-start | bytes 294920 | tf_op jit(solution)/shard_map/ppermute | solution.py:17
  200.9 22.8 %copy-start.15 = (bf16[4,48,256]{2,1,0:T(8,128)(2,1)}, bf16[4,48,256]{2,1,0:T(8,128)(2,1)S(1)}, u32[]{:S(2)}) copy-start(bf16[4,48,256]{2,1,0:T(8,128)(2,1)S(1)} %collective-permute-done.34.refs_1_) | copy-start | bytes 294916
  204.9 18.8 %copy-start.16 = (bf16[4,48,256]{2,1,0:T(8,128)(2,1)}, bf16[4,48,256]{2,1,0:T(8,128)(2,1)S(1)}, u32[]{:S(2)}) copy-start(bf16[4,48,256]{2,1,0:T(8,128)(2,1)S(1)} %collective-permute-done.35.refs_2_) | copy-start | bytes 294916
  206.1 17.6 %copy-start.17 = (bf16[4,48,256]{2,1,0:T(8,128)(2,1)}, bf16[4,48,256]{2,1,0:T(8,128)(2,1)S(1)}, u32[]{:S(2)}) copy-start(bf16[4,48,256]{2,1,0:T(8,128)(2,1)S(1)} %collective-permute-done.36.refs_3_) | copy-start | bytes 294916
  216.6 1.9 collective-permute-start.38
  216.6 5.8 %collective-permute-start.39 = (bf16[4,48,256]{2,1,0:T(8,128)(2,1)}, bf16[4,48,256]{2,1,0:T(8,128)(2,1)S(1)}, u32[]{:S(2)}, u32[]{:S(2)}) collective-permute-start(bf16[4,48,256]{2,1,0:T(8,128)(2,1)} %get-tuple-element.504), channel_id=1, source_target_pairs={{0,8},{4,12},{8,0},{12,4},{1,9},{5,13},{9,1},{13,5},{2,10},{6,14},... | collective-permute-start | bytes 294920 | tf_op jit(solution)/shard_map/ppermute | solution.py:17
  218.0 5.7 %collective-permute-start.40 = (bf16[4,48,256]{2,1,0:T(8,128)(2,1)}, bf16[4,48,256]{2,1,0:T(8,128)(2,1)S(1)}, u32[]{:S(2)}, u32[]{:S(2)}) collective-permute-start(bf16[4,48,256]{2,1,0:T(8,128)(2,1)} %get-tuple-element.505), channel_id=1, source_target_pairs={{0,12},{4,8},{8,4},{12,0},{1,13},{5,9},{9,5},{13,1},{2,14},{6,10},... | collective-permute-start | bytes 294920 | tf_op jit(solution)/shard_map/ppermute | solution.py:17
  (21 other events, 116.6 us)

commit v19 on v17

--- a/solution.py
+++ b/solution.py
@@ -311,7 +311,7 @@
     pair = plus(kept_rest, arrived)
     pair = step(pair)
     mirrored = over_middle(pair[:, width:].astype(jnp.bfloat16))
-    pair, mirrored, value_terms = step((pair, mirrored, value_terms))
+    pair, mirrored = step((pair, mirrored))
     blocks = [plus(own, second, mirror, first[:direct]), plus(pair[:, :width], mirrored)]
     own = jnp.concatenate([block.astype(jnp.bfloat16) for block in blocks], axis=0)
 

time: 222 us -> 236 us (1.063)
  starting transfers between devices: 57.2 us -> 72.9 us
    ppermute x4, starting transfers between devices: 14 us -> 29.9 us  [shifted_2(): lax.ppermute(shard, axis, [(i, (i + by) % count) for i in range(count)])]
  transfers between devices with their start and end apart: 41 -> 41, of which waited for: 18 -> 18; matrix products, arithmetic and copies ran while one was open for 13% -> 12% of each run, Pallas kernels for 7% -> 7%
where the time goes in v19:
time: 236 us; the launch traced here: 235 us
  waiting for transfers between devices  97.6 us (41%)
  starting transfers between devices  72.9 us (31%)
  local copies, waits for them, and re-layouts  22.9 us (10%)
  Pallas kernels  15.7 us (7%)
  other arithmetic  14.9 us (6%)
  matrix products  9.93 us (4%)
    ppermute x32, waiting for transfers between devices, swapped(): lax.ppermute(shard, axis, [(i, i ^ bit) for i in range(lax.axis_size(axis...  61.6 us
    ppermute x32, starting transfers between devices, swapped(): lax.ppermute(shard, axis, [(i, i ^ bit) for i in range(lax.axis_size(axis...  34 us
    ppermute x4, starting transfers between devices, shifted_2(): lax.ppermute(shard, axis, [(i, (i + by) % count) for i in range(count)])  29.9 us
    ppermute x4, waiting for transfers between devices, shifted_2(): lax.ppermute(shard, axis, [(i, (i + by) % count) for i in range(count)])  21.6 us
    pallas_call x2, Pallas kernels, product_terms(): pl.pallas_call(terms_body, out_shape=shapes, grid_spec=pltpu.PrefetchScal...  15.7 us
    ppermute x5, waiting for transfers between devices, moved(): return lax.ppermute(shard, ('tile', 'head'), pairs)  14.5 us
    dot_general x11, matrix products, add_columns(): return jnp.dot(operand, portion, preferred_element_type=jnp.float32)  9.74 us
    ppermute x5, starting transfers between devices, moved(): return lax.ppermute(shard, ('tile', 'head'), pairs)  9.02 us
  transfers between devices with their start and end apart: 41, of which 18 were waited for; matrix products, arithmetic and copies ran while one was open for 12% of the time, Pallas kernels for 7%

profile of v19, /device:TPU:0, one launch (start us, length us, event | category | flops | bytes accessed | tf_op | source)
XLA Modules:
  0.0 235.5 jit_solution(5365134115128524683)
XLA Ops:
  0.0 3.0 %fusion.23 = (bf16[1024,128]{1,0:T(8,128)(2,1)S(1)}, bf16[1024,128]{1,0:T(8,128)(2,1)}, bf16[1024,128]{1,0:T(8,128)(2,1)S(1)}, bf16[1024,128]{1,0:T(8,128)(2,1)S(1)}) fusion(bf16[2048,512]{1,0:T(8,128)(2,1)} %param.17, s32[]{:T(128)S(6)} %select_n.304, s32[]{:T(128)S(6)} %select_n.309, s32[]{:T(128)S(6)} %select_n.300, s32[]{:T(128)S(6)} %select_n.302), kind=kLoop, calls=%fused_computation.124 | loop fusion | bytes 2097168 | tf_op jit(solution)/shard_map/dynamic_slice | solution.py:248
  3.0 2.9 %collective-permute-start.12 = (bf16[1024,128]{1,0:T(8,128)(2,1)S(1)}, bf16[1024,128]{1,0:T(8,128)(2,1)S(1)}, u32[]{:S(2)}, u32[]{:S(2)}) collective-permute-start(bf16[1024,128]{1,0:T(8,128)(2,1)S(1)} %get-tuple-element.577), channel_id=1, source_target_pairs={{0,8},{4,12},{8,0},{12,4},{1,9},{5,13},{9,1},{13,5},{2,10},{6,14},... | collective-permute-start | bytes 786440 | tf_op jit(solution)/shard_map/ppermute | solution.py:17
  6.0 1.3 collective-permute-start.13
  7.3 4.7 %collective-permute-start.16 = (bf16[1024,128]{1,0:T(8,128)(2,1)S(1)}, bf16[1024,128]{1,0:T(8,128)(2,1)S(1)}, u32[]{:S(2)}, u32[]{:S(2)}) collective-permute-start(bf16[1024,128]{1,0:T(8,128)(2,1)S(1)} %get-tuple-element.575), channel_id=1, source_target_pairs={{0,8},{4,12},{8,0},{12,4},{1,9},{5,13},{9,1},{13,5},{2,10},{6,14},... | collective-permute-start | bytes 786440 | tf_op jit(solution)/shard_map/ppermute | solution.py:17
  14.0 4.3 %collective-permute-start.15 = (bf16[1024,128]{1,0:T(8,128)(2,1)S(1)}, bf16[1024,128]{1,0:T(8,128)(2,1)S(1)}, u32[]{:S(2)}, u32[]{:S(2)}) collective-permute-start(bf16[1024,128]{1,0:T(8,128)(2,1)S(1)} %get-tuple-element.585), channel_id=1, source_target_pairs={{0,2},{1,6},{2,4},{3,0},{4,3},{5,7},{6,5},{7,1},{8,10},{9,14},{10,... | collective-permute-start | bytes 786440 | tf_op jit(solution)/shard_map/ppermute | solution.py:165
  18.8 10.8 %collective-permute-done.15 = bf16[1024,128]{1,0:T(8,128)(2,1)S(1)} collective-permute-done((bf16[1024,128]{1,0:T(8,128)(2,1)S(1)}, bf16[1024,128]{1,0:T(8,128)(2,1)S(1)}, u32[]{:S(2)}, u32[]{:S(2)}) %collective-permute-start.15) | collective-permute-done | bytes 262176 | tf_op jit(solution)/shard_map/ppermute | solution.py:165
  30.8 7.1 %constant_dynamic-slice_fusion = (bf16[576,1920]{1,0:T(8,128)(2,1)}, bf16[576,1920]{1,0:T(8,128)(2,1)}, bf16[576,1920]{1,0:T(8,128)(2,1)}, bf16[576,1920]{1,0:T(8,128)(2,1)}) fusion(bf16[576,7680]{1,0:T(8,128)(2,1)} %bitcast.134, s32[]{:T(128)S(6)} %select_n.313, s32[]{:T(128)S(6)} %select_n.312, s32[]{:T(128)S(6)} %select_n.311, s32[]{:T(128)S(6)} %select_n.310), kind=kLoop, calls=%fused_computation.115 | loop fusion | bytes 17694736 | tf_op jit(solution)/shard_map/dynamic_slice | solution.py:171
  38.0 5.8 %collective-permute-done.17 = bf16[1024,256]{1,0:T(8,128)(2,1)S(1)} collective-permute-done((bf16[1024,256]{1,0:T(8,128)(2,1)S(1)}, bf16[1024,256]{1,0:T(8,128)(2,1)S(1)}, u32[]{:S(2)}, u32[]{:S(2)}) %collective-permute-start.17) | collective-permute-done | bytes 524320 | tf_op jit(solution)/shard_map/ppermute | solution.py:17
  45.5 2.0 collective-permute-start.20
  47.6 7.7 %shard_map.82 = (f32[1280,128]{1,0:T(8,128)S(1)}, bf16[1280,128]{1,0:T(8,128)(2,1)}, bf16[1280,128]{1,0:T(8,128)(2,1)}, bf16[2560,128]{1,0:T(8,128)(2,1)}, f32[640,256]{1,0:T(8,128)S(1)}) custom-call(s32[1]{0:T(128)} %bitcast.11.choice, bf16[1920,2048]{1,0:T(8,128)(2,1)} %weight.1, bf16[2048,256]{1,0:T(8,128)(2,1)S(1)} %pad_maximum_fusion.7.near, ...), custom_call_target="tpu_custom_call" | custom-call | flops 4026531840 | bytes 12419072 | tf_op jit(solution)/shard_map/pallas_call | solution.py:118
  55.3 3.7 %collective-permute-done.20 = bf16[1024,128]{1,0:T(8,128)(2,1)S(1)} collective-permute-done((bf16[1024,128]{1,0:T(8,128)(2,1)S(1)}, bf16[1024,128]{1,0:T(8,128)(2,1)S(1)}, u32[]{:S(2)}, u32[]{:S(2)}) %collective-permute-start.20) | collective-permute-done | bytes 262176 | tf_op jit(solution)/shard_map/ppermute | solution.py:165
  61.1 2.8 %collective-permute-start.23 = (bf16[1280,128]{1,0:T(8,128)(2,1)}, bf16[1280,128]{1,0:T(8,128)(2,1)}, u32[]{:S(2)}, u32[]{:S(2)}) collective-permute-start(bf16[1280,128]{1,0:T(8,128)(2,1)} %get-tuple-element.425), channel_id=1, source_target_pairs={{0,3},{1,2},{2,1},{3,0},{4,7},{5,6},{6,5},{7,4},{8,11},{9,10},{10,... | collective-permute-start | bytes 983048 | tf_op jit(solution)/shard_map/ppermute | solution.py:17
  64.8 26.8 %while.54 = (s32[]{:T(128)}, bf16[1024,256]{1,0:T(8,128)(2,1)}, f32[1,512]{1,0:T(1,128)S(1)}, f32[1920,128]{1,0:T(8,128)}, bf16[1920,128]{1,0:T(8,128)(2,1)}, /*...) while((s32[]{:T(128)}, bf16[1024,256]{1,0:T(8,128)(2,1)}, ...), condition=%wide.region_3.4_spmd, body=%wide.region_2.3_spmd.sunk | while | flops 4029153792 | bytes 23972084 | solution.py:203
  66.5 1.3 collective-permute-start.1
  67.8 11.8 %collective-permute-done.1 = f32[1,512]{1,0:T(1,128)S(1)} collective-permute-done((f32[1,512]{1,0:T(1,128)S(1)}, f32[1,512]{1,0:T(1,128)S(1)}, u32[]{:S(2)}, u32[]{:S(2)}) %collective-permute-start.1) | collective-permute-done | bytes 2080 | tf_op jit(solution)/shard_map/while/body/ppermute | solution.py:17
  81.5 2.1 collective-permute-done.2.far
  83.6 8.0 %body.1 = (f32[1920,128]{1,0:T(8,128)}, bf16[1920,128]{1,0:T(8,128)(2,1)}, bf16[1920,128]{1,0:T(8,128)(2,1)}, bf16[1920,128]{1,0:T(8,128)(2,1)}) custom-call(s32[1]{0:T(128)} %get-tuple-element.919.choice, bf16[1920,2048]{1,0:T(8,128)(2,1)} %get-tuple-element.920.weight, bf16[2048,256]{1,0:T(8,128)(2,1)S(1)} %pad_maximum_fusion.18.near, ...), custom_call_target="tpu_custom_call" | custom-call | flops 4026531840 | bytes 12419072 | tf_op jit(solution)/shard_map/while/body/pallas_call | solution.py:118
  92.8 1.9 collective-permute-start.28
  95.4 1.7 collective-permute-start.26
  98.1 1.3 add_convert_fusion.1
  99.5 2.3 collective-permute-done.28
  101.9 34.4 %while.55 = (s32[]{:T(128)}, bf16[1920,128]{1,0:T(8,128)(2,1)S(1)}, bf16[12,48,256]{2,1,0:T(8,128)(2,1)}, s32[]{:T(128)}, pred[]{:T(512)}, /*index=5*/bf16[576,1...) while((s32[]{:T(128)}, bf16[1920,128]{1,0:T(8,128)(2,1)S(1)}, ...), condition=%wide.region_7.8_spmd, body=%wide.region_4.7_spmd.sunk | while | flops 2271905024 | bytes 76995496 | solution.py:203
  102.0 1.5 collective-permute-start.3
  103.4 1.4 collective-permute-start.4
  104.8 8.8 %collective-permute-done.3 = bf16[1920,128]{1,0:T(8,128)(2,1)S(1)} collective-permute-done((bf16[1920,128]{1,0:T(8,128)(2,1)S(1)}, bf16[1920,128]{1,0:T(8,128)(2,1)S(1)}, u32[]{:S(2)}, u32[]{:S(2)}) %collective-permute-start.3) | collective-permute-done | bytes 491552 | tf_op jit(solution)/shard_map/while/body/ppermute | solution.py:17
  115.7 13.0 %collective-permute-done.5 = bf16[1920,128]{1,0:T(8,128)(2,1)S(1)} collective-permute-done((bf16[1920,128]{1,0:T(8,128)(2,1)S(1)}, bf16[1920,128]{1,0:T(8,128)(2,1)S(1)}, u32[]{:S(2)}, u32[]{:S(2)}) %collective-permute-start.5) | collective-permute-done | bytes 491552 | tf_op jit(solution)/shard_map/while/body/ppermute | solution.py:17
  130.5 2.1 convolution_add_fusion.10
  136.4 1.6 add_convert_fusion
  138.7 1.4 collective-permute-start.31
  140.3 22.4 %collective-permute-start.29 = (bf16[12,48,256]{2,1,0:T(8,128)(2,1)S(1)}, bf16[12,48,256]{2,1,0:T(8,128)(2,1)S(1)}, u32[]{:S(2)}, u32[]{:S(2)}) collective-permute-start(bf16[12,48,256]{2,1,0:T(8,128)(2,1)S(1)} %copy-done.12), channel_id=1, source_target_pairs={{0,1},{1,2},{2,3},{3,0},{4,5},{5,6},{6,7},{7,4},{8,9},{9,10},{10,1... | collective-permute-start | bytes 884744 | tf_op jit(solution)/shard_map/ppermute | solution.py:13
  162.9 6.2 %collective-permute-done.29 = bf16[12,48,256]{2,1,0:T(8,128)(2,1)S(1)} collective-permute-done((bf16[12,48,256]{2,1,0:T(8,128)(2,1)S(1)}, bf16[12,48,256]{2,1,0:T(8,128)(2,1)S(1)}, u32[]{:S(2)}, u32[]{:S(2)}) %collective-permute-start.29) | collective-permute-done | bytes 294944 | tf_op jit(solution)/shard_map/ppermute | solution.py:13
  169.9 7.4 %collective-permute-start.32 = (bf16[12,48,256]{2,1,0:T(8,128)(2,1)}, bf16[12,48,256]{2,1,0:T(8,128)(2,1)}, u32[]{:S(2)}, u32[]{:S(2)}) collective-permute-start(bf16[12,48,256]{2,1,0:T(8,128)(2,1)} %broadcast_select_fusion.15), channel_id=1, source_target_pairs={{0,2},{1,3},{2,0},{3,1},{4,6},{5,7},{6,4},{7,5},{8,10},{9,11},{10,... | collective-permute-start | bytes 884744 | tf_op jit(solution)/shard_map/ppermute | solution.py:13
  177.3 20.1 %while.56 = (s32[]{:T(128)}, bf16[1920,128]{1,0:T(8,128)(2,1)S(1)}, bf16[1920,128]{1,0:T(8,128)(2,1)S(1)}, bf16[1920,128]{1,0:T(8,128)(2,1)S(1)}, bf16[12,48,256...) while((s32[]{:T(128)}, bf16[1920,128]{1,0:T(8,128)(2,1)S(1)}, ...), condition=%wide.region_9.10_spmd, body=%wide.region_8.9_spmd.sunk | while | flops 2271166464 | bytes 77368712 | solution.py:203
  178.3 1.4 collective-permute-start.9
  180.4 1.4 collective-permute-start.8
  181.8 5.1 %collective-permute-done.9 = bf16[960,128]{1,0:T(8,128)(2,1)S(1)} collective-permute-done((bf16[960,128]{1,0:T(8,128)(2,1)}, bf16[960,128]{1,0:T(8,128)(2,1)S(1)}, u32[]{:S(2)}, u32[]{:S(2)}) %collective-permute-start.9) | collective-permute-done | bytes 245792 | tf_op jit(solution)/shard_map/while/body/ppermute | solution.py:17
  186.9 1.8 collective-permute-done.8
  189.1 1.3 copy-done.8
  192.0 2.1 convolution_add_fusion.12
  197.4 1.2 broadcast_select_fusion.13
  199.7 9.3 %collective-permute-done.33 = bf16[12,48,256]{2,1,0:T(8,128)(2,1)S(1)} collective-permute-done((bf16[12,48,256]{2,1,0:T(8,128)(2,1)S(1)}, bf16[12,48,256]{2,1,0:T(8,128)(2,1)S(1)}, u32[]{:S(2)}, u32[]{:S(2)}) %collective-permute-start.33) | collective-permute-done | bytes 294944 | tf_op jit(solution)/shard_map/ppermute | solution.py:13
  211.1 3.8 %collective-permute-done.35 = bf16[4,48,2,1,128]{4,2,1,0,3:T(2,128)(2,1)S(1)} collective-permute-done((bf16[4,48,2,1,128]{4,2,1,0,3:T(2,128)(2,1)S(1)}, bf16[4,48,2,1,128]{4,2,1,0,3:T(2,128)(2,1)S(1)}, u32[]{:S(2)}, u32[]{:S(2)}) %collective-permute-start.35) | collective-permute-done | bytes 98336 | tf_op jit(solution)/shard_map/ppermute | solution.py:17
  214.9 1.2 collective-permute-done.36
  216.1 6.0 %collective-permute-done.37 = bf16[12,48,256]{2,1,0:T(8,128)(2,1)S(1)} collective-permute-done((bf16[12,48,256]{2,1,0:T(8,128)(2,1)S(1)}, bf16[12,48,256]{2,1,0:T(8,128)(2,1)S(1)}, u32[]{:S(2)}, u32[]{:S(2)}) %collective-permute-start.37) | collective-permute-done | bytes 294944 | tf_op jit(solution)/shard_map/ppermute | solution.py:13
  223.9 1.3 collective-permute-start.40
  225.3 3.4 %collective-permute-done.39 = bf16[4,48,2,1,128]{4,2,1,0,3:T(2,128)(2,1)S(1)} collective-permute-done((bf16[4,48,2,1,128]{4,2,1,0,3:T(2,128)(2,1)S(1)}, bf16[4,48,2,1,128]{4,2,1,0,3:T(2,128)(2,1)S(1)}, u32[]{:S(2)}, u32[]{:S(2)}) %collective-permute-start.39) | collective-permute-done | bytes 98336 | tf_op jit(solution)/shard_map/ppermute | solution.py:17
  228.8 1.3 collective-permute-done.40
  233.4 2.1 copy.19
  (172 shorter events, 39.0 us)
Async XLA Ops:
  0.0 18.4 %copy-start = (bf16[2048,512]{1,0:T(8,128)(2,1)S(1)}, bf16[2048,512]{1,0:T(8,128)(2,1)}, u32[]{:S(2)}) copy-start(bf16[2048,512]{1,0:T(8,128)(2,1)} %param.17) | copy-start | bytes 6291460
  0.0 12.0 %copy-start.18 = (s32[4]{0:T(128)S(1)}, s32[4]{0:T(128)}, u32[]{:S(2)}) copy-start(s32[4]{0:T(128)} %param.20) | copy-start | bytes 52
  3.0 10.3 %collective-permute-start.12 = (bf16[1024,128]{1,0:T(8,128)(2,1)S(1)}, bf16[1024,128]{1,0:T(8,128)(2,1)S(1)}, u32[]{:S(2)}, u32[]{:S(2)}) collective-permute-start(bf16[1024,128]{1,0:T(8,128)(2,1)S(1)} %get-tuple-element.577), channel_id=1, source_target_pairs={{0,8},{4,12},{8,0},{12,4},{1,9},{5,13},{9,1},{13,5},{2,10},{6,14},... | collective-permute-start | bytes 786440 | tf_op jit(solution)/shard_map/ppermute | solution.py:17
  6.0 7.3 %collective-permute-start.13 = (bf16[2048]{0:T(1024)(128)(2,1)}, bf16[2048]{0:T(1024)(128)(2,1)S(1)}, u32[]{:S(2)}, u32[]{:S(2)}) collective-permute-start(bf16[2048]{0:T(1024)(128)(2,1)} %param.16), channel_id=1, source_target_pairs={{0,0},{1,4},{2,8},{3,12},{4,1},{5,5},{6,9},{7,13},{8,2},{9,6},{10,... | collective-permute-start | bytes 12296 | tf_op jit(solution)/shard_map/ppermute | solution.py:165
  7.3 11.5 %collective-permute-start.16 = (bf16[1024,128]{1,0:T(8,128)(2,1)S(1)}, bf16[1024,128]{1,0:T(8,128)(2,1)S(1)}, u32[]{:S(2)}, u32[]{:S(2)}) collective-permute-start(bf16[1024,128]{1,0:T(8,128)(2,1)S(1)} %get-tuple-element.575), channel_id=1, source_target_pairs={{0,8},{4,12},{8,0},{12,4},{1,9},{5,13},{9,1},{13,5},{2,10},{6,14},... | collective-permute-start | bytes 786440 | tf_op jit(solution)/shard_map/ppermute | solution.py:17
  13.4 5.4 %collective-permute-start.14 = (bf16[1024,128]{1,0:T(8,128)(2,1)S(1)}, bf16[1024,128]{1,0:T(8,128)(2,1)S(1)}, u32[]{:S(2)}, u32[]{:S(2)}) collective-permute-start(bf16[1024,128]{1,0:T(8,128)(2,1)S(1)} %get-tuple-element.586), channel_id=1, source_target_pairs={{0,0},{1,4},{2,6},{3,2},{4,1},{5,5},{6,7},{7,3},{8,8},{9,12},{10,1... | collective-permute-start | bytes 786440 | tf_op jit(solution)/shard_map/ppermute | solution.py:165
  14.0 15.5 %collective-permute-start.15 = (bf16[1024,128]{1,0:T(8,128)(2,1)S(1)}, bf16[1024,128]{1,0:T(8,128)(2,1)S(1)}, u32[]{:S(2)}, u32[]{:S(2)}) collective-permute-start(bf16[1024,128]{1,0:T(8,128)(2,1)S(1)} %get-tuple-element.585), channel_id=1, source_target_pairs={{0,2},{1,6},{2,4},{3,0},{4,3},{5,7},{6,5},{7,1},{8,10},{9,14},{10,... | collective-permute-start | bytes 786440 | tf_op jit(solution)/shard_map/ppermute | solution.py:165
  18.8 19.2 %copy-start.13 = (bf16[1024,128]{1,0:T(8,128)(2,1)}, bf16[1024,128]{1,0:T(8,128)(2,1)S(1)}, u32[]{:S(2)}) copy-start(bf16[1024,128]{1,0:T(8,128)(2,1)S(1)} %collective-permute-done.16) | copy-start | bytes 786436
  29.7 14.1 %collective-permute-start.17 = (bf16[1024,256]{1,0:T(8,128)(2,1)S(1)}, bf16[1024,256]{1,0:T(8,128)(2,1)S(1)}, u32[]{:S(2)}, u32[]{:S(2)}) collective-permute-start(bf16[1024,256]{1,0:T(8,128)(2,1)S(1)} %constant_dynamic-update-slice_fusion.2), channel_id=1, source_target_pairs={{0,8},{4,12},{8,0},{12,4},{1,9},{5,13},{9,1},{13,5},{2,10},{6,14},... | collective-permute-start | bytes 1572872 | tf_op jit(solution)/shard_map/ppermute | solution.py:17
  44.0 3.6 %collective-permute-start.18 = (bf16[2048,256]{1,0:T(8,128)(2,1)S(1)}, bf16[2048,256]{1,0:T(8,128)(2,1)S(1)}, u32[]{:S(2)}, u32[]{:S(2)}) collective-permute-start(bf16[2048,256]{1,0:T(8,128)(2,1)S(1)} %pad_maximum_fusion.7.near), channel_id=1, source_target_pairs={{0,4},{4,0},{8,12},{12,8},{1,5},{5,1},{9,13},{13,9},{2,6},{6,2},{1... | collective-permute-start | bytes 3145736 | tf_op jit(solution)/shard_map/ppermute | solution.py:17
  44.2 3.3 %collective-permute-start.21 = (f32[1,512]{1,0:T(1,128)S(1)}, f32[1,512]{1,0:T(1,128)S(1)}, u32[]{:S(2)}, u32[]{:S(2)}) collective-permute-start(f32[1,512]{1,0:T(1,128)S(1)} %fusion.29), channel_id=1, source_target_pairs={{0,4},{4,0},{8,12},{12,8},{1,5},{5,1},{9,13},{13,9},{2,6},{6,2},{1... | collective-permute-start | bytes 6152 | tf_op jit(solution)/shard_map/ppermute | solution.py:17
  44.9 10.4 %collective-permute-start.19 = (bf16[1024,128]{1,0:T(8,128)(2,1)S(1)}, bf16[1024,128]{1,0:T(8,128)(2,1)S(1)}, u32[]{:S(2)}, u32[]{:S(2)}) collective-permute-start(bf16[1024,128]{1,0:T(8,128)(2,1)S(1)} %get-tuple-element.584), channel_id=1, source_target_pairs={{0,0},{1,4},{2,6},{3,2},{4,1},{5,5},{6,7},{7,3},{8,8},{9,12},{10,1... | collective-permute-start | bytes 786440 | tf_op jit(solution)/shard_map/ppermute | solution.py:165
  45.5 13.4 %collective-permute-start.20 = (bf16[1024,128]{1,0:T(8,128)(2,1)S(1)}, bf16[1024,128]{1,0:T(8,128)(2,1)S(1)}, u32[]{:S(2)}, u32[]{:S(2)}) collective-permute-start(bf16[1024,128]{1,0:T(8,128)(2,1)S(1)} %get-tuple-element.583), channel_id=1, source_target_pairs={{0,2},{1,6},{2,4},{3,0},{4,3},{5,7},{6,5},{7,1},{8,10},{9,14},{10,... | collective-permute-start | bytes 786440 | tf_op jit(solution)/shard_map/ppermute | solution.py:165
  59.5 32.1 %collective-permute-start.24 = (bf16[2560,128]{1,0:T(8,128)(2,1)}, bf16[2560,128]{1,0:T(8,128)(2,1)}, u32[]{:S(2)}, u32[]{:S(2)}) collective-permute-start(bf16[2560,128]{1,0:T(8,128)(2,1)} %get-tuple-element.426), channel_id=1, source_target_pairs={{0,1},{1,0},{2,3},{3,2},{4,5},{5,4},{6,7},{7,6},{8,9},{9,8},{10,11... | collective-permute-start | bytes 1966088 | tf_op jit(solution)/shard_map/ppermute | solution.py:17
  60.0 31.6 %collective-permute-start.22 = (bf16[1280,128]{1,0:T(8,128)(2,1)}, bf16[1280,128]{1,0:T(8,128)(2,1)}, u32[]{:S(2)}, u32[]{:S(2)}) collective-permute-start(bf16[1280,128]{1,0:T(8,128)(2,1)} %get-tuple-element.424), channel_id=1, source_target_pairs={{0,2},{1,3},{2,0},{3,1},{4,6},{5,7},{6,4},{7,5},{8,10},{9,11},{10,... | collective-permute-start | bytes 983048 | tf_op jit(solution)/shard_map/ppermute | solution.py:17
  61.1 30.6 %collective-permute-start.23 = (bf16[1280,128]{1,0:T(8,128)(2,1)}, bf16[1280,128]{1,0:T(8,128)(2,1)}, u32[]{:S(2)}, u32[]{:S(2)}) collective-permute-start(bf16[1280,128]{1,0:T(8,128)(2,1)} %get-tuple-element.425), channel_id=1, source_target_pairs={{0,3},{1,2},{2,1},{3,0},{4,7},{5,6},{6,5},{7,4},{8,11},{9,10},{10,... | collective-permute-start | bytes 983048 | tf_op jit(solution)/shard_map/ppermute | solution.py:17
  65.8 13.9 %collective-permute-start = (bf16[1024,256]{1,0:T(8,128)(2,1)S(1)}, bf16[1024,256]{1,0:T(8,128)(2,1)}, u32[]{:S(2)}, u32[]{:S(2)}) collective-permute-start(bf16[1024,256]{1,0:T(8,128)(2,1)S(1)} %copy.33), channel_id=1, source_target_pairs={{0,8},{4,12},{8,0},{12,4},{1,9},{5,13},{9,1},{13,5},{2,10},{6,14},... | collective-permute-start | bytes 1572872 | tf_op jit(solution)/shard_map/while/body/ppermute | solution.py:17
  66.5 13.1 %collective-permute-start.1 = (f32[1,512]{1,0:T(1,128)S(1)}, f32[1,512]{1,0:T(1,128)S(1)}, u32[]{:S(2)}, u32[]{:S(2)}) collective-permute-start(f32[1,512]{1,0:T(1,128)S(1)} %copy.34), channel_id=1, source_target_pairs={{0,8},{4,12},{8,0},{12,4},{1,9},{5,13},{9,1},{13,5},{2,10},{6,14},... | collective-permute-start | bytes 6152 | tf_op jit(solution)/shard_map/while/body/ppermute | solution.py:17
  80.9 2.7 %collective-permute-start.2 = (bf16[2048,256]{1,0:T(8,128)(2,1)S(1)}, bf16[2048,256]{1,0:T(8,128)(2,1)S(1)}, u32[]{:S(2)}, u32[]{:S(2)}) collective-permute-start(bf16[2048,256]{1,0:T(8,128)(2,1)S(1)} %pad_maximum_fusion.18.near), channel_id=1, source_target_pairs={{0,4},{4,0},{8,12},{12,8},{1,5},{5,1},{9,13},{13,9},{2,6},{6,2},{1... | collective-permute-start | bytes 3145736 | tf_op jit(solution)/shard_map/while/body/ppermute | solution.py:17
  92.7 9.1 %copy-start.15 = (f32[1,512]{1,0:T(1,128)S(1)}, f32[1,512]{1,0:T(1,128)}, u32[]{:S(2)}) copy-start(f32[1,512]{1,0:T(1,128)} %get-tuple-element.455) | copy-start | bytes 6148
  92.7 9.1 %copy-start.16 = (f32[1,128]{1,0:T(1,128)S(1)}, f32[1,128]{1,0:T(1,128)}, u32[]{:S(2)}) copy-start(f32[1,128]{1,0:T(1,128)} %param.18) | copy-start | bytes 1540
  92.8 9.0 %collective-permute-start.28 = (bf16[640,128]{1,0:T(8,128)(2,1)S(1)}, bf16[640,128]{1,0:T(8,128)(2,1)S(1)}, u32[]{:S(2)}, u32[]{:S(2)}) collective-permute-start(bf16[640,128]{1,0:T(8,128)(2,1)S(1)} %slice.147), channel_id=1, source_target_pairs={{0,3},{1,2},{2,1},{3,0},{4,7},{5,6},{6,5},{7,4},{8,11},{9,10},{10,... | collective-permute-start | bytes 491528 | tf_op jit(solution)/shard_map/ppermute | solution.py:17
  94.6 41.7 %collective-permute-start.25 = (bf16[1920,128]{1,0:T(8,128)(2,1)}, bf16[1920,128]{1,0:T(8,128)(2,1)}, u32[]{:S(2)}, u32[]{:S(2)}) collective-permute-start(bf16[1920,128]{1,0:T(8,128)(2,1)} %get-tuple-element.440), channel_id=1, source_target_pairs={{0,2},{1,3},{2,0},{3,1},{4,6},{5,7},{6,4},{7,5},{8,10},{9,11},{10,... | collective-permute-start | bytes 1474568 | tf_op jit(solution)/shard_map/ppermute | solution.py:17
  95.4 40.9 %collective-permute-start.26 = (bf16[1920,128]{1,0:T(8,128)(2,1)}, bf16[1920,128]{1,0:T(8,128)(2,1)}, u32[]{:S(2)}, u32[]{:S(2)}) collective-permute-start(bf16[1920,128]{1,0:T(8,128)(2,1)} %get-tuple-element.441), channel_id=1, source_target_pairs={{0,3},{1,2},{2,1},{3,0},{4,7},{5,6},{6,5},{7,4},{8,11},{9,10},{10,... | collective-permute-start | bytes 1474568 | tf_op jit(solution)/shard_map/ppermute | solution.py:17
  97.1 39.2 %collective-permute-start.27 = (bf16[1920,128]{1,0:T(8,128)(2,1)}, bf16[1920,128]{1,0:T(8,128)(2,1)}, u32[]{:S(2)}, u32[]{:S(2)}) collective-permute-start(bf16[1920,128]{1,0:T(8,128)(2,1)} %get-tuple-element.442), channel_id=1, source_target_pairs={{0,1},{1,0},{2,3},{3,2},{4,5},{5,4},{6,7},{7,6},{8,9},{9,8},{10,11... | collective-permute-start | bytes 1474568 | tf_op jit(solution)/shard_map/ppermute | solution.py:17
  101.9 34.5 %copy-start.10 = (f32[1920,128]{1,0:T(8,128)S(1)}, f32[1920,128]{1,0:T(8,128)}, u32[]{:S(2)}) copy-start(f32[1920,128]{1,0:T(8,128)} %get-tuple-element.458) | copy-start | bytes 2949124
  102.0 11.6 %collective-permute-start.3 = (bf16[1920,128]{1,0:T(8,128)(2,1)S(1)}, bf16[1920,128]{1,0:T(8,128)(2,1)S(1)}, u32[]{:S(2)}, u32[]{:S(2)}) collective-permute-start(bf16[1920,128]{1,0:T(8,128)(2,1)S(1)} %copy.52), channel_id=1, source_target_pairs={{0,8},{4,12},{8,0},{12,4},{1,9},{5,13},{9,1},{13,5},{2,10},{6,14},... | collective-permute-start | bytes 1474568 | tf_op jit(solution)/shard_map/while/body/ppermute | solution.py:17
  103.4 11.3 %collective-permute-start.4 = (bf16[1920,128]{1,0:T(8,128)(2,1)S(1)}, bf16[1920,128]{1,0:T(8,128)(2,1)S(1)}, u32[]{:S(2)}, u32[]{:S(2)}) collective-permute-start(bf16[1920,128]{1,0:T(8,128)(2,1)S(1)} %copy.52), channel_id=1, source_target_pairs={{0,16},{16,0},{1,17},{17,1},{2,18},{18,2},{3,19},{19,3},{4,20},{20... | collective-permute-start | bytes 1474568 | tf_op jit(solution)/shard_map/while/body/ppermute | solution.py:17
  114.9 13.7 %collective-permute-start.6 = (bf16[1920,256]{1,0:T(8,128)(2,1)S(1)}, bf16[1920,256]{1,0:T(8,128)(2,1)}, u32[]{:S(2)}, u32[]{:S(2)}) collective-permute-start(bf16[1920,256]{1,0:T(8,128)(2,1)S(1)} %pad_maximum_fusion.19), channel_id=1, source_target_pairs={{0,4},{4,0},{8,12},{12,8},{1,5},{5,1},{9,13},{13,9},{2,6},{6,2},{1... | collective-permute-start | bytes 2949128 | tf_op jit(solution)/shard_map/while/body/ppermute | solution.py:17
  115.0 13.6 %collective-permute-start.5 = (bf16[1920,128]{1,0:T(8,128)(2,1)S(1)}, bf16[1920,128]{1,0:T(8,128)(2,1)S(1)}, u32[]{:S(2)}, u32[]{:S(2)}) collective-permute-start(bf16[1920,128]{1,0:T(8,128)(2,1)S(1)} %collective-permute-done.4), channel_id=1, source_target_pairs={{0,8},{4,12},{8,0},{12,4},{1,9},{5,13},{9,1},{13,5},{2,10},{6,14},... | collective-permute-start | bytes 1474568 | tf_op jit(solution)/shard_map/while/body/ppermute | solution.py:17
  115.7 13.2 %copy-start.7 = (bf16[576,1920]{1,0:T(8,128)(2,1)S(1)}, bf16[576,1920]{1,0:T(8,128)(2,1)}, u32[]{:S(2)}) copy-start(bf16[576,1920]{1,0:T(8,128)(2,1)} %get-tuple-element.951) | copy-start | bytes 6635524 | tf_op jit(solution)/shard_map/while
  128.8 4.7 %collective-permute-start.7 = (bf16[1920,256]{1,0:T(8,128)(2,1)S(1)}, bf16[1920,256]{1,0:T(8,128)(2,1)S(1)}, u32[]{:S(2)}, u32[]{:S(2)}) collective-permute-start(bf16[1920,256]{1,0:T(8,128)(2,1)S(1)} %pad_maximum_fusion.20), channel_id=1, source_target_pairs={{0,4},{4,0},{8,12},{12,8},{1,5},{5,1},{9,13},{13,9},{2,6},{6,2},{1... | collective-permute-start | bytes 2949128 | tf_op jit(solution)/shard_map/while/body/ppermute | solution.py:17
  138.0 31.1 %collective-permute-start.30 = (bf16[1920,128]{1,0:T(8,128)(2,1)S(1)}, bf16[1920,128]{1,0:T(8,128)(2,1)S(1)}, u32[]{:S(2)}, u32[]{:S(2)}) collective-permute-start(bf16[1920,128]{1,0:T(8,128)(2,1)S(1)} %add_convert_fusion), channel_id=1, source_target_pairs={{0,8},{4,12},{8,0},{12,4},{1,9},{5,13},{9,1},{13,5},{2,10},{6,14},... | collective-permute-start | bytes 1474568 | tf_op jit(solution)/shard_map/ppermute | solution.py:17
  138.7 30.4 %collective-permute-start.31 = (bf16[1920,128]{1,0:T(8,128)(2,1)S(1)}, bf16[1920,128]{1,0:T(8,128)(2,1)S(1)}, u32[]{:S(2)}, u32[]{:S(2)}) collective-permute-start(bf16[1920,128]{1,0:T(8,128)(2,1)S(1)} %add_convert_fusion), channel_id=1, source_target_pairs={{0,16},{16,0},{1,17},{17,1},{2,18},{18,2},{3,19},{19,3},{4,20},{20... | collective-permute-start | bytes 1474568 | tf_op jit(solution)/shard_map/ppermute | solution.py:17
  140.3 28.8 %collective-permute-start.29 = (bf16[12,48,256]{2,1,0:T(8,128)(2,1)S(1)}, bf16[12,48,256]{2,1,0:T(8,128)(2,1)S(1)}, u32[]{:S(2)}, u32[]{:S(2)}) collective-permute-start(bf16[12,48,256]{2,1,0:T(8,128)(2,1)S(1)} %copy-done.12), channel_id=1, source_target_pairs={{0,1},{1,2},{2,3},{3,0},{4,5},{5,6},{6,7},{7,4},{8,9},{9,10},{10,1... | collective-permute-start | bytes 884744 | tf_op jit(solution)/shard_map/ppermute | solution.py:13
  169.9 27.4 %collective-permute-start.32 = (bf16[12,48,256]{2,1,0:T(8,128)(2,1)}, bf16[12,48,256]{2,1,0:T(8,128)(2,1)}, u32[]{:S(2)}, u32[]{:S(2)}) collective-permute-start(bf16[12,48,256]{2,1,0:T(8,128)(2,1)} %broadcast_select_fusion.15), channel_id=1, source_target_pairs={{0,2},{1,3},{2,0},{3,1},{4,6},{5,7},{6,4},{7,5},{8,10},{9,11},{10,... | collective-permute-start | bytes 884744 | tf_op jit(solution)/shard_map/ppermute | solution.py:13
  177.6 11.2 %collective-permute-start.10 = (bf16[1920,256]{1,0:T(8,128)(2,1)S(1)}, bf16[1920,256]{1,0:T(8,128)(2,1)}, u32[]{:S(2)}, u32[]{:S(2)}) collective-permute-start(bf16[1920,256]{1,0:T(8,128)(2,1)S(1)} %pad_maximum_fusion.22), channel_id=1, source_target_pairs={{0,4},{4,0},{8,12},{12,8},{1,5},{5,1},{9,13},{13,9},{2,6},{6,2},{1... | collective-permute-start | bytes 2949128 | tf_op jit(solution)/shard_map/while/body/ppermute | solution.py:17
  178.3 8.6 %collective-permute-start.9 = (bf16[960,128]{1,0:T(8,128)(2,1)}, bf16[960,128]{1,0:T(8,128)(2,1)S(1)}, u32[]{:S(2)}, u32[]{:S(2)}) collective-permute-start(bf16[960,128]{1,0:T(8,128)(2,1)} %slice.171), channel_id=1, source_target_pairs={{0,8},{4,12},{8,0},{12,4},{1,9},{5,13},{9,1},{13,5},{2,10},{6,14},... | collective-permute-start | bytes 737288 | tf_op jit(solution)/shard_map/while/body/ppermute | solution.py:17
  180.4 8.3 %collective-permute-start.8 = (bf16[960,128]{1,0:T(8,128)(2,1)}, bf16[960,128]{1,0:T(8,128)(2,1)S(1)}, u32[]{:S(2)}, u32[]{:S(2)}) collective-permute-start(bf16[960,128]{1,0:T(8,128)(2,1)} %slice.170), channel_id=1, source_target_pairs={{0,16},{16,0},{1,17},{17,1},{2,18},{18,2},{3,19},{19,3},{4,20},{20... | collective-permute-start | bytes 737288 | tf_op jit(solution)/shard_map/while/body/ppermute | solution.py:17
  189.0 5.9 %collective-permute-start.11 = (bf16[1920,256]{1,0:T(8,128)(2,1)S(1)}, bf16[1920,256]{1,0:T(8,128)(2,1)S(1)}, u32[]{:S(2)}, u32[]{:S(2)}) collective-permute-start(bf16[1920,256]{1,0:T(8,128)(2,1)S(1)} %pad_maximum_fusion.23), channel_id=1, source_target_pairs={{0,4},{4,0},{8,12},{12,8},{1,5},{5,1},{9,13},{13,9},{2,6},{6,2},{1... | collective-permute-start | bytes 2949128 | tf_op jit(solution)/shard_map/while/body/ppermute | solution.py:17
  198.7 10.3 %collective-permute-start.33 = (bf16[12,48,256]{2,1,0:T(8,128)(2,1)S(1)}, bf16[12,48,256]{2,1,0:T(8,128)(2,1)S(1)}, u32[]{:S(2)}, u32[]{:S(2)}) collective-permute-start(bf16[12,48,256]{2,1,0:T(8,128)(2,1)S(1)} %copy-done.11), channel_id=1, source_target_pairs={{0,1},{1,2},{2,3},{3,0},{4,5},{5,6},{6,7},{7,4},{8,9},{9,10},{10,1... | collective-permute-start | bytes 884744 | tf_op jit(solution)/shard_map/ppermute | solution.py:13
  209.1 13.0 %collective-permute-start.37 = (bf16[12,48,256]{2,1,0:T(8,128)(2,1)S(1)}, bf16[12,48,256]{2,1,0:T(8,128)(2,1)S(1)}, u32[]{:S(2)}, u32[]{:S(2)}) collective-permute-start(bf16[12,48,256]{2,1,0:T(8,128)(2,1)S(1)} %broadcast_select_fusion.14), channel_id=1, source_target_pairs={{0,2},{1,3},{2,0},{3,1},{4,6},{5,7},{6,4},{7,5},{8,10},{9,11},{10,... | collective-permute-start | bytes 884744 | tf_op jit(solution)/shard_map/ppermute | solution.py:13
  209.2 1.9 collective-permute-start.34
  209.3 5.7 %collective-permute-start.35 = (bf16[4,48,2,1,128]{4,2,1,0,3:T(2,128)(2,1)S(1)}, bf16[4,48,2,1,128]{4,2,1,0,3:T(2,128)(2,1)S(1)}, u32[]{:S(2)}, u32[]{:S(2)}) collective-permute-start(bf16[4,48,2,1,128]{4,2,1,0,3:T(2,128)(2,1)S(1)} %squeeze.30), channel_id=1, source_target_pairs={{0,8},{4,12},{8,0},{12,4},{1,9},{5,13},{9,1},{13,5},{2,10},{6,14},... | collective-permute-start | bytes 294920 | tf_op jit(solution)/shard_map/ppermute | solution.py:17
  210.0 6.1 %collective-permute-start.36 = (bf16[4,48,2,1,128]{4,2,1,0,3:T(2,128)(2,1)S(1)}, bf16[4,48,2,1,128]{4,2,1,0,3:T(2,128)(2,1)S(1)}, u32[]{:S(2)}, u32[]{:S(2)}) collective-permute-start(bf16[4,48,2,1,128]{4,2,1,0,3:T(2,128)(2,1)S(1)} %squeeze.31), channel_id=1, source_target_pairs={{0,12},{4,8},{8,4},{12,0},{1,13},{5,9},{9,5},{13,1},{2,14},{6,10},... | collective-permute-start | bytes 294920 | tf_op jit(solution)/shard_map/ppermute | solution.py:17
  222.9 2.4 %collective-permute-start.38 = (bf16[4,48,2,1,128]{4,2,1,0,3:T(2,128)(2,1)S(1)}, bf16[4,48,2,1,128]{4,2,1,0,3:T(2,128)(2,1)S(1)}, u32[]{:S(2)}, u32[]{:S(2)}) collective-permute-start(bf16[4,48,2,1,128]{4,2,1,0,3:T(2,128)(2,1)S(1)} %squeeze.33), channel_id=1, source_target_pairs={{0,4},{4,0},{8,12},{12,8},{1,5},{5,1},{9,13},{13,9},{2,6},{6,2},{1... | collective-permute-start | bytes 294920 | tf_op jit(solution)/shard_map/ppermute | solution.py:17
  223.1 5.7 %collective-permute-start.39 = (bf16[4,48,2,1,128]{4,2,1,0,3:T(2,128)(2,1)S(1)}, bf16[4,48,2,1,128]{4,2,1,0,3:T(2,128)(2,1)S(1)}, u32[]{:S(2)}, u32[]{:S(2)}) collective-permute-start(bf16[4,48,2,1,128]{4,2,1,0,3:T(2,128)(2,1)S(1)} %squeeze.34), channel_id=1, source_target_pairs={{0,8},{4,12},{8,0},{12,4},{1,9},{5,13},{9,1},{13,5},{2,10},{6,14},... | collective-permute-start | bytes 294920 | tf_op jit(solution)/shard_map/ppermute | solution.py:17
  223.9 6.1 %collective-permute-start.40 = (bf16[4,48,2,1,128]{4,2,1,0,3:T(2,128)(2,1)S(1)}, bf16[4,48,2,1,128]{4,2,1,0,3:T(2,128)(2,1)S(1)}, u32[]{:S(2)}, u32[]{:S(2)}) collective-permute-start(bf16[4,48,2,1,128]{4,2,1,0,3:T(2,128)(2,1)S(1)} %squeeze.35), channel_id=1, source_target_pairs={{0,12},{4,8},{8,4},{12,0},{1,13},{5,9},{9,5},{13,1},{2,14},{6,10},... | collective-permute-start | bytes 294920 | tf_op jit(solution)/shard_map/ppermute | solution.py:17
  (13 other events, 37.7 us)

commit v20 on v17

--- a/solution.py
+++ b/solution.py
@@ -197,8 +197,6 @@
             block = block + other.astype(jnp.float32)
         return block
 
-    once = jnp.minimum(jnp.max(tile_count), 1)
-
     def in_loop(chain, given, empty):
         return lax.fori_loop(0, once, lambda _, carry: chain(carry[0]), (given, empty))[1]
 
@@ -242,8 +240,8 @@
 
     column, half = group * 2 * head_dim, kv_weight.shape[0] // 2
 
-    def halves(part):
-        mine = lax.dynamic_slice_in_dim(kv_weight, column + part * head_dim, head_dim, axis=1)
+    def halves(weight, part):
+        mine = lax.dynamic_slice_in_dim(weight, column + part * head_dim, head_dim, axis=1)
         ours = lax.dynamic_slice_in_dim(mine, tile // 2 * half, half, axis=0)
         return ours, lax.dynamic_slice_in_dim(mine, half - tile // 2 * half, half, axis=0)
 
@@ -256,15 +254,19 @@
             )
         return pieces
 
-    key_stays, key_leaves = halves(0)
+    key_stays, key_leaves, rows_later = step((*halves(kv_weight, 0), kv_weight))
     bias_rows = moved(proj_bias, lambda t, h: (h, t))
-    key_stays, key_comes, bias_rows = step((key_stays, swapped(key_leaves, "tile", 2), bias_rows))
-
-    value_stays, value_leaves = halves(1)
+    key_stays, key_comes, bias_rows, counts_later = step(
+        (key_stays, swapped(key_leaves, "tile", 2), bias_rows, tile_count)
+    )
+
+    once = jnp.minimum(jnp.max(counts_later), 1)
+
+    value_stays, value_leaves = halves(rows_later, 1)
     tokens = jax.ShapeDtypeStruct((tile_slots, shard_len, 2 * width), jnp.bfloat16)
     shapes = term_shapes(depth, width, True) + [tokens, tokens]
     *no_terms, no_keys, no_values = blank_arrays(shapes)
-    bias_part = add_columns(bias_rows[None], kv_weight)
+    bias_part = add_columns(bias_rows[None], rows_later)
     key_pieces, value_stays, value_comes, bias_part, once = step(
         (
             to_planes(key_stays, key_comes),

time: 222 us -> 222 us (level)
    ppermute x32, starting transfers between devices: 34.2 us -> 36.8 us  [swapped(): lax.ppermute(shard, axis, [(i, i ^ bit) for i in range(lax.axis_size(axis...]
  transfers between devices with their start and end apart: 41 -> 41, of which waited for: 18 -> 19; matrix products, arithmetic and copies ran while one was open for 13% -> 14% of each run, Pallas kernels for 7% -> 7%
where the time goes in v20:
time: 222 us; the launch traced here: 221 us
  waiting for transfers between devices  96.8 us (44%)
  starting transfers between devices  57.9 us (26%)
  local copies, waits for them, and re-layouts  23.9 us (11%)
  Pallas kernels  15.7 us (7%)
  other arithmetic  15.6 us (7%)
  matrix products  9.93 us (4%)
    ppermute x32, waiting for transfers between devices, swapped(): lax.ppermute(shard, axis, [(i, i ^ bit) for i in range(lax.axis_size(axis...  63.6 us
    ppermute x32, starting transfers between devices, swapped(): lax.ppermute(shard, axis, [(i, i ^ bit) for i in range(lax.axis_size(axis...  36.8 us
    ppermute x4, waiting for transfers between devices, shifted_2(): lax.ppermute(shard, axis, [(i, (i + by) % count) for i in range(count)])  20.6 us
    pallas_call x2, Pallas kernels, product_terms(): pl.pallas_call(terms_body, out_shape=shapes, grid_spec=pltpu.PrefetchScal...  15.7 us
    ppermute x4, starting transfers between devices, shifted_2(): lax.ppermute(shard, axis, [(i, (i + by) % count) for i in range(count)])  13.4 us
    ppermute x5, waiting for transfers between devices, moved(): return lax.ppermute(shard, ('tile', 'head'), pairs)  12.6 us
    dot_general x11, matrix products, add_columns(): return jnp.dot(operand, portion, preferred_element_type=jnp.float32)  9.74 us
    ppermute x5, starting transfers between devices, moved(): return lax.ppermute(shard, ('tile', 'head'), pairs)  7.69 us
  transfers between devices with their start and end apart: 41, of which 19 were waited for; matrix products, arithmetic and copies ran while one was open for 14% of the time, Pallas kernels for 7%

profile of v20, /device:TPU:0, one launch (start us, length us, event | category | flops | bytes accessed | tf_op | source)
XLA Modules:
  0.0 221.2 jit_solution(12345151261668597430)
XLA Ops:
  0.0 1.7 fusion.24
  1.7 3.0 %collective-permute-start.12 = (bf16[1024,128]{1,0:T(8,128)(2,1)S(1)}, bf16[1024,128]{1,0:T(8,128)(2,1)S(1)}, u32[]{:S(2)}, u32[]{:S(2)}) collective-permute-start(bf16[1024,128]{1,0:T(8,128)(2,1)S(1)} %get-tuple-element.418), channel_id=1, source_target_pairs={{0,8},{4,12},{8,0},{12,4},{1,9},{5,13},{9,1},{13,5},{2,10},{6,14},... | collective-permute-start | bytes 786440 | tf_op jit(solution)/shard_map/ppermute | solution.py:17
  4.7 1.3 collective-permute-start.13
  6.1 2.3 %fusion.23 = (bf16[1024,128]{1,0:T(8,128)(2,1)S(1)}, bf16[1024,128]{1,0:T(8,128)(2,1)}) fusion(bf16[2048,512]{1,0:T(8,128)(2,1)} %param.17, s32[]{:T(128)S(6)} %select_n.304, s32[]{:T(128)S(6)} %select_n.309, s32[]{:T(128)S(6)} %select_n.300), kind=kLoop, calls=%fused_computation.124 | loop fusion | bytes 1048588 | tf_op jit(solution)/shard_map/dynamic_slice | solution.py:246
  8.3 4.6 %collective-permute-start.16 = (bf16[1024,128]{1,0:T(8,128)(2,1)S(1)}, bf16[1024,128]{1,0:T(8,128)(2,1)S(1)}, u32[]{:S(2)}, u32[]{:S(2)}) collective-permute-start(bf16[1024,128]{1,0:T(8,128)(2,1)S(1)} %get-tuple-element.591), channel_id=1, source_target_pairs={{0,8},{4,12},{8,0},{12,4},{1,9},{5,13},{9,1},{13,5},{2,10},{6,14},... | collective-permute-start | bytes 786440 | tf_op jit(solution)/shard_map/ppermute | solution.py:17
  13.7 1.6 collective-permute-start.14
  15.3 2.3 %collective-permute-start.15 = (bf16[1024,128]{1,0:T(8,128)(2,1)S(1)}, bf16[1024,128]{1,0:T(8,128)(2,1)S(1)}, u32[]{:S(2)}, u32[]{:S(2)}) collective-permute-start(bf16[1024,128]{1,0:T(8,128)(2,1)S(1)} %get-tuple-element.601), channel_id=1, source_target_pairs={{0,2},{1,6},{2,4},{3,0},{4,3},{5,7},{6,5},{7,1},{8,10},{9,14},{10,... | collective-permute-start | bytes 786440 | tf_op jit(solution)/shard_map/ppermute | solution.py:165
  19.8 9.4 %collective-permute-done.15 = bf16[1024,128]{1,0:T(8,128)(2,1)S(1)} collective-permute-done((bf16[1024,128]{1,0:T(8,128)(2,1)S(1)}, bf16[1024,128]{1,0:T(8,128)(2,1)S(1)}, u32[]{:S(2)}, u32[]{:S(2)}) %collective-permute-start.15) | collective-permute-done | bytes 262176 | tf_op jit(solution)/shard_map/ppermute | solution.py:165
  30.4 7.2 %constant_dynamic-slice_fusion = (bf16[576,1920]{1,0:T(8,128)(2,1)}, bf16[576,1920]{1,0:T(8,128)(2,1)}, bf16[576,1920]{1,0:T(8,128)(2,1)}, bf16[576,1920]{1,0:T(8,128)(2,1)}) fusion(bf16[576,7680]{1,0:T(8,128)(2,1)} %bitcast.134, s32[]{:T(128)S(6)} %select_n.313, s32[]{:T(128)S(6)} %select_n.312, s32[]{:T(128)S(6)} %select_n.311, s32[]{:T(128)S(6)} %select_n.310), kind=kLoop, calls=%fused_computation.115 | loop fusion | bytes 17694736 | tf_op jit(solution)/shard_map/dynamic_slice | solution.py:171
  37.6 5.8 %collective-permute-done.17 = bf16[1024,256]{1,0:T(8,128)(2,1)S(1)} collective-permute-done((bf16[1024,256]{1,0:T(8,128)(2,1)S(1)}, bf16[1024,256]{1,0:T(8,128)(2,1)S(1)}, u32[]{:S(2)}, u32[]{:S(2)}) %collective-permute-start.17) | collective-permute-done | bytes 524320 | tf_op jit(solution)/shard_map/ppermute | solution.py:17
  45.1 1.8 collective-permute-start.20
  46.8 7.7 %shard_map.82 = (f32[1280,128]{1,0:T(8,128)S(1)}, bf16[1280,128]{1,0:T(8,128)(2,1)}, bf16[1280,128]{1,0:T(8,128)(2,1)}, bf16[2560,128]{1,0:T(8,128)(2,1)}, f32[640,256]{1,0:T(8,128)S(1)}) custom-call(s32[1]{0:T(128)} %bitcast.11.choice, bf16[1920,2048]{1,0:T(8,128)(2,1)} %weight.1, bf16[2048,256]{1,0:T(8,128)(2,1)S(1)} %pad_maximum_fusion.7.near, ...), custom_call_target="tpu_custom_call" | custom-call | flops 4026531840 | bytes 12419072 | tf_op jit(solution)/shard_map/pallas_call | solution.py:118
  54.5 3.2 %collective-permute-done.20 = bf16[1024,128]{1,0:T(8,128)(2,1)S(1)} collective-permute-done((bf16[1024,128]{1,0:T(8,128)(2,1)S(1)}, bf16[1024,128]{1,0:T(8,128)(2,1)S(1)}, u32[]{:S(2)}, u32[]{:S(2)}) %collective-permute-start.20) | collective-permute-done | bytes 262176 | tf_op jit(solution)/shard_map/ppermute | solution.py:165
  58.3 1.9 collective-permute-start.24
  60.2 1.6 collective-permute-start.22
  63.6 27.7 %while.54 = (s32[]{:T(128)}, bf16[1024,256]{1,0:T(8,128)(2,1)}, f32[1,512]{1,0:T(1,128)S(1)}, f32[1920,128]{1,0:T(8,128)}, bf16[1920,128]{1,0:T(8,128)(2,1)}, /*...) while((s32[]{:T(128)}, bf16[1024,256]{1,0:T(8,128)(2,1)}, ...), condition=%wide.region_3.4_spmd, body=%wide.region_2.3_spmd.sunk | while | flops 4029153792 | bytes 23972084 | solution.py:201
  66.6 12.5 %collective-permute-done.1 = f32[1,512]{1,0:T(1,128)S(1)} collective-permute-done((f32[1,512]{1,0:T(1,128)S(1)}, f32[1,512]{1,0:T(1,128)S(1)}, u32[]{:S(2)}, u32[]{:S(2)}) %collective-permute-start.1) | collective-permute-done | bytes 2080 | tf_op jit(solution)/shard_map/while/body/ppermute | solution.py:17
  81.5 1.7 collective-permute-done.2.far
  83.2 8.0 %body.1 = (f32[1920,128]{1,0:T(8,128)}, bf16[1920,128]{1,0:T(8,128)(2,1)}, bf16[1920,128]{1,0:T(8,128)(2,1)}, bf16[1920,128]{1,0:T(8,128)(2,1)}) custom-call(s32[1]{0:T(128)} %get-tuple-element.935.choice, bf16[1920,2048]{1,0:T(8,128)(2,1)} %get-tuple-element.936.weight, bf16[2048,256]{1,0:T(8,128)(2,1)S(1)} %pad_maximum_fusion.18.near, ...), custom_call_target="tpu_custom_call" | custom-call | flops 4026531840 | bytes 12419072 | tf_op jit(solution)/shard_map/while/body/pallas_call | solution.py:118
  92.4 2.4 %collective-permute-start.25 = (bf16[640,128]{1,0:T(8,128)(2,1)S(1)}, bf16[640,128]{1,0:T(8,128)(2,1)S(1)}, u32[]{:S(2)}, u32[]{:S(2)}) collective-permute-start(bf16[640,128]{1,0:T(8,128)(2,1)S(1)} %slice.147), channel_id=1, source_target_pairs={{0,3},{1,2},{2,1},{3,0},{4,7},{5,6},{6,5},{7,4},{8,11},{9,10},{10,... | collective-permute-start | bytes 491528 | tf_op jit(solution)/shard_map/ppermute | solution.py:17
  94.8 1.3 add_convert_fusion.1
  96.2 4.7 %collective-permute-done.25 = bf16[640,128]{1,0:T(8,128)(2,1)S(1)} collective-permute-done((bf16[640,128]{1,0:T(8,128)(2,1)S(1)}, bf16[640,128]{1,0:T(8,128)(2,1)S(1)}, u32[]{:S(2)}, u32[]{:S(2)}) %collective-permute-start.25) | collective-permute-done | bytes 163872 | tf_op jit(solution)/shard_map/ppermute | solution.py:17
  100.9 3.4 %collective-permute-start.26 = (bf16[1920,128]{1,0:T(8,128)(2,1)}, bf16[1920,128]{1,0:T(8,128)(2,1)}, u32[]{:S(2)}, u32[]{:S(2)}) collective-permute-start(bf16[1920,128]{1,0:T(8,128)(2,1)} %get-tuple-element.458), channel_id=1, source_target_pairs={{0,2},{1,3},{2,0},{3,1},{4,6},{5,7},{6,4},{7,5},{8,10},{9,11},{10,... | collective-permute-start | bytes 1474568 | tf_op jit(solution)/shard_map/ppermute | solution.py:17
  104.3 1.3 collective-permute-start.27
  105.7 33.4 %while.55 = (s32[]{:T(128)}, bf16[1920,128]{1,0:T(8,128)(2,1)S(1)}, bf16[12,48,256]{2,1,0:T(8,128)(2,1)}, s32[]{:T(128)}, pred[]{:T(512)}, /*index=5*/bf16[576,1...) while((s32[]{:T(128)}, bf16[1920,128]{1,0:T(8,128)(2,1)S(1)}, ...), condition=%wide.region_7.8_spmd, body=%wide.region_4.7_spmd.sunk | while | flops 2271905024 | bytes 76995496 | solution.py:201
  106.6 1.5 collective-permute-start.4
  108.1 9.0 %collective-permute-done.3 = bf16[1920,128]{1,0:T(8,128)(2,1)S(1)} collective-permute-done((bf16[1920,128]{1,0:T(8,128)(2,1)S(1)}, bf16[1920,128]{1,0:T(8,128)(2,1)S(1)}, u32[]{:S(2)}, u32[]{:S(2)}) %collective-permute-start.3) | collective-permute-done | bytes 491552 | tf_op jit(solution)/shard_map/while/body/ppermute | solution.py:17
  117.8 1.4 collective-permute-start.5
  119.2 12.3 %collective-permute-done.5 = bf16[1920,128]{1,0:T(8,128)(2,1)S(1)} collective-permute-done((bf16[1920,128]{1,0:T(8,128)(2,1)S(1)}, bf16[1920,128]{1,0:T(8,128)(2,1)S(1)}, u32[]{:S(2)}, u32[]{:S(2)}) %collective-permute-start.5) | collective-permute-done | bytes 491552 | tf_op jit(solution)/shard_map/while/body/ppermute | solution.py:17
  133.4 2.1 convolution_add_fusion.10
  139.2 1.6 add_convert_fusion
  140.8 1.4 collective-permute-start.30
  142.1 1.4 collective-permute-start.31
  143.7 8.0 %collective-permute-start.29 = (bf16[12,48,256]{2,1,0:T(8,128)(2,1)S(1)}, bf16[12,48,256]{2,1,0:T(8,128)(2,1)S(1)}, u32[]{:S(2)}, u32[]{:S(2)}) collective-permute-start(bf16[12,48,256]{2,1,0:T(8,128)(2,1)S(1)} %copy-done.12), channel_id=1, source_target_pairs={{0,1},{1,2},{2,3},{3,0},{4,5},{5,6},{6,7},{7,4},{8,9},{9,10},{10,1... | collective-permute-start | bytes 884744 | tf_op jit(solution)/shard_map/ppermute | solution.py:13
  151.8 5.6 %collective-permute-done.29 = bf16[12,48,256]{2,1,0:T(8,128)(2,1)S(1)} collective-permute-done((bf16[12,48,256]{2,1,0:T(8,128)(2,1)S(1)}, bf16[12,48,256]{2,1,0:T(8,128)(2,1)S(1)}, u32[]{:S(2)}, u32[]{:S(2)}) %collective-permute-start.29) | collective-permute-done | bytes 294944 | tf_op jit(solution)/shard_map/ppermute | solution.py:13
  158.3 4.2 %collective-permute-start.32 = (bf16[12,48,256]{2,1,0:T(8,128)(2,1)}, bf16[12,48,256]{2,1,0:T(8,128)(2,1)}, u32[]{:S(2)}, u32[]{:S(2)}) collective-permute-start(bf16[12,48,256]{2,1,0:T(8,128)(2,1)} %broadcast_select_fusion.15), channel_id=1, source_target_pairs={{0,2},{1,3},{2,0},{3,1},{4,6},{5,7},{6,4},{7,5},{8,10},{9,11},{10,... | collective-permute-start | bytes 884744 | tf_op jit(solution)/shard_map/ppermute | solution.py:13
  162.5 20.0 %while.56 = (s32[]{:T(128)}, bf16[1920,128]{1,0:T(8,128)(2,1)S(1)}, bf16[1920,128]{1,0:T(8,128)(2,1)S(1)}, bf16[1920,128]{1,0:T(8,128)(2,1)S(1)}, bf16[12,48,256...) while((s32[]{:T(128)}, bf16[1920,128]{1,0:T(8,128)(2,1)S(1)}, ...), condition=%wide.region_9.10_spmd, body=%wide.region_8.9_spmd.sunk | while | flops 2271166464 | bytes 77368712 | solution.py:201
  163.5 1.3 collective-permute-start.9
  165.5 1.4 collective-permute-start.8
  166.9 5.1 %collective-permute-done.9 = bf16[960,128]{1,0:T(8,128)(2,1)S(1)} collective-permute-done((bf16[960,128]{1,0:T(8,128)(2,1)}, bf16[960,128]{1,0:T(8,128)(2,1)S(1)}, u32[]{:S(2)}, u32[]{:S(2)}) %collective-permute-start.9) | collective-permute-done | bytes 245792 | tf_op jit(solution)/shard_map/while/body/ppermute | solution.py:17
  172.1 1.7 collective-permute-done.8
  177.1 2.1 convolution_add_fusion.12
  185.8 8.3 %collective-permute-done.33 = bf16[12,48,256]{2,1,0:T(8,128)(2,1)S(1)} collective-permute-done((bf16[12,48,256]{2,1,0:T(8,128)(2,1)S(1)}, bf16[12,48,256]{2,1,0:T(8,128)(2,1)S(1)}, u32[]{:S(2)}, u32[]{:S(2)}) %collective-permute-start.33) | collective-permute-done | bytes 294944 | tf_op jit(solution)/shard_map/ppermute | solution.py:13
  196.2 3.8 %collective-permute-done.35 = bf16[4,48,2,1,128]{4,2,1,0,3:T(2,128)(2,1)S(1)} collective-permute-done((bf16[4,48,2,1,128]{4,2,1,0,3:T(2,128)(2,1)S(1)}, bf16[4,48,2,1,128]{4,2,1,0,3:T(2,128)(2,1)S(1)}, u32[]{:S(2)}, u32[]{:S(2)}) %collective-permute-start.35) | collective-permute-done | bytes 98336 | tf_op jit(solution)/shard_map/ppermute | solution.py:17
  201.2 6.7 %collective-permute-done.37 = bf16[12,48,256]{2,1,0:T(8,128)(2,1)S(1)} collective-permute-done((bf16[12,48,256]{2,1,0:T(8,128)(2,1)S(1)}, bf16[12,48,256]{2,1,0:T(8,128)(2,1)S(1)}, u32[]{:S(2)}, u32[]{:S(2)}) %collective-permute-start.37) | collective-permute-done | bytes 294944 | tf_op jit(solution)/shard_map/ppermute | solution.py:13
  211.1 3.4 %collective-permute-done.39 = bf16[4,48,2,1,128]{4,2,1,0,3:T(2,128)(2,1)S(1)} collective-permute-done((bf16[4,48,2,1,128]{4,2,1,0,3:T(2,128)(2,1)S(1)}, bf16[4,48,2,1,128]{4,2,1,0,3:T(2,128)(2,1)S(1)}, u32[]{:S(2)}, u32[]{:S(2)}) %collective-permute-start.39) | collective-permute-done | bytes 98336 | tf_op jit(solution)/shard_map/ppermute | solution.py:17
  214.5 1.3 collective-permute-done.40
  219.2 2.1 copy.19
  (173 shorter events, 43.2 us)
Async XLA Ops:
  0.0 18.9 %copy-start = (bf16[2048,512]{1,0:T(8,128)(2,1)S(1)}, bf16[2048,512]{1,0:T(8,128)(2,1)}, u32[]{:S(2)}) copy-start(bf16[2048,512]{1,0:T(8,128)(2,1)} %param.17) | copy-start | bytes 6291460
  0.0 17.6 %copy-start.18 = (s32[4]{0:T(128)S(1)}, s32[4]{0:T(128)}, u32[]{:S(2)}) copy-start(s32[4]{0:T(128)} %param.20) | copy-start | bytes 52
  1.7 11.2 %collective-permute-start.12 = (bf16[1024,128]{1,0:T(8,128)(2,1)S(1)}, bf16[1024,128]{1,0:T(8,128)(2,1)S(1)}, u32[]{:S(2)}, u32[]{:S(2)}) collective-permute-start(bf16[1024,128]{1,0:T(8,128)(2,1)S(1)} %get-tuple-element.418), channel_id=1, source_target_pairs={{0,8},{4,12},{8,0},{12,4},{1,9},{5,13},{9,1},{13,5},{2,10},{6,14},... | collective-permute-start | bytes 786440 | tf_op jit(solution)/shard_map/ppermute | solution.py:17
  4.7 8.2 %collective-permute-start.13 = (bf16[2048]{0:T(1024)(128)(2,1)}, bf16[2048]{0:T(1024)(128)(2,1)S(1)}, u32[]{:S(2)}, u32[]{:S(2)}) collective-permute-start(bf16[2048]{0:T(1024)(128)(2,1)} %param.16), channel_id=1, source_target_pairs={{0,0},{1,4},{2,8},{3,12},{4,1},{5,5},{6,9},{7,13},{8,2},{9,6},{10,... | collective-permute-start | bytes 12296 | tf_op jit(solution)/shard_map/ppermute | solution.py:165
  8.3 11.4 %collective-permute-start.16 = (bf16[1024,128]{1,0:T(8,128)(2,1)S(1)}, bf16[1024,128]{1,0:T(8,128)(2,1)S(1)}, u32[]{:S(2)}, u32[]{:S(2)}) collective-permute-start(bf16[1024,128]{1,0:T(8,128)(2,1)S(1)} %get-tuple-element.591), channel_id=1, source_target_pairs={{0,8},{4,12},{8,0},{12,4},{1,9},{5,13},{9,1},{13,5},{2,10},{6,14},... | collective-permute-start | bytes 786440 | tf_op jit(solution)/shard_map/ppermute | solution.py:17
  13.7 6.1 %collective-permute-start.14 = (bf16[1024,128]{1,0:T(8,128)(2,1)}, bf16[1024,128]{1,0:T(8,128)(2,1)S(1)}, u32[]{:S(2)}, u32[]{:S(2)}) collective-permute-start(bf16[1024,128]{1,0:T(8,128)(2,1)} %get-tuple-element.602), channel_id=1, source_target_pairs={{0,0},{1,4},{2,6},{3,2},{4,1},{5,5},{6,7},{7,3},{8,8},{9,12},{10,1... | collective-permute-start | bytes 786440 | tf_op jit(solution)/shard_map/ppermute | solution.py:165
  15.3 13.9 %collective-permute-start.15 = (bf16[1024,128]{1,0:T(8,128)(2,1)S(1)}, bf16[1024,128]{1,0:T(8,128)(2,1)S(1)}, u32[]{:S(2)}, u32[]{:S(2)}) collective-permute-start(bf16[1024,128]{1,0:T(8,128)(2,1)S(1)} %get-tuple-element.601), channel_id=1, source_target_pairs={{0,2},{1,6},{2,4},{3,0},{4,3},{5,7},{6,5},{7,1},{8,10},{9,14},{10,... | collective-permute-start | bytes 786440 | tf_op jit(solution)/shard_map/ppermute | solution.py:165
  19.8 17.8 %copy-start.13 = (bf16[1024,128]{1,0:T(8,128)(2,1)}, bf16[1024,128]{1,0:T(8,128)(2,1)S(1)}, u32[]{:S(2)}) copy-start(bf16[1024,128]{1,0:T(8,128)(2,1)S(1)} %collective-permute-done.16) | copy-start | bytes 786436
  29.3 14.0 %collective-permute-start.17 = (bf16[1024,256]{1,0:T(8,128)(2,1)S(1)}, bf16[1024,256]{1,0:T(8,128)(2,1)S(1)}, u32[]{:S(2)}, u32[]{:S(2)}) collective-permute-start(bf16[1024,256]{1,0:T(8,128)(2,1)S(1)} %constant_dynamic-update-slice_fusion.2), channel_id=1, source_target_pairs={{0,8},{4,12},{8,0},{12,4},{1,9},{5,13},{9,1},{13,5},{2,10},{6,14},... | collective-permute-start | bytes 1572872 | tf_op jit(solution)/shard_map/ppermute | solution.py:17
  43.5 3.4 %collective-permute-start.18 = (bf16[2048,256]{1,0:T(8,128)(2,1)S(1)}, bf16[2048,256]{1,0:T(8,128)(2,1)S(1)}, u32[]{:S(2)}, u32[]{:S(2)}) collective-permute-start(bf16[2048,256]{1,0:T(8,128)(2,1)S(1)} %pad_maximum_fusion.7.near), channel_id=1, source_target_pairs={{0,4},{4,0},{8,12},{12,8},{1,5},{5,1},{9,13},{13,9},{2,6},{6,2},{1... | collective-permute-start | bytes 3145736 | tf_op jit(solution)/shard_map/ppermute | solution.py:17
  43.7 3.1 %collective-permute-start.21 = (f32[1,512]{1,0:T(1,128)S(1)}, f32[1,512]{1,0:T(1,128)S(1)}, u32[]{:S(2)}, u32[]{:S(2)}) collective-permute-start(f32[1,512]{1,0:T(1,128)S(1)} %fusion.30), channel_id=1, source_target_pairs={{0,4},{4,0},{8,12},{12,8},{1,5},{5,1},{9,13},{13,9},{2,6},{6,2},{1... | collective-permute-start | bytes 6152 | tf_op jit(solution)/shard_map/ppermute | solution.py:17
  44.4 10.2 %collective-permute-start.19 = (bf16[1024,128]{1,0:T(8,128)(2,1)S(1)}, bf16[1024,128]{1,0:T(8,128)(2,1)S(1)}, u32[]{:S(2)}, u32[]{:S(2)}) collective-permute-start(bf16[1024,128]{1,0:T(8,128)(2,1)S(1)} %get-tuple-element.600), channel_id=1, source_target_pairs={{0,0},{1,4},{2,6},{3,2},{4,1},{5,5},{6,7},{7,3},{8,8},{9,12},{10,1... | collective-permute-start | bytes 786440 | tf_op jit(solution)/shard_map/ppermute | solution.py:165
  45.1 12.7 %collective-permute-start.20 = (bf16[1024,128]{1,0:T(8,128)(2,1)S(1)}, bf16[1024,128]{1,0:T(8,128)(2,1)S(1)}, u32[]{:S(2)}, u32[]{:S(2)}) collective-permute-start(bf16[1024,128]{1,0:T(8,128)(2,1)S(1)} %get-tuple-element.599), channel_id=1, source_target_pairs={{0,2},{1,6},{2,4},{3,0},{4,3},{5,7},{6,5},{7,1},{8,10},{9,14},{10,... | collective-permute-start | bytes 786440 | tf_op jit(solution)/shard_map/ppermute | solution.py:165
  58.3 33.0 %collective-permute-start.24 = (bf16[2560,128]{1,0:T(8,128)(2,1)}, bf16[2560,128]{1,0:T(8,128)(2,1)}, u32[]{:S(2)}, u32[]{:S(2)}) collective-permute-start(bf16[2560,128]{1,0:T(8,128)(2,1)} %get-tuple-element.439), channel_id=1, source_target_pairs={{0,1},{1,0},{2,3},{3,2},{4,5},{5,4},{6,7},{7,6},{8,9},{9,8},{10,11... | collective-permute-start | bytes 1966088 | tf_op jit(solution)/shard_map/ppermute | solution.py:17
  60.2 31.1 %collective-permute-start.22 = (bf16[1280,128]{1,0:T(8,128)(2,1)}, bf16[1280,128]{1,0:T(8,128)(2,1)}, u32[]{:S(2)}, u32[]{:S(2)}) collective-permute-start(bf16[1280,128]{1,0:T(8,128)(2,1)} %get-tuple-element.437), channel_id=1, source_target_pairs={{0,2},{1,3},{2,0},{3,1},{4,6},{5,7},{6,4},{7,5},{8,10},{9,11},{10,... | collective-permute-start | bytes 983048 | tf_op jit(solution)/shard_map/ppermute | solution.py:17
  61.7 29.5 %collective-permute-start.23 = (bf16[1280,128]{1,0:T(8,128)(2,1)}, bf16[1280,128]{1,0:T(8,128)(2,1)}, u32[]{:S(2)}, u32[]{:S(2)}) collective-permute-start(bf16[1280,128]{1,0:T(8,128)(2,1)} %get-tuple-element.438), channel_id=1, source_target_pairs={{0,3},{1,2},{2,1},{3,0},{4,7},{5,6},{6,5},{7,4},{8,11},{9,10},{10,... | collective-permute-start | bytes 983048 | tf_op jit(solution)/shard_map/ppermute | solution.py:17
  64.6 14.6 %collective-permute-start = (bf16[1024,256]{1,0:T(8,128)(2,1)S(1)}, bf16[1024,256]{1,0:T(8,128)(2,1)}, u32[]{:S(2)}, u32[]{:S(2)}) collective-permute-start(bf16[1024,256]{1,0:T(8,128)(2,1)S(1)} %copy.33), channel_id=1, source_target_pairs={{0,8},{4,12},{8,0},{12,4},{1,9},{5,13},{9,1},{13,5},{2,10},{6,14},... | collective-permute-start | bytes 1572872 | tf_op jit(solution)/shard_map/while/body/ppermute | solution.py:17
  65.7 13.5 %collective-permute-start.1 = (f32[1,512]{1,0:T(1,128)S(1)}, f32[1,512]{1,0:T(1,128)S(1)}, u32[]{:S(2)}, u32[]{:S(2)}) collective-permute-start(f32[1,512]{1,0:T(1,128)S(1)} %copy.34), channel_id=1, source_target_pairs={{0,8},{4,12},{8,0},{12,4},{1,9},{5,13},{9,1},{13,5},{2,10},{6,14},... | collective-permute-start | bytes 6152 | tf_op jit(solution)/shard_map/while/body/ppermute | solution.py:17
  80.4 2.9 %collective-permute-start.2 = (bf16[2048,256]{1,0:T(8,128)(2,1)S(1)}, bf16[2048,256]{1,0:T(8,128)(2,1)S(1)}, u32[]{:S(2)}, u32[]{:S(2)}) collective-permute-start(bf16[2048,256]{1,0:T(8,128)(2,1)S(1)} %pad_maximum_fusion.18.near), channel_id=1, source_target_pairs={{0,4},{4,0},{8,12},{12,8},{1,5},{5,1},{9,13},{13,9},{2,6},{6,2},{1... | collective-permute-start | bytes 3145736 | tf_op jit(solution)/shard_map/while/body/ppermute | solution.py:17
  92.3 13.3 %copy-start.15 = (f32[1,512]{1,0:T(1,128)S(1)}, f32[1,512]{1,0:T(1,128)}, u32[]{:S(2)}) copy-start(f32[1,512]{1,0:T(1,128)} %get-tuple-element.471) | copy-start | bytes 6148
  92.4 13.3 %copy-start.16 = (f32[1,128]{1,0:T(1,128)S(1)}, f32[1,128]{1,0:T(1,128)}, u32[]{:S(2)}) copy-start(f32[1,128]{1,0:T(1,128)} %param.18) | copy-start | bytes 1540
  92.4 8.4 %collective-permute-start.25 = (bf16[640,128]{1,0:T(8,128)(2,1)S(1)}, bf16[640,128]{1,0:T(8,128)(2,1)S(1)}, u32[]{:S(2)}, u32[]{:S(2)}) collective-permute-start(bf16[640,128]{1,0:T(8,128)(2,1)S(1)} %slice.147), channel_id=1, source_target_pairs={{0,3},{1,2},{2,1},{3,0},{4,7},{5,6},{6,5},{7,4},{8,11},{9,10},{10,... | collective-permute-start | bytes 491528 | tf_op jit(solution)/shard_map/ppermute | solution.py:17
  100.9 38.3 %collective-permute-start.26 = (bf16[1920,128]{1,0:T(8,128)(2,1)}, bf16[1920,128]{1,0:T(8,128)(2,1)}, u32[]{:S(2)}, u32[]{:S(2)}) collective-permute-start(bf16[1920,128]{1,0:T(8,128)(2,1)} %get-tuple-element.458), channel_id=1, source_target_pairs={{0,2},{1,3},{2,0},{3,1},{4,6},{5,7},{6,4},{7,5},{8,10},{9,11},{10,... | collective-permute-start | bytes 1474568 | tf_op jit(solution)/shard_map/ppermute | solution.py:17
  104.3 34.9 %collective-permute-start.27 = (bf16[1920,128]{1,0:T(8,128)(2,1)}, bf16[1920,128]{1,0:T(8,128)(2,1)}, u32[]{:S(2)}, u32[]{:S(2)}) collective-permute-start(bf16[1920,128]{1,0:T(8,128)(2,1)} %get-tuple-element.459), channel_id=1, source_target_pairs={{0,3},{1,2},{2,1},{3,0},{4,7},{5,6},{6,5},{7,4},{8,11},{9,10},{10,... | collective-permute-start | bytes 1474568 | tf_op jit(solution)/shard_map/ppermute | solution.py:17
  105.6 33.6 %collective-permute-start.28 = (bf16[1920,128]{1,0:T(8,128)(2,1)}, bf16[1920,128]{1,0:T(8,128)(2,1)}, u32[]{:S(2)}, u32[]{:S(2)}) collective-permute-start(bf16[1920,128]{1,0:T(8,128)(2,1)} %get-tuple-element.460), channel_id=1, source_target_pairs={{0,1},{1,0},{2,3},{3,2},{4,5},{5,4},{6,7},{7,6},{8,9},{9,8},{10,11... | collective-permute-start | bytes 1474568 | tf_op jit(solution)/shard_map/ppermute | solution.py:17
  105.7 33.5 %copy-start.10 = (f32[1920,128]{1,0:T(8,128)S(1)}, f32[1920,128]{1,0:T(8,128)}, u32[]{:S(2)}) copy-start(f32[1920,128]{1,0:T(8,128)} %get-tuple-element.474) | copy-start | bytes 2949124
  105.8 11.3 %collective-permute-start.3 = (bf16[1920,128]{1,0:T(8,128)(2,1)S(1)}, bf16[1920,128]{1,0:T(8,128)(2,1)S(1)}, u32[]{:S(2)}, u32[]{:S(2)}) collective-permute-start(bf16[1920,128]{1,0:T(8,128)(2,1)S(1)} %copy.52), channel_id=1, source_target_pairs={{0,8},{4,12},{8,0},{12,4},{1,9},{5,13},{9,1},{13,5},{2,10},{6,14},... | collective-permute-start | bytes 1474568 | tf_op jit(solution)/shard_map/while/body/ppermute | solution.py:17
  106.6 11.0 %collective-permute-start.4 = (bf16[1920,128]{1,0:T(8,128)(2,1)S(1)}, bf16[1920,128]{1,0:T(8,128)(2,1)S(1)}, u32[]{:S(2)}, u32[]{:S(2)}) collective-permute-start(bf16[1920,128]{1,0:T(8,128)(2,1)S(1)} %copy.52), channel_id=1, source_target_pairs={{0,16},{16,0},{1,17},{17,1},{2,18},{18,2},{3,19},{19,3},{4,20},{20... | collective-permute-start | bytes 1474568 | tf_op jit(solution)/shard_map/while/body/ppermute | solution.py:17
  117.7 13.7 %collective-permute-start.6 = (bf16[1920,256]{1,0:T(8,128)(2,1)S(1)}, bf16[1920,256]{1,0:T(8,128)(2,1)}, u32[]{:S(2)}, u32[]{:S(2)}) collective-permute-start(bf16[1920,256]{1,0:T(8,128)(2,1)S(1)} %pad_maximum_fusion.19), channel_id=1, source_target_pairs={{0,4},{4,0},{8,12},{12,8},{1,5},{5,1},{9,13},{13,9},{2,6},{6,2},{1... | collective-permute-start | bytes 2949128 | tf_op jit(solution)/shard_map/while/body/ppermute | solution.py:17
  117.8 13.6 %collective-permute-start.5 = (bf16[1920,128]{1,0:T(8,128)(2,1)S(1)}, bf16[1920,128]{1,0:T(8,128)(2,1)S(1)}, u32[]{:S(2)}, u32[]{:S(2)}) collective-permute-start(bf16[1920,128]{1,0:T(8,128)(2,1)S(1)} %collective-permute-done.4), channel_id=1, source_target_pairs={{0,8},{4,12},{8,0},{12,4},{1,9},{5,13},{9,1},{13,5},{2,10},{6,14},... | collective-permute-start | bytes 1474568 | tf_op jit(solution)/shard_map/while/body/ppermute | solution.py:17
  119.2 12.5 %copy-start.7 = (bf16[576,1920]{1,0:T(8,128)(2,1)S(1)}, bf16[576,1920]{1,0:T(8,128)(2,1)}, u32[]{:S(2)}) copy-start(bf16[576,1920]{1,0:T(8,128)(2,1)} %get-tuple-element.967) | copy-start | bytes 6635524 | tf_op jit(solution)/shard_map/while
  131.6 4.7 %collective-permute-start.7 = (bf16[1920,256]{1,0:T(8,128)(2,1)S(1)}, bf16[1920,256]{1,0:T(8,128)(2,1)S(1)}, u32[]{:S(2)}, u32[]{:S(2)}) collective-permute-start(bf16[1920,256]{1,0:T(8,128)(2,1)S(1)} %pad_maximum_fusion.20), channel_id=1, source_target_pairs={{0,4},{4,0},{8,12},{12,8},{1,5},{5,1},{9,13},{13,9},{2,6},{6,2},{1... | collective-permute-start | bytes 2949128 | tf_op jit(solution)/shard_map/while/body/ppermute | solution.py:17
  140.8 16.7 %collective-permute-start.30 = (bf16[1920,128]{1,0:T(8,128)(2,1)S(1)}, bf16[1920,128]{1,0:T(8,128)(2,1)S(1)}, u32[]{:S(2)}, u32[]{:S(2)}) collective-permute-start(bf16[1920,128]{1,0:T(8,128)(2,1)S(1)} %add_convert_fusion), channel_id=1, source_target_pairs={{0,8},{4,12},{8,0},{12,4},{1,9},{5,13},{9,1},{13,5},{2,10},{6,14},... | collective-permute-start | bytes 1474568 | tf_op jit(solution)/shard_map/ppermute | solution.py:17
  142.1 15.3 %collective-permute-start.31 = (bf16[1920,128]{1,0:T(8,128)(2,1)S(1)}, bf16[1920,128]{1,0:T(8,128)(2,1)S(1)}, u32[]{:S(2)}, u32[]{:S(2)}) collective-permute-start(bf16[1920,128]{1,0:T(8,128)(2,1)S(1)} %add_convert_fusion), channel_id=1, source_target_pairs={{0,16},{16,0},{1,17},{17,1},{2,18},{18,2},{3,19},{19,3},{4,20},{20... | collective-permute-start | bytes 1474568 | tf_op jit(solution)/shard_map/ppermute | solution.py:17
  143.7 13.8 %collective-permute-start.29 = (bf16[12,48,256]{2,1,0:T(8,128)(2,1)S(1)}, bf16[12,48,256]{2,1,0:T(8,128)(2,1)S(1)}, u32[]{:S(2)}, u32[]{:S(2)}) collective-permute-start(bf16[12,48,256]{2,1,0:T(8,128)(2,1)S(1)} %copy-done.12), channel_id=1, source_target_pairs={{0,1},{1,2},{2,3},{3,0},{4,5},{5,6},{6,7},{7,4},{8,9},{9,10},{10,1... | collective-permute-start | bytes 884744 | tf_op jit(solution)/shard_map/ppermute | solution.py:13
  158.3 24.2 %collective-permute-start.32 = (bf16[12,48,256]{2,1,0:T(8,128)(2,1)}, bf16[12,48,256]{2,1,0:T(8,128)(2,1)}, u32[]{:S(2)}, u32[]{:S(2)}) collective-permute-start(bf16[12,48,256]{2,1,0:T(8,128)(2,1)} %broadcast_select_fusion.15), channel_id=1, source_target_pairs={{0,2},{1,3},{2,0},{3,1},{4,6},{5,7},{6,4},{7,5},{8,10},{9,11},{10,... | collective-permute-start | bytes 884744 | tf_op jit(solution)/shard_map/ppermute | solution.py:13
  162.7 11.1 %collective-permute-start.10 = (bf16[1920,256]{1,0:T(8,128)(2,1)S(1)}, bf16[1920,256]{1,0:T(8,128)(2,1)}, u32[]{:S(2)}, u32[]{:S(2)}) collective-permute-start(bf16[1920,256]{1,0:T(8,128)(2,1)S(1)} %pad_maximum_fusion.22), channel_id=1, source_target_pairs={{0,4},{4,0},{8,12},{12,8},{1,5},{5,1},{9,13},{13,9},{2,6},{6,2},{1... | collective-permute-start | bytes 2949128 | tf_op jit(solution)/shard_map/while/body/ppermute | solution.py:17
  163.5 8.6 %collective-permute-start.9 = (bf16[960,128]{1,0:T(8,128)(2,1)}, bf16[960,128]{1,0:T(8,128)(2,1)S(1)}, u32[]{:S(2)}, u32[]{:S(2)}) collective-permute-start(bf16[960,128]{1,0:T(8,128)(2,1)} %slice.171), channel_id=1, source_target_pairs={{0,8},{4,12},{8,0},{12,4},{1,9},{5,13},{9,1},{13,5},{2,10},{6,14},... | collective-permute-start | bytes 737288 | tf_op jit(solution)/shard_map/while/body/ppermute | solution.py:17
  165.5 8.3 %collective-permute-start.8 = (bf16[960,128]{1,0:T(8,128)(2,1)}, bf16[960,128]{1,0:T(8,128)(2,1)S(1)}, u32[]{:S(2)}, u32[]{:S(2)}) collective-permute-start(bf16[960,128]{1,0:T(8,128)(2,1)} %slice.170), channel_id=1, source_target_pairs={{0,16},{16,0},{1,17},{17,1},{2,18},{18,2},{3,19},{19,3},{4,20},{20... | collective-permute-start | bytes 737288 | tf_op jit(solution)/shard_map/while/body/ppermute | solution.py:17
  174.1 5.9 %collective-permute-start.11 = (bf16[1920,256]{1,0:T(8,128)(2,1)S(1)}, bf16[1920,256]{1,0:T(8,128)(2,1)S(1)}, u32[]{:S(2)}, u32[]{:S(2)}) collective-permute-start(bf16[1920,256]{1,0:T(8,128)(2,1)S(1)} %pad_maximum_fusion.23), channel_id=1, source_target_pairs={{0,4},{4,0},{8,12},{12,8},{1,5},{5,1},{9,13},{13,9},{2,6},{6,2},{1... | collective-permute-start | bytes 2949128 | tf_op jit(solution)/shard_map/while/body/ppermute | solution.py:17
  183.8 10.3 %collective-permute-start.33 = (bf16[12,48,256]{2,1,0:T(8,128)(2,1)S(1)}, bf16[12,48,256]{2,1,0:T(8,128)(2,1)S(1)}, u32[]{:S(2)}, u32[]{:S(2)}) collective-permute-start(bf16[12,48,256]{2,1,0:T(8,128)(2,1)S(1)} %copy-done.11), channel_id=1, source_target_pairs={{0,1},{1,2},{2,3},{3,0},{4,5},{5,6},{6,7},{7,4},{8,9},{9,10},{10,1... | collective-permute-start | bytes 884744 | tf_op jit(solution)/shard_map/ppermute | solution.py:13
  194.2 13.7 %collective-permute-start.37 = (bf16[12,48,256]{2,1,0:T(8,128)(2,1)S(1)}, bf16[12,48,256]{2,1,0:T(8,128)(2,1)S(1)}, u32[]{:S(2)}, u32[]{:S(2)}) collective-permute-start(bf16[12,48,256]{2,1,0:T(8,128)(2,1)S(1)} %broadcast_select_fusion.14), channel_id=1, source_target_pairs={{0,2},{1,3},{2,0},{3,1},{4,6},{5,7},{6,4},{7,5},{8,10},{9,11},{10,... | collective-permute-start | bytes 884744 | tf_op jit(solution)/shard_map/ppermute | solution.py:13
  194.3 1.9 collective-permute-start.34
  194.4 5.7 %collective-permute-start.35 = (bf16[4,48,2,1,128]{4,2,1,0,3:T(2,128)(2,1)S(1)}, bf16[4,48,2,1,128]{4,2,1,0,3:T(2,128)(2,1)S(1)}, u32[]{:S(2)}, u32[]{:S(2)}) collective-permute-start(bf16[4,48,2,1,128]{4,2,1,0,3:T(2,128)(2,1)S(1)} %squeeze.30), channel_id=1, source_target_pairs={{0,8},{4,12},{8,0},{12,4},{1,9},{5,13},{9,1},{13,5},{2,10},{6,14},... | collective-permute-start | bytes 294920 | tf_op jit(solution)/shard_map/ppermute | solution.py:17
  195.1 6.1 %collective-permute-start.36 = (bf16[4,48,2,1,128]{4,2,1,0,3:T(2,128)(2,1)S(1)}, bf16[4,48,2,1,128]{4,2,1,0,3:T(2,128)(2,1)S(1)}, u32[]{:S(2)}, u32[]{:S(2)}) collective-permute-start(bf16[4,48,2,1,128]{4,2,1,0,3:T(2,128)(2,1)S(1)} %squeeze.31), channel_id=1, source_target_pairs={{0,12},{4,8},{8,4},{12,0},{1,13},{5,9},{9,5},{13,1},{2,14},{6,10},... | collective-permute-start | bytes 294920 | tf_op jit(solution)/shard_map/ppermute | solution.py:17
  208.7 2.4 %collective-permute-start.38 = (bf16[4,48,2,1,128]{4,2,1,0,3:T(2,128)(2,1)S(1)}, bf16[4,48,2,1,128]{4,2,1,0,3:T(2,128)(2,1)S(1)}, u32[]{:S(2)}, u32[]{:S(2)}) collective-permute-start(bf16[4,48,2,1,128]{4,2,1,0,3:T(2,128)(2,1)S(1)} %squeeze.33), channel_id=1, source_target_pairs={{0,4},{4,0},{8,12},{12,8},{1,5},{5,1},{9,13},{13,9},{2,6},{6,2},{1... | collective-permute-start | bytes 294920 | tf_op jit(solution)/shard_map/ppermute | solution.py:17
  208.9 5.7 %collective-permute-start.39 = (bf16[4,48,2,1,128]{4,2,1,0,3:T(2,128)(2,1)S(1)}, bf16[4,48,2,1,128]{4,2,1,0,3:T(2,128)(2,1)S(1)}, u32[]{:S(2)}, u32[]{:S(2)}) collective-permute-start(bf16[4,48,2,1,128]{4,2,1,0,3:T(2,128)(2,1)S(1)} %squeeze.34), channel_id=1, source_target_pairs={{0,8},{4,12},{8,0},{12,4},{1,9},{5,13},{9,1},{13,5},{2,10},{6,14},... | collective-permute-start | bytes 294920 | tf_op jit(solution)/shard_map/ppermute | solution.py:17
  209.8 6.1 %collective-permute-start.40 = (bf16[4,48,2,1,128]{4,2,1,0,3:T(2,128)(2,1)S(1)}, bf16[4,48,2,1,128]{4,2,1,0,3:T(2,128)(2,1)S(1)}, u32[]{:S(2)}, u32[]{:S(2)}) collective-permute-start(bf16[4,48,2,1,128]{4,2,1,0,3:T(2,128)(2,1)S(1)} %squeeze.35), channel_id=1, source_target_pairs={{0,12},{4,8},{8,4},{12,0},{1,13},{5,9},{9,5},{13,1},{2,14},{6,10},... | collective-permute-start | bytes 294920 | tf_op jit(solution)/shard_map/ppermute | solution.py:17
  (13 other events, 38.2 us)

commit v21 on v20

--- a/solution.py
+++ b/solution.py
@@ -256,13 +256,20 @@
 
     key_stays, key_leaves, rows_later = step((*halves(kv_weight, 0), kv_weight))
     bias_rows = moved(proj_bias, lambda t, h: (h, t))
-    key_stays, key_comes, bias_rows, counts_later = step(
-        (key_stays, swapped(key_leaves, "tile", 2), bias_rows, tile_count)
+    value_stays, value_leaves = halves(rows_later, 1)
+    key_stays, key_comes, bias_rows, counts_later, value_stays, value_leaves = step(
+        (
+            key_stays,
+            swapped(key_leaves, "tile", 2),
+            bias_rows,
+            tile_count,
+            value_stays,
+            value_leaves,
+        )
     )
 
     once = jnp.minimum(jnp.max(counts_later), 1)
 
-    value_stays, value_leaves = halves(rows_later, 1)
     tokens = jax.ShapeDtypeStruct((tile_slots, shard_len, 2 * width), jnp.bfloat16)
     shapes = term_shapes(depth, width, True) + [tokens, tokens]
     *no_terms, no_keys, no_values = blank_arrays(shapes)

time: 222 us -> 221 us (level)
  starting transfers between devices: 57.9 us -> 53.1 us
  waiting for transfers between devices: 96.8 us -> 101 us
    ppermute x32, starting transfers between devices: 36.8 us -> 29.6 us  [swapped(): lax.ppermute(shard, axis, [(i, i ^ bit) for i in range(lax.axis_size(axis...]
    ppermute x32, waiting for transfers between devices: 63.6 us -> 67.4 us  [swapped(): lax.ppermute(shard, axis, [(i, i ^ bit) for i in range(lax.axis_size(axis...]
where the time goes in v21:
time: 221 us
  waiting for transfers between devices  101 us (46%)
  starting transfers between devices  53.1 us (24%)
  local copies, waits for them, and re-layouts  24.9 us (11%)
  Pallas kernels  15.7 us (7%)
  other arithmetic  14.9 us (7%)
  matrix products  9.93 us (4%)
    ppermute x32, waiting for transfers between devices, swapped(): lax.ppermute(shard, axis, [(i, i ^ bit) for i in range(lax.axis_size(axis...  67.4 us
    ppermute x32, starting transfers between devices, swapped(): lax.ppermute(shard, axis, [(i, i ^ bit) for i in range(lax.axis_size(axis...  29.6 us
    ppermute x4, waiting for transfers between devices, shifted_2(): lax.ppermute(shard, axis, [(i, (i + by) % count) for i in range(count)])  20.6 us
    pallas_call x2, Pallas kernels, product_terms(): pl.pallas_call(terms_body, out_shape=shapes, grid_spec=pltpu.PrefetchScal...  15.7 us
    ppermute x4, starting transfers between devices, shifted_2(): lax.ppermute(shard, axis, [(i, (i + by) % count) for i in range(count)])  14.1 us
    ppermute x5, waiting for transfers between devices, moved(): return lax.ppermute(shard, ('tile', 'head'), pairs)  12.6 us
    dot_general x11, matrix products, add_columns(): return jnp.dot(operand, portion, preferred_element_type=jnp.float32)  9.74 us
    ppermute x5, starting transfers between devices, moved(): return lax.ppermute(shard, ('tile', 'head'), pairs)  9.46 us
  transfers between devices with their start and end apart: 41, of which 19 were waited for; matrix products, arithmetic and copies ran while one was open for 14% of the time, Pallas kernels for 7%

profile of v21, /device:TPU:0, one launch (start us, length us, event | category | flops | bytes accessed | tf_op | source)
XLA Modules:
  0.0 220.7 jit_solution(10802077180674597923)
XLA Ops:
  0.0 1.7 fusion.24
  1.7 3.0 %collective-permute-start.12 = (bf16[1024,128]{1,0:T(8,128)(2,1)S(1)}, bf16[1024,128]{1,0:T(8,128)(2,1)S(1)}, u32[]{:S(2)}, u32[]{:S(2)}) collective-permute-start(bf16[1024,128]{1,0:T(8,128)(2,1)S(1)} %get-tuple-element.420), channel_id=1, source_target_pairs={{0,8},{4,12},{8,0},{12,4},{1,9},{5,13},{9,1},{13,5},{2,10},{6,14},... | collective-permute-start | bytes 786440 | tf_op jit(solution)/shard_map/ppermute | solution.py:17
  4.7 1.3 collective-permute-start.13
  6.1 2.2 %fusion.23 = (bf16[1024,128]{1,0:T(8,128)(2,1)S(1)}, bf16[1024,128]{1,0:T(8,128)(2,1)}) fusion(bf16[2048,512]{1,0:T(8,128)(2,1)} %param.17, s32[]{:T(128)S(6)} %select_n.304, s32[]{:T(128)S(6)} %select_n.306, s32[]{:T(128)S(6)} %select_n.300), kind=kLoop, calls=%fused_computation.124 | loop fusion | bytes 1048588 | tf_op jit(solution)/shard_map/dynamic_slice | solution.py:246
  8.3 2.7 %collective-permute-done.12 = bf16[1024,128]{1,0:T(8,128)(2,1)S(1)} collective-permute-done((bf16[1024,128]{1,0:T(8,128)(2,1)S(1)}, bf16[1024,128]{1,0:T(8,128)(2,1)S(1)}, u32[]{:S(2)}, u32[]{:S(2)}) %collective-permute-start.12) | collective-permute-done | bytes 262176 | tf_op jit(solution)/shard_map/ppermute | solution.py:17
  11.8 5.1 %collective-permute-start.15 = (bf16[1024,128]{1,0:T(8,128)(2,1)S(1)}, bf16[1024,128]{1,0:T(8,128)(2,1)}, u32[]{:S(2)}, u32[]{:S(2)}) collective-permute-start(bf16[1024,128]{1,0:T(8,128)(2,1)S(1)} %get-tuple-element.605), channel_id=1, source_target_pairs={{0,2},{1,6},{2,4},{3,0},{4,3},{5,7},{6,5},{7,1},{8,10},{9,14},{10,... | collective-permute-start | bytes 786440 | tf_op jit(solution)/shard_map/ppermute | solution.py:165
  19.1 9.0 %collective-permute-done.15 = bf16[1024,128]{1,0:T(8,128)(2,1)} collective-permute-done((bf16[1024,128]{1,0:T(8,128)(2,1)S(1)}, bf16[1024,128]{1,0:T(8,128)(2,1)}, u32[]{:S(2)}, u32[]{:S(2)}) %collective-permute-start.15) | collective-permute-done | bytes 262176 | tf_op jit(solution)/shard_map/ppermute | solution.py:165
  30.0 7.2 %constant_dynamic-slice_fusion = (bf16[576,1920]{1,0:T(8,128)(2,1)}, bf16[576,1920]{1,0:T(8,128)(2,1)}, bf16[576,1920]{1,0:T(8,128)(2,1)}, bf16[576,1920]{1,0:T(8,128)(2,1)}) fusion(bf16[576,7680]{1,0:T(8,128)(2,1)} %bitcast.134, s32[]{:T(128)S(6)} %select_n.313, s32[]{:T(128)S(6)} %select_n.312, s32[]{:T(128)S(6)} %select_n.311, s32[]{:T(128)S(6)} %select_n.310), kind=kLoop, calls=%fused_computation.115 | loop fusion | bytes 17694736 | tf_op jit(solution)/shard_map/dynamic_slice | solution.py:171
  37.2 6.5 %collective-permute-done.17 = bf16[1024,256]{1,0:T(8,128)(2,1)S(1)} collective-permute-done((bf16[1024,256]{1,0:T(8,128)(2,1)S(1)}, bf16[1024,256]{1,0:T(8,128)(2,1)S(1)}, u32[]{:S(2)}, u32[]{:S(2)}) %collective-permute-start.17) | collective-permute-done | bytes 524320 | tf_op jit(solution)/shard_map/ppermute | solution.py:17
  45.4 1.7 collective-permute-start.20
  47.1 7.7 %shard_map.82 = (f32[1280,128]{1,0:T(8,128)S(1)}, bf16[1280,128]{1,0:T(8,128)(2,1)}, bf16[1280,128]{1,0:T(8,128)(2,1)}, bf16[2560,128]{1,0:T(8,128)(2,1)}, f32[640,256]{1,0:T(8,128)S(1)}) custom-call(s32[1]{0:T(128)} %bitcast.11.choice, bf16[1920,2048]{1,0:T(8,128)(2,1)} %weight.1, bf16[2048,256]{1,0:T(8,128)(2,1)S(1)} %pad_maximum_fusion.7.near, ...), custom_call_target="tpu_custom_call" | custom-call | flops 4026531840 | bytes 12419072 | tf_op jit(solution)/shard_map/pallas_call | solution.py:118
  54.8 3.6 %collective-permute-done.20 = bf16[1024,128]{1,0:T(8,128)(2,1)S(1)} collective-permute-done((bf16[1024,128]{1,0:T(8,128)(2,1)S(1)}, bf16[1024,128]{1,0:T(8,128)(2,1)S(1)}, u32[]{:S(2)}, u32[]{:S(2)}) %collective-permute-start.20) | collective-permute-done | bytes 262176 | tf_op jit(solution)/shard_map/ppermute | solution.py:165
  59.6 1.4 collective-permute-start.22
  61.0 2.4 %collective-permute-start.23 = (bf16[1280,128]{1,0:T(8,128)(2,1)}, bf16[1280,128]{1,0:T(8,128)(2,1)}, u32[]{:S(2)}, u32[]{:S(2)}) collective-permute-start(bf16[1280,128]{1,0:T(8,128)(2,1)} %get-tuple-element.442), channel_id=1, source_target_pairs={{0,3},{1,2},{2,1},{3,0},{4,7},{5,6},{6,5},{7,4},{8,11},{9,10},{10,... | collective-permute-start | bytes 983048 | tf_op jit(solution)/shard_map/ppermute | solution.py:17
  64.2 27.0 %while.54 = (s32[]{:T(128)}, bf16[1024,256]{1,0:T(8,128)(2,1)}, f32[1,512]{1,0:T(1,128)S(1)}, f32[1920,128]{1,0:T(8,128)}, bf16[1920,128]{1,0:T(8,128)(2,1)}, /*...) while((s32[]{:T(128)}, bf16[1024,256]{1,0:T(8,128)(2,1)}, ...), condition=%wide.region_3.4_spmd, body=%wide.region_2.3_spmd.sunk | while | flops 4029153792 | bytes 23972084 | solution.py:201
  65.9 1.4 collective-permute-start.1
  67.3 11.9 %collective-permute-done.1 = f32[1,512]{1,0:T(1,128)S(1)} collective-permute-done((f32[1,512]{1,0:T(1,128)S(1)}, f32[1,512]{1,0:T(1,128)S(1)}, u32[]{:S(2)}, u32[]{:S(2)}) %collective-permute-start.1) | collective-permute-done | bytes 2080 | tf_op jit(solution)/shard_map/while/body/ppermute | solution.py:17
  81.0 2.1 collective-permute-done.2.far
  83.1 8.0 %body.1 = (f32[1920,128]{1,0:T(8,128)}, bf16[1920,128]{1,0:T(8,128)(2,1)}, bf16[1920,128]{1,0:T(8,128)(2,1)}, bf16[1920,128]{1,0:T(8,128)(2,1)}) custom-call(s32[1]{0:T(128)} %get-tuple-element.939.choice, bf16[1920,2048]{1,0:T(8,128)(2,1)} %get-tuple-element.940.weight, bf16[2048,256]{1,0:T(8,128)(2,1)S(1)} %pad_maximum_fusion.18.near, ...), custom_call_target="tpu_custom_call" | custom-call | flops 4026531840 | bytes 12419072 | tf_op jit(solution)/shard_map/while/body/pallas_call | solution.py:118
  92.3 1.9 collective-permute-start.25
  94.2 1.3 add_convert_fusion.1
  95.5 5.0 %collective-permute-done.25 = bf16[640,128]{1,0:T(8,128)(2,1)S(1)} collective-permute-done((bf16[640,128]{1,0:T(8,128)(2,1)S(1)}, bf16[640,128]{1,0:T(8,128)(2,1)S(1)}, u32[]{:S(2)}, u32[]{:S(2)}) %collective-permute-start.25) | collective-permute-done | bytes 163872 | tf_op jit(solution)/shard_map/ppermute | solution.py:17
  100.5 3.1 %collective-permute-start.26 = (bf16[1920,128]{1,0:T(8,128)(2,1)}, bf16[1920,128]{1,0:T(8,128)(2,1)}, u32[]{:S(2)}, u32[]{:S(2)}) collective-permute-start(bf16[1920,128]{1,0:T(8,128)(2,1)} %get-tuple-element.462), channel_id=1, source_target_pairs={{0,2},{1,3},{2,0},{3,1},{4,6},{5,7},{6,4},{7,5},{8,10},{9,11},{10,... | collective-permute-start | bytes 1474568 | tf_op jit(solution)/shard_map/ppermute | solution.py:17
  105.0 34.4 %while.55 = (s32[]{:T(128)}, bf16[1920,128]{1,0:T(8,128)(2,1)S(1)}, bf16[12,48,256]{2,1,0:T(8,128)(2,1)}, s32[]{:T(128)}, pred[]{:T(512)}, /*index=5*/bf16[576,1...) while((s32[]{:T(128)}, bf16[1920,128]{1,0:T(8,128)(2,1)S(1)}, ...), condition=%wide.region_7.8_spmd, body=%wide.region_4.7_spmd.sunk | while | flops 2271905024 | bytes 76995496 | solution.py:201
  105.1 1.6 collective-permute-start.3
  106.7 1.5 collective-permute-start.4
  108.2 8.3 %collective-permute-done.3 = bf16[1920,128]{1,0:T(8,128)(2,1)S(1)} collective-permute-done((bf16[1920,128]{1,0:T(8,128)(2,1)S(1)}, bf16[1920,128]{1,0:T(8,128)(2,1)S(1)}, u32[]{:S(2)}, u32[]{:S(2)}) %collective-permute-start.3) | collective-permute-done | bytes 491552 | tf_op jit(solution)/shard_map/while/body/ppermute | solution.py:17
  116.5 1.3 collective-permute-done.4
  118.6 13.1 %collective-permute-done.5 = bf16[1920,128]{1,0:T(8,128)(2,1)S(1)} collective-permute-done((bf16[1920,128]{1,0:T(8,128)(2,1)S(1)}, bf16[1920,128]{1,0:T(8,128)(2,1)S(1)}, u32[]{:S(2)}, u32[]{:S(2)}) %collective-permute-start.5) | collective-permute-done | bytes 491552 | tf_op jit(solution)/shard_map/while/body/ppermute | solution.py:17
  133.6 2.1 convolution_add_fusion.10
  139.4 1.6 add_convert_fusion
  141.6 1.5 collective-permute-start.31
  143.3 8.7 %collective-permute-start.29 = (bf16[12,48,256]{2,1,0:T(8,128)(2,1)S(1)}, bf16[12,48,256]{2,1,0:T(8,128)(2,1)S(1)}, u32[]{:S(2)}, u32[]{:S(2)}) collective-permute-start(bf16[12,48,256]{2,1,0:T(8,128)(2,1)S(1)} %copy-done.12), channel_id=1, source_target_pairs={{0,1},{1,2},{2,3},{3,0},{4,5},{5,6},{6,7},{7,4},{8,9},{9,10},{10,1... | collective-permute-start | bytes 884744 | tf_op jit(solution)/shard_map/ppermute | solution.py:13
  152.1 5.6 %collective-permute-done.29 = bf16[12,48,256]{2,1,0:T(8,128)(2,1)S(1)} collective-permute-done((bf16[12,48,256]{2,1,0:T(8,128)(2,1)S(1)}, bf16[12,48,256]{2,1,0:T(8,128)(2,1)S(1)}, u32[]{:S(2)}, u32[]{:S(2)}) %collective-permute-start.29) | collective-permute-done | bytes 294944 | tf_op jit(solution)/shard_map/ppermute | solution.py:13
  158.5 4.2 %collective-permute-start.32 = (bf16[12,48,256]{2,1,0:T(8,128)(2,1)}, bf16[12,48,256]{2,1,0:T(8,128)(2,1)}, u32[]{:S(2)}, u32[]{:S(2)}) collective-permute-start(bf16[12,48,256]{2,1,0:T(8,128)(2,1)} %broadcast_select_fusion.15), channel_id=1, source_target_pairs={{0,2},{1,3},{2,0},{3,1},{4,6},{5,7},{6,4},{7,5},{8,10},{9,11},{10,... | collective-permute-start | bytes 884744 | tf_op jit(solution)/shard_map/ppermute | solution.py:13
  162.8 19.1 %while.56 = (s32[]{:T(128)}, bf16[1920,128]{1,0:T(8,128)(2,1)S(1)}, bf16[1920,128]{1,0:T(8,128)(2,1)S(1)}, bf16[1920,128]{1,0:T(8,128)(2,1)S(1)}, bf16[12,48,256...) while((s32[]{:T(128)}, bf16[1920,128]{1,0:T(8,128)(2,1)S(1)}, ...), condition=%wide.region_9.10_spmd, body=%wide.region_8.9_spmd.sunk | while | flops 2271166464 | bytes 77368712 | solution.py:201
  164.9 1.5 collective-permute-start.8
  166.5 5.8 %collective-permute-done.9 = bf16[960,128]{1,0:T(8,128)(2,1)S(1)} collective-permute-done((bf16[960,128]{1,0:T(8,128)(2,1)}, bf16[960,128]{1,0:T(8,128)(2,1)S(1)}, u32[]{:S(2)}, u32[]{:S(2)}) %collective-permute-start.9) | collective-permute-done | bytes 245792 | tf_op jit(solution)/shard_map/while/body/ppermute | solution.py:17
  173.6 1.3 copy-done.8
  176.5 2.1 convolution_add_fusion.12
  185.2 8.3 %collective-permute-done.33 = bf16[12,48,256]{2,1,0:T(8,128)(2,1)S(1)} collective-permute-done((bf16[12,48,256]{2,1,0:T(8,128)(2,1)S(1)}, bf16[12,48,256]{2,1,0:T(8,128)(2,1)S(1)}, u32[]{:S(2)}, u32[]{:S(2)}) %collective-permute-start.33) | collective-permute-done | bytes 294944 | tf_op jit(solution)/shard_map/ppermute | solution.py:13
  193.8 1.6 collective-permute-start.35
  195.6 3.8 %collective-permute-done.35 = bf16[4,48,2,1,128]{4,2,1,0,3:T(2,128)(2,1)S(1)} collective-permute-done((bf16[4,48,2,1,128]{4,2,1,0,3:T(2,128)(2,1)S(1)}, bf16[4,48,2,1,128]{4,2,1,0,3:T(2,128)(2,1)S(1)}, u32[]{:S(2)}, u32[]{:S(2)}) %collective-permute-start.35) | collective-permute-done | bytes 98336 | tf_op jit(solution)/shard_map/ppermute | solution.py:17
  200.6 6.7 %collective-permute-done.37 = bf16[12,48,256]{2,1,0:T(8,128)(2,1)S(1)} collective-permute-done((bf16[12,48,256]{2,1,0:T(8,128)(2,1)S(1)}, bf16[12,48,256]{2,1,0:T(8,128)(2,1)S(1)}, u32[]{:S(2)}, u32[]{:S(2)}) %collective-permute-start.37) | collective-permute-done | bytes 294944 | tf_op jit(solution)/shard_map/ppermute | solution.py:13
  208.3 1.6 collective-permute-start.39
  210.5 3.4 %collective-permute-done.39 = bf16[4,48,2,1,128]{4,2,1,0,3:T(2,128)(2,1)S(1)} collective-permute-done((bf16[4,48,2,1,128]{4,2,1,0,3:T(2,128)(2,1)S(1)}, bf16[4,48,2,1,128]{4,2,1,0,3:T(2,128)(2,1)S(1)}, u32[]{:S(2)}, u32[]{:S(2)}) %collective-permute-start.39) | collective-permute-done | bytes 98336 | tf_op jit(solution)/shard_map/ppermute | solution.py:17
  213.9 1.3 collective-permute-done.40
  218.6 2.1 copy.19
  (173 shorter events, 39.7 us)
Async XLA Ops:
  0.0 18.7 %copy-start = (bf16[2048,512]{1,0:T(8,128)(2,1)S(1)}, bf16[2048,512]{1,0:T(8,128)(2,1)}, u32[]{:S(2)}) copy-start(bf16[2048,512]{1,0:T(8,128)(2,1)} %param.17) | copy-start | bytes 6291460
  0.0 17.4 %copy-start.18 = (s32[4]{0:T(128)S(1)}, s32[4]{0:T(128)}, u32[]{:S(2)}) copy-start(s32[4]{0:T(128)} %param.20) | copy-start | bytes 52
  1.7 9.3 %collective-permute-start.12 = (bf16[1024,128]{1,0:T(8,128)(2,1)S(1)}, bf16[1024,128]{1,0:T(8,128)(2,1)S(1)}, u32[]{:S(2)}, u32[]{:S(2)}) collective-permute-start(bf16[1024,128]{1,0:T(8,128)(2,1)S(1)} %get-tuple-element.420), channel_id=1, source_target_pairs={{0,8},{4,12},{8,0},{12,4},{1,9},{5,13},{9,1},{13,5},{2,10},{6,14},... | collective-permute-start | bytes 786440 | tf_op jit(solution)/shard_map/ppermute | solution.py:17
  4.7 3.6 %collective-permute-start.13 = (bf16[2048]{0:T(1024)(128)(2,1)}, bf16[2048]{0:T(1024)(128)(2,1)S(1)}, u32[]{:S(2)}, u32[]{:S(2)}) collective-permute-start(bf16[2048]{0:T(1024)(128)(2,1)} %param.16), channel_id=1, source_target_pairs={{0,0},{1,4},{2,8},{3,12},{4,1},{5,5},{6,9},{7,13},{8,2},{9,6},{10,... | collective-permute-start | bytes 12296 | tf_op jit(solution)/shard_map/ppermute | solution.py:165
  11.1 8.0 %collective-permute-start.14 = (bf16[1024,128]{1,0:T(8,128)(2,1)S(1)}, bf16[1024,128]{1,0:T(8,128)(2,1)S(1)}, u32[]{:S(2)}, u32[]{:S(2)}) collective-permute-start(bf16[1024,128]{1,0:T(8,128)(2,1)S(1)} %get-tuple-element.606), channel_id=1, source_target_pairs={{0,0},{1,4},{2,6},{3,2},{4,1},{5,5},{6,7},{7,3},{8,8},{9,12},{10,1... | collective-permute-start | bytes 786440 | tf_op jit(solution)/shard_map/ppermute | solution.py:165
  11.8 16.3 %collective-permute-start.15 = (bf16[1024,128]{1,0:T(8,128)(2,1)S(1)}, bf16[1024,128]{1,0:T(8,128)(2,1)}, u32[]{:S(2)}, u32[]{:S(2)}) collective-permute-start(bf16[1024,128]{1,0:T(8,128)(2,1)S(1)} %get-tuple-element.605), channel_id=1, source_target_pairs={{0,2},{1,6},{2,4},{3,0},{4,3},{5,7},{6,5},{7,1},{8,10},{9,14},{10,... | collective-permute-start | bytes 786440 | tf_op jit(solution)/shard_map/ppermute | solution.py:165
  16.8 11.2 %collective-permute-start.16 = (bf16[1024,128]{1,0:T(8,128)(2,1)S(1)}, bf16[1024,128]{1,0:T(8,128)(2,1)S(1)}, u32[]{:S(2)}, u32[]{:S(2)}) collective-permute-start(bf16[1024,128]{1,0:T(8,128)(2,1)S(1)} %get-tuple-element.425), channel_id=1, source_target_pairs={{0,8},{4,12},{8,0},{12,4},{1,9},{5,13},{9,1},{13,5},{2,10},{6,14},... | collective-permute-start | bytes 786440 | tf_op jit(solution)/shard_map/ppermute | solution.py:17
  28.1 9.1 %copy-start.13 = (bf16[1024,128]{1,0:T(8,128)(2,1)}, bf16[1024,128]{1,0:T(8,128)(2,1)S(1)}, u32[]{:S(2)}) copy-start(bf16[1024,128]{1,0:T(8,128)(2,1)S(1)} %collective-permute-done.16) | copy-start | bytes 786436
  29.2 14.5 %collective-permute-start.17 = (bf16[1024,256]{1,0:T(8,128)(2,1)S(1)}, bf16[1024,256]{1,0:T(8,128)(2,1)S(1)}, u32[]{:S(2)}, u32[]{:S(2)}) collective-permute-start(bf16[1024,256]{1,0:T(8,128)(2,1)S(1)} %constant_dynamic-update-slice_fusion.2), channel_id=1, source_target_pairs={{0,8},{4,12},{8,0},{12,4},{1,9},{5,13},{9,1},{13,5},{2,10},{6,14},... | collective-permute-start | bytes 1572872 | tf_op jit(solution)/shard_map/ppermute | solution.py:17
  43.8 3.3 %collective-permute-start.18 = (bf16[2048,256]{1,0:T(8,128)(2,1)S(1)}, bf16[2048,256]{1,0:T(8,128)(2,1)S(1)}, u32[]{:S(2)}, u32[]{:S(2)}) collective-permute-start(bf16[2048,256]{1,0:T(8,128)(2,1)S(1)} %pad_maximum_fusion.7.near), channel_id=1, source_target_pairs={{0,4},{4,0},{8,12},{12,8},{1,5},{5,1},{9,13},{13,9},{2,6},{6,2},{1... | collective-permute-start | bytes 3145736 | tf_op jit(solution)/shard_map/ppermute | solution.py:17
  44.1 3.0 %collective-permute-start.21 = (f32[1,512]{1,0:T(1,128)S(1)}, f32[1,512]{1,0:T(1,128)S(1)}, u32[]{:S(2)}, u32[]{:S(2)}) collective-permute-start(f32[1,512]{1,0:T(1,128)S(1)} %fusion.30), channel_id=1, source_target_pairs={{0,4},{4,0},{8,12},{12,8},{1,5},{5,1},{9,13},{13,9},{2,6},{6,2},{1... | collective-permute-start | bytes 6152 | tf_op jit(solution)/shard_map/ppermute | solution.py:17
  44.7 10.1 %collective-permute-start.19 = (bf16[1024,128]{1,0:T(8,128)(2,1)S(1)}, bf16[1024,128]{1,0:T(8,128)(2,1)S(1)}, u32[]{:S(2)}, u32[]{:S(2)}) collective-permute-start(bf16[1024,128]{1,0:T(8,128)(2,1)S(1)} %get-tuple-element.604), channel_id=1, source_target_pairs={{0,0},{1,4},{2,6},{3,2},{4,1},{5,5},{6,7},{7,3},{8,8},{9,12},{10,1... | collective-permute-start | bytes 786440 | tf_op jit(solution)/shard_map/ppermute | solution.py:165
  45.4 13.0 %collective-permute-start.20 = (bf16[1024,128]{1,0:T(8,128)(2,1)S(1)}, bf16[1024,128]{1,0:T(8,128)(2,1)S(1)}, u32[]{:S(2)}, u32[]{:S(2)}) collective-permute-start(bf16[1024,128]{1,0:T(8,128)(2,1)S(1)} %get-tuple-element.603), channel_id=1, source_target_pairs={{0,2},{1,6},{2,4},{3,0},{4,3},{5,7},{6,5},{7,1},{8,10},{9,14},{10,... | collective-permute-start | bytes 786440 | tf_op jit(solution)/shard_map/ppermute | solution.py:165
  59.0 32.2 %collective-permute-start.24 = (bf16[2560,128]{1,0:T(8,128)(2,1)}, bf16[2560,128]{1,0:T(8,128)(2,1)}, u32[]{:S(2)}, u32[]{:S(2)}) collective-permute-start(bf16[2560,128]{1,0:T(8,128)(2,1)} %get-tuple-element.443), channel_id=1, source_target_pairs={{0,1},{1,0},{2,3},{3,2},{4,5},{5,4},{6,7},{7,6},{8,9},{9,8},{10,11... | collective-permute-start | bytes 1966088 | tf_op jit(solution)/shard_map/ppermute | solution.py:17
  59.6 31.6 %collective-permute-start.22 = (bf16[1280,128]{1,0:T(8,128)(2,1)}, bf16[1280,128]{1,0:T(8,128)(2,1)}, u32[]{:S(2)}, u32[]{:S(2)}) collective-permute-start(bf16[1280,128]{1,0:T(8,128)(2,1)} %get-tuple-element.441), channel_id=1, source_target_pairs={{0,2},{1,3},{2,0},{3,1},{4,6},{5,7},{6,4},{7,5},{8,10},{9,11},{10,... | collective-permute-start | bytes 983048 | tf_op jit(solution)/shard_map/ppermute | solution.py:17
  61.0 30.2 %collective-permute-start.23 = (bf16[1280,128]{1,0:T(8,128)(2,1)}, bf16[1280,128]{1,0:T(8,128)(2,1)}, u32[]{:S(2)}, u32[]{:S(2)}) collective-permute-start(bf16[1280,128]{1,0:T(8,128)(2,1)} %get-tuple-element.442), channel_id=1, source_target_pairs={{0,3},{1,2},{2,1},{3,0},{4,7},{5,6},{6,5},{7,4},{8,11},{9,10},{10,... | collective-permute-start | bytes 983048 | tf_op jit(solution)/shard_map/ppermute | solution.py:17
  65.3 14.0 %collective-permute-start = (bf16[1024,256]{1,0:T(8,128)(2,1)S(1)}, bf16[1024,256]{1,0:T(8,128)(2,1)}, u32[]{:S(2)}, u32[]{:S(2)}) collective-permute-start(bf16[1024,256]{1,0:T(8,128)(2,1)S(1)} %copy.33), channel_id=1, source_target_pairs={{0,8},{4,12},{8,0},{12,4},{1,9},{5,13},{9,1},{13,5},{2,10},{6,14},... | collective-permute-start | bytes 1572872 | tf_op jit(solution)/shard_map/while/body/ppermute | solution.py:17
  65.9 13.3 %collective-permute-start.1 = (f32[1,512]{1,0:T(1,128)S(1)}, f32[1,512]{1,0:T(1,128)S(1)}, u32[]{:S(2)}, u32[]{:S(2)}) collective-permute-start(f32[1,512]{1,0:T(1,128)S(1)} %copy.34), channel_id=1, source_target_pairs={{0,8},{4,12},{8,0},{12,4},{1,9},{5,13},{9,1},{13,5},{2,10},{6,14},... | collective-permute-start | bytes 6152 | tf_op jit(solution)/shard_map/while/body/ppermute | solution.py:17
  80.4 2.7 %collective-permute-start.2 = (bf16[2048,256]{1,0:T(8,128)(2,1)S(1)}, bf16[2048,256]{1,0:T(8,128)(2,1)S(1)}, u32[]{:S(2)}, u32[]{:S(2)}) collective-permute-start(bf16[2048,256]{1,0:T(8,128)(2,1)S(1)} %pad_maximum_fusion.18.near), channel_id=1, source_target_pairs={{0,4},{4,0},{8,12},{12,8},{1,5},{5,1},{9,13},{13,9},{2,6},{6,2},{1... | collective-permute-start | bytes 3145736 | tf_op jit(solution)/shard_map/while/body/ppermute | solution.py:17
  92.3 12.7 %copy-start.15 = (f32[1,512]{1,0:T(1,128)S(1)}, f32[1,512]{1,0:T(1,128)}, u32[]{:S(2)}) copy-start(f32[1,512]{1,0:T(1,128)} %get-tuple-element.475) | copy-start | bytes 6148
  92.3 12.7 %copy-start.16 = (f32[1,128]{1,0:T(1,128)S(1)}, f32[1,128]{1,0:T(1,128)}, u32[]{:S(2)}) copy-start(f32[1,128]{1,0:T(1,128)} %param.18) | copy-start | bytes 1540
  92.3 8.2 %collective-permute-start.25 = (bf16[640,128]{1,0:T(8,128)(2,1)S(1)}, bf16[640,128]{1,0:T(8,128)(2,1)S(1)}, u32[]{:S(2)}, u32[]{:S(2)}) collective-permute-start(bf16[640,128]{1,0:T(8,128)(2,1)S(1)} %slice.147), channel_id=1, source_target_pairs={{0,3},{1,2},{2,1},{3,0},{4,7},{5,6},{6,5},{7,4},{8,11},{9,10},{10,... | collective-permute-start | bytes 491528 | tf_op jit(solution)/shard_map/ppermute | solution.py:17
  100.5 38.9 %collective-permute-start.26 = (bf16[1920,128]{1,0:T(8,128)(2,1)}, bf16[1920,128]{1,0:T(8,128)(2,1)}, u32[]{:S(2)}, u32[]{:S(2)}) collective-permute-start(bf16[1920,128]{1,0:T(8,128)(2,1)} %get-tuple-element.462), channel_id=1, source_target_pairs={{0,2},{1,3},{2,0},{3,1},{4,6},{5,7},{6,4},{7,5},{8,10},{9,11},{10,... | collective-permute-start | bytes 1474568 | tf_op jit(solution)/shard_map/ppermute | solution.py:17
  103.6 35.8 %collective-permute-start.27 = (bf16[1920,128]{1,0:T(8,128)(2,1)}, bf16[1920,128]{1,0:T(8,128)(2,1)}, u32[]{:S(2)}, u32[]{:S(2)}) collective-permute-start(bf16[1920,128]{1,0:T(8,128)(2,1)} %get-tuple-element.463), channel_id=1, source_target_pairs={{0,3},{1,2},{2,1},{3,0},{4,7},{5,6},{6,5},{7,4},{8,11},{9,10},{10,... | collective-permute-start | bytes 1474568 | tf_op jit(solution)/shard_map/ppermute | solution.py:17
  104.9 34.5 %collective-permute-start.28 = (bf16[1920,128]{1,0:T(8,128)(2,1)}, bf16[1920,128]{1,0:T(8,128)(2,1)}, u32[]{:S(2)}, u32[]{:S(2)}) collective-permute-start(bf16[1920,128]{1,0:T(8,128)(2,1)} %get-tuple-element.464), channel_id=1, source_target_pairs={{0,1},{1,0},{2,3},{3,2},{4,5},{5,4},{6,7},{7,6},{8,9},{9,8},{10,11... | collective-permute-start | bytes 1474568 | tf_op jit(solution)/shard_map/ppermute | solution.py:17
  105.0 34.4 %copy-start.10 = (f32[1920,128]{1,0:T(8,128)S(1)}, f32[1920,128]{1,0:T(8,128)}, u32[]{:S(2)}) copy-start(f32[1920,128]{1,0:T(8,128)} %get-tuple-element.478) | copy-start | bytes 2949124
  105.1 11.4 %collective-permute-start.3 = (bf16[1920,128]{1,0:T(8,128)(2,1)S(1)}, bf16[1920,128]{1,0:T(8,128)(2,1)S(1)}, u32[]{:S(2)}, u32[]{:S(2)}) collective-permute-start(bf16[1920,128]{1,0:T(8,128)(2,1)S(1)} %copy.52), channel_id=1, source_target_pairs={{0,8},{4,12},{8,0},{12,4},{1,9},{5,13},{9,1},{13,5},{2,10},{6,14},... | collective-permute-start | bytes 1474568 | tf_op jit(solution)/shard_map/while/body/ppermute | solution.py:17
  106.7 11.1 %collective-permute-start.4 = (bf16[1920,128]{1,0:T(8,128)(2,1)S(1)}, bf16[1920,128]{1,0:T(8,128)(2,1)S(1)}, u32[]{:S(2)}, u32[]{:S(2)}) collective-permute-start(bf16[1920,128]{1,0:T(8,128)(2,1)S(1)} %copy.52), channel_id=1, source_target_pairs={{0,16},{16,0},{1,17},{17,1},{2,18},{18,2},{3,19},{19,3},{4,20},{20... | collective-permute-start | bytes 1474568 | tf_op jit(solution)/shard_map/while/body/ppermute | solution.py:17
  118.0 13.7 %collective-permute-start.6 = (bf16[1920,256]{1,0:T(8,128)(2,1)S(1)}, bf16[1920,256]{1,0:T(8,128)(2,1)}, u32[]{:S(2)}, u32[]{:S(2)}) collective-permute-start(bf16[1920,256]{1,0:T(8,128)(2,1)S(1)} %pad_maximum_fusion.19), channel_id=1, source_target_pairs={{0,4},{4,0},{8,12},{12,8},{1,5},{5,1},{9,13},{13,9},{2,6},{6,2},{1... | collective-permute-start | bytes 2949128 | tf_op jit(solution)/shard_map/while/body/ppermute | solution.py:17
  118.1 13.6 %collective-permute-start.5 = (bf16[1920,128]{1,0:T(8,128)(2,1)S(1)}, bf16[1920,128]{1,0:T(8,128)(2,1)S(1)}, u32[]{:S(2)}, u32[]{:S(2)}) collective-permute-start(bf16[1920,128]{1,0:T(8,128)(2,1)S(1)} %collective-permute-done.4), channel_id=1, source_target_pairs={{0,8},{4,12},{8,0},{12,4},{1,9},{5,13},{9,1},{13,5},{2,10},{6,14},... | collective-permute-start | bytes 1474568 | tf_op jit(solution)/shard_map/while/body/ppermute | solution.py:17
  118.6 13.4 %copy-start.7 = (bf16[576,1920]{1,0:T(8,128)(2,1)S(1)}, bf16[576,1920]{1,0:T(8,128)(2,1)}, u32[]{:S(2)}) copy-start(bf16[576,1920]{1,0:T(8,128)(2,1)} %get-tuple-element.971) | copy-start | bytes 6635524 | tf_op jit(solution)/shard_map/while
  131.9 4.7 %collective-permute-start.7 = (bf16[1920,256]{1,0:T(8,128)(2,1)S(1)}, bf16[1920,256]{1,0:T(8,128)(2,1)S(1)}, u32[]{:S(2)}, u32[]{:S(2)}) collective-permute-start(bf16[1920,256]{1,0:T(8,128)(2,1)S(1)} %pad_maximum_fusion.20), channel_id=1, source_target_pairs={{0,4},{4,0},{8,12},{12,8},{1,5},{5,1},{9,13},{13,9},{2,6},{6,2},{1... | collective-permute-start | bytes 2949128 | tf_op jit(solution)/shard_map/while/body/ppermute | solution.py:17
  141.0 16.7 %collective-permute-start.30 = (bf16[1920,128]{1,0:T(8,128)(2,1)S(1)}, bf16[1920,128]{1,0:T(8,128)(2,1)S(1)}, u32[]{:S(2)}, u32[]{:S(2)}) collective-permute-start(bf16[1920,128]{1,0:T(8,128)(2,1)S(1)} %add_convert_fusion), channel_id=1, source_target_pairs={{0,8},{4,12},{8,0},{12,4},{1,9},{5,13},{9,1},{13,5},{2,10},{6,14},... | collective-permute-start | bytes 1474568 | tf_op jit(solution)/shard_map/ppermute | solution.py:17
  141.6 16.2 %collective-permute-start.31 = (bf16[1920,128]{1,0:T(8,128)(2,1)S(1)}, bf16[1920,128]{1,0:T(8,128)(2,1)S(1)}, u32[]{:S(2)}, u32[]{:S(2)}) collective-permute-start(bf16[1920,128]{1,0:T(8,128)(2,1)S(1)} %add_convert_fusion), channel_id=1, source_target_pairs={{0,16},{16,0},{1,17},{17,1},{2,18},{18,2},{3,19},{19,3},{4,20},{20... | collective-permute-start | bytes 1474568 | tf_op jit(solution)/shard_map/ppermute | solution.py:17
  143.3 14.4 %collective-permute-start.29 = (bf16[12,48,256]{2,1,0:T(8,128)(2,1)S(1)}, bf16[12,48,256]{2,1,0:T(8,128)(2,1)S(1)}, u32[]{:S(2)}, u32[]{:S(2)}) collective-permute-start(bf16[12,48,256]{2,1,0:T(8,128)(2,1)S(1)} %copy-done.12), channel_id=1, source_target_pairs={{0,1},{1,2},{2,3},{3,0},{4,5},{5,6},{6,7},{7,4},{8,9},{9,10},{10,1... | collective-permute-start | bytes 884744 | tf_op jit(solution)/shard_map/ppermute | solution.py:13
  158.5 23.3 %collective-permute-start.32 = (bf16[12,48,256]{2,1,0:T(8,128)(2,1)}, bf16[12,48,256]{2,1,0:T(8,128)(2,1)}, u32[]{:S(2)}, u32[]{:S(2)}) collective-permute-start(bf16[12,48,256]{2,1,0:T(8,128)(2,1)} %broadcast_select_fusion.15), channel_id=1, source_target_pairs={{0,2},{1,3},{2,0},{3,1},{4,6},{5,7},{6,4},{7,5},{8,10},{9,11},{10,... | collective-permute-start | bytes 884744 | tf_op jit(solution)/shard_map/ppermute | solution.py:13
  163.0 10.2 %collective-permute-start.10 = (bf16[1920,256]{1,0:T(8,128)(2,1)S(1)}, bf16[1920,256]{1,0:T(8,128)(2,1)}, u32[]{:S(2)}, u32[]{:S(2)}) collective-permute-start(bf16[1920,256]{1,0:T(8,128)(2,1)S(1)} %pad_maximum_fusion.22), channel_id=1, source_target_pairs={{0,4},{4,0},{8,12},{12,8},{1,5},{5,1},{9,13},{13,9},{2,6},{6,2},{1... | collective-permute-start | bytes 2949128 | tf_op jit(solution)/shard_map/while/body/ppermute | solution.py:17
  163.8 8.6 %collective-permute-start.9 = (bf16[960,128]{1,0:T(8,128)(2,1)}, bf16[960,128]{1,0:T(8,128)(2,1)S(1)}, u32[]{:S(2)}, u32[]{:S(2)}) collective-permute-start(bf16[960,128]{1,0:T(8,128)(2,1)} %slice.171), channel_id=1, source_target_pairs={{0,8},{4,12},{8,0},{12,4},{1,9},{5,13},{9,1},{13,5},{2,10},{6,14},... | collective-permute-start | bytes 737288 | tf_op jit(solution)/shard_map/while/body/ppermute | solution.py:17
  164.9 8.3 %collective-permute-start.8 = (bf16[960,128]{1,0:T(8,128)(2,1)}, bf16[960,128]{1,0:T(8,128)(2,1)S(1)}, u32[]{:S(2)}, u32[]{:S(2)}) collective-permute-start(bf16[960,128]{1,0:T(8,128)(2,1)} %slice.170), channel_id=1, source_target_pairs={{0,16},{16,0},{1,17},{17,1},{2,18},{18,2},{3,19},{19,3},{4,20},{20... | collective-permute-start | bytes 737288 | tf_op jit(solution)/shard_map/while/body/ppermute | solution.py:17
  173.5 5.9 %collective-permute-start.11 = (bf16[1920,256]{1,0:T(8,128)(2,1)S(1)}, bf16[1920,256]{1,0:T(8,128)(2,1)S(1)}, u32[]{:S(2)}, u32[]{:S(2)}) collective-permute-start(bf16[1920,256]{1,0:T(8,128)(2,1)S(1)} %pad_maximum_fusion.23), channel_id=1, source_target_pairs={{0,4},{4,0},{8,12},{12,8},{1,5},{5,1},{9,13},{13,9},{2,6},{6,2},{1... | collective-permute-start | bytes 2949128 | tf_op jit(solution)/shard_map/while/body/ppermute | solution.py:17
  183.2 10.3 %collective-permute-start.33 = (bf16[12,48,256]{2,1,0:T(8,128)(2,1)S(1)}, bf16[12,48,256]{2,1,0:T(8,128)(2,1)S(1)}, u32[]{:S(2)}, u32[]{:S(2)}) collective-permute-start(bf16[12,48,256]{2,1,0:T(8,128)(2,1)S(1)} %copy-done.11), channel_id=1, source_target_pairs={{0,1},{1,2},{2,3},{3,0},{4,5},{5,6},{6,7},{7,4},{8,9},{9,10},{10,1... | collective-permute-start | bytes 884744 | tf_op jit(solution)/shard_map/ppermute | solution.py:13
  193.6 13.7 %collective-permute-start.37 = (bf16[12,48,256]{2,1,0:T(8,128)(2,1)S(1)}, bf16[12,48,256]{2,1,0:T(8,128)(2,1)S(1)}, u32[]{:S(2)}, u32[]{:S(2)}) collective-permute-start(bf16[12,48,256]{2,1,0:T(8,128)(2,1)S(1)} %broadcast_select_fusion.14), channel_id=1, source_target_pairs={{0,2},{1,3},{2,0},{3,1},{4,6},{5,7},{6,4},{7,5},{8,10},{9,11},{10,... | collective-permute-start | bytes 884744 | tf_op jit(solution)/shard_map/ppermute | solution.py:13
  193.7 1.9 collective-permute-start.34
  193.8 5.7 %collective-permute-start.35 = (bf16[4,48,2,1,128]{4,2,1,0,3:T(2,128)(2,1)S(1)}, bf16[4,48,2,1,128]{4,2,1,0,3:T(2,128)(2,1)S(1)}, u32[]{:S(2)}, u32[]{:S(2)}) collective-permute-start(bf16[4,48,2,1,128]{4,2,1,0,3:T(2,128)(2,1)S(1)} %squeeze.30), channel_id=1, source_target_pairs={{0,8},{4,12},{8,0},{12,4},{1,9},{5,13},{9,1},{13,5},{2,10},{6,14},... | collective-permute-start | bytes 294920 | tf_op jit(solution)/shard_map/ppermute | solution.py:17
  195.4 5.2 %collective-permute-start.36 = (bf16[4,48,2,1,128]{4,2,1,0,3:T(2,128)(2,1)S(1)}, bf16[4,48,2,1,128]{4,2,1,0,3:T(2,128)(2,1)S(1)}, u32[]{:S(2)}, u32[]{:S(2)}) collective-permute-start(bf16[4,48,2,1,128]{4,2,1,0,3:T(2,128)(2,1)S(1)} %squeeze.31), channel_id=1, source_target_pairs={{0,12},{4,8},{8,4},{12,0},{1,13},{5,9},{9,5},{13,1},{2,14},{6,10},... | collective-permute-start | bytes 294920 | tf_op jit(solution)/shard_map/ppermute | solution.py:17
  208.1 2.4 %collective-permute-start.38 = (bf16[4,48,2,1,128]{4,2,1,0,3:T(2,128)(2,1)S(1)}, bf16[4,48,2,1,128]{4,2,1,0,3:T(2,128)(2,1)S(1)}, u32[]{:S(2)}, u32[]{:S(2)}) collective-permute-start(bf16[4,48,2,1,128]{4,2,1,0,3:T(2,128)(2,1)S(1)} %squeeze.33), channel_id=1, source_target_pairs={{0,4},{4,0},{8,12},{12,8},{1,5},{5,1},{9,13},{13,9},{2,6},{6,2},{1... | collective-permute-start | bytes 294920 | tf_op jit(solution)/shard_map/ppermute | solution.py:17
  208.3 5.7 %collective-permute-start.39 = (bf16[4,48,2,1,128]{4,2,1,0,3:T(2,128)(2,1)S(1)}, bf16[4,48,2,1,128]{4,2,1,0,3:T(2,128)(2,1)S(1)}, u32[]{:S(2)}, u32[]{:S(2)}) collective-permute-start(bf16[4,48,2,1,128]{4,2,1,0,3:T(2,128)(2,1)S(1)} %squeeze.34), channel_id=1, source_target_pairs={{0,8},{4,12},{8,0},{12,4},{1,9},{5,13},{9,1},{13,5},{2,10},{6,14},... | collective-permute-start | bytes 294920 | tf_op jit(solution)/shard_map/ppermute | solution.py:17
  210.0 5.2 %collective-permute-start.40 = (bf16[4,48,2,1,128]{4,2,1,0,3:T(2,128)(2,1)S(1)}, bf16[4,48,2,1,128]{4,2,1,0,3:T(2,128)(2,1)S(1)}, u32[]{:S(2)}, u32[]{:S(2)}) collective-permute-start(bf16[4,48,2,1,128]{4,2,1,0,3:T(2,128)(2,1)S(1)} %squeeze.35), channel_id=1, source_target_pairs={{0,12},{4,8},{8,4},{12,0},{1,13},{5,9},{9,5},{13,1},{2,14},{6,10},... | collective-permute-start | bytes 294920 | tf_op jit(solution)/shard_map/ppermute | solution.py:17
  (13 other events, 39.6 us)

commit v22 on v21

--- a/solution.py
+++ b/solution.py
@@ -371,7 +371,7 @@
     shifted, values = step((shifted_2(keys, "head", 2), values))
 
     picked = outgoing(rolled(keys, shifted, 2))
-    shifted, picked = step((shifted_2(values, "head", 1), picked))
+    values, shifted = step((values, shifted_2(values, "head", 1)))
 
     values = step(rolled(values, shifted, 1))
     arrived, shifted = step((to_owners(picked), shifted_2(values, "head", 2)))

time: 221 us -> 220 us (level)
  no operation moved by 1% of the time
where the time goes in v22:
time: 220 us; the launch traced here: 219 us
  waiting for transfers between devices  99.5 us (45%)
  starting transfers between devices  53.2 us (24%)
  local copies, waits for them, and re-layouts  24.9 us (11%)
  Pallas kernels  15.7 us (7%)
  other arithmetic  14.8 us (7%)
  matrix products  9.93 us (5%)
    ppermute x32, waiting for transfers between devices, swapped(): lax.ppermute(shard, axis, [(i, i ^ bit) for i in range(lax.axis_size(axis...  67.2 us
    ppermute x32, starting transfers between devices, swapped(): lax.ppermute(shard, axis, [(i, i ^ bit) for i in range(lax.axis_size(axis...  29.7 us
    ppermute x4, waiting for transfers between devices, shifted_2(): lax.ppermute(shard, axis, [(i, (i + by) % count) for i in range(count)])  19.7 us
    pallas_call x2, Pallas kernels, product_terms(): pl.pallas_call(terms_body, out_shape=shapes, grid_spec=pltpu.PrefetchScal...  15.7 us
    ppermute x4, starting transfers between devices, shifted_2(): lax.ppermute(shard, axis, [(i, (i + by) % count) for i in range(count)])  14 us
    ppermute x5, waiting for transfers between devices, moved(): return lax.ppermute(shard, ('tile', 'head'), pairs)  12.6 us
    dot_general x11, matrix products, add_columns(): return jnp.dot(operand, portion, preferred_element_type=jnp.float32)  9.74 us
    ppermute x5, starting transfers between devices, moved(): return lax.ppermute(shard, ('tile', 'head'), pairs)  9.46 us
  transfers between devices with their start and end apart: 41, of which 19 were waited for; matrix products, arithmetic and copies ran while one was open for 14% of the time, Pallas kernels for 7%

profile of v22, /device:TPU:0, one launch (start us, length us, event | category | flops | bytes accessed | tf_op | source)
XLA Modules:
  0.0 219.5 jit_solution(11139340679815796385)
XLA Ops:
  0.0 1.7 fusion.24
  1.7 3.0 %collective-permute-start.12 = (bf16[1024,128]{1,0:T(8,128)(2,1)S(1)}, bf16[1024,128]{1,0:T(8,128)(2,1)S(1)}, u32[]{:S(2)}, u32[]{:S(2)}) collective-permute-start(bf16[1024,128]{1,0:T(8,128)(2,1)S(1)} %get-tuple-element.417), channel_id=1, source_target_pairs={{0,8},{4,12},{8,0},{12,4},{1,9},{5,13},{9,1},{13,5},{2,10},{6,14},... | collective-permute-start | bytes 786440 | tf_op jit(solution)/shard_map/ppermute | solution.py:17
  4.7 1.3 collective-permute-start.13
  6.1 2.2 %fusion.23 = (bf16[1024,128]{1,0:T(8,128)(2,1)S(1)}, bf16[1024,128]{1,0:T(8,128)(2,1)}) fusion(bf16[2048,512]{1,0:T(8,128)(2,1)} %param.17, s32[]{:T(128)S(6)} %select_n.307, s32[]{:T(128)S(6)} %select_n.309, s32[]{:T(128)S(6)} %select_n.303), kind=kLoop, calls=%fused_computation.124 | loop fusion | bytes 1048588 | tf_op jit(solution)/shard_map/dynamic_slice | solution.py:246
  8.3 2.7 %collective-permute-done.12 = bf16[1024,128]{1,0:T(8,128)(2,1)S(1)} collective-permute-done((bf16[1024,128]{1,0:T(8,128)(2,1)S(1)}, bf16[1024,128]{1,0:T(8,128)(2,1)S(1)}, u32[]{:S(2)}, u32[]{:S(2)}) %collective-permute-start.12) | collective-permute-done | bytes 262176 | tf_op jit(solution)/shard_map/ppermute | solution.py:17
  11.8 5.1 %collective-permute-start.15 = (bf16[1024,128]{1,0:T(8,128)(2,1)S(1)}, bf16[1024,128]{1,0:T(8,128)(2,1)}, u32[]{:S(2)}, u32[]{:S(2)}) collective-permute-start(bf16[1024,128]{1,0:T(8,128)(2,1)S(1)} %get-tuple-element.599), channel_id=1, source_target_pairs={{0,2},{1,6},{2,4},{3,0},{4,3},{5,7},{6,5},{7,1},{8,10},{9,14},{10,... | collective-permute-start | bytes 786440 | tf_op jit(solution)/shard_map/ppermute | solution.py:165
  19.1 9.0 %collective-permute-done.15 = bf16[1024,128]{1,0:T(8,128)(2,1)} collective-permute-done((bf16[1024,128]{1,0:T(8,128)(2,1)S(1)}, bf16[1024,128]{1,0:T(8,128)(2,1)}, u32[]{:S(2)}, u32[]{:S(2)}) %collective-permute-start.15) | collective-permute-done | bytes 262176 | tf_op jit(solution)/shard_map/ppermute | solution.py:165
  30.0 7.2 %constant_dynamic-slice_fusion = (bf16[576,1920]{1,0:T(8,128)(2,1)}, bf16[576,1920]{1,0:T(8,128)(2,1)}, bf16[576,1920]{1,0:T(8,128)(2,1)}, bf16[576,1920]{1,0:T(8,128)(2,1)}) fusion(bf16[576,7680]{1,0:T(8,128)(2,1)} %bitcast.134, s32[]{:T(128)S(6)} %select_n.316, s32[]{:T(128)S(6)} %select_n.315, s32[]{:T(128)S(6)} %select_n.314, s32[]{:T(128)S(6)} %select_n.313), kind=kLoop, calls=%fused_computation.115 | loop fusion | bytes 17694736 | tf_op jit(solution)/shard_map/dynamic_slice | solution.py:171
  37.2 6.5 %collective-permute-done.17 = bf16[1024,256]{1,0:T(8,128)(2,1)S(1)} collective-permute-done((bf16[1024,256]{1,0:T(8,128)(2,1)S(1)}, bf16[1024,256]{1,0:T(8,128)(2,1)S(1)}, u32[]{:S(2)}, u32[]{:S(2)}) %collective-permute-start.17) | collective-permute-done | bytes 524320 | tf_op jit(solution)/shard_map/ppermute | solution.py:17
  45.4 1.7 collective-permute-start.20
  47.1 7.7 %shard_map.82 = (f32[1280,128]{1,0:T(8,128)S(1)}, bf16[1280,128]{1,0:T(8,128)(2,1)}, bf16[1280,128]{1,0:T(8,128)(2,1)}, bf16[2560,128]{1,0:T(8,128)(2,1)}, f32[640,256]{1,0:T(8,128)S(1)}) custom-call(s32[1]{0:T(128)} %bitcast.13.choice, bf16[1920,2048]{1,0:T(8,128)(2,1)} %weight.1, bf16[2048,256]{1,0:T(8,128)(2,1)S(1)} %pad_maximum_fusion.7.near, ...), custom_call_target="tpu_custom_call" | custom-call | flops 4026531840 | bytes 12419072 | tf_op jit(solution)/shard_map/pallas_call | solution.py:118
  54.8 3.6 %collective-permute-done.20 = bf16[1024,128]{1,0:T(8,128)(2,1)S(1)} collective-permute-done((bf16[1024,128]{1,0:T(8,128)(2,1)S(1)}, bf16[1024,128]{1,0:T(8,128)(2,1)S(1)}, u32[]{:S(2)}, u32[]{:S(2)}) %collective-permute-start.20) | collective-permute-done | bytes 262176 | tf_op jit(solution)/shard_map/ppermute | solution.py:165
  59.6 1.4 collective-permute-start.22
  61.0 2.4 %collective-permute-start.23 = (bf16[1280,128]{1,0:T(8,128)(2,1)}, bf16[1280,128]{1,0:T(8,128)(2,1)}, u32[]{:S(2)}, u32[]{:S(2)}) collective-permute-start(bf16[1280,128]{1,0:T(8,128)(2,1)} %get-tuple-element.439), channel_id=1, source_target_pairs={{0,3},{1,2},{2,1},{3,0},{4,7},{5,6},{6,5},{7,4},{8,11},{9,10},{10,... | collective-permute-start | bytes 983048 | tf_op jit(solution)/shard_map/ppermute | solution.py:17
  64.2 27.0 %while.54 = (s32[]{:T(128)}, bf16[1024,256]{1,0:T(8,128)(2,1)}, f32[1,512]{1,0:T(1,128)S(1)}, f32[1920,128]{1,0:T(8,128)}, bf16[1920,128]{1,0:T(8,128)(2,1)}, /*...) while((s32[]{:T(128)}, bf16[1024,256]{1,0:T(8,128)(2,1)}, ...), condition=%wide.region_3.4_spmd, body=%wide.region_2.3_spmd.sunk | while | flops 4029153792 | bytes 23972084 | solution.py:201
  65.9 1.4 collective-permute-start.1
  67.3 11.9 %collective-permute-done.1 = f32[1,512]{1,0:T(1,128)S(1)} collective-permute-done((f32[1,512]{1,0:T(1,128)S(1)}, f32[1,512]{1,0:T(1,128)S(1)}, u32[]{:S(2)}, u32[]{:S(2)}) %collective-permute-start.1) | collective-permute-done | bytes 2080 | tf_op jit(solution)/shard_map/while/body/ppermute | solution.py:17
  81.0 2.1 collective-permute-done.2.far
  83.1 8.0 %body.1 = (f32[1920,128]{1,0:T(8,128)}, bf16[1920,128]{1,0:T(8,128)(2,1)}, bf16[1920,128]{1,0:T(8,128)(2,1)}, bf16[1920,128]{1,0:T(8,128)(2,1)}) custom-call(s32[1]{0:T(128)} %get-tuple-element.933.choice, bf16[1920,2048]{1,0:T(8,128)(2,1)} %get-tuple-element.934.weight, bf16[2048,256]{1,0:T(8,128)(2,1)S(1)} %pad_maximum_fusion.18.near, ...), custom_call_target="tpu_custom_call" | custom-call | flops 4026531840 | bytes 12419072 | tf_op jit(solution)/shard_map/while/body/pallas_call | solution.py:118
  92.3 1.9 collective-permute-start.25
  94.2 1.3 add_convert_fusion.1
  95.5 5.0 %collective-permute-done.25 = bf16[640,128]{1,0:T(8,128)(2,1)S(1)} collective-permute-done((bf16[640,128]{1,0:T(8,128)(2,1)S(1)}, bf16[640,128]{1,0:T(8,128)(2,1)S(1)}, u32[]{:S(2)}, u32[]{:S(2)}) %collective-permute-start.25) | collective-permute-done | bytes 163872 | tf_op jit(solution)/shard_map/ppermute | solution.py:17
  100.5 3.1 %collective-permute-start.26 = (bf16[1920,128]{1,0:T(8,128)(2,1)}, bf16[1920,128]{1,0:T(8,128)(2,1)}, u32[]{:S(2)}, u32[]{:S(2)}) collective-permute-start(bf16[1920,128]{1,0:T(8,128)(2,1)} %get-tuple-element.459), channel_id=1, source_target_pairs={{0,2},{1,3},{2,0},{3,1},{4,6},{5,7},{6,4},{7,5},{8,10},{9,11},{10,... | collective-permute-start | bytes 1474568 | tf_op jit(solution)/shard_map/ppermute | solution.py:17
  105.0 34.4 %while.55 = (s32[]{:T(128)}, bf16[1920,128]{1,0:T(8,128)(2,1)S(1)}, bf16[12,48,256]{2,1,0:T(8,128)(2,1)}, s32[]{:T(128)}, pred[]{:T(512)}, /*index=5*/bf16[576,1...) while((s32[]{:T(128)}, bf16[1920,128]{1,0:T(8,128)(2,1)S(1)}, ...), condition=%wide.region_7.8_spmd, body=%wide.region_4.7_spmd.sunk | while | flops 2271905024 | bytes 76995496 | solution.py:201
  105.1 1.6 collective-permute-start.3
  106.7 1.5 collective-permute-start.4
  108.2 8.3 %collective-permute-done.3 = bf16[1920,128]{1,0:T(8,128)(2,1)S(1)} collective-permute-done((bf16[1920,128]{1,0:T(8,128)(2,1)S(1)}, bf16[1920,128]{1,0:T(8,128)(2,1)S(1)}, u32[]{:S(2)}, u32[]{:S(2)}) %collective-permute-start.3) | collective-permute-done | bytes 491552 | tf_op jit(solution)/shard_map/while/body/ppermute | solution.py:17
  116.5 1.3 collective-permute-done.4
  118.6 13.1 %collective-permute-done.5 = bf16[1920,128]{1,0:T(8,128)(2,1)S(1)} collective-permute-done((bf16[1920,128]{1,0:T(8,128)(2,1)S(1)}, bf16[1920,128]{1,0:T(8,128)(2,1)S(1)}, u32[]{:S(2)}, u32[]{:S(2)}) %collective-permute-start.5) | collective-permute-done | bytes 491552 | tf_op jit(solution)/shard_map/while/body/ppermute | solution.py:17
  133.6 2.1 convolution_add_fusion.10
  139.4 1.6 add_convert_fusion
  141.6 1.5 collective-permute-start.31
  143.3 8.7 %collective-permute-start.29 = (bf16[12,48,256]{2,1,0:T(8,128)(2,1)S(1)}, bf16[12,48,256]{2,1,0:T(8,128)(2,1)S(1)}, u32[]{:S(2)}, u32[]{:S(2)}) collective-permute-start(bf16[12,48,256]{2,1,0:T(8,128)(2,1)S(1)} %copy-done.12), channel_id=1, source_target_pairs={{0,1},{1,2},{2,3},{3,0},{4,5},{5,6},{6,7},{7,4},{8,9},{9,10},{10,1... | collective-permute-start | bytes 884744 | tf_op jit(solution)/shard_map/ppermute | solution.py:13
  152.1 5.6 %collective-permute-done.29 = bf16[12,48,256]{2,1,0:T(8,128)(2,1)S(1)} collective-permute-done((bf16[12,48,256]{2,1,0:T(8,128)(2,1)S(1)}, bf16[12,48,256]{2,1,0:T(8,128)(2,1)S(1)}, u32[]{:S(2)}, u32[]{:S(2)}) %collective-permute-start.29) | collective-permute-done | bytes 294944 | tf_op jit(solution)/shard_map/ppermute | solution.py:13
  158.5 4.2 %collective-permute-start.32 = (bf16[12,48,256]{2,1,0:T(8,128)(2,1)}, bf16[12,48,256]{2,1,0:T(8,128)(2,1)}, u32[]{:S(2)}, u32[]{:S(2)}) collective-permute-start(bf16[12,48,256]{2,1,0:T(8,128)(2,1)} %broadcast_select_fusion.13), channel_id=1, source_target_pairs={{0,2},{1,3},{2,0},{3,1},{4,6},{5,7},{6,4},{7,5},{8,10},{9,11},{10,... | collective-permute-start | bytes 884744 | tf_op jit(solution)/shard_map/ppermute | solution.py:13
  162.8 19.1 %while.56 = (s32[]{:T(128)}, bf16[1920,128]{1,0:T(8,128)(2,1)S(1)}, bf16[1920,128]{1,0:T(8,128)(2,1)S(1)}, bf16[1920,128]{1,0:T(8,128)(2,1)S(1)}, bf16[12,48,256...) while((s32[]{:T(128)}, bf16[1920,128]{1,0:T(8,128)(2,1)S(1)}, ...), condition=%wide.region_9.10_spmd, body=%wide.region_8.9_spmd.sunk | while | flops 2271166464 | bytes 77368712 | solution.py:201
  164.9 1.5 collective-permute-start.8
  166.5 5.8 %collective-permute-done.9 = bf16[960,128]{1,0:T(8,128)(2,1)S(1)} collective-permute-done((bf16[960,128]{1,0:T(8,128)(2,1)}, bf16[960,128]{1,0:T(8,128)(2,1)S(1)}, u32[]{:S(2)}, u32[]{:S(2)}) %collective-permute-start.9) | collective-permute-done | bytes 245792 | tf_op jit(solution)/shard_map/while/body/ppermute | solution.py:17
  176.5 2.1 convolution_add_fusion.12
  184.4 7.9 %collective-permute-done.36 = bf16[12,48,256]{2,1,0:T(8,128)(2,1)S(1)} collective-permute-done((bf16[12,48,256]{2,1,0:T(8,128)(2,1)}, bf16[12,48,256]{2,1,0:T(8,128)(2,1)S(1)}, u32[]{:S(2)}, u32[]{:S(2)}) %collective-permute-start.36) | collective-permute-done | bytes 294944 | tf_op jit(solution)/shard_map/ppermute | solution.py:13
  192.9 1.6 collective-permute-start.34
  195.2 3.4 %collective-permute-done.34 = bf16[4,48,2,1,128]{4,2,1,0,3:T(2,128)(2,1)S(1)} collective-permute-done((bf16[4,48,2,1,128]{4,2,1,0,3:T(2,128)(2,1)S(1)}, bf16[4,48,2,1,128]{4,2,1,0,3:T(2,128)(2,1)S(1)}, u32[]{:S(2)}, u32[]{:S(2)}) %collective-permute-start.34) | collective-permute-done | bytes 98336 | tf_op jit(solution)/shard_map/ppermute | solution.py:17
  198.6 1.3 collective-permute-done.35
  199.9 6.2 %collective-permute-done.37 = bf16[12,48,256]{2,1,0:T(8,128)(2,1)S(1)} collective-permute-done((bf16[12,48,256]{2,1,0:T(8,128)(2,1)S(1)}, bf16[12,48,256]{2,1,0:T(8,128)(2,1)S(1)}, u32[]{:S(2)}, u32[]{:S(2)}) %collective-permute-start.37) | collective-permute-done | bytes 294944 | tf_op jit(solution)/shard_map/ppermute | solution.py:13
  207.1 1.6 collective-permute-start.39
  209.3 3.4 %collective-permute-done.39 = bf16[4,48,2,1,128]{4,2,1,0,3:T(2,128)(2,1)S(1)} collective-permute-done((bf16[4,48,2,1,128]{4,2,1,0,3:T(2,128)(2,1)S(1)}, bf16[4,48,2,1,128]{4,2,1,0,3:T(2,128)(2,1)S(1)}, u32[]{:S(2)}, u32[]{:S(2)}) %collective-permute-start.39) | collective-permute-done | bytes 98336 | tf_op jit(solution)/shard_map/ppermute | solution.py:17
  212.7 1.3 collective-permute-done.40
  217.4 2.1 copy.19
  (173 shorter events, 39.8 us)
Async XLA Ops:
  0.0 18.7 %copy-start = (bf16[2048,512]{1,0:T(8,128)(2,1)S(1)}, bf16[2048,512]{1,0:T(8,128)(2,1)}, u32[]{:S(2)}) copy-start(bf16[2048,512]{1,0:T(8,128)(2,1)} %param.17) | copy-start | bytes 6291460
  0.0 17.4 %copy-start.18 = (s32[4]{0:T(128)S(1)}, s32[4]{0:T(128)}, u32[]{:S(2)}) copy-start(s32[4]{0:T(128)} %param.20) | copy-start | bytes 52
  1.7 9.3 %collective-permute-start.12 = (bf16[1024,128]{1,0:T(8,128)(2,1)S(1)}, bf16[1024,128]{1,0:T(8,128)(2,1)S(1)}, u32[]{:S(2)}, u32[]{:S(2)}) collective-permute-start(bf16[1024,128]{1,0:T(8,128)(2,1)S(1)} %get-tuple-element.417), channel_id=1, source_target_pairs={{0,8},{4,12},{8,0},{12,4},{1,9},{5,13},{9,1},{13,5},{2,10},{6,14},... | collective-permute-start | bytes 786440 | tf_op jit(solution)/shard_map/ppermute | solution.py:17
  4.7 3.6 %collective-permute-start.13 = (bf16[2048]{0:T(1024)(128)(2,1)}, bf16[2048]{0:T(1024)(128)(2,1)S(1)}, u32[]{:S(2)}, u32[]{:S(2)}) collective-permute-start(bf16[2048]{0:T(1024)(128)(2,1)} %param.16), channel_id=1, source_target_pairs={{0,0},{1,4},{2,8},{3,12},{4,1},{5,5},{6,9},{7,13},{8,2},{9,6},{10,... | collective-permute-start | bytes 12296 | tf_op jit(solution)/shard_map/ppermute | solution.py:165
  11.1 8.0 %collective-permute-start.14 = (bf16[1024,128]{1,0:T(8,128)(2,1)S(1)}, bf16[1024,128]{1,0:T(8,128)(2,1)S(1)}, u32[]{:S(2)}, u32[]{:S(2)}) collective-permute-start(bf16[1024,128]{1,0:T(8,128)(2,1)S(1)} %get-tuple-element.600), channel_id=1, source_target_pairs={{0,0},{1,4},{2,6},{3,2},{4,1},{5,5},{6,7},{7,3},{8,8},{9,12},{10,1... | collective-permute-start | bytes 786440 | tf_op jit(solution)/shard_map/ppermute | solution.py:165
  11.8 16.3 %collective-permute-start.15 = (bf16[1024,128]{1,0:T(8,128)(2,1)S(1)}, bf16[1024,128]{1,0:T(8,128)(2,1)}, u32[]{:S(2)}, u32[]{:S(2)}) collective-permute-start(bf16[1024,128]{1,0:T(8,128)(2,1)S(1)} %get-tuple-element.599), channel_id=1, source_target_pairs={{0,2},{1,6},{2,4},{3,0},{4,3},{5,7},{6,5},{7,1},{8,10},{9,14},{10,... | collective-permute-start | bytes 786440 | tf_op jit(solution)/shard_map/ppermute | solution.py:165
  16.8 11.2 %collective-permute-start.16 = (bf16[1024,128]{1,0:T(8,128)(2,1)S(1)}, bf16[1024,128]{1,0:T(8,128)(2,1)S(1)}, u32[]{:S(2)}, u32[]{:S(2)}) collective-permute-start(bf16[1024,128]{1,0:T(8,128)(2,1)S(1)} %get-tuple-element.422), channel_id=1, source_target_pairs={{0,8},{4,12},{8,0},{12,4},{1,9},{5,13},{9,1},{13,5},{2,10},{6,14},... | collective-permute-start | bytes 786440 | tf_op jit(solution)/shard_map/ppermute | solution.py:17
  29.2 14.5 %collective-permute-start.17 = (bf16[1024,256]{1,0:T(8,128)(2,1)S(1)}, bf16[1024,256]{1,0:T(8,128)(2,1)S(1)}, u32[]{:S(2)}, u32[]{:S(2)}) collective-permute-start(bf16[1024,256]{1,0:T(8,128)(2,1)S(1)} %constant_dynamic-update-slice_fusion.2), channel_id=1, source_target_pairs={{0,8},{4,12},{8,0},{12,4},{1,9},{5,13},{9,1},{13,5},{2,10},{6,14},... | collective-permute-start | bytes 1572872 | tf_op jit(solution)/shard_map/ppermute | solution.py:17
  43.8 3.3 %collective-permute-start.18 = (bf16[2048,256]{1,0:T(8,128)(2,1)S(1)}, bf16[2048,256]{1,0:T(8,128)(2,1)S(1)}, u32[]{:S(2)}, u32[]{:S(2)}) collective-permute-start(bf16[2048,256]{1,0:T(8,128)(2,1)S(1)} %pad_maximum_fusion.7.near), channel_id=1, source_target_pairs={{0,4},{4,0},{8,12},{12,8},{1,5},{5,1},{9,13},{13,9},{2,6},{6,2},{1... | collective-permute-start | bytes 3145736 | tf_op jit(solution)/shard_map/ppermute | solution.py:17
  44.1 3.0 %collective-permute-start.21 = (f32[1,512]{1,0:T(1,128)S(1)}, f32[1,512]{1,0:T(1,128)S(1)}, u32[]{:S(2)}, u32[]{:S(2)}) collective-permute-start(f32[1,512]{1,0:T(1,128)S(1)} %fusion.30), channel_id=1, source_target_pairs={{0,4},{4,0},{8,12},{12,8},{1,5},{5,1},{9,13},{13,9},{2,6},{6,2},{1... | collective-permute-start | bytes 6152 | tf_op jit(solution)/shard_map/ppermute | solution.py:17
  44.7 10.1 %collective-permute-start.19 = (bf16[1024,128]{1,0:T(8,128)(2,1)S(1)}, bf16[1024,128]{1,0:T(8,128)(2,1)S(1)}, u32[]{:S(2)}, u32[]{:S(2)}) collective-permute-start(bf16[1024,128]{1,0:T(8,128)(2,1)S(1)} %get-tuple-element.598), channel_id=1, source_target_pairs={{0,0},{1,4},{2,6},{3,2},{4,1},{5,5},{6,7},{7,3},{8,8},{9,12},{10,1... | collective-permute-start | bytes 786440 | tf_op jit(solution)/shard_map/ppermute | solution.py:165
  45.4 13.0 %collective-permute-start.20 = (bf16[1024,128]{1,0:T(8,128)(2,1)S(1)}, bf16[1024,128]{1,0:T(8,128)(2,1)S(1)}, u32[]{:S(2)}, u32[]{:S(2)}) collective-permute-start(bf16[1024,128]{1,0:T(8,128)(2,1)S(1)} %get-tuple-element.597), channel_id=1, source_target_pairs={{0,2},{1,6},{2,4},{3,0},{4,3},{5,7},{6,5},{7,1},{8,10},{9,14},{10,... | collective-permute-start | bytes 786440 | tf_op jit(solution)/shard_map/ppermute | solution.py:165
  59.0 32.2 %collective-permute-start.24 = (bf16[2560,128]{1,0:T(8,128)(2,1)}, bf16[2560,128]{1,0:T(8,128)(2,1)}, u32[]{:S(2)}, u32[]{:S(2)}) collective-permute-start(bf16[2560,128]{1,0:T(8,128)(2,1)} %get-tuple-element.440), channel_id=1, source_target_pairs={{0,1},{1,0},{2,3},{3,2},{4,5},{5,4},{6,7},{7,6},{8,9},{9,8},{10,11... | collective-permute-start | bytes 1966088 | tf_op jit(solution)/shard_map/ppermute | solution.py:17
  59.6 31.6 %collective-permute-start.22 = (bf16[1280,128]{1,0:T(8,128)(2,1)}, bf16[1280,128]{1,0:T(8,128)(2,1)}, u32[]{:S(2)}, u32[]{:S(2)}) collective-permute-start(bf16[1280,128]{1,0:T(8,128)(2,1)} %get-tuple-element.438), channel_id=1, source_target_pairs={{0,2},{1,3},{2,0},{3,1},{4,6},{5,7},{6,4},{7,5},{8,10},{9,11},{10,... | collective-permute-start | bytes 983048 | tf_op jit(solution)/shard_map/ppermute | solution.py:17
  61.0 30.2 %collective-permute-start.23 = (bf16[1280,128]{1,0:T(8,128)(2,1)}, bf16[1280,128]{1,0:T(8,128)(2,1)}, u32[]{:S(2)}, u32[]{:S(2)}) collective-permute-start(bf16[1280,128]{1,0:T(8,128)(2,1)} %get-tuple-element.439), channel_id=1, source_target_pairs={{0,3},{1,2},{2,1},{3,0},{4,7},{5,6},{6,5},{7,4},{8,11},{9,10},{10,... | collective-permute-start | bytes 983048 | tf_op jit(solution)/shard_map/ppermute | solution.py:17
  65.3 14.0 %collective-permute-start = (bf16[1024,256]{1,0:T(8,128)(2,1)S(1)}, bf16[1024,256]{1,0:T(8,128)(2,1)}, u32[]{:S(2)}, u32[]{:S(2)}) collective-permute-start(bf16[1024,256]{1,0:T(8,128)(2,1)S(1)} %copy.33), channel_id=1, source_target_pairs={{0,8},{4,12},{8,0},{12,4},{1,9},{5,13},{9,1},{13,5},{2,10},{6,14},... | collective-permute-start | bytes 1572872 | tf_op jit(solution)/shard_map/while/body/ppermute | solution.py:17
  65.9 13.3 %collective-permute-start.1 = (f32[1,512]{1,0:T(1,128)S(1)}, f32[1,512]{1,0:T(1,128)S(1)}, u32[]{:S(2)}, u32[]{:S(2)}) collective-permute-start(f32[1,512]{1,0:T(1,128)S(1)} %copy.34), channel_id=1, source_target_pairs={{0,8},{4,12},{8,0},{12,4},{1,9},{5,13},{9,1},{13,5},{2,10},{6,14},... | collective-permute-start | bytes 6152 | tf_op jit(solution)/shard_map/while/body/ppermute | solution.py:17
  80.4 2.7 %collective-permute-start.2 = (bf16[2048,256]{1,0:T(8,128)(2,1)S(1)}, bf16[2048,256]{1,0:T(8,128)(2,1)S(1)}, u32[]{:S(2)}, u32[]{:S(2)}) collective-permute-start(bf16[2048,256]{1,0:T(8,128)(2,1)S(1)} %pad_maximum_fusion.18.near), channel_id=1, source_target_pairs={{0,4},{4,0},{8,12},{12,8},{1,5},{5,1},{9,13},{13,9},{2,6},{6,2},{1... | collective-permute-start | bytes 3145736 | tf_op jit(solution)/shard_map/while/body/ppermute | solution.py:17
  92.3 12.7 %copy-start.15 = (f32[1,512]{1,0:T(1,128)S(1)}, f32[1,512]{1,0:T(1,128)}, u32[]{:S(2)}) copy-start(f32[1,512]{1,0:T(1,128)} %get-tuple-element.472) | copy-start | bytes 6148
  92.3 12.7 %copy-start.16 = (f32[1,128]{1,0:T(1,128)S(1)}, f32[1,128]{1,0:T(1,128)}, u32[]{:S(2)}) copy-start(f32[1,128]{1,0:T(1,128)} %param.18) | copy-start | bytes 1540
  92.3 8.2 %collective-permute-start.25 = (bf16[640,128]{1,0:T(8,128)(2,1)S(1)}, bf16[640,128]{1,0:T(8,128)(2,1)S(1)}, u32[]{:S(2)}, u32[]{:S(2)}) collective-permute-start(bf16[640,128]{1,0:T(8,128)(2,1)S(1)} %slice.147), channel_id=1, source_target_pairs={{0,3},{1,2},{2,1},{3,0},{4,7},{5,6},{6,5},{7,4},{8,11},{9,10},{10,... | collective-permute-start | bytes 491528 | tf_op jit(solution)/shard_map/ppermute | solution.py:17
  100.5 38.9 %collective-permute-start.26 = (bf16[1920,128]{1,0:T(8,128)(2,1)}, bf16[1920,128]{1,0:T(8,128)(2,1)}, u32[]{:S(2)}, u32[]{:S(2)}) collective-permute-start(bf16[1920,128]{1,0:T(8,128)(2,1)} %get-tuple-element.459), channel_id=1, source_target_pairs={{0,2},{1,3},{2,0},{3,1},{4,6},{5,7},{6,4},{7,5},{8,10},{9,11},{10,... | collective-permute-start | bytes 1474568 | tf_op jit(solution)/shard_map/ppermute | solution.py:17
  103.6 35.8 %collective-permute-start.27 = (bf16[1920,128]{1,0:T(8,128)(2,1)}, bf16[1920,128]{1,0:T(8,128)(2,1)}, u32[]{:S(2)}, u32[]{:S(2)}) collective-permute-start(bf16[1920,128]{1,0:T(8,128)(2,1)} %get-tuple-element.460), channel_id=1, source_target_pairs={{0,3},{1,2},{2,1},{3,0},{4,7},{5,6},{6,5},{7,4},{8,11},{9,10},{10,... | collective-permute-start | bytes 1474568 | tf_op jit(solution)/shard_map/ppermute | solution.py:17
  104.9 34.5 %collective-permute-start.28 = (bf16[1920,128]{1,0:T(8,128)(2,1)}, bf16[1920,128]{1,0:T(8,128)(2,1)}, u32[]{:S(2)}, u32[]{:S(2)}) collective-permute-start(bf16[1920,128]{1,0:T(8,128)(2,1)} %get-tuple-element.461), channel_id=1, source_target_pairs={{0,1},{1,0},{2,3},{3,2},{4,5},{5,4},{6,7},{7,6},{8,9},{9,8},{10,11... | collective-permute-start | bytes 1474568 | tf_op jit(solution)/shard_map/ppermute | solution.py:17
  105.0 34.4 %copy-start.10 = (f32[1920,128]{1,0:T(8,128)S(1)}, f32[1920,128]{1,0:T(8,128)}, u32[]{:S(2)}) copy-start(f32[1920,128]{1,0:T(8,128)} %get-tuple-element.475) | copy-start | bytes 2949124
  105.1 11.4 %collective-permute-start.3 = (bf16[1920,128]{1,0:T(8,128)(2,1)S(1)}, bf16[1920,128]{1,0:T(8,128)(2,1)S(1)}, u32[]{:S(2)}, u32[]{:S(2)}) collective-permute-start(bf16[1920,128]{1,0:T(8,128)(2,1)S(1)} %copy.52), channel_id=1, source_target_pairs={{0,8},{4,12},{8,0},{12,4},{1,9},{5,13},{9,1},{13,5},{2,10},{6,14},... | collective-permute-start | bytes 1474568 | tf_op jit(solution)/shard_map/while/body/ppermute | solution.py:17
  106.7 11.1 %collective-permute-start.4 = (bf16[1920,128]{1,0:T(8,128)(2,1)S(1)}, bf16[1920,128]{1,0:T(8,128)(2,1)S(1)}, u32[]{:S(2)}, u32[]{:S(2)}) collective-permute-start(bf16[1920,128]{1,0:T(8,128)(2,1)S(1)} %copy.52), channel_id=1, source_target_pairs={{0,16},{16,0},{1,17},{17,1},{2,18},{18,2},{3,19},{19,3},{4,20},{20... | collective-permute-start | bytes 1474568 | tf_op jit(solution)/shard_map/while/body/ppermute | solution.py:17
  118.0 13.7 %collective-permute-start.6 = (bf16[1920,256]{1,0:T(8,128)(2,1)S(1)}, bf16[1920,256]{1,0:T(8,128)(2,1)}, u32[]{:S(2)}, u32[]{:S(2)}) collective-permute-start(bf16[1920,256]{1,0:T(8,128)(2,1)S(1)} %pad_maximum_fusion.19), channel_id=1, source_target_pairs={{0,4},{4,0},{8,12},{12,8},{1,5},{5,1},{9,13},{13,9},{2,6},{6,2},{1... | collective-permute-start | bytes 2949128 | tf_op jit(solution)/shard_map/while/body/ppermute | solution.py:17
  118.1 13.6 %collective-permute-start.5 = (bf16[1920,128]{1,0:T(8,128)(2,1)S(1)}, bf16[1920,128]{1,0:T(8,128)(2,1)S(1)}, u32[]{:S(2)}, u32[]{:S(2)}) collective-permute-start(bf16[1920,128]{1,0:T(8,128)(2,1)S(1)} %collective-permute-done.4), channel_id=1, source_target_pairs={{0,8},{4,12},{8,0},{12,4},{1,9},{5,13},{9,1},{13,5},{2,10},{6,14},... | collective-permute-start | bytes 1474568 | tf_op jit(solution)/shard_map/while/body/ppermute | solution.py:17
  118.6 13.4 %copy-start.7 = (bf16[576,1920]{1,0:T(8,128)(2,1)S(1)}, bf16[576,1920]{1,0:T(8,128)(2,1)}, u32[]{:S(2)}) copy-start(bf16[576,1920]{1,0:T(8,128)(2,1)} %get-tuple-element.965) | copy-start | bytes 6635524 | tf_op jit(solution)/shard_map/while
  131.9 4.7 %collective-permute-start.7 = (bf16[1920,256]{1,0:T(8,128)(2,1)S(1)}, bf16[1920,256]{1,0:T(8,128)(2,1)S(1)}, u32[]{:S(2)}, u32[]{:S(2)}) collective-permute-start(bf16[1920,256]{1,0:T(8,128)(2,1)S(1)} %pad_maximum_fusion.20), channel_id=1, source_target_pairs={{0,4},{4,0},{8,12},{12,8},{1,5},{5,1},{9,13},{13,9},{2,6},{6,2},{1... | collective-permute-start | bytes 2949128 | tf_op jit(solution)/shard_map/while/body/ppermute | solution.py:17
  141.0 16.7 %collective-permute-start.30 = (bf16[1920,128]{1,0:T(8,128)(2,1)S(1)}, bf16[1920,128]{1,0:T(8,128)(2,1)S(1)}, u32[]{:S(2)}, u32[]{:S(2)}) collective-permute-start(bf16[1920,128]{1,0:T(8,128)(2,1)S(1)} %add_convert_fusion), channel_id=1, source_target_pairs={{0,8},{4,12},{8,0},{12,4},{1,9},{5,13},{9,1},{13,5},{2,10},{6,14},... | collective-permute-start | bytes 1474568 | tf_op jit(solution)/shard_map/ppermute | solution.py:17
  141.6 16.2 %collective-permute-start.31 = (bf16[1920,128]{1,0:T(8,128)(2,1)S(1)}, bf16[1920,128]{1,0:T(8,128)(2,1)S(1)}, u32[]{:S(2)}, u32[]{:S(2)}) collective-permute-start(bf16[1920,128]{1,0:T(8,128)(2,1)S(1)} %add_convert_fusion), channel_id=1, source_target_pairs={{0,16},{16,0},{1,17},{17,1},{2,18},{18,2},{3,19},{19,3},{4,20},{20... | collective-permute-start | bytes 1474568 | tf_op jit(solution)/shard_map/ppermute | solution.py:17
  143.3 14.4 %collective-permute-start.29 = (bf16[12,48,256]{2,1,0:T(8,128)(2,1)S(1)}, bf16[12,48,256]{2,1,0:T(8,128)(2,1)S(1)}, u32[]{:S(2)}, u32[]{:S(2)}) collective-permute-start(bf16[12,48,256]{2,1,0:T(8,128)(2,1)S(1)} %copy-done.12), channel_id=1, source_target_pairs={{0,1},{1,2},{2,3},{3,0},{4,5},{5,6},{6,7},{7,4},{8,9},{9,10},{10,1... | collective-permute-start | bytes 884744 | tf_op jit(solution)/shard_map/ppermute | solution.py:13
  158.5 23.3 %collective-permute-start.32 = (bf16[12,48,256]{2,1,0:T(8,128)(2,1)}, bf16[12,48,256]{2,1,0:T(8,128)(2,1)}, u32[]{:S(2)}, u32[]{:S(2)}) collective-permute-start(bf16[12,48,256]{2,1,0:T(8,128)(2,1)} %broadcast_select_fusion.13), channel_id=1, source_target_pairs={{0,2},{1,3},{2,0},{3,1},{4,6},{5,7},{6,4},{7,5},{8,10},{9,11},{10,... | collective-permute-start | bytes 884744 | tf_op jit(solution)/shard_map/ppermute | solution.py:13
  163.0 10.2 %collective-permute-start.10 = (bf16[1920,256]{1,0:T(8,128)(2,1)S(1)}, bf16[1920,256]{1,0:T(8,128)(2,1)}, u32[]{:S(2)}, u32[]{:S(2)}) collective-permute-start(bf16[1920,256]{1,0:T(8,128)(2,1)S(1)} %pad_maximum_fusion.22), channel_id=1, source_target_pairs={{0,4},{4,0},{8,12},{12,8},{1,5},{5,1},{9,13},{13,9},{2,6},{6,2},{1... | collective-permute-start | bytes 2949128 | tf_op jit(solution)/shard_map/while/body/ppermute | solution.py:17
  163.8 8.6 %collective-permute-start.9 = (bf16[960,128]{1,0:T(8,128)(2,1)}, bf16[960,128]{1,0:T(8,128)(2,1)S(1)}, u32[]{:S(2)}, u32[]{:S(2)}) collective-permute-start(bf16[960,128]{1,0:T(8,128)(2,1)} %slice.171), channel_id=1, source_target_pairs={{0,8},{4,12},{8,0},{12,4},{1,9},{5,13},{9,1},{13,5},{2,10},{6,14},... | collective-permute-start | bytes 737288 | tf_op jit(solution)/shard_map/while/body/ppermute | solution.py:17
  164.9 8.3 %collective-permute-start.8 = (bf16[960,128]{1,0:T(8,128)(2,1)}, bf16[960,128]{1,0:T(8,128)(2,1)S(1)}, u32[]{:S(2)}, u32[]{:S(2)}) collective-permute-start(bf16[960,128]{1,0:T(8,128)(2,1)} %slice.170), channel_id=1, source_target_pairs={{0,16},{16,0},{1,17},{17,1},{2,18},{18,2},{3,19},{19,3},{4,20},{20... | collective-permute-start | bytes 737288 | tf_op jit(solution)/shard_map/while/body/ppermute | solution.py:17
  173.5 5.9 %collective-permute-start.11 = (bf16[1920,256]{1,0:T(8,128)(2,1)S(1)}, bf16[1920,256]{1,0:T(8,128)(2,1)S(1)}, u32[]{:S(2)}, u32[]{:S(2)}) collective-permute-start(bf16[1920,256]{1,0:T(8,128)(2,1)S(1)} %pad_maximum_fusion.23), channel_id=1, source_target_pairs={{0,4},{4,0},{8,12},{12,8},{1,5},{5,1},{9,13},{13,9},{2,6},{6,2},{1... | collective-permute-start | bytes 2949128 | tf_op jit(solution)/shard_map/while/body/ppermute | solution.py:17
  181.9 10.4 %copy-start.11 = (bf16[12,48,256]{2,1,0:T(8,128)(2,1)S(1)}, bf16[12,48,256]{2,1,0:T(8,128)(2,1)}, u32[]{:S(2)}) copy-start(bf16[12,48,256]{2,1,0:T(8,128)(2,1)} %get-tuple-element.487) | copy-start | bytes 884740
  181.9 10.4 %collective-permute-start.36 = (bf16[12,48,256]{2,1,0:T(8,128)(2,1)}, bf16[12,48,256]{2,1,0:T(8,128)(2,1)S(1)}, u32[]{:S(2)}, u32[]{:S(2)}) collective-permute-start(bf16[12,48,256]{2,1,0:T(8,128)(2,1)} %get-tuple-element.487), channel_id=1, source_target_pairs={{0,1},{1,2},{2,3},{3,0},{4,5},{5,6},{6,7},{7,4},{8,9},{9,10},{10,1... | collective-permute-start | bytes 884744 | tf_op jit(solution)/shard_map/ppermute | solution.py:13
  192.4 13.7 %collective-permute-start.37 = (bf16[12,48,256]{2,1,0:T(8,128)(2,1)S(1)}, bf16[12,48,256]{2,1,0:T(8,128)(2,1)S(1)}, u32[]{:S(2)}, u32[]{:S(2)}) collective-permute-start(bf16[12,48,256]{2,1,0:T(8,128)(2,1)S(1)} %broadcast_select_fusion.12), channel_id=1, source_target_pairs={{0,2},{1,3},{2,0},{3,1},{4,6},{5,7},{6,4},{7,5},{8,10},{9,11},{10,... | collective-permute-start | bytes 884744 | tf_op jit(solution)/shard_map/ppermute | solution.py:13
  192.7 2.4 %collective-permute-start.33 = (bf16[4,48,2,1,128]{4,2,1,0,3:T(2,128)(2,1)S(1)}, bf16[4,48,2,1,128]{4,2,1,0,3:T(2,128)(2,1)S(1)}, u32[]{:S(2)}, u32[]{:S(2)}) collective-permute-start(bf16[4,48,2,1,128]{4,2,1,0,3:T(2,128)(2,1)S(1)} %squeeze.29), channel_id=1, source_target_pairs={{0,4},{4,0},{8,12},{12,8},{1,5},{5,1},{9,13},{13,9},{2,6},{6,2},{1... | collective-permute-start | bytes 294920 | tf_op jit(solution)/shard_map/ppermute | solution.py:17
  192.9 5.7 %collective-permute-start.34 = (bf16[4,48,2,1,128]{4,2,1,0,3:T(2,128)(2,1)S(1)}, bf16[4,48,2,1,128]{4,2,1,0,3:T(2,128)(2,1)S(1)}, u32[]{:S(2)}, u32[]{:S(2)}) collective-permute-start(bf16[4,48,2,1,128]{4,2,1,0,3:T(2,128)(2,1)S(1)} %squeeze.30), channel_id=1, source_target_pairs={{0,8},{4,12},{8,0},{12,4},{1,9},{5,13},{9,1},{13,5},{2,10},{6,14},... | collective-permute-start | bytes 294920 | tf_op jit(solution)/shard_map/ppermute | solution.py:17
  194.7 5.2 %collective-permute-start.35 = (bf16[4,48,2,1,128]{4,2,1,0,3:T(2,128)(2,1)S(1)}, bf16[4,48,2,1,128]{4,2,1,0,3:T(2,128)(2,1)S(1)}, u32[]{:S(2)}, u32[]{:S(2)}) collective-permute-start(bf16[4,48,2,1,128]{4,2,1,0,3:T(2,128)(2,1)S(1)} %squeeze.31), channel_id=1, source_target_pairs={{0,12},{4,8},{8,4},{12,0},{1,13},{5,9},{9,5},{13,1},{2,14},{6,10},... | collective-permute-start | bytes 294920 | tf_op jit(solution)/shard_map/ppermute | solution.py:17
  206.9 2.4 %collective-permute-start.38 = (bf16[4,48,2,1,128]{4,2,1,0,3:T(2,128)(2,1)S(1)}, bf16[4,48,2,1,128]{4,2,1,0,3:T(2,128)(2,1)S(1)}, u32[]{:S(2)}, u32[]{:S(2)}) collective-permute-start(bf16[4,48,2,1,128]{4,2,1,0,3:T(2,128)(2,1)S(1)} %squeeze.33), channel_id=1, source_target_pairs={{0,4},{4,0},{8,12},{12,8},{1,5},{5,1},{9,13},{13,9},{2,6},{6,2},{1... | collective-permute-start | bytes 294920 | tf_op jit(solution)/shard_map/ppermute | solution.py:17
  207.1 5.7 %collective-permute-start.39 = (bf16[4,48,2,1,128]{4,2,1,0,3:T(2,128)(2,1)S(1)}, bf16[4,48,2,1,128]{4,2,1,0,3:T(2,128)(2,1)S(1)}, u32[]{:S(2)}, u32[]{:S(2)}) collective-permute-start(bf16[4,48,2,1,128]{4,2,1,0,3:T(2,128)(2,1)S(1)} %squeeze.34), channel_id=1, source_target_pairs={{0,8},{4,12},{8,0},{12,4},{1,9},{5,13},{9,1},{13,5},{2,10},{6,14},... | collective-permute-start | bytes 294920 | tf_op jit(solution)/shard_map/ppermute | solution.py:17
  208.8 5.2 %collective-permute-start.40 = (bf16[4,48,2,1,128]{4,2,1,0,3:T(2,128)(2,1)S(1)}, bf16[4,48,2,1,128]{4,2,1,0,3:T(2,128)(2,1)S(1)}, u32[]{:S(2)}, u32[]{:S(2)}) collective-permute-start(bf16[4,48,2,1,128]{4,2,1,0,3:T(2,128)(2,1)S(1)} %squeeze.35), channel_id=1, source_target_pairs={{0,12},{4,8},{8,4},{12,0},{1,13},{5,9},{9,5},{13,1},{2,14},{6,10},... | collective-permute-start | bytes 294920 | tf_op jit(solution)/shard_map/ppermute | solution.py:17
  (13 other events, 47.4 us)

commit v23 on v22

--- a/solution.py
+++ b/solution.py
@@ -376,8 +376,9 @@
     values = step(rolled(values, shifted, 1))
     arrived, shifted = step((to_owners(picked), shifted_2(values, "head", 2)))
 
-    value_cache = in_order(to_owners(outgoing(rolled(values, shifted, 2))))
-    cache = jnp.stack([in_order(arrived), value_cache], axis=-2)
+    pieces = to_owners(outgoing(rolled(values, shifted, 2)))
+    key_cache, pieces = step((in_order(arrived), pieces))
+    cache = jnp.stack([key_cache, in_order(pieces)], axis=-2)
     return cache.reshape(1, 1, most_tiles * 4 * shard_len, 4 * layers, head_dim)
 
 

time: 220 us -> 219 us (level)
  transfers between devices with their start and end apart: 41 -> 41, of which waited for: 19 -> 19; matrix products, arithmetic and copies ran while one was open for 14% -> 15% of each run, Pallas kernels for 7% -> 7%
where the time goes in v23:
time: 219 us; the launch traced here: 218 us
  waiting for transfers between devices  98.2 us (45%)
  starting transfers between devices  53.2 us (24%)
  local copies, waits for them, and re-layouts  24.9 us (11%)
  Pallas kernels  15.7 us (7%)
  other arithmetic  14.9 us (7%)
  matrix products  9.93 us (5%)
    ppermute x32, waiting for transfers between devices, swapped(): lax.ppermute(shard, axis, [(i, i ^ bit) for i in range(lax.axis_size(axis...  66 us
    ppermute x32, starting transfers between devices, swapped(): lax.ppermute(shard, axis, [(i, i ^ bit) for i in range(lax.axis_size(axis...  29.7 us
    ppermute x4, waiting for transfers between devices, shifted_2(): lax.ppermute(shard, axis, [(i, (i + by) % count) for i in range(count)])  19.7 us
    pallas_call x2, Pallas kernels, product_terms(): pl.pallas_call(terms_body, out_shape=shapes, grid_spec=pltpu.PrefetchScal...  15.7 us
    ppermute x4, starting transfers between devices, shifted_2(): lax.ppermute(shard, axis, [(i, (i + by) % count) for i in range(count)])  14 us
    ppermute x5, waiting for transfers between devices, moved(): return lax.ppermute(shard, ('tile', 'head'), pairs)  12.5 us
    dot_general x11, matrix products, add_columns(): return jnp.dot(operand, portion, preferred_element_type=jnp.float32)  9.74 us
    ppermute x5, starting transfers between devices, moved(): return lax.ppermute(shard, ('tile', 'head'), pairs)  9.46 us
  transfers between devices with their start and end apart: 41, of which 19 were waited for; matrix products, arithmetic and copies ran while one was open for 15% of the time, Pallas kernels for 7%

profile of v23, /device:TPU:0, one launch (start us, length us, event | category | flops | bytes accessed | tf_op | source)
XLA Modules:
  0.0 218.4 jit_solution(14069410382390577920)
XLA Ops:
  0.0 1.7 fusion.24
  1.7 3.0 %collective-permute-start.12 = (bf16[1024,128]{1,0:T(8,128)(2,1)S(1)}, bf16[1024,128]{1,0:T(8,128)(2,1)S(1)}, u32[]{:S(2)}, u32[]{:S(2)}) collective-permute-start(bf16[1024,128]{1,0:T(8,128)(2,1)S(1)} %get-tuple-element.422), channel_id=1, source_target_pairs={{0,8},{4,12},{8,0},{12,4},{1,9},{5,13},{9,1},{13,5},{2,10},{6,14},... | collective-permute-start | bytes 786440 | tf_op jit(solution)/shard_map/ppermute | solution.py:17
  4.7 1.3 collective-permute-start.13
  6.1 2.2 %fusion.23 = (bf16[1024,128]{1,0:T(8,128)(2,1)S(1)}, bf16[1024,128]{1,0:T(8,128)(2,1)}) fusion(bf16[2048,512]{1,0:T(8,128)(2,1)} %param.17, s32[]{:T(128)S(6)} %select_n.307, s32[]{:T(128)S(6)} %select_n.309, s32[]{:T(128)S(6)} %select_n.303), kind=kLoop, calls=%fused_computation.124 | loop fusion | bytes 1048588 | tf_op jit(solution)/shard_map/dynamic_slice | solution.py:246
  8.3 2.7 %collective-permute-done.12 = bf16[1024,128]{1,0:T(8,128)(2,1)S(1)} collective-permute-done((bf16[1024,128]{1,0:T(8,128)(2,1)S(1)}, bf16[1024,128]{1,0:T(8,128)(2,1)S(1)}, u32[]{:S(2)}, u32[]{:S(2)}) %collective-permute-start.12) | collective-permute-done | bytes 262176 | tf_op jit(solution)/shard_map/ppermute | solution.py:17
  11.8 5.1 %collective-permute-start.15 = (bf16[1024,128]{1,0:T(8,128)(2,1)S(1)}, bf16[1024,128]{1,0:T(8,128)(2,1)}, u32[]{:S(2)}, u32[]{:S(2)}) collective-permute-start(bf16[1024,128]{1,0:T(8,128)(2,1)S(1)} %get-tuple-element.609), channel_id=1, source_target_pairs={{0,2},{1,6},{2,4},{3,0},{4,3},{5,7},{6,5},{7,1},{8,10},{9,14},{10,... | collective-permute-start | bytes 786440 | tf_op jit(solution)/shard_map/ppermute | solution.py:165
  19.2 8.9 %collective-permute-done.15 = bf16[1024,128]{1,0:T(8,128)(2,1)} collective-permute-done((bf16[1024,128]{1,0:T(8,128)(2,1)S(1)}, bf16[1024,128]{1,0:T(8,128)(2,1)}, u32[]{:S(2)}, u32[]{:S(2)}) %collective-permute-start.15) | collective-permute-done | bytes 262176 | tf_op jit(solution)/shard_map/ppermute | solution.py:165
  30.0 7.2 %constant_dynamic-slice_fusion = (bf16[576,1920]{1,0:T(8,128)(2,1)}, bf16[576,1920]{1,0:T(8,128)(2,1)}, bf16[576,1920]{1,0:T(8,128)(2,1)}, bf16[576,1920]{1,0:T(8,128)(2,1)}) fusion(bf16[576,7680]{1,0:T(8,128)(2,1)} %bitcast.133, s32[]{:T(128)S(6)} %select_n.316, s32[]{:T(128)S(6)} %select_n.315, s32[]{:T(128)S(6)} %select_n.314, s32[]{:T(128)S(6)} %select_n.313), kind=kLoop, calls=%fused_computation.115 | loop fusion | bytes 17694736 | tf_op jit(solution)/shard_map/dynamic_slice | solution.py:171
  37.2 6.4 %collective-permute-done.17 = bf16[1024,256]{1,0:T(8,128)(2,1)S(1)} collective-permute-done((bf16[1024,256]{1,0:T(8,128)(2,1)S(1)}, bf16[1024,256]{1,0:T(8,128)(2,1)S(1)}, u32[]{:S(2)}, u32[]{:S(2)}) %collective-permute-start.17) | collective-permute-done | bytes 524320 | tf_op jit(solution)/shard_map/ppermute | solution.py:17
  45.4 1.7 collective-permute-start.20
  47.1 7.7 %shard_map.82 = (f32[1280,128]{1,0:T(8,128)S(1)}, bf16[1280,128]{1,0:T(8,128)(2,1)}, bf16[1280,128]{1,0:T(8,128)(2,1)}, bf16[2560,128]{1,0:T(8,128)(2,1)}, f32[640,256]{1,0:T(8,128)S(1)}) custom-call(s32[1]{0:T(128)} %bitcast.13.choice, bf16[1920,2048]{1,0:T(8,128)(2,1)} %weight.1, bf16[2048,256]{1,0:T(8,128)(2,1)S(1)} %pad_maximum_fusion.7.near, ...), custom_call_target="tpu_custom_call" | custom-call | flops 4026531840 | bytes 12419072 | tf_op jit(solution)/shard_map/pallas_call | solution.py:118
  54.8 3.6 %collective-permute-done.20 = bf16[1024,128]{1,0:T(8,128)(2,1)S(1)} collective-permute-done((bf16[1024,128]{1,0:T(8,128)(2,1)S(1)}, bf16[1024,128]{1,0:T(8,128)(2,1)S(1)}, u32[]{:S(2)}, u32[]{:S(2)}) %collective-permute-start.20) | collective-permute-done | bytes 262176 | tf_op jit(solution)/shard_map/ppermute | solution.py:165
  59.6 1.4 collective-permute-start.22
  61.0 2.4 %collective-permute-start.23 = (bf16[1280,128]{1,0:T(8,128)(2,1)}, bf16[1280,128]{1,0:T(8,128)(2,1)}, u32[]{:S(2)}, u32[]{:S(2)}) collective-permute-start(bf16[1280,128]{1,0:T(8,128)(2,1)} %get-tuple-element.444), channel_id=1, source_target_pairs={{0,3},{1,2},{2,1},{3,0},{4,7},{5,6},{6,5},{7,4},{8,11},{9,10},{10,... | collective-permute-start | bytes 983048 | tf_op jit(solution)/shard_map/ppermute | solution.py:17
  64.2 27.0 %while.54 = (s32[]{:T(128)}, bf16[1024,256]{1,0:T(8,128)(2,1)}, f32[1,512]{1,0:T(1,128)S(1)}, f32[1920,128]{1,0:T(8,128)}, bf16[1920,128]{1,0:T(8,128)(2,1)}, /*...) while((s32[]{:T(128)}, bf16[1024,256]{1,0:T(8,128)(2,1)}, ...), condition=%wide.region_3.4_spmd, body=%wide.region_2.3_spmd.sunk | while | flops 4029153792 | bytes 23972084 | solution.py:201
  65.9 1.4 collective-permute-start.1
  67.3 11.9 %collective-permute-done.1 = f32[1,512]{1,0:T(1,128)S(1)} collective-permute-done((f32[1,512]{1,0:T(1,128)S(1)}, f32[1,512]{1,0:T(1,128)S(1)}, u32[]{:S(2)}, u32[]{:S(2)}) %collective-permute-start.1) | collective-permute-done | bytes 2080 | tf_op jit(solution)/shard_map/while/body/ppermute | solution.py:17
  81.0 2.1 collective-permute-done.2.far
  83.1 8.0 %body.1 = (f32[1920,128]{1,0:T(8,128)}, bf16[1920,128]{1,0:T(8,128)(2,1)}, bf16[1920,128]{1,0:T(8,128)(2,1)}, bf16[1920,128]{1,0:T(8,128)(2,1)}) custom-call(s32[1]{0:T(128)} %get-tuple-element.940.choice, bf16[1920,2048]{1,0:T(8,128)(2,1)} %get-tuple-element.941.weight, bf16[2048,256]{1,0:T(8,128)(2,1)S(1)} %pad_maximum_fusion.19.near, ...), custom_call_target="tpu_custom_call" | custom-call | flops 4026531840 | bytes 12419072 | tf_op jit(solution)/shard_map/while/body/pallas_call | solution.py:118
  92.3 1.9 collective-permute-start.25
  94.2 1.3 add_convert_fusion.1
  95.5 5.0 %collective-permute-done.25 = bf16[640,128]{1,0:T(8,128)(2,1)S(1)} collective-permute-done((bf16[640,128]{1,0:T(8,128)(2,1)S(1)}, bf16[640,128]{1,0:T(8,128)(2,1)S(1)}, u32[]{:S(2)}, u32[]{:S(2)}) %collective-permute-start.25) | collective-permute-done | bytes 163872 | tf_op jit(solution)/shard_map/ppermute | solution.py:17
  100.5 3.1 %collective-permute-start.26 = (bf16[1920,128]{1,0:T(8,128)(2,1)}, bf16[1920,128]{1,0:T(8,128)(2,1)}, u32[]{:S(2)}, u32[]{:S(2)}) collective-permute-start(bf16[1920,128]{1,0:T(8,128)(2,1)} %get-tuple-element.464), channel_id=1, source_target_pairs={{0,2},{1,3},{2,0},{3,1},{4,6},{5,7},{6,4},{7,5},{8,10},{9,11},{10,... | collective-permute-start | bytes 1474568 | tf_op jit(solution)/shard_map/ppermute | solution.py:17
  105.0 34.4 %while.55 = (s32[]{:T(128)}, bf16[1920,128]{1,0:T(8,128)(2,1)S(1)}, bf16[12,48,256]{2,1,0:T(8,128)(2,1)}, s32[]{:T(128)}, pred[]{:T(512)}, /*index=5*/bf16[576,1...) while((s32[]{:T(128)}, bf16[1920,128]{1,0:T(8,128)(2,1)S(1)}, ...), condition=%wide.region_7.8_spmd, body=%wide.region_4.7_spmd.sunk | while | flops 2271905024 | bytes 76995496 | solution.py:201
  105.1 1.6 collective-permute-start.3
  106.7 1.5 collective-permute-start.4
  108.2 8.3 %collective-permute-done.3 = bf16[1920,128]{1,0:T(8,128)(2,1)S(1)} collective-permute-done((bf16[1920,128]{1,0:T(8,128)(2,1)S(1)}, bf16[1920,128]{1,0:T(8,128)(2,1)S(1)}, u32[]{:S(2)}, u32[]{:S(2)}) %collective-permute-start.3) | collective-permute-done | bytes 491552 | tf_op jit(solution)/shard_map/while/body/ppermute | solution.py:17
  116.5 1.3 collective-permute-done.4
  118.6 13.1 %collective-permute-done.5 = bf16[1920,128]{1,0:T(8,128)(2,1)S(1)} collective-permute-done((bf16[1920,128]{1,0:T(8,128)(2,1)S(1)}, bf16[1920,128]{1,0:T(8,128)(2,1)S(1)}, u32[]{:S(2)}, u32[]{:S(2)}) %collective-permute-start.5) | collective-permute-done | bytes 491552 | tf_op jit(solution)/shard_map/while/body/ppermute | solution.py:17
  133.6 2.1 convolution_add_fusion.10
  139.4 1.6 add_convert_fusion
  141.6 1.5 collective-permute-start.31
  143.3 8.7 %collective-permute-start.29 = (bf16[12,48,256]{2,1,0:T(8,128)(2,1)S(1)}, bf16[12,48,256]{2,1,0:T(8,128)(2,1)S(1)}, u32[]{:S(2)}, u32[]{:S(2)}) collective-permute-start(bf16[12,48,256]{2,1,0:T(8,128)(2,1)S(1)} %copy-done.12), channel_id=1, source_target_pairs={{0,1},{1,2},{2,3},{3,0},{4,5},{5,6},{6,7},{7,4},{8,9},{9,10},{10,1... | collective-permute-start | bytes 884744 | tf_op jit(solution)/shard_map/ppermute | solution.py:13
  152.1 5.6 %collective-permute-done.29 = bf16[12,48,256]{2,1,0:T(8,128)(2,1)S(1)} collective-permute-done((bf16[12,48,256]{2,1,0:T(8,128)(2,1)S(1)}, bf16[12,48,256]{2,1,0:T(8,128)(2,1)S(1)}, u32[]{:S(2)}, u32[]{:S(2)}) %collective-permute-start.29) | collective-permute-done | bytes 294944 | tf_op jit(solution)/shard_map/ppermute | solution.py:13
  158.5 4.2 %collective-permute-start.32 = (bf16[12,48,256]{2,1,0:T(8,128)(2,1)}, bf16[12,48,256]{2,1,0:T(8,128)(2,1)}, u32[]{:S(2)}, u32[]{:S(2)}) collective-permute-start(bf16[12,48,256]{2,1,0:T(8,128)(2,1)} %broadcast_select_fusion.13), channel_id=1, source_target_pairs={{0,2},{1,3},{2,0},{3,1},{4,6},{5,7},{6,4},{7,5},{8,10},{9,11},{10,... | collective-permute-start | bytes 884744 | tf_op jit(solution)/shard_map/ppermute | solution.py:13
  162.7 19.1 %while.56 = (s32[]{:T(128)}, bf16[1920,128]{1,0:T(8,128)(2,1)S(1)}, bf16[1920,128]{1,0:T(8,128)(2,1)S(1)}, bf16[1920,128]{1,0:T(8,128)(2,1)S(1)}, bf16[12,48,256...) while((s32[]{:T(128)}, bf16[1920,128]{1,0:T(8,128)(2,1)S(1)}, ...), condition=%wide.region_9.10_spmd, body=%wide.region_8.9_spmd.sunk | while | flops 2271166464 | bytes 77368712 | solution.py:201
  164.9 1.5 collective-permute-start.8
  166.5 5.8 %collective-permute-done.9 = bf16[960,128]{1,0:T(8,128)(2,1)S(1)} collective-permute-done((bf16[960,128]{1,0:T(8,128)(2,1)}, bf16[960,128]{1,0:T(8,128)(2,1)S(1)}, u32[]{:S(2)}, u32[]{:S(2)}) %collective-permute-start.9) | collective-permute-done | bytes 245792 | tf_op jit(solution)/shard_map/while/body/ppermute | solution.py:17
  173.6 1.3 copy-done.8
  176.5 2.1 convolution_add_fusion.12
  184.4 7.9 %collective-permute-done.36 = bf16[12,48,256]{2,1,0:T(8,128)(2,1)S(1)} collective-permute-done((bf16[12,48,256]{2,1,0:T(8,128)(2,1)}, bf16[12,48,256]{2,1,0:T(8,128)(2,1)S(1)}, u32[]{:S(2)}, u32[]{:S(2)}) %collective-permute-start.36) | collective-permute-done | bytes 294944 | tf_op jit(solution)/shard_map/ppermute | solution.py:13
  192.9 1.6 collective-permute-start.34
  195.2 3.4 %collective-permute-done.34 = bf16[4,48,2,1,128]{4,2,1,0,3:T(2,128)(2,1)S(1)} collective-permute-done((bf16[4,48,2,1,128]{4,2,1,0,3:T(2,128)(2,1)S(1)}, bf16[4,48,2,1,128]{4,2,1,0,3:T(2,128)(2,1)S(1)}, u32[]{:S(2)}, u32[]{:S(2)}) %collective-permute-start.34) | collective-permute-done | bytes 98336 | tf_op jit(solution)/shard_map/ppermute | solution.py:17
  198.6 1.3 collective-permute-done.35
  199.9 6.2 %collective-permute-done.37 = bf16[12,48,256]{2,1,0:T(8,128)(2,1)S(1)} collective-permute-done((bf16[12,48,256]{2,1,0:T(8,128)(2,1)S(1)}, bf16[12,48,256]{2,1,0:T(8,128)(2,1)S(1)}, u32[]{:S(2)}, u32[]{:S(2)}) %collective-permute-start.37) | collective-permute-done | bytes 294944 | tf_op jit(solution)/shard_map/ppermute | solution.py:13
  207.1 1.6 collective-permute-start.39
  210.4 2.3 %collective-permute-done.39 = bf16[4,48,2,1,128]{4,2,1,0,3:T(2,128)(2,1)S(1)} collective-permute-done((bf16[4,48,2,1,128]{4,2,1,0,3:T(2,128)(2,1)S(1)}, bf16[4,48,2,1,128]{4,2,1,0,3:T(2,128)(2,1)S(1)}, u32[]{:S(2)}, u32[]{:S(2)}) %collective-permute-start.39) | collective-permute-done | bytes 98336 | tf_op jit(solution)/shard_map/ppermute | solution.py:17
  216.3 2.1 copy.19
  (173 shorter events, 39.8 us)
Async XLA Ops:
  0.0 18.8 %copy-start = (bf16[2048,512]{1,0:T(8,128)(2,1)S(1)}, bf16[2048,512]{1,0:T(8,128)(2,1)}, u32[]{:S(2)}) copy-start(bf16[2048,512]{1,0:T(8,128)(2,1)} %param.17) | copy-start | bytes 6291460
  0.0 17.4 %copy-start.19 = (s32[4]{0:T(128)S(1)}, s32[4]{0:T(128)}, u32[]{:S(2)}) copy-start(s32[4]{0:T(128)} %param.20) | copy-start | bytes 52
  1.7 9.3 %collective-permute-start.12 = (bf16[1024,128]{1,0:T(8,128)(2,1)S(1)}, bf16[1024,128]{1,0:T(8,128)(2,1)S(1)}, u32[]{:S(2)}, u32[]{:S(2)}) collective-permute-start(bf16[1024,128]{1,0:T(8,128)(2,1)S(1)} %get-tuple-element.422), channel_id=1, source_target_pairs={{0,8},{4,12},{8,0},{12,4},{1,9},{5,13},{9,1},{13,5},{2,10},{6,14},... | collective-permute-start | bytes 786440 | tf_op jit(solution)/shard_map/ppermute | solution.py:17
  4.7 3.6 %collective-permute-start.13 = (bf16[2048]{0:T(1024)(128)(2,1)}, bf16[2048]{0:T(1024)(128)(2,1)S(1)}, u32[]{:S(2)}, u32[]{:S(2)}) collective-permute-start(bf16[2048]{0:T(1024)(128)(2,1)} %param.16), channel_id=1, source_target_pairs={{0,0},{1,4},{2,8},{3,12},{4,1},{5,5},{6,9},{7,13},{8,2},{9,6},{10,... | collective-permute-start | bytes 12296 | tf_op jit(solution)/shard_map/ppermute | solution.py:165
  11.1 8.1 %collective-permute-start.14 = (bf16[1024,128]{1,0:T(8,128)(2,1)S(1)}, bf16[1024,128]{1,0:T(8,128)(2,1)S(1)}, u32[]{:S(2)}, u32[]{:S(2)}) collective-permute-start(bf16[1024,128]{1,0:T(8,128)(2,1)S(1)} %get-tuple-element.610), channel_id=1, source_target_pairs={{0,0},{1,4},{2,6},{3,2},{4,1},{5,5},{6,7},{7,3},{8,8},{9,12},{10,1... | collective-permute-start | bytes 786440 | tf_op jit(solution)/shard_map/ppermute | solution.py:165
  11.8 16.3 %collective-permute-start.15 = (bf16[1024,128]{1,0:T(8,128)(2,1)S(1)}, bf16[1024,128]{1,0:T(8,128)(2,1)}, u32[]{:S(2)}, u32[]{:S(2)}) collective-permute-start(bf16[1024,128]{1,0:T(8,128)(2,1)S(1)} %get-tuple-element.609), channel_id=1, source_target_pairs={{0,2},{1,6},{2,4},{3,0},{4,3},{5,7},{6,5},{7,1},{8,10},{9,14},{10,... | collective-permute-start | bytes 786440 | tf_op jit(solution)/shard_map/ppermute | solution.py:165
  16.8 11.2 %collective-permute-start.16 = (bf16[1024,128]{1,0:T(8,128)(2,1)S(1)}, bf16[1024,128]{1,0:T(8,128)(2,1)S(1)}, u32[]{:S(2)}, u32[]{:S(2)}) collective-permute-start(bf16[1024,128]{1,0:T(8,128)(2,1)S(1)} %get-tuple-element.427), channel_id=1, source_target_pairs={{0,8},{4,12},{8,0},{12,4},{1,9},{5,13},{9,1},{13,5},{2,10},{6,14},... | collective-permute-start | bytes 786440 | tf_op jit(solution)/shard_map/ppermute | solution.py:17
  29.2 14.5 %collective-permute-start.17 = (bf16[1024,256]{1,0:T(8,128)(2,1)S(1)}, bf16[1024,256]{1,0:T(8,128)(2,1)S(1)}, u32[]{:S(2)}, u32[]{:S(2)}) collective-permute-start(bf16[1024,256]{1,0:T(8,128)(2,1)S(1)} %constant_dynamic-update-slice_fusion.2), channel_id=1, source_target_pairs={{0,8},{4,12},{8,0},{12,4},{1,9},{5,13},{9,1},{13,5},{2,10},{6,14},... | collective-permute-start | bytes 1572872 | tf_op jit(solution)/shard_map/ppermute | solution.py:17
  43.8 3.3 %collective-permute-start.18 = (bf16[2048,256]{1,0:T(8,128)(2,1)S(1)}, bf16[2048,256]{1,0:T(8,128)(2,1)S(1)}, u32[]{:S(2)}, u32[]{:S(2)}) collective-permute-start(bf16[2048,256]{1,0:T(8,128)(2,1)S(1)} %pad_maximum_fusion.7.near), channel_id=1, source_target_pairs={{0,4},{4,0},{8,12},{12,8},{1,5},{5,1},{9,13},{13,9},{2,6},{6,2},{1... | collective-permute-start | bytes 3145736 | tf_op jit(solution)/shard_map/ppermute | solution.py:17
  44.1 3.0 %collective-permute-start.21 = (f32[1,512]{1,0:T(1,128)S(1)}, f32[1,512]{1,0:T(1,128)S(1)}, u32[]{:S(2)}, u32[]{:S(2)}) collective-permute-start(f32[1,512]{1,0:T(1,128)S(1)} %fusion.30), channel_id=1, source_target_pairs={{0,4},{4,0},{8,12},{12,8},{1,5},{5,1},{9,13},{13,9},{2,6},{6,2},{1... | collective-permute-start | bytes 6152 | tf_op jit(solution)/shard_map/ppermute | solution.py:17
  44.7 10.1 %collective-permute-start.19 = (bf16[1024,128]{1,0:T(8,128)(2,1)S(1)}, bf16[1024,128]{1,0:T(8,128)(2,1)S(1)}, u32[]{:S(2)}, u32[]{:S(2)}) collective-permute-start(bf16[1024,128]{1,0:T(8,128)(2,1)S(1)} %get-tuple-element.608), channel_id=1, source_target_pairs={{0,0},{1,4},{2,6},{3,2},{4,1},{5,5},{6,7},{7,3},{8,8},{9,12},{10,1... | collective-permute-start | bytes 786440 | tf_op jit(solution)/shard_map/ppermute | solution.py:165
  45.4 13.0 %collective-permute-start.20 = (bf16[1024,128]{1,0:T(8,128)(2,1)S(1)}, bf16[1024,128]{1,0:T(8,128)(2,1)S(1)}, u32[]{:S(2)}, u32[]{:S(2)}) collective-permute-start(bf16[1024,128]{1,0:T(8,128)(2,1)S(1)} %get-tuple-element.607), channel_id=1, source_target_pairs={{0,2},{1,6},{2,4},{3,0},{4,3},{5,7},{6,5},{7,1},{8,10},{9,14},{10,... | collective-permute-start | bytes 786440 | tf_op jit(solution)/shard_map/ppermute | solution.py:165
  59.0 32.2 %collective-permute-start.24 = (bf16[2560,128]{1,0:T(8,128)(2,1)}, bf16[2560,128]{1,0:T(8,128)(2,1)}, u32[]{:S(2)}, u32[]{:S(2)}) collective-permute-start(bf16[2560,128]{1,0:T(8,128)(2,1)} %get-tuple-element.445), channel_id=1, source_target_pairs={{0,1},{1,0},{2,3},{3,2},{4,5},{5,4},{6,7},{7,6},{8,9},{9,8},{10,11... | collective-permute-start | bytes 1966088 | tf_op jit(solution)/shard_map/ppermute | solution.py:17
  59.6 31.6 %collective-permute-start.22 = (bf16[1280,128]{1,0:T(8,128)(2,1)}, bf16[1280,128]{1,0:T(8,128)(2,1)}, u32[]{:S(2)}, u32[]{:S(2)}) collective-permute-start(bf16[1280,128]{1,0:T(8,128)(2,1)} %get-tuple-element.443), channel_id=1, source_target_pairs={{0,2},{1,3},{2,0},{3,1},{4,6},{5,7},{6,4},{7,5},{8,10},{9,11},{10,... | collective-permute-start | bytes 983048 | tf_op jit(solution)/shard_map/ppermute | solution.py:17
  61.0 30.2 %collective-permute-start.23 = (bf16[1280,128]{1,0:T(8,128)(2,1)}, bf16[1280,128]{1,0:T(8,128)(2,1)}, u32[]{:S(2)}, u32[]{:S(2)}) collective-permute-start(bf16[1280,128]{1,0:T(8,128)(2,1)} %get-tuple-element.444), channel_id=1, source_target_pairs={{0,3},{1,2},{2,1},{3,0},{4,7},{5,6},{6,5},{7,4},{8,11},{9,10},{10,... | collective-permute-start | bytes 983048 | tf_op jit(solution)/shard_map/ppermute | solution.py:17
  65.3 14.0 %collective-permute-start = (bf16[1024,256]{1,0:T(8,128)(2,1)S(1)}, bf16[1024,256]{1,0:T(8,128)(2,1)}, u32[]{:S(2)}, u32[]{:S(2)}) collective-permute-start(bf16[1024,256]{1,0:T(8,128)(2,1)S(1)} %copy.33), channel_id=1, source_target_pairs={{0,8},{4,12},{8,0},{12,4},{1,9},{5,13},{9,1},{13,5},{2,10},{6,14},... | collective-permute-start | bytes 1572872 | tf_op jit(solution)/shard_map/while/body/ppermute | solution.py:17
  65.9 13.3 %collective-permute-start.1 = (f32[1,512]{1,0:T(1,128)S(1)}, f32[1,512]{1,0:T(1,128)S(1)}, u32[]{:S(2)}, u32[]{:S(2)}) collective-permute-start(f32[1,512]{1,0:T(1,128)S(1)} %copy.34), channel_id=1, source_target_pairs={{0,8},{4,12},{8,0},{12,4},{1,9},{5,13},{9,1},{13,5},{2,10},{6,14},... | collective-permute-start | bytes 6152 | tf_op jit(solution)/shard_map/while/body/ppermute | solution.py:17
  80.4 2.7 %collective-permute-start.2 = (bf16[2048,256]{1,0:T(8,128)(2,1)S(1)}, bf16[2048,256]{1,0:T(8,128)(2,1)S(1)}, u32[]{:S(2)}, u32[]{:S(2)}) collective-permute-start(bf16[2048,256]{1,0:T(8,128)(2,1)S(1)} %pad_maximum_fusion.19.near), channel_id=1, source_target_pairs={{0,4},{4,0},{8,12},{12,8},{1,5},{5,1},{9,13},{13,9},{2,6},{6,2},{1... | collective-permute-start | bytes 3145736 | tf_op jit(solution)/shard_map/while/body/ppermute | solution.py:17
  92.3 12.7 %copy-start.15 = (f32[1,512]{1,0:T(1,128)S(1)}, f32[1,512]{1,0:T(1,128)}, u32[]{:S(2)}) copy-start(f32[1,512]{1,0:T(1,128)} %get-tuple-element.477) | copy-start | bytes 6148
  92.3 12.7 %copy-start.16 = (f32[1,128]{1,0:T(1,128)S(1)}, f32[1,128]{1,0:T(1,128)}, u32[]{:S(2)}) copy-start(f32[1,128]{1,0:T(1,128)} %param.18) | copy-start | bytes 1540
  92.3 8.2 %collective-permute-start.25 = (bf16[640,128]{1,0:T(8,128)(2,1)S(1)}, bf16[640,128]{1,0:T(8,128)(2,1)S(1)}, u32[]{:S(2)}, u32[]{:S(2)}) collective-permute-start(bf16[640,128]{1,0:T(8,128)(2,1)S(1)} %slice.147), channel_id=1, source_target_pairs={{0,3},{1,2},{2,1},{3,0},{4,7},{5,6},{6,5},{7,4},{8,11},{9,10},{10,... | collective-permute-start | bytes 491528 | tf_op jit(solution)/shard_map/ppermute | solution.py:17
  100.5 38.9 %collective-permute-start.26 = (bf16[1920,128]{1,0:T(8,128)(2,1)}, bf16[1920,128]{1,0:T(8,128)(2,1)}, u32[]{:S(2)}, u32[]{:S(2)}) collective-permute-start(bf16[1920,128]{1,0:T(8,128)(2,1)} %get-tuple-element.464), channel_id=1, source_target_pairs={{0,2},{1,3},{2,0},{3,1},{4,6},{5,7},{6,4},{7,5},{8,10},{9,11},{10,... | collective-permute-start | bytes 1474568 | tf_op jit(solution)/shard_map/ppermute | solution.py:17
  103.6 35.8 %collective-permute-start.27 = (bf16[1920,128]{1,0:T(8,128)(2,1)}, bf16[1920,128]{1,0:T(8,128)(2,1)}, u32[]{:S(2)}, u32[]{:S(2)}) collective-permute-start(bf16[1920,128]{1,0:T(8,128)(2,1)} %get-tuple-element.465), channel_id=1, source_target_pairs={{0,3},{1,2},{2,1},{3,0},{4,7},{5,6},{6,5},{7,4},{8,11},{9,10},{10,... | collective-permute-start | bytes 1474568 | tf_op jit(solution)/shard_map/ppermute | solution.py:17
  104.9 34.5 %collective-permute-start.28 = (bf16[1920,128]{1,0:T(8,128)(2,1)}, bf16[1920,128]{1,0:T(8,128)(2,1)}, u32[]{:S(2)}, u32[]{:S(2)}) collective-permute-start(bf16[1920,128]{1,0:T(8,128)(2,1)} %get-tuple-element.466), channel_id=1, source_target_pairs={{0,1},{1,0},{2,3},{3,2},{4,5},{5,4},{6,7},{7,6},{8,9},{9,8},{10,11... | collective-permute-start | bytes 1474568 | tf_op jit(solution)/shard_map/ppermute | solution.py:17
  105.0 34.4 %copy-start.10 = (f32[1920,128]{1,0:T(8,128)S(1)}, f32[1920,128]{1,0:T(8,128)}, u32[]{:S(2)}) copy-start(f32[1920,128]{1,0:T(8,128)} %get-tuple-element.480) | copy-start | bytes 2949124
  105.1 11.4 %collective-permute-start.3 = (bf16[1920,128]{1,0:T(8,128)(2,1)S(1)}, bf16[1920,128]{1,0:T(8,128)(2,1)S(1)}, u32[]{:S(2)}, u32[]{:S(2)}) collective-permute-start(bf16[1920,128]{1,0:T(8,128)(2,1)S(1)} %copy.52), channel_id=1, source_target_pairs={{0,8},{4,12},{8,0},{12,4},{1,9},{5,13},{9,1},{13,5},{2,10},{6,14},... | collective-permute-start | bytes 1474568 | tf_op jit(solution)/shard_map/while/body/ppermute | solution.py:17
  106.7 11.1 %collective-permute-start.4 = (bf16[1920,128]{1,0:T(8,128)(2,1)S(1)}, bf16[1920,128]{1,0:T(8,128)(2,1)S(1)}, u32[]{:S(2)}, u32[]{:S(2)}) collective-permute-start(bf16[1920,128]{1,0:T(8,128)(2,1)S(1)} %copy.52), channel_id=1, source_target_pairs={{0,16},{16,0},{1,17},{17,1},{2,18},{18,2},{3,19},{19,3},{4,20},{20... | collective-permute-start | bytes 1474568 | tf_op jit(solution)/shard_map/while/body/ppermute | solution.py:17
  118.0 13.7 %collective-permute-start.6 = (bf16[1920,256]{1,0:T(8,128)(2,1)S(1)}, bf16[1920,256]{1,0:T(8,128)(2,1)}, u32[]{:S(2)}, u32[]{:S(2)}) collective-permute-start(bf16[1920,256]{1,0:T(8,128)(2,1)S(1)} %pad_maximum_fusion.20), channel_id=1, source_target_pairs={{0,4},{4,0},{8,12},{12,8},{1,5},{5,1},{9,13},{13,9},{2,6},{6,2},{1... | collective-permute-start | bytes 2949128 | tf_op jit(solution)/shard_map/while/body/ppermute | solution.py:17
  118.1 13.6 %collective-permute-start.5 = (bf16[1920,128]{1,0:T(8,128)(2,1)S(1)}, bf16[1920,128]{1,0:T(8,128)(2,1)S(1)}, u32[]{:S(2)}, u32[]{:S(2)}) collective-permute-start(bf16[1920,128]{1,0:T(8,128)(2,1)S(1)} %collective-permute-done.4), channel_id=1, source_target_pairs={{0,8},{4,12},{8,0},{12,4},{1,9},{5,13},{9,1},{13,5},{2,10},{6,14},... | collective-permute-start | bytes 1474568 | tf_op jit(solution)/shard_map/while/body/ppermute | solution.py:17
  118.6 13.4 %copy-start.7 = (bf16[576,1920]{1,0:T(8,128)(2,1)S(1)}, bf16[576,1920]{1,0:T(8,128)(2,1)}, u32[]{:S(2)}) copy-start(bf16[576,1920]{1,0:T(8,128)(2,1)} %get-tuple-element.972) | copy-start | bytes 6635524 | tf_op jit(solution)/shard_map/while
  131.9 4.7 %collective-permute-start.7 = (bf16[1920,256]{1,0:T(8,128)(2,1)S(1)}, bf16[1920,256]{1,0:T(8,128)(2,1)S(1)}, u32[]{:S(2)}, u32[]{:S(2)}) collective-permute-start(bf16[1920,256]{1,0:T(8,128)(2,1)S(1)} %pad_maximum_fusion.21), channel_id=1, source_target_pairs={{0,4},{4,0},{8,12},{12,8},{1,5},{5,1},{9,13},{13,9},{2,6},{6,2},{1... | collective-permute-start | bytes 2949128 | tf_op jit(solution)/shard_map/while/body/ppermute | solution.py:17
  141.0 16.7 %collective-permute-start.30 = (bf16[1920,128]{1,0:T(8,128)(2,1)S(1)}, bf16[1920,128]{1,0:T(8,128)(2,1)S(1)}, u32[]{:S(2)}, u32[]{:S(2)}) collective-permute-start(bf16[1920,128]{1,0:T(8,128)(2,1)S(1)} %add_convert_fusion), channel_id=1, source_target_pairs={{0,8},{4,12},{8,0},{12,4},{1,9},{5,13},{9,1},{13,5},{2,10},{6,14},... | collective-permute-start | bytes 1474568 | tf_op jit(solution)/shard_map/ppermute | solution.py:17
  141.6 16.2 %collective-permute-start.31 = (bf16[1920,128]{1,0:T(8,128)(2,1)S(1)}, bf16[1920,128]{1,0:T(8,128)(2,1)S(1)}, u32[]{:S(2)}, u32[]{:S(2)}) collective-permute-start(bf16[1920,128]{1,0:T(8,128)(2,1)S(1)} %add_convert_fusion), channel_id=1, source_target_pairs={{0,16},{16,0},{1,17},{17,1},{2,18},{18,2},{3,19},{19,3},{4,20},{20... | collective-permute-start | bytes 1474568 | tf_op jit(solution)/shard_map/ppermute | solution.py:17
  143.3 14.4 %collective-permute-start.29 = (bf16[12,48,256]{2,1,0:T(8,128)(2,1)S(1)}, bf16[12,48,256]{2,1,0:T(8,128)(2,1)S(1)}, u32[]{:S(2)}, u32[]{:S(2)}) collective-permute-start(bf16[12,48,256]{2,1,0:T(8,128)(2,1)S(1)} %copy-done.12), channel_id=1, source_target_pairs={{0,1},{1,2},{2,3},{3,0},{4,5},{5,6},{6,7},{7,4},{8,9},{9,10},{10,1... | collective-permute-start | bytes 884744 | tf_op jit(solution)/shard_map/ppermute | solution.py:13
  158.5 23.3 %collective-permute-start.32 = (bf16[12,48,256]{2,1,0:T(8,128)(2,1)}, bf16[12,48,256]{2,1,0:T(8,128)(2,1)}, u32[]{:S(2)}, u32[]{:S(2)}) collective-permute-start(bf16[12,48,256]{2,1,0:T(8,128)(2,1)} %broadcast_select_fusion.13), channel_id=1, source_target_pairs={{0,2},{1,3},{2,0},{3,1},{4,6},{5,7},{6,4},{7,5},{8,10},{9,11},{10,... | collective-permute-start | bytes 884744 | tf_op jit(solution)/shard_map/ppermute | solution.py:13
  163.0 10.2 %collective-permute-start.10 = (bf16[1920,256]{1,0:T(8,128)(2,1)S(1)}, bf16[1920,256]{1,0:T(8,128)(2,1)}, u32[]{:S(2)}, u32[]{:S(2)}) collective-permute-start(bf16[1920,256]{1,0:T(8,128)(2,1)S(1)} %pad_maximum_fusion.23), channel_id=1, source_target_pairs={{0,4},{4,0},{8,12},{12,8},{1,5},{5,1},{9,13},{13,9},{2,6},{6,2},{1... | collective-permute-start | bytes 2949128 | tf_op jit(solution)/shard_map/while/body/ppermute | solution.py:17
  163.8 8.6 %collective-permute-start.9 = (bf16[960,128]{1,0:T(8,128)(2,1)}, bf16[960,128]{1,0:T(8,128)(2,1)S(1)}, u32[]{:S(2)}, u32[]{:S(2)}) collective-permute-start(bf16[960,128]{1,0:T(8,128)(2,1)} %slice.171), channel_id=1, source_target_pairs={{0,8},{4,12},{8,0},{12,4},{1,9},{5,13},{9,1},{13,5},{2,10},{6,14},... | collective-permute-start | bytes 737288 | tf_op jit(solution)/shard_map/while/body/ppermute | solution.py:17
  164.9 8.3 %collective-permute-start.8 = (bf16[960,128]{1,0:T(8,128)(2,1)}, bf16[960,128]{1,0:T(8,128)(2,1)S(1)}, u32[]{:S(2)}, u32[]{:S(2)}) collective-permute-start(bf16[960,128]{1,0:T(8,128)(2,1)} %slice.170), channel_id=1, source_target_pairs={{0,16},{16,0},{1,17},{17,1},{2,18},{18,2},{3,19},{19,3},{4,20},{20... | collective-permute-start | bytes 737288 | tf_op jit(solution)/shard_map/while/body/ppermute | solution.py:17
  173.5 5.9 %collective-permute-start.11 = (bf16[1920,256]{1,0:T(8,128)(2,1)S(1)}, bf16[1920,256]{1,0:T(8,128)(2,1)S(1)}, u32[]{:S(2)}, u32[]{:S(2)}) collective-permute-start(bf16[1920,256]{1,0:T(8,128)(2,1)S(1)} %pad_maximum_fusion.24), channel_id=1, source_target_pairs={{0,4},{4,0},{8,12},{12,8},{1,5},{5,1},{9,13},{13,9},{2,6},{6,2},{1... | collective-permute-start | bytes 2949128 | tf_op jit(solution)/shard_map/while/body/ppermute | solution.py:17
  181.9 10.4 %copy-start.11 = (bf16[12,48,256]{2,1,0:T(8,128)(2,1)S(1)}, bf16[12,48,256]{2,1,0:T(8,128)(2,1)}, u32[]{:S(2)}) copy-start(bf16[12,48,256]{2,1,0:T(8,128)(2,1)} %get-tuple-element.492) | copy-start | bytes 884740
  181.9 10.4 %collective-permute-start.36 = (bf16[12,48,256]{2,1,0:T(8,128)(2,1)}, bf16[12,48,256]{2,1,0:T(8,128)(2,1)S(1)}, u32[]{:S(2)}, u32[]{:S(2)}) collective-permute-start(bf16[12,48,256]{2,1,0:T(8,128)(2,1)} %get-tuple-element.492), channel_id=1, source_target_pairs={{0,1},{1,2},{2,3},{3,0},{4,5},{5,6},{6,7},{7,4},{8,9},{9,10},{10,1... | collective-permute-start | bytes 884744 | tf_op jit(solution)/shard_map/ppermute | solution.py:13
  192.4 13.7 %collective-permute-start.37 = (bf16[12,48,256]{2,1,0:T(8,128)(2,1)S(1)}, bf16[12,48,256]{2,1,0:T(8,128)(2,1)S(1)}, u32[]{:S(2)}, u32[]{:S(2)}) collective-permute-start(bf16[12,48,256]{2,1,0:T(8,128)(2,1)S(1)} %broadcast_select_fusion.12), channel_id=1, source_target_pairs={{0,2},{1,3},{2,0},{3,1},{4,6},{5,7},{6,4},{7,5},{8,10},{9,11},{10,... | collective-permute-start | bytes 884744 | tf_op jit(solution)/shard_map/ppermute | solution.py:13
  192.7 2.4 %collective-permute-start.33 = (bf16[4,48,2,1,128]{4,2,1,0,3:T(2,128)(2,1)S(1)}, bf16[4,48,2,1,128]{4,2,1,0,3:T(2,128)(2,1)S(1)}, u32[]{:S(2)}, u32[]{:S(2)}) collective-permute-start(bf16[4,48,2,1,128]{4,2,1,0,3:T(2,128)(2,1)S(1)} %squeeze.29), channel_id=1, source_target_pairs={{0,4},{4,0},{8,12},{12,8},{1,5},{5,1},{9,13},{13,9},{2,6},{6,2},{1... | collective-permute-start | bytes 294920 | tf_op jit(solution)/shard_map/ppermute | solution.py:17
  192.9 5.7 %collective-permute-start.34 = (bf16[4,48,2,1,128]{4,2,1,0,3:T(2,128)(2,1)S(1)}, bf16[4,48,2,1,128]{4,2,1,0,3:T(2,128)(2,1)S(1)}, u32[]{:S(2)}, u32[]{:S(2)}) collective-permute-start(bf16[4,48,2,1,128]{4,2,1,0,3:T(2,128)(2,1)S(1)} %squeeze.30), channel_id=1, source_target_pairs={{0,8},{4,12},{8,0},{12,4},{1,9},{5,13},{9,1},{13,5},{2,10},{6,14},... | collective-permute-start | bytes 294920 | tf_op jit(solution)/shard_map/ppermute | solution.py:17
  194.7 5.2 %collective-permute-start.35 = (bf16[4,48,2,1,128]{4,2,1,0,3:T(2,128)(2,1)S(1)}, bf16[4,48,2,1,128]{4,2,1,0,3:T(2,128)(2,1)S(1)}, u32[]{:S(2)}, u32[]{:S(2)}) collective-permute-start(bf16[4,48,2,1,128]{4,2,1,0,3:T(2,128)(2,1)S(1)} %squeeze.31), channel_id=1, source_target_pairs={{0,12},{4,8},{8,4},{12,0},{1,13},{5,9},{9,5},{13,1},{2,14},{6,10},... | collective-permute-start | bytes 294920 | tf_op jit(solution)/shard_map/ppermute | solution.py:17
  206.9 3.5 %collective-permute-start.38 = (bf16[4,48,2,1,128]{4,2,1,0,3:T(2,128)(2,1)S(1)}, bf16[4,48,2,1,128]{4,2,1,0,3:T(2,128)(2,1)S(1)}, u32[]{:S(2)}, u32[]{:S(2)}) collective-permute-start(bf16[4,48,2,1,128]{4,2,1,0,3:T(2,128)(2,1)S(1)} %squeeze.33), channel_id=1, source_target_pairs={{0,4},{4,0},{8,12},{12,8},{1,5},{5,1},{9,13},{13,9},{2,6},{6,2},{1... | collective-permute-start | bytes 294920 | tf_op jit(solution)/shard_map/ppermute | solution.py:17
  207.1 5.7 %collective-permute-start.39 = (bf16[4,48,2,1,128]{4,2,1,0,3:T(2,128)(2,1)S(1)}, bf16[4,48,2,1,128]{4,2,1,0,3:T(2,128)(2,1)S(1)}, u32[]{:S(2)}, u32[]{:S(2)}) collective-permute-start(bf16[4,48,2,1,128]{4,2,1,0,3:T(2,128)(2,1)S(1)} %squeeze.34), channel_id=1, source_target_pairs={{0,8},{4,12},{8,0},{12,4},{1,9},{5,13},{9,1},{13,5},{2,10},{6,14},... | collective-permute-start | bytes 294920 | tf_op jit(solution)/shard_map/ppermute | solution.py:17
  208.9 5.2 %collective-permute-start.40 = (bf16[4,48,2,1,128]{4,2,1,0,3:T(2,128)(2,1)S(1)}, bf16[4,48,2,1,128]{4,2,1,0,3:T(2,128)(2,1)S(1)}, u32[]{:S(2)}, u32[]{:S(2)}) collective-permute-start(bf16[4,48,2,1,128]{4,2,1,0,3:T(2,128)(2,1)S(1)} %squeeze.35), channel_id=1, source_target_pairs={{0,12},{4,8},{8,4},{12,0},{1,13},{5,9},{9,5},{13,1},{2,14},{6,10},... | collective-permute-start | bytes 294920 | tf_op jit(solution)/shard_map/ppermute | solution.py:17
  (13 other events, 47.3 us)

commit v24 on v23

--- a/solution.py
+++ b/solution.py
@@ -247,12 +247,12 @@
 
     def to_planes(stays, comes):
         pieces = []
-        for j in range(2):
+        for j in (1, 0):
             piece = jnp.where(tile // 2 == (head // 2) ^ j, stays, comes)
             pieces.append(
                 moved(piece, lambda t, h: (t // 2 * 2 + outer_core(h), t % 2 + 2 * ((h // 2) ^ j)))
             )
-        return pieces
+        return pieces[::-1]
 
     key_stays, key_leaves, rows_later = step((*halves(kv_weight, 0), kv_weight))
     bias_rows = moved(proj_bias, lambda t, h: (h, t))

time: 219 us -> 219 us (level)
  no operation moved by 1% of the time
where the time goes in v24:
time: 219 us; the launch traced here: 218 us
  waiting for transfers between devices  98.2 us (45%)
  starting transfers between devices  53.2 us (24%)
  local copies, waits for them, and re-layouts  24.9 us (11%)
  Pallas kernels  15.7 us (7%)
  other arithmetic  14.9 us (7%)
  matrix products  9.93 us (5%)
    ppermute x32, waiting for transfers between devices, swapped(): lax.ppermute(shard, axis, [(i, i ^ bit) for i in range(lax.axis_size(axis...  66 us
    ppermute x32, starting transfers between devices, swapped(): lax.ppermute(shard, axis, [(i, i ^ bit) for i in range(lax.axis_size(axis...  29.7 us
    ppermute x4, waiting for transfers between devices, shifted_2(): lax.ppermute(shard, axis, [(i, (i + by) % count) for i in range(count)])  19.7 us
    pallas_call x2, Pallas kernels, product_terms(): pl.pallas_call(terms_body, out_shape=shapes, grid_spec=pltpu.PrefetchScal...  15.7 us
    ppermute x4, starting transfers between devices, shifted_2(): lax.ppermute(shard, axis, [(i, (i + by) % count) for i in range(count)])  14 us
    ppermute x5, waiting for transfers between devices, moved(): return lax.ppermute(shard, ('tile', 'head'), pairs)  12.5 us
    dot_general x11, matrix products, add_columns(): return jnp.dot(operand, portion, preferred_element_type=jnp.float32)  9.74 us
    ppermute x5, starting transfers between devices, moved(): return lax.ppermute(shard, ('tile', 'head'), pairs)  9.46 us
  transfers between devices with their start and end apart: 41, of which 19 were waited for; matrix products, arithmetic and copies ran while one was open for 15% of the time, Pallas kernels for 7%

profile of v24, /device:TPU:0, one launch (start us, length us, event | category | flops | bytes accessed | tf_op | source)
XLA Modules:
  0.0 218.4 jit_solution(14069410382390577920)
XLA Ops:
  0.0 1.7 fusion.24
  1.7 3.0 %collective-permute-start.12 = (bf16[1024,128]{1,0:T(8,128)(2,1)S(1)}, bf16[1024,128]{1,0:T(8,128)(2,1)S(1)}, u32[]{:S(2)}, u32[]{:S(2)}) collective-permute-start(bf16[1024,128]{1,0:T(8,128)(2,1)S(1)} %get-tuple-element.422), channel_id=1, source_target_pairs={{0,8},{4,12},{8,0},{12,4},{1,9},{5,13},{9,1},{13,5},{2,10},{6,14},... | collective-permute-start | bytes 786440 | tf_op jit(solution)/shard_map/ppermute | solution.py:17
  4.7 1.3 collective-permute-start.13
  6.1 2.2 %fusion.23 = (bf16[1024,128]{1,0:T(8,128)(2,1)S(1)}, bf16[1024,128]{1,0:T(8,128)(2,1)}) fusion(bf16[2048,512]{1,0:T(8,128)(2,1)} %param.17, s32[]{:T(128)S(6)} %select_n.307, s32[]{:T(128)S(6)} %select_n.309, s32[]{:T(128)S(6)} %select_n.303), kind=kLoop, calls=%fused_computation.124 | loop fusion | bytes 1048588 | tf_op jit(solution)/shard_map/dynamic_slice | solution.py:246
  8.3 2.7 %collective-permute-done.12 = bf16[1024,128]{1,0:T(8,128)(2,1)S(1)} collective-permute-done((bf16[1024,128]{1,0:T(8,128)(2,1)S(1)}, bf16[1024,128]{1,0:T(8,128)(2,1)S(1)}, u32[]{:S(2)}, u32[]{:S(2)}) %collective-permute-start.12) | collective-permute-done | bytes 262176 | tf_op jit(solution)/shard_map/ppermute | solution.py:17
  11.8 5.1 %collective-permute-start.15 = (bf16[1024,128]{1,0:T(8,128)(2,1)S(1)}, bf16[1024,128]{1,0:T(8,128)(2,1)}, u32[]{:S(2)}, u32[]{:S(2)}) collective-permute-start(bf16[1024,128]{1,0:T(8,128)(2,1)S(1)} %get-tuple-element.609), channel_id=1, source_target_pairs={{0,2},{1,6},{2,4},{3,0},{4,3},{5,7},{6,5},{7,1},{8,10},{9,14},{10,... | collective-permute-start | bytes 786440 | tf_op jit(solution)/shard_map/ppermute | solution.py:165
  19.2 8.9 %collective-permute-done.15 = bf16[1024,128]{1,0:T(8,128)(2,1)} collective-permute-done((bf16[1024,128]{1,0:T(8,128)(2,1)S(1)}, bf16[1024,128]{1,0:T(8,128)(2,1)}, u32[]{:S(2)}, u32[]{:S(2)}) %collective-permute-start.15) | collective-permute-done | bytes 262176 | tf_op jit(solution)/shard_map/ppermute | solution.py:165
  30.0 7.2 %constant_dynamic-slice_fusion = (bf16[576,1920]{1,0:T(8,128)(2,1)}, bf16[576,1920]{1,0:T(8,128)(2,1)}, bf16[576,1920]{1,0:T(8,128)(2,1)}, bf16[576,1920]{1,0:T(8,128)(2,1)}) fusion(bf16[576,7680]{1,0:T(8,128)(2,1)} %bitcast.133, s32[]{:T(128)S(6)} %select_n.316, s32[]{:T(128)S(6)} %select_n.315, s32[]{:T(128)S(6)} %select_n.314, s32[]{:T(128)S(6)} %select_n.313), kind=kLoop, calls=%fused_computation.115 | loop fusion | bytes 17694736 | tf_op jit(solution)/shard_map/dynamic_slice | solution.py:171
  37.2 6.4 %collective-permute-done.17 = bf16[1024,256]{1,0:T(8,128)(2,1)S(1)} collective-permute-done((bf16[1024,256]{1,0:T(8,128)(2,1)S(1)}, bf16[1024,256]{1,0:T(8,128)(2,1)S(1)}, u32[]{:S(2)}, u32[]{:S(2)}) %collective-permute-start.17) | collective-permute-done | bytes 524320 | tf_op jit(solution)/shard_map/ppermute | solution.py:17
  45.4 1.7 collective-permute-start.20
  47.1 7.7 %shard_map.82 = (f32[1280,128]{1,0:T(8,128)S(1)}, bf16[1280,128]{1,0:T(8,128)(2,1)}, bf16[1280,128]{1,0:T(8,128)(2,1)}, bf16[2560,128]{1,0:T(8,128)(2,1)}, f32[640,256]{1,0:T(8,128)S(1)}) custom-call(s32[1]{0:T(128)} %bitcast.13.choice, bf16[1920,2048]{1,0:T(8,128)(2,1)} %weight.1, bf16[2048,256]{1,0:T(8,128)(2,1)S(1)} %pad_maximum_fusion.7.near, ...), custom_call_target="tpu_custom_call" | custom-call | flops 4026531840 | bytes 12419072 | tf_op jit(solution)/shard_map/pallas_call | solution.py:118
  54.8 3.6 %collective-permute-done.20 = bf16[1024,128]{1,0:T(8,128)(2,1)S(1)} collective-permute-done((bf16[1024,128]{1,0:T(8,128)(2,1)S(1)}, bf16[1024,128]{1,0:T(8,128)(2,1)S(1)}, u32[]{:S(2)}, u32[]{:S(2)}) %collective-permute-start.20) | collective-permute-done | bytes 262176 | tf_op jit(solution)/shard_map/ppermute | solution.py:165
  59.6 1.4 collective-permute-start.22
  61.0 2.4 %collective-permute-start.23 = (bf16[1280,128]{1,0:T(8,128)(2,1)}, bf16[1280,128]{1,0:T(8,128)(2,1)}, u32[]{:S(2)}, u32[]{:S(2)}) collective-permute-start(bf16[1280,128]{1,0:T(8,128)(2,1)} %get-tuple-element.444), channel_id=1, source_target_pairs={{0,3},{1,2},{2,1},{3,0},{4,7},{5,6},{6,5},{7,4},{8,11},{9,10},{10,... | collective-permute-start | bytes 983048 | tf_op jit(solution)/shard_map/ppermute | solution.py:17
  64.2 27.0 %while.54 = (s32[]{:T(128)}, bf16[1024,256]{1,0:T(8,128)(2,1)}, f32[1,512]{1,0:T(1,128)S(1)}, f32[1920,128]{1,0:T(8,128)}, bf16[1920,128]{1,0:T(8,128)(2,1)}, /*...) while((s32[]{:T(128)}, bf16[1024,256]{1,0:T(8,128)(2,1)}, ...), condition=%wide.region_3.4_spmd, body=%wide.region_2.3_spmd.sunk | while | flops 4029153792 | bytes 23972084 | solution.py:201
  65.9 1.4 collective-permute-start.1
  67.3 11.9 %collective-permute-done.1 = f32[1,512]{1,0:T(1,128)S(1)} collective-permute-done((f32[1,512]{1,0:T(1,128)S(1)}, f32[1,512]{1,0:T(1,128)S(1)}, u32[]{:S(2)}, u32[]{:S(2)}) %collective-permute-start.1) | collective-permute-done | bytes 2080 | tf_op jit(solution)/shard_map/while/body/ppermute | solution.py:17
  81.0 2.1 collective-permute-done.2.far
  83.1 8.0 %body.1 = (f32[1920,128]{1,0:T(8,128)}, bf16[1920,128]{1,0:T(8,128)(2,1)}, bf16[1920,128]{1,0:T(8,128)(2,1)}, bf16[1920,128]{1,0:T(8,128)(2,1)}) custom-call(s32[1]{0:T(128)} %get-tuple-element.940.choice, bf16[1920,2048]{1,0:T(8,128)(2,1)} %get-tuple-element.941.weight, bf16[2048,256]{1,0:T(8,128)(2,1)S(1)} %pad_maximum_fusion.19.near, ...), custom_call_target="tpu_custom_call" | custom-call | flops 4026531840 | bytes 12419072 | tf_op jit(solution)/shard_map/while/body/pallas_call | solution.py:118
  92.3 1.9 collective-permute-start.25
  94.2 1.3 add_convert_fusion.1
  95.5 5.0 %collective-permute-done.25 = bf16[640,128]{1,0:T(8,128)(2,1)S(1)} collective-permute-done((bf16[640,128]{1,0:T(8,128)(2,1)S(1)}, bf16[640,128]{1,0:T(8,128)(2,1)S(1)}, u32[]{:S(2)}, u32[]{:S(2)}) %collective-permute-start.25) | collective-permute-done | bytes 163872 | tf_op jit(solution)/shard_map/ppermute | solution.py:17
  100.5 3.1 %collective-permute-start.26 = (bf16[1920,128]{1,0:T(8,128)(2,1)}, bf16[1920,128]{1,0:T(8,128)(2,1)}, u32[]{:S(2)}, u32[]{:S(2)}) collective-permute-start(bf16[1920,128]{1,0:T(8,128)(2,1)} %get-tuple-element.464), channel_id=1, source_target_pairs={{0,2},{1,3},{2,0},{3,1},{4,6},{5,7},{6,4},{7,5},{8,10},{9,11},{10,... | collective-permute-start | bytes 1474568 | tf_op jit(solution)/shard_map/ppermute | solution.py:17
  105.0 34.4 %while.55 = (s32[]{:T(128)}, bf16[1920,128]{1,0:T(8,128)(2,1)S(1)}, bf16[12,48,256]{2,1,0:T(8,128)(2,1)}, s32[]{:T(128)}, pred[]{:T(512)}, /*index=5*/bf16[576,1...) while((s32[]{:T(128)}, bf16[1920,128]{1,0:T(8,128)(2,1)S(1)}, ...), condition=%wide.region_7.8_spmd, body=%wide.region_4.7_spmd.sunk | while | flops 2271905024 | bytes 76995496 | solution.py:201
  105.1 1.6 collective-permute-start.3
  106.7 1.5 collective-permute-start.4
  108.2 8.3 %collective-permute-done.3 = bf16[1920,128]{1,0:T(8,128)(2,1)S(1)} collective-permute-done((bf16[1920,128]{1,0:T(8,128)(2,1)S(1)}, bf16[1920,128]{1,0:T(8,128)(2,1)S(1)}, u32[]{:S(2)}, u32[]{:S(2)}) %collective-permute-start.3) | collective-permute-done | bytes 491552 | tf_op jit(solution)/shard_map/while/body/ppermute | solution.py:17
  116.5 1.3 collective-permute-done.4
  118.6 13.1 %collective-permute-done.5 = bf16[1920,128]{1,0:T(8,128)(2,1)S(1)} collective-permute-done((bf16[1920,128]{1,0:T(8,128)(2,1)S(1)}, bf16[1920,128]{1,0:T(8,128)(2,1)S(1)}, u32[]{:S(2)}, u32[]{:S(2)}) %collective-permute-start.5) | collective-permute-done | bytes 491552 | tf_op jit(solution)/shard_map/while/body/ppermute | solution.py:17
  133.6 2.1 convolution_add_fusion.10
  139.4 1.6 add_convert_fusion
  141.6 1.5 collective-permute-start.31
  143.3 8.7 %collective-permute-start.29 = (bf16[12,48,256]{2,1,0:T(8,128)(2,1)S(1)}, bf16[12,48,256]{2,1,0:T(8,128)(2,1)S(1)}, u32[]{:S(2)}, u32[]{:S(2)}) collective-permute-start(bf16[12,48,256]{2,1,0:T(8,128)(2,1)S(1)} %copy-done.12), channel_id=1, source_target_pairs={{0,1},{1,2},{2,3},{3,0},{4,5},{5,6},{6,7},{7,4},{8,9},{9,10},{10,1... | collective-permute-start | bytes 884744 | tf_op jit(solution)/shard_map/ppermute | solution.py:13
  152.1 5.6 %collective-permute-done.29 = bf16[12,48,256]{2,1,0:T(8,128)(2,1)S(1)} collective-permute-done((bf16[12,48,256]{2,1,0:T(8,128)(2,1)S(1)}, bf16[12,48,256]{2,1,0:T(8,128)(2,1)S(1)}, u32[]{:S(2)}, u32[]{:S(2)}) %collective-permute-start.29) | collective-permute-done | bytes 294944 | tf_op jit(solution)/shard_map/ppermute | solution.py:13
  158.5 4.2 %collective-permute-start.32 = (bf16[12,48,256]{2,1,0:T(8,128)(2,1)}, bf16[12,48,256]{2,1,0:T(8,128)(2,1)}, u32[]{:S(2)}, u32[]{:S(2)}) collective-permute-start(bf16[12,48,256]{2,1,0:T(8,128)(2,1)} %broadcast_select_fusion.13), channel_id=1, source_target_pairs={{0,2},{1,3},{2,0},{3,1},{4,6},{5,7},{6,4},{7,5},{8,10},{9,11},{10,... | collective-permute-start | bytes 884744 | tf_op jit(solution)/shard_map/ppermute | solution.py:13
  162.7 19.1 %while.56 = (s32[]{:T(128)}, bf16[1920,128]{1,0:T(8,128)(2,1)S(1)}, bf16[1920,128]{1,0:T(8,128)(2,1)S(1)}, bf16[1920,128]{1,0:T(8,128)(2,1)S(1)}, bf16[12,48,256...) while((s32[]{:T(128)}, bf16[1920,128]{1,0:T(8,128)(2,1)S(1)}, ...), condition=%wide.region_9.10_spmd, body=%wide.region_8.9_spmd.sunk | while | flops 2271166464 | bytes 77368712 | solution.py:201
  164.9 1.5 collective-permute-start.8
  166.5 5.8 %collective-permute-done.9 = bf16[960,128]{1,0:T(8,128)(2,1)S(1)} collective-permute-done((bf16[960,128]{1,0:T(8,128)(2,1)}, bf16[960,128]{1,0:T(8,128)(2,1)S(1)}, u32[]{:S(2)}, u32[]{:S(2)}) %collective-permute-start.9) | collective-permute-done | bytes 245792 | tf_op jit(solution)/shard_map/while/body/ppermute | solution.py:17
  173.6 1.3 copy-done.8
  176.5 2.1 convolution_add_fusion.12
  184.4 7.9 %collective-permute-done.36 = bf16[12,48,256]{2,1,0:T(8,128)(2,1)S(1)} collective-permute-done((bf16[12,48,256]{2,1,0:T(8,128)(2,1)}, bf16[12,48,256]{2,1,0:T(8,128)(2,1)S(1)}, u32[]{:S(2)}, u32[]{:S(2)}) %collective-permute-start.36) | collective-permute-done | bytes 294944 | tf_op jit(solution)/shard_map/ppermute | solution.py:13
  192.9 1.6 collective-permute-start.34
  195.2 3.4 %collective-permute-done.34 = bf16[4,48,2,1,128]{4,2,1,0,3:T(2,128)(2,1)S(1)} collective-permute-done((bf16[4,48,2,1,128]{4,2,1,0,3:T(2,128)(2,1)S(1)}, bf16[4,48,2,1,128]{4,2,1,0,3:T(2,128)(2,1)S(1)}, u32[]{:S(2)}, u32[]{:S(2)}) %collective-permute-start.34) | collective-permute-done | bytes 98336 | tf_op jit(solution)/shard_map/ppermute | solution.py:17
  198.6 1.3 collective-permute-done.35
  199.9 6.2 %collective-permute-done.37 = bf16[12,48,256]{2,1,0:T(8,128)(2,1)S(1)} collective-permute-done((bf16[12,48,256]{2,1,0:T(8,128)(2,1)S(1)}, bf16[12,48,256]{2,1,0:T(8,128)(2,1)S(1)}, u32[]{:S(2)}, u32[]{:S(2)}) %collective-permute-start.37) | collective-permute-done | bytes 294944 | tf_op jit(solution)/shard_map/ppermute | solution.py:13
  207.1 1.6 collective-permute-start.39
  210.4 2.3 %collective-permute-done.39 = bf16[4,48,2,1,128]{4,2,1,0,3:T(2,128)(2,1)S(1)} collective-permute-done((bf16[4,48,2,1,128]{4,2,1,0,3:T(2,128)(2,1)S(1)}, bf16[4,48,2,1,128]{4,2,1,0,3:T(2,128)(2,1)S(1)}, u32[]{:S(2)}, u32[]{:S(2)}) %collective-permute-start.39) | collective-permute-done | bytes 98336 | tf_op jit(solution)/shard_map/ppermute | solution.py:17
  216.3 2.1 copy.19
  (173 shorter events, 39.8 us)
Async XLA Ops:
  0.0 18.8 %copy-start = (bf16[2048,512]{1,0:T(8,128)(2,1)S(1)}, bf16[2048,512]{1,0:T(8,128)(2,1)}, u32[]{:S(2)}) copy-start(bf16[2048,512]{1,0:T(8,128)(2,1)} %param.17) | copy-start | bytes 6291460
  0.0 17.4 %copy-start.19 = (s32[4]{0:T(128)S(1)}, s32[4]{0:T(128)}, u32[]{:S(2)}) copy-start(s32[4]{0:T(128)} %param.20) | copy-start | bytes 52
  1.7 9.3 %collective-permute-start.12 = (bf16[1024,128]{1,0:T(8,128)(2,1)S(1)}, bf16[1024,128]{1,0:T(8,128)(2,1)S(1)}, u32[]{:S(2)}, u32[]{:S(2)}) collective-permute-start(bf16[1024,128]{1,0:T(8,128)(2,1)S(1)} %get-tuple-element.422), channel_id=1, source_target_pairs={{0,8},{4,12},{8,0},{12,4},{1,9},{5,13},{9,1},{13,5},{2,10},{6,14},... | collective-permute-start | bytes 786440 | tf_op jit(solution)/shard_map/ppermute | solution.py:17
  4.7 3.6 %collective-permute-start.13 = (bf16[2048]{0:T(1024)(128)(2,1)}, bf16[2048]{0:T(1024)(128)(2,1)S(1)}, u32[]{:S(2)}, u32[]{:S(2)}) collective-permute-start(bf16[2048]{0:T(1024)(128)(2,1)} %param.16), channel_id=1, source_target_pairs={{0,0},{1,4},{2,8},{3,12},{4,1},{5,5},{6,9},{7,13},{8,2},{9,6},{10,... | collective-permute-start | bytes 12296 | tf_op jit(solution)/shard_map/ppermute | solution.py:165
  11.1 8.1 %collective-permute-start.14 = (bf16[1024,128]{1,0:T(8,128)(2,1)S(1)}, bf16[1024,128]{1,0:T(8,128)(2,1)S(1)}, u32[]{:S(2)}, u32[]{:S(2)}) collective-permute-start(bf16[1024,128]{1,0:T(8,128)(2,1)S(1)} %get-tuple-element.610), channel_id=1, source_target_pairs={{0,0},{1,4},{2,6},{3,2},{4,1},{5,5},{6,7},{7,3},{8,8},{9,12},{10,1... | collective-permute-start | bytes 786440 | tf_op jit(solution)/shard_map/ppermute | solution.py:165
  11.8 16.3 %collective-permute-start.15 = (bf16[1024,128]{1,0:T(8,128)(2,1)S(1)}, bf16[1024,128]{1,0:T(8,128)(2,1)}, u32[]{:S(2)}, u32[]{:S(2)}) collective-permute-start(bf16[1024,128]{1,0:T(8,128)(2,1)S(1)} %get-tuple-element.609), channel_id=1, source_target_pairs={{0,2},{1,6},{2,4},{3,0},{4,3},{5,7},{6,5},{7,1},{8,10},{9,14},{10,... | collective-permute-start | bytes 786440 | tf_op jit(solution)/shard_map/ppermute | solution.py:165
  16.8 11.2 %collective-permute-start.16 = (bf16[1024,128]{1,0:T(8,128)(2,1)S(1)}, bf16[1024,128]{1,0:T(8,128)(2,1)S(1)}, u32[]{:S(2)}, u32[]{:S(2)}) collective-permute-start(bf16[1024,128]{1,0:T(8,128)(2,1)S(1)} %get-tuple-element.427), channel_id=1, source_target_pairs={{0,8},{4,12},{8,0},{12,4},{1,9},{5,13},{9,1},{13,5},{2,10},{6,14},... | collective-permute-start | bytes 786440 | tf_op jit(solution)/shard_map/ppermute | solution.py:17
  29.2 14.5 %collective-permute-start.17 = (bf16[1024,256]{1,0:T(8,128)(2,1)S(1)}, bf16[1024,256]{1,0:T(8,128)(2,1)S(1)}, u32[]{:S(2)}, u32[]{:S(2)}) collective-permute-start(bf16[1024,256]{1,0:T(8,128)(2,1)S(1)} %constant_dynamic-update-slice_fusion.2), channel_id=1, source_target_pairs={{0,8},{4,12},{8,0},{12,4},{1,9},{5,13},{9,1},{13,5},{2,10},{6,14},... | collective-permute-start | bytes 1572872 | tf_op jit(solution)/shard_map/ppermute | solution.py:17
  43.8 3.3 %collective-permute-start.18 = (bf16[2048,256]{1,0:T(8,128)(2,1)S(1)}, bf16[2048,256]{1,0:T(8,128)(2,1)S(1)}, u32[]{:S(2)}, u32[]{:S(2)}) collective-permute-start(bf16[2048,256]{1,0:T(8,128)(2,1)S(1)} %pad_maximum_fusion.7.near), channel_id=1, source_target_pairs={{0,4},{4,0},{8,12},{12,8},{1,5},{5,1},{9,13},{13,9},{2,6},{6,2},{1... | collective-permute-start | bytes 3145736 | tf_op jit(solution)/shard_map/ppermute | solution.py:17
  44.1 3.0 %collective-permute-start.21 = (f32[1,512]{1,0:T(1,128)S(1)}, f32[1,512]{1,0:T(1,128)S(1)}, u32[]{:S(2)}, u32[]{:S(2)}) collective-permute-start(f32[1,512]{1,0:T(1,128)S(1)} %fusion.30), channel_id=1, source_target_pairs={{0,4},{4,0},{8,12},{12,8},{1,5},{5,1},{9,13},{13,9},{2,6},{6,2},{1... | collective-permute-start | bytes 6152 | tf_op jit(solution)/shard_map/ppermute | solution.py:17
  44.7 10.1 %collective-permute-start.19 = (bf16[1024,128]{1,0:T(8,128)(2,1)S(1)}, bf16[1024,128]{1,0:T(8,128)(2,1)S(1)}, u32[]{:S(2)}, u32[]{:S(2)}) collective-permute-start(bf16[1024,128]{1,0:T(8,128)(2,1)S(1)} %get-tuple-element.608), channel_id=1, source_target_pairs={{0,0},{1,4},{2,6},{3,2},{4,1},{5,5},{6,7},{7,3},{8,8},{9,12},{10,1... | collective-permute-start | bytes 786440 | tf_op jit(solution)/shard_map/ppermute | solution.py:165
  45.4 13.0 %collective-permute-start.20 = (bf16[1024,128]{1,0:T(8,128)(2,1)S(1)}, bf16[1024,128]{1,0:T(8,128)(2,1)S(1)}, u32[]{:S(2)}, u32[]{:S(2)}) collective-permute-start(bf16[1024,128]{1,0:T(8,128)(2,1)S(1)} %get-tuple-element.607), channel_id=1, source_target_pairs={{0,2},{1,6},{2,4},{3,0},{4,3},{5,7},{6,5},{7,1},{8,10},{9,14},{10,... | collective-permute-start | bytes 786440 | tf_op jit(solution)/shard_map/ppermute | solution.py:165
  59.0 32.2 %collective-permute-start.24 = (bf16[2560,128]{1,0:T(8,128)(2,1)}, bf16[2560,128]{1,0:T(8,128)(2,1)}, u32[]{:S(2)}, u32[]{:S(2)}) collective-permute-start(bf16[2560,128]{1,0:T(8,128)(2,1)} %get-tuple-element.445), channel_id=1, source_target_pairs={{0,1},{1,0},{2,3},{3,2},{4,5},{5,4},{6,7},{7,6},{8,9},{9,8},{10,11... | collective-permute-start | bytes 1966088 | tf_op jit(solution)/shard_map/ppermute | solution.py:17
  59.6 31.6 %collective-permute-start.22 = (bf16[1280,128]{1,0:T(8,128)(2,1)}, bf16[1280,128]{1,0:T(8,128)(2,1)}, u32[]{:S(2)}, u32[]{:S(2)}) collective-permute-start(bf16[1280,128]{1,0:T(8,128)(2,1)} %get-tuple-element.443), channel_id=1, source_target_pairs={{0,2},{1,3},{2,0},{3,1},{4,6},{5,7},{6,4},{7,5},{8,10},{9,11},{10,... | collective-permute-start | bytes 983048 | tf_op jit(solution)/shard_map/ppermute | solution.py:17
  61.0 30.2 %collective-permute-start.23 = (bf16[1280,128]{1,0:T(8,128)(2,1)}, bf16[1280,128]{1,0:T(8,128)(2,1)}, u32[]{:S(2)}, u32[]{:S(2)}) collective-permute-start(bf16[1280,128]{1,0:T(8,128)(2,1)} %get-tuple-element.444), channel_id=1, source_target_pairs={{0,3},{1,2},{2,1},{3,0},{4,7},{5,6},{6,5},{7,4},{8,11},{9,10},{10,... | collective-permute-start | bytes 983048 | tf_op jit(solution)/shard_map/ppermute | solution.py:17
  65.3 14.0 %collective-permute-start = (bf16[1024,256]{1,0:T(8,128)(2,1)S(1)}, bf16[1024,256]{1,0:T(8,128)(2,1)}, u32[]{:S(2)}, u32[]{:S(2)}) collective-permute-start(bf16[1024,256]{1,0:T(8,128)(2,1)S(1)} %copy.33), channel_id=1, source_target_pairs={{0,8},{4,12},{8,0},{12,4},{1,9},{5,13},{9,1},{13,5},{2,10},{6,14},... | collective-permute-start | bytes 1572872 | tf_op jit(solution)/shard_map/while/body/ppermute | solution.py:17
  65.9 13.3 %collective-permute-start.1 = (f32[1,512]{1,0:T(1,128)S(1)}, f32[1,512]{1,0:T(1,128)S(1)}, u32[]{:S(2)}, u32[]{:S(2)}) collective-permute-start(f32[1,512]{1,0:T(1,128)S(1)} %copy.34), channel_id=1, source_target_pairs={{0,8},{4,12},{8,0},{12,4},{1,9},{5,13},{9,1},{13,5},{2,10},{6,14},... | collective-permute-start | bytes 6152 | tf_op jit(solution)/shard_map/while/body/ppermute | solution.py:17
  80.4 2.7 %collective-permute-start.2 = (bf16[2048,256]{1,0:T(8,128)(2,1)S(1)}, bf16[2048,256]{1,0:T(8,128)(2,1)S(1)}, u32[]{:S(2)}, u32[]{:S(2)}) collective-permute-start(bf16[2048,256]{1,0:T(8,128)(2,1)S(1)} %pad_maximum_fusion.19.near), channel_id=1, source_target_pairs={{0,4},{4,0},{8,12},{12,8},{1,5},{5,1},{9,13},{13,9},{2,6},{6,2},{1... | collective-permute-start | bytes 3145736 | tf_op jit(solution)/shard_map/while/body/ppermute | solution.py:17
  92.3 12.7 %copy-start.15 = (f32[1,512]{1,0:T(1,128)S(1)}, f32[1,512]{1,0:T(1,128)}, u32[]{:S(2)}) copy-start(f32[1,512]{1,0:T(1,128)} %get-tuple-element.477) | copy-start | bytes 6148
  92.3 12.7 %copy-start.16 = (f32[1,128]{1,0:T(1,128)S(1)}, f32[1,128]{1,0:T(1,128)}, u32[]{:S(2)}) copy-start(f32[1,128]{1,0:T(1,128)} %param.18) | copy-start | bytes 1540
  92.3 8.2 %collective-permute-start.25 = (bf16[640,128]{1,0:T(8,128)(2,1)S(1)}, bf16[640,128]{1,0:T(8,128)(2,1)S(1)}, u32[]{:S(2)}, u32[]{:S(2)}) collective-permute-start(bf16[640,128]{1,0:T(8,128)(2,1)S(1)} %slice.147), channel_id=1, source_target_pairs={{0,3},{1,2},{2,1},{3,0},{4,7},{5,6},{6,5},{7,4},{8,11},{9,10},{10,... | collective-permute-start | bytes 491528 | tf_op jit(solution)/shard_map/ppermute | solution.py:17
  100.5 38.9 %collective-permute-start.26 = (bf16[1920,128]{1,0:T(8,128)(2,1)}, bf16[1920,128]{1,0:T(8,128)(2,1)}, u32[]{:S(2)}, u32[]{:S(2)}) collective-permute-start(bf16[1920,128]{1,0:T(8,128)(2,1)} %get-tuple-element.464), channel_id=1, source_target_pairs={{0,2},{1,3},{2,0},{3,1},{4,6},{5,7},{6,4},{7,5},{8,10},{9,11},{10,... | collective-permute-start | bytes 1474568 | tf_op jit(solution)/shard_map/ppermute | solution.py:17
  103.6 35.8 %collective-permute-start.27 = (bf16[1920,128]{1,0:T(8,128)(2,1)}, bf16[1920,128]{1,0:T(8,128)(2,1)}, u32[]{:S(2)}, u32[]{:S(2)}) collective-permute-start(bf16[1920,128]{1,0:T(8,128)(2,1)} %get-tuple-element.465), channel_id=1, source_target_pairs={{0,3},{1,2},{2,1},{3,0},{4,7},{5,6},{6,5},{7,4},{8,11},{9,10},{10,... | collective-permute-start | bytes 1474568 | tf_op jit(solution)/shard_map/ppermute | solution.py:17
  104.9 34.5 %collective-permute-start.28 = (bf16[1920,128]{1,0:T(8,128)(2,1)}, bf16[1920,128]{1,0:T(8,128)(2,1)}, u32[]{:S(2)}, u32[]{:S(2)}) collective-permute-start(bf16[1920,128]{1,0:T(8,128)(2,1)} %get-tuple-element.466), channel_id=1, source_target_pairs={{0,1},{1,0},{2,3},{3,2},{4,5},{5,4},{6,7},{7,6},{8,9},{9,8},{10,11... | collective-permute-start | bytes 1474568 | tf_op jit(solution)/shard_map/ppermute | solution.py:17
  105.0 34.4 %copy-start.10 = (f32[1920,128]{1,0:T(8,128)S(1)}, f32[1920,128]{1,0:T(8,128)}, u32[]{:S(2)}) copy-start(f32[1920,128]{1,0:T(8,128)} %get-tuple-element.480) | copy-start | bytes 2949124
  105.1 11.4 %collective-permute-start.3 = (bf16[1920,128]{1,0:T(8,128)(2,1)S(1)}, bf16[1920,128]{1,0:T(8,128)(2,1)S(1)}, u32[]{:S(2)}, u32[]{:S(2)}) collective-permute-start(bf16[1920,128]{1,0:T(8,128)(2,1)S(1)} %copy.52), channel_id=1, source_target_pairs={{0,8},{4,12},{8,0},{12,4},{1,9},{5,13},{9,1},{13,5},{2,10},{6,14},... | collective-permute-start | bytes 1474568 | tf_op jit(solution)/shard_map/while/body/ppermute | solution.py:17
  106.7 11.1 %collective-permute-start.4 = (bf16[1920,128]{1,0:T(8,128)(2,1)S(1)}, bf16[1920,128]{1,0:T(8,128)(2,1)S(1)}, u32[]{:S(2)}, u32[]{:S(2)}) collective-permute-start(bf16[1920,128]{1,0:T(8,128)(2,1)S(1)} %copy.52), channel_id=1, source_target_pairs={{0,16},{16,0},{1,17},{17,1},{2,18},{18,2},{3,19},{19,3},{4,20},{20... | collective-permute-start | bytes 1474568 | tf_op jit(solution)/shard_map/while/body/ppermute | solution.py:17
  118.0 13.7 %collective-permute-start.6 = (bf16[1920,256]{1,0:T(8,128)(2,1)S(1)}, bf16[1920,256]{1,0:T(8,128)(2,1)}, u32[]{:S(2)}, u32[]{:S(2)}) collective-permute-start(bf16[1920,256]{1,0:T(8,128)(2,1)S(1)} %pad_maximum_fusion.20), channel_id=1, source_target_pairs={{0,4},{4,0},{8,12},{12,8},{1,5},{5,1},{9,13},{13,9},{2,6},{6,2},{1... | collective-permute-start | bytes 2949128 | tf_op jit(solution)/shard_map/while/body/ppermute | solution.py:17
  118.1 13.6 %collective-permute-start.5 = (bf16[1920,128]{1,0:T(8,128)(2,1)S(1)}, bf16[1920,128]{1,0:T(8,128)(2,1)S(1)}, u32[]{:S(2)}, u32[]{:S(2)}) collective-permute-start(bf16[1920,128]{1,0:T(8,128)(2,1)S(1)} %collective-permute-done.4), channel_id=1, source_target_pairs={{0,8},{4,12},{8,0},{12,4},{1,9},{5,13},{9,1},{13,5},{2,10},{6,14},... | collective-permute-start | bytes 1474568 | tf_op jit(solution)/shard_map/while/body/ppermute | solution.py:17
  118.6 13.4 %copy-start.7 = (bf16[576,1920]{1,0:T(8,128)(2,1)S(1)}, bf16[576,1920]{1,0:T(8,128)(2,1)}, u32[]{:S(2)}) copy-start(bf16[576,1920]{1,0:T(8,128)(2,1)} %get-tuple-element.972) | copy-start | bytes 6635524 | tf_op jit(solution)/shard_map/while
  131.9 4.7 %collective-permute-start.7 = (bf16[1920,256]{1,0:T(8,128)(2,1)S(1)}, bf16[1920,256]{1,0:T(8,128)(2,1)S(1)}, u32[]{:S(2)}, u32[]{:S(2)}) collective-permute-start(bf16[1920,256]{1,0:T(8,128)(2,1)S(1)} %pad_maximum_fusion.21), channel_id=1, source_target_pairs={{0,4},{4,0},{8,12},{12,8},{1,5},{5,1},{9,13},{13,9},{2,6},{6,2},{1... | collective-permute-start | bytes 2949128 | tf_op jit(solution)/shard_map/while/body/ppermute | solution.py:17
  141.0 16.7 %collective-permute-start.30 = (bf16[1920,128]{1,0:T(8,128)(2,1)S(1)}, bf16[1920,128]{1,0:T(8,128)(2,1)S(1)}, u32[]{:S(2)}, u32[]{:S(2)}) collective-permute-start(bf16[1920,128]{1,0:T(8,128)(2,1)S(1)} %add_convert_fusion), channel_id=1, source_target_pairs={{0,8},{4,12},{8,0},{12,4},{1,9},{5,13},{9,1},{13,5},{2,10},{6,14},... | collective-permute-start | bytes 1474568 | tf_op jit(solution)/shard_map/ppermute | solution.py:17
  141.6 16.2 %collective-permute-start.31 = (bf16[1920,128]{1,0:T(8,128)(2,1)S(1)}, bf16[1920,128]{1,0:T(8,128)(2,1)S(1)}, u32[]{:S(2)}, u32[]{:S(2)}) collective-permute-start(bf16[1920,128]{1,0:T(8,128)(2,1)S(1)} %add_convert_fusion), channel_id=1, source_target_pairs={{0,16},{16,0},{1,17},{17,1},{2,18},{18,2},{3,19},{19,3},{4,20},{20... | collective-permute-start | bytes 1474568 | tf_op jit(solution)/shard_map/ppermute | solution.py:17
  143.3 14.4 %collective-permute-start.29 = (bf16[12,48,256]{2,1,0:T(8,128)(2,1)S(1)}, bf16[12,48,256]{2,1,0:T(8,128)(2,1)S(1)}, u32[]{:S(2)}, u32[]{:S(2)}) collective-permute-start(bf16[12,48,256]{2,1,0:T(8,128)(2,1)S(1)} %copy-done.12), channel_id=1, source_target_pairs={{0,1},{1,2},{2,3},{3,0},{4,5},{5,6},{6,7},{7,4},{8,9},{9,10},{10,1... | collective-permute-start | bytes 884744 | tf_op jit(solution)/shard_map/ppermute | solution.py:13
  158.5 23.3 %collective-permute-start.32 = (bf16[12,48,256]{2,1,0:T(8,128)(2,1)}, bf16[12,48,256]{2,1,0:T(8,128)(2,1)}, u32[]{:S(2)}, u32[]{:S(2)}) collective-permute-start(bf16[12,48,256]{2,1,0:T(8,128)(2,1)} %broadcast_select_fusion.13), channel_id=1, source_target_pairs={{0,2},{1,3},{2,0},{3,1},{4,6},{5,7},{6,4},{7,5},{8,10},{9,11},{10,... | collective-permute-start | bytes 884744 | tf_op jit(solution)/shard_map/ppermute | solution.py:13
  163.0 10.2 %collective-permute-start.10 = (bf16[1920,256]{1,0:T(8,128)(2,1)S(1)}, bf16[1920,256]{1,0:T(8,128)(2,1)}, u32[]{:S(2)}, u32[]{:S(2)}) collective-permute-start(bf16[1920,256]{1,0:T(8,128)(2,1)S(1)} %pad_maximum_fusion.23), channel_id=1, source_target_pairs={{0,4},{4,0},{8,12},{12,8},{1,5},{5,1},{9,13},{13,9},{2,6},{6,2},{1... | collective-permute-start | bytes 2949128 | tf_op jit(solution)/shard_map/while/body/ppermute | solution.py:17
  163.8 8.6 %collective-permute-start.9 = (bf16[960,128]{1,0:T(8,128)(2,1)}, bf16[960,128]{1,0:T(8,128)(2,1)S(1)}, u32[]{:S(2)}, u32[]{:S(2)}) collective-permute-start(bf16[960,128]{1,0:T(8,128)(2,1)} %slice.171), channel_id=1, source_target_pairs={{0,8},{4,12},{8,0},{12,4},{1,9},{5,13},{9,1},{13,5},{2,10},{6,14},... | collective-permute-start | bytes 737288 | tf_op jit(solution)/shard_map/while/body/ppermute | solution.py:17
  164.9 8.3 %collective-permute-start.8 = (bf16[960,128]{1,0:T(8,128)(2,1)}, bf16[960,128]{1,0:T(8,128)(2,1)S(1)}, u32[]{:S(2)}, u32[]{:S(2)}) collective-permute-start(bf16[960,128]{1,0:T(8,128)(2,1)} %slice.170), channel_id=1, source_target_pairs={{0,16},{16,0},{1,17},{17,1},{2,18},{18,2},{3,19},{19,3},{4,20},{20... | collective-permute-start | bytes 737288 | tf_op jit(solution)/shard_map/while/body/ppermute | solution.py:17
  173.5 5.9 %collective-permute-start.11 = (bf16[1920,256]{1,0:T(8,128)(2,1)S(1)}, bf16[1920,256]{1,0:T(8,128)(2,1)S(1)}, u32[]{:S(2)}, u32[]{:S(2)}) collective-permute-start(bf16[1920,256]{1,0:T(8,128)(2,1)S(1)} %pad_maximum_fusion.24), channel_id=1, source_target_pairs={{0,4},{4,0},{8,12},{12,8},{1,5},{5,1},{9,13},{13,9},{2,6},{6,2},{1... | collective-permute-start | bytes 2949128 | tf_op jit(solution)/shard_map/while/body/ppermute | solution.py:17
  181.9 10.4 %copy-start.11 = (bf16[12,48,256]{2,1,0:T(8,128)(2,1)S(1)}, bf16[12,48,256]{2,1,0:T(8,128)(2,1)}, u32[]{:S(2)}) copy-start(bf16[12,48,256]{2,1,0:T(8,128)(2,1)} %get-tuple-element.492) | copy-start | bytes 884740
  181.9 10.4 %collective-permute-start.36 = (bf16[12,48,256]{2,1,0:T(8,128)(2,1)}, bf16[12,48,256]{2,1,0:T(8,128)(2,1)S(1)}, u32[]{:S(2)}, u32[]{:S(2)}) collective-permute-start(bf16[12,48,256]{2,1,0:T(8,128)(2,1)} %get-tuple-element.492), channel_id=1, source_target_pairs={{0,1},{1,2},{2,3},{3,0},{4,5},{5,6},{6,7},{7,4},{8,9},{9,10},{10,1... | collective-permute-start | bytes 884744 | tf_op jit(solution)/shard_map/ppermute | solution.py:13
  192.4 13.7 %collective-permute-start.37 = (bf16[12,48,256]{2,1,0:T(8,128)(2,1)S(1)}, bf16[12,48,256]{2,1,0:T(8,128)(2,1)S(1)}, u32[]{:S(2)}, u32[]{:S(2)}) collective-permute-start(bf16[12,48,256]{2,1,0:T(8,128)(2,1)S(1)} %broadcast_select_fusion.12), channel_id=1, source_target_pairs={{0,2},{1,3},{2,0},{3,1},{4,6},{5,7},{6,4},{7,5},{8,10},{9,11},{10,... | collective-permute-start | bytes 884744 | tf_op jit(solution)/shard_map/ppermute | solution.py:13
  192.7 2.4 %collective-permute-start.33 = (bf16[4,48,2,1,128]{4,2,1,0,3:T(2,128)(2,1)S(1)}, bf16[4,48,2,1,128]{4,2,1,0,3:T(2,128)(2,1)S(1)}, u32[]{:S(2)}, u32[]{:S(2)}) collective-permute-start(bf16[4,48,2,1,128]{4,2,1,0,3:T(2,128)(2,1)S(1)} %squeeze.29), channel_id=1, source_target_pairs={{0,4},{4,0},{8,12},{12,8},{1,5},{5,1},{9,13},{13,9},{2,6},{6,2},{1... | collective-permute-start | bytes 294920 | tf_op jit(solution)/shard_map/ppermute | solution.py:17
  192.9 5.7 %collective-permute-start.34 = (bf16[4,48,2,1,128]{4,2,1,0,3:T(2,128)(2,1)S(1)}, bf16[4,48,2,1,128]{4,2,1,0,3:T(2,128)(2,1)S(1)}, u32[]{:S(2)}, u32[]{:S(2)}) collective-permute-start(bf16[4,48,2,1,128]{4,2,1,0,3:T(2,128)(2,1)S(1)} %squeeze.30), channel_id=1, source_target_pairs={{0,8},{4,12},{8,0},{12,4},{1,9},{5,13},{9,1},{13,5},{2,10},{6,14},... | collective-permute-start | bytes 294920 | tf_op jit(solution)/shard_map/ppermute | solution.py:17
  194.7 5.2 %collective-permute-start.35 = (bf16[4,48,2,1,128]{4,2,1,0,3:T(2,128)(2,1)S(1)}, bf16[4,48,2,1,128]{4,2,1,0,3:T(2,128)(2,1)S(1)}, u32[]{:S(2)}, u32[]{:S(2)}) collective-permute-start(bf16[4,48,2,1,128]{4,2,1,0,3:T(2,128)(2,1)S(1)} %squeeze.31), channel_id=1, source_target_pairs={{0,12},{4,8},{8,4},{12,0},{1,13},{5,9},{9,5},{13,1},{2,14},{6,10},... | collective-permute-start | bytes 294920 | tf_op jit(solution)/shard_map/ppermute | solution.py:17
  206.9 3.5 %collective-permute-start.38 = (bf16[4,48,2,1,128]{4,2,1,0,3:T(2,128)(2,1)S(1)}, bf16[4,48,2,1,128]{4,2,1,0,3:T(2,128)(2,1)S(1)}, u32[]{:S(2)}, u32[]{:S(2)}) collective-permute-start(bf16[4,48,2,1,128]{4,2,1,0,3:T(2,128)(2,1)S(1)} %squeeze.33), channel_id=1, source_target_pairs={{0,4},{4,0},{8,12},{12,8},{1,5},{5,1},{9,13},{13,9},{2,6},{6,2},{1... | collective-permute-start | bytes 294920 | tf_op jit(solution)/shard_map/ppermute | solution.py:17
  207.1 5.7 %collective-permute-start.39 = (bf16[4,48,2,1,128]{4,2,1,0,3:T(2,128)(2,1)S(1)}, bf16[4,48,2,1,128]{4,2,1,0,3:T(2,128)(2,1)S(1)}, u32[]{:S(2)}, u32[]{:S(2)}) collective-permute-start(bf16[4,48,2,1,128]{4,2,1,0,3:T(2,128)(2,1)S(1)} %squeeze.34), channel_id=1, source_target_pairs={{0,8},{4,12},{8,0},{12,4},{1,9},{5,13},{9,1},{13,5},{2,10},{6,14},... | collective-permute-start | bytes 294920 | tf_op jit(solution)/shard_map/ppermute | solution.py:17
  208.9 5.2 %collective-permute-start.40 = (bf16[4,48,2,1,128]{4,2,1,0,3:T(2,128)(2,1)S(1)}, bf16[4,48,2,1,128]{4,2,1,0,3:T(2,128)(2,1)S(1)}, u32[]{:S(2)}, u32[]{:S(2)}) collective-permute-start(bf16[4,48,2,1,128]{4,2,1,0,3:T(2,128)(2,1)S(1)} %squeeze.35), channel_id=1, source_target_pairs={{0,12},{4,8},{8,4},{12,0},{1,13},{5,9},{9,5},{13,1},{2,14},{6,10},... | collective-permute-start | bytes 294920 | tf_op jit(solution)/shard_map/ppermute | solution.py:17
  (13 other events, 47.3 us)
